TPU v7x, 32 devices: a whole 2x2x4 slice. The times are simulated.
32 devices in a mesh: rep: 2 (over x), ctx: 16 (over z, y, core).
Axes of the slice: x: 2, y: 2, z: 4, core: 2. Of those that a mesh axis runs over, the one named last changes fastest.
Arguments:
- q_nope: bfloat16 [2048, 16384], P(('rep', 'ctx')), parts along dimension 0, may hold values from -40 to 40
- q_rope: bfloat16 [2048, 2048], P(('rep', 'ctx')), parts along dimension 0, may hold values from -3 to 3
- c_kv: bfloat16 [2048, 512], P(('rep', 'ctx')), parts along dimension 0, may hold values from -4 to 4
- k_rope: bfloat16 [2048, 64], P(('rep', 'ctx')), parts along dimension 0, may hold values from -4 to 4
- w_value: bfloat16 [32, 512, 128], replicated, may hold values from -0.25 to 0.25
- norm_gain: float32 [4096], replicated, may hold values from 0.5 to 1.5
- expert_ids: int32 [2048, 1], P(('rep', 'ctx')), parts along dimension 0, may hold values from 0 to 1; in each aligned block of 64 rows (0 to 63, 64 to 127, ...) at most 64 rows name the same one
- gate_fixed: int32 [2048, 1], P(('rep', 'ctx')), parts along dimension 0, may hold values from 16384 to 65535
- w_gate: bfloat16 [16, 4096, 256], P('ctx'), may hold values from -0.09375 to 0.09375
- w_up: bfloat16 [16, 4096, 256], P('ctx'), may hold values from -0.09375 to 0.09375
- w_down: bfloat16 [16, 256, 4096], P('ctx'), may hold values from -0.125 to 0.125
Outputs:
- mixed_out: bfloat16 [2048, 4096], P(('rep', 'ctx')), parts along dimension 0
There are 2 independent parts, one for each index of `rep`. A program takes and returns all parts, laid end to end along the dimension named above; an argument that names none is the same for every part. Nothing has to cross between parts.
Inputs may be any that keep to these rules, and one draw needn't show every extreme that they name: `expert_ids`: in the rows of one device no expert is named more than 64 times, and in every draw some device names some expert exactly 64 times.
All inputs are finite; a program needn't handle non-finite values.
Results may differ from a plain program's by a relative error of at most 0.018.
Values may be sent and summed in bfloat16 or wider, within the bound.
No kernel may reach another device: no remote copies, remote signals or barrier semaphores. Data moves between devices by JAX's collectives and lax.ppermute only.
A program may use at most 128 MiB of HBM per device.

v0:
```python
import jax
import jax.numpy as jnp
from jax import lax
from jax.sharding import PartitionSpec as P

HEADS = 32
LAT = 512
ROPE = 64
VD = 128
SPAN = 8
TOP = 1


SCORE_SCALE = 192.0 ** (-0.5)
NORM_EPS = 1e-06
NEG_FILL = -1e30


def from_behind(block, axis, distance):
    devices = range(lax.axis_size(axis))
    route = [(i - distance, i) for i in devices if i - distance in devices]
    return lax.ppermute(block, axis, route)


def block_update(
    soft_state, query_rows, rope_rows, row_pos, latent_keys, rope_keys, key_pos, seq_length
):
    row_max, row_sum, mix_acc = soft_state
    contract = (((1,), (1,)), ((), ()))
    scores = lax.dot_general(query_rows, latent_keys, contract, preferred_element_type=jnp.float32)
    scores = scores + lax.dot_general(
        rope_rows, rope_keys, contract, preferred_element_type=jnp.float32
    )
    scores = scores * SCORE_SCALE
    allowed = (key_pos[None, :] <= row_pos[:, None]) & (key_pos[None, :] >= 0)
    allowed = allowed & (key_pos[None, :] // seq_length == row_pos[:, None] // seq_length)
    scores = jnp.where(allowed, scores, NEG_FILL)
    new_max = jnp.maximum(row_max, jnp.max(scores, axis=1))
    weights_f = jnp.where(allowed, jnp.exp(scores - new_max[:, None]), 0.0)
    rescale = jnp.exp(row_max - new_max)
    row_sum = row_sum * rescale + jnp.sum(weights_f, axis=1)
    mix_acc = mix_acc * rescale[:, None] + jnp.dot(
        weights_f.astype(jnp.bfloat16), latent_keys, preferred_element_type=jnp.float32
    )
    return (new_max, row_sum, mix_acc)


def expert_rows(received, w_gate, w_up, w_down):
    sources, slot_count, features = received.shape
    flat_rows = received.reshape(sources * slot_count, features)
    gate_act = jnp.dot(flat_rows, w_gate[0], preferred_element_type=jnp.float32)
    up_act = jnp.dot(flat_rows, w_up[0], preferred_element_type=jnp.float32)
    hidden = (jax.nn.silu(gate_act) * up_act).astype(jnp.bfloat16)
    partial_out = jnp.dot(hidden, w_down[0], preferred_element_type=jnp.float32).astype(
        jnp.bfloat16
    )
    return partial_out.reshape(sources, slot_count, features)


def local(
    q_nope, q_rope, c_kv, k_rope, w_value, norm_gain, expert_ids, gate_fixed, w_gate, w_up, w_down
):
    tok_here = c_kv.shape[0]
    n_ctx = lax.axis_size("ctx")
    seq_length = tok_here * n_ctx
    my_index = lax.axis_index("ctx")
    first_row = my_index * tok_here
    query_rows = q_nope.reshape(tok_here * HEADS, LAT)
    rope_rows = q_rope.reshape(tok_here * HEADS, ROPE)
    row_pos = first_row + jnp.arange(tok_here * HEADS, dtype=jnp.int32) // HEADS
    local_pos = jnp.arange(tok_here, dtype=jnp.int32)
    start_state = (
        jnp.full((tok_here * HEADS,), NEG_FILL, jnp.float32),
        jnp.zeros((tok_here * HEADS,), jnp.float32),
        jnp.zeros((tok_here * HEADS, LAT), jnp.float32),
    )
    soft_state = block_update(
        start_state, query_rows, rope_rows, row_pos, c_kv, k_rope, first_row + local_pos, seq_length
    )

    def cycle_turn(turn_index, carry):
        blocks, inner_state = carry
        blocks = from_behind((blocks[0], blocks[1]), "ctx", 1)
        key_pos = (my_index - turn_index) * tok_here + local_pos

        def attend(state_in):
            return block_update(
                state_in, query_rows, rope_rows, row_pos, blocks[0], blocks[1], key_pos, seq_length
            )

        inner_state = lax.cond(
            turn_index <= my_index, attend, lambda state_in: state_in, inner_state
        )
        return (blocks, inner_state)

    _, soft_state = lax.fori_loop(1, n_ctx, cycle_turn, ((c_kv, k_rope), soft_state))
    row_max, row_sum, mix_acc = soft_state
    latent_out = (mix_acc / row_sum[:, None]).astype(jnp.bfloat16).reshape(tok_here, HEADS, LAT)
    values = jnp.einsum("thc,hcv->thv", latent_out, w_value, preferred_element_type=jnp.float32)
    values = values.astype(jnp.bfloat16).reshape(tok_here, HEADS * VD)
    values_f = values.astype(jnp.float32)
    normed = (
        values_f
        * lax.rsqrt(jnp.mean(values_f * values_f, axis=1, keepdims=True) + NORM_EPS)
        * norm_gain
    )
    normed = normed.astype(jnp.bfloat16)
    features = normed.shape[1]
    experts = n_ctx // SPAN
    capacity = min(tok_here, 3 * tok_here * TOP // experts)
    pair_ids = expert_ids.reshape(tok_here * TOP)
    one_hot = (pair_ids[:, None] == jnp.arange(experts, dtype=jnp.int32)[None, :]).astype(jnp.int32)
    earlier = jnp.cumsum(one_hot, axis=0) - one_hot
    pair_slot = jnp.sum(earlier * one_hot, axis=1)
    pair_target = pair_ids * capacity + pair_slot
    select = pair_target[None, :] == jnp.arange(experts * capacity, dtype=jnp.int32)[:, None]
    select = jnp.any(select.reshape(experts * capacity, tok_here, TOP), axis=2).astype(jnp.bfloat16)
    packed = jnp.dot(select, normed, preferred_element_type=jnp.float32).astype(jnp.bfloat16)
    packed = packed.reshape(experts, 1, capacity, features)
    send_rows = jnp.broadcast_to(packed, (experts, SPAN, capacity, features)).reshape(
        n_ctx, capacity, features
    )
    partials = expert_rows(
        lax.all_to_all(send_rows, "ctx", split_axis=0, concat_axis=0, tiled=True),
        w_gate,
        w_up,
        w_down,
    )
    returned_parts = lax.all_to_all(partials, "ctx", split_axis=0, concat_axis=0, tiled=True)
    summed = jnp.sum(
        returned_parts.reshape(experts, SPAN, capacity, features).astype(jnp.float32), axis=1
    )
    summed = summed.reshape(experts * capacity, features)
    picked = jnp.take(summed, pair_target, axis=0).reshape(tok_here, TOP, features)
    gate_weight = gate_fixed.astype(jnp.float32) / 65536.0
    branch = jnp.sum(gate_weight[:, :, None] * picked, axis=1)
    return (values_f + branch).astype(jnp.bfloat16)


def solution(mesh):
    in_specs = (
        P(("rep", "ctx"), None),
        P(("rep", "ctx"), None),
        P(("rep", "ctx"), None),
        P(("rep", "ctx"), None),
        P(),
        P(),
        P(("rep", "ctx"), None),
        P(("rep", "ctx"), None),
        P("ctx", None, None),
        P("ctx", None, None),
        P("ctx", None, None),
    )
    out_specs = P(("rep", "ctx"), None)
    return jax.shard_map(local, mesh=mesh, in_specs=in_specs, out_specs=out_specs, check_vma=False)
```

profile of v0, /device:TPU:13, one launch (start us, length us, event | category | flops | bytes accessed | tf_op | source)
XLA Modules:
  0.0 651.4 jit_solution(2800348153075208098)
XLA Ops:
  12.3 211.7 %while.22 = (s32[]{:T(128)}, bf16[64,512]{1,0:T(8,128)(2,1)S(1)}, bf16[64,64]{1,0:T(8,128)(2,1)S(1)}, f32[2048]{0:T(1024)S(1)}, f32[2048]{0:T(1024)S(1)}, /*inde...) while((s32[]{:T(128)}, bf16[64,512]{1,0:T(8,128)(2,1)S(1)}, ...), condition=%wide.region_7.8_spmd.clone, body=%wide.region_2.7_spmd.clone.sunk | while | flops 290247744 | bytes 14200231 | solution.py:96
  19.1 8.1 %conditional.3 = ((f32[2048]{0:T(1024)S(1)}, f32[2048]{0:T(1024)S(1)}, f32[2048,512]{1,0:T(8,128)})) conditional(s32[]{:T(128)} %convert_element_type.114, (f32[2048]{0:T(1024)S(1)}, f32[2048]{0:T(1024)S(1)}, f32[2048,512]{1,0:T(8,128)}) %tuple.64, (s32[]{:T(128)}, s32[]{:T(128)}, s32[64]{0:T(128)S(1)}, s32[]{:T(128)}, ...), branch_computations={%region_3.3_spmd, %region_4.6_spmd.clone} | conditional | flops 290245696 | bytes 13740868 | solution.py:91
  22.2 5.0 multiply_add_fusion
  35.1 8.1 %conditional.3 = ((f32[2048]{0:T(1024)S(1)}, f32[2048]{0:T(1024)S(1)}, f32[2048,512]{1,0:T(8,128)})) conditional(s32[]{:T(128)} %convert_element_type.114, (f32[2048]{0:T(1024)S(1)}, f32[2048]{0:T(1024)S(1)}, f32[2048,512]{1,0:T(8,128)}) %tuple.64, (s32[]{:T(128)}, s32[]{:T(128)}, s32[64]{0:T(128)S(1)}, s32[]{:T(128)}, ...), branch_computations={%region_3.3_spmd, %region_4.6_spmd.clone} | conditional | flops 290245696 | bytes 13740868 | solution.py:91
  38.2 5.0 multiply_add_fusion
  51.1 8.1 %conditional.3 = ((f32[2048]{0:T(1024)S(1)}, f32[2048]{0:T(1024)S(1)}, f32[2048,512]{1,0:T(8,128)})) conditional(s32[]{:T(128)} %convert_element_type.114, (f32[2048]{0:T(1024)S(1)}, f32[2048]{0:T(1024)S(1)}, f32[2048,512]{1,0:T(8,128)}) %tuple.64, (s32[]{:T(128)}, s32[]{:T(128)}, s32[64]{0:T(128)S(1)}, s32[]{:T(128)}, ...), branch_computations={%region_3.3_spmd, %region_4.6_spmd.clone} | conditional | flops 290245696 | bytes 13740868 | solution.py:91
  54.2 5.0 multiply_add_fusion
  59.2 4.8 collective-permute-start
  67.1 8.1 %conditional.3 = ((f32[2048]{0:T(1024)S(1)}, f32[2048]{0:T(1024)S(1)}, f32[2048,512]{1,0:T(8,128)})) conditional(s32[]{:T(128)} %convert_element_type.114, (f32[2048]{0:T(1024)S(1)}, f32[2048]{0:T(1024)S(1)}, f32[2048,512]{1,0:T(8,128)}) %tuple.64, (s32[]{:T(128)}, s32[]{:T(128)}, s32[64]{0:T(128)S(1)}, s32[]{:T(128)}, ...), branch_computations={%region_3.3_spmd, %region_4.6_spmd.clone} | conditional | flops 290245696 | bytes 13740868 | solution.py:91
  70.2 5.0 multiply_add_fusion
  75.2 4.8 collective-permute-start
  83.1 8.1 %conditional.3 = ((f32[2048]{0:T(1024)S(1)}, f32[2048]{0:T(1024)S(1)}, f32[2048,512]{1,0:T(8,128)})) conditional(s32[]{:T(128)} %convert_element_type.114, (f32[2048]{0:T(1024)S(1)}, f32[2048]{0:T(1024)S(1)}, f32[2048,512]{1,0:T(8,128)}) %tuple.64, (s32[]{:T(128)}, s32[]{:T(128)}, s32[64]{0:T(128)S(1)}, s32[]{:T(128)}, ...), branch_computations={%region_3.3_spmd, %region_4.6_spmd.clone} | conditional | flops 290245696 | bytes 13740868 | solution.py:91
  86.2 5.0 multiply_add_fusion
  91.2 4.8 collective-permute-start
  99.1 8.1 %conditional.3 = ((f32[2048]{0:T(1024)S(1)}, f32[2048]{0:T(1024)S(1)}, f32[2048,512]{1,0:T(8,128)})) conditional(s32[]{:T(128)} %convert_element_type.114, (f32[2048]{0:T(1024)S(1)}, f32[2048]{0:T(1024)S(1)}, f32[2048,512]{1,0:T(8,128)}) %tuple.64, (s32[]{:T(128)}, s32[]{:T(128)}, s32[64]{0:T(128)S(1)}, s32[]{:T(128)}, ...), branch_computations={%region_3.3_spmd, %region_4.6_spmd.clone} | conditional | flops 290245696 | bytes 13740868 | solution.py:91
  102.2 5.0 multiply_add_fusion
  107.2 4.8 collective-permute-start
  115.1 8.1 %conditional.3 = ((f32[2048]{0:T(1024)S(1)}, f32[2048]{0:T(1024)S(1)}, f32[2048,512]{1,0:T(8,128)})) conditional(s32[]{:T(128)} %convert_element_type.114, (f32[2048]{0:T(1024)S(1)}, f32[2048]{0:T(1024)S(1)}, f32[2048,512]{1,0:T(8,128)}) %tuple.64, (s32[]{:T(128)}, s32[]{:T(128)}, s32[64]{0:T(128)S(1)}, s32[]{:T(128)}, ...), branch_computations={%region_3.3_spmd, %region_4.6_spmd.clone} | conditional | flops 290245696 | bytes 13740868 | solution.py:91
  118.2 5.0 multiply_add_fusion
  131.2 12.8 %collective-permute-start = (bf16[64,512]{1,0:T(8,128)(2,1)S(1)}, bf16[64,512]{1,0:T(8,128)(2,1)S(1)}, u32[]{:S(2)}, u32[]{:S(2)}) collective-permute-start(bf16[64,512]{1,0:T(8,128)(2,1)S(1)} %get-tuple-element.472), channel_id=1, source_target_pairs={{0,1},{1,2},{2,3},{3,4},{4,5},{5,6},{6,7},{7,8},{8,9},{9,10},{10,1... | collective-permute-start | bytes 196616 | tf_op jit(solution)/shard_map/while/body/eval_jaxpr/ppermute | solution.py:22
  152.0 7.1 %collective-permute-start.1 = (bf16[64,64]{1,0:T(8,128)(2,1)S(1)}, bf16[64,64]{1,0:T(8,128)(2,1)S(1)}, u32[]{:S(2)}, u32[]{:S(2)}) collective-permute-start(bf16[64,64]{1,0:T(8,128)(2,1)S(1)} %get-tuple-element.473), channel_id=1, source_target_pairs={{0,1},{1,2},{2,3},{3,4},{4,5},{5,6},{6,7},{7,8},{8,9},{9,10},{10,1... | collective-permute-start | bytes 24584 | tf_op jit(solution)/shard_map/while/body/eval_jaxpr/ppermute | solution.py:22
  160.1 5.1 collective-permute-start
  168.3 12.5 %collective-permute-start = (bf16[64,512]{1,0:T(8,128)(2,1)S(1)}, bf16[64,512]{1,0:T(8,128)(2,1)S(1)}, u32[]{:S(2)}, u32[]{:S(2)}) collective-permute-start(bf16[64,512]{1,0:T(8,128)(2,1)S(1)} %get-tuple-element.472), channel_id=1, source_target_pairs={{0,1},{1,2},{2,3},{3,4},{4,5},{5,6},{6,7},{7,8},{8,9},{9,10},{10,1... | collective-permute-start | bytes 196616 | tf_op jit(solution)/shard_map/while/body/eval_jaxpr/ppermute | solution.py:22
  184.0 5.1 collective-permute-start
  189.2 10.0 %collective-permute-start.1 = (bf16[64,64]{1,0:T(8,128)(2,1)S(1)}, bf16[64,64]{1,0:T(8,128)(2,1)S(1)}, u32[]{:S(2)}, u32[]{:S(2)}) collective-permute-start(bf16[64,64]{1,0:T(8,128)(2,1)S(1)} %get-tuple-element.473), channel_id=1, source_target_pairs={{0,1},{1,2},{2,3},{3,4},{4,5},{5,6},{6,7},{7,8},{8,9},{9,10},{10,1... | collective-permute-start | bytes 24584 | tf_op jit(solution)/shard_map/while/body/eval_jaxpr/ppermute | solution.py:22
  200.0 5.1 collective-permute-start
  208.3 12.5 %collective-permute-start = (bf16[64,512]{1,0:T(8,128)(2,1)S(1)}, bf16[64,512]{1,0:T(8,128)(2,1)S(1)}, u32[]{:S(2)}, u32[]{:S(2)}) collective-permute-start(bf16[64,512]{1,0:T(8,128)(2,1)S(1)} %get-tuple-element.472), channel_id=1, source_target_pairs={{0,1},{1,2},{2,3},{3,4},{4,5},{5,6},{6,7},{7,8},{8,9},{9,10},{10,1... | collective-permute-start | bytes 196616 | tf_op jit(solution)/shard_map/while/body/eval_jaxpr/ppermute | solution.py:22
  232.1 208.3 %all_to_all.10 = bf16[16,64,4096]{2,1,0:T(8,128)(2,1)S(1)} all-to-all(bf16[16,64,4096]{2,1,0:T(8,128)(2,1)S(1)} %bitcast.70), channel_id=1, replica_groups=mesh['rep'=2,'ctx'=16] {'ctx'}, dimensions={0} | all-to-all | bytes 16777216 | tf_op jit(solution)/shard_map/all_to_all | solution.py:124
  445.2 5.6 convolution_convert_fusion
  450.8 5.8 all-to-all-start.1
  456.7 182.3 %all-to-all-done.1 = bf16[16,64,4096]{2,1,0:T(8,128)(2,1)} async-done(((bf16[16,64,4096]{2,1,0:T(8,128)(2,1)}), bf16[16,64,4096]{2,1,0:T(8,128)(2,1)}, u32[]{:S(2)}, u32[]{:S(2)}) %all-to-all-start.1) | async-done | bytes 8388640 | tf_op jit(solution)/shard_map/all_to_all | solution.py:129
  639.0 6.3 convert_reduce_fusion
  (239 shorter events, 117.0 us)
Async XLA Ops:
  0.0 445.2 %copy-start = (bf16[1,256,4096]{2,1,0:T(8,128)(2,1)S(1)}, bf16[1,256,4096]{2,1,0:T(8,128)(2,1)}, u32[]{:S(2)}) copy-start(bf16[1,256,4096]{2,1,0:T(8,128)(2,1)} %param.25) | copy-start | bytes 6291460
  12.3 6.8 %collective-permute-start = (bf16[64,512]{1,0:T(8,128)(2,1)S(1)}, bf16[64,512]{1,0:T(8,128)(2,1)S(1)}, u32[]{:S(2)}, u32[]{:S(2)}) collective-permute-start(bf16[64,512]{1,0:T(8,128)(2,1)S(1)} %get-tuple-element.472), channel_id=1, source_target_pairs={{0,1},{1,2},{2,3},{3,4},{4,5},{5,6},{6,7},{7,8},{8,9},{9,10},{10,1... | collective-permute-start | bytes 196616 | tf_op jit(solution)/shard_map/while/body/eval_jaxpr/ppermute | solution.py:22
  16.0 3.1 collective-permute-start.1
  27.2 7.9 %collective-permute-start = (bf16[64,512]{1,0:T(8,128)(2,1)S(1)}, bf16[64,512]{1,0:T(8,128)(2,1)S(1)}, u32[]{:S(2)}, u32[]{:S(2)}) collective-permute-start(bf16[64,512]{1,0:T(8,128)(2,1)S(1)} %get-tuple-element.472), channel_id=1, source_target_pairs={{0,1},{1,2},{2,3},{3,4},{4,5},{5,6},{6,7},{7,8},{8,9},{9,10},{10,1... | collective-permute-start | bytes 196616 | tf_op jit(solution)/shard_map/while/body/eval_jaxpr/ppermute | solution.py:22
  32.0 3.1 collective-permute-start.1
  43.2 7.9 %collective-permute-start = (bf16[64,512]{1,0:T(8,128)(2,1)S(1)}, bf16[64,512]{1,0:T(8,128)(2,1)S(1)}, u32[]{:S(2)}, u32[]{:S(2)}) collective-permute-start(bf16[64,512]{1,0:T(8,128)(2,1)S(1)} %get-tuple-element.472), channel_id=1, source_target_pairs={{0,1},{1,2},{2,3},{3,4},{4,5},{5,6},{6,7},{7,8},{8,9},{9,10},{10,1... | collective-permute-start | bytes 196616 | tf_op jit(solution)/shard_map/while/body/eval_jaxpr/ppermute | solution.py:22
  48.0 3.1 collective-permute-start.1
  59.2 7.9 %collective-permute-start = (bf16[64,512]{1,0:T(8,128)(2,1)S(1)}, bf16[64,512]{1,0:T(8,128)(2,1)S(1)}, u32[]{:S(2)}, u32[]{:S(2)}) collective-permute-start(bf16[64,512]{1,0:T(8,128)(2,1)S(1)} %get-tuple-element.472), channel_id=1, source_target_pairs={{0,1},{1,2},{2,3},{3,4},{4,5},{5,6},{6,7},{7,8},{8,9},{9,10},{10,1... | collective-permute-start | bytes 196616 | tf_op jit(solution)/shard_map/while/body/eval_jaxpr/ppermute | solution.py:22
  64.0 3.1 collective-permute-start.1
  75.2 7.9 %collective-permute-start = (bf16[64,512]{1,0:T(8,128)(2,1)S(1)}, bf16[64,512]{1,0:T(8,128)(2,1)S(1)}, u32[]{:S(2)}, u32[]{:S(2)}) collective-permute-start(bf16[64,512]{1,0:T(8,128)(2,1)S(1)} %get-tuple-element.472), channel_id=1, source_target_pairs={{0,1},{1,2},{2,3},{3,4},{4,5},{5,6},{6,7},{7,8},{8,9},{9,10},{10,1... | collective-permute-start | bytes 196616 | tf_op jit(solution)/shard_map/while/body/eval_jaxpr/ppermute | solution.py:22
  80.0 3.1 collective-permute-start.1
  91.2 7.9 %collective-permute-start = (bf16[64,512]{1,0:T(8,128)(2,1)S(1)}, bf16[64,512]{1,0:T(8,128)(2,1)S(1)}, u32[]{:S(2)}, u32[]{:S(2)}) collective-permute-start(bf16[64,512]{1,0:T(8,128)(2,1)S(1)} %get-tuple-element.472), channel_id=1, source_target_pairs={{0,1},{1,2},{2,3},{3,4},{4,5},{5,6},{6,7},{7,8},{8,9},{9,10},{10,1... | collective-permute-start | bytes 196616 | tf_op jit(solution)/shard_map/while/body/eval_jaxpr/ppermute | solution.py:22
  96.0 3.1 collective-permute-start.1
  107.2 7.9 %collective-permute-start = (bf16[64,512]{1,0:T(8,128)(2,1)S(1)}, bf16[64,512]{1,0:T(8,128)(2,1)S(1)}, u32[]{:S(2)}, u32[]{:S(2)}) collective-permute-start(bf16[64,512]{1,0:T(8,128)(2,1)S(1)} %get-tuple-element.472), channel_id=1, source_target_pairs={{0,1},{1,2},{2,3},{3,4},{4,5},{5,6},{6,7},{7,8},{8,9},{9,10},{10,1... | collective-permute-start | bytes 196616 | tf_op jit(solution)/shard_map/while/body/eval_jaxpr/ppermute | solution.py:22
  112.0 3.1 collective-permute-start.1
  123.2 7.9 %collective-permute-start = (bf16[64,512]{1,0:T(8,128)(2,1)S(1)}, bf16[64,512]{1,0:T(8,128)(2,1)S(1)}, u32[]{:S(2)}, u32[]{:S(2)}) collective-permute-start(bf16[64,512]{1,0:T(8,128)(2,1)S(1)} %get-tuple-element.472), channel_id=1, source_target_pairs={{0,1},{1,2},{2,3},{3,4},{4,5},{5,6},{6,7},{7,8},{8,9},{9,10},{10,1... | collective-permute-start | bytes 196616 | tf_op jit(solution)/shard_map/while/body/eval_jaxpr/ppermute | solution.py:22
  128.0 3.1 collective-permute-start.1
  131.2 15.9 %collective-permute-start = (bf16[64,512]{1,0:T(8,128)(2,1)S(1)}, bf16[64,512]{1,0:T(8,128)(2,1)S(1)}, u32[]{:S(2)}, u32[]{:S(2)}) collective-permute-start(bf16[64,512]{1,0:T(8,128)(2,1)S(1)} %get-tuple-element.472), channel_id=1, source_target_pairs={{0,1},{1,2},{2,3},{3,4},{4,5},{5,6},{6,7},{7,8},{8,9},{9,10},{10,1... | collective-permute-start | bytes 196616 | tf_op jit(solution)/shard_map/while/body/eval_jaxpr/ppermute | solution.py:22
  144.1 3.1 collective-permute-start.1
  147.2 12.8 %collective-permute-start = (bf16[64,512]{1,0:T(8,128)(2,1)S(1)}, bf16[64,512]{1,0:T(8,128)(2,1)S(1)}, u32[]{:S(2)}, u32[]{:S(2)}) collective-permute-start(bf16[64,512]{1,0:T(8,128)(2,1)S(1)} %get-tuple-element.472), channel_id=1, source_target_pairs={{0,1},{1,2},{2,3},{3,4},{4,5},{5,6},{6,7},{7,8},{8,9},{9,10},{10,1... | collective-permute-start | bytes 196616 | tf_op jit(solution)/shard_map/while/body/eval_jaxpr/ppermute | solution.py:22
  152.0 8.0 %collective-permute-start.1 = (bf16[64,64]{1,0:T(8,128)(2,1)S(1)}, bf16[64,64]{1,0:T(8,128)(2,1)S(1)}, u32[]{:S(2)}, u32[]{:S(2)}) collective-permute-start(bf16[64,64]{1,0:T(8,128)(2,1)S(1)} %get-tuple-element.473), channel_id=1, source_target_pairs={{0,1},{1,2},{2,3},{3,4},{4,5},{5,6},{6,7},{7,8},{8,9},{9,10},{10,1... | collective-permute-start | bytes 24584 | tf_op jit(solution)/shard_map/while/body/eval_jaxpr/ppermute | solution.py:22
  160.1 8.2 %collective-permute-start = (bf16[64,512]{1,0:T(8,128)(2,1)S(1)}, bf16[64,512]{1,0:T(8,128)(2,1)S(1)}, u32[]{:S(2)}, u32[]{:S(2)}) collective-permute-start(bf16[64,512]{1,0:T(8,128)(2,1)S(1)} %get-tuple-element.472), channel_id=1, source_target_pairs={{0,1},{1,2},{2,3},{3,4},{4,5},{5,6},{6,7},{7,8},{8,9},{9,10},{10,1... | collective-permute-start | bytes 196616 | tf_op jit(solution)/shard_map/while/body/eval_jaxpr/ppermute | solution.py:22
  165.2 3.1 collective-permute-start.1
  168.3 15.6 %collective-permute-start = (bf16[64,512]{1,0:T(8,128)(2,1)S(1)}, bf16[64,512]{1,0:T(8,128)(2,1)S(1)}, u32[]{:S(2)}, u32[]{:S(2)}) collective-permute-start(bf16[64,512]{1,0:T(8,128)(2,1)S(1)} %get-tuple-element.472), channel_id=1, source_target_pairs={{0,1},{1,2},{2,3},{3,4},{4,5},{5,6},{6,7},{7,8},{8,9},{9,10},{10,1... | collective-permute-start | bytes 196616 | tf_op jit(solution)/shard_map/while/body/eval_jaxpr/ppermute | solution.py:22
  180.8 3.1 collective-permute-start.1
  184.0 15.9 %collective-permute-start = (bf16[64,512]{1,0:T(8,128)(2,1)S(1)}, bf16[64,512]{1,0:T(8,128)(2,1)S(1)}, u32[]{:S(2)}, u32[]{:S(2)}) collective-permute-start(bf16[64,512]{1,0:T(8,128)(2,1)S(1)} %get-tuple-element.472), channel_id=1, source_target_pairs={{0,1},{1,2},{2,3},{3,4},{4,5},{5,6},{6,7},{7,8},{8,9},{9,10},{10,1... | collective-permute-start | bytes 196616 | tf_op jit(solution)/shard_map/while/body/eval_jaxpr/ppermute | solution.py:22
  189.2 10.8 %collective-permute-start.1 = (bf16[64,64]{1,0:T(8,128)(2,1)S(1)}, bf16[64,64]{1,0:T(8,128)(2,1)S(1)}, u32[]{:S(2)}, u32[]{:S(2)}) collective-permute-start(bf16[64,64]{1,0:T(8,128)(2,1)S(1)} %get-tuple-element.473), channel_id=1, source_target_pairs={{0,1},{1,2},{2,3},{3,4},{4,5},{5,6},{6,7},{7,8},{8,9},{9,10},{10,1... | collective-permute-start | bytes 24584 | tf_op jit(solution)/shard_map/while/body/eval_jaxpr/ppermute | solution.py:22
  200.0 8.2 %collective-permute-start = (bf16[64,512]{1,0:T(8,128)(2,1)S(1)}, bf16[64,512]{1,0:T(8,128)(2,1)S(1)}, u32[]{:S(2)}, u32[]{:S(2)}) collective-permute-start(bf16[64,512]{1,0:T(8,128)(2,1)S(1)} %get-tuple-element.472), channel_id=1, source_target_pairs={{0,1},{1,2},{2,3},{3,4},{4,5},{5,6},{6,7},{7,8},{8,9},{9,10},{10,1... | collective-permute-start | bytes 196616 | tf_op jit(solution)/shard_map/while/body/eval_jaxpr/ppermute | solution.py:22
  205.2 3.1 collective-permute-start.1
  208.3 15.6 %collective-permute-start = (bf16[64,512]{1,0:T(8,128)(2,1)S(1)}, bf16[64,512]{1,0:T(8,128)(2,1)S(1)}, u32[]{:S(2)}, u32[]{:S(2)}) collective-permute-start(bf16[64,512]{1,0:T(8,128)(2,1)S(1)} %get-tuple-element.472), channel_id=1, source_target_pairs={{0,1},{1,2},{2,3},{3,4},{4,5},{5,6},{6,7},{7,8},{8,9},{9,10},{10,1... | collective-permute-start | bytes 196616 | tf_op jit(solution)/shard_map/while/body/eval_jaxpr/ppermute | solution.py:22
  220.8 3.1 collective-permute-start.1
  450.8 188.2 %all-to-all-start.1 = ((bf16[16,64,4096]{2,1,0:T(8,128)(2,1)}), bf16[16,64,4096]{2,1,0:T(8,128)(2,1)}, u32[]{:S(2)}, u32[]{:S(2)}) async-start(bf16[16,64,4096]{2,1,0:T(8,128)(2,1)} %bitcast.69), calls=%async_computation.1 | async-start | bytes 16777216 | tf_op jit(solution)/shard_map/all_to_all | solution.py:129
  (7 other events, 233.1 us)
where the time goes:
time: 654 us; the launch traced here: 651 us
  blocking collectives  208 us (32%)
  waiting for transfers between devices  198 us (30%)
  starting transfers between devices  144 us (22%)
  matrix products  72.7 us (11%)
  other arithmetic  14.3 us (2%)
  local copies, waits for them, and re-layouts  12.3 us (2%)
    all_to_all x1, blocking collectives, local(): lax.all_to_all(send_rows, 'ctx', split_axis=0, concat_axis=0, tiled=True)  208 us
    all_to_all x1, waiting for transfers between devices, local(): lax.all_to_all(partials, 'ctx', split_axis=0, concat_axis=0, tiled=True)  182 us
    ppermute x30, starting transfers between devices, from_behind(): return lax.ppermute(block, axis, route)  138 us
    dot_general x8, matrix products, block_update(): jnp.dot(weights_f.astype(jnp.bfloat16), latent_keys, preferred_element_ty...  37.7 us
    dot_general x8, matrix products, block_update(): lax.dot_general(query_rows, latent_keys, contract, preferred_element_type...  18.7 us
    ppermute x30, waiting for transfers between devices, from_behind(): return lax.ppermute(block, axis, route)  15.8 us
  transfers between devices with their start and end apart: 31, of which 16 were waited for; matrix products, arithmetic and copies ran while one was open for 0% of the time, Pallas kernels for 0%

commit v1 on v0

v1 whole, which is shorter than its diff:
```python
import functools

import jax
import jax.numpy as jnp
from jax import lax
from jax.experimental import pallas as pl
from jax.experimental.pallas import tpu as pltpu
from jax.sharding import PartitionSpec as P

HEADS = 32
LAT = 512
ROPE = 64
VD = 128
SPAN = 8
CORES = 2

SCORE_SCALE = 192.0 ** (-0.5)
NORM_EPS = 1e-06
NEG_FILL = -1e30

HEAD_GROUP = 8
KEY_BLOCK = 512


def attention_kernel(
    index_ref, q_ref, qr_ref, keys_ref, wv_ref, gain_ref, values_ref, normed_ref, stack_ref,
    max_ref, sum_ref, acc_ref, *, tok, key_block,
):
    group = pl.program_id(0)
    my_index = index_ref[0]
    rows = HEAD_GROUP * tok
    lane = lax.broadcasted_iota(jnp.int32, (tok, 2 * ROPE), 1)
    for head in range(HEAD_GROUP):
        at = pl.ds(head * tok, tok)
        stack_ref[at, 0:LAT] = q_ref[:, head * LAT : (head + 1) * LAT]
        pair = qr_ref[:, (head // 2) * 2 * ROPE : (head // 2 + 1) * 2 * ROPE]
        keep = (lane < ROPE) if head % 2 == 0 else (lane >= ROPE)
        stack_ref[at, LAT : LAT + 2 * ROPE] = jnp.where(keep, pair, jnp.zeros_like(pair))
    max_ref[...] = jnp.full_like(max_ref, NEG_FILL)
    sum_ref[...] = jnp.zeros_like(sum_ref)
    acc_ref[...] = jnp.zeros_like(acc_ref)
    row_pos = my_index * tok + lax.rem(
        lax.broadcasted_iota(jnp.int32, (rows, key_block), 0), jnp.int32(tok)
    )
    key_iota = lax.broadcasted_iota(jnp.int32, (rows, key_block), 1)

    def step(block, carry):
        start = pl.multiple_of(block * key_block, key_block)
        keys = keys_ref[pl.ds(start, key_block), :]
        scores = lax.dot_general(
            stack_ref[...], keys, (((1,), (1,)), ((), ())), preferred_element_type=jnp.float32
        )
        scores = jnp.where(key_iota + start <= row_pos, scores * SCORE_SCALE, NEG_FILL)
        old_max = max_ref[...]
        new_max = jnp.maximum(old_max, jnp.max(scores, axis=1, keepdims=True))
        weights = jnp.exp(scores - new_max)
        rescale = jnp.exp(old_max - new_max)
        max_ref[...] = new_max
        sum_ref[...] = sum_ref[...] * rescale + jnp.sum(weights, axis=1, keepdims=True)
        acc_ref[...] = acc_ref[...] * rescale + jnp.dot(
            weights.astype(jnp.bfloat16), keys[:, 0:LAT], preferred_element_type=jnp.float32
        )
        return carry

    blocks = ((my_index + 1) * tok + key_block - 1) // key_block
    lax.fori_loop(0, blocks, step, 0)
    latent = (acc_ref[...] / sum_ref[...]).astype(jnp.bfloat16)
    parts = [
        jnp.dot(
            latent[head * tok : (head + 1) * tok], wv_ref[head], preferred_element_type=jnp.float32
        ).astype(jnp.bfloat16)
        for head in range(HEAD_GROUP)
    ]
    wide = HEAD_GROUP * VD
    values_ref[:, pl.ds(pl.multiple_of(group * wide, wide), wide)] = jnp.concatenate(parts, axis=1)

    @pl.when(group == HEADS // HEAD_GROUP - 1)
    def _():
        values = values_ref[...].astype(jnp.float32)
        square = jnp.mean(values * values, axis=1, keepdims=True)
        normed = values * lax.rsqrt(square + NORM_EPS) * gain_ref[...]
        normed_ref[...] = normed.astype(jnp.bfloat16)


def attention(my_index, q_nope, q_rope, keys, w_value, norm_gain):
    tok = q_nope.shape[0]
    total = keys.shape[0]
    key_block = min(KEY_BLOCK, total)
    rows = HEAD_GROUP * tok
    grid_spec = pltpu.PrefetchScalarGridSpec(
        num_scalar_prefetch=1,
        grid=(HEADS // HEAD_GROUP,),
        in_specs=[
            pl.BlockSpec((tok, HEAD_GROUP * LAT), lambda g, i: (0, g)),
            pl.BlockSpec((tok, HEAD_GROUP * ROPE), lambda g, i: (0, g)),
            pl.BlockSpec(keys.shape, lambda g, i: (0, 0)),
            pl.BlockSpec((HEAD_GROUP, LAT, VD), lambda g, i: (g, 0, 0)),
            pl.BlockSpec((1, HEADS * VD), lambda g, i: (0, 0)),
        ],
        out_specs=[
            pl.BlockSpec((tok, HEADS * VD), lambda g, i: (0, 0)),
            pl.BlockSpec((tok, HEADS * VD), lambda g, i: (0, 0)),
        ],
        scratch_shapes=[
            pltpu.VMEM((rows, LAT + 2 * ROPE), jnp.bfloat16),
            pltpu.VMEM((rows, 1), jnp.float32),
            pltpu.VMEM((rows, 1), jnp.float32),
            pltpu.VMEM((rows, LAT), jnp.float32),
        ],
    )
    shape = jax.ShapeDtypeStruct((tok, HEADS * VD), jnp.bfloat16)
    work = HEADS * tok * total
    return pl.pallas_call(
        functools.partial(attention_kernel, tok=tok, key_block=key_block),
        grid_spec=grid_spec,
        out_shape=[shape, shape],
        compiler_params=pltpu.CompilerParams(vmem_limit_bytes=40 << 20),
        cost_estimate=pl.CostEstimate(
            flops=2 * work * (2 * LAT + 2 * ROPE), bytes_accessed=8 << 20, transcendentals=work
        ),
    )(my_index.reshape(1), q_nope, q_rope, keys, w_value, norm_gain.reshape(1, HEADS * VD))


def local(
    q_nope, q_rope, c_kv, k_rope, w_value, norm_gain, expert_ids, gate_fixed, w_gate, w_up, w_down
):
    tok = c_kv.shape[0]
    n_ctx = lax.axis_size("ctx")
    chips = n_ctx // CORES
    my_index = lax.axis_index("ctx")
    my_expert = my_index // SPAN
    same_core = [[chip * CORES + core for chip in range(chips)] for core in range(CORES)]
    siblings = [(i, i ^ 1) for i in range(n_ctx)]

    keys = jnp.concatenate([c_kv, k_rope, k_rope], axis=1)
    keys = lax.all_gather(keys, "ctx", axis=0, tiled=True)
    row_ids = lax.all_gather(expert_ids, "ctx", axis=0, tiled=True, axis_index_groups=same_core)
    other_gate, other_up, other_down = (
        lax.ppermute(w, "ctx", siblings) for w in (w_gate[0], w_up[0], w_down[0])
    )

    values, normed = attention(my_index, q_nope, q_rope, keys, w_value, norm_gain)

    rows = lax.all_gather(normed, "ctx", axis=0, tiled=True, axis_index_groups=same_core)

    def hidden_of(gate_w, up_w):
        gate_act = jnp.dot(rows, gate_w, preferred_element_type=jnp.float32)
        up_act = jnp.dot(rows, up_w, preferred_element_type=jnp.float32)
        act = jax.nn.silu(gate_act) * up_act
        return jnp.where(row_ids == my_expert, act, 0.0).astype(jnp.bfloat16)

    part = jnp.dot(hidden_of(w_gate[0], w_up[0]), w_down[0], preferred_element_type=jnp.float32)
    part = part + jnp.dot(
        hidden_of(other_gate, other_up), other_down, preferred_element_type=jnp.float32
    )
    expert_out = lax.psum_scatter(
        part.astype(jnp.bfloat16), "ctx", scatter_dimension=0, tiled=True,
        axis_index_groups=same_core,
    )
    gate_weight = gate_fixed.astype(jnp.float32) / 65536.0
    mixed = values.astype(jnp.float32) + gate_weight * expert_out.astype(jnp.float32)
    return mixed.astype(jnp.bfloat16)


def solution(mesh):
    in_specs = (
        P(("rep", "ctx"), None),
        P(("rep", "ctx"), None),
        P(("rep", "ctx"), None),
        P(("rep", "ctx"), None),
        P(),
        P(),
        P(("rep", "ctx"), None),
        P(("rep", "ctx"), None),
        P("ctx", None, None),
        P("ctx", None, None),
        P("ctx", None, None),
    )
    out_specs = P(("rep", "ctx"), None)
    return jax.shard_map(local, mesh=mesh, in_specs=in_specs, out_specs=out_specs, check_vma=False)
```

time: 654 us -> 272 us (0.42)
  the two profiles are of different devices: /device:TPU:13 before, /device:TPU:0 now
where the time goes in v1:
time: 272 us
  waiting for transfers between devices  188 us (69%)
  matrix products  30.9 us (11%)
  blocking collectives  16.4 us (6%)
  between operations  13.8 us (5%)
  Pallas kernels  9.49 us (3%)
  local copies, waits for them, and re-layouts  8.14 us (3%)
  other arithmetic  3.66 us (1%)
    reduce_scatter x1, waiting for transfers between devices, local(): lax.psum_scatter(part.astype(jnp.bfloat16), 'ctx', scatter_dimension=0, t...  85.7 us
    all_gather x1, waiting for transfers between devices, local(): lax.all_gather(normed, 'ctx', axis=0, tiled=True, axis_index_groups=same_...  59.7 us
    all_gather x1, waiting for transfers between devices, local(): keys = lax.all_gather(keys, 'ctx', axis=0, tiled=True)  43 us
    unnamed x1, blocking collectives  16.4 us
    dot_general x1, matrix products, local(): jnp.dot(hidden_of(other_gate, other_up), other_down, preferred_element_ty...  12.2 us
    dot_general x1, matrix products, local(): jnp.dot(hidden_of(w_gate[0], w_up[0]), w_down[0], preferred_element_type=...  10.7 us
    pallas_call x1, Pallas kernels, attention(): pl.pallas_call(functools.partial(attention_kernel, tok=tok, key_block=key...  9.49 us
    unnamed x23, local copies, waits for them, and re-layouts  8.14 us
  transfers between devices with their start and end apart: 6, of which 3 were waited for; matrix products, arithmetic and copies ran while one was open for 7% of the time, Pallas kernels for 0%

profile of v1, /device:TPU:0, one launch (start us, length us, event | category | flops | bytes accessed | tf_op | source)
XLA Modules:
  0.0 271.7 jit_solution(11109150198986375711)
XLA Ops:
  6.5 0.0 all-gather.3.cloned.1.call-start
  6.5 1.6 pad_maximum_fusion
  8.1 0.0 all-gather.3.cloned.1.call-update
  8.2 0.0 all-gather.5.cloned.1.call-start
  8.2 43.0 %all-gather.3.cloned.1.call-done.keys_ref = bf16[1024,640]{1,0:T(8,128)(2,1)} async-done(((bf16[64,640]{1,0:T(8,128)(2,1)}), bf16[1024,640]{1,0:T(8,128)(2,1)}) %all-gather.3.cloned.1.call-update) | async-done | bytes 1310736 | tf_op jit(solution)/shard_map/all_gather | solution.py:136
  51.2 2.2 copy-done
  53.4 1.6 copy-done.1
  55.0 1.3 copy-done.2
  56.3 0.9 copy-done.3
  57.2 0.7 copy-done.4
  57.9 9.5 %shard_map.109 = (bf16[64,4096]{1,0:T(8,128)(2,1)S(1)}, bf16[64,4096]{1,0:T(8,128)(2,1)}) custom-call(s32[1]{0:T(128)} %bitcast.index_ref, bf16[64,16384]{1,0:T(8,128)(2,1)S(1)} %copy-done.1, bf16[64,2048]{1,0:T(8,128)(2,1)S(1)} %copy-done.3, bf16[1024,640]{1,0:T(8,128)(2,1)S(1)} %copy-done.2, bf16[32,512,128]{2,1,0:T(8,128)(2,1)S(1)} %copy-done, ...), custom_call_target="tpu_custom_call" | custom-call | flops 4831838208 | bytes 8388608 | tf_op jit(solution)/shard_map/pallas_call | solution.py:113
  67.4 0.0 all-gather.5.cloned.1.call-update
  67.5 0.0 reduce-scatter.2.cloned.1.call-start
  67.5 0.3 collective-permute-start
  67.8 0.0 copy-done.6
  67.8 0.2 collective-permute-start.1
  68.1 0.3 collective-permute-start.2
  68.4 0.6 dynamic-slice
  69.6 0.1 bitcast_dynamic-update-slice_fusion
  69.7 16.4 %all-reduce = s32[512]{0:T(512)S(1)} all-reduce(s32[512]{0:T(512)S(1)} %bitcast_dynamic-update-slice_fusion), channel_id=1, replica_groups={{0,2,4,6,8,10,12,14},{1,3,5,7,9,11,13,15},{16,18,20,22,24,26,28,30},{17..., use_global_device_ids=true, to_apply=%add | all-reduce | flops 512 | bytes 4096
  86.2 59.7 %all-gather.5.cloned.1.call-done = bf16[512,4096]{1,0:T(8,128)(2,1)} async-done(((bf16[64,4096]{1,0:T(8,128)(2,1)}), bf16[512,4096]{1,0:T(8,128)(2,1)}) %all-gather.5.cloned.1.call-update) | async-done | bytes 4194320 | tf_op jit(solution)/shard_map/all_gather | solution.py:144
  145.9 5.0 %fusion.17 = f32[512,256]{1,0:T(8,128)} fusion(bf16[512,4096]{1,0:T(8,128)(2,1)} %all-gather.5.cloned.1.call-done, bf16[1,4096,256]{2,1,0:T(8,128)(2,1)} %param.19), kind=kOutput, calls=%fused_computation.24 | convolution fusion | flops 1073741824 | bytes 6815744 | tf_op jit(solution)/shard_map/dot_general | solution.py:147
  150.9 0.0 collective-permute-done
  150.9 2.9 %fusion.25 = f32[512,256]{1,0:T(8,128)S(1)} fusion(bf16[512,4096]{1,0:T(8,128)(2,1)S(1)} %copy-done.5, bf16[4096,256]{1,0:T(8,128)(2,1)} %collective-permute-done), kind=kOutput, calls=%fused_computation.31 | convolution fusion | flops 1073741824 | bytes 6815744 | tf_op jit(solution)/shard_map/dot_general | solution.py:147
  153.8 10.7 %fusion.2 = f32[512,4096]{1,0:T(8,128)} fusion(bf16[512,4096]{1,0:T(8,128)(2,1)} %all-gather.5.cloned.1.call-done, f32[512,256]{1,0:T(8,128)} %fusion.17, pred[512]{0:T(512)(128)(4,1)S(1)} %broadcast_compare_fusion, bf16[1,256,4096]{2,1,0:T(8,128)(2,1)} %param.21, bf16[1,4096,256]{2,1,0:T(8,128)(2,1)S(1)} %copy-done.6), kind=kOutput, calls=%fused_computation.4 | convolution fusion | flops 2148401152 | bytes 17302016 | tf_op jit(solution)/shard_map/dot_general | solution.py:152
  164.6 0.0 collective-permute-done.1
  164.6 0.0 collective-permute-done.2
  164.6 12.2 %add_convert_fusion = bf16[512,4096]{1,0:T(8,128)(2,1)} fusion(f32[512,4096]{1,0:T(8,128)} %fusion.2, bf16[256,4096]{1,0:T(8,128)(2,1)} %collective-permute-done.2, f32[512,256]{1,0:T(8,128)S(1)} %fusion.25, pred[512]{0:T(512)(128)(4,1)S(1)} %broadcast_compare_fusion, bf16[512,4096]{1,0:T(8,128)(2,1)} %all-gather.5.cloned.1.call-done, ...), kind=kOutput, calls=%fused_computation | convolution fusion | flops 2152595456 | bytes 21496320 | tf_op jit(solution)/shard_map/dot_general | solution.py:153
  176.8 0.0 reduce-scatter.2.cloned.1.call-update
  176.8 0.6 copy-done.8
  177.5 85.7 %reduce-scatter.2.cloned.1.call-done = bf16[64,4096]{1,0:T(8,128)(2,1)} async-done(((bf16[512,4096]{1,0:T(8,128)(2,1)}), bf16[64,4096]{1,0:T(8,128)(2,1)}) %reduce-scatter.2.cloned.1.call-update) | async-done | bytes 524304 | tf_op jit(solution)/shard_map/reduce_scatter | solution.py:156
  263.1 2.1 add_convert_fusion.1
  (16 shorter events, 0.0 us)
Async XLA Ops:
  6.5 44.6 %all-gather.3.cloned.1.call-start = ((), (), s32[]{:S(2)}) async-start(), calls=%async_computation.1 | async-start | bytes 1392640 | tf_op jit(solution)/shard_map/all_gather | solution.py:136
  8.2 137.7 %all-gather.5.cloned.1.call-start = ((), (), s32[]{:S(2)}) async-start(), calls=%async_computation.2 | async-start | bytes 4718592 | tf_op jit(solution)/shard_map/all_gather | solution.py:144
  51.2 2.2 copy-start
  53.4 1.6 copy-start.1
  55.0 1.3 copy-start.2
  56.3 0.9 copy-start.3
  57.2 0.7 copy-start.4
  57.9 9.9 %copy-start.6 = (bf16[1,4096,256]{2,1,0:T(8,128)(2,1)S(1)}, bf16[1,4096,256]{2,1,0:T(8,128)(2,1)}, u32[]{:S(2)}) copy-start(bf16[1,4096,256]{2,1,0:T(8,128)(2,1)} %param.20) | copy-start | bytes 6291460
  57.9 10.4 %copy-start.9 = (u32[32]{0:T(128)S(1)}, u32[32]{0:T(128)}, u32[]{:S(2)}) copy-start(u32[32]{0:T(128)} %constant.34) | copy-start | bytes 388
  57.9 11.7 %copy-start.7 = (s32[64,1]{0,1:T(1,128)S(1)}, s32[64,1]{0,1:T(1,128)}, u32[]{:S(2)}) copy-start(s32[64,1]{0,1:T(1,128)} %param.17) | copy-start | bytes 772
  67.5 195.7 %reduce-scatter.2.cloned.1.call-start = ((), (), s32[]{:S(2)}) async-start(), calls=%async_computation.3 | async-start | bytes 4718592 | tf_op jit(solution)/shard_map/reduce_scatter | solution.py:156
  67.5 83.4 %collective-permute-start = (bf16[4096,256]{1,0:T(8,128)(2,1)}, bf16[4096,256]{1,0:T(8,128)(2,1)}, u32[]{:S(2)}, u32[]{:S(2)}) collective-permute-start(bf16[4096,256]{1,0:T(8,128)(2,1)} %bitcast.27), channel_id=1, source_target_pairs={{0,1},{1,0},{2,3},{3,2},{4,5},{5,4},{6,7},{7,6},{8,9},{9,8},{10,11... | collective-permute-start | bytes 6291464 | tf_op jit(solution)/shard_map/ppermute | solution.py:139
  67.8 96.7 %collective-permute-start.1 = (bf16[4096,256]{1,0:T(8,128)(2,1)S(1)}, bf16[4096,256]{1,0:T(8,128)(2,1)}, u32[]{:S(2)}, u32[]{:S(2)}) collective-permute-start(bf16[4096,256]{1,0:T(8,128)(2,1)S(1)} %bitcast.25), channel_id=1, source_target_pairs={{0,1},{1,0},{2,3},{3,2},{4,5},{5,4},{6,7},{7,6},{8,9},{9,8},{10,11... | collective-permute-start | bytes 6291464 | tf_op jit(solution)/shard_map/ppermute | solution.py:139
  68.1 96.5 %collective-permute-start.2 = (bf16[256,4096]{1,0:T(8,128)(2,1)}, bf16[256,4096]{1,0:T(8,128)(2,1)}, u32[]{:S(2)}, u32[]{:S(2)}) collective-permute-start(bf16[256,4096]{1,0:T(8,128)(2,1)} %bitcast.26), channel_id=1, source_target_pairs={{0,1},{1,0},{2,3},{3,2},{4,5},{5,4},{6,7},{7,6},{8,9},{9,8},{10,11... | collective-permute-start | bytes 6291464 | tf_op jit(solution)/shard_map/ppermute | solution.py:139
  145.9 5.1 %copy-start.5 = (bf16[512,4096]{1,0:T(8,128)(2,1)S(1)}, bf16[512,4096]{1,0:T(8,128)(2,1)}, u32[]{:S(2)}) copy-start(bf16[512,4096]{1,0:T(8,128)(2,1)} %all-gather.5.cloned.1.call-done) | copy-start | bytes 12582916
  176.8 0.7 copy-start.8
Sparse Core Ops, SparseCore 0:
  9.6 41.4 all-gather.2
  67.6 78.2 all-gather.4
  177.0 86.1 reduce-scatter.1

commit v2 on v1

v2 whole, which is shorter than its diff:
```python
import functools

import jax
import jax.numpy as jnp
from jax import lax
from jax.experimental import pallas as pl
from jax.experimental.pallas import tpu as pltpu
from jax.sharding import PartitionSpec as P

HEADS = 32
LAT = 512
ROPE = 64
VD = 128
SPAN = 8
CORES = 2

SCORE_SCALE = 192.0 ** (-0.5)
NORM_EPS = 1e-06
NEG_FILL = -1e30

HEAD_GROUP = 8
CHIP_BLOCK = 4


def attention_kernel(
    index_ref, q_ref, qr_ref, mine_ref, other_ref, wv_ref, gain_ref, values_ref, normed_ref,
    stack_ref, max_ref, sum_ref, acc_ref, *, tok, chip_block,
):
    group = pl.program_id(0)
    my_index = index_ref[0]
    my_chip, my_core = my_index // CORES, lax.rem(my_index, CORES)
    rows = HEAD_GROUP * tok
    part = chip_block * tok
    lane = lax.broadcasted_iota(jnp.int32, (tok, 2 * ROPE), 1)
    for head in range(HEAD_GROUP):
        at = pl.ds(head * tok, tok)
        stack_ref[at, 0:LAT] = q_ref[:, head * LAT : (head + 1) * LAT]
        pair = qr_ref[:, (head // 2) * 2 * ROPE : (head // 2 + 1) * 2 * ROPE]
        if head % 2:
            pair = jnp.concatenate([pair[:, ROPE:], pair[:, :ROPE]], axis=1)
        stack_ref[at, LAT : LAT + 2 * ROPE] = jnp.where(lane < ROPE, pair, jnp.zeros_like(pair))
    max_ref[...] = jnp.full_like(max_ref, NEG_FILL)
    sum_ref[...] = jnp.zeros_like(sum_ref)
    acc_ref[...] = jnp.zeros_like(acc_ref)
    row_tok = lax.rem(lax.broadcasted_iota(jnp.int32, (rows, part), 0), jnp.int32(tok))
    key_iota = lax.broadcasted_iota(jnp.int32, (rows, part), 1)
    key_chip, key_tok = key_iota // tok, lax.rem(key_iota, jnp.int32(tok))

    def scores_of(keys, core, first_chip):
        scores = lax.dot_general(
            stack_ref[...], keys, (((1,), (1,)), ((), ())), preferred_element_type=jnp.float32
        )
        key_pos = ((key_chip + first_chip) * CORES + core) * tok + key_tok
        return jnp.where(key_pos <= row_tok + my_index * tok, scores * SCORE_SCALE, NEG_FILL)

    def step(block, carry):
        start = pl.multiple_of(block * part, part)
        mine, other = mine_ref[pl.ds(start, part), :], other_ref[pl.ds(start, part), :]
        scores_a = scores_of(mine, my_core, block * chip_block)
        scores_b = scores_of(other, 1 - my_core, block * chip_block)
        old_max = max_ref[...]
        new_max = jnp.maximum(
            old_max, jnp.max(jnp.maximum(scores_a, scores_b), axis=1, keepdims=True)
        )
        weights_a = jnp.exp(scores_a - new_max)
        weights_b = jnp.exp(scores_b - new_max)
        rescale = jnp.exp(old_max - new_max)
        max_ref[...] = new_max
        sum_ref[...] = sum_ref[...] * rescale + jnp.sum(
            weights_a + weights_b, axis=1, keepdims=True
        )
        mixed = jnp.dot(
            weights_a.astype(jnp.bfloat16), mine[:, 0:LAT], preferred_element_type=jnp.float32
        ) + jnp.dot(
            weights_b.astype(jnp.bfloat16), other[:, 0:LAT], preferred_element_type=jnp.float32
        )
        acc_ref[...] = acc_ref[...] * rescale + mixed
        return carry

    lax.fori_loop(0, my_chip // chip_block + 1, step, 0)
    latent = (acc_ref[...] / sum_ref[...]).astype(jnp.bfloat16)
    parts = [
        jnp.dot(
            latent[head * tok : (head + 1) * tok], wv_ref[head], preferred_element_type=jnp.float32
        ).astype(jnp.bfloat16)
        for head in range(HEAD_GROUP)
    ]
    wide = HEAD_GROUP * VD
    values_ref[:, pl.ds(pl.multiple_of(group * wide, wide), wide)] = jnp.concatenate(parts, axis=1)

    @pl.when(group == HEADS // HEAD_GROUP - 1)
    def _():
        values = values_ref[...].astype(jnp.float32)
        square = jnp.mean(values * values, axis=1, keepdims=True)
        normed = values * lax.rsqrt(square + NORM_EPS) * gain_ref[...]
        normed_ref[...] = normed.astype(jnp.bfloat16)


def attention(my_index, q_nope, q_rope, mine, other, w_value, norm_gain):
    tok = q_nope.shape[0]
    total = mine.shape[0]
    chip_block = min(CHIP_BLOCK, total // tok)
    rows = HEAD_GROUP * tok
    grid_spec = pltpu.PrefetchScalarGridSpec(
        num_scalar_prefetch=1,
        grid=(HEADS // HEAD_GROUP,),
        in_specs=[
            pl.BlockSpec((tok, HEAD_GROUP * LAT), lambda g, i: (0, g)),
            pl.BlockSpec((tok, HEAD_GROUP * ROPE), lambda g, i: (0, g)),
            pl.BlockSpec(mine.shape, lambda g, i: (0, 0)),
            pl.BlockSpec(mine.shape, lambda g, i: (0, 0)),
            pl.BlockSpec((HEAD_GROUP, LAT, VD), lambda g, i: (g, 0, 0)),
            pl.BlockSpec((1, HEADS * VD), lambda g, i: (0, 0)),
        ],
        out_specs=[
            pl.BlockSpec((tok, HEADS * VD), lambda g, i: (0, 0)),
            pl.BlockSpec((tok, HEADS * VD), lambda g, i: (0, 0)),
        ],
        scratch_shapes=[
            pltpu.VMEM((rows, LAT + 2 * ROPE), jnp.bfloat16),
            pltpu.VMEM((rows, 1), jnp.float32),
            pltpu.VMEM((rows, 1), jnp.float32),
            pltpu.VMEM((rows, LAT), jnp.float32),
        ],
    )
    shape = jax.ShapeDtypeStruct((tok, HEADS * VD), jnp.bfloat16)
    work = HEADS * tok * total * CORES
    return pl.pallas_call(
        functools.partial(attention_kernel, tok=tok, chip_block=chip_block),
        grid_spec=grid_spec,
        out_shape=[shape, shape],
        compiler_params=pltpu.CompilerParams(vmem_limit_bytes=56 << 20),
        cost_estimate=pl.CostEstimate(
            flops=2 * work * (2 * LAT + 2 * ROPE), bytes_accessed=8 << 20, transcendentals=work
        ),
    )(my_index.reshape(1), q_nope, q_rope, mine, other, w_value, norm_gain.reshape(1, HEADS * VD))


def expert_kernel(up_rows, down_rows, mask, gate_a, gate_b, up_a, up_b, down_a, down_b, out_a, out_b):
    half = up_rows.shape[0]
    rows = jnp.concatenate([up_rows[...], down_rows[...]], axis=0)
    keep = mask[...] > 0.0

    def hidden(gate_ref, up_ref):
        gate_act = jnp.dot(rows, gate_ref[...], preferred_element_type=jnp.float32)
        up_act = jnp.dot(rows, up_ref[...], preferred_element_type=jnp.float32)
        act = gate_act * (1.0 / (1.0 + jnp.exp(-gate_act))) * up_act
        return jnp.where(keep, act, 0.0).astype(jnp.bfloat16)

    hidden_a, hidden_b = hidden(gate_a, up_a), hidden(gate_b, up_b)
    part = jnp.dot(hidden_a, down_a[...], preferred_element_type=jnp.float32)
    part = part + jnp.dot(hidden_b, down_b[...], preferred_element_type=jnp.float32)
    out_a[...] = part[:half]
    out_b[...] = part[half:]


def expert_part(rows_up, rows_down, mask, weights):
    half, features = rows_up.shape
    units = 2 * weights[0].shape[1]
    shape = jax.ShapeDtypeStruct((half, features), jnp.float32)
    return pl.pallas_call(
        expert_kernel,
        in_specs=[pl.BlockSpec(memory_space=pltpu.VMEM)] * 9,
        out_specs=[pl.BlockSpec(memory_space=pltpu.VMEM)] * 2,
        out_shape=[shape, shape],
        compiler_params=pltpu.CompilerParams(vmem_limit_bytes=24 << 20),
        cost_estimate=pl.CostEstimate(
            flops=12 * half * features * units, bytes_accessed=14 << 20, transcendentals=0
        ),
    )(rows_up, rows_down, mask, *weights)


def local(
    q_nope, q_rope, c_kv, k_rope, w_value, norm_gain, expert_ids, gate_fixed, w_gate, w_up, w_down
):
    tok = c_kv.shape[0]
    half = tok // 2
    n_ctx = lax.axis_size("ctx")
    chips = n_ctx // CORES
    my_index = lax.axis_index("ctx")
    my_chip, my_core = my_index // CORES, my_index % CORES
    my_expert = my_index // SPAN
    same_core = [[chip * CORES + core for chip in range(chips)] for core in range(CORES)]
    siblings = [(i, i ^ 1) for i in range(n_ctx)]
    ring = list(range(0, chips, 2)) + list(range(1, chips, 2))[::-1]
    place = [ring.index(chip) for chip in range(chips)]
    ahead = [
        (ring[p] * CORES + core, ring[(p + 1) % chips] * CORES + core)
        for p in range(chips) for core in range(CORES)
    ]
    behind = [(there, here) for here, there in ahead]

    ids = jnp.broadcast_to(expert_ids.astype(jnp.bfloat16), (tok, ROPE))
    block = jnp.concatenate([c_kv, k_rope, ids], axis=1)
    mine = lax.all_gather(block, "ctx", axis=0, tiled=True, axis_index_groups=same_core)
    other = lax.ppermute(mine, "ctx", siblings)

    own, mine, other = lax.optimization_barrier(((w_gate[0], w_up[0], w_down[0]), mine, other))
    swapped = tuple(lax.ppermute(w, "ctx", siblings) for w in own)
    weights = (own[0], swapped[0], own[1], swapped[1], own[2], swapped[2])

    values, normed = attention(my_index, q_nope, q_rope, mine, other, w_value, norm_gain)

    row_ids = mine[:, LAT + ROPE].reshape(chips, tok)
    hits = (row_ids == my_expert.astype(jnp.bfloat16)).astype(jnp.float32)
    my_place = jnp.asarray(place, jnp.int32)[my_chip]
    hops = jnp.arange(chips, dtype=jnp.int32)
    order = jnp.asarray(ring, jnp.int32)
    from_behind = order[(my_place - hops) % chips]
    from_ahead = order[(my_place + hops) % chips]
    masks = jnp.concatenate([hits[from_behind, :half], hits[from_ahead, half:]], axis=1)
    masks = masks[:, :, None]

    rows_up, rows_down = normed[:half], normed[half:]
    home_up, home_down = expert_part(rows_up, rows_down, masks[0], weights)
    sum_up = sum_down = None
    for hop in range(1, chips):
        rows_up = lax.ppermute(rows_up, "ctx", ahead)
        rows_down = lax.ppermute(rows_down, "ctx", behind)
        part_up, part_down = expert_part(rows_up, rows_down, masks[hop], weights)
        if hop > 1:
            part_up = part_up + sum_up.astype(jnp.float32)
            part_down = part_down + sum_down.astype(jnp.float32)
        sum_up = lax.ppermute(part_up.astype(jnp.bfloat16), "ctx", ahead)
        sum_down = lax.ppermute(part_down.astype(jnp.bfloat16), "ctx", behind)
    expert_out = jnp.concatenate(
        [home_up + sum_up.astype(jnp.float32), home_down + sum_down.astype(jnp.float32)], axis=0
    )
    gate_weight = gate_fixed.astype(jnp.float32) / 65536.0
    return (values.astype(jnp.float32) + gate_weight * expert_out).astype(jnp.bfloat16)


def solution(mesh):
    in_specs = (
        P(("rep", "ctx"), None),
        P(("rep", "ctx"), None),
        P(("rep", "ctx"), None),
        P(("rep", "ctx"), None),
        P(),
        P(),
        P(("rep", "ctx"), None),
        P(("rep", "ctx"), None),
        P("ctx", None, None),
        P("ctx", None, None),
        P("ctx", None, None),
    )
    out_specs = P(("rep", "ctx"), None)
    return jax.shard_map(local, mesh=mesh, in_specs=in_specs, out_specs=out_specs, check_vma=False)
```

time: 272 us -> 227 us (0.83)
  waiting for transfers between devices: 188 us -> 57.6 us
  Pallas kernels: 9.49 us -> 54.4 us
  local copies, waits for them, and re-layouts: 8.14 us -> 43.9 us
  matrix products: 30.9 us -> 0 us
  starting transfers between devices: 0.92 us -> 31.1 us
  blocking collectives: 16.4 us -> 33.4 us
  between operations: 13.8 us -> 0.28 us
    all_gather x2 -> x0, waiting for transfers between devices: 103 us -> none  [the longest x1 59.7 us: local(): lax.all_gather(normed, 'ctx', axis=0, tiled=True, axis_index_groups=same_...]
    reduce_scatter x1 -> x0, waiting for transfers between devices: 85.7 us -> none  [local(): lax.psum_scatter(part.astype(jnp.bfloat16), 'ctx', scatter_dimension=0, t...]
    ppermute x3 -> x32, waiting for transfers between devices: 0.01 us -> 57.6 us  [the longest x7 33.4 us: local(): sum_down = lax.ppermute(part_down.astype(jnp.bfloat16), 'ctx', behind)]
    pallas_call x1 -> x9, Pallas kernels: 9.49 us -> 54.4 us  [the longest x8 42.7 us: expert_part(): pl.pallas_call(expert_kernel, in_specs=[pl.BlockSpec(memory_space=pltpu.V...]
    all_gather x0 -> x1, blocking collectives: none -> 33.4 us  [local(): lax.all_gather(block, 'ctx', axis=0, tiled=True, axis_index_groups=same_c...]
    gather x0 -> x66, local copies, waits for them, and re-layouts: none -> 33.3 us
    dot_general x4 -> x0, matrix products: 30.9 us -> none  [the longest x1 12.2 us: local(): jnp.dot(hidden_of(other_gate, other_up), other_down, preferred_element_ty...]
    ppermute x3 -> x32, starting transfers between devices: 0.84 us -> 31.1 us  [the longest x7 10.8 us: local(): rows_down = lax.ppermute(rows_down, 'ctx', behind)]
  transfers between devices with their start and end apart: 6 -> 32, of which waited for: 3 -> 15; matrix products, arithmetic and copies ran while one was open for 7% -> 18% of each run, Pallas kernels for 0% -> 19%
where the time goes in v2:
time: 227 us; the launch traced here: 226 us
  waiting for transfers between devices  57.6 us (25%)
  Pallas kernels  54.4 us (24%)
  local copies, waits for them, and re-layouts  43.9 us (19%)
  blocking collectives  33.4 us (15%)
  starting transfers between devices  31.1 us (14%)
  other arithmetic  5.17 us (2%)
    pallas_call x8, Pallas kernels, expert_part(): pl.pallas_call(expert_kernel, in_specs=[pl.BlockSpec(memory_space=pltpu.V...  42.7 us
    ppermute x7, waiting for transfers between devices, local(): sum_down = lax.ppermute(part_down.astype(jnp.bfloat16), 'ctx', behind)  33.4 us
    all_gather x1, blocking collectives, local(): lax.all_gather(block, 'ctx', axis=0, tiled=True, axis_index_groups=same_c...  33.4 us
    gather x64, local copies, waits for them, and re-layouts  32 us
    ppermute x7, waiting for transfers between devices, local(): rows_down = lax.ppermute(rows_down, 'ctx', behind)  18.7 us
    pallas_call x1, Pallas kernels, attention(): pl.pallas_call(functools.partial(attention_kernel, tok=tok, chip_block=ch...  11.7 us
    ppermute x7, starting transfers between devices, local(): rows_down = lax.ppermute(rows_down, 'ctx', behind)  10.8 us
    ppermute x7, starting transfers between devices, local(): sum_down = lax.ppermute(part_down.astype(jnp.bfloat16), 'ctx', behind)  9.26 us
  transfers between devices with their start and end apart: 32, of which 15 were waited for; matrix products, arithmetic and copies ran while one was open for 18% of the time, Pallas kernels for 19%

profile of v2, /device:TPU:0, one launch (start us, length us, event | category | flops | bytes accessed | tf_op | source)
XLA Modules:
  0.0 225.9 jit_solution(12724992626084284906)
XLA Ops:
  1.7 33.4 %all_gather.3.mine_ref = bf16[512,640]{1,0:T(8,128)(2,1)S(1)} all-gather(bf16[64,640]{1,0:T(8,128)(2,1)S(1)} %pad_maximum_fusion), channel_id=1, replica_groups={{0,2,4,6,8,10,12,14},{1,3,5,7,9,11,13,15},{16,18,20,22,24,26,28,30},{17..., dimensions={0}, use_global_device_ids=true | all-gather | bytes 737280 | tf_op jit(solution)/shard_map/all_gather | solution.py:195
  38.0 11.7 %shard_map.127 = (bf16[64,4096]{1,0:T(8,128)(2,1)}, bf16[64,4096]{1,0:T(8,128)(2,1)}) custom-call(s32[1]{0:T(128)} %bitcast.index_ref, bf16[64,16384]{1,0:T(8,128)(2,1)} %q_ref.1, bf16[64,2048]{1,0:T(8,128)(2,1)} %qr_ref.1, bf16[512,640]{1,0:T(8,128)(2,1)} %copy-done.8, bf16[512,640]{1,0:T(8,128)(2,1)} %copy-done.10, bf16[32,512,128]{2,1,0:T(8,128)(2,1)} %wv_ref.1, ...), custom_call_target="tpu_custom_call" | custom-call | flops 4831838208 | bytes 8388608 | tf_op jit(solution)/shard_map/pallas_call | solution.py:128
  50.9 1.7 collective-permute-start.11
  53.6 5.8 %collective-permute-done.11.down_rows = bf16[32,4096]{1,0:T(8,128)(2,1)S(1)} collective-permute-done((bf16[32,4096]{1,0:T(8,128)(2,1)S(1)}, bf16[32,4096]{1,0:T(8,128)(2,1)S(1)}, u32[]{:S(2)}, u32[]{:S(2)}) %collective-permute-start.11) | collective-permute-done | bytes 262176 | tf_op jit(solution)/shard_map/ppermute | solution.py:219
  59.5 1.7 collective-permute-start.12
  63.0 5.6 %collective-permute-done.12.down_rows = bf16[32,4096]{1,0:T(8,128)(2,1)S(1)} collective-permute-done((bf16[32,4096]{1,0:T(8,128)(2,1)S(1)}, bf16[32,4096]{1,0:T(8,128)(2,1)S(1)}, u32[]{:S(2)}, u32[]{:S(2)}) %collective-permute-start.12) | collective-permute-done | bytes 262176 | tf_op jit(solution)/shard_map/ppermute | solution.py:219
  68.7 2.7 %collective-permute-start.13 = (bf16[32,4096]{1,0:T(8,128)(2,1)S(1)}, bf16[32,4096]{1,0:T(8,128)(2,1)}, u32[]{:S(2)}, u32[]{:S(2)}) collective-permute-start(bf16[32,4096]{1,0:T(8,128)(2,1)S(1)} %collective-permute-done.12.down_rows), channel_id=1, source_target_pairs={{4,0},{5,1},{8,4},{9,5},{12,8},{13,9},{14,12},{15,13},{10,14},{11,... | collective-permute-start | bytes 786440 | tf_op jit(solution)/shard_map/ppermute | solution.py:219
  73.9 3.8 %collective-permute-done.13.down_rows = bf16[32,4096]{1,0:T(8,128)(2,1)} collective-permute-done((bf16[32,4096]{1,0:T(8,128)(2,1)S(1)}, bf16[32,4096]{1,0:T(8,128)(2,1)}, u32[]{:S(2)}, u32[]{:S(2)}) %collective-permute-start.13) | collective-permute-done | bytes 262176 | tf_op jit(solution)/shard_map/ppermute | solution.py:219
  78.7 2.7 %collective-permute-done.6.up_rows = bf16[32,4096]{1,0:T(8,128)(2,1)} collective-permute-done((bf16[32,4096]{1,0:T(8,128)(2,1)}, bf16[32,4096]{1,0:T(8,128)(2,1)}, u32[]{:S(2)}, u32[]{:S(2)}) %collective-permute-start.6) | collective-permute-done | bytes 262176 | tf_op jit(solution)/shard_map/ppermute | solution.py:218
  82.0 15.5 %while.3 = (s32[]{:T(128)}, f32[8,64]{1,0:T(8,128)S(1)}, s32[8,2]{0,1:T(2,128)S(1)}, f32[8,32]{1,0:T(8,128)S(1)}, s32[]{:T(128)}, /*index=5*/s32[]{:T(128)}) while((s32[]{:T(128)}, f32[8,64]{1,0:T(8,128)S(1)}, s32[8,2]{0,1:T(2,128)S(1)}, f32[8,32]{1,0:T(8,128)S(1)}, s32[]{:T(128)}, /*index=5*/s32[]{:T(128)}) %tuple.44), condition=%wide.while_cond.1, body=%wide.while_body.1.sunk | while | flops 2 | bytes 633 | solution.py:211
  100.3 16.5 %while.2 = (s32[]{:T(128)}, f32[8,64]{1,0:T(8,128)S(1)}, s32[8,2]{0,1:T(2,128)S(1)}, f32[8,32]{1,0:T(8,128)S(1)}, s32[]{:T(128)}, /*index=5*/s32[]{:T(128)}) while((s32[]{:T(128)}, f32[8,64]{1,0:T(8,128)S(1)}, s32[8,2]{0,1:T(2,128)S(1)}, f32[8,32]{1,0:T(8,128)S(1)}, s32[]{:T(128)}, /*index=5*/s32[]{:T(128)}) %tuple.50), condition=%wide.while_cond, body=%wide.while_body.sunk | while | flops 2 | bytes 633 | solution.py:211
  109.2 1.4 dynamic-slice.13
  122.2 3.4 %collective-permute-done.16.down_rows = bf16[32,4096]{1,0:T(8,128)(2,1)} collective-permute-done((bf16[32,4096]{1,0:T(8,128)(2,1)}, bf16[32,4096]{1,0:T(8,128)(2,1)}, u32[]{:S(2)}, u32[]{:S(2)}) %collective-permute-start.16) | collective-permute-done | bytes 262176 | tf_op jit(solution)/shard_map/ppermute | solution.py:219
  127.7 1.6 copy-done.1
  129.2 1.6 copy-done.2
  131.6 5.2 %shard_map.135 = (f32[32,4096]{1,0:T(8,128)S(1)}, f32[32,4096]{1,0:T(8,128)S(1)}) custom-call(bf16[32,4096]{1,0:T(8,128)(2,1)S(1)} %collective-permute-done.4.up_rows, bf16[32,4096]{1,0:T(8,128)(2,1)S(1)} %collective-permute-done.11.down_rows, f32[64,1]{1,0:T(8,128)S(1)} %copy-done.6, bf16[4096,256]{1,0:T(8,128)(2,1)S(1)} %bitcast.47, ...), custom_call_target="tpu_custom_call" | custom-call | flops 805306368 | bytes 14680064 | tf_op jit(solution)/shard_map/pallas_call | solution.py:161
  139.0 5.3 %shard_map.134 = (f32[32,4096]{1,0:T(8,128)S(1)}, f32[32,4096]{1,0:T(8,128)S(1)}) custom-call(bf16[32,4096]{1,0:T(8,128)(2,1)} %collective-permute-done.5.up_rows, bf16[32,4096]{1,0:T(8,128)(2,1)S(1)} %collective-permute-done.12.down_rows, f32[64,1]{1,0:T(8,128)S(1)} %copy-done.5, bf16[4096,256]{1,0:T(8,128)(2,1)S(1)} %bitcast.48, ...), custom_call_target="tpu_custom_call" | custom-call | flops 805306368 | bytes 14680064 | tf_op jit(solution)/shard_map/pallas_call | solution.py:161
  144.4 5.4 %shard_map.133 = (f32[32,4096]{1,0:T(8,128)S(1)}, f32[32,4096]{1,0:T(8,128)S(1)}) custom-call(bf16[32,4096]{1,0:T(8,128)(2,1)} %collective-permute-done.6.up_rows, bf16[32,4096]{1,0:T(8,128)(2,1)} %collective-permute-done.13.down_rows, f32[64,1]{1,0:T(8,128)S(1)} %copy-done.4, bf16[4096,256]{1,0:T(8,128)(2,1)S(1)} %bitcast.49, ...), custom_call_target="tpu_custom_call" | custom-call | flops 805306368 | bytes 14680064 | tf_op jit(solution)/shard_map/pallas_call | solution.py:161
  149.8 5.4 %shard_map.132 = (f32[32,4096]{1,0:T(8,128)S(1)}, f32[32,4096]{1,0:T(8,128)S(1)}) custom-call(bf16[32,4096]{1,0:T(8,128)(2,1)} %collective-permute-done.7.up_rows, bf16[32,4096]{1,0:T(8,128)(2,1)} %collective-permute-done.14.down_rows, f32[64,1]{1,0:T(8,128)S(1)} %copy-done.3, bf16[4096,256]{1,0:T(8,128)(2,1)S(1)} %bitcast.50, ...), custom_call_target="tpu_custom_call" | custom-call | flops 805306368 | bytes 14680064 | tf_op jit(solution)/shard_map/pallas_call | solution.py:161
  155.2 5.4 %shard_map.131 = (f32[32,4096]{1,0:T(8,128)S(1)}, f32[32,4096]{1,0:T(8,128)S(1)}) custom-call(bf16[32,4096]{1,0:T(8,128)(2,1)} %collective-permute-done.8.up_rows, bf16[32,4096]{1,0:T(8,128)(2,1)} %collective-permute-done.15.down_rows, f32[64,1]{1,0:T(8,128)S(1)} %copy.25.mask, bf16[4096,256]{1,0:T(8,128)(2,1)S(1)} %bitcast.51, ...), custom_call_target="tpu_custom_call" | custom-call | flops 805306368 | bytes 14680064 | tf_op jit(solution)/shard_map/pallas_call | solution.py:161
  160.6 5.4 %shard_map.130 = (f32[32,4096]{1,0:T(8,128)S(1)}, f32[32,4096]{1,0:T(8,128)S(1)}) custom-call(bf16[32,4096]{1,0:T(8,128)(2,1)} %collective-permute-done.9.up_rows, bf16[32,4096]{1,0:T(8,128)(2,1)} %collective-permute-done.16.down_rows, f32[64,1]{1,0:T(8,128)S(1)} %copy.24.mask, bf16[4096,256]{1,0:T(8,128)(2,1)S(1)} %bitcast.52, ...), custom_call_target="tpu_custom_call" | custom-call | flops 805306368 | bytes 14680064 | tf_op jit(solution)/shard_map/pallas_call | solution.py:161
  166.0 5.2 %shard_map.128 = (f32[32,4096]{1,0:T(8,128)S(1)}, f32[32,4096]{1,0:T(8,128)S(1)}) custom-call(bf16[32,4096]{1,0:T(8,128)(2,1)S(1)} %get-tuple-element.88.up_rows, bf16[32,4096]{1,0:T(8,128)(2,1)S(1)} %get-tuple-element.87.down_rows, f32[64,1]{1,0:T(8,128)S(1)} %copy.22.mask, bf16[4096,256]{1,0:T(8,128)(2,1)S(1)} %bitcast.53, ...), custom_call_target="tpu_custom_call" | custom-call | flops 805306368 | bytes 14680064 | tf_op jit(solution)/shard_map/pallas_call | solution.py:161
  171.3 5.2 %shard_map.129 = (f32[32,4096]{1,0:T(8,128)S(1)}, f32[32,4096]{1,0:T(8,128)S(1)}) custom-call(bf16[32,4096]{1,0:T(8,128)(2,1)S(1)} %collective-permute-done.10.up_rows, bf16[32,4096]{1,0:T(8,128)(2,1)S(1)} %collective-permute-done.17.down_rows, f32[64,1]{1,0:T(8,128)S(1)} %copy.23.mask, bf16[4096,256]{1,0:T(8,128)(2,1)S(1)} %bitcast.54, ...), custom_call_target="tpu_custom_call" | custom-call | flops 805306368 | bytes 14680064 | tf_op jit(solution)/shard_map/pallas_call | solution.py:161
  178.8 4.5 %collective-permute-done.26 = bf16[32,4096]{1,0:T(8,128)(2,1)S(1)} collective-permute-done((bf16[32,4096]{1,0:T(8,128)(2,1)S(1)}, bf16[32,4096]{1,0:T(8,128)(2,1)S(1)}, u32[]{:S(2)}, u32[]{:S(2)}) %collective-permute-start.26) | collective-permute-done | bytes 262176 | tf_op jit(solution)/shard_map/ppermute | solution.py:225
  185.6 5.6 %collective-permute-done.27 = bf16[32,4096]{1,0:T(8,128)(2,1)S(1)} collective-permute-done((bf16[32,4096]{1,0:T(8,128)(2,1)S(1)}, bf16[32,4096]{1,0:T(8,128)(2,1)S(1)}, u32[]{:S(2)}, u32[]{:S(2)}) %collective-permute-start.27) | collective-permute-done | bytes 262176 | tf_op jit(solution)/shard_map/ppermute | solution.py:225
  191.2 1.6 collective-permute-start.28
  193.4 6.6 %collective-permute-done.28 = bf16[32,4096]{1,0:T(8,128)(2,1)S(1)} collective-permute-done((bf16[32,4096]{1,0:T(8,128)(2,1)S(1)}, bf16[32,4096]{1,0:T(8,128)(2,1)S(1)}, u32[]{:S(2)}, u32[]{:S(2)}) %collective-permute-start.28) | collective-permute-done | bytes 262176 | tf_op jit(solution)/shard_map/ppermute | solution.py:225
  200.1 1.6 collective-permute-start.29
  202.4 6.6 %collective-permute-done.29 = bf16[32,4096]{1,0:T(8,128)(2,1)S(1)} collective-permute-done((bf16[32,4096]{1,0:T(8,128)(2,1)S(1)}, bf16[32,4096]{1,0:T(8,128)(2,1)S(1)}, u32[]{:S(2)}, u32[]{:S(2)}) %collective-permute-start.29) | collective-permute-done | bytes 262176 | tf_op jit(solution)/shard_map/ppermute | solution.py:225
  209.0 1.4 collective-permute-start.30
  211.2 5.9 %collective-permute-done.30 = bf16[32,4096]{1,0:T(8,128)(2,1)S(1)} collective-permute-done((bf16[32,4096]{1,0:T(8,128)(2,1)S(1)}, bf16[32,4096]{1,0:T(8,128)(2,1)S(1)}, u32[]{:S(2)}, u32[]{:S(2)}) %collective-permute-start.30) | collective-permute-done | bytes 262176 | tf_op jit(solution)/shard_map/ppermute | solution.py:225
  219.4 4.2 %collective-permute-done.31 = bf16[32,4096]{1,0:T(8,128)(2,1)S(1)} collective-permute-done((bf16[32,4096]{1,0:T(8,128)(2,1)S(1)}, bf16[32,4096]{1,0:T(8,128)(2,1)S(1)}, u32[]{:S(2)}, u32[]{:S(2)}) %collective-permute-start.31) | collective-permute-done | bytes 262176 | tf_op jit(solution)/shard_map/ppermute | solution.py:225
  (178 shorter events, 67.7 us)
Async XLA Ops:
  35.0 2.1 collective-permute-start
  50.9 8.6 %collective-permute-start.11 = (bf16[32,4096]{1,0:T(8,128)(2,1)S(1)}, bf16[32,4096]{1,0:T(8,128)(2,1)S(1)}, u32[]{:S(2)}, u32[]{:S(2)}) collective-permute-start(bf16[32,4096]{1,0:T(8,128)(2,1)S(1)} %get-tuple-element.87.down_rows), channel_id=1, source_target_pairs={{4,0},{5,1},{8,4},{9,5},{12,8},{13,9},{14,12},{15,13},{10,14},{11,... | collective-permute-start | bytes 786440 | tf_op jit(solution)/shard_map/ppermute | solution.py:219
  52.6 8.5 %collective-permute-start.4 = (bf16[32,4096]{1,0:T(8,128)(2,1)S(1)}, bf16[32,4096]{1,0:T(8,128)(2,1)S(1)}, u32[]{:S(2)}, u32[]{:S(2)}) collective-permute-start(bf16[32,4096]{1,0:T(8,128)(2,1)S(1)} %get-tuple-element.88.up_rows), channel_id=1, source_target_pairs={{0,4},{1,5},{4,8},{5,9},{8,12},{9,13},{12,14},{13,15},{14,10},{15,... | collective-permute-start | bytes 786440 | tf_op jit(solution)/shard_map/ppermute | solution.py:218
  59.5 9.2 %collective-permute-start.12 = (bf16[32,4096]{1,0:T(8,128)(2,1)S(1)}, bf16[32,4096]{1,0:T(8,128)(2,1)S(1)}, u32[]{:S(2)}, u32[]{:S(2)}) collective-permute-start(bf16[32,4096]{1,0:T(8,128)(2,1)S(1)} %collective-permute-done.11.down_rows), channel_id=1, source_target_pairs={{4,0},{5,1},{8,4},{9,5},{12,8},{13,9},{14,12},{15,13},{10,14},{11,... | collective-permute-start | bytes 786440 | tf_op jit(solution)/shard_map/ppermute | solution.py:219
  61.1 11.5 %collective-permute-start.5 = (bf16[32,4096]{1,0:T(8,128)(2,1)S(1)}, bf16[32,4096]{1,0:T(8,128)(2,1)}, u32[]{:S(2)}, u32[]{:S(2)}) collective-permute-start(bf16[32,4096]{1,0:T(8,128)(2,1)S(1)} %collective-permute-done.4.up_rows), channel_id=1, source_target_pairs={{0,4},{1,5},{4,8},{5,9},{8,12},{9,13},{12,14},{13,15},{14,10},{15,... | collective-permute-start | bytes 786440 | tf_op jit(solution)/shard_map/ppermute | solution.py:218
  68.7 9.0 %collective-permute-start.13 = (bf16[32,4096]{1,0:T(8,128)(2,1)S(1)}, bf16[32,4096]{1,0:T(8,128)(2,1)}, u32[]{:S(2)}, u32[]{:S(2)}) collective-permute-start(bf16[32,4096]{1,0:T(8,128)(2,1)S(1)} %collective-permute-done.12.down_rows), channel_id=1, source_target_pairs={{4,0},{5,1},{8,4},{9,5},{12,8},{13,9},{14,12},{15,13},{10,14},{11,... | collective-permute-start | bytes 786440 | tf_op jit(solution)/shard_map/ppermute | solution.py:219
  72.7 8.7 %collective-permute-start.6 = (bf16[32,4096]{1,0:T(8,128)(2,1)}, bf16[32,4096]{1,0:T(8,128)(2,1)}, u32[]{:S(2)}, u32[]{:S(2)}) collective-permute-start(bf16[32,4096]{1,0:T(8,128)(2,1)} %collective-permute-done.5.up_rows), channel_id=1, source_target_pairs={{0,4},{1,5},{4,8},{5,9},{8,12},{9,13},{12,14},{13,15},{14,10},{15,... | collective-permute-start | bytes 786440 | tf_op jit(solution)/shard_map/ppermute | solution.py:218
  77.7 20.5 %collective-permute-start.14 = (bf16[32,4096]{1,0:T(8,128)(2,1)}, bf16[32,4096]{1,0:T(8,128)(2,1)}, u32[]{:S(2)}, u32[]{:S(2)}) collective-permute-start(bf16[32,4096]{1,0:T(8,128)(2,1)} %collective-permute-done.13.down_rows), channel_id=1, source_target_pairs={{4,0},{5,1},{8,4},{9,5},{12,8},{13,9},{14,12},{15,13},{10,14},{11,... | collective-permute-start | bytes 786440 | tf_op jit(solution)/shard_map/ppermute | solution.py:219
  81.4 18.2 %collective-permute-start.7 = (bf16[32,4096]{1,0:T(8,128)(2,1)}, bf16[32,4096]{1,0:T(8,128)(2,1)}, u32[]{:S(2)}, u32[]{:S(2)}) collective-permute-start(bf16[32,4096]{1,0:T(8,128)(2,1)} %collective-permute-done.6.up_rows), channel_id=1, source_target_pairs={{0,4},{1,5},{4,8},{5,9},{8,12},{9,13},{12,14},{13,15},{14,10},{15,... | collective-permute-start | bytes 786440 | tf_op jit(solution)/shard_map/ppermute | solution.py:218
  97.6 30.1 %collective-permute-start.1 = (bf16[4096,256]{1,0:T(8,128)(2,1)S(1)}, bf16[4096,256]{1,0:T(8,128)(2,1)}, u32[]{:S(2)}, u32[]{:S(2)}) collective-permute-start(bf16[4096,256]{1,0:T(8,128)(2,1)S(1)} %bitcast.46), channel_id=1, source_target_pairs={{0,1},{1,0},{2,3},{3,2},{4,5},{5,4},{6,7},{7,6},{8,9},{9,8},{10,11... | collective-permute-start | bytes 6291464 | tf_op jit(solution)/shard_map/ppermute | solution.py:199
  97.6 30.0 %collective-permute-start.2 = (bf16[4096,256]{1,0:T(8,128)(2,1)}, bf16[4096,256]{1,0:T(8,128)(2,1)}, u32[]{:S(2)}, u32[]{:S(2)}) collective-permute-start(bf16[4096,256]{1,0:T(8,128)(2,1)} %bitcast.55), channel_id=1, source_target_pairs={{0,1},{1,0},{2,3},{3,2},{4,5},{5,4},{6,7},{7,6},{8,9},{9,8},{10,11... | collective-permute-start | bytes 6291464 | tf_op jit(solution)/shard_map/ppermute | solution.py:199
  98.1 29.5 %collective-permute-start.3 = (bf16[256,4096]{1,0:T(8,128)(2,1)}, bf16[256,4096]{1,0:T(8,128)(2,1)}, u32[]{:S(2)}, u32[]{:S(2)}) collective-permute-start(bf16[256,4096]{1,0:T(8,128)(2,1)} %bitcast.64), channel_id=1, source_target_pairs={{0,1},{1,0},{2,3},{3,2},{4,5},{5,4},{6,7},{7,6},{8,9},{9,8},{10,11... | collective-permute-start | bytes 6291464 | tf_op jit(solution)/shard_map/ppermute | solution.py:199
  98.2 18.6 %collective-permute-start.15 = (bf16[32,4096]{1,0:T(8,128)(2,1)}, bf16[32,4096]{1,0:T(8,128)(2,1)}, u32[]{:S(2)}, u32[]{:S(2)}) collective-permute-start(bf16[32,4096]{1,0:T(8,128)(2,1)} %collective-permute-done.14.down_rows), channel_id=1, source_target_pairs={{4,0},{5,1},{8,4},{9,5},{12,8},{13,9},{14,12},{15,13},{10,14},{11,... | collective-permute-start | bytes 786440 | tf_op jit(solution)/shard_map/ppermute | solution.py:219
  99.6 18.6 %collective-permute-start.8 = (bf16[32,4096]{1,0:T(8,128)(2,1)}, bf16[32,4096]{1,0:T(8,128)(2,1)}, u32[]{:S(2)}, u32[]{:S(2)}) collective-permute-start(bf16[32,4096]{1,0:T(8,128)(2,1)} %collective-permute-done.7.up_rows), channel_id=1, source_target_pairs={{0,4},{1,5},{4,8},{5,9},{8,12},{9,13},{12,14},{13,15},{14,10},{15,... | collective-permute-start | bytes 786440 | tf_op jit(solution)/shard_map/ppermute | solution.py:218
  116.9 8.7 %collective-permute-start.16 = (bf16[32,4096]{1,0:T(8,128)(2,1)}, bf16[32,4096]{1,0:T(8,128)(2,1)}, u32[]{:S(2)}, u32[]{:S(2)}) collective-permute-start(bf16[32,4096]{1,0:T(8,128)(2,1)} %collective-permute-done.15.down_rows), channel_id=1, source_target_pairs={{4,0},{5,1},{8,4},{9,5},{12,8},{13,9},{14,12},{15,13},{10,14},{11,... | collective-permute-start | bytes 786440 | tf_op jit(solution)/shard_map/ppermute | solution.py:219
  118.2 8.4 %collective-permute-start.9 = (bf16[32,4096]{1,0:T(8,128)(2,1)}, bf16[32,4096]{1,0:T(8,128)(2,1)}, u32[]{:S(2)}, u32[]{:S(2)}) collective-permute-start(bf16[32,4096]{1,0:T(8,128)(2,1)} %collective-permute-done.8.up_rows), channel_id=1, source_target_pairs={{0,4},{1,5},{4,8},{5,9},{8,12},{9,13},{12,14},{13,15},{14,10},{15,... | collective-permute-start | bytes 786440 | tf_op jit(solution)/shard_map/ppermute | solution.py:218
  125.6 45.7 %collective-permute-start.17 = (bf16[32,4096]{1,0:T(8,128)(2,1)}, bf16[32,4096]{1,0:T(8,128)(2,1)S(1)}, u32[]{:S(2)}, u32[]{:S(2)}) collective-permute-start(bf16[32,4096]{1,0:T(8,128)(2,1)} %collective-permute-done.16.down_rows), channel_id=1, source_target_pairs={{4,0},{5,1},{8,4},{9,5},{12,8},{13,9},{14,12},{15,13},{10,14},{11,... | collective-permute-start | bytes 786440 | tf_op jit(solution)/shard_map/ppermute | solution.py:219
  126.6 44.7 %collective-permute-start.10 = (bf16[32,4096]{1,0:T(8,128)(2,1)}, bf16[32,4096]{1,0:T(8,128)(2,1)S(1)}, u32[]{:S(2)}, u32[]{:S(2)}) collective-permute-start(bf16[32,4096]{1,0:T(8,128)(2,1)} %collective-permute-done.9.up_rows), channel_id=1, source_target_pairs={{0,4},{1,5},{4,8},{5,9},{8,12},{9,13},{12,14},{13,15},{14,10},{15,... | collective-permute-start | bytes 786440 | tf_op jit(solution)/shard_map/ppermute | solution.py:218
  136.9 39.6 %collective-permute-start.25 = (bf16[32,4096]{1,0:T(8,128)(2,1)S(1)}, bf16[32,4096]{1,0:T(8,128)(2,1)S(1)}, u32[]{:S(2)}, u32[]{:S(2)}) collective-permute-start(bf16[32,4096]{1,0:T(8,128)(2,1)S(1)} %convert_element_type.125), channel_id=1, source_target_pairs={{4,0},{5,1},{8,4},{9,5},{12,8},{13,9},{14,12},{15,13},{10,14},{11,... | collective-permute-start | bytes 786440 | tf_op jit(solution)/shard_map/ppermute | solution.py:225
  138.0 39.7 %collective-permute-start.18 = (bf16[32,4096]{1,0:T(8,128)(2,1)S(1)}, bf16[32,4096]{1,0:T(8,128)(2,1)S(1)}, u32[]{:S(2)}, u32[]{:S(2)}) collective-permute-start(bf16[32,4096]{1,0:T(8,128)(2,1)S(1)} %convert_element_type.111), channel_id=1, source_target_pairs={{0,4},{1,5},{4,8},{5,9},{8,12},{9,13},{12,14},{13,15},{14,10},{15,... | collective-permute-start | bytes 786440 | tf_op jit(solution)/shard_map/ppermute | solution.py:224
  176.6 6.7 %collective-permute-start.26 = (bf16[32,4096]{1,0:T(8,128)(2,1)S(1)}, bf16[32,4096]{1,0:T(8,128)(2,1)S(1)}, u32[]{:S(2)}, u32[]{:S(2)}) collective-permute-start(bf16[32,4096]{1,0:T(8,128)(2,1)S(1)} %add_convert_fusion.5), channel_id=1, source_target_pairs={{4,0},{5,1},{8,4},{9,5},{12,8},{13,9},{14,12},{15,13},{10,14},{11,... | collective-permute-start | bytes 786440 | tf_op jit(solution)/shard_map/ppermute | solution.py:225
  177.8 6.9 %collective-permute-start.19 = (bf16[32,4096]{1,0:T(8,128)(2,1)S(1)}, bf16[32,4096]{1,0:T(8,128)(2,1)S(1)}, u32[]{:S(2)}, u32[]{:S(2)}) collective-permute-start(bf16[32,4096]{1,0:T(8,128)(2,1)S(1)} %add_convert_fusion.11), channel_id=1, source_target_pairs={{0,4},{1,5},{4,8},{5,9},{8,12},{9,13},{12,14},{13,15},{14,10},{15,... | collective-permute-start | bytes 786440 | tf_op jit(solution)/shard_map/ppermute | solution.py:224
  183.4 7.7 %collective-permute-start.27 = (bf16[32,4096]{1,0:T(8,128)(2,1)S(1)}, bf16[32,4096]{1,0:T(8,128)(2,1)S(1)}, u32[]{:S(2)}, u32[]{:S(2)}) collective-permute-start(bf16[32,4096]{1,0:T(8,128)(2,1)S(1)} %add_convert_fusion.4), channel_id=1, source_target_pairs={{4,0},{5,1},{8,4},{9,5},{12,8},{13,9},{14,12},{15,13},{10,14},{11,... | collective-permute-start | bytes 786440 | tf_op jit(solution)/shard_map/ppermute | solution.py:225
  184.7 8.0 %collective-permute-start.20 = (bf16[32,4096]{1,0:T(8,128)(2,1)S(1)}, bf16[32,4096]{1,0:T(8,128)(2,1)S(1)}, u32[]{:S(2)}, u32[]{:S(2)}) collective-permute-start(bf16[32,4096]{1,0:T(8,128)(2,1)S(1)} %add_convert_fusion.10), channel_id=1, source_target_pairs={{0,4},{1,5},{4,8},{5,9},{8,12},{9,13},{12,14},{13,15},{14,10},{15,... | collective-permute-start | bytes 786440 | tf_op jit(solution)/shard_map/ppermute | solution.py:224
  191.2 8.9 %collective-permute-start.28 = (bf16[32,4096]{1,0:T(8,128)(2,1)S(1)}, bf16[32,4096]{1,0:T(8,128)(2,1)S(1)}, u32[]{:S(2)}, u32[]{:S(2)}) collective-permute-start(bf16[32,4096]{1,0:T(8,128)(2,1)S(1)} %add_convert_fusion.3), channel_id=1, source_target_pairs={{4,0},{5,1},{8,4},{9,5},{12,8},{13,9},{14,12},{15,13},{10,14},{11,... | collective-permute-start | bytes 786440 | tf_op jit(solution)/shard_map/ppermute | solution.py:225
  192.8 9.1 %collective-permute-start.21 = (bf16[32,4096]{1,0:T(8,128)(2,1)S(1)}, bf16[32,4096]{1,0:T(8,128)(2,1)S(1)}, u32[]{:S(2)}, u32[]{:S(2)}) collective-permute-start(bf16[32,4096]{1,0:T(8,128)(2,1)S(1)} %add_convert_fusion.9), channel_id=1, source_target_pairs={{0,4},{1,5},{4,8},{5,9},{8,12},{9,13},{12,14},{13,15},{14,10},{15,... | collective-permute-start | bytes 786440 | tf_op jit(solution)/shard_map/ppermute | solution.py:224
  200.1 8.8 %collective-permute-start.29 = (bf16[32,4096]{1,0:T(8,128)(2,1)S(1)}, bf16[32,4096]{1,0:T(8,128)(2,1)S(1)}, u32[]{:S(2)}, u32[]{:S(2)}) collective-permute-start(bf16[32,4096]{1,0:T(8,128)(2,1)S(1)} %add_convert_fusion.2), channel_id=1, source_target_pairs={{4,0},{5,1},{8,4},{9,5},{12,8},{13,9},{14,12},{15,13},{10,14},{11,... | collective-permute-start | bytes 786440 | tf_op jit(solution)/shard_map/ppermute | solution.py:225
  202.0 8.5 %collective-permute-start.22 = (bf16[32,4096]{1,0:T(8,128)(2,1)S(1)}, bf16[32,4096]{1,0:T(8,128)(2,1)S(1)}, u32[]{:S(2)}, u32[]{:S(2)}) collective-permute-start(bf16[32,4096]{1,0:T(8,128)(2,1)S(1)} %add_convert_fusion.8), channel_id=1, source_target_pairs={{0,4},{1,5},{4,8},{5,9},{8,12},{9,13},{12,14},{13,15},{14,10},{15,... | collective-permute-start | bytes 786440 | tf_op jit(solution)/shard_map/ppermute | solution.py:224
  209.0 8.1 %collective-permute-start.30 = (bf16[32,4096]{1,0:T(8,128)(2,1)S(1)}, bf16[32,4096]{1,0:T(8,128)(2,1)S(1)}, u32[]{:S(2)}, u32[]{:S(2)}) collective-permute-start(bf16[32,4096]{1,0:T(8,128)(2,1)S(1)} %add_convert_fusion.1), channel_id=1, source_target_pairs={{4,0},{5,1},{8,4},{9,5},{12,8},{13,9},{14,12},{15,13},{10,14},{11,... | collective-permute-start | bytes 786440 | tf_op jit(solution)/shard_map/ppermute | solution.py:225
  210.5 7.8 %collective-permute-start.23 = (bf16[32,4096]{1,0:T(8,128)(2,1)S(1)}, bf16[32,4096]{1,0:T(8,128)(2,1)S(1)}, u32[]{:S(2)}, u32[]{:S(2)}) collective-permute-start(bf16[32,4096]{1,0:T(8,128)(2,1)S(1)} %add_convert_fusion.7), channel_id=1, source_target_pairs={{0,4},{1,5},{4,8},{5,9},{8,12},{9,13},{12,14},{13,15},{14,10},{15,... | collective-permute-start | bytes 786440 | tf_op jit(solution)/shard_map/ppermute | solution.py:224
  217.2 6.4 %collective-permute-start.31 = (bf16[32,4096]{1,0:T(8,128)(2,1)S(1)}, bf16[32,4096]{1,0:T(8,128)(2,1)S(1)}, u32[]{:S(2)}, u32[]{:S(2)}) collective-permute-start(bf16[32,4096]{1,0:T(8,128)(2,1)S(1)} %add_convert_fusion), channel_id=1, source_target_pairs={{4,0},{5,1},{8,4},{9,5},{12,8},{13,9},{14,12},{15,13},{10,14},{11,... | collective-permute-start | bytes 786440 | tf_op jit(solution)/shard_map/ppermute | solution.py:225
  218.4 6.4 %collective-permute-start.24 = (bf16[32,4096]{1,0:T(8,128)(2,1)S(1)}, bf16[32,4096]{1,0:T(8,128)(2,1)S(1)}, u32[]{:S(2)}, u32[]{:S(2)}) collective-permute-start(bf16[32,4096]{1,0:T(8,128)(2,1)S(1)} %add_convert_fusion.6), channel_id=1, source_target_pairs={{0,4},{1,5},{4,8},{5,9},{8,12},{9,13},{12,14},{13,15},{14,10},{15,... | collective-permute-start | bytes 786440 | tf_op jit(solution)/shard_map/ppermute | solution.py:224
  (12 other events, 120.8 us)

commit v3 on v2

v3 whole, which is shorter than its diff:
```python
import functools
import math

import jax
import jax.numpy as jnp
from jax import lax
from jax.experimental import pallas as pl
from jax.experimental.pallas import tpu as pltpu
from jax.sharding import PartitionSpec as P

HEADS = 32
LAT = 512
ROPE = 64
VD = 128
SPAN = 8
CORES = 2

SCORE_SCALE = 192.0 ** (-0.5)
NORM_EPS = 1e-06
NEG_FILL = -1e30

HEAD_GROUP = 8
SUB_HEADS = 4
LOG2_SCALE = SCORE_SCALE * math.log2(math.e)


def attention_kernel(
    index_ref, q_ref, qr_ref, mine_ref, other_ref, wv_ref, gain_ref, values_ref, normed_ref,
    hits_ref, stack_ref, bias_a_ref, bias_b_ref, *, tok,
):
    group = pl.program_id(0)
    my_index = index_ref[0]
    my_chip, my_core = my_index // CORES, lax.rem(my_index, CORES)
    keys = mine_ref.shape[0]

    @pl.when(group == 0)
    def _():
        row_pos = my_index * tok + lax.broadcasted_iota(jnp.int32, (tok, keys), 0)
        key_iota = lax.broadcasted_iota(jnp.int32, (tok, keys), 1)
        key_chip = (key_iota // tok) ^ my_chip
        key_tok = lax.rem(key_iota, jnp.int32(tok))
        for core, bias_ref in ((my_core, bias_a_ref), (1 - my_core, bias_b_ref)):
            key_pos = (key_chip * CORES + core) * tok + key_tok
            bias_ref[...] = jnp.where(key_pos <= row_pos, 0.0, NEG_FILL)
        last = mine_ref[:, LAT : LAT + 2 * ROPE].astype(jnp.float32)
        lane = lax.broadcasted_iota(jnp.int32, last.shape, 1)
        named = jnp.max(jnp.where(lane >= ROPE, last, -1.0), axis=1, keepdims=True)
        my_expert = (my_index // SPAN).astype(jnp.float32)
        hits_ref[...] = jnp.where(named == my_expert, 1.0, 0.0)

    lane = lax.broadcasted_iota(jnp.int32, (tok, 2 * ROPE), 1)
    for head in range(HEAD_GROUP):
        at = pl.ds(head * tok, tok)
        stack_ref[at, 0:LAT] = q_ref[:, head * LAT : (head + 1) * LAT]
        pair = qr_ref[:, (head // 2) * 2 * ROPE : (head // 2 + 1) * 2 * ROPE]
        if head % 2:
            pair = jnp.concatenate([pair[:, ROPE:], pair[:, :ROPE]], axis=1)
        stack_ref[at, LAT : LAT + 2 * ROPE] = jnp.where(lane < ROPE, pair, jnp.zeros_like(pair))

    rows = SUB_HEADS * tok
    parts = []
    for sub in range(HEAD_GROUP // SUB_HEADS):
        queries = stack_ref[sub * rows : (sub + 1) * rows, :]

        def scores_of(keys_ref, bias_ref):
            scores = lax.dot_general(
                queries, keys_ref[...], (((1,), (1,)), ((), ())),
                preferred_element_type=jnp.float32,
            )
            return scores.reshape(SUB_HEADS, tok, keys) * LOG2_SCALE + bias_ref[...][None]

        scores_a = scores_of(mine_ref, bias_a_ref)
        scores_b = scores_of(other_ref, bias_b_ref)
        top = jnp.max(jnp.maximum(scores_a, scores_b), axis=2, keepdims=True)
        weights_a = jnp.exp2(scores_a - top)
        weights_b = jnp.exp2(scores_b - top)
        total = jnp.sum(weights_a + weights_b, axis=2, keepdims=True)
        mixed = jnp.dot(
            weights_a.astype(jnp.bfloat16).reshape(rows, keys), mine_ref[:, 0:LAT],
            preferred_element_type=jnp.float32,
        ) + jnp.dot(
            weights_b.astype(jnp.bfloat16).reshape(rows, keys), other_ref[:, 0:LAT],
            preferred_element_type=jnp.float32,
        )
        latent = (mixed.reshape(SUB_HEADS, tok, LAT) / total).astype(jnp.bfloat16)
        for head in range(SUB_HEADS):
            value = jnp.dot(
                latent[head], wv_ref[sub * SUB_HEADS + head], preferred_element_type=jnp.float32
            )
            parts.append(value.astype(jnp.bfloat16))
    wide = HEAD_GROUP * VD
    values_ref[:, pl.ds(pl.multiple_of(group * wide, wide), wide)] = jnp.concatenate(parts, axis=1)

    @pl.when(group == HEADS // HEAD_GROUP - 1)
    def _():
        values = values_ref[...].astype(jnp.float32)
        square = jnp.mean(values * values, axis=1, keepdims=True)
        normed = values * lax.rsqrt(square + NORM_EPS) * gain_ref[...]
        normed_ref[...] = normed.astype(jnp.bfloat16)


def attention(my_index, q_nope, q_rope, mine, other, w_value, norm_gain):
    tok = q_nope.shape[0]
    total = mine.shape[0]
    rows = HEAD_GROUP * tok
    grid_spec = pltpu.PrefetchScalarGridSpec(
        num_scalar_prefetch=1,
        grid=(HEADS // HEAD_GROUP,),
        in_specs=[
            pl.BlockSpec((tok, HEAD_GROUP * LAT), lambda g, i: (0, g)),
            pl.BlockSpec((tok, HEAD_GROUP * ROPE), lambda g, i: (0, g)),
            pl.BlockSpec(mine.shape, lambda g, i: (0, 0)),
            pl.BlockSpec(mine.shape, lambda g, i: (0, 0)),
            pl.BlockSpec((HEAD_GROUP, LAT, VD), lambda g, i: (g, 0, 0)),
            pl.BlockSpec((1, HEADS * VD), lambda g, i: (0, 0)),
        ],
        out_specs=[
            pl.BlockSpec((tok, HEADS * VD), lambda g, i: (0, 0)),
            pl.BlockSpec((tok, HEADS * VD), lambda g, i: (0, 0)),
            pl.BlockSpec((total, 1), lambda g, i: (0, 0)),
        ],
        scratch_shapes=[
            pltpu.VMEM((rows, LAT + 2 * ROPE), jnp.bfloat16),
            pltpu.VMEM((tok, total), jnp.float32),
            pltpu.VMEM((tok, total), jnp.float32),
        ],
    )
    shape = jax.ShapeDtypeStruct((tok, HEADS * VD), jnp.bfloat16)
    work = HEADS * tok * total * CORES
    return pl.pallas_call(
        functools.partial(attention_kernel, tok=tok),
        grid_spec=grid_spec,
        out_shape=[shape, shape, jax.ShapeDtypeStruct((total, 1), jnp.float32)],
        compiler_params=pltpu.CompilerParams(vmem_limit_bytes=56 << 20),
        cost_estimate=pl.CostEstimate(
            flops=2 * work * (2 * LAT + 2 * ROPE), bytes_accessed=8 << 20, transcendentals=work
        ),
    )(my_index.reshape(1), q_nope, q_rope, mine, other, w_value, norm_gain.reshape(1, HEADS * VD))


def ring_place(chip, chips):
    return jnp.where(chip % 2 == 0, chip // 2, chips - 1 - chip // 2)


def ring_chip(place, chips):
    return jnp.where(place < chips // 2, 2 * place, 2 * (chips - 1 - place) + 1)


def expert_kernel(
    index_ref, up_rows, down_rows, hits_ref, gate_a, gate_b, up_a, up_b, down_a, down_b, out_a,
    out_b, *, hop, chips,
):
    half = up_rows.shape[0]
    my_chip = index_ref[0] // CORES
    place = ring_place(my_chip, chips)
    from_behind = ring_chip(lax.rem(place - hop + chips, chips), chips) ^ my_chip
    from_ahead = ring_chip(lax.rem(place + hop, chips), chips) ^ my_chip
    tok = 2 * half
    keep = jnp.concatenate(
        [
            hits_ref[pl.ds(pl.multiple_of(from_behind * tok, half), half), :],
            hits_ref[pl.ds(pl.multiple_of(from_ahead * tok + half, half), half), :],
        ],
        axis=0,
    ) > 0.0
    rows = jnp.concatenate([up_rows[...], down_rows[...]], axis=0)

    def hidden(gate_ref, up_ref):
        gate_act = jnp.dot(rows, gate_ref[...], preferred_element_type=jnp.float32)
        up_act = jnp.dot(rows, up_ref[...], preferred_element_type=jnp.float32)
        act = gate_act * (1.0 / (1.0 + jnp.exp(-gate_act))) * up_act
        return jnp.where(keep, act, 0.0).astype(jnp.bfloat16)

    hidden_a, hidden_b = hidden(gate_a, up_a), hidden(gate_b, up_b)
    part = jnp.dot(hidden_a, down_a[...], preferred_element_type=jnp.float32)
    part = part + jnp.dot(hidden_b, down_b[...], preferred_element_type=jnp.float32)
    out_a[...] = part[:half]
    out_b[...] = part[half:]


def expert_part(my_index, rows_up, rows_down, hits, weights, hop, chips):
    half, features = rows_up.shape
    units = 2 * weights[0].shape[1]
    shape = jax.ShapeDtypeStruct((half, features), jnp.float32)
    return pl.pallas_call(
        functools.partial(expert_kernel, hop=hop, chips=chips),
        in_specs=[pl.BlockSpec(memory_space=pltpu.SMEM)]
        + [pl.BlockSpec(memory_space=pltpu.VMEM)] * 9,
        out_specs=[pl.BlockSpec(memory_space=pltpu.VMEM)] * 2,
        out_shape=[shape, shape],
        compiler_params=pltpu.CompilerParams(vmem_limit_bytes=24 << 20),
        cost_estimate=pl.CostEstimate(
            flops=12 * half * features * units, bytes_accessed=14 << 20, transcendentals=0
        ),
    )(my_index.reshape(1), rows_up, rows_down, hits, *weights)


def local(
    q_nope, q_rope, c_kv, k_rope, w_value, norm_gain, expert_ids, gate_fixed, w_gate, w_up, w_down
):
    tok = c_kv.shape[0]
    half = tok // 2
    n_ctx = lax.axis_size("ctx")
    chips = n_ctx // CORES
    my_index = lax.axis_index("ctx")
    siblings = [(i, i ^ 1) for i in range(n_ctx)]
    ring = list(range(0, chips, 2)) + list(range(1, chips, 2))[::-1]
    ahead = [
        (ring[p] * CORES + core, ring[(p + 1) % chips] * CORES + core)
        for p in range(chips) for core in range(CORES)
    ]
    behind = [(there, here) for here, there in ahead]

    def from_chip(block, step):
        return lax.ppermute(block, "ctx", [(i, i ^ (step * CORES)) for i in range(n_ctx)])

    ids = jnp.broadcast_to(expert_ids.astype(jnp.bfloat16), (tok, ROPE))
    block = jnp.concatenate([c_kv, k_rope, ids], axis=1)
    across = from_chip(block, chips // 2)
    near = [block] + [from_chip(block, step) for step in range(1, chips // 2)]
    far = [across] + [from_chip(across, step) for step in range(1, chips // 2)]
    mine = jnp.concatenate(near + far, axis=0)
    other = lax.ppermute(mine, "ctx", siblings)

    own, mine, other = lax.optimization_barrier(((w_gate[0], w_up[0], w_down[0]), mine, other))
    swapped = tuple(lax.ppermute(w, "ctx", siblings) for w in own)
    values, normed, hits = attention(my_index, q_nope, q_rope, mine, other, w_value, norm_gain)
    normed, swapped = lax.optimization_barrier((normed, swapped))
    weights = (own[0], swapped[0], own[1], swapped[1], own[2], swapped[2])

    def part_of(rows, hop):
        return expert_part(my_index, rows[0], rows[1], hits, weights, hop, chips)

    def move(pair):
        return (lax.ppermute(pair[0], "ctx", ahead), lax.ppermute(pair[1], "ctx", behind))

    def rounded(pair):
        return tuple(x.astype(jnp.bfloat16) for x in pair)

    start = (normed[:half], normed[half:])
    rows = move(start)
    home = part_of(start, 0)
    rows, home = lax.optimization_barrier((rows, home))
    later = move(rows) if chips > 2 else None
    sums = rounded(part_of(rows, 1))
    for hop in range(1, chips):
        rows = later
        if hop + 2 < chips:
            rows, sums = lax.optimization_barrier((rows, sums))
            later = move(rows)
        arrived = move(sums)
        if hop + 1 < chips:
            part = part_of(rows, hop + 1)
            sums = rounded(tuple(p + a.astype(jnp.float32) for p, a in zip(part, arrived)))
    expert_out = jnp.concatenate(
        [h + a.astype(jnp.float32) for h, a in zip(home, arrived)], axis=0
    )
    gate_weight = gate_fixed.astype(jnp.float32) / 65536.0
    return (values.astype(jnp.float32) + gate_weight * expert_out).astype(jnp.bfloat16)


def solution(mesh):
    in_specs = (
        P(("rep", "ctx"), None),
        P(("rep", "ctx"), None),
        P(("rep", "ctx"), None),
        P(("rep", "ctx"), None),
        P(),
        P(),
        P(("rep", "ctx"), None),
        P(("rep", "ctx"), None),
        P("ctx", None, None),
        P("ctx", None, None),
        P("ctx", None, None),
    )
    out_specs = P(("rep", "ctx"), None)
    return jax.shard_map(local, mesh=mesh, in_specs=in_specs, out_specs=out_specs, check_vma=False)
```

time: 227 us -> 133 us (0.59)
  local copies, waits for them, and re-layouts: 43.9 us -> 2.46 us
  blocking collectives: 33.4 us -> 0 us
  waiting for transfers between devices: 57.6 us -> 31.9 us
  starting transfers between devices: 31.1 us -> 39.9 us
    all_gather x1 -> x0, blocking collectives: 33.4 us -> none  [local(): lax.all_gather(block, 'ctx', axis=0, tiled=True, axis_index_groups=same_c...]
    gather x66 -> x0, local copies, waits for them, and re-layouts: 33.3 us -> none
    ppermute x28 -> x35, waiting for transfers between devices: 57.4 us -> 29.8 us  [the longest x14 18 us: move(): lax.ppermute(pair[0], 'ctx', ahead)]
    ppermute x28 -> x35, starting transfers between devices: 30.4 us -> 39.2 us  [the longest x14 14.3 us: move(): lax.ppermute(pair[0], 'ctx', ahead)]
    unnamed x26 -> x22, local copies, waits for them, and re-layouts: 4.81 us -> 1.3 us
    squeeze x9 -> x0, local copies, waits for them, and re-layouts: 3.17 us -> none  [the longest x8 3.07 us: local(): part_up, part_down = expert_part(rows_up, rows_down, masks[hop], weights)]
  transfers between devices with their start and end apart: 32 -> 39, of which waited for: 15 -> 18; matrix products, arithmetic and copies ran while one was open for 18% -> 1% of each run, Pallas kernels for 19% -> 41%
where the time goes in v3:
time: 133 us
  Pallas kernels  55.1 us (41%)
  starting transfers between devices  39.9 us (30%)
  waiting for transfers between devices  31.9 us (24%)
  other arithmetic  3.32 us (2%)
  local copies, waits for them, and re-layouts  2.46 us (2%)
    pallas_call x8, Pallas kernels, expert_part(): pl.pallas_call(functools.partial(expert_kernel, hop=hop, chips=chips), in...  42 us
    ppermute x14, waiting for transfers between devices, move(): lax.ppermute(pair[0], 'ctx', ahead)  18 us
    ppermute x14, starting transfers between devices, move(): lax.ppermute(pair[0], 'ctx', ahead)  14.3 us
    ppermute x14, starting transfers between devices, move(): lax.ppermute(pair[1], 'ctx', behind)  13.5 us
    pallas_call x1, Pallas kernels, attention(): pl.pallas_call(functools.partial(attention_kernel, tok=tok), grid_spec=gr...  13.1 us
    ppermute x7, starting transfers between devices, from_chip(): lax.ppermute(block, 'ctx', [(i, i ^ step * CORES) for i in range(n_ctx)])  11.4 us
    ppermute x14, waiting for transfers between devices, move(): lax.ppermute(pair[1], 'ctx', behind)  7.22 us
    ppermute x7, waiting for transfers between devices, from_chip(): lax.ppermute(block, 'ctx', [(i, i ^ step * CORES) for i in range(n_ctx)])  4.54 us
  transfers between devices with their start and end apart: 39, of which 18 were waited for; matrix products, arithmetic and copies ran while one was open for 1% of the time, Pallas kernels for 41%

profile of v3, /device:TPU:0, one launch (start us, length us, event | category | flops | bytes accessed | tf_op | source)
XLA Modules:
  0.0 132.9 jit_solution(11318417570213134691)
XLA Ops:
  1.7 4.1 %collective-permute-start.3 = (bf16[64,640]{1,0:T(8,128)(2,1)S(1)}, bf16[64,640]{1,0:T(8,128)(2,1)S(1)}, u32[]{:S(2)}, u32[]{:S(2)}) collective-permute-start(bf16[64,640]{1,0:T(8,128)(2,1)S(1)} %get-tuple-element.111), channel_id=1, source_target_pairs={{0,8},{1,9},{2,10},{3,11},{4,12},{5,13},{6,14},{7,15},{8,0},{9,1},... | collective-permute-start | bytes 245768 | tf_op jit(solution)/shard_map/ppermute | solution.py:215
  5.8 1.5 %collective-permute-start = (bf16[64,640]{1,0:T(8,128)(2,1)S(1)}, bf16[64,640]{1,0:T(8,128)(2,1)S(1)}, u32[]{:S(2)}, u32[]{:S(2)}) collective-permute-start(bf16[64,640]{1,0:T(8,128)(2,1)S(1)} %get-tuple-element.111), channel_id=1, source_target_pairs={{0,2},{1,3},{2,0},{3,1},{4,6},{5,7},{6,4},{7,5},{8,10},{9,11},{10,... | collective-permute-start | bytes 245768 | tf_op jit(solution)/shard_map/ppermute | solution.py:215
  7.3 1.6 %collective-permute-start.1 = (bf16[64,640]{1,0:T(8,128)(2,1)S(1)}, bf16[64,640]{1,0:T(8,128)(2,1)S(1)}, u32[]{:S(2)}, u32[]{:S(2)}) collective-permute-start(bf16[64,640]{1,0:T(8,128)(2,1)S(1)} %get-tuple-element.111), channel_id=1, source_target_pairs={{0,4},{1,5},{2,6},{3,7},{4,0},{5,1},{6,2},{7,3},{8,12},{9,13},{10,... | collective-permute-start | bytes 245768 | tf_op jit(solution)/shard_map/ppermute | solution.py:215
  9.8 1.6 %collective-permute-start.4 = (bf16[64,640]{1,0:T(8,128)(2,1)S(1)}, bf16[64,640]{1,0:T(8,128)(2,1)S(1)}, u32[]{:S(2)}, u32[]{:S(2)}) collective-permute-start(bf16[64,640]{1,0:T(8,128)(2,1)S(1)} %collective-permute-done.3), channel_id=1, source_target_pairs={{0,2},{1,3},{2,0},{3,1},{4,6},{5,7},{6,4},{7,5},{8,10},{9,11},{10,... | collective-permute-start | bytes 245768 | tf_op jit(solution)/shard_map/ppermute | solution.py:215
  12.4 1.3 collective-permute-start.6
  15.9 1.8 %collective-permute-done.6 = bf16[64,640]{1,0:T(8,128)(2,1)S(1)} collective-permute-done((bf16[64,640]{1,0:T(8,128)(2,1)S(1)}, bf16[64,640]{1,0:T(8,128)(2,1)S(1)}, u32[]{:S(2)}, u32[]{:S(2)}) %collective-permute-start.6) | collective-permute-done | bytes 81952 | tf_op jit(solution)/shard_map/ppermute | solution.py:215
  17.8 2.1 %collective-permute-done.7.other_ref = bf16[512,640]{1,0:T(8,128)(2,1)S(1)} collective-permute-done((bf16[512,640]{1,0:T(8,128)(2,1)S(1)}, bf16[512,640]{1,0:T(8,128)(2,1)S(1)}, u32[]{:S(2)}, u32[]{:S(2)}) %collective-permute-start.7) | collective-permute-done | bytes 655392 | tf_op jit(solution)/shard_map/ppermute | solution.py:223
  20.8 13.1 %shard_map.109 = (bf16[64,4096]{1,0:T(8,128)(2,1)}, bf16[64,4096]{1,0:T(8,128)(2,1)}, f32[512,1]{1,0:T(8,128)}) custom-call(s32[1]{0:T(128)} %bitcast.index_ref, bf16[64,16384]{1,0:T(8,128)(2,1)} %q_ref.1, bf16[64,2048]{1,0:T(8,128)(2,1)} %qr_ref.1, bf16[512,640]{1,0:T(8,128)(2,1)} %copy-done.5, bf16[512,640]{1,0:T(8,128)(2,1)} %copy-done.6, ...), custom_call_target="tpu_custom_call" | custom-call | flops 4831838208 | bytes 8388608 | tf_op jit(solution)/shard_map/pallas_call | solution.py:130
  38.0 5.2 %shard_map.110 = (f32[32,4096]{1,0:T(8,128)S(1)}, f32[32,4096]{1,0:T(8,128)S(1)}) custom-call(s32[1]{0:T(128)} %bitcast.index_ref, bf16[32,4096]{1,0:T(8,128)(2,1)S(1)} %get-tuple-element.110.up_rows, bf16[32,4096]{1,0:T(8,128)(2,1)S(1)} %get-tuple-element.109.down_rows, f32[512,1]{1,0:T(8,128)S(1)} %copy-done.3, bf16[4096,256]{1,0:T(8,128)(2,1)S(1)} %bitcast.10, ...), custom_call_target="tpu_custom_call" | custom-call | flops 805306368 | bytes 14680064 | tf_op jit(solution)/shard_map/pallas_call | solution.py:185
  43.4 1.8 %collective-permute-done.12.down_rows = bf16[32,4096]{1,0:T(8,128)(2,1)S(1)} collective-permute-done((bf16[32,4096]{1,0:T(8,128)(2,1)S(1)}, bf16[32,4096]{1,0:T(8,128)(2,1)S(1)}, u32[]{:S(2)}, u32[]{:S(2)}) %collective-permute-start.12) | collective-permute-done | bytes 262176 | tf_op jit(solution)/shard_map/ppermute | solution.py:235
  45.1 1.7 %collective-permute-start.13 = (bf16[32,4096]{1,0:T(8,128)(2,1)S(1)}, bf16[32,4096]{1,0:T(8,128)(2,1)S(1)}, u32[]{:S(2)}, u32[]{:S(2)}) collective-permute-start(bf16[32,4096]{1,0:T(8,128)(2,1)S(1)} %collective-permute-done.11.up_rows), channel_id=1, source_target_pairs={{0,4},{1,5},{4,8},{5,9},{8,12},{9,13},{12,14},{13,15},{14,10},{15,... | collective-permute-start | bytes 786440 | tf_op jit(solution)/shard_map/ppermute | solution.py:235
  47.2 5.3 %shard_map.111 = (f32[32,4096]{1,0:T(8,128)S(1)}, f32[32,4096]{1,0:T(8,128)S(1)}) custom-call(s32[1]{0:T(128)} %bitcast.index_ref, bf16[32,4096]{1,0:T(8,128)(2,1)S(1)} %collective-permute-done.11.up_rows, bf16[32,4096]{1,0:T(8,128)(2,1)S(1)} %collective-permute-done.12.down_rows, f32[512,1]{1,0:T(8,128)S(1)} %copy-done.3, bf16[4096,256]{1,0:T(8,128)(2,1)S(1)} %bitcast.11, ...), custom_call_target="tpu_custom_call" | custom-call | flops 805306368 | bytes 14680064 | tf_op jit(solution)/shard_map/pallas_call | solution.py:185
  52.7 1.1 collective-permute-done.14.down_rows
  54.4 1.4 %collective-permute-start.17 = (bf16[32,4096]{1,0:T(8,128)(2,1)S(1)}, bf16[32,4096]{1,0:T(8,128)(2,1)S(1)}, u32[]{:S(2)}, u32[]{:S(2)}) collective-permute-start(bf16[32,4096]{1,0:T(8,128)(2,1)S(1)} %convert_element_type.99), channel_id=1, source_target_pairs={{0,4},{1,5},{4,8},{5,9},{8,12},{9,13},{12,14},{13,15},{14,10},{15,... | collective-permute-start | bytes 786440 | tf_op jit(solution)/shard_map/ppermute | solution.py:235
  56.7 1.2 collective-permute-start.16
  57.9 5.2 %shard_map.112 = (f32[32,4096]{1,0:T(8,128)S(1)}, f32[32,4096]{1,0:T(8,128)S(1)}) custom-call(s32[1]{0:T(128)} %bitcast.index_ref, bf16[32,4096]{1,0:T(8,128)(2,1)S(1)} %collective-permute-done.13.up_rows, bf16[32,4096]{1,0:T(8,128)(2,1)S(1)} %collective-permute-done.14.down_rows, f32[512,1]{1,0:T(8,128)S(1)} %copy-done.3, bf16[4096,256]{1,0:T(8,128)(2,1)S(1)} %bitcast.12, ...), custom_call_target="tpu_custom_call" | custom-call | flops 805306368 | bytes 14680064 | tf_op jit(solution)/shard_map/pallas_call | solution.py:185
  63.3 2.8 %collective-permute-done.15.up_rows = bf16[32,4096]{1,0:T(8,128)(2,1)S(1)} collective-permute-done((bf16[32,4096]{1,0:T(8,128)(2,1)S(1)}, bf16[32,4096]{1,0:T(8,128)(2,1)S(1)}, u32[]{:S(2)}, u32[]{:S(2)}) %collective-permute-start.15) | collective-permute-done | bytes 262176 | tf_op jit(solution)/shard_map/ppermute | solution.py:235
  66.7 1.5 %collective-permute-start.21 = (bf16[32,4096]{1,0:T(8,128)(2,1)S(1)}, bf16[32,4096]{1,0:T(8,128)(2,1)S(1)}, u32[]{:S(2)}, u32[]{:S(2)}) collective-permute-start(bf16[32,4096]{1,0:T(8,128)(2,1)S(1)} %add_convert_fusion.11), channel_id=1, source_target_pairs={{0,4},{1,5},{4,8},{5,9},{8,12},{9,13},{12,14},{13,15},{14,10},{15,... | collective-permute-start | bytes 786440 | tf_op jit(solution)/shard_map/ppermute | solution.py:235
  70.2 5.2 %shard_map.113 = (f32[32,4096]{1,0:T(8,128)S(1)}, f32[32,4096]{1,0:T(8,128)S(1)}) custom-call(s32[1]{0:T(128)} %bitcast.index_ref, bf16[32,4096]{1,0:T(8,128)(2,1)S(1)} %collective-permute-done.15.up_rows, bf16[32,4096]{1,0:T(8,128)(2,1)S(1)} %collective-permute-done.16.down_rows, f32[512,1]{1,0:T(8,128)S(1)} %copy-done.3, bf16[4096,256]{1,0:T(8,128)(2,1)S(1)} %bitcast.13, ...), custom_call_target="tpu_custom_call" | custom-call | flops 805306368 | bytes 14680064 | tf_op jit(solution)/shard_map/pallas_call | solution.py:185
  75.5 2.2 %collective-permute-done.19.up_rows = bf16[32,4096]{1,0:T(8,128)(2,1)S(1)} collective-permute-done((bf16[32,4096]{1,0:T(8,128)(2,1)S(1)}, bf16[32,4096]{1,0:T(8,128)(2,1)S(1)}, u32[]{:S(2)}, u32[]{:S(2)}) %collective-permute-start.19) | collective-permute-done | bytes 262176 | tf_op jit(solution)/shard_map/ppermute | solution.py:235
  77.7 1.6 %collective-permute-start.26 = (bf16[32,4096]{1,0:T(8,128)(2,1)S(1)}, bf16[32,4096]{1,0:T(8,128)(2,1)S(1)}, u32[]{:S(2)}, u32[]{:S(2)}) collective-permute-start(bf16[32,4096]{1,0:T(8,128)(2,1)S(1)} %add_convert_fusion.8), channel_id=1, source_target_pairs={{4,0},{5,1},{8,4},{9,5},{12,8},{13,9},{14,12},{15,13},{10,14},{11,... | collective-permute-start | bytes 786440 | tf_op jit(solution)/shard_map/ppermute | solution.py:235
  79.7 1.7 %collective-permute-start.23 = (bf16[32,4096]{1,0:T(8,128)(2,1)S(1)}, bf16[32,4096]{1,0:T(8,128)(2,1)S(1)}, u32[]{:S(2)}, u32[]{:S(2)}) collective-permute-start(bf16[32,4096]{1,0:T(8,128)(2,1)S(1)} %collective-permute-done.19.up_rows), channel_id=1, source_target_pairs={{0,4},{1,5},{4,8},{5,9},{8,12},{9,13},{12,14},{13,15},{14,10},{15,... | collective-permute-start | bytes 786440 | tf_op jit(solution)/shard_map/ppermute | solution.py:235
  81.8 5.2 %shard_map.114 = (f32[32,4096]{1,0:T(8,128)S(1)}, f32[32,4096]{1,0:T(8,128)S(1)}) custom-call(s32[1]{0:T(128)} %bitcast.index_ref, bf16[32,4096]{1,0:T(8,128)(2,1)S(1)} %collective-permute-done.19.up_rows, bf16[32,4096]{1,0:T(8,128)(2,1)S(1)} %collective-permute-done.20.down_rows, f32[512,1]{1,0:T(8,128)S(1)} %copy-done.3, bf16[4096,256]{1,0:T(8,128)(2,1)S(1)} %bitcast.14, ...), custom_call_target="tpu_custom_call" | custom-call | flops 805306368 | bytes 14680064 | tf_op jit(solution)/shard_map/pallas_call | solution.py:185
  87.1 3.4 %collective-permute-done.23.up_rows = bf16[32,4096]{1,0:T(8,128)(2,1)S(1)} collective-permute-done((bf16[32,4096]{1,0:T(8,128)(2,1)S(1)}, bf16[32,4096]{1,0:T(8,128)(2,1)S(1)}, u32[]{:S(2)}, u32[]{:S(2)}) %collective-permute-start.23) | collective-permute-done | bytes 262176 | tf_op jit(solution)/shard_map/ppermute | solution.py:235
  90.6 1.3 collective-permute-start.30
  94.6 5.2 %shard_map.115 = (f32[32,4096]{1,0:T(8,128)S(1)}, f32[32,4096]{1,0:T(8,128)S(1)}) custom-call(s32[1]{0:T(128)} %bitcast.index_ref, bf16[32,4096]{1,0:T(8,128)(2,1)S(1)} %collective-permute-done.23.up_rows, bf16[32,4096]{1,0:T(8,128)(2,1)S(1)} %collective-permute-done.24.down_rows, f32[512,1]{1,0:T(8,128)S(1)} %copy-done.3, bf16[4096,256]{1,0:T(8,128)(2,1)S(1)} %bitcast.15, ...), custom_call_target="tpu_custom_call" | custom-call | flops 805306368 | bytes 14680064 | tf_op jit(solution)/shard_map/pallas_call | solution.py:185
  100.0 5.0 %collective-permute-done.27.up_rows = bf16[32,4096]{1,0:T(8,128)(2,1)S(1)} collective-permute-done((bf16[32,4096]{1,0:T(8,128)(2,1)S(1)}, bf16[32,4096]{1,0:T(8,128)(2,1)S(1)}, u32[]{:S(2)}, u32[]{:S(2)}) %collective-permute-start.27) | collective-permute-done | bytes 262176 | tf_op jit(solution)/shard_map/ppermute | solution.py:235
  107.4 1.8 %collective-permute-start.36 = (bf16[32,4096]{1,0:T(8,128)(2,1)S(1)}, bf16[32,4096]{1,0:T(8,128)(2,1)S(1)}, u32[]{:S(2)}, u32[]{:S(2)}) collective-permute-start(bf16[32,4096]{1,0:T(8,128)(2,1)S(1)} %add_convert_fusion.4), channel_id=1, source_target_pairs={{4,0},{5,1},{8,4},{9,5},{12,8},{13,9},{14,12},{15,13},{10,14},{11,... | collective-permute-start | bytes 786440 | tf_op jit(solution)/shard_map/ppermute | solution.py:235
  109.1 5.2 %shard_map.117 = (f32[32,4096]{1,0:T(8,128)S(1)}, f32[32,4096]{1,0:T(8,128)S(1)}) custom-call(s32[1]{0:T(128)} %bitcast.index_ref, bf16[32,4096]{1,0:T(8,128)(2,1)S(1)} %collective-permute-done.27.up_rows, bf16[32,4096]{1,0:T(8,128)(2,1)S(1)} %collective-permute-done.28.down_rows, f32[512,1]{1,0:T(8,128)S(1)} %copy-done.3, bf16[4096,256]{1,0:T(8,128)(2,1)S(1)} %bitcast.16, ...), custom_call_target="tpu_custom_call" | custom-call | flops 805306368 | bytes 14680064 | tf_op jit(solution)/shard_map/pallas_call | solution.py:185
  114.8 3.1 %collective-permute-done.36 = bf16[32,4096]{1,0:T(8,128)(2,1)S(1)} collective-permute-done((bf16[32,4096]{1,0:T(8,128)(2,1)S(1)}, bf16[32,4096]{1,0:T(8,128)(2,1)S(1)}, u32[]{:S(2)}, u32[]{:S(2)}) %collective-permute-start.36) | collective-permute-done | bytes 262176 | tf_op jit(solution)/shard_map/ppermute | solution.py:235
  118.9 5.2 %shard_map.116 = (f32[32,4096]{1,0:T(8,128)S(1)}, f32[32,4096]{1,0:T(8,128)S(1)}) custom-call(s32[1]{0:T(128)} %bitcast.index_ref, bf16[32,4096]{1,0:T(8,128)(2,1)S(1)} %collective-permute-done.31.up_rows, bf16[32,4096]{1,0:T(8,128)(2,1)S(1)} %collective-permute-done.32.down_rows, f32[512,1]{1,0:T(8,128)S(1)} %copy-done.3, bf16[4096,256]{1,0:T(8,128)(2,1)S(1)} %bitcast.17, ...), custom_call_target="tpu_custom_call" | custom-call | flops 805306368 | bytes 14680064 | tf_op jit(solution)/shard_map/pallas_call | solution.py:185
  126.5 4.2 %collective-permute-done.35 = bf16[32,4096]{1,0:T(8,128)(2,1)S(1)} collective-permute-done((bf16[32,4096]{1,0:T(8,128)(2,1)S(1)}, bf16[32,4096]{1,0:T(8,128)(2,1)S(1)}, u32[]{:S(2)}, u32[]{:S(2)}) %collective-permute-start.35) | collective-permute-done | bytes 262176 | tf_op jit(solution)/shard_map/ppermute | solution.py:235
  (100 shorter events, 27.8 us)
Async XLA Ops:
  1.7 8.1 %collective-permute-start.3 = (bf16[64,640]{1,0:T(8,128)(2,1)S(1)}, bf16[64,640]{1,0:T(8,128)(2,1)S(1)}, u32[]{:S(2)}, u32[]{:S(2)}) collective-permute-start(bf16[64,640]{1,0:T(8,128)(2,1)S(1)} %get-tuple-element.111), channel_id=1, source_target_pairs={{0,8},{1,9},{2,10},{3,11},{4,12},{5,13},{6,14},{7,15},{8,0},{9,1},... | collective-permute-start | bytes 245768 | tf_op jit(solution)/shard_map/ppermute | solution.py:215
  5.8 6.6 %collective-permute-start = (bf16[64,640]{1,0:T(8,128)(2,1)S(1)}, bf16[64,640]{1,0:T(8,128)(2,1)S(1)}, u32[]{:S(2)}, u32[]{:S(2)}) collective-permute-start(bf16[64,640]{1,0:T(8,128)(2,1)S(1)} %get-tuple-element.111), channel_id=1, source_target_pairs={{0,2},{1,3},{2,0},{3,1},{4,6},{5,7},{6,4},{7,5},{8,10},{9,11},{10,... | collective-permute-start | bytes 245768 | tf_op jit(solution)/shard_map/ppermute | solution.py:215
  19.9 14.0 %collective-permute-start.10 = (bf16[256,4096]{1,0:T(8,128)(2,1)}, bf16[256,4096]{1,0:T(8,128)(2,1)}, u32[]{:S(2)}, u32[]{:S(2)}) collective-permute-start(bf16[256,4096]{1,0:T(8,128)(2,1)} %bitcast.27), channel_id=1, source_target_pairs={{0,1},{1,0},{2,3},{3,2},{4,5},{5,4},{6,7},{7,6},{8,9},{9,8},{10,11... | collective-permute-start | bytes 6291464 | tf_op jit(solution)/shard_map/ppermute | solution.py:226
  20.0 13.8 %collective-permute-start.8 = (bf16[4096,256]{1,0:T(8,128)(2,1)}, bf16[4096,256]{1,0:T(8,128)(2,1)}, u32[]{:S(2)}, u32[]{:S(2)}) collective-permute-start(bf16[4096,256]{1,0:T(8,128)(2,1)} %bitcast.9), channel_id=1, source_target_pairs={{0,1},{1,0},{2,3},{3,2},{4,5},{5,4},{6,7},{7,6},{8,9},{9,8},{10,11... | collective-permute-start | bytes 6291464 | tf_op jit(solution)/shard_map/ppermute | solution.py:226
  20.4 13.5 %collective-permute-start.9 = (bf16[4096,256]{1,0:T(8,128)(2,1)}, bf16[4096,256]{1,0:T(8,128)(2,1)}, u32[]{:S(2)}, u32[]{:S(2)}) collective-permute-start(bf16[4096,256]{1,0:T(8,128)(2,1)} %bitcast.18), channel_id=1, source_target_pairs={{0,1},{1,0},{2,3},{3,2},{4,5},{5,4},{6,7},{7,6},{8,9},{9,8},{10,11... | collective-permute-start | bytes 6291464 | tf_op jit(solution)/shard_map/ppermute | solution.py:226
  34.9 8.4 %collective-permute-start.11 = (bf16[32,4096]{1,0:T(8,128)(2,1)S(1)}, bf16[32,4096]{1,0:T(8,128)(2,1)S(1)}, u32[]{:S(2)}, u32[]{:S(2)}) collective-permute-start(bf16[32,4096]{1,0:T(8,128)(2,1)S(1)} %get-tuple-element.110.up_rows), channel_id=1, source_target_pairs={{0,4},{1,5},{4,8},{5,9},{8,12},{9,13},{12,14},{13,15},{14,10},{15,... | collective-permute-start | bytes 786440 | tf_op jit(solution)/shard_map/ppermute | solution.py:235
  36.1 9.1 %collective-permute-start.12 = (bf16[32,4096]{1,0:T(8,128)(2,1)S(1)}, bf16[32,4096]{1,0:T(8,128)(2,1)S(1)}, u32[]{:S(2)}, u32[]{:S(2)}) collective-permute-start(bf16[32,4096]{1,0:T(8,128)(2,1)S(1)} %get-tuple-element.109.down_rows), channel_id=1, source_target_pairs={{4,0},{5,1},{8,4},{9,5},{12,8},{13,9},{14,12},{15,13},{10,14},{11,... | collective-permute-start | bytes 786440 | tf_op jit(solution)/shard_map/ppermute | solution.py:235
  45.1 7.5 %collective-permute-start.13 = (bf16[32,4096]{1,0:T(8,128)(2,1)S(1)}, bf16[32,4096]{1,0:T(8,128)(2,1)S(1)}, u32[]{:S(2)}, u32[]{:S(2)}) collective-permute-start(bf16[32,4096]{1,0:T(8,128)(2,1)S(1)} %collective-permute-done.11.up_rows), channel_id=1, source_target_pairs={{0,4},{1,5},{4,8},{5,9},{8,12},{9,13},{12,14},{13,15},{14,10},{15,... | collective-permute-start | bytes 786440 | tf_op jit(solution)/shard_map/ppermute | solution.py:235
  46.9 6.9 %collective-permute-start.14 = (bf16[32,4096]{1,0:T(8,128)(2,1)S(1)}, bf16[32,4096]{1,0:T(8,128)(2,1)S(1)}, u32[]{:S(2)}, u32[]{:S(2)}) collective-permute-start(bf16[32,4096]{1,0:T(8,128)(2,1)S(1)} %collective-permute-done.12.down_rows), channel_id=1, source_target_pairs={{4,0},{5,1},{8,4},{9,5},{12,8},{13,9},{14,12},{15,13},{10,14},{11,... | collective-permute-start | bytes 786440 | tf_op jit(solution)/shard_map/ppermute | solution.py:235
  53.8 9.3 %collective-permute-start.18 = (bf16[32,4096]{1,0:T(8,128)(2,1)S(1)}, bf16[32,4096]{1,0:T(8,128)(2,1)S(1)}, u32[]{:S(2)}, u32[]{:S(2)}) collective-permute-start(bf16[32,4096]{1,0:T(8,128)(2,1)S(1)} %convert_element_type.100), channel_id=1, source_target_pairs={{4,0},{5,1},{8,4},{9,5},{12,8},{13,9},{14,12},{15,13},{10,14},{11,... | collective-permute-start | bytes 786440 | tf_op jit(solution)/shard_map/ppermute | solution.py:235
  54.4 8.9 %collective-permute-start.17 = (bf16[32,4096]{1,0:T(8,128)(2,1)S(1)}, bf16[32,4096]{1,0:T(8,128)(2,1)S(1)}, u32[]{:S(2)}, u32[]{:S(2)}) collective-permute-start(bf16[32,4096]{1,0:T(8,128)(2,1)S(1)} %convert_element_type.99), channel_id=1, source_target_pairs={{0,4},{1,5},{4,8},{5,9},{8,12},{9,13},{12,14},{13,15},{14,10},{15,... | collective-permute-start | bytes 786440 | tf_op jit(solution)/shard_map/ppermute | solution.py:235
  55.9 10.2 %collective-permute-start.15 = (bf16[32,4096]{1,0:T(8,128)(2,1)S(1)}, bf16[32,4096]{1,0:T(8,128)(2,1)S(1)}, u32[]{:S(2)}, u32[]{:S(2)}) collective-permute-start(bf16[32,4096]{1,0:T(8,128)(2,1)S(1)} %collective-permute-done.13.up_rows), channel_id=1, source_target_pairs={{0,4},{1,5},{4,8},{5,9},{8,12},{9,13},{12,14},{13,15},{14,10},{15,... | collective-permute-start | bytes 786440 | tf_op jit(solution)/shard_map/ppermute | solution.py:235
  56.7 9.4 %collective-permute-start.16 = (bf16[32,4096]{1,0:T(8,128)(2,1)S(1)}, bf16[32,4096]{1,0:T(8,128)(2,1)S(1)}, u32[]{:S(2)}, u32[]{:S(2)}) collective-permute-start(bf16[32,4096]{1,0:T(8,128)(2,1)S(1)} %collective-permute-done.14.down_rows), channel_id=1, source_target_pairs={{4,0},{5,1},{8,4},{9,5},{12,8},{13,9},{14,12},{15,13},{10,14},{11,... | collective-permute-start | bytes 786440 | tf_op jit(solution)/shard_map/ppermute | solution.py:235
  66.1 9.3 %collective-permute-start.22 = (bf16[32,4096]{1,0:T(8,128)(2,1)S(1)}, bf16[32,4096]{1,0:T(8,128)(2,1)S(1)}, u32[]{:S(2)}, u32[]{:S(2)}) collective-permute-start(bf16[32,4096]{1,0:T(8,128)(2,1)S(1)} %add_convert_fusion.10), channel_id=1, source_target_pairs={{4,0},{5,1},{8,4},{9,5},{12,8},{13,9},{14,12},{15,13},{10,14},{11,... | collective-permute-start | bytes 786440 | tf_op jit(solution)/shard_map/ppermute | solution.py:235
  66.7 8.8 %collective-permute-start.21 = (bf16[32,4096]{1,0:T(8,128)(2,1)S(1)}, bf16[32,4096]{1,0:T(8,128)(2,1)S(1)}, u32[]{:S(2)}, u32[]{:S(2)}) collective-permute-start(bf16[32,4096]{1,0:T(8,128)(2,1)S(1)} %add_convert_fusion.11), channel_id=1, source_target_pairs={{0,4},{1,5},{4,8},{5,9},{8,12},{9,13},{12,14},{13,15},{14,10},{15,... | collective-permute-start | bytes 786440 | tf_op jit(solution)/shard_map/ppermute | solution.py:235
  68.1 9.6 %collective-permute-start.19 = (bf16[32,4096]{1,0:T(8,128)(2,1)S(1)}, bf16[32,4096]{1,0:T(8,128)(2,1)S(1)}, u32[]{:S(2)}, u32[]{:S(2)}) collective-permute-start(bf16[32,4096]{1,0:T(8,128)(2,1)S(1)} %collective-permute-done.15.up_rows), channel_id=1, source_target_pairs={{0,4},{1,5},{4,8},{5,9},{8,12},{9,13},{12,14},{13,15},{14,10},{15,... | collective-permute-start | bytes 786440 | tf_op jit(solution)/shard_map/ppermute | solution.py:235
  69.2 8.5 %collective-permute-start.20 = (bf16[32,4096]{1,0:T(8,128)(2,1)S(1)}, bf16[32,4096]{1,0:T(8,128)(2,1)S(1)}, u32[]{:S(2)}, u32[]{:S(2)}) collective-permute-start(bf16[32,4096]{1,0:T(8,128)(2,1)S(1)} %collective-permute-done.16.down_rows), channel_id=1, source_target_pairs={{4,0},{5,1},{8,4},{9,5},{12,8},{13,9},{14,12},{15,13},{10,14},{11,... | collective-permute-start | bytes 786440 | tf_op jit(solution)/shard_map/ppermute | solution.py:235
  77.7 9.3 %collective-permute-start.26 = (bf16[32,4096]{1,0:T(8,128)(2,1)S(1)}, bf16[32,4096]{1,0:T(8,128)(2,1)S(1)}, u32[]{:S(2)}, u32[]{:S(2)}) collective-permute-start(bf16[32,4096]{1,0:T(8,128)(2,1)S(1)} %add_convert_fusion.8), channel_id=1, source_target_pairs={{4,0},{5,1},{8,4},{9,5},{12,8},{13,9},{14,12},{15,13},{10,14},{11,... | collective-permute-start | bytes 786440 | tf_op jit(solution)/shard_map/ppermute | solution.py:235
  79.3 7.8 %collective-permute-start.25 = (bf16[32,4096]{1,0:T(8,128)(2,1)S(1)}, bf16[32,4096]{1,0:T(8,128)(2,1)S(1)}, u32[]{:S(2)}, u32[]{:S(2)}) collective-permute-start(bf16[32,4096]{1,0:T(8,128)(2,1)S(1)} %add_convert_fusion.9), channel_id=1, source_target_pairs={{0,4},{1,5},{4,8},{5,9},{8,12},{9,13},{12,14},{13,15},{14,10},{15,... | collective-permute-start | bytes 786440 | tf_op jit(solution)/shard_map/ppermute | solution.py:235
  79.7 10.8 %collective-permute-start.23 = (bf16[32,4096]{1,0:T(8,128)(2,1)S(1)}, bf16[32,4096]{1,0:T(8,128)(2,1)S(1)}, u32[]{:S(2)}, u32[]{:S(2)}) collective-permute-start(bf16[32,4096]{1,0:T(8,128)(2,1)S(1)} %collective-permute-done.19.up_rows), channel_id=1, source_target_pairs={{0,4},{1,5},{4,8},{5,9},{8,12},{9,13},{12,14},{13,15},{14,10},{15,... | collective-permute-start | bytes 786440 | tf_op jit(solution)/shard_map/ppermute | solution.py:235
  81.4 9.2 %collective-permute-start.24 = (bf16[32,4096]{1,0:T(8,128)(2,1)S(1)}, bf16[32,4096]{1,0:T(8,128)(2,1)S(1)}, u32[]{:S(2)}, u32[]{:S(2)}) collective-permute-start(bf16[32,4096]{1,0:T(8,128)(2,1)S(1)} %collective-permute-done.20.down_rows), channel_id=1, source_target_pairs={{4,0},{5,1},{8,4},{9,5},{12,8},{13,9},{14,12},{15,13},{10,14},{11,... | collective-permute-start | bytes 786440 | tf_op jit(solution)/shard_map/ppermute | solution.py:235
  90.6 9.3 %collective-permute-start.30 = (bf16[32,4096]{1,0:T(8,128)(2,1)S(1)}, bf16[32,4096]{1,0:T(8,128)(2,1)S(1)}, u32[]{:S(2)}, u32[]{:S(2)}) collective-permute-start(bf16[32,4096]{1,0:T(8,128)(2,1)S(1)} %add_convert_fusion.6), channel_id=1, source_target_pairs={{4,0},{5,1},{8,4},{9,5},{12,8},{13,9},{14,12},{15,13},{10,14},{11,... | collective-permute-start | bytes 786440 | tf_op jit(solution)/shard_map/ppermute | solution.py:235
  91.9 8.1 %collective-permute-start.29 = (bf16[32,4096]{1,0:T(8,128)(2,1)S(1)}, bf16[32,4096]{1,0:T(8,128)(2,1)S(1)}, u32[]{:S(2)}, u32[]{:S(2)}) collective-permute-start(bf16[32,4096]{1,0:T(8,128)(2,1)S(1)} %add_convert_fusion.7), channel_id=1, source_target_pairs={{0,4},{1,5},{4,8},{5,9},{8,12},{9,13},{12,14},{13,15},{14,10},{15,... | collective-permute-start | bytes 786440 | tf_op jit(solution)/shard_map/ppermute | solution.py:235
  92.6 12.5 %collective-permute-start.27 = (bf16[32,4096]{1,0:T(8,128)(2,1)S(1)}, bf16[32,4096]{1,0:T(8,128)(2,1)S(1)}, u32[]{:S(2)}, u32[]{:S(2)}) collective-permute-start(bf16[32,4096]{1,0:T(8,128)(2,1)S(1)} %collective-permute-done.23.up_rows), channel_id=1, source_target_pairs={{0,4},{1,5},{4,8},{5,9},{8,12},{9,13},{12,14},{13,15},{14,10},{15,... | collective-permute-start | bytes 786440 | tf_op jit(solution)/shard_map/ppermute | solution.py:235
  93.6 11.5 %collective-permute-start.28 = (bf16[32,4096]{1,0:T(8,128)(2,1)S(1)}, bf16[32,4096]{1,0:T(8,128)(2,1)S(1)}, u32[]{:S(2)}, u32[]{:S(2)}) collective-permute-start(bf16[32,4096]{1,0:T(8,128)(2,1)S(1)} %collective-permute-done.24.down_rows), channel_id=1, source_target_pairs={{4,0},{5,1},{8,4},{9,5},{12,8},{13,9},{14,12},{15,13},{10,14},{11,... | collective-permute-start | bytes 786440 | tf_op jit(solution)/shard_map/ppermute | solution.py:235
  105.1 9.3 %collective-permute-start.33 = (bf16[32,4096]{1,0:T(8,128)(2,1)S(1)}, bf16[32,4096]{1,0:T(8,128)(2,1)S(1)}, u32[]{:S(2)}, u32[]{:S(2)}) collective-permute-start(bf16[32,4096]{1,0:T(8,128)(2,1)S(1)} %add_convert_fusion.5), channel_id=1, source_target_pairs={{0,4},{1,5},{4,8},{5,9},{8,12},{9,13},{12,14},{13,15},{14,10},{15,... | collective-permute-start | bytes 786440 | tf_op jit(solution)/shard_map/ppermute | solution.py:235
  105.3 13.6 %collective-permute-start.31 = (bf16[32,4096]{1,0:T(8,128)(2,1)S(1)}, bf16[32,4096]{1,0:T(8,128)(2,1)S(1)}, u32[]{:S(2)}, u32[]{:S(2)}) collective-permute-start(bf16[32,4096]{1,0:T(8,128)(2,1)S(1)} %collective-permute-done.27.up_rows), channel_id=1, source_target_pairs={{0,4},{1,5},{4,8},{5,9},{8,12},{9,13},{12,14},{13,15},{14,10},{15,... | collective-permute-start | bytes 786440 | tf_op jit(solution)/shard_map/ppermute | solution.py:235
  106.5 12.5 %collective-permute-start.32 = (bf16[32,4096]{1,0:T(8,128)(2,1)S(1)}, bf16[32,4096]{1,0:T(8,128)(2,1)S(1)}, u32[]{:S(2)}, u32[]{:S(2)}) collective-permute-start(bf16[32,4096]{1,0:T(8,128)(2,1)S(1)} %collective-permute-done.28.down_rows), channel_id=1, source_target_pairs={{4,0},{5,1},{8,4},{9,5},{12,8},{13,9},{14,12},{15,13},{10,14},{11,... | collective-permute-start | bytes 786440 | tf_op jit(solution)/shard_map/ppermute | solution.py:235
  107.4 10.5 %collective-permute-start.36 = (bf16[32,4096]{1,0:T(8,128)(2,1)S(1)}, bf16[32,4096]{1,0:T(8,128)(2,1)S(1)}, u32[]{:S(2)}, u32[]{:S(2)}) collective-permute-start(bf16[32,4096]{1,0:T(8,128)(2,1)S(1)} %add_convert_fusion.4), channel_id=1, source_target_pairs={{4,0},{5,1},{8,4},{9,5},{12,8},{13,9},{14,12},{15,13},{10,14},{11,... | collective-permute-start | bytes 786440 | tf_op jit(solution)/shard_map/ppermute | solution.py:235
  114.4 9.8 %collective-permute-start.34 = (bf16[32,4096]{1,0:T(8,128)(2,1)S(1)}, bf16[32,4096]{1,0:T(8,128)(2,1)S(1)}, u32[]{:S(2)}, u32[]{:S(2)}) collective-permute-start(bf16[32,4096]{1,0:T(8,128)(2,1)S(1)} %add_convert_fusion.3), channel_id=1, source_target_pairs={{0,4},{1,5},{4,8},{5,9},{8,12},{9,13},{12,14},{13,15},{14,10},{15,... | collective-permute-start | bytes 786440 | tf_op jit(solution)/shard_map/ppermute | solution.py:235
  117.9 7.5 %collective-permute-start.37 = (bf16[32,4096]{1,0:T(8,128)(2,1)S(1)}, bf16[32,4096]{1,0:T(8,128)(2,1)S(1)}, u32[]{:S(2)}, u32[]{:S(2)}) collective-permute-start(bf16[32,4096]{1,0:T(8,128)(2,1)S(1)} %add_convert_fusion.1), channel_id=1, source_target_pairs={{4,0},{5,1},{8,4},{9,5},{12,8},{13,9},{14,12},{15,13},{10,14},{11,... | collective-permute-start | bytes 786440 | tf_op jit(solution)/shard_map/ppermute | solution.py:235
  124.3 6.4 %collective-permute-start.35 = (bf16[32,4096]{1,0:T(8,128)(2,1)S(1)}, bf16[32,4096]{1,0:T(8,128)(2,1)S(1)}, u32[]{:S(2)}, u32[]{:S(2)}) collective-permute-start(bf16[32,4096]{1,0:T(8,128)(2,1)S(1)} %add_convert_fusion.2), channel_id=1, source_target_pairs={{0,4},{1,5},{4,8},{5,9},{8,12},{9,13},{12,14},{13,15},{14,10},{15,... | collective-permute-start | bytes 786440 | tf_op jit(solution)/shard_map/ppermute | solution.py:235
  (15 other events, 102.4 us)

commit v4 on v3

--- a/solution.py
+++ b/solution.py
@@ -25,8 +25,8 @@
 
 
 def attention_kernel(
-    index_ref, q_ref, qr_ref, mine_ref, other_ref, wv_ref, gain_ref, values_ref, normed_ref,
-    hits_ref, stack_ref, bias_a_ref, bias_b_ref, *, tok,
+    index_ref, q_ref, qr_ref, mine_ref, other_ref, wv_ref, gain_ref, values_ref, up_ref,
+    down_ref, hits_ref, stack_ref, bias_a_ref, bias_b_ref, *, tok,
 ):
     group = pl.program_id(0)
     my_index = index_ref[0]
@@ -96,7 +96,9 @@
         values = values_ref[...].astype(jnp.float32)
         square = jnp.mean(values * values, axis=1, keepdims=True)
         normed = values * lax.rsqrt(square + NORM_EPS) * gain_ref[...]
-        normed_ref[...] = normed.astype(jnp.bfloat16)
+        normed = normed.astype(jnp.bfloat16)
+        up_ref[...] = normed[: tok // 2]
+        down_ref[...] = normed[tok // 2 :]
 
 
 def attention(my_index, q_nope, q_rope, mine, other, w_value, norm_gain):
@@ -116,7 +118,8 @@
         ],
         out_specs=[
             pl.BlockSpec((tok, HEADS * VD), lambda g, i: (0, 0)),
-            pl.BlockSpec((tok, HEADS * VD), lambda g, i: (0, 0)),
+            pl.BlockSpec((tok // 2, HEADS * VD), lambda g, i: (0, 0)),
+            pl.BlockSpec((tok // 2, HEADS * VD), lambda g, i: (0, 0)),
             pl.BlockSpec((total, 1), lambda g, i: (0, 0)),
         ],
         scratch_shapes=[
@@ -126,11 +129,13 @@
         ],
     )
     shape = jax.ShapeDtypeStruct((tok, HEADS * VD), jnp.bfloat16)
+    half_shape = jax.ShapeDtypeStruct((tok // 2, HEADS * VD), jnp.bfloat16)
+    hits_shape = jax.ShapeDtypeStruct((total, 1), jnp.float32)
     work = HEADS * tok * total * CORES
     return pl.pallas_call(
         functools.partial(attention_kernel, tok=tok),
         grid_spec=grid_spec,
-        out_shape=[shape, shape, jax.ShapeDtypeStruct((total, 1), jnp.float32)],
+        out_shape=[shape, half_shape, half_shape, hits_shape],
         compiler_params=pltpu.CompilerParams(vmem_limit_bytes=56 << 20),
         cost_estimate=pl.CostEstimate(
             flops=2 * work * (2 * LAT + 2 * ROPE), bytes_accessed=8 << 20, transcendentals=work
@@ -199,7 +204,6 @@
     q_nope, q_rope, c_kv, k_rope, w_value, norm_gain, expert_ids, gate_fixed, w_gate, w_up, w_down
 ):
     tok = c_kv.shape[0]
-    half = tok // 2
     n_ctx = lax.axis_size("ctx")
     chips = n_ctx // CORES
     my_index = lax.axis_index("ctx")
@@ -224,8 +228,10 @@
 
     own, mine, other = lax.optimization_barrier(((w_gate[0], w_up[0], w_down[0]), mine, other))
     swapped = tuple(lax.ppermute(w, "ctx", siblings) for w in own)
-    values, normed, hits = attention(my_index, q_nope, q_rope, mine, other, w_value, norm_gain)
-    normed, swapped = lax.optimization_barrier((normed, swapped))
+    values, start_up, start_down, hits = attention(
+        my_index, q_nope, q_rope, mine, other, w_value, norm_gain
+    )
+    start, swapped = lax.optimization_barrier(((start_up, start_down), swapped))
     weights = (own[0], swapped[0], own[1], swapped[1], own[2], swapped[2])
 
     def part_of(rows, hop):
@@ -237,21 +243,21 @@
     def rounded(pair):
         return tuple(x.astype(jnp.bfloat16) for x in pair)
 
-    start = (normed[:half], normed[half:])
+    def after(pair, first):
+        return lax.optimization_barrier((pair, first))[0]
+
     rows = move(start)
-    home = part_of(start, 0)
-    rows, home = lax.optimization_barrier((rows, home))
     later = move(rows) if chips > 2 else None
     sums = rounded(part_of(rows, 1))
     for hop in range(1, chips):
+        arrived = move(sums)
         rows = later
         if hop + 2 < chips:
-            rows, sums = lax.optimization_barrier((rows, sums))
-            later = move(rows)
-        arrived = move(sums)
+            later = move(after(rows, sums))
         if hop + 1 < chips:
             part = part_of(rows, hop + 1)
             sums = rounded(tuple(p + a.astype(jnp.float32) for p, a in zip(part, arrived)))
+    home = part_of(after(start, sums), 0)
     expert_out = jnp.concatenate(
         [h + a.astype(jnp.float32) for h, a in zip(home, arrived)], axis=0
     )

time: 133 us -> 128 us (0.962)
  waiting for transfers between devices: 31.9 us -> 26.1 us
  starting transfers between devices: 39.9 us -> 41.7 us
    ppermute x14, waiting for transfers between devices: 7.22 us -> 0.69 us  [move(): lax.ppermute(pair[1], 'ctx', behind)]
    ppermute x14, starting transfers between devices: 13.5 us -> 17.5 us  [move(): lax.ppermute(pair[1], 'ctx', behind)]
    ppermute x14, starting transfers between devices: 14.3 us -> 12.1 us  [move(): lax.ppermute(pair[0], 'ctx', ahead)]
  transfers between devices with their start and end apart: 39 -> 39, of which waited for: 18 -> 15; matrix products, arithmetic and copies ran while one was open for 1% -> 1% of each run, Pallas kernels for 41% -> 43%
where the time goes in v4:
time: 128 us
  Pallas kernels  55.1 us (43%)
  starting transfers between devices  41.7 us (33%)
  waiting for transfers between devices  26.1 us (20%)
  other arithmetic  3.32 us (3%)
  local copies, waits for them, and re-layouts  1.4 us (1%)
    pallas_call x8, Pallas kernels, expert_part(): pl.pallas_call(functools.partial(expert_kernel, hop=hop, chips=chips), in...  42 us
    ppermute x14, waiting for transfers between devices, move(): lax.ppermute(pair[0], 'ctx', ahead)  18.8 us
    ppermute x14, starting transfers between devices, move(): lax.ppermute(pair[1], 'ctx', behind)  17.5 us
    pallas_call x1, Pallas kernels, attention(): pl.pallas_call(functools.partial(attention_kernel, tok=tok), grid_spec=gr...  13.1 us
    ppermute x14, starting transfers between devices, move(): lax.ppermute(pair[0], 'ctx', ahead)  12.1 us
    ppermute x7, starting transfers between devices, from_chip(): lax.ppermute(block, 'ctx', [(i, i ^ step * CORES) for i in range(n_ctx)])  11.4 us
    ppermute x7, waiting for transfers between devices, from_chip(): lax.ppermute(block, 'ctx', [(i, i ^ step * CORES) for i in range(n_ctx)])  4.54 us
  transfers between devices with their start and end apart: 39, of which 15 were waited for; matrix products, arithmetic and copies ran while one was open for 1% of the time, Pallas kernels for 43%

profile of v4, /device:TPU:0, one launch (start us, length us, event | category | flops | bytes accessed | tf_op | source)
XLA Modules:
  0.0 128.0 jit_solution(3911126365539238066)
XLA Ops:
  1.7 4.1 %collective-permute-start.3 = (bf16[64,640]{1,0:T(8,128)(2,1)S(1)}, bf16[64,640]{1,0:T(8,128)(2,1)S(1)}, u32[]{:S(2)}, u32[]{:S(2)}) collective-permute-start(bf16[64,640]{1,0:T(8,128)(2,1)S(1)} %get-tuple-element.89), channel_id=1, source_target_pairs={{0,8},{1,9},{2,10},{3,11},{4,12},{5,13},{6,14},{7,15},{8,0},{9,1},... | collective-permute-start | bytes 245768 | tf_op jit(solution)/shard_map/ppermute | solution.py:219
  5.8 1.5 %collective-permute-start = (bf16[64,640]{1,0:T(8,128)(2,1)S(1)}, bf16[64,640]{1,0:T(8,128)(2,1)S(1)}, u32[]{:S(2)}, u32[]{:S(2)}) collective-permute-start(bf16[64,640]{1,0:T(8,128)(2,1)S(1)} %get-tuple-element.89), channel_id=1, source_target_pairs={{0,2},{1,3},{2,0},{3,1},{4,6},{5,7},{6,4},{7,5},{8,10},{9,11},{10,... | collective-permute-start | bytes 245768 | tf_op jit(solution)/shard_map/ppermute | solution.py:219
  7.3 1.6 %collective-permute-start.1 = (bf16[64,640]{1,0:T(8,128)(2,1)S(1)}, bf16[64,640]{1,0:T(8,128)(2,1)S(1)}, u32[]{:S(2)}, u32[]{:S(2)}) collective-permute-start(bf16[64,640]{1,0:T(8,128)(2,1)S(1)} %get-tuple-element.89), channel_id=1, source_target_pairs={{0,4},{1,5},{2,6},{3,7},{4,0},{5,1},{6,2},{7,3},{8,12},{9,13},{10,... | collective-permute-start | bytes 245768 | tf_op jit(solution)/shard_map/ppermute | solution.py:219
  9.8 1.6 %collective-permute-start.4 = (bf16[64,640]{1,0:T(8,128)(2,1)S(1)}, bf16[64,640]{1,0:T(8,128)(2,1)S(1)}, u32[]{:S(2)}, u32[]{:S(2)}) collective-permute-start(bf16[64,640]{1,0:T(8,128)(2,1)S(1)} %collective-permute-done.3), channel_id=1, source_target_pairs={{0,2},{1,3},{2,0},{3,1},{4,6},{5,7},{6,4},{7,5},{8,10},{9,11},{10,... | collective-permute-start | bytes 245768 | tf_op jit(solution)/shard_map/ppermute | solution.py:219
  15.9 1.8 %collective-permute-done.6 = bf16[64,640]{1,0:T(8,128)(2,1)S(1)} collective-permute-done((bf16[64,640]{1,0:T(8,128)(2,1)S(1)}, bf16[64,640]{1,0:T(8,128)(2,1)S(1)}, u32[]{:S(2)}, u32[]{:S(2)}) %collective-permute-start.6) | collective-permute-done | bytes 81952 | tf_op jit(solution)/shard_map/ppermute | solution.py:219
  17.8 2.1 %collective-permute-done.7.other_ref = bf16[512,640]{1,0:T(8,128)(2,1)S(1)} collective-permute-done((bf16[512,640]{1,0:T(8,128)(2,1)S(1)}, bf16[512,640]{1,0:T(8,128)(2,1)S(1)}, u32[]{:S(2)}, u32[]{:S(2)}) %collective-permute-start.7) | collective-permute-done | bytes 655392 | tf_op jit(solution)/shard_map/ppermute | solution.py:227
  20.8 13.1 %shard_map.109 = (bf16[64,4096]{1,0:T(8,128)(2,1)}, bf16[32,4096]{1,0:T(8,128)(2,1)}, bf16[32,4096]{1,0:T(8,128)(2,1)}, f32[512,1]{1,0:T(8,128)}) custom-call(s32[1]{0:T(128)} %bitcast.index_ref, bf16[64,16384]{1,0:T(8,128)(2,1)} %q_ref.1, bf16[64,2048]{1,0:T(8,128)(2,1)} %qr_ref.1, bf16[512,640]{1,0:T(8,128)(2,1)} %copy-done.8, bf16[512,640]{1,0:T(8,128)(2,1)} %copy-done.9, ...), custom_call_target="tpu_custom_call" | custom-call | flops 4831838208 | bytes 8388608 | tf_op jit(solution)/shard_map/pallas_call | solution.py:135
  36.0 6.6 %collective-permute-done.11.up_rows = bf16[32,4096]{1,0:T(8,128)(2,1)S(1)} collective-permute-done((bf16[32,4096]{1,0:T(8,128)(2,1)}, bf16[32,4096]{1,0:T(8,128)(2,1)S(1)}, u32[]{:S(2)}, u32[]{:S(2)}) %collective-permute-start.11) | collective-permute-done | bytes 262176 | tf_op jit(solution)/shard_map/ppermute | solution.py:241
  42.5 1.4 %collective-permute-start.12 = (bf16[32,4096]{1,0:T(8,128)(2,1)S(1)}, bf16[32,4096]{1,0:T(8,128)(2,1)S(1)}, u32[]{:S(2)}, u32[]{:S(2)}) collective-permute-start(bf16[32,4096]{1,0:T(8,128)(2,1)S(1)} %collective-permute-done.11.up_rows), channel_id=1, source_target_pairs={{0,4},{1,5},{4,8},{5,9},{8,12},{9,13},{12,14},{13,15},{14,10},{15,... | collective-permute-start | bytes 786440 | tf_op jit(solution)/shard_map/ppermute | solution.py:241
  45.5 5.3 %shard_map.110 = (f32[32,4096]{1,0:T(8,128)S(1)}, f32[32,4096]{1,0:T(8,128)S(1)}) custom-call(s32[1]{0:T(128)} %bitcast.index_ref, bf16[32,4096]{1,0:T(8,128)(2,1)S(1)} %collective-permute-done.11.up_rows, bf16[32,4096]{1,0:T(8,128)(2,1)S(1)} %collective-permute-done.13.down_rows, f32[512,1]{1,0:T(8,128)S(1)} %copy-done.3, bf16[4096,256]{1,0:T(8,128)(2,1)S(1)} %bitcast.10, ...), custom_call_target="tpu_custom_call" | custom-call | flops 805306368 | bytes 14680064 | tf_op jit(solution)/shard_map/pallas_call | solution.py:190
  51.5 1.4 %collective-permute-start.17 = (bf16[32,4096]{1,0:T(8,128)(2,1)S(1)}, bf16[32,4096]{1,0:T(8,128)(2,1)S(1)}, u32[]{:S(2)}, u32[]{:S(2)}) collective-permute-start(bf16[32,4096]{1,0:T(8,128)(2,1)S(1)} %convert_element_type.99), channel_id=1, source_target_pairs={{0,4},{1,5},{4,8},{5,9},{8,12},{9,13},{12,14},{13,15},{14,10},{15,... | collective-permute-start | bytes 786440 | tf_op jit(solution)/shard_map/ppermute | solution.py:241
  53.0 1.8 %collective-permute-start.15 = (bf16[32,4096]{1,0:T(8,128)(2,1)S(1)}, bf16[32,4096]{1,0:T(8,128)(2,1)S(1)}, u32[]{:S(2)}, u32[]{:S(2)}) collective-permute-start(bf16[32,4096]{1,0:T(8,128)(2,1)S(1)} %collective-permute-done.12.up_rows), channel_id=1, source_target_pairs={{0,4},{1,5},{4,8},{5,9},{8,12},{9,13},{12,14},{13,15},{14,10},{15,... | collective-permute-start | bytes 786440 | tf_op jit(solution)/shard_map/ppermute | solution.py:241
  55.0 5.2 %shard_map.111 = (f32[32,4096]{1,0:T(8,128)S(1)}, f32[32,4096]{1,0:T(8,128)S(1)}) custom-call(s32[1]{0:T(128)} %bitcast.index_ref, bf16[32,4096]{1,0:T(8,128)(2,1)S(1)} %collective-permute-done.12.up_rows, bf16[32,4096]{1,0:T(8,128)(2,1)S(1)} %collective-permute-done.14.down_rows, f32[512,1]{1,0:T(8,128)S(1)} %copy-done.3, bf16[4096,256]{1,0:T(8,128)(2,1)S(1)} %bitcast.11, ...), custom_call_target="tpu_custom_call" | custom-call | flops 805306368 | bytes 14680064 | tf_op jit(solution)/shard_map/pallas_call | solution.py:190
  62.5 3.9 %collective-permute-done.15.up_rows = bf16[32,4096]{1,0:T(8,128)(2,1)S(1)} collective-permute-done((bf16[32,4096]{1,0:T(8,128)(2,1)S(1)}, bf16[32,4096]{1,0:T(8,128)(2,1)S(1)}, u32[]{:S(2)}, u32[]{:S(2)}) %collective-permute-start.15) | collective-permute-done | bytes 262176 | tf_op jit(solution)/shard_map/ppermute | solution.py:241
  66.5 1.4 %collective-permute-start.19 = (bf16[32,4096]{1,0:T(8,128)(2,1)S(1)}, bf16[32,4096]{1,0:T(8,128)(2,1)S(1)}, u32[]{:S(2)}, u32[]{:S(2)}) collective-permute-start(bf16[32,4096]{1,0:T(8,128)(2,1)S(1)} %collective-permute-done.15.up_rows), channel_id=1, source_target_pairs={{0,4},{1,5},{4,8},{5,9},{8,12},{9,13},{12,14},{13,15},{14,10},{15,... | collective-permute-start | bytes 786440 | tf_op jit(solution)/shard_map/ppermute | solution.py:241
  68.5 5.2 %shard_map.112 = (f32[32,4096]{1,0:T(8,128)S(1)}, f32[32,4096]{1,0:T(8,128)S(1)}) custom-call(s32[1]{0:T(128)} %bitcast.index_ref, bf16[32,4096]{1,0:T(8,128)(2,1)S(1)} %collective-permute-done.15.up_rows, bf16[32,4096]{1,0:T(8,128)(2,1)S(1)} %collective-permute-done.16.down_rows, f32[512,1]{1,0:T(8,128)S(1)} %copy-done.3, bf16[4096,256]{1,0:T(8,128)(2,1)S(1)} %bitcast.12, ...), custom_call_target="tpu_custom_call" | custom-call | flops 805306368 | bytes 14680064 | tf_op jit(solution)/shard_map/pallas_call | solution.py:190
  73.8 2.1 %collective-permute-start.26 = (bf16[32,4096]{1,0:T(8,128)(2,1)S(1)}, bf16[32,4096]{1,0:T(8,128)(2,1)S(1)}, u32[]{:S(2)}, u32[]{:S(2)}) collective-permute-start(bf16[32,4096]{1,0:T(8,128)(2,1)S(1)} %add_convert_fusion.8), channel_id=1, source_target_pairs={{4,0},{5,1},{8,4},{9,5},{12,8},{13,9},{14,12},{15,13},{10,14},{11,... | collective-permute-start | bytes 786440 | tf_op jit(solution)/shard_map/ppermute | solution.py:241
  76.0 1.7 %collective-permute-done.19.up_rows = bf16[32,4096]{1,0:T(8,128)(2,1)S(1)} collective-permute-done((bf16[32,4096]{1,0:T(8,128)(2,1)S(1)}, bf16[32,4096]{1,0:T(8,128)(2,1)S(1)}, u32[]{:S(2)}, u32[]{:S(2)}) %collective-permute-start.19) | collective-permute-done | bytes 262176 | tf_op jit(solution)/shard_map/ppermute | solution.py:241
  77.7 1.4 %collective-permute-start.23 = (bf16[32,4096]{1,0:T(8,128)(2,1)S(1)}, bf16[32,4096]{1,0:T(8,128)(2,1)S(1)}, u32[]{:S(2)}, u32[]{:S(2)}) collective-permute-start(bf16[32,4096]{1,0:T(8,128)(2,1)S(1)} %collective-permute-done.19.up_rows), channel_id=1, source_target_pairs={{0,4},{1,5},{4,8},{5,9},{8,12},{9,13},{12,14},{13,15},{14,10},{15,... | collective-permute-start | bytes 786440 | tf_op jit(solution)/shard_map/ppermute | solution.py:241
  79.7 5.2 %shard_map.113 = (f32[32,4096]{1,0:T(8,128)S(1)}, f32[32,4096]{1,0:T(8,128)S(1)}) custom-call(s32[1]{0:T(128)} %bitcast.index_ref, bf16[32,4096]{1,0:T(8,128)(2,1)S(1)} %collective-permute-done.19.up_rows, bf16[32,4096]{1,0:T(8,128)(2,1)S(1)} %collective-permute-done.20.down_rows, f32[512,1]{1,0:T(8,128)S(1)} %copy-done.3, bf16[4096,256]{1,0:T(8,128)(2,1)S(1)} %bitcast.13, ...), custom_call_target="tpu_custom_call" | custom-call | flops 805306368 | bytes 14680064 | tf_op jit(solution)/shard_map/pallas_call | solution.py:190
  85.0 2.1 %collective-permute-start.30 = (bf16[32,4096]{1,0:T(8,128)(2,1)S(1)}, bf16[32,4096]{1,0:T(8,128)(2,1)S(1)}, u32[]{:S(2)}, u32[]{:S(2)}) collective-permute-start(bf16[32,4096]{1,0:T(8,128)(2,1)S(1)} %add_convert_fusion.6), channel_id=1, source_target_pairs={{4,0},{5,1},{8,4},{9,5},{12,8},{13,9},{14,12},{15,13},{10,14},{11,... | collective-permute-start | bytes 786440 | tf_op jit(solution)/shard_map/ppermute | solution.py:241
  87.2 2.0 %collective-permute-done.23.up_rows = bf16[32,4096]{1,0:T(8,128)(2,1)S(1)} collective-permute-done((bf16[32,4096]{1,0:T(8,128)(2,1)S(1)}, bf16[32,4096]{1,0:T(8,128)(2,1)S(1)}, u32[]{:S(2)}, u32[]{:S(2)}) %collective-permute-start.23) | collective-permute-done | bytes 262176 | tf_op jit(solution)/shard_map/ppermute | solution.py:241
  89.3 1.6 %collective-permute-start.27 = (bf16[32,4096]{1,0:T(8,128)(2,1)S(1)}, bf16[32,4096]{1,0:T(8,128)(2,1)S(1)}, u32[]{:S(2)}, u32[]{:S(2)}) collective-permute-start(bf16[32,4096]{1,0:T(8,128)(2,1)S(1)} %collective-permute-done.23.up_rows), channel_id=1, source_target_pairs={{0,4},{1,5},{4,8},{5,9},{8,12},{9,13},{12,14},{13,15},{14,10},{15,... | collective-permute-start | bytes 786440 | tf_op jit(solution)/shard_map/ppermute | solution.py:241
  91.7 5.3 %shard_map.114 = (f32[32,4096]{1,0:T(8,128)S(1)}, f32[32,4096]{1,0:T(8,128)S(1)}) custom-call(s32[1]{0:T(128)} %bitcast.index_ref, bf16[32,4096]{1,0:T(8,128)(2,1)S(1)} %collective-permute-done.23.up_rows, bf16[32,4096]{1,0:T(8,128)(2,1)S(1)} %collective-permute-done.24.down_rows, f32[512,1]{1,0:T(8,128)S(1)} %copy-done.3, bf16[4096,256]{1,0:T(8,128)(2,1)S(1)} %bitcast.14, ...), custom_call_target="tpu_custom_call" | custom-call | flops 805306368 | bytes 14680064 | tf_op jit(solution)/shard_map/pallas_call | solution.py:190
  97.0 2.1 %collective-permute-start.35 = (bf16[32,4096]{1,0:T(8,128)(2,1)S(1)}, bf16[32,4096]{1,0:T(8,128)(2,1)S(1)}, u32[]{:S(2)}, u32[]{:S(2)}) collective-permute-start(bf16[32,4096]{1,0:T(8,128)(2,1)S(1)} %add_convert_fusion.4), channel_id=1, source_target_pairs={{4,0},{5,1},{8,4},{9,5},{12,8},{13,9},{14,12},{15,13},{10,14},{11,... | collective-permute-start | bytes 786440 | tf_op jit(solution)/shard_map/ppermute | solution.py:241
  99.2 2.9 %collective-permute-done.27.up_rows = bf16[32,4096]{1,0:T(8,128)(2,1)S(1)} collective-permute-done((bf16[32,4096]{1,0:T(8,128)(2,1)S(1)}, bf16[32,4096]{1,0:T(8,128)(2,1)S(1)}, u32[]{:S(2)}, u32[]{:S(2)}) %collective-permute-start.27) | collective-permute-done | bytes 262176 | tf_op jit(solution)/shard_map/ppermute | solution.py:241
  102.1 2.0 %collective-permute-start.32 = (bf16[32,4096]{1,0:T(8,128)(2,1)S(1)}, bf16[32,4096]{1,0:T(8,128)(2,1)S(1)}, u32[]{:S(2)}, u32[]{:S(2)}) collective-permute-start(bf16[32,4096]{1,0:T(8,128)(2,1)S(1)} %collective-permute-done.28.down_rows), channel_id=1, source_target_pairs={{4,0},{5,1},{8,4},{9,5},{12,8},{13,9},{14,12},{15,13},{10,14},{11,... | collective-permute-start | bytes 786440 | tf_op jit(solution)/shard_map/ppermute | solution.py:241
  104.1 5.3 %shard_map.116 = (f32[32,4096]{1,0:T(8,128)S(1)}, f32[32,4096]{1,0:T(8,128)S(1)}) custom-call(s32[1]{0:T(128)} %bitcast.index_ref, bf16[32,4096]{1,0:T(8,128)(2,1)S(1)} %collective-permute-done.27.up_rows, bf16[32,4096]{1,0:T(8,128)(2,1)S(1)} %collective-permute-done.28.down_rows, f32[512,1]{1,0:T(8,128)S(1)} %copy-done.3, bf16[4096,256]{1,0:T(8,128)(2,1)S(1)} %bitcast.15, ...), custom_call_target="tpu_custom_call" | custom-call | flops 805306368 | bytes 14680064 | tf_op jit(solution)/shard_map/pallas_call | solution.py:190
  109.4 1.8 %collective-permute-start.36 = (bf16[32,4096]{1,0:T(8,128)(2,1)S(1)}, bf16[32,4096]{1,0:T(8,128)(2,1)S(1)}, u32[]{:S(2)}, u32[]{:S(2)}) collective-permute-start(bf16[32,4096]{1,0:T(8,128)(2,1)S(1)} %add_convert_fusion.1), channel_id=1, source_target_pairs={{4,0},{5,1},{8,4},{9,5},{12,8},{13,9},{14,12},{15,13},{10,14},{11,... | collective-permute-start | bytes 786440 | tf_op jit(solution)/shard_map/ppermute | solution.py:241
  112.3 5.3 %shard_map.115 = (f32[32,4096]{1,0:T(8,128)S(1)}, f32[32,4096]{1,0:T(8,128)S(1)}) custom-call(s32[1]{0:T(128)} %bitcast.index_ref, bf16[32,4096]{1,0:T(8,128)(2,1)S(1)} %collective-permute-done.31.up_rows, bf16[32,4096]{1,0:T(8,128)(2,1)S(1)} %collective-permute-done.32.down_rows, f32[512,1]{1,0:T(8,128)S(1)} %copy-done.3, bf16[4096,256]{1,0:T(8,128)(2,1)S(1)} %bitcast.16, ...), custom_call_target="tpu_custom_call" | custom-call | flops 805306368 | bytes 14680064 | tf_op jit(solution)/shard_map/pallas_call | solution.py:190
  117.9 2.5 %collective-permute-start.38 = (bf16[32,4096]{1,0:T(8,128)(2,1)S(1)}, bf16[32,4096]{1,0:T(8,128)(2,1)S(1)}, u32[]{:S(2)}, u32[]{:S(2)}) collective-permute-start(bf16[32,4096]{1,0:T(8,128)(2,1)S(1)} %add_convert_fusion), channel_id=1, source_target_pairs={{4,0},{5,1},{8,4},{9,5},{12,8},{13,9},{14,12},{15,13},{10,14},{11,... | collective-permute-start | bytes 786440 | tf_op jit(solution)/shard_map/ppermute | solution.py:241
  120.6 5.3 %shard_map.117 = (f32[32,4096]{1,0:T(8,128)S(1)}, f32[32,4096]{1,0:T(8,128)S(1)}) custom-call(s32[1]{0:T(128)} %bitcast.index_ref, bf16[32,4096]{1,0:T(8,128)(2,1)S(1)} %copy-done.5, bf16[32,4096]{1,0:T(8,128)(2,1)S(1)} %copy-done.6, f32[512,1]{1,0:T(8,128)S(1)} %copy-done.4, bf16[4096,256]{1,0:T(8,128)(2,1)S(1)} %bitcast.17, ...), custom_call_target="tpu_custom_call" | custom-call | flops 805306368 | bytes 14680064 | tf_op jit(solution)/shard_map/pallas_call | solution.py:190
  (105 shorter events, 21.2 us)
Async XLA Ops:
  1.7 8.1 %collective-permute-start.3 = (bf16[64,640]{1,0:T(8,128)(2,1)S(1)}, bf16[64,640]{1,0:T(8,128)(2,1)S(1)}, u32[]{:S(2)}, u32[]{:S(2)}) collective-permute-start(bf16[64,640]{1,0:T(8,128)(2,1)S(1)} %get-tuple-element.89), channel_id=1, source_target_pairs={{0,8},{1,9},{2,10},{3,11},{4,12},{5,13},{6,14},{7,15},{8,0},{9,1},... | collective-permute-start | bytes 245768 | tf_op jit(solution)/shard_map/ppermute | solution.py:219
  5.8 6.6 %collective-permute-start = (bf16[64,640]{1,0:T(8,128)(2,1)S(1)}, bf16[64,640]{1,0:T(8,128)(2,1)S(1)}, u32[]{:S(2)}, u32[]{:S(2)}) collective-permute-start(bf16[64,640]{1,0:T(8,128)(2,1)S(1)} %get-tuple-element.89), channel_id=1, source_target_pairs={{0,2},{1,3},{2,0},{3,1},{4,6},{5,7},{6,4},{7,5},{8,10},{9,11},{10,... | collective-permute-start | bytes 245768 | tf_op jit(solution)/shard_map/ppermute | solution.py:219
  19.9 14.0 %collective-permute-start.8 = (bf16[4096,256]{1,0:T(8,128)(2,1)}, bf16[4096,256]{1,0:T(8,128)(2,1)}, u32[]{:S(2)}, u32[]{:S(2)}) collective-permute-start(bf16[4096,256]{1,0:T(8,128)(2,1)} %bitcast.9), channel_id=1, source_target_pairs={{0,1},{1,0},{2,3},{3,2},{4,5},{5,4},{6,7},{7,6},{8,9},{9,8},{10,11... | collective-permute-start | bytes 6291464 | tf_op jit(solution)/shard_map/ppermute | solution.py:230
  20.0 13.8 %collective-permute-start.9 = (bf16[4096,256]{1,0:T(8,128)(2,1)}, bf16[4096,256]{1,0:T(8,128)(2,1)}, u32[]{:S(2)}, u32[]{:S(2)}) collective-permute-start(bf16[4096,256]{1,0:T(8,128)(2,1)} %bitcast.18), channel_id=1, source_target_pairs={{0,1},{1,0},{2,3},{3,2},{4,5},{5,4},{6,7},{7,6},{8,9},{9,8},{10,11... | collective-permute-start | bytes 6291464 | tf_op jit(solution)/shard_map/ppermute | solution.py:230
  20.4 13.5 %collective-permute-start.10 = (bf16[256,4096]{1,0:T(8,128)(2,1)}, bf16[256,4096]{1,0:T(8,128)(2,1)}, u32[]{:S(2)}, u32[]{:S(2)}) collective-permute-start(bf16[256,4096]{1,0:T(8,128)(2,1)} %bitcast.27), channel_id=1, source_target_pairs={{0,1},{1,0},{2,3},{3,2},{4,5},{5,4},{6,7},{7,6},{8,9},{9,8},{10,11... | collective-permute-start | bytes 6291464 | tf_op jit(solution)/shard_map/ppermute | solution.py:230
  33.9 8.6 %collective-permute-start.11 = (bf16[32,4096]{1,0:T(8,128)(2,1)}, bf16[32,4096]{1,0:T(8,128)(2,1)S(1)}, u32[]{:S(2)}, u32[]{:S(2)}) collective-permute-start(bf16[32,4096]{1,0:T(8,128)(2,1)} %get-tuple-element.85.up_rows), channel_id=1, source_target_pairs={{0,4},{1,5},{4,8},{5,9},{8,12},{9,13},{12,14},{13,15},{14,10},{15,... | collective-permute-start | bytes 786440 | tf_op jit(solution)/shard_map/ppermute | solution.py:241
  35.0 9.3 %collective-permute-start.13 = (bf16[32,4096]{1,0:T(8,128)(2,1)}, bf16[32,4096]{1,0:T(8,128)(2,1)S(1)}, u32[]{:S(2)}, u32[]{:S(2)}) collective-permute-start(bf16[32,4096]{1,0:T(8,128)(2,1)} %get-tuple-element.86.down_rows), channel_id=1, source_target_pairs={{4,0},{5,1},{8,4},{9,5},{12,8},{13,9},{14,12},{15,13},{10,14},{11,... | collective-permute-start | bytes 786440 | tf_op jit(solution)/shard_map/ppermute | solution.py:241
  42.5 10.5 %collective-permute-start.12 = (bf16[32,4096]{1,0:T(8,128)(2,1)S(1)}, bf16[32,4096]{1,0:T(8,128)(2,1)S(1)}, u32[]{:S(2)}, u32[]{:S(2)}) collective-permute-start(bf16[32,4096]{1,0:T(8,128)(2,1)S(1)} %collective-permute-done.11.up_rows), channel_id=1, source_target_pairs={{0,4},{1,5},{4,8},{5,9},{8,12},{9,13},{12,14},{13,15},{14,10},{15,... | collective-permute-start | bytes 786440 | tf_op jit(solution)/shard_map/ppermute | solution.py:241
  44.3 8.7 %collective-permute-start.14 = (bf16[32,4096]{1,0:T(8,128)(2,1)S(1)}, bf16[32,4096]{1,0:T(8,128)(2,1)S(1)}, u32[]{:S(2)}, u32[]{:S(2)}) collective-permute-start(bf16[32,4096]{1,0:T(8,128)(2,1)S(1)} %collective-permute-done.13.down_rows), channel_id=1, source_target_pairs={{4,0},{5,1},{8,4},{9,5},{12,8},{13,9},{14,12},{15,13},{10,14},{11,... | collective-permute-start | bytes 786440 | tf_op jit(solution)/shard_map/ppermute | solution.py:241
  50.8 9.5 %collective-permute-start.18 = (bf16[32,4096]{1,0:T(8,128)(2,1)S(1)}, bf16[32,4096]{1,0:T(8,128)(2,1)S(1)}, u32[]{:S(2)}, u32[]{:S(2)}) collective-permute-start(bf16[32,4096]{1,0:T(8,128)(2,1)S(1)} %convert_element_type.100), channel_id=1, source_target_pairs={{4,0},{5,1},{8,4},{9,5},{12,8},{13,9},{14,12},{15,13},{10,14},{11,... | collective-permute-start | bytes 786440 | tf_op jit(solution)/shard_map/ppermute | solution.py:241
  51.5 9.6 %collective-permute-start.17 = (bf16[32,4096]{1,0:T(8,128)(2,1)S(1)}, bf16[32,4096]{1,0:T(8,128)(2,1)S(1)}, u32[]{:S(2)}, u32[]{:S(2)}) collective-permute-start(bf16[32,4096]{1,0:T(8,128)(2,1)S(1)} %convert_element_type.99), channel_id=1, source_target_pairs={{0,4},{1,5},{4,8},{5,9},{8,12},{9,13},{12,14},{13,15},{14,10},{15,... | collective-permute-start | bytes 786440 | tf_op jit(solution)/shard_map/ppermute | solution.py:241
  53.0 13.5 %collective-permute-start.15 = (bf16[32,4096]{1,0:T(8,128)(2,1)S(1)}, bf16[32,4096]{1,0:T(8,128)(2,1)S(1)}, u32[]{:S(2)}, u32[]{:S(2)}) collective-permute-start(bf16[32,4096]{1,0:T(8,128)(2,1)S(1)} %collective-permute-done.12.up_rows), channel_id=1, source_target_pairs={{0,4},{1,5},{4,8},{5,9},{8,12},{9,13},{12,14},{13,15},{14,10},{15,... | collective-permute-start | bytes 786440 | tf_op jit(solution)/shard_map/ppermute | solution.py:241
  54.8 11.7 %collective-permute-start.16 = (bf16[32,4096]{1,0:T(8,128)(2,1)S(1)}, bf16[32,4096]{1,0:T(8,128)(2,1)S(1)}, u32[]{:S(2)}, u32[]{:S(2)}) collective-permute-start(bf16[32,4096]{1,0:T(8,128)(2,1)S(1)} %collective-permute-done.14.down_rows), channel_id=1, source_target_pairs={{4,0},{5,1},{8,4},{9,5},{12,8},{13,9},{14,12},{15,13},{10,14},{11,... | collective-permute-start | bytes 786440 | tf_op jit(solution)/shard_map/ppermute | solution.py:241
  60.3 13.4 %collective-permute-start.22 = (bf16[32,4096]{1,0:T(8,128)(2,1)S(1)}, bf16[32,4096]{1,0:T(8,128)(2,1)S(1)}, u32[]{:S(2)}, u32[]{:S(2)}) collective-permute-start(bf16[32,4096]{1,0:T(8,128)(2,1)S(1)} %add_convert_fusion.10), channel_id=1, source_target_pairs={{4,0},{5,1},{8,4},{9,5},{12,8},{13,9},{14,12},{15,13},{10,14},{11,... | collective-permute-start | bytes 786440 | tf_op jit(solution)/shard_map/ppermute | solution.py:241
  61.2 14.7 %collective-permute-start.21 = (bf16[32,4096]{1,0:T(8,128)(2,1)S(1)}, bf16[32,4096]{1,0:T(8,128)(2,1)S(1)}, u32[]{:S(2)}, u32[]{:S(2)}) collective-permute-start(bf16[32,4096]{1,0:T(8,128)(2,1)S(1)} %add_convert_fusion.11), channel_id=1, source_target_pairs={{0,4},{1,5},{4,8},{5,9},{8,12},{9,13},{12,14},{13,15},{14,10},{15,... | collective-permute-start | bytes 786440 | tf_op jit(solution)/shard_map/ppermute | solution.py:241
  66.5 11.2 %collective-permute-start.19 = (bf16[32,4096]{1,0:T(8,128)(2,1)S(1)}, bf16[32,4096]{1,0:T(8,128)(2,1)S(1)}, u32[]{:S(2)}, u32[]{:S(2)}) collective-permute-start(bf16[32,4096]{1,0:T(8,128)(2,1)S(1)} %collective-permute-done.15.up_rows), channel_id=1, source_target_pairs={{0,4},{1,5},{4,8},{5,9},{8,12},{9,13},{12,14},{13,15},{14,10},{15,... | collective-permute-start | bytes 786440 | tf_op jit(solution)/shard_map/ppermute | solution.py:241
  67.8 9.9 %collective-permute-start.20 = (bf16[32,4096]{1,0:T(8,128)(2,1)S(1)}, bf16[32,4096]{1,0:T(8,128)(2,1)S(1)}, u32[]{:S(2)}, u32[]{:S(2)}) collective-permute-start(bf16[32,4096]{1,0:T(8,128)(2,1)S(1)} %collective-permute-done.16.down_rows), channel_id=1, source_target_pairs={{4,0},{5,1},{8,4},{9,5},{12,8},{13,9},{14,12},{15,13},{10,14},{11,... | collective-permute-start | bytes 786440 | tf_op jit(solution)/shard_map/ppermute | solution.py:241
  73.8 11.2 %collective-permute-start.26 = (bf16[32,4096]{1,0:T(8,128)(2,1)S(1)}, bf16[32,4096]{1,0:T(8,128)(2,1)S(1)}, u32[]{:S(2)}, u32[]{:S(2)}) collective-permute-start(bf16[32,4096]{1,0:T(8,128)(2,1)S(1)} %add_convert_fusion.8), channel_id=1, source_target_pairs={{4,0},{5,1},{8,4},{9,5},{12,8},{13,9},{14,12},{15,13},{10,14},{11,... | collective-permute-start | bytes 786440 | tf_op jit(solution)/shard_map/ppermute | solution.py:241
  75.9 11.2 %collective-permute-start.25 = (bf16[32,4096]{1,0:T(8,128)(2,1)S(1)}, bf16[32,4096]{1,0:T(8,128)(2,1)S(1)}, u32[]{:S(2)}, u32[]{:S(2)}) collective-permute-start(bf16[32,4096]{1,0:T(8,128)(2,1)S(1)} %add_convert_fusion.9), channel_id=1, source_target_pairs={{0,4},{1,5},{4,8},{5,9},{8,12},{9,13},{12,14},{13,15},{14,10},{15,... | collective-permute-start | bytes 786440 | tf_op jit(solution)/shard_map/ppermute | solution.py:241
  77.7 11.6 %collective-permute-start.23 = (bf16[32,4096]{1,0:T(8,128)(2,1)S(1)}, bf16[32,4096]{1,0:T(8,128)(2,1)S(1)}, u32[]{:S(2)}, u32[]{:S(2)}) collective-permute-start(bf16[32,4096]{1,0:T(8,128)(2,1)S(1)} %collective-permute-done.19.up_rows), channel_id=1, source_target_pairs={{0,4},{1,5},{4,8},{5,9},{8,12},{9,13},{12,14},{13,15},{14,10},{15,... | collective-permute-start | bytes 786440 | tf_op jit(solution)/shard_map/ppermute | solution.py:241
  79.1 10.2 %collective-permute-start.24 = (bf16[32,4096]{1,0:T(8,128)(2,1)S(1)}, bf16[32,4096]{1,0:T(8,128)(2,1)S(1)}, u32[]{:S(2)}, u32[]{:S(2)}) collective-permute-start(bf16[32,4096]{1,0:T(8,128)(2,1)S(1)} %collective-permute-done.20.down_rows), channel_id=1, source_target_pairs={{4,0},{5,1},{8,4},{9,5},{12,8},{13,9},{14,12},{15,13},{10,14},{11,... | collective-permute-start | bytes 786440 | tf_op jit(solution)/shard_map/ppermute | solution.py:241
  85.0 11.9 %collective-permute-start.30 = (bf16[32,4096]{1,0:T(8,128)(2,1)S(1)}, bf16[32,4096]{1,0:T(8,128)(2,1)S(1)}, u32[]{:S(2)}, u32[]{:S(2)}) collective-permute-start(bf16[32,4096]{1,0:T(8,128)(2,1)S(1)} %add_convert_fusion.6), channel_id=1, source_target_pairs={{4,0},{5,1},{8,4},{9,5},{12,8},{13,9},{14,12},{15,13},{10,14},{11,... | collective-permute-start | bytes 786440 | tf_op jit(solution)/shard_map/ppermute | solution.py:241
  87.2 11.9 %collective-permute-start.29 = (bf16[32,4096]{1,0:T(8,128)(2,1)S(1)}, bf16[32,4096]{1,0:T(8,128)(2,1)S(1)}, u32[]{:S(2)}, u32[]{:S(2)}) collective-permute-start(bf16[32,4096]{1,0:T(8,128)(2,1)S(1)} %add_convert_fusion.7), channel_id=1, source_target_pairs={{0,4},{1,5},{4,8},{5,9},{8,12},{9,13},{12,14},{13,15},{14,10},{15,... | collective-permute-start | bytes 786440 | tf_op jit(solution)/shard_map/ppermute | solution.py:241
  89.3 12.8 %collective-permute-start.27 = (bf16[32,4096]{1,0:T(8,128)(2,1)S(1)}, bf16[32,4096]{1,0:T(8,128)(2,1)S(1)}, u32[]{:S(2)}, u32[]{:S(2)}) collective-permute-start(bf16[32,4096]{1,0:T(8,128)(2,1)S(1)} %collective-permute-done.23.up_rows), channel_id=1, source_target_pairs={{0,4},{1,5},{4,8},{5,9},{8,12},{9,13},{12,14},{13,15},{14,10},{15,... | collective-permute-start | bytes 786440 | tf_op jit(solution)/shard_map/ppermute | solution.py:241
  90.9 11.2 %collective-permute-start.28 = (bf16[32,4096]{1,0:T(8,128)(2,1)S(1)}, bf16[32,4096]{1,0:T(8,128)(2,1)S(1)}, u32[]{:S(2)}, u32[]{:S(2)}) collective-permute-start(bf16[32,4096]{1,0:T(8,128)(2,1)S(1)} %collective-permute-done.24.down_rows), channel_id=1, source_target_pairs={{4,0},{5,1},{8,4},{9,5},{12,8},{13,9},{14,12},{15,13},{10,14},{11,... | collective-permute-start | bytes 786440 | tf_op jit(solution)/shard_map/ppermute | solution.py:241
  97.0 12.4 %collective-permute-start.35 = (bf16[32,4096]{1,0:T(8,128)(2,1)S(1)}, bf16[32,4096]{1,0:T(8,128)(2,1)S(1)}, u32[]{:S(2)}, u32[]{:S(2)}) collective-permute-start(bf16[32,4096]{1,0:T(8,128)(2,1)S(1)} %add_convert_fusion.4), channel_id=1, source_target_pairs={{4,0},{5,1},{8,4},{9,5},{12,8},{13,9},{14,12},{15,13},{10,14},{11,... | collective-permute-start | bytes 786440 | tf_op jit(solution)/shard_map/ppermute | solution.py:241
  99.1 12.1 %collective-permute-start.33 = (bf16[32,4096]{1,0:T(8,128)(2,1)S(1)}, bf16[32,4096]{1,0:T(8,128)(2,1)S(1)}, u32[]{:S(2)}, u32[]{:S(2)}) collective-permute-start(bf16[32,4096]{1,0:T(8,128)(2,1)S(1)} %add_convert_fusion.5), channel_id=1, source_target_pairs={{0,4},{1,5},{4,8},{5,9},{8,12},{9,13},{12,14},{13,15},{14,10},{15,... | collective-permute-start | bytes 786440 | tf_op jit(solution)/shard_map/ppermute | solution.py:241
  102.1 10.2 %collective-permute-start.31 = (bf16[32,4096]{1,0:T(8,128)(2,1)S(1)}, bf16[32,4096]{1,0:T(8,128)(2,1)S(1)}, u32[]{:S(2)}, u32[]{:S(2)}) collective-permute-start(bf16[32,4096]{1,0:T(8,128)(2,1)S(1)} %collective-permute-done.27.up_rows), channel_id=1, source_target_pairs={{0,4},{1,5},{4,8},{5,9},{8,12},{9,13},{12,14},{13,15},{14,10},{15,... | collective-permute-start | bytes 786440 | tf_op jit(solution)/shard_map/ppermute | solution.py:241
  102.1 10.2 %collective-permute-start.32 = (bf16[32,4096]{1,0:T(8,128)(2,1)S(1)}, bf16[32,4096]{1,0:T(8,128)(2,1)S(1)}, u32[]{:S(2)}, u32[]{:S(2)}) collective-permute-start(bf16[32,4096]{1,0:T(8,128)(2,1)S(1)} %collective-permute-done.28.down_rows), channel_id=1, source_target_pairs={{4,0},{5,1},{8,4},{9,5},{12,8},{13,9},{14,12},{15,13},{10,14},{11,... | collective-permute-start | bytes 786440 | tf_op jit(solution)/shard_map/ppermute | solution.py:241
  109.4 8.4 %collective-permute-start.36 = (bf16[32,4096]{1,0:T(8,128)(2,1)S(1)}, bf16[32,4096]{1,0:T(8,128)(2,1)S(1)}, u32[]{:S(2)}, u32[]{:S(2)}) collective-permute-start(bf16[32,4096]{1,0:T(8,128)(2,1)S(1)} %add_convert_fusion.1), channel_id=1, source_target_pairs={{4,0},{5,1},{8,4},{9,5},{12,8},{13,9},{14,12},{15,13},{10,14},{11,... | collective-permute-start | bytes 786440 | tf_op jit(solution)/shard_map/ppermute | solution.py:241
  111.3 9.2 %collective-permute-start.34 = (bf16[32,4096]{1,0:T(8,128)(2,1)S(1)}, bf16[32,4096]{1,0:T(8,128)(2,1)S(1)}, u32[]{:S(2)}, u32[]{:S(2)}) collective-permute-start(bf16[32,4096]{1,0:T(8,128)(2,1)S(1)} %add_convert_fusion.3), channel_id=1, source_target_pairs={{0,4},{1,5},{4,8},{5,9},{8,12},{9,13},{12,14},{13,15},{14,10},{15,... | collective-permute-start | bytes 786440 | tf_op jit(solution)/shard_map/ppermute | solution.py:241
  117.9 8.0 %collective-permute-start.38 = (bf16[32,4096]{1,0:T(8,128)(2,1)S(1)}, bf16[32,4096]{1,0:T(8,128)(2,1)S(1)}, u32[]{:S(2)}, u32[]{:S(2)}) collective-permute-start(bf16[32,4096]{1,0:T(8,128)(2,1)S(1)} %add_convert_fusion), channel_id=1, source_target_pairs={{4,0},{5,1},{8,4},{9,5},{12,8},{13,9},{14,12},{15,13},{10,14},{11,... | collective-permute-start | bytes 786440 | tf_op jit(solution)/shard_map/ppermute | solution.py:241
  (18 other events, 128.1 us)

commit v5 on v3

--- a/solution.py
+++ b/solution.py
@@ -126,11 +126,12 @@
         ],
     )
     shape = jax.ShapeDtypeStruct((tok, HEADS * VD), jnp.bfloat16)
+    hits_shape = jax.ShapeDtypeStruct((total, 1), jnp.float32)
     work = HEADS * tok * total * CORES
     return pl.pallas_call(
         functools.partial(attention_kernel, tok=tok),
         grid_spec=grid_spec,
-        out_shape=[shape, shape, jax.ShapeDtypeStruct((total, 1), jnp.float32)],
+        out_shape=[shape, shape, hits_shape],
         compiler_params=pltpu.CompilerParams(vmem_limit_bytes=56 << 20),
         cost_estimate=pl.CostEstimate(
             flops=2 * work * (2 * LAT + 2 * ROPE), bytes_accessed=8 << 20, transcendentals=work
@@ -147,23 +148,21 @@
 
 
 def expert_kernel(
-    index_ref, up_rows, down_rows, hits_ref, gate_a, gate_b, up_a, up_b, down_a, down_b, out_a,
-    out_b, *, hop, chips,
+    index_ref, rows_ref, hits_ref, gate_a, up_a, down_a, gate_hbm, up_hbm, down_hbm, out_ref,
+    gate_b, up_b, down_b, sems, *, hop, chips,
 ):
-    half = up_rows.shape[0]
-    my_chip = index_ref[0] // CORES
-    place = ring_place(my_chip, chips)
-    from_behind = ring_chip(lax.rem(place - hop + chips, chips), chips) ^ my_chip
-    from_ahead = ring_chip(lax.rem(place + hop, chips), chips) ^ my_chip
-    tok = 2 * half
-    keep = jnp.concatenate(
-        [
-            hits_ref[pl.ds(pl.multiple_of(from_behind * tok, half), half), :],
-            hits_ref[pl.ds(pl.multiple_of(from_ahead * tok + half, half), half), :],
-        ],
-        axis=0,
-    ) > 0.0
-    rows = jnp.concatenate([up_rows[...], down_rows[...]], axis=0)
+    copies = [
+        pltpu.make_async_copy(there, here, sems.at[i])
+        for i, (there, here) in enumerate(((gate_hbm, gate_b), (up_hbm, up_b), (down_hbm, down_b)))
+    ]
+    for copy in copies:
+        copy.start()
+    tok = rows_ref.shape[0]
+    my_chip, my_core = index_ref[0] // CORES, lax.rem(index_ref[0], CORES)
+    place = ring_place(my_chip, chips) + chips + hop * (2 * my_core - 1)
+    source = ring_chip(lax.rem(place, chips), chips) ^ my_chip
+    keep = hits_ref[pl.ds(pl.multiple_of(source * tok, tok), tok), :] > 0.0
+    rows = rows_ref[...]
 
     def hidden(gate_ref, up_ref):
         gate_act = jnp.dot(rows, gate_ref[...], preferred_element_type=jnp.float32)
@@ -171,45 +170,45 @@
         act = gate_act * (1.0 / (1.0 + jnp.exp(-gate_act))) * up_act
         return jnp.where(keep, act, 0.0).astype(jnp.bfloat16)
 
-    hidden_a, hidden_b = hidden(gate_a, up_a), hidden(gate_b, up_b)
-    part = jnp.dot(hidden_a, down_a[...], preferred_element_type=jnp.float32)
-    part = part + jnp.dot(hidden_b, down_b[...], preferred_element_type=jnp.float32)
-    out_a[...] = part[:half]
-    out_b[...] = part[half:]
-
-
-def expert_part(my_index, rows_up, rows_down, hits, weights, hop, chips):
-    half, features = rows_up.shape
-    units = 2 * weights[0].shape[1]
-    shape = jax.ShapeDtypeStruct((half, features), jnp.float32)
+    part = jnp.dot(hidden(gate_a, up_a), down_a[...], preferred_element_type=jnp.float32)
+    copies[0].wait()
+    copies[1].wait()
+    hidden_b = hidden(gate_b, up_b)
+    copies[2].wait()
+    out_ref[...] = part + jnp.dot(hidden_b, down_b[...], preferred_element_type=jnp.float32)
+
+
+def expert_part(my_index, rows, hits, own, swapped, hop, chips):
+    tok, features = rows.shape
+    units = 2 * own[0].shape[1]
+    vmem, anywhere = pl.BlockSpec(memory_space=pltpu.VMEM), pl.BlockSpec(memory_space=pl.ANY)
     return pl.pallas_call(
         functools.partial(expert_kernel, hop=hop, chips=chips),
-        in_specs=[pl.BlockSpec(memory_space=pltpu.SMEM)]
-        + [pl.BlockSpec(memory_space=pltpu.VMEM)] * 9,
-        out_specs=[pl.BlockSpec(memory_space=pltpu.VMEM)] * 2,
-        out_shape=[shape, shape],
+        in_specs=[pl.BlockSpec(memory_space=pltpu.SMEM)] + [vmem] * 5 + [anywhere] * 3,
+        out_specs=vmem,
+        out_shape=jax.ShapeDtypeStruct((tok, features), jnp.float32),
+        scratch_shapes=[pltpu.VMEM(w.shape, w.dtype) for w in swapped]
+        + [pltpu.SemaphoreType.DMA((3,))],
         compiler_params=pltpu.CompilerParams(vmem_limit_bytes=24 << 20),
         cost_estimate=pl.CostEstimate(
-            flops=12 * half * features * units, bytes_accessed=14 << 20, transcendentals=0
+            flops=6 * tok * features * units, bytes_accessed=14 << 20, transcendentals=0
         ),
-    )(my_index.reshape(1), rows_up, rows_down, hits, *weights)
+    )(my_index.reshape(1), rows, hits, *own, *swapped)
 
 
 def local(
     q_nope, q_rope, c_kv, k_rope, w_value, norm_gain, expert_ids, gate_fixed, w_gate, w_up, w_down
 ):
     tok = c_kv.shape[0]
-    half = tok // 2
     n_ctx = lax.axis_size("ctx")
     chips = n_ctx // CORES
     my_index = lax.axis_index("ctx")
     siblings = [(i, i ^ 1) for i in range(n_ctx)]
     ring = list(range(0, chips, 2)) + list(range(1, chips, 2))[::-1]
-    ahead = [
-        (ring[p] * CORES + core, ring[(p + 1) % chips] * CORES + core)
+    route = [
+        (ring[p] * CORES + core, ring[(p + 1 - 2 * core) % chips] * CORES + core)
         for p in range(chips) for core in range(CORES)
     ]
-    behind = [(there, here) for here, there in ahead]
 
     def from_chip(block, step):
         return lax.ppermute(block, "ctx", [(i, i ^ (step * CORES)) for i in range(n_ctx)])
@@ -224,37 +223,31 @@
 
     own, mine, other = lax.optimization_barrier(((w_gate[0], w_up[0], w_down[0]), mine, other))
     swapped = tuple(lax.ppermute(w, "ctx", siblings) for w in own)
-    values, normed, hits = attention(my_index, q_nope, q_rope, mine, other, w_value, norm_gain)
-    normed, swapped = lax.optimization_barrier((normed, swapped))
-    weights = (own[0], swapped[0], own[1], swapped[1], own[2], swapped[2])
+    values, start, hits = attention(
+        my_index, q_nope, q_rope, mine, other, w_value, norm_gain
+    )
+    start, swapped = lax.optimization_barrier((start, swapped))
 
     def part_of(rows, hop):
-        return expert_part(my_index, rows[0], rows[1], hits, weights, hop, chips)
-
-    def move(pair):
-        return (lax.ppermute(pair[0], "ctx", ahead), lax.ppermute(pair[1], "ctx", behind))
-
-    def rounded(pair):
-        return tuple(x.astype(jnp.bfloat16) for x in pair)
-
-    start = (normed[:half], normed[half:])
+        return expert_part(my_index, rows, hits, own, swapped, hop, chips)
+
+    def move(block):
+        return lax.ppermute(block, "ctx", route)
+
+    def after(block, first):
+        return lax.optimization_barrier((block, first))[0]
+
     rows = move(start)
-    home = part_of(start, 0)
-    rows, home = lax.optimization_barrier((rows, home))
     later = move(rows) if chips > 2 else None
-    sums = rounded(part_of(rows, 1))
+    sums = part_of(rows, 1).astype(jnp.bfloat16)
     for hop in range(1, chips):
+        arrived = move(sums)
         rows = later
         if hop + 2 < chips:
-            rows, sums = lax.optimization_barrier((rows, sums))
-            later = move(rows)
-        arrived = move(sums)
+            later = move(after(rows, sums))
         if hop + 1 < chips:
-            part = part_of(rows, hop + 1)
-            sums = rounded(tuple(p + a.astype(jnp.float32) for p, a in zip(part, arrived)))
-    expert_out = jnp.concatenate(
-        [h + a.astype(jnp.float32) for h, a in zip(home, arrived)], axis=0
-    )
+            sums = (part_of(rows, hop + 1) + arrived.astype(jnp.float32)).astype(jnp.bfloat16)
+    expert_out = part_of(after(start, sums), 0) + arrived.astype(jnp.float32)
     gate_weight = gate_fixed.astype(jnp.float32) / 65536.0
     return (values.astype(jnp.float32) + gate_weight * expert_out).astype(jnp.bfloat16)
 

time: 133 us -> 126 us (0.947)
  Pallas kernels: 55.1 us -> 50.3 us
  starting transfers between devices: 39.9 us -> 36.4 us
  waiting for transfers between devices: 31.9 us -> 34.5 us
    pallas_call x8, Pallas kernels: 42 us -> 37.3 us  [expert_part(): pl.pallas_call(functools.partial(expert_kernel, hop=hop, chips=chips), in...]
    ppermute x28 -> x14, starting transfers between devices: 27.8 us -> 24.3 us  [move(): return lax.ppermute(block, 'ctx', route)]
    ppermute x28 -> x14, waiting for transfers between devices: 25.3 us -> 27.9 us  [move(): return lax.ppermute(block, 'ctx', route)]
  transfers between devices with their start and end apart: 39 -> 25, of which waited for: 18 -> 15; matrix products, arithmetic and copies ran while one was open for 1% -> 0% of each run, Pallas kernels for 41% -> 40%
where the time goes in v5:
time: 126 us
  Pallas kernels  50.3 us (40%)
  starting transfers between devices  36.4 us (29%)
  waiting for transfers between devices  34.5 us (27%)
  other arithmetic  3.23 us (3%)
  local copies, waits for them, and re-layouts  1.36 us (1%)
    pallas_call x8, Pallas kernels, expert_part(): pl.pallas_call(functools.partial(expert_kernel, hop=hop, chips=chips), in...  37.3 us
    ppermute x14, waiting for transfers between devices, move(): return lax.ppermute(block, 'ctx', route)  27.9 us
    ppermute x14, starting transfers between devices, move(): return lax.ppermute(block, 'ctx', route)  24.3 us
    pallas_call x1, Pallas kernels, attention(): pl.pallas_call(functools.partial(attention_kernel, tok=tok), grid_spec=gr...  13.1 us
    ppermute x7, starting transfers between devices, from_chip(): lax.ppermute(block, 'ctx', [(i, i ^ step * CORES) for i in range(n_ctx)])  11.4 us
    ppermute x7, waiting for transfers between devices, from_chip(): lax.ppermute(block, 'ctx', [(i, i ^ step * CORES) for i in range(n_ctx)])  4.54 us
  transfers between devices with their start and end apart: 25, of which 15 were waited for; matrix products, arithmetic and copies ran while one was open for 0% of the time, Pallas kernels for 40%

profile of v5, /device:TPU:0, one launch (start us, length us, event | category | flops | bytes accessed | tf_op | source)
XLA Modules:
  0.0 126.2 jit_solution(13314511266511136467)
XLA Ops:
  1.7 4.1 %collective-permute-start.3 = (bf16[64,640]{1,0:T(8,128)(2,1)S(1)}, bf16[64,640]{1,0:T(8,128)(2,1)S(1)}, u32[]{:S(2)}, u32[]{:S(2)}) collective-permute-start(bf16[64,640]{1,0:T(8,128)(2,1)S(1)} %get-tuple-element.41), channel_id=1, source_target_pairs={{0,8},{1,9},{2,10},{3,11},{4,12},{5,13},{6,14},{7,15},{8,0},{9,1},... | collective-permute-start | bytes 245768 | tf_op jit(solution)/shard_map/ppermute | solution.py:214
  5.8 1.5 %collective-permute-start = (bf16[64,640]{1,0:T(8,128)(2,1)S(1)}, bf16[64,640]{1,0:T(8,128)(2,1)S(1)}, u32[]{:S(2)}, u32[]{:S(2)}) collective-permute-start(bf16[64,640]{1,0:T(8,128)(2,1)S(1)} %get-tuple-element.41), channel_id=1, source_target_pairs={{0,2},{1,3},{2,0},{3,1},{4,6},{5,7},{6,4},{7,5},{8,10},{9,11},{10,... | collective-permute-start | bytes 245768 | tf_op jit(solution)/shard_map/ppermute | solution.py:214
  7.3 1.6 %collective-permute-start.1 = (bf16[64,640]{1,0:T(8,128)(2,1)S(1)}, bf16[64,640]{1,0:T(8,128)(2,1)S(1)}, u32[]{:S(2)}, u32[]{:S(2)}) collective-permute-start(bf16[64,640]{1,0:T(8,128)(2,1)S(1)} %get-tuple-element.41), channel_id=1, source_target_pairs={{0,4},{1,5},{2,6},{3,7},{4,0},{5,1},{6,2},{7,3},{8,12},{9,13},{10,... | collective-permute-start | bytes 245768 | tf_op jit(solution)/shard_map/ppermute | solution.py:214
  9.8 1.6 %collective-permute-start.4 = (bf16[64,640]{1,0:T(8,128)(2,1)S(1)}, bf16[64,640]{1,0:T(8,128)(2,1)S(1)}, u32[]{:S(2)}, u32[]{:S(2)}) collective-permute-start(bf16[64,640]{1,0:T(8,128)(2,1)S(1)} %collective-permute-done.3), channel_id=1, source_target_pairs={{0,2},{1,3},{2,0},{3,1},{4,6},{5,7},{6,4},{7,5},{8,10},{9,11},{10,... | collective-permute-start | bytes 245768 | tf_op jit(solution)/shard_map/ppermute | solution.py:214
  12.4 1.3 collective-permute-start.6
  15.9 1.8 %collective-permute-done.6 = bf16[64,640]{1,0:T(8,128)(2,1)S(1)} collective-permute-done((bf16[64,640]{1,0:T(8,128)(2,1)S(1)}, bf16[64,640]{1,0:T(8,128)(2,1)S(1)}, u32[]{:S(2)}, u32[]{:S(2)}) %collective-permute-start.6) | collective-permute-done | bytes 81952 | tf_op jit(solution)/shard_map/ppermute | solution.py:214
  17.8 2.1 %collective-permute-done.7.other_ref = bf16[512,640]{1,0:T(8,128)(2,1)S(1)} collective-permute-done((bf16[512,640]{1,0:T(8,128)(2,1)S(1)}, bf16[512,640]{1,0:T(8,128)(2,1)S(1)}, u32[]{:S(2)}, u32[]{:S(2)}) %collective-permute-start.7) | collective-permute-done | bytes 655392 | tf_op jit(solution)/shard_map/ppermute | solution.py:222
  20.7 13.1 %shard_map.109 = (bf16[64,4096]{1,0:T(8,128)(2,1)}, bf16[64,4096]{1,0:T(8,128)(2,1)}, f32[512,1]{1,0:T(8,128)}) custom-call(s32[1]{0:T(128)} %bitcast.index_ref, bf16[64,16384]{1,0:T(8,128)(2,1)} %q_ref.1, bf16[64,2048]{1,0:T(8,128)(2,1)} %qr_ref.1, bf16[512,640]{1,0:T(8,128)(2,1)} %copy-done.7, bf16[512,640]{1,0:T(8,128)(2,1)} %copy-done.8, ...), custom_call_target="tpu_custom_call" | custom-call | flops 4831838208 | bytes 8388608 | tf_op jit(solution)/shard_map/pallas_call | solution.py:131
  33.8 1.1 collective-permute-start.11
  35.0 8.3 %collective-permute-done.11.rows_ref = bf16[64,4096]{1,0:T(8,128)(2,1)S(1)} collective-permute-done((bf16[64,4096]{1,0:T(8,128)(2,1)}, bf16[64,4096]{1,0:T(8,128)(2,1)S(1)}, u32[]{:S(2)}, u32[]{:S(2)}) %collective-permute-start.11) | collective-permute-done | bytes 524320 | tf_op jit(solution)/shard_map/ppermute | solution.py:235
  43.3 1.4 %collective-permute-start.12 = (bf16[64,4096]{1,0:T(8,128)(2,1)S(1)}, bf16[64,4096]{1,0:T(8,128)(2,1)S(1)}, u32[]{:S(2)}, u32[]{:S(2)}) collective-permute-start(bf16[64,4096]{1,0:T(8,128)(2,1)S(1)} %collective-permute-done.11.rows_ref), channel_id=1, source_target_pairs={{0,4},{1,3},{4,8},{5,1},{8,12},{9,5},{12,14},{13,9},{14,10},{15,13... | collective-permute-start | bytes 1572872 | tf_op jit(solution)/shard_map/ppermute | solution.py:235
  45.7 4.7 %shard_map.110 = f32[64,4096]{1,0:T(8,128)S(1)} custom-call(s32[1]{0:T(128)} %bitcast.index_ref, bf16[64,4096]{1,0:T(8,128)(2,1)S(1)} %collective-permute-done.11.rows_ref, f32[512,1]{1,0:T(8,128)S(1)} %copy-done.3, bf16[4096,256]{1,0:T(8,128)(2,1)S(1)} %bitcast.10, bf16[4096,256]{1,0:T(8,128)(2,1)S(1)} %bitcast.19, bf16[256,4096]{1,0:T(8,128)(2,1)S(1)} %bitcast.28, ...), custom_call_target="tpu_custom_call" | custom-call | flops 805306368 | bytes 14680064 | tf_op jit(solution)/shard_map/pallas_call | solution.py:185
  50.4 2.4 %collective-permute-start.14 = (bf16[64,4096]{1,0:T(8,128)(2,1)S(1)}, bf16[64,4096]{1,0:T(8,128)(2,1)S(1)}, u32[]{:S(2)}, u32[]{:S(2)}) collective-permute-start(bf16[64,4096]{1,0:T(8,128)(2,1)S(1)} %convert_element_type.57), channel_id=1, source_target_pairs={{0,4},{1,3},{4,8},{5,1},{8,12},{9,5},{12,14},{13,9},{14,10},{15,13... | collective-permute-start | bytes 1572872 | tf_op jit(solution)/shard_map/ppermute | solution.py:235
  53.9 4.7 %shard_map.111 = f32[64,4096]{1,0:T(8,128)S(1)} custom-call(s32[1]{0:T(128)} %bitcast.index_ref, bf16[64,4096]{1,0:T(8,128)(2,1)S(1)} %collective-permute-done.12.rows_ref, f32[512,1]{1,0:T(8,128)S(1)} %copy-done.3, bf16[4096,256]{1,0:T(8,128)(2,1)S(1)} %bitcast.11, bf16[4096,256]{1,0:T(8,128)(2,1)S(1)} %bitcast.20, bf16[256,4096]{1,0:T(8,128)(2,1)S(1)} %bitcast.29, ...), custom_call_target="tpu_custom_call" | custom-call | flops 805306368 | bytes 14680064 | tf_op jit(solution)/shard_map/pallas_call | solution.py:185
  59.7 2.4 %collective-permute-start.16 = (bf16[64,4096]{1,0:T(8,128)(2,1)S(1)}, bf16[64,4096]{1,0:T(8,128)(2,1)S(1)}, u32[]{:S(2)}, u32[]{:S(2)}) collective-permute-start(bf16[64,4096]{1,0:T(8,128)(2,1)S(1)} %add_convert_fusion.6), channel_id=1, source_target_pairs={{0,4},{1,3},{4,8},{5,1},{8,12},{9,5},{12,14},{13,9},{14,10},{15,13... | collective-permute-start | bytes 1572872 | tf_op jit(solution)/shard_map/ppermute | solution.py:235
  62.1 3.1 %collective-permute-done.13.rows_ref = bf16[64,4096]{1,0:T(8,128)(2,1)S(1)} collective-permute-done((bf16[64,4096]{1,0:T(8,128)(2,1)S(1)}, bf16[64,4096]{1,0:T(8,128)(2,1)S(1)}, u32[]{:S(2)}, u32[]{:S(2)}) %collective-permute-start.13) | collective-permute-done | bytes 524320 | tf_op jit(solution)/shard_map/ppermute | solution.py:235
  65.2 2.4 %collective-permute-start.15 = (bf16[64,4096]{1,0:T(8,128)(2,1)S(1)}, bf16[64,4096]{1,0:T(8,128)(2,1)S(1)}, u32[]{:S(2)}, u32[]{:S(2)}) collective-permute-start(bf16[64,4096]{1,0:T(8,128)(2,1)S(1)} %collective-permute-done.13.rows_ref), channel_id=1, source_target_pairs={{0,4},{1,3},{4,8},{5,1},{8,12},{9,5},{12,14},{13,9},{14,10},{15,13... | collective-permute-start | bytes 1572872 | tf_op jit(solution)/shard_map/ppermute | solution.py:235
  67.6 4.7 %shard_map.112 = f32[64,4096]{1,0:T(8,128)S(1)} custom-call(s32[1]{0:T(128)} %bitcast.index_ref, bf16[64,4096]{1,0:T(8,128)(2,1)S(1)} %collective-permute-done.13.rows_ref, f32[512,1]{1,0:T(8,128)S(1)} %copy-done.3, bf16[4096,256]{1,0:T(8,128)(2,1)S(1)} %bitcast.12, bf16[4096,256]{1,0:T(8,128)(2,1)S(1)} %bitcast.21, bf16[256,4096]{1,0:T(8,128)(2,1)S(1)} %bitcast.30, ...), custom_call_target="tpu_custom_call" | custom-call | flops 805306368 | bytes 14680064 | tf_op jit(solution)/shard_map/pallas_call | solution.py:185
  73.4 3.1 %collective-permute-done.15.rows_ref = bf16[64,4096]{1,0:T(8,128)(2,1)S(1)} collective-permute-done((bf16[64,4096]{1,0:T(8,128)(2,1)S(1)}, bf16[64,4096]{1,0:T(8,128)(2,1)S(1)}, u32[]{:S(2)}, u32[]{:S(2)}) %collective-permute-start.15) | collective-permute-done | bytes 524320 | tf_op jit(solution)/shard_map/ppermute | solution.py:235
  76.5 2.4 %collective-permute-start.17 = (bf16[64,4096]{1,0:T(8,128)(2,1)S(1)}, bf16[64,4096]{1,0:T(8,128)(2,1)S(1)}, u32[]{:S(2)}, u32[]{:S(2)}) collective-permute-start(bf16[64,4096]{1,0:T(8,128)(2,1)S(1)} %collective-permute-done.15.rows_ref), channel_id=1, source_target_pairs={{0,4},{1,3},{4,8},{5,1},{8,12},{9,5},{12,14},{13,9},{14,10},{15,13... | collective-permute-start | bytes 1572872 | tf_op jit(solution)/shard_map/ppermute | solution.py:235
  78.9 4.7 %shard_map.113 = f32[64,4096]{1,0:T(8,128)S(1)} custom-call(s32[1]{0:T(128)} %bitcast.index_ref, bf16[64,4096]{1,0:T(8,128)(2,1)S(1)} %collective-permute-done.15.rows_ref, f32[512,1]{1,0:T(8,128)S(1)} %copy-done.3, bf16[4096,256]{1,0:T(8,128)(2,1)S(1)} %bitcast.13, bf16[4096,256]{1,0:T(8,128)(2,1)S(1)} %bitcast.22, bf16[256,4096]{1,0:T(8,128)(2,1)S(1)} %bitcast.31, ...), custom_call_target="tpu_custom_call" | custom-call | flops 805306368 | bytes 14680064 | tf_op jit(solution)/shard_map/pallas_call | solution.py:185
  84.6 3.1 %collective-permute-done.17.rows_ref = bf16[64,4096]{1,0:T(8,128)(2,1)S(1)} collective-permute-done((bf16[64,4096]{1,0:T(8,128)(2,1)S(1)}, bf16[64,4096]{1,0:T(8,128)(2,1)S(1)}, u32[]{:S(2)}, u32[]{:S(2)}) %collective-permute-start.17) | collective-permute-done | bytes 524320 | tf_op jit(solution)/shard_map/ppermute | solution.py:235
  87.7 2.4 %collective-permute-start.19 = (bf16[64,4096]{1,0:T(8,128)(2,1)S(1)}, bf16[64,4096]{1,0:T(8,128)(2,1)S(1)}, u32[]{:S(2)}, u32[]{:S(2)}) collective-permute-start(bf16[64,4096]{1,0:T(8,128)(2,1)S(1)} %collective-permute-done.17.rows_ref), channel_id=1, source_target_pairs={{0,4},{1,3},{4,8},{5,1},{8,12},{9,5},{12,14},{13,9},{14,10},{15,13... | collective-permute-start | bytes 1572872 | tf_op jit(solution)/shard_map/ppermute | solution.py:235
  90.1 4.7 %shard_map.114 = f32[64,4096]{1,0:T(8,128)S(1)} custom-call(s32[1]{0:T(128)} %bitcast.index_ref, bf16[64,4096]{1,0:T(8,128)(2,1)S(1)} %collective-permute-done.17.rows_ref, f32[512,1]{1,0:T(8,128)S(1)} %copy-done.3, bf16[4096,256]{1,0:T(8,128)(2,1)S(1)} %bitcast.14, bf16[4096,256]{1,0:T(8,128)(2,1)S(1)} %bitcast.23, bf16[256,4096]{1,0:T(8,128)(2,1)S(1)} %bitcast.32, ...), custom_call_target="tpu_custom_call" | custom-call | flops 805306368 | bytes 14680064 | tf_op jit(solution)/shard_map/pallas_call | solution.py:185
  95.9 3.1 %collective-permute-done.19.rows_ref = bf16[64,4096]{1,0:T(8,128)(2,1)S(1)} collective-permute-done((bf16[64,4096]{1,0:T(8,128)(2,1)S(1)}, bf16[64,4096]{1,0:T(8,128)(2,1)S(1)}, u32[]{:S(2)}, u32[]{:S(2)}) %collective-permute-start.19) | collective-permute-done | bytes 524320 | tf_op jit(solution)/shard_map/ppermute | solution.py:235
  98.9 2.4 %collective-permute-start.21 = (bf16[64,4096]{1,0:T(8,128)(2,1)S(1)}, bf16[64,4096]{1,0:T(8,128)(2,1)S(1)}, u32[]{:S(2)}, u32[]{:S(2)}) collective-permute-start(bf16[64,4096]{1,0:T(8,128)(2,1)S(1)} %collective-permute-done.19.rows_ref), channel_id=1, source_target_pairs={{0,4},{1,3},{4,8},{5,1},{8,12},{9,5},{12,14},{13,9},{14,10},{15,13... | collective-permute-start | bytes 1572872 | tf_op jit(solution)/shard_map/ppermute | solution.py:235
  101.3 4.7 %shard_map.116 = f32[64,4096]{1,0:T(8,128)S(1)} custom-call(s32[1]{0:T(128)} %bitcast.index_ref, bf16[64,4096]{1,0:T(8,128)(2,1)S(1)} %collective-permute-done.19.rows_ref, f32[512,1]{1,0:T(8,128)S(1)} %copy-done.3, bf16[4096,256]{1,0:T(8,128)(2,1)S(1)} %bitcast.15, bf16[4096,256]{1,0:T(8,128)(2,1)S(1)} %bitcast.24, bf16[256,4096]{1,0:T(8,128)(2,1)S(1)} %bitcast.33, ...), custom_call_target="tpu_custom_call" | custom-call | flops 805306368 | bytes 14680064 | tf_op jit(solution)/shard_map/pallas_call | solution.py:185
  107.1 3.1 %collective-permute-done.21.rows_ref = bf16[64,4096]{1,0:T(8,128)(2,1)S(1)} collective-permute-done((bf16[64,4096]{1,0:T(8,128)(2,1)S(1)}, bf16[64,4096]{1,0:T(8,128)(2,1)S(1)}, u32[]{:S(2)}, u32[]{:S(2)}) %collective-permute-start.21) | collective-permute-done | bytes 524320 | tf_op jit(solution)/shard_map/ppermute | solution.py:235
  110.2 4.7 %shard_map.115 = f32[64,4096]{1,0:T(8,128)S(1)} custom-call(s32[1]{0:T(128)} %bitcast.index_ref, bf16[64,4096]{1,0:T(8,128)(2,1)S(1)} %collective-permute-done.21.rows_ref, f32[512,1]{1,0:T(8,128)S(1)} %copy-done.3, bf16[4096,256]{1,0:T(8,128)(2,1)S(1)} %bitcast.16, bf16[4096,256]{1,0:T(8,128)(2,1)S(1)} %bitcast.25, bf16[256,4096]{1,0:T(8,128)(2,1)S(1)} %bitcast.34, ...), custom_call_target="tpu_custom_call" | custom-call | flops 805306368 | bytes 14680064 | tf_op jit(solution)/shard_map/pallas_call | solution.py:185
  115.9 2.4 %collective-permute-start.24 = (bf16[64,4096]{1,0:T(8,128)(2,1)S(1)}, bf16[64,4096]{1,0:T(8,128)(2,1)S(1)}, u32[]{:S(2)}, u32[]{:S(2)}) collective-permute-start(bf16[64,4096]{1,0:T(8,128)(2,1)S(1)} %add_convert_fusion.1), channel_id=1, source_target_pairs={{0,4},{1,3},{4,8},{5,1},{8,12},{9,5},{12,14},{13,9},{14,10},{15,13... | collective-permute-start | bytes 1572872 | tf_op jit(solution)/shard_map/ppermute | solution.py:235
  118.4 4.7 %shard_map.117 = f32[64,4096]{1,0:T(8,128)S(1)} custom-call(s32[1]{0:T(128)} %bitcast.index_ref, bf16[64,4096]{1,0:T(8,128)(2,1)S(1)} %copy-done.5, f32[512,1]{1,0:T(8,128)S(1)} %copy-done.4, bf16[4096,256]{1,0:T(8,128)(2,1)S(1)} %bitcast.17, bf16[4096,256]{1,0:T(8,128)(2,1)S(1)} %bitcast.26, bf16[256,4096]{1,0:T(8,128)(2,1)S(1)} %bitcast.35, ...), custom_call_target="tpu_custom_call" | custom-call | flops 805306368 | bytes 14680064 | tf_op jit(solution)/shard_map/pallas_call | solution.py:185
  123.0 2.1 %collective-permute-done.24 = bf16[64,4096]{1,0:T(8,128)(2,1)S(1)} collective-permute-done((bf16[64,4096]{1,0:T(8,128)(2,1)S(1)}, bf16[64,4096]{1,0:T(8,128)(2,1)S(1)}, u32[]{:S(2)}, u32[]{:S(2)}) %collective-permute-start.24) | collective-permute-done | bytes 524320 | tf_op jit(solution)/shard_map/ppermute | solution.py:235
  (66 shorter events, 16.4 us)
Async XLA Ops:
  1.7 8.1 %collective-permute-start.3 = (bf16[64,640]{1,0:T(8,128)(2,1)S(1)}, bf16[64,640]{1,0:T(8,128)(2,1)S(1)}, u32[]{:S(2)}, u32[]{:S(2)}) collective-permute-start(bf16[64,640]{1,0:T(8,128)(2,1)S(1)} %get-tuple-element.41), channel_id=1, source_target_pairs={{0,8},{1,9},{2,10},{3,11},{4,12},{5,13},{6,14},{7,15},{8,0},{9,1},... | collective-permute-start | bytes 245768 | tf_op jit(solution)/shard_map/ppermute | solution.py:214
  5.8 6.6 %collective-permute-start = (bf16[64,640]{1,0:T(8,128)(2,1)S(1)}, bf16[64,640]{1,0:T(8,128)(2,1)S(1)}, u32[]{:S(2)}, u32[]{:S(2)}) collective-permute-start(bf16[64,640]{1,0:T(8,128)(2,1)S(1)} %get-tuple-element.41), channel_id=1, source_target_pairs={{0,2},{1,3},{2,0},{3,1},{4,6},{5,7},{6,4},{7,5},{8,10},{9,11},{10,... | collective-permute-start | bytes 245768 | tf_op jit(solution)/shard_map/ppermute | solution.py:214
  7.3 6.3 %collective-permute-start.1 = (bf16[64,640]{1,0:T(8,128)(2,1)S(1)}, bf16[64,640]{1,0:T(8,128)(2,1)S(1)}, u32[]{:S(2)}, u32[]{:S(2)}) collective-permute-start(bf16[64,640]{1,0:T(8,128)(2,1)S(1)} %get-tuple-element.41), channel_id=1, source_target_pairs={{0,4},{1,5},{2,6},{3,7},{4,0},{5,1},{6,2},{7,3},{8,12},{9,13},{10,... | collective-permute-start | bytes 245768 | tf_op jit(solution)/shard_map/ppermute | solution.py:214
  8.9 5.6 %collective-permute-start.2 = (bf16[64,640]{1,0:T(8,128)(2,1)S(1)}, bf16[64,640]{1,0:T(8,128)(2,1)S(1)}, u32[]{:S(2)}, u32[]{:S(2)}) collective-permute-start(bf16[64,640]{1,0:T(8,128)(2,1)S(1)} %get-tuple-element.41), channel_id=1, source_target_pairs={{0,6},{1,7},{2,4},{3,5},{4,2},{5,3},{6,0},{7,1},{8,14},{9,15},{10,... | collective-permute-start | bytes 245768 | tf_op jit(solution)/shard_map/ppermute | solution.py:214
  9.8 5.5 %collective-permute-start.4 = (bf16[64,640]{1,0:T(8,128)(2,1)S(1)}, bf16[64,640]{1,0:T(8,128)(2,1)S(1)}, u32[]{:S(2)}, u32[]{:S(2)}) collective-permute-start(bf16[64,640]{1,0:T(8,128)(2,1)S(1)} %collective-permute-done.3), channel_id=1, source_target_pairs={{0,2},{1,3},{2,0},{3,1},{4,6},{5,7},{6,4},{7,5},{8,10},{9,11},{10,... | collective-permute-start | bytes 245768 | tf_op jit(solution)/shard_map/ppermute | solution.py:214
  11.4 4.5 %collective-permute-start.5 = (bf16[64,640]{1,0:T(8,128)(2,1)S(1)}, bf16[64,640]{1,0:T(8,128)(2,1)S(1)}, u32[]{:S(2)}, u32[]{:S(2)}) collective-permute-start(bf16[64,640]{1,0:T(8,128)(2,1)S(1)} %collective-permute-done.3), channel_id=1, source_target_pairs={{0,4},{1,5},{2,6},{3,7},{4,0},{5,1},{6,2},{7,3},{8,12},{9,13},{10,... | collective-permute-start | bytes 245768 | tf_op jit(solution)/shard_map/ppermute | solution.py:214
  12.4 5.3 %collective-permute-start.6 = (bf16[64,640]{1,0:T(8,128)(2,1)S(1)}, bf16[64,640]{1,0:T(8,128)(2,1)S(1)}, u32[]{:S(2)}, u32[]{:S(2)}) collective-permute-start(bf16[64,640]{1,0:T(8,128)(2,1)S(1)} %collective-permute-done.3), channel_id=1, source_target_pairs={{0,6},{1,7},{2,4},{3,5},{4,2},{5,3},{6,0},{7,1},{8,14},{9,15},{10,... | collective-permute-start | bytes 245768 | tf_op jit(solution)/shard_map/ppermute | solution.py:214
  17.7 2.2 %collective-permute-start.7 = (bf16[512,640]{1,0:T(8,128)(2,1)S(1)}, bf16[512,640]{1,0:T(8,128)(2,1)S(1)}, u32[]{:S(2)}, u32[]{:S(2)}) collective-permute-start(bf16[512,640]{1,0:T(8,128)(2,1)S(1)} %constant_dynamic-update-slice_fusion.mine_ref), channel_id=1, source_target_pairs={{0,1},{1,0},{2,3},{3,2},{4,5},{5,4},{6,7},{7,6},{8,9},{9,8},{10,11... | collective-permute-start | bytes 1966088 | tf_op jit(solution)/shard_map/ppermute | solution.py:222
  19.9 13.9 %collective-permute-start.8 = (bf16[4096,256]{1,0:T(8,128)(2,1)}, bf16[4096,256]{1,0:T(8,128)(2,1)}, u32[]{:S(2)}, u32[]{:S(2)}) collective-permute-start(bf16[4096,256]{1,0:T(8,128)(2,1)} %bitcast.9), channel_id=1, source_target_pairs={{0,1},{1,0},{2,3},{3,2},{4,5},{5,4},{6,7},{7,6},{8,9},{9,8},{10,11... | collective-permute-start | bytes 6291464 | tf_op jit(solution)/shard_map/ppermute | solution.py:225
  20.0 13.8 %collective-permute-start.9 = (bf16[4096,256]{1,0:T(8,128)(2,1)}, bf16[4096,256]{1,0:T(8,128)(2,1)}, u32[]{:S(2)}, u32[]{:S(2)}) collective-permute-start(bf16[4096,256]{1,0:T(8,128)(2,1)} %bitcast.18), channel_id=1, source_target_pairs={{0,1},{1,0},{2,3},{3,2},{4,5},{5,4},{6,7},{7,6},{8,9},{9,8},{10,11... | collective-permute-start | bytes 6291464 | tf_op jit(solution)/shard_map/ppermute | solution.py:225
  20.4 13.4 %collective-permute-start.10 = (bf16[256,4096]{1,0:T(8,128)(2,1)}, bf16[256,4096]{1,0:T(8,128)(2,1)}, u32[]{:S(2)}, u32[]{:S(2)}) collective-permute-start(bf16[256,4096]{1,0:T(8,128)(2,1)} %bitcast.27), channel_id=1, source_target_pairs={{0,1},{1,0},{2,3},{3,2},{4,5},{5,4},{6,7},{7,6},{8,9},{9,8},{10,11... | collective-permute-start | bytes 6291464 | tf_op jit(solution)/shard_map/ppermute | solution.py:225
  20.7 24.0 %copy-start = (bf16[1,4096,256]{2,1,0:T(8,128)(2,1)S(1)}, bf16[1,4096,256]{2,1,0:T(8,128)(2,1)}, u32[]{:S(2)}) copy-start(bf16[1,4096,256]{2,1,0:T(8,128)(2,1)} %param.19) | copy-start | bytes 6291460
  20.7 24.0 %copy-start.1 = (bf16[1,4096,256]{2,1,0:T(8,128)(2,1)S(1)}, bf16[1,4096,256]{2,1,0:T(8,128)(2,1)}, u32[]{:S(2)}) copy-start(bf16[1,4096,256]{2,1,0:T(8,128)(2,1)} %param.20) | copy-start | bytes 6291460
  20.7 24.0 %copy-start.2 = (bf16[1,256,4096]{2,1,0:T(8,128)(2,1)S(1)}, bf16[1,256,4096]{2,1,0:T(8,128)(2,1)}, u32[]{:S(2)}) copy-start(bf16[1,256,4096]{2,1,0:T(8,128)(2,1)} %param.21) | copy-start | bytes 6291460
  33.8 9.4 %collective-permute-start.11 = (bf16[64,4096]{1,0:T(8,128)(2,1)}, bf16[64,4096]{1,0:T(8,128)(2,1)S(1)}, u32[]{:S(2)}, u32[]{:S(2)}) collective-permute-start(bf16[64,4096]{1,0:T(8,128)(2,1)} %get-tuple-element.40.rows_ref), channel_id=1, source_target_pairs={{0,4},{1,3},{4,8},{5,1},{8,12},{9,5},{12,14},{13,9},{14,10},{15,13... | collective-permute-start | bytes 1572872 | tf_op jit(solution)/shard_map/ppermute | solution.py:235
  43.3 9.6 %collective-permute-start.12 = (bf16[64,4096]{1,0:T(8,128)(2,1)S(1)}, bf16[64,4096]{1,0:T(8,128)(2,1)S(1)}, u32[]{:S(2)}, u32[]{:S(2)}) collective-permute-start(bf16[64,4096]{1,0:T(8,128)(2,1)S(1)} %collective-permute-done.11.rows_ref), channel_id=1, source_target_pairs={{0,4},{1,3},{4,8},{5,1},{8,12},{9,5},{12,14},{13,9},{14,10},{15,13... | collective-permute-start | bytes 1572872 | tf_op jit(solution)/shard_map/ppermute | solution.py:235
  50.4 9.2 %collective-permute-start.14 = (bf16[64,4096]{1,0:T(8,128)(2,1)S(1)}, bf16[64,4096]{1,0:T(8,128)(2,1)S(1)}, u32[]{:S(2)}, u32[]{:S(2)}) collective-permute-start(bf16[64,4096]{1,0:T(8,128)(2,1)S(1)} %convert_element_type.57), channel_id=1, source_target_pairs={{0,4},{1,3},{4,8},{5,1},{8,12},{9,5},{12,14},{13,9},{14,10},{15,13... | collective-permute-start | bytes 1572872 | tf_op jit(solution)/shard_map/ppermute | solution.py:235
  52.8 12.4 %collective-permute-start.13 = (bf16[64,4096]{1,0:T(8,128)(2,1)S(1)}, bf16[64,4096]{1,0:T(8,128)(2,1)S(1)}, u32[]{:S(2)}, u32[]{:S(2)}) collective-permute-start(bf16[64,4096]{1,0:T(8,128)(2,1)S(1)} %collective-permute-done.12.rows_ref), channel_id=1, source_target_pairs={{0,4},{1,3},{4,8},{5,1},{8,12},{9,5},{12,14},{13,9},{14,10},{15,13... | collective-permute-start | bytes 1572872 | tf_op jit(solution)/shard_map/ppermute | solution.py:235
  59.7 12.6 %collective-permute-start.16 = (bf16[64,4096]{1,0:T(8,128)(2,1)S(1)}, bf16[64,4096]{1,0:T(8,128)(2,1)S(1)}, u32[]{:S(2)}, u32[]{:S(2)}) collective-permute-start(bf16[64,4096]{1,0:T(8,128)(2,1)S(1)} %add_convert_fusion.6), channel_id=1, source_target_pairs={{0,4},{1,3},{4,8},{5,1},{8,12},{9,5},{12,14},{13,9},{14,10},{15,13... | collective-permute-start | bytes 1572872 | tf_op jit(solution)/shard_map/ppermute | solution.py:235
  65.2 11.2 %collective-permute-start.15 = (bf16[64,4096]{1,0:T(8,128)(2,1)S(1)}, bf16[64,4096]{1,0:T(8,128)(2,1)S(1)}, u32[]{:S(2)}, u32[]{:S(2)}) collective-permute-start(bf16[64,4096]{1,0:T(8,128)(2,1)S(1)} %collective-permute-done.13.rows_ref), channel_id=1, source_target_pairs={{0,4},{1,3},{4,8},{5,1},{8,12},{9,5},{12,14},{13,9},{14,10},{15,13... | collective-permute-start | bytes 1572872 | tf_op jit(solution)/shard_map/ppermute | solution.py:235
  72.4 11.1 %collective-permute-start.18 = (bf16[64,4096]{1,0:T(8,128)(2,1)S(1)}, bf16[64,4096]{1,0:T(8,128)(2,1)S(1)}, u32[]{:S(2)}, u32[]{:S(2)}) collective-permute-start(bf16[64,4096]{1,0:T(8,128)(2,1)S(1)} %add_convert_fusion.5), channel_id=1, source_target_pairs={{0,4},{1,3},{4,8},{5,1},{8,12},{9,5},{12,14},{13,9},{14,10},{15,13... | collective-permute-start | bytes 1572872 | tf_op jit(solution)/shard_map/ppermute | solution.py:235
  76.5 11.2 %collective-permute-start.17 = (bf16[64,4096]{1,0:T(8,128)(2,1)S(1)}, bf16[64,4096]{1,0:T(8,128)(2,1)S(1)}, u32[]{:S(2)}, u32[]{:S(2)}) collective-permute-start(bf16[64,4096]{1,0:T(8,128)(2,1)S(1)} %collective-permute-done.15.rows_ref), channel_id=1, source_target_pairs={{0,4},{1,3},{4,8},{5,1},{8,12},{9,5},{12,14},{13,9},{14,10},{15,13... | collective-permute-start | bytes 1572872 | tf_op jit(solution)/shard_map/ppermute | solution.py:235
  83.6 11.1 %collective-permute-start.20 = (bf16[64,4096]{1,0:T(8,128)(2,1)S(1)}, bf16[64,4096]{1,0:T(8,128)(2,1)S(1)}, u32[]{:S(2)}, u32[]{:S(2)}) collective-permute-start(bf16[64,4096]{1,0:T(8,128)(2,1)S(1)} %add_convert_fusion.4), channel_id=1, source_target_pairs={{0,4},{1,3},{4,8},{5,1},{8,12},{9,5},{12,14},{13,9},{14,10},{15,13... | collective-permute-start | bytes 1572872 | tf_op jit(solution)/shard_map/ppermute | solution.py:235
  87.7 11.2 %collective-permute-start.19 = (bf16[64,4096]{1,0:T(8,128)(2,1)S(1)}, bf16[64,4096]{1,0:T(8,128)(2,1)S(1)}, u32[]{:S(2)}, u32[]{:S(2)}) collective-permute-start(bf16[64,4096]{1,0:T(8,128)(2,1)S(1)} %collective-permute-done.17.rows_ref), channel_id=1, source_target_pairs={{0,4},{1,3},{4,8},{5,1},{8,12},{9,5},{12,14},{13,9},{14,10},{15,13... | collective-permute-start | bytes 1572872 | tf_op jit(solution)/shard_map/ppermute | solution.py:235
  94.9 11.1 %collective-permute-start.22 = (bf16[64,4096]{1,0:T(8,128)(2,1)S(1)}, bf16[64,4096]{1,0:T(8,128)(2,1)S(1)}, u32[]{:S(2)}, u32[]{:S(2)}) collective-permute-start(bf16[64,4096]{1,0:T(8,128)(2,1)S(1)} %add_convert_fusion.3), channel_id=1, source_target_pairs={{0,4},{1,3},{4,8},{5,1},{8,12},{9,5},{12,14},{13,9},{14,10},{15,13... | collective-permute-start | bytes 1572872 | tf_op jit(solution)/shard_map/ppermute | solution.py:235
  98.9 11.2 %collective-permute-start.21 = (bf16[64,4096]{1,0:T(8,128)(2,1)S(1)}, bf16[64,4096]{1,0:T(8,128)(2,1)S(1)}, u32[]{:S(2)}, u32[]{:S(2)}) collective-permute-start(bf16[64,4096]{1,0:T(8,128)(2,1)S(1)} %collective-permute-done.19.rows_ref), channel_id=1, source_target_pairs={{0,4},{1,3},{4,8},{5,1},{8,12},{9,5},{12,14},{13,9},{14,10},{15,13... | collective-permute-start | bytes 1572872 | tf_op jit(solution)/shard_map/ppermute | solution.py:235
  106.1 9.7 %collective-permute-start.23 = (bf16[64,4096]{1,0:T(8,128)(2,1)S(1)}, bf16[64,4096]{1,0:T(8,128)(2,1)S(1)}, u32[]{:S(2)}, u32[]{:S(2)}) collective-permute-start(bf16[64,4096]{1,0:T(8,128)(2,1)S(1)} %add_convert_fusion.2), channel_id=1, source_target_pairs={{0,4},{1,3},{4,8},{5,1},{8,12},{9,5},{12,14},{13,9},{14,10},{15,13... | collective-permute-start | bytes 1572872 | tf_op jit(solution)/shard_map/ppermute | solution.py:235
  114.9 3.5 %copy-start.9 = (s32[64,1]{0,1:T(1,128)S(1)}, s32[64,1]{0,1:T(1,128)}, u32[]{:S(2)}) copy-start(s32[64,1]{0,1:T(1,128)} %param.18) | copy-start | bytes 772
  114.9 3.5 %copy-start.4 = (f32[512,1]{1,0:T(8,128)S(1)}, f32[512,1]{1,0:T(8,128)}, u32[]{:S(2)}) copy-start(f32[512,1]{1,0:T(8,128)} %get-tuple-element.31.hits_ref) | copy-start | bytes 6148
  114.9 3.5 %copy-start.5 = (bf16[64,4096]{1,0:T(8,128)(2,1)S(1)}, bf16[64,4096]{1,0:T(8,128)(2,1)}, u32[]{:S(2)}) copy-start(bf16[64,4096]{1,0:T(8,128)(2,1)} %get-tuple-element.40.rows_ref) | copy-start | bytes 1572868
  115.9 9.2 %collective-permute-start.24 = (bf16[64,4096]{1,0:T(8,128)(2,1)S(1)}, bf16[64,4096]{1,0:T(8,128)(2,1)S(1)}, u32[]{:S(2)}, u32[]{:S(2)}) collective-permute-start(bf16[64,4096]{1,0:T(8,128)(2,1)S(1)} %add_convert_fusion.1), channel_id=1, source_target_pairs={{0,4},{1,3},{4,8},{5,1},{8,12},{9,5},{12,14},{13,9},{14,10},{15,13... | collective-permute-start | bytes 1572872 | tf_op jit(solution)/shard_map/ppermute | solution.py:235
  118.3 6.8 %copy-start.6 = (bf16[64,4096]{1,0:T(8,128)(2,1)S(1)}, bf16[64,4096]{1,0:T(8,128)(2,1)}, u32[]{:S(2)}) copy-start(bf16[64,4096]{1,0:T(8,128)(2,1)} %get-tuple-element.25) | copy-start | bytes 1572868
  (3 other events, 4.6 us)

commit v6 on v5

--- a/solution.py
+++ b/solution.py
@@ -21,12 +21,13 @@
 
 HEAD_GROUP = 8
 SUB_HEADS = 4
+SHARES = 2
 LOG2_SCALE = SCORE_SCALE * math.log2(math.e)
 
 
 def attention_kernel(
-    index_ref, q_ref, qr_ref, mine_ref, other_ref, wv_ref, gain_ref, values_ref, normed_ref,
-    hits_ref, stack_ref, bias_a_ref, bias_b_ref, *, tok,
+    index_ref, q_ref, qr_ref, mine_ref, other_ref, wv_ref, values_ref, hits_ref, stack_ref,
+    bias_a_ref, bias_b_ref, *, tok,
 ):
     group = pl.program_id(0)
     my_index = index_ref[0]
@@ -46,7 +47,12 @@
         lane = lax.broadcasted_iota(jnp.int32, last.shape, 1)
         named = jnp.max(jnp.where(lane >= ROPE, last, -1.0), axis=1, keepdims=True)
         my_expert = (my_index // SPAN).astype(jnp.float32)
-        hits_ref[...] = jnp.where(named == my_expert, 1.0, 0.0)
+        hits = jnp.where(named == my_expert, 1.0, 0.0)
+        column = lax.broadcasted_iota(jnp.int32, hits_ref.shape, 1)
+        table = jnp.zeros(hits_ref.shape, jnp.float32)
+        for place in range(keys // tok):
+            table = jnp.where(column == place, hits[place * tok : (place + 1) * tok], table)
+        hits_ref[...] = table
 
     lane = lax.broadcasted_iota(jnp.int32, (tok, 2 * ROPE), 1)
     for head in range(HEAD_GROUP):
@@ -83,41 +89,36 @@
             preferred_element_type=jnp.float32,
         )
         latent = (mixed.reshape(SUB_HEADS, tok, LAT) / total).astype(jnp.bfloat16)
-        for head in range(SUB_HEADS):
-            value = jnp.dot(
-                latent[head], wv_ref[sub * SUB_HEADS + head], preferred_element_type=jnp.float32
-            )
-            parts.append(value.astype(jnp.bfloat16))
-    wide = HEAD_GROUP * VD
-    values_ref[:, pl.ds(pl.multiple_of(group * wide, wide), wide)] = jnp.concatenate(parts, axis=1)
-
-    @pl.when(group == HEADS // HEAD_GROUP - 1)
-    def _():
-        values = values_ref[...].astype(jnp.float32)
-        square = jnp.mean(values * values, axis=1, keepdims=True)
-        normed = values * lax.rsqrt(square + NORM_EPS) * gain_ref[...]
-        normed_ref[...] = normed.astype(jnp.bfloat16)
-
-
-def attention(my_index, q_nope, q_rope, mine, other, w_value, norm_gain):
+        for head in range(0, SUB_HEADS, 2):
+            first = sub * SUB_HEADS + head
+            pair = jnp.dot(
+                latent[head : head + 2].reshape(2 * tok, LAT),
+                jnp.concatenate([wv_ref[first], wv_ref[first + 1]], axis=1),
+                preferred_element_type=jnp.float32,
+            ).astype(jnp.bfloat16)
+            parts.extend([pair[:tok, :VD], pair[tok:, VD:]])
+    values_ref[...] = jnp.concatenate(parts, axis=1)
+
+
+def attention(my_index, q_nope, q_rope, mine, other, w_value, share):
     tok = q_nope.shape[0]
     total = mine.shape[0]
     rows = HEAD_GROUP * tok
+    steps = HEADS // HEAD_GROUP // SHARES
+    first = share * steps
     grid_spec = pltpu.PrefetchScalarGridSpec(
         num_scalar_prefetch=1,
-        grid=(HEADS // HEAD_GROUP,),
+        grid=(steps,),
         in_specs=[
-            pl.BlockSpec((tok, HEAD_GROUP * LAT), lambda g, i: (0, g)),
-            pl.BlockSpec((tok, HEAD_GROUP * ROPE), lambda g, i: (0, g)),
+            pl.BlockSpec((tok, HEAD_GROUP * LAT), lambda g, i: (0, g + first)),
+            pl.BlockSpec((tok, HEAD_GROUP * ROPE), lambda g, i: (0, g + first)),
             pl.BlockSpec(mine.shape, lambda g, i: (0, 0)),
             pl.BlockSpec(mine.shape, lambda g, i: (0, 0)),
-            pl.BlockSpec((HEAD_GROUP, LAT, VD), lambda g, i: (g, 0, 0)),
-            pl.BlockSpec((1, HEADS * VD), lambda g, i: (0, 0)),
+            pl.BlockSpec((HEAD_GROUP, LAT, VD), lambda g, i: (g + first, 0, 0)),
         ],
         out_specs=[
-            pl.BlockSpec((tok, HEADS * VD), lambda g, i: (0, 0)),
-            pl.BlockSpec((tok, HEADS * VD), lambda g, i: (0, 0)),
-            pl.BlockSpec((total, 1), lambda g, i: (0, 0)),
+            pl.BlockSpec((tok, HEAD_GROUP * VD), lambda g, i: (0, g)),
+            pl.BlockSpec((tok, total // tok), lambda g, i: (0, 0)),
         ],
         scratch_shapes=[
             pltpu.VMEM((rows, LAT + 2 * ROPE), jnp.bfloat16),
@@ -125,18 +126,18 @@
             pltpu.VMEM((tok, total), jnp.float32),
         ],
     )
-    shape = jax.ShapeDtypeStruct((tok, HEADS * VD), jnp.bfloat16)
-    hits_shape = jax.ShapeDtypeStruct((total, 1), jnp.float32)
-    work = HEADS * tok * total * CORES
+    values_shape = jax.ShapeDtypeStruct((tok, HEADS * VD // SHARES), jnp.bfloat16)
+    hits_shape = jax.ShapeDtypeStruct((tok, total // tok), jnp.float32)
+    work = HEADS * tok * total * CORES // SHARES
     return pl.pallas_call(
         functools.partial(attention_kernel, tok=tok),
         grid_spec=grid_spec,
-        out_shape=[shape, shape, hits_shape],
+        out_shape=[values_shape, hits_shape],
         compiler_params=pltpu.CompilerParams(vmem_limit_bytes=56 << 20),
         cost_estimate=pl.CostEstimate(
-            flops=2 * work * (2 * LAT + 2 * ROPE), bytes_accessed=8 << 20, transcendentals=work
+            flops=2 * work * (2 * LAT + 2 * ROPE), bytes_accessed=5 << 20, transcendentals=work
         ),
-    )(my_index.reshape(1), q_nope, q_rope, mine, other, w_value, norm_gain.reshape(1, HEADS * VD))
+    )(my_index.reshape(1), q_nope, q_rope, mine, other, w_value)
 
 
 def ring_place(chip, chips):
@@ -148,8 +149,8 @@
 
 
 def expert_kernel(
-    index_ref, rows_ref, hits_ref, gate_a, up_a, down_a, gate_hbm, up_hbm, down_hbm, out_ref,
-    gate_b, up_b, down_b, sems, *, hop, chips,
+    index_ref, left_ref, right_ref, hits_ref, gain_ref, gate_a, up_a, down_a, gate_hbm, up_hbm,
+    down_hbm, left_out, right_out, gate_b, up_b, down_b, sems, *, hop, chips,
 ):
     copies = [
         pltpu.make_async_copy(there, here, sems.at[i])
@@ -157,12 +158,24 @@
     ]
     for copy in copies:
         copy.start()
-    tok = rows_ref.shape[0]
+    tok, width = left_ref.shape
     my_chip, my_core = index_ref[0] // CORES, lax.rem(index_ref[0], CORES)
     place = ring_place(my_chip, chips) + chips + hop * (2 * my_core - 1)
     source = ring_chip(lax.rem(place, chips), chips) ^ my_chip
-    keep = hits_ref[pl.ds(pl.multiple_of(source * tok, tok), tok), :] > 0.0
-    rows = rows_ref[...]
+    column = lax.broadcasted_iota(jnp.int32, hits_ref.shape, 1)
+    keep = jnp.max(jnp.where(column == source, hits_ref[...], 0.0), axis=1, keepdims=True) > 0.0
+
+    left, right = left_ref[...].astype(jnp.float32), right_ref[...].astype(jnp.float32)
+    square = jnp.sum(left * left, axis=1, keepdims=True)
+    square = square + jnp.sum(right * right, axis=1, keepdims=True)
+    scale = lax.rsqrt(square / (2 * width) + NORM_EPS)
+    rows = jnp.concatenate(
+        [
+            (left * scale * gain_ref[:, :width]).astype(jnp.bfloat16),
+            (right * scale * gain_ref[:, width:]).astype(jnp.bfloat16),
+        ],
+        axis=1,
+    )
 
     def hidden(gate_ref, up_ref):
         gate_act = jnp.dot(rows, gate_ref[...], preferred_element_type=jnp.float32)
@@ -175,25 +188,27 @@
     copies[1].wait()
     hidden_b = hidden(gate_b, up_b)
     copies[2].wait()
-    out_ref[...] = part + jnp.dot(hidden_b, down_b[...], preferred_element_type=jnp.float32)
-
-
-def expert_part(my_index, rows, hits, own, swapped, hop, chips):
-    tok, features = rows.shape
+    part = part + jnp.dot(hidden_b, down_b[...], preferred_element_type=jnp.float32)
+    left_out[...] = part[:, :width]
+    right_out[...] = part[:, width:]
+
+
+def expert_part(my_index, rows, hits, gain, own, swapped, hop, chips):
+    tok, width = rows[0].shape
     units = 2 * own[0].shape[1]
     vmem, anywhere = pl.BlockSpec(memory_space=pltpu.VMEM), pl.BlockSpec(memory_space=pl.ANY)
     return pl.pallas_call(
         functools.partial(expert_kernel, hop=hop, chips=chips),
-        in_specs=[pl.BlockSpec(memory_space=pltpu.SMEM)] + [vmem] * 5 + [anywhere] * 3,
-        out_specs=vmem,
-        out_shape=jax.ShapeDtypeStruct((tok, features), jnp.float32),
+        in_specs=[pl.BlockSpec(memory_space=pltpu.SMEM)] + [vmem] * 7 + [anywhere] * 3,
+        out_specs=[vmem] * 2,
+        out_shape=[jax.ShapeDtypeStruct((tok, width), jnp.float32)] * 2,
         scratch_shapes=[pltpu.VMEM(w.shape, w.dtype) for w in swapped]
         + [pltpu.SemaphoreType.DMA((3,))],
         compiler_params=pltpu.CompilerParams(vmem_limit_bytes=24 << 20),
         cost_estimate=pl.CostEstimate(
-            flops=6 * tok * features * units, bytes_accessed=14 << 20, transcendentals=0
+            flops=12 * tok * width * units, bytes_accessed=14 << 20, transcendentals=0
         ),
-    )(my_index.reshape(1), rows, hits, *own, *swapped)
+    )(my_index.reshape(1), *rows, hits, gain, *own, *swapped)
 
 
 def local(
@@ -223,33 +238,41 @@
 
     own, mine, other = lax.optimization_barrier(((w_gate[0], w_up[0], w_down[0]), mine, other))
     swapped = tuple(lax.ppermute(w, "ctx", siblings) for w in own)
-    values, start, hits = attention(
-        my_index, q_nope, q_rope, mine, other, w_value, norm_gain
-    )
-    start, swapped = lax.optimization_barrier((start, swapped))
+    first, hits = attention(my_index, q_nope, q_rope, mine, other, w_value, 0)
+    second, _ = attention(my_index, q_nope, q_rope, mine, other, w_value, 1)
+    second, swapped = lax.optimization_barrier((second, swapped))
+    start = (first, second)
+    gain = norm_gain.reshape(1, HEADS * VD)
 
     def part_of(rows, hop):
-        return expert_part(my_index, rows, hits, own, swapped, hop, chips)
-
-    def move(block):
-        return lax.ppermute(block, "ctx", route)
-
-    def after(block, first):
-        return lax.optimization_barrier((block, first))[0]
+        return expert_part(my_index, rows, hits, gain, own, swapped, hop, chips)
+
+    def move(halves):
+        return tuple(lax.ppermute(x, "ctx", route) for x in halves)
+
+    def after(halves, before):
+        return tuple(lax.optimization_barrier(pair)[0] for pair in zip(halves, before))
+
+    def added(part, arrived):
+        return tuple(x + y.astype(jnp.float32) for x, y in zip(part, arrived))
+
+    def rounded(part):
+        return tuple(x.astype(jnp.bfloat16) for x in part)
 
     rows = move(start)
     later = move(rows) if chips > 2 else None
-    sums = part_of(rows, 1).astype(jnp.bfloat16)
+    sums = rounded(part_of(rows, 1))
     for hop in range(1, chips):
         arrived = move(sums)
         rows = later
         if hop + 2 < chips:
             later = move(after(rows, sums))
         if hop + 1 < chips:
-            sums = (part_of(rows, hop + 1) + arrived.astype(jnp.float32)).astype(jnp.bfloat16)
-    expert_out = part_of(after(start, sums), 0) + arrived.astype(jnp.float32)
+            sums = rounded(added(part_of(rows, hop + 1), arrived))
+    expert_out = added(part_of(after(start, sums), 0), arrived)
     gate_weight = gate_fixed.astype(jnp.float32) / 65536.0
-    return (values.astype(jnp.float32) + gate_weight * expert_out).astype(jnp.bfloat16)
+    mixed = [x.astype(jnp.float32) + gate_weight * y for x, y in zip(start, expert_out)]
+    return jnp.concatenate([x.astype(jnp.bfloat16) for x in mixed], axis=1)
 
 
 def solution(mesh):

time: 126 us -> 146 us (1.16)
  waiting for transfers between devices: 34.5 us -> 48.1 us
  Pallas kernels: 50.3 us -> 53.9 us
  starting transfers between devices: 36.4 us -> 39.6 us
    ppermute x14 -> x28, waiting for transfers between devices: 27.9 us -> 41.5 us  [move(): return tuple((lax.ppermute(x, 'ctx', route) for x in halves))]
    ppermute x14 -> x28, starting transfers between devices: 24.3 us -> 27.5 us  [move(): return tuple((lax.ppermute(x, 'ctx', route) for x in halves))]
    pallas_call x1 -> x2, Pallas kernels: 13.1 us -> 15.5 us  [attention(): pl.pallas_call(functools.partial(attention_kernel, tok=tok), grid_spec=gr...]
  transfers between devices with their start and end apart: 25 -> 39, of which waited for: 15 -> 15; matrix products, arithmetic and copies ran while one was open for 0% -> 0% of each run, Pallas kernels for 40% -> 37%
where the time goes in v6:
time: 146 us
  Pallas kernels  53.9 us (37%)
  waiting for transfers between devices  48.1 us (33%)
  starting transfers between devices  39.6 us (27%)
  other arithmetic  3.33 us (2%)
    ppermute x28, waiting for transfers between devices, move(): return tuple((lax.ppermute(x, 'ctx', route) for x in halves))  41.5 us
    pallas_call x8, Pallas kernels, expert_part(): pl.pallas_call(functools.partial(expert_kernel, hop=hop, chips=chips), in...  38.3 us
    ppermute x28, starting transfers between devices, move(): return tuple((lax.ppermute(x, 'ctx', route) for x in halves))  27.5 us
    pallas_call x2, Pallas kernels, attention(): pl.pallas_call(functools.partial(attention_kernel, tok=tok), grid_spec=gr...  15.5 us
    ppermute x7, starting transfers between devices, from_chip(): lax.ppermute(block, 'ctx', [(i, i ^ step * CORES) for i in range(n_ctx)])  11.4 us
    ppermute x7, waiting for transfers between devices, from_chip(): lax.ppermute(block, 'ctx', [(i, i ^ step * CORES) for i in range(n_ctx)])  4.54 us
  transfers between devices with their start and end apart: 39, of which 15 were waited for; matrix products, arithmetic and copies ran while one was open for 0% of the time, Pallas kernels for 37%

profile of v6, /device:TPU:0, one launch (start us, length us, event | category | flops | bytes accessed | tf_op | source)
XLA Modules:
  0.0 145.7 jit_solution(15366521669247628055)
XLA Ops:
  1.7 4.1 %collective-permute-start.3 = (bf16[64,640]{1,0:T(8,128)(2,1)S(1)}, bf16[64,640]{1,0:T(8,128)(2,1)S(1)}, u32[]{:S(2)}, u32[]{:S(2)}) collective-permute-start(bf16[64,640]{1,0:T(8,128)(2,1)S(1)} %get-tuple-element.85), channel_id=1, source_target_pairs={{0,8},{1,9},{2,10},{3,11},{4,12},{5,13},{6,14},{7,15},{8,0},{9,1},... | collective-permute-start | bytes 245768 | tf_op jit(solution)/shard_map/ppermute | solution.py:229
  5.8 1.5 %collective-permute-start = (bf16[64,640]{1,0:T(8,128)(2,1)S(1)}, bf16[64,640]{1,0:T(8,128)(2,1)S(1)}, u32[]{:S(2)}, u32[]{:S(2)}) collective-permute-start(bf16[64,640]{1,0:T(8,128)(2,1)S(1)} %get-tuple-element.85), channel_id=1, source_target_pairs={{0,2},{1,3},{2,0},{3,1},{4,6},{5,7},{6,4},{7,5},{8,10},{9,11},{10,... | collective-permute-start | bytes 245768 | tf_op jit(solution)/shard_map/ppermute | solution.py:229
  7.3 1.6 %collective-permute-start.1 = (bf16[64,640]{1,0:T(8,128)(2,1)S(1)}, bf16[64,640]{1,0:T(8,128)(2,1)S(1)}, u32[]{:S(2)}, u32[]{:S(2)}) collective-permute-start(bf16[64,640]{1,0:T(8,128)(2,1)S(1)} %get-tuple-element.85), channel_id=1, source_target_pairs={{0,4},{1,5},{2,6},{3,7},{4,0},{5,1},{6,2},{7,3},{8,12},{9,13},{10,... | collective-permute-start | bytes 245768 | tf_op jit(solution)/shard_map/ppermute | solution.py:229
  9.8 1.6 %collective-permute-start.4 = (bf16[64,640]{1,0:T(8,128)(2,1)S(1)}, bf16[64,640]{1,0:T(8,128)(2,1)S(1)}, u32[]{:S(2)}, u32[]{:S(2)}) collective-permute-start(bf16[64,640]{1,0:T(8,128)(2,1)S(1)} %collective-permute-done.3), channel_id=1, source_target_pairs={{0,2},{1,3},{2,0},{3,1},{4,6},{5,7},{6,4},{7,5},{8,10},{9,11},{10,... | collective-permute-start | bytes 245768 | tf_op jit(solution)/shard_map/ppermute | solution.py:229
  12.4 1.3 collective-permute-start.6
  15.9 1.8 %collective-permute-done.6 = bf16[64,640]{1,0:T(8,128)(2,1)S(1)} collective-permute-done((bf16[64,640]{1,0:T(8,128)(2,1)S(1)}, bf16[64,640]{1,0:T(8,128)(2,1)S(1)}, u32[]{:S(2)}, u32[]{:S(2)}) %collective-permute-start.6) | collective-permute-done | bytes 81952 | tf_op jit(solution)/shard_map/ppermute | solution.py:229
  17.8 2.1 %collective-permute-done.7.other_ref = bf16[512,640]{1,0:T(8,128)(2,1)S(1)} collective-permute-done((bf16[512,640]{1,0:T(8,128)(2,1)S(1)}, bf16[512,640]{1,0:T(8,128)(2,1)S(1)}, u32[]{:S(2)}, u32[]{:S(2)}) %collective-permute-start.7) | collective-permute-done | bytes 655392 | tf_op jit(solution)/shard_map/ppermute | solution.py:237
  20.8 7.5 %shard_map.109 = (bf16[64,2048]{1,0:T(8,128)(2,1)}, f32[64,8]{1,0:T(8,128)}) custom-call(s32[1]{0:T(128)} %bitcast.index_ref, bf16[64,16384]{1,0:T(8,128)(2,1)} %q_ref.3, bf16[64,2048]{1,0:T(8,128)(2,1)} %qr_ref.3, bf16[512,640]{1,0:T(8,128)(2,1)} %copy-done.7, bf16[512,640]{1,0:T(8,128)(2,1)} %copy-done.8, bf16[32,512,128]{2,1,0:T(8,128)(2,1)} %wv_ref.3), custom_call_target="tpu_custom_call" | custom-call | flops 2415919104 | bytes 5242880 | tf_op jit(solution)/shard_map/pallas_call | solution.py:132
  29.4 8.1 %shard_map.110 = (bf16[64,2048]{1,0:T(8,128)(2,1)}, f32[64,8]{1,0:T(8,128)}) custom-call(s32[1]{0:T(128)} %bitcast.index_ref, bf16[64,16384]{1,0:T(8,128)(2,1)} %q_ref.3, bf16[64,2048]{1,0:T(8,128)(2,1)} %qr_ref.3, bf16[512,640]{1,0:T(8,128)(2,1)} %copy-done.7, bf16[512,640]{1,0:T(8,128)(2,1)} %copy-done.8, bf16[32,512,128]{2,1,0:T(8,128)(2,1)} %wv_ref.3), custom_call_target="tpu_custom_call" | custom-call | flops 2415919104 | bytes 5242880 | tf_op jit(solution)/shard_map/pallas_call | solution.py:132
  37.5 2.2 %collective-permute-start.13 = (bf16[64,2048]{1,0:T(8,128)(2,1)}, bf16[64,2048]{1,0:T(8,128)(2,1)S(1)}, u32[]{:S(2)}, u32[]{:S(2)}) collective-permute-start(bf16[64,2048]{1,0:T(8,128)(2,1)} %get-tuple-element.82.right_ref), channel_id=1, source_target_pairs={{0,4},{1,3},{4,8},{5,1},{8,12},{9,5},{12,14},{13,9},{14,10},{15,13... | collective-permute-start | bytes 786440 | tf_op jit(solution)/shard_map/ppermute | solution.py:251
  40.3 3.8 %collective-permute-done.13.right_ref = bf16[64,2048]{1,0:T(8,128)(2,1)S(1)} collective-permute-done((bf16[64,2048]{1,0:T(8,128)(2,1)}, bf16[64,2048]{1,0:T(8,128)(2,1)S(1)}, u32[]{:S(2)}, u32[]{:S(2)}) %collective-permute-start.13) | collective-permute-done | bytes 262176 | tf_op jit(solution)/shard_map/ppermute | solution.py:251
  44.1 2.2 %collective-permute-start.15 = (bf16[64,2048]{1,0:T(8,128)(2,1)S(1)}, bf16[64,2048]{1,0:T(8,128)(2,1)S(1)}, u32[]{:S(2)}, u32[]{:S(2)}) collective-permute-start(bf16[64,2048]{1,0:T(8,128)(2,1)S(1)} %collective-permute-done.13.right_ref), channel_id=1, source_target_pairs={{0,4},{1,3},{4,8},{5,1},{8,12},{9,5},{12,14},{13,9},{14,10},{15,13... | collective-permute-start | bytes 786440 | tf_op jit(solution)/shard_map/ppermute | solution.py:251
  46.4 4.8 %shard_map.111 = (f32[64,2048]{1,0:T(8,128)S(1)}, f32[64,2048]{1,0:T(8,128)S(1)}) custom-call(s32[1]{0:T(128)} %bitcast.index_ref, bf16[64,2048]{1,0:T(8,128)(2,1)S(1)} %collective-permute-done.8.left_ref, bf16[64,2048]{1,0:T(8,128)(2,1)S(1)} %collective-permute-done.13.right_ref, f32[64,8]{1,0:T(8,128)S(1)} %copy-done.3, f32[1,4096]{1,0:T(1,128)S(1)} %bitcast.36, ...), custom_call_target="tpu_custom_call" | custom-call | flops 805306368 | bytes 14680064 | tf_op jit(solution)/shard_map/pallas_call | solution.py:200
  51.8 1.6 %collective-permute-start.14 = (bf16[64,2048]{1,0:T(8,128)(2,1)S(1)}, bf16[64,2048]{1,0:T(8,128)(2,1)S(1)}, u32[]{:S(2)}, u32[]{:S(2)}) collective-permute-start(bf16[64,2048]{1,0:T(8,128)(2,1)S(1)} %collective-permute-done.9.left_ref), channel_id=1, source_target_pairs={{0,4},{1,3},{4,8},{5,1},{8,12},{9,5},{12,14},{13,9},{14,10},{15,13... | collective-permute-start | bytes 786440 | tf_op jit(solution)/shard_map/ppermute | solution.py:251
  54.4 4.8 %shard_map.112 = (f32[64,2048]{1,0:T(8,128)S(1)}, f32[64,2048]{1,0:T(8,128)S(1)}) custom-call(s32[1]{0:T(128)} %bitcast.index_ref, bf16[64,2048]{1,0:T(8,128)(2,1)S(1)} %collective-permute-done.9.left_ref, bf16[64,2048]{1,0:T(8,128)(2,1)S(1)} %collective-permute-done.15.right_ref, f32[64,8]{1,0:T(8,128)S(1)} %copy-done.3, f32[1,4096]{1,0:T(1,128)S(1)} %bitcast.37, ...), custom_call_target="tpu_custom_call" | custom-call | flops 805306368 | bytes 14680064 | tf_op jit(solution)/shard_map/pallas_call | solution.py:200
  61.0 1.6 %collective-permute-start.18 = (bf16[64,2048]{1,0:T(8,128)(2,1)S(1)}, bf16[64,2048]{1,0:T(8,128)(2,1)S(1)}, u32[]{:S(2)}, u32[]{:S(2)}) collective-permute-start(bf16[64,2048]{1,0:T(8,128)(2,1)S(1)} %collective-permute-done.15.right_ref), channel_id=1, source_target_pairs={{0,4},{1,3},{4,8},{5,1},{8,12},{9,5},{12,14},{13,9},{14,10},{15,13... | collective-permute-start | bytes 786440 | tf_op jit(solution)/shard_map/ppermute | solution.py:251
  64.1 7.6 %collective-permute-done.18.right_ref = bf16[64,2048]{1,0:T(8,128)(2,1)S(1)} collective-permute-done((bf16[64,2048]{1,0:T(8,128)(2,1)S(1)}, bf16[64,2048]{1,0:T(8,128)(2,1)S(1)}, u32[]{:S(2)}, u32[]{:S(2)}) %collective-permute-start.18) | collective-permute-done | bytes 262176 | tf_op jit(solution)/shard_map/ppermute | solution.py:251
  71.7 4.8 %shard_map.113 = (f32[64,2048]{1,0:T(8,128)S(1)}, f32[64,2048]{1,0:T(8,128)S(1)}) custom-call(s32[1]{0:T(128)} %bitcast.index_ref, bf16[64,2048]{1,0:T(8,128)(2,1)S(1)} %collective-permute-done.14.left_ref, bf16[64,2048]{1,0:T(8,128)(2,1)S(1)} %collective-permute-done.18.right_ref, f32[64,8]{1,0:T(8,128)S(1)} %copy-done.3, f32[1,4096]{1,0:T(1,128)S(1)} %bitcast.38, ...), custom_call_target="tpu_custom_call" | custom-call | flops 805306368 | bytes 14680064 | tf_op jit(solution)/shard_map/pallas_call | solution.py:200
  77.2 1.6 %collective-permute-start.20 = (bf16[64,2048]{1,0:T(8,128)(2,1)S(1)}, bf16[64,2048]{1,0:T(8,128)(2,1)S(1)}, u32[]{:S(2)}, u32[]{:S(2)}) collective-permute-start(bf16[64,2048]{1,0:T(8,128)(2,1)S(1)} %collective-permute-done.17.left_ref), channel_id=1, source_target_pairs={{0,4},{1,3},{4,8},{5,1},{8,12},{9,5},{12,14},{13,9},{14,10},{15,13... | collective-permute-start | bytes 786440 | tf_op jit(solution)/shard_map/ppermute | solution.py:251
  79.8 8.7 %collective-permute-done.22.right_ref = bf16[64,2048]{1,0:T(8,128)(2,1)S(1)} collective-permute-done((bf16[64,2048]{1,0:T(8,128)(2,1)S(1)}, bf16[64,2048]{1,0:T(8,128)(2,1)S(1)}, u32[]{:S(2)}, u32[]{:S(2)}) %collective-permute-start.22) | collective-permute-done | bytes 262176 | tf_op jit(solution)/shard_map/ppermute | solution.py:251
  88.6 4.8 %shard_map.114 = (f32[64,2048]{1,0:T(8,128)S(1)}, f32[64,2048]{1,0:T(8,128)S(1)}) custom-call(s32[1]{0:T(128)} %bitcast.index_ref, bf16[64,2048]{1,0:T(8,128)(2,1)S(1)} %collective-permute-done.17.left_ref, bf16[64,2048]{1,0:T(8,128)(2,1)S(1)} %collective-permute-done.22.right_ref, f32[64,8]{1,0:T(8,128)S(1)} %copy-done.3, f32[1,4096]{1,0:T(1,128)S(1)} %bitcast.39, ...), custom_call_target="tpu_custom_call" | custom-call | flops 805306368 | bytes 14680064 | tf_op jit(solution)/shard_map/pallas_call | solution.py:200
  94.1 1.6 %collective-permute-start.24 = (bf16[64,2048]{1,0:T(8,128)(2,1)S(1)}, bf16[64,2048]{1,0:T(8,128)(2,1)S(1)}, u32[]{:S(2)}, u32[]{:S(2)}) collective-permute-start(bf16[64,2048]{1,0:T(8,128)(2,1)S(1)} %collective-permute-done.20.left_ref), channel_id=1, source_target_pairs={{0,4},{1,3},{4,8},{5,1},{8,12},{9,5},{12,14},{13,9},{14,10},{15,13... | collective-permute-start | bytes 786440 | tf_op jit(solution)/shard_map/ppermute | solution.py:251
  96.7 8.7 %collective-permute-done.26.right_ref = bf16[64,2048]{1,0:T(8,128)(2,1)S(1)} collective-permute-done((bf16[64,2048]{1,0:T(8,128)(2,1)S(1)}, bf16[64,2048]{1,0:T(8,128)(2,1)S(1)}, u32[]{:S(2)}, u32[]{:S(2)}) %collective-permute-start.26) | collective-permute-done | bytes 262176 | tf_op jit(solution)/shard_map/ppermute | solution.py:251
  105.5 4.8 %shard_map.115 = (f32[64,2048]{1,0:T(8,128)S(1)}, f32[64,2048]{1,0:T(8,128)S(1)}) custom-call(s32[1]{0:T(128)} %bitcast.index_ref, bf16[64,2048]{1,0:T(8,128)(2,1)S(1)} %collective-permute-done.20.left_ref, bf16[64,2048]{1,0:T(8,128)(2,1)S(1)} %collective-permute-done.26.right_ref, f32[64,8]{1,0:T(8,128)S(1)} %copy-done.3, f32[1,4096]{1,0:T(1,128)S(1)} %bitcast.40, ...), custom_call_target="tpu_custom_call" | custom-call | flops 805306368 | bytes 14680064 | tf_op jit(solution)/shard_map/pallas_call | solution.py:200
  111.0 1.6 %collective-permute-start.28 = (bf16[64,2048]{1,0:T(8,128)(2,1)S(1)}, bf16[64,2048]{1,0:T(8,128)(2,1)S(1)}, u32[]{:S(2)}, u32[]{:S(2)}) collective-permute-start(bf16[64,2048]{1,0:T(8,128)(2,1)S(1)} %collective-permute-done.24.left_ref), channel_id=1, source_target_pairs={{0,4},{1,3},{4,8},{5,1},{8,12},{9,5},{12,14},{13,9},{14,10},{15,13... | collective-permute-start | bytes 786440 | tf_op jit(solution)/shard_map/ppermute | solution.py:251
  113.6 8.7 %collective-permute-done.30.right_ref = bf16[64,2048]{1,0:T(8,128)(2,1)S(1)} collective-permute-done((bf16[64,2048]{1,0:T(8,128)(2,1)S(1)}, bf16[64,2048]{1,0:T(8,128)(2,1)S(1)}, u32[]{:S(2)}, u32[]{:S(2)}) %collective-permute-start.30) | collective-permute-done | bytes 262176 | tf_op jit(solution)/shard_map/ppermute | solution.py:251
  123.0 4.8 %shard_map.117 = (f32[64,2048]{1,0:T(8,128)S(1)}, f32[64,2048]{1,0:T(8,128)S(1)}) custom-call(s32[1]{0:T(128)} %bitcast.index_ref, bf16[64,2048]{1,0:T(8,128)(2,1)S(1)} %collective-permute-done.24.left_ref, bf16[64,2048]{1,0:T(8,128)(2,1)S(1)} %collective-permute-done.30.right_ref, f32[64,8]{1,0:T(8,128)S(1)} %copy-done.3, f32[1,4096]{1,0:T(1,128)S(1)} %bitcast.41, ...), custom_call_target="tpu_custom_call" | custom-call | flops 805306368 | bytes 14680064 | tf_op jit(solution)/shard_map/pallas_call | solution.py:200
  127.8 1.6 %collective-permute-start.34 = (bf16[64,2048]{1,0:T(8,128)(2,1)S(1)}, bf16[64,2048]{1,0:T(8,128)(2,1)S(1)}, u32[]{:S(2)}, u32[]{:S(2)}) collective-permute-start(bf16[64,2048]{1,0:T(8,128)(2,1)S(1)} %add_convert_fusion.5), channel_id=1, source_target_pairs={{0,4},{1,3},{4,8},{5,1},{8,12},{9,5},{12,14},{13,9},{14,10},{15,13... | collective-permute-start | bytes 786440 | tf_op jit(solution)/shard_map/ppermute | solution.py:251
  130.5 4.8 %shard_map.116 = (f32[64,2048]{1,0:T(8,128)S(1)}, f32[64,2048]{1,0:T(8,128)S(1)}) custom-call(s32[1]{0:T(128)} %bitcast.index_ref, bf16[64,2048]{1,0:T(8,128)(2,1)S(1)} %collective-permute-done.28.left_ref, bf16[64,2048]{1,0:T(8,128)(2,1)S(1)} %collective-permute-done.32.right_ref, f32[64,8]{1,0:T(8,128)S(1)} %copy-done.3, f32[1,4096]{1,0:T(1,128)S(1)} %bitcast.42, ...), custom_call_target="tpu_custom_call" | custom-call | flops 805306368 | bytes 14680064 | tf_op jit(solution)/shard_map/pallas_call | solution.py:200
  135.9 1.1 collective-permute-done.36
  137.1 1.6 %collective-permute-start.38 = (bf16[64,2048]{1,0:T(8,128)(2,1)S(1)}, bf16[64,2048]{1,0:T(8,128)(2,1)S(1)}, u32[]{:S(2)}, u32[]{:S(2)}) collective-permute-start(bf16[64,2048]{1,0:T(8,128)(2,1)S(1)} %add_convert_fusion.2), channel_id=1, source_target_pairs={{0,4},{1,3},{4,8},{5,1},{8,12},{9,5},{12,14},{13,9},{14,10},{15,13... | collective-permute-start | bytes 786440 | tf_op jit(solution)/shard_map/ppermute | solution.py:251
  138.8 4.8 %shard_map.118 = (f32[64,2048]{1,0:T(8,128)S(1)}, f32[64,2048]{1,0:T(8,128)S(1)}) custom-call(s32[1]{0:T(128)} %bitcast.index_ref, bf16[64,2048]{1,0:T(8,128)(2,1)S(1)} %copy-done.5, bf16[64,2048]{1,0:T(8,128)(2,1)S(1)} %copy-done.6, f32[64,8]{1,0:T(8,128)S(1)} %copy-done.3, f32[1,4096]{1,0:T(1,128)S(1)} %bitcast.43, bf16[4096,256]{1,0:T(8,128)(2,1)S(1)} %bitcast.17, ...), custom_call_target="tpu_custom_call" | custom-call | flops 805306368 | bytes 14680064 | tf_op jit(solution)/shard_map/pallas_call | solution.py:200
  (103 shorter events, 23.3 us)
Async XLA Ops:
  1.7 8.1 %collective-permute-start.3 = (bf16[64,640]{1,0:T(8,128)(2,1)S(1)}, bf16[64,640]{1,0:T(8,128)(2,1)S(1)}, u32[]{:S(2)}, u32[]{:S(2)}) collective-permute-start(bf16[64,640]{1,0:T(8,128)(2,1)S(1)} %get-tuple-element.85), channel_id=1, source_target_pairs={{0,8},{1,9},{2,10},{3,11},{4,12},{5,13},{6,14},{7,15},{8,0},{9,1},... | collective-permute-start | bytes 245768 | tf_op jit(solution)/shard_map/ppermute | solution.py:229
  19.9 17.6 %collective-permute-start.10 = (bf16[4096,256]{1,0:T(8,128)(2,1)}, bf16[4096,256]{1,0:T(8,128)(2,1)}, u32[]{:S(2)}, u32[]{:S(2)}) collective-permute-start(bf16[4096,256]{1,0:T(8,128)(2,1)} %bitcast.9), channel_id=1, source_target_pairs={{0,1},{1,0},{2,3},{3,2},{4,5},{5,4},{6,7},{7,6},{8,9},{9,8},{10,11... | collective-permute-start | bytes 6291464 | tf_op jit(solution)/shard_map/ppermute | solution.py:240
  20.0 17.5 %collective-permute-start.11 = (bf16[4096,256]{1,0:T(8,128)(2,1)}, bf16[4096,256]{1,0:T(8,128)(2,1)}, u32[]{:S(2)}, u32[]{:S(2)}) collective-permute-start(bf16[4096,256]{1,0:T(8,128)(2,1)} %bitcast.18), channel_id=1, source_target_pairs={{0,1},{1,0},{2,3},{3,2},{4,5},{5,4},{6,7},{7,6},{8,9},{9,8},{10,11... | collective-permute-start | bytes 6291464 | tf_op jit(solution)/shard_map/ppermute | solution.py:240
  20.4 17.1 %collective-permute-start.12 = (bf16[256,4096]{1,0:T(8,128)(2,1)}, bf16[256,4096]{1,0:T(8,128)(2,1)}, u32[]{:S(2)}, u32[]{:S(2)}) collective-permute-start(bf16[256,4096]{1,0:T(8,128)(2,1)} %bitcast.27), channel_id=1, source_target_pairs={{0,1},{1,0},{2,3},{3,2},{4,5},{5,4},{6,7},{7,6},{8,9},{9,8},{10,11... | collective-permute-start | bytes 6291464 | tf_op jit(solution)/shard_map/ppermute | solution.py:240
  28.3 11.5 %collective-permute-start.8 = (bf16[64,2048]{1,0:T(8,128)(2,1)}, bf16[64,2048]{1,0:T(8,128)(2,1)S(1)}, u32[]{:S(2)}, u32[]{:S(2)}) collective-permute-start(bf16[64,2048]{1,0:T(8,128)(2,1)} %get-tuple-element.79.left_ref), channel_id=1, source_target_pairs={{0,4},{1,3},{4,8},{5,1},{8,12},{9,5},{12,14},{13,9},{14,10},{15,13... | collective-permute-start | bytes 786440 | tf_op jit(solution)/shard_map/ppermute | solution.py:251
  37.5 6.6 %collective-permute-start.13 = (bf16[64,2048]{1,0:T(8,128)(2,1)}, bf16[64,2048]{1,0:T(8,128)(2,1)S(1)}, u32[]{:S(2)}, u32[]{:S(2)}) collective-permute-start(bf16[64,2048]{1,0:T(8,128)(2,1)} %get-tuple-element.82.right_ref), channel_id=1, source_target_pairs={{0,4},{1,3},{4,8},{5,1},{8,12},{9,5},{12,14},{13,9},{14,10},{15,13... | collective-permute-start | bytes 786440 | tf_op jit(solution)/shard_map/ppermute | solution.py:251
  39.8 12.1 %collective-permute-start.9 = (bf16[64,2048]{1,0:T(8,128)(2,1)S(1)}, bf16[64,2048]{1,0:T(8,128)(2,1)S(1)}, u32[]{:S(2)}, u32[]{:S(2)}) collective-permute-start(bf16[64,2048]{1,0:T(8,128)(2,1)S(1)} %collective-permute-done.8.left_ref), channel_id=1, source_target_pairs={{0,4},{1,3},{4,8},{5,1},{8,12},{9,5},{12,14},{13,9},{14,10},{15,13... | collective-permute-start | bytes 786440 | tf_op jit(solution)/shard_map/ppermute | solution.py:251
  44.1 10.3 %collective-permute-start.15 = (bf16[64,2048]{1,0:T(8,128)(2,1)S(1)}, bf16[64,2048]{1,0:T(8,128)(2,1)S(1)}, u32[]{:S(2)}, u32[]{:S(2)}) collective-permute-start(bf16[64,2048]{1,0:T(8,128)(2,1)S(1)} %collective-permute-done.13.right_ref), channel_id=1, source_target_pairs={{0,4},{1,3},{4,8},{5,1},{8,12},{9,5},{12,14},{13,9},{14,10},{15,13... | collective-permute-start | bytes 786440 | tf_op jit(solution)/shard_map/ppermute | solution.py:251
  51.2 8.0 %collective-permute-start.16 = (bf16[64,2048]{1,0:T(8,128)(2,1)S(1)}, bf16[64,2048]{1,0:T(8,128)(2,1)S(1)}, u32[]{:S(2)}, u32[]{:S(2)}) collective-permute-start(bf16[64,2048]{1,0:T(8,128)(2,1)S(1)} %convert_element_type.105), channel_id=1, source_target_pairs={{0,4},{1,3},{4,8},{5,1},{8,12},{9,5},{12,14},{13,9},{14,10},{15,13... | collective-permute-start | bytes 786440 | tf_op jit(solution)/shard_map/ppermute | solution.py:251
  51.8 8.6 %collective-permute-start.14 = (bf16[64,2048]{1,0:T(8,128)(2,1)S(1)}, bf16[64,2048]{1,0:T(8,128)(2,1)S(1)}, u32[]{:S(2)}, u32[]{:S(2)}) collective-permute-start(bf16[64,2048]{1,0:T(8,128)(2,1)S(1)} %collective-permute-done.9.left_ref), channel_id=1, source_target_pairs={{0,4},{1,3},{4,8},{5,1},{8,12},{9,5},{12,14},{13,9},{14,10},{15,13... | collective-permute-start | bytes 786440 | tf_op jit(solution)/shard_map/ppermute | solution.py:251
  53.4 9.8 %collective-permute-start.21 = (bf16[64,2048]{1,0:T(8,128)(2,1)S(1)}, bf16[64,2048]{1,0:T(8,128)(2,1)S(1)}, u32[]{:S(2)}, u32[]{:S(2)}) collective-permute-start(bf16[64,2048]{1,0:T(8,128)(2,1)S(1)} %convert_element_type.108), channel_id=1, source_target_pairs={{0,4},{1,3},{4,8},{5,1},{8,12},{9,5},{12,14},{13,9},{14,10},{15,13... | collective-permute-start | bytes 786440 | tf_op jit(solution)/shard_map/ppermute | solution.py:251
  59.3 17.2 %collective-permute-start.19 = (bf16[64,2048]{1,0:T(8,128)(2,1)S(1)}, bf16[64,2048]{1,0:T(8,128)(2,1)S(1)}, u32[]{:S(2)}, u32[]{:S(2)}) collective-permute-start(bf16[64,2048]{1,0:T(8,128)(2,1)S(1)} %add_convert_fusion.13), channel_id=1, source_target_pairs={{0,4},{1,3},{4,8},{5,1},{8,12},{9,5},{12,14},{13,9},{14,10},{15,13... | collective-permute-start | bytes 786440 | tf_op jit(solution)/shard_map/ppermute | solution.py:251
  60.4 16.7 %collective-permute-start.17 = (bf16[64,2048]{1,0:T(8,128)(2,1)S(1)}, bf16[64,2048]{1,0:T(8,128)(2,1)S(1)}, u32[]{:S(2)}, u32[]{:S(2)}) collective-permute-start(bf16[64,2048]{1,0:T(8,128)(2,1)S(1)} %collective-permute-done.14.left_ref), channel_id=1, source_target_pairs={{0,4},{1,3},{4,8},{5,1},{8,12},{9,5},{12,14},{13,9},{14,10},{15,13... | collective-permute-start | bytes 786440 | tf_op jit(solution)/shard_map/ppermute | solution.py:251
  61.0 10.7 %collective-permute-start.18 = (bf16[64,2048]{1,0:T(8,128)(2,1)S(1)}, bf16[64,2048]{1,0:T(8,128)(2,1)S(1)}, u32[]{:S(2)}, u32[]{:S(2)}) collective-permute-start(bf16[64,2048]{1,0:T(8,128)(2,1)S(1)} %collective-permute-done.15.right_ref), channel_id=1, source_target_pairs={{0,4},{1,3},{4,8},{5,1},{8,12},{9,5},{12,14},{13,9},{14,10},{15,13... | collective-permute-start | bytes 786440 | tf_op jit(solution)/shard_map/ppermute | solution.py:251
  63.3 16.4 %collective-permute-start.25 = (bf16[64,2048]{1,0:T(8,128)(2,1)S(1)}, bf16[64,2048]{1,0:T(8,128)(2,1)S(1)}, u32[]{:S(2)}, u32[]{:S(2)}) collective-permute-start(bf16[64,2048]{1,0:T(8,128)(2,1)S(1)} %add_convert_fusion.11), channel_id=1, source_target_pairs={{0,4},{1,3},{4,8},{5,1},{8,12},{9,5},{12,14},{13,9},{14,10},{15,13... | collective-permute-start | bytes 786440 | tf_op jit(solution)/shard_map/ppermute | solution.py:251
  76.5 16.8 %collective-permute-start.23 = (bf16[64,2048]{1,0:T(8,128)(2,1)S(1)}, bf16[64,2048]{1,0:T(8,128)(2,1)S(1)}, u32[]{:S(2)}, u32[]{:S(2)}) collective-permute-start(bf16[64,2048]{1,0:T(8,128)(2,1)S(1)} %add_convert_fusion.12), channel_id=1, source_target_pairs={{0,4},{1,3},{4,8},{5,1},{8,12},{9,5},{12,14},{13,9},{14,10},{15,13... | collective-permute-start | bytes 786440 | tf_op jit(solution)/shard_map/ppermute | solution.py:251
  77.2 16.9 %collective-permute-start.20 = (bf16[64,2048]{1,0:T(8,128)(2,1)S(1)}, bf16[64,2048]{1,0:T(8,128)(2,1)S(1)}, u32[]{:S(2)}, u32[]{:S(2)}) collective-permute-start(bf16[64,2048]{1,0:T(8,128)(2,1)S(1)} %collective-permute-done.17.left_ref), channel_id=1, source_target_pairs={{0,4},{1,3},{4,8},{5,1},{8,12},{9,5},{12,14},{13,9},{14,10},{15,13... | collective-permute-start | bytes 786440 | tf_op jit(solution)/shard_map/ppermute | solution.py:251
  78.7 9.8 %collective-permute-start.22 = (bf16[64,2048]{1,0:T(8,128)(2,1)S(1)}, bf16[64,2048]{1,0:T(8,128)(2,1)S(1)}, u32[]{:S(2)}, u32[]{:S(2)}) collective-permute-start(bf16[64,2048]{1,0:T(8,128)(2,1)S(1)} %collective-permute-done.18.right_ref), channel_id=1, source_target_pairs={{0,4},{1,3},{4,8},{5,1},{8,12},{9,5},{12,14},{13,9},{14,10},{15,13... | collective-permute-start | bytes 786440 | tf_op jit(solution)/shard_map/ppermute | solution.py:251
  79.7 16.9 %collective-permute-start.29 = (bf16[64,2048]{1,0:T(8,128)(2,1)S(1)}, bf16[64,2048]{1,0:T(8,128)(2,1)S(1)}, u32[]{:S(2)}, u32[]{:S(2)}) collective-permute-start(bf16[64,2048]{1,0:T(8,128)(2,1)S(1)} %add_convert_fusion.9), channel_id=1, source_target_pairs={{0,4},{1,3},{4,8},{5,1},{8,12},{9,5},{12,14},{13,9},{14,10},{15,13... | collective-permute-start | bytes 786440 | tf_op jit(solution)/shard_map/ppermute | solution.py:251
  93.4 16.8 %collective-permute-start.27 = (bf16[64,2048]{1,0:T(8,128)(2,1)S(1)}, bf16[64,2048]{1,0:T(8,128)(2,1)S(1)}, u32[]{:S(2)}, u32[]{:S(2)}) collective-permute-start(bf16[64,2048]{1,0:T(8,128)(2,1)S(1)} %add_convert_fusion.10), channel_id=1, source_target_pairs={{0,4},{1,3},{4,8},{5,1},{8,12},{9,5},{12,14},{13,9},{14,10},{15,13... | collective-permute-start | bytes 786440 | tf_op jit(solution)/shard_map/ppermute | solution.py:251
  94.1 16.9 %collective-permute-start.24 = (bf16[64,2048]{1,0:T(8,128)(2,1)S(1)}, bf16[64,2048]{1,0:T(8,128)(2,1)S(1)}, u32[]{:S(2)}, u32[]{:S(2)}) collective-permute-start(bf16[64,2048]{1,0:T(8,128)(2,1)S(1)} %collective-permute-done.20.left_ref), channel_id=1, source_target_pairs={{0,4},{1,3},{4,8},{5,1},{8,12},{9,5},{12,14},{13,9},{14,10},{15,13... | collective-permute-start | bytes 786440 | tf_op jit(solution)/shard_map/ppermute | solution.py:251
  95.6 9.8 %collective-permute-start.26 = (bf16[64,2048]{1,0:T(8,128)(2,1)S(1)}, bf16[64,2048]{1,0:T(8,128)(2,1)S(1)}, u32[]{:S(2)}, u32[]{:S(2)}) collective-permute-start(bf16[64,2048]{1,0:T(8,128)(2,1)S(1)} %collective-permute-done.22.right_ref), channel_id=1, source_target_pairs={{0,4},{1,3},{4,8},{5,1},{8,12},{9,5},{12,14},{13,9},{14,10},{15,13... | collective-permute-start | bytes 786440 | tf_op jit(solution)/shard_map/ppermute | solution.py:251
  96.6 16.9 %collective-permute-start.31 = (bf16[64,2048]{1,0:T(8,128)(2,1)S(1)}, bf16[64,2048]{1,0:T(8,128)(2,1)S(1)}, u32[]{:S(2)}, u32[]{:S(2)}) collective-permute-start(bf16[64,2048]{1,0:T(8,128)(2,1)S(1)} %add_convert_fusion.7), channel_id=1, source_target_pairs={{0,4},{1,3},{4,8},{5,1},{8,12},{9,5},{12,14},{13,9},{14,10},{15,13... | collective-permute-start | bytes 786440 | tf_op jit(solution)/shard_map/ppermute | solution.py:251
  110.3 17.4 %collective-permute-start.33 = (bf16[64,2048]{1,0:T(8,128)(2,1)S(1)}, bf16[64,2048]{1,0:T(8,128)(2,1)S(1)}, u32[]{:S(2)}, u32[]{:S(2)}) collective-permute-start(bf16[64,2048]{1,0:T(8,128)(2,1)S(1)} %add_convert_fusion.8), channel_id=1, source_target_pairs={{0,4},{1,3},{4,8},{5,1},{8,12},{9,5},{12,14},{13,9},{14,10},{15,13... | collective-permute-start | bytes 786440 | tf_op jit(solution)/shard_map/ppermute | solution.py:251
  111.0 19.5 %collective-permute-start.28 = (bf16[64,2048]{1,0:T(8,128)(2,1)S(1)}, bf16[64,2048]{1,0:T(8,128)(2,1)S(1)}, u32[]{:S(2)}, u32[]{:S(2)}) collective-permute-start(bf16[64,2048]{1,0:T(8,128)(2,1)S(1)} %collective-permute-done.24.left_ref), channel_id=1, source_target_pairs={{0,4},{1,3},{4,8},{5,1},{8,12},{9,5},{12,14},{13,9},{14,10},{15,13... | collective-permute-start | bytes 786440 | tf_op jit(solution)/shard_map/ppermute | solution.py:251
  112.5 9.8 %collective-permute-start.30 = (bf16[64,2048]{1,0:T(8,128)(2,1)S(1)}, bf16[64,2048]{1,0:T(8,128)(2,1)S(1)}, u32[]{:S(2)}, u32[]{:S(2)}) collective-permute-start(bf16[64,2048]{1,0:T(8,128)(2,1)S(1)} %collective-permute-done.26.right_ref), channel_id=1, source_target_pairs={{0,4},{1,3},{4,8},{5,1},{8,12},{9,5},{12,14},{13,9},{14,10},{15,13... | collective-permute-start | bytes 786440 | tf_op jit(solution)/shard_map/ppermute | solution.py:251
  113.5 15.9 %collective-permute-start.35 = (bf16[64,2048]{1,0:T(8,128)(2,1)S(1)}, bf16[64,2048]{1,0:T(8,128)(2,1)S(1)}, u32[]{:S(2)}, u32[]{:S(2)}) collective-permute-start(bf16[64,2048]{1,0:T(8,128)(2,1)S(1)} %add_convert_fusion.6), channel_id=1, source_target_pairs={{0,4},{1,3},{4,8},{5,1},{8,12},{9,5},{12,14},{13,9},{14,10},{15,13... | collective-permute-start | bytes 786440 | tf_op jit(solution)/shard_map/ppermute | solution.py:251
  122.4 8.1 %collective-permute-start.32 = (bf16[64,2048]{1,0:T(8,128)(2,1)S(1)}, bf16[64,2048]{1,0:T(8,128)(2,1)S(1)}, u32[]{:S(2)}, u32[]{:S(2)}) collective-permute-start(bf16[64,2048]{1,0:T(8,128)(2,1)S(1)} %collective-permute-done.30.right_ref), channel_id=1, source_target_pairs={{0,4},{1,3},{4,8},{5,1},{8,12},{9,5},{12,14},{13,9},{14,10},{15,13... | collective-permute-start | bytes 786440 | tf_op jit(solution)/shard_map/ppermute | solution.py:251
  127.8 7.5 %collective-permute-start.34 = (bf16[64,2048]{1,0:T(8,128)(2,1)S(1)}, bf16[64,2048]{1,0:T(8,128)(2,1)S(1)}, u32[]{:S(2)}, u32[]{:S(2)}) collective-permute-start(bf16[64,2048]{1,0:T(8,128)(2,1)S(1)} %add_convert_fusion.5), channel_id=1, source_target_pairs={{0,4},{1,3},{4,8},{5,1},{8,12},{9,5},{12,14},{13,9},{14,10},{15,13... | collective-permute-start | bytes 786440 | tf_op jit(solution)/shard_map/ppermute | solution.py:251
  129.5 7.5 %collective-permute-start.36 = (bf16[64,2048]{1,0:T(8,128)(2,1)S(1)}, bf16[64,2048]{1,0:T(8,128)(2,1)S(1)}, u32[]{:S(2)}, u32[]{:S(2)}) collective-permute-start(bf16[64,2048]{1,0:T(8,128)(2,1)S(1)} %add_convert_fusion.3), channel_id=1, source_target_pairs={{0,4},{1,3},{4,8},{5,1},{8,12},{9,5},{12,14},{13,9},{14,10},{15,13... | collective-permute-start | bytes 786440 | tf_op jit(solution)/shard_map/ppermute | solution.py:251
  135.4 8.2 %collective-permute-start.37 = (bf16[64,2048]{1,0:T(8,128)(2,1)S(1)}, bf16[64,2048]{1,0:T(8,128)(2,1)S(1)}, u32[]{:S(2)}, u32[]{:S(2)}) collective-permute-start(bf16[64,2048]{1,0:T(8,128)(2,1)S(1)} %add_convert_fusion.4), channel_id=1, source_target_pairs={{0,4},{1,3},{4,8},{5,1},{8,12},{9,5},{12,14},{13,9},{14,10},{15,13... | collective-permute-start | bytes 786440 | tf_op jit(solution)/shard_map/ppermute | solution.py:251
  137.1 7.5 %collective-permute-start.38 = (bf16[64,2048]{1,0:T(8,128)(2,1)S(1)}, bf16[64,2048]{1,0:T(8,128)(2,1)S(1)}, u32[]{:S(2)}, u32[]{:S(2)}) collective-permute-start(bf16[64,2048]{1,0:T(8,128)(2,1)S(1)} %add_convert_fusion.2), channel_id=1, source_target_pairs={{0,4},{1,3},{4,8},{5,1},{8,12},{9,5},{12,14},{13,9},{14,10},{15,13... | collective-permute-start | bytes 786440 | tf_op jit(solution)/shard_map/ppermute | solution.py:251
  (17 other events, 140.5 us)

commit v7 on v5

--- a/solution.py
+++ b/solution.py
@@ -25,8 +25,8 @@
 
 
 def attention_kernel(
-    index_ref, q_ref, qr_ref, mine_ref, other_ref, wv_ref, gain_ref, values_ref, normed_ref,
-    hits_ref, stack_ref, bias_a_ref, bias_b_ref, *, tok,
+    index_ref, q_ref, qr_ref, mine_ref, other_ref, wv_ref, gain_ref, values_ref, up_ref,
+    down_ref, hits_ref, stack_ref, bias_a_ref, bias_b_ref, *, tok,
 ):
     group = pl.program_id(0)
     my_index = index_ref[0]
@@ -46,7 +46,12 @@
         lane = lax.broadcasted_iota(jnp.int32, last.shape, 1)
         named = jnp.max(jnp.where(lane >= ROPE, last, -1.0), axis=1, keepdims=True)
         my_expert = (my_index // SPAN).astype(jnp.float32)
-        hits_ref[...] = jnp.where(named == my_expert, 1.0, 0.0)
+        hits = jnp.where(named == my_expert, 1.0, 0.0)
+        column = lax.broadcasted_iota(jnp.int32, hits_ref.shape, 1)
+        table = jnp.zeros(hits_ref.shape, jnp.float32)
+        for place in range(keys // tok):
+            table = jnp.where(column == place, hits[place * tok : (place + 1) * tok], table)
+        hits_ref[...] = table
 
     lane = lax.broadcasted_iota(jnp.int32, (tok, 2 * ROPE), 1)
     for head in range(HEAD_GROUP):
@@ -83,11 +88,14 @@
             preferred_element_type=jnp.float32,
         )
         latent = (mixed.reshape(SUB_HEADS, tok, LAT) / total).astype(jnp.bfloat16)
-        for head in range(SUB_HEADS):
-            value = jnp.dot(
-                latent[head], wv_ref[sub * SUB_HEADS + head], preferred_element_type=jnp.float32
-            )
-            parts.append(value.astype(jnp.bfloat16))
+        for head in range(0, SUB_HEADS, 2):
+            first = sub * SUB_HEADS + head
+            pair = jnp.dot(
+                latent[head : head + 2].reshape(2 * tok, LAT),
+                jnp.concatenate([wv_ref[first], wv_ref[first + 1]], axis=1),
+                preferred_element_type=jnp.float32,
+            ).astype(jnp.bfloat16)
+            parts.extend([pair[:tok, :VD], pair[tok:, VD:]])
     wide = HEAD_GROUP * VD
     values_ref[:, pl.ds(pl.multiple_of(group * wide, wide), wide)] = jnp.concatenate(parts, axis=1)
 
@@ -96,7 +104,9 @@
         values = values_ref[...].astype(jnp.float32)
         square = jnp.mean(values * values, axis=1, keepdims=True)
         normed = values * lax.rsqrt(square + NORM_EPS) * gain_ref[...]
-        normed_ref[...] = normed.astype(jnp.bfloat16)
+        normed = normed.astype(jnp.bfloat16)
+        up_ref[...] = normed[: tok // 2]
+        down_ref[...] = normed[tok // 2 :]
 
 
 def attention(my_index, q_nope, q_rope, mine, other, w_value, norm_gain):
@@ -116,8 +126,9 @@
         ],
         out_specs=[
             pl.BlockSpec((tok, HEADS * VD), lambda g, i: (0, 0)),
-            pl.BlockSpec((tok, HEADS * VD), lambda g, i: (0, 0)),
-            pl.BlockSpec((total, 1), lambda g, i: (0, 0)),
+            pl.BlockSpec((tok // 2, HEADS * VD), lambda g, i: (0, 0)),
+            pl.BlockSpec((tok // 2, HEADS * VD), lambda g, i: (0, 0)),
+            pl.BlockSpec((tok, total // tok), lambda g, i: (0, 0)),
         ],
         scratch_shapes=[
             pltpu.VMEM((rows, LAT + 2 * ROPE), jnp.bfloat16),
@@ -126,12 +137,13 @@
         ],
     )
     shape = jax.ShapeDtypeStruct((tok, HEADS * VD), jnp.bfloat16)
-    hits_shape = jax.ShapeDtypeStruct((total, 1), jnp.float32)
+    half_shape = jax.ShapeDtypeStruct((tok // 2, HEADS * VD), jnp.bfloat16)
+    hits_shape = jax.ShapeDtypeStruct((tok, total // tok), jnp.float32)
     work = HEADS * tok * total * CORES
     return pl.pallas_call(
         functools.partial(attention_kernel, tok=tok),
         grid_spec=grid_spec,
-        out_shape=[shape, shape, hits_shape],
+        out_shape=[shape, half_shape, half_shape, hits_shape],
         compiler_params=pltpu.CompilerParams(vmem_limit_bytes=56 << 20),
         cost_estimate=pl.CostEstimate(
             flops=2 * work * (2 * LAT + 2 * ROPE), bytes_accessed=8 << 20, transcendentals=work
@@ -148,8 +160,8 @@
 
 
 def expert_kernel(
-    index_ref, rows_ref, hits_ref, gate_a, up_a, down_a, gate_hbm, up_hbm, down_hbm, out_ref,
-    gate_b, up_b, down_b, sems, *, hop, chips,
+    index_ref, upper_ref, lower_ref, hits_ref, gate_a, up_a, down_a, gate_hbm, up_hbm, down_hbm, upper_out,
+    lower_out, gate_b, up_b, down_b, sems, *, hop, chips,
 ):
     copies = [
         pltpu.make_async_copy(there, here, sems.at[i])
@@ -157,12 +169,12 @@
     ]
     for copy in copies:
         copy.start()
-    tok = rows_ref.shape[0]
     my_chip, my_core = index_ref[0] // CORES, lax.rem(index_ref[0], CORES)
     place = ring_place(my_chip, chips) + chips + hop * (2 * my_core - 1)
     source = ring_chip(lax.rem(place, chips), chips) ^ my_chip
-    keep = hits_ref[pl.ds(pl.multiple_of(source * tok, tok), tok), :] > 0.0
-    rows = rows_ref[...]
+    column = lax.broadcasted_iota(jnp.int32, hits_ref.shape, 1)
+    keep = jnp.max(jnp.where(column == source, hits_ref[...], 0.0), axis=1, keepdims=True) > 0.0
+    rows = jnp.concatenate([upper_ref[...], lower_ref[...]], axis=0)
 
     def hidden(gate_ref, up_ref):
         gate_act = jnp.dot(rows, gate_ref[...], preferred_element_type=jnp.float32)
@@ -175,25 +187,27 @@
     copies[1].wait()
     hidden_b = hidden(gate_b, up_b)
     copies[2].wait()
-    out_ref[...] = part + jnp.dot(hidden_b, down_b[...], preferred_element_type=jnp.float32)
+    part = part + jnp.dot(hidden_b, down_b[...], preferred_element_type=jnp.float32)
+    upper_out[...] = part[: upper_ref.shape[0]]
+    lower_out[...] = part[upper_ref.shape[0] :]
 
 
 def expert_part(my_index, rows, hits, own, swapped, hop, chips):
-    tok, features = rows.shape
+    tok, features = 2 * rows[0].shape[0], rows[0].shape[1]
     units = 2 * own[0].shape[1]
     vmem, anywhere = pl.BlockSpec(memory_space=pltpu.VMEM), pl.BlockSpec(memory_space=pl.ANY)
     return pl.pallas_call(
         functools.partial(expert_kernel, hop=hop, chips=chips),
-        in_specs=[pl.BlockSpec(memory_space=pltpu.SMEM)] + [vmem] * 5 + [anywhere] * 3,
-        out_specs=vmem,
-        out_shape=jax.ShapeDtypeStruct((tok, features), jnp.float32),
+        in_specs=[pl.BlockSpec(memory_space=pltpu.SMEM)] + [vmem] * 6 + [anywhere] * 3,
+        out_specs=[vmem] * 2,
+        out_shape=[jax.ShapeDtypeStruct(x.shape, jnp.float32) for x in rows],
         scratch_shapes=[pltpu.VMEM(w.shape, w.dtype) for w in swapped]
         + [pltpu.SemaphoreType.DMA((3,))],
         compiler_params=pltpu.CompilerParams(vmem_limit_bytes=24 << 20),
         cost_estimate=pl.CostEstimate(
-            flops=6 * tok * features * units, bytes_accessed=14 << 20, transcendentals=0
+            flops=40 * tok * features * units, bytes_accessed=14 << 20, transcendentals=0
         ),
-    )(my_index.reshape(1), rows, hits, *own, *swapped)
+    )(my_index.reshape(1), *rows, hits, *own, *swapped)
 
 
 def local(
@@ -223,31 +237,38 @@
 
     own, mine, other = lax.optimization_barrier(((w_gate[0], w_up[0], w_down[0]), mine, other))
     swapped = tuple(lax.ppermute(w, "ctx", siblings) for w in own)
-    values, start, hits = attention(
+    values, upper, lower, hits = attention(
         my_index, q_nope, q_rope, mine, other, w_value, norm_gain
     )
-    start, swapped = lax.optimization_barrier((start, swapped))
+    start, swapped = lax.optimization_barrier(((upper, lower), swapped))
 
     def part_of(rows, hop):
         return expert_part(my_index, rows, hits, own, swapped, hop, chips)
 
-    def move(block):
-        return lax.ppermute(block, "ctx", route)
-
-    def after(block, first):
-        return lax.optimization_barrier((block, first))[0]
-
-    rows = move(start)
-    later = move(rows) if chips > 2 else None
-    sums = part_of(rows, 1).astype(jnp.bfloat16)
+    def move(blocks):
+        return tuple(lax.ppermute(x, "ctx", route) for x in blocks)
+
+    def after(blocks, first):
+        return tuple(lax.optimization_barrier((x, first))[0] for x in blocks)
+
+    def rounded(parts):
+        return tuple(x.astype(jnp.bfloat16) for x in parts)
+
+    def added(parts, arrived):
+        return tuple(x + y.astype(jnp.float32) for x, y in zip(parts, arrived))
+
+    rows = [start]
+    for hop in range(1, min(4, chips)):
+        rows.append(move(rows[-1]))
+    sums = rounded(part_of(rows[1], 1))
     for hop in range(1, chips):
         arrived = move(sums)
-        rows = later
-        if hop + 2 < chips:
-            later = move(after(rows, sums))
+        if hop + 3 < chips:
+            rows.append(move(after(rows[hop + 2], sums[0])))
         if hop + 1 < chips:
-            sums = (part_of(rows, hop + 1) + arrived.astype(jnp.float32)).astype(jnp.bfloat16)
-    expert_out = part_of(after(start, sums), 0) + arrived.astype(jnp.float32)
+            sums = rounded(added(part_of(rows[hop + 1], hop + 1), arrived))
+    home = part_of(after(start, sums[-1]), 0)
+    expert_out = jnp.concatenate(added(home, arrived), axis=0)
     gate_weight = gate_fixed.astype(jnp.float32) / 65536.0
     return (values.astype(jnp.float32) + gate_weight * expert_out).astype(jnp.bfloat16)
 

time: 126 us -> 130 us (1.032)
  waiting for transfers between devices: 34.5 us -> 38.4 us
    ppermute x14 -> x28, waiting for transfers between devices: 27.9 us -> 31.6 us  [move(): return tuple((lax.ppermute(x, 'ctx', route) for x in blocks))]
    ppermute x14 -> x28, starting transfers between devices: 24.3 us -> 24.5 us  [move(): return tuple((lax.ppermute(x, 'ctx', route) for x in blocks))]
  transfers between devices with their start and end apart: 25 -> 39, of which waited for: 15 -> 14; matrix products, arithmetic and copies ran while one was open for 0% -> 1% of each run, Pallas kernels for 40% -> 39%
where the time goes in v7:
time: 130 us
  Pallas kernels  50.4 us (39%)
  waiting for transfers between devices  38.4 us (30%)
  starting transfers between devices  36.3 us (28%)
  other arithmetic  3.32 us (3%)
    pallas_call x8, Pallas kernels, expert_part(): pl.pallas_call(functools.partial(expert_kernel, hop=hop, chips=chips), in...  37.3 us
    ppermute x28, waiting for transfers between devices, move(): return tuple((lax.ppermute(x, 'ctx', route) for x in blocks))  31.6 us
    ppermute x28, starting transfers between devices, move(): return tuple((lax.ppermute(x, 'ctx', route) for x in blocks))  24.5 us
    pallas_call x1, Pallas kernels, attention(): pl.pallas_call(functools.partial(attention_kernel, tok=tok), grid_spec=gr...  13.2 us
    ppermute x7, starting transfers between devices, from_chip(): lax.ppermute(block, 'ctx', [(i, i ^ step * CORES) for i in range(n_ctx)])  11.1 us
    ppermute x7, waiting for transfers between devices, from_chip(): lax.ppermute(block, 'ctx', [(i, i ^ step * CORES) for i in range(n_ctx)])  4.77 us
  transfers between devices with their start and end apart: 39, of which 14 were waited for; matrix products, arithmetic and copies ran while one was open for 1% of the time, Pallas kernels for 39%

profile of v7, /device:TPU:0, one launch (start us, length us, event | category | flops | bytes accessed | tf_op | source)
XLA Modules:
  0.0 130.0 jit_solution(14494311289598411883)
XLA Ops:
  1.7 4.1 %collective-permute-start.3 = (bf16[64,640]{1,0:T(8,128)(2,1)S(1)}, bf16[64,640]{1,0:T(8,128)(2,1)S(1)}, u32[]{:S(2)}, u32[]{:S(2)}) collective-permute-start(bf16[64,640]{1,0:T(8,128)(2,1)S(1)} %get-tuple-element.85), channel_id=1, source_target_pairs={{0,8},{1,9},{2,10},{3,11},{4,12},{5,13},{6,14},{7,15},{8,0},{9,1},... | collective-permute-start | bytes 245768 | tf_op jit(solution)/shard_map/ppermute | solution.py:228
  5.8 1.5 %collective-permute-start = (bf16[64,640]{1,0:T(8,128)(2,1)S(1)}, bf16[64,640]{1,0:T(8,128)(2,1)S(1)}, u32[]{:S(2)}, u32[]{:S(2)}) collective-permute-start(bf16[64,640]{1,0:T(8,128)(2,1)S(1)} %get-tuple-element.85), channel_id=1, source_target_pairs={{0,2},{1,3},{2,0},{3,1},{4,6},{5,7},{6,4},{7,5},{8,10},{9,11},{10,... | collective-permute-start | bytes 245768 | tf_op jit(solution)/shard_map/ppermute | solution.py:228
  7.3 1.5 %collective-permute-start.2 = (bf16[64,640]{1,0:T(8,128)(2,1)S(1)}, bf16[64,640]{1,0:T(8,128)(2,1)S(1)}, u32[]{:S(2)}, u32[]{:S(2)}) collective-permute-start(bf16[64,640]{1,0:T(8,128)(2,1)S(1)} %get-tuple-element.85), channel_id=1, source_target_pairs={{0,6},{1,7},{2,4},{3,5},{4,2},{5,3},{6,0},{7,1},{8,14},{9,15},{10,... | collective-permute-start | bytes 245768 | tf_op jit(solution)/shard_map/ppermute | solution.py:228
  9.8 2.0 %collective-permute-start.6 = (bf16[64,640]{1,0:T(8,128)(2,1)S(1)}, bf16[64,640]{1,0:T(8,128)(2,1)S(1)}, u32[]{:S(2)}, u32[]{:S(2)}) collective-permute-start(bf16[64,640]{1,0:T(8,128)(2,1)S(1)} %collective-permute-done.3), channel_id=1, source_target_pairs={{0,6},{1,7},{2,4},{3,5},{4,2},{5,3},{6,0},{7,1},{8,14},{9,15},{10,... | collective-permute-start | bytes 245768 | tf_op jit(solution)/shard_map/ppermute | solution.py:228
  11.8 1.3 %collective-permute-start.5 = (bf16[64,640]{1,0:T(8,128)(2,1)S(1)}, bf16[64,640]{1,0:T(8,128)(2,1)S(1)}, u32[]{:S(2)}, u32[]{:S(2)}) collective-permute-start(bf16[64,640]{1,0:T(8,128)(2,1)S(1)} %collective-permute-done.3), channel_id=1, source_target_pairs={{0,4},{1,5},{2,6},{3,7},{4,0},{5,1},{6,2},{7,3},{8,12},{9,13},{10,... | collective-permute-start | bytes 245768 | tf_op jit(solution)/shard_map/ppermute | solution.py:228
  14.0 3.6 %collective-permute-done.4 = bf16[64,640]{1,0:T(8,128)(2,1)S(1)} collective-permute-done((bf16[64,640]{1,0:T(8,128)(2,1)S(1)}, bf16[64,640]{1,0:T(8,128)(2,1)S(1)}, u32[]{:S(2)}, u32[]{:S(2)}) %collective-permute-start.4) | collective-permute-done | bytes 81952 | tf_op jit(solution)/shard_map/ppermute | solution.py:228
  17.8 2.1 %collective-permute-done.7.other_ref = bf16[512,640]{1,0:T(8,128)(2,1)S(1)} collective-permute-done((bf16[512,640]{1,0:T(8,128)(2,1)S(1)}, bf16[512,640]{1,0:T(8,128)(2,1)S(1)}, u32[]{:S(2)}, u32[]{:S(2)}) %collective-permute-start.7) | collective-permute-done | bytes 655392 | tf_op jit(solution)/shard_map/ppermute | solution.py:236
  20.7 13.2 %shard_map.109 = (bf16[64,4096]{1,0:T(8,128)(2,1)}, bf16[32,4096]{1,0:T(8,128)(2,1)}, bf16[32,4096]{1,0:T(8,128)(2,1)}, f32[64,8]{1,0:T(8,128)}) custom-call(s32[1]{0:T(128)} %bitcast.index_ref, bf16[64,16384]{1,0:T(8,128)(2,1)} %q_ref.1, bf16[64,2048]{1,0:T(8,128)(2,1)} %qr_ref.1, bf16[512,640]{1,0:T(8,128)(2,1)} %copy-done.8, bf16[512,640]{1,0:T(8,128)(2,1)} %copy-done.9, ...), custom_call_target="tpu_custom_call" | custom-call | flops 4831838208 | bytes 8388608 | tf_op jit(solution)/shard_map/pallas_call | solution.py:143
  33.9 1.0 collective-permute-start.11
  34.9 1.6 %collective-permute-start.14 = (bf16[32,4096]{1,0:T(8,128)(2,1)}, bf16[32,4096]{1,0:T(8,128)(2,1)S(1)}, u32[]{:S(2)}, u32[]{:S(2)}) collective-permute-start(bf16[32,4096]{1,0:T(8,128)(2,1)} %get-tuple-element.79.lower_ref), channel_id=1, source_target_pairs={{0,4},{1,3},{4,8},{5,1},{8,12},{9,5},{12,14},{13,9},{14,10},{15,13... | collective-permute-start | bytes 786440 | tf_op jit(solution)/shard_map/ppermute | solution.py:249
  36.5 4.0 %collective-permute-done.11.upper_ref = bf16[32,4096]{1,0:T(8,128)(2,1)S(1)} collective-permute-done((bf16[32,4096]{1,0:T(8,128)(2,1)}, bf16[32,4096]{1,0:T(8,128)(2,1)S(1)}, u32[]{:S(2)}, u32[]{:S(2)}) %collective-permute-start.11) | collective-permute-done | bytes 262176 | tf_op jit(solution)/shard_map/ppermute | solution.py:249
  41.5 1.8 %collective-permute-done.14.lower_ref = bf16[32,4096]{1,0:T(8,128)(2,1)S(1)} collective-permute-done((bf16[32,4096]{1,0:T(8,128)(2,1)}, bf16[32,4096]{1,0:T(8,128)(2,1)S(1)}, u32[]{:S(2)}, u32[]{:S(2)}) %collective-permute-start.14) | collective-permute-done | bytes 262176 | tf_op jit(solution)/shard_map/ppermute | solution.py:249
  45.1 4.7 %shard_map.110 = (f32[32,4096]{1,0:T(8,128)S(1)}, f32[32,4096]{1,0:T(8,128)S(1)}) custom-call(s32[1]{0:T(128)} %bitcast.index_ref, bf16[32,4096]{1,0:T(8,128)(2,1)S(1)} %collective-permute-done.11.upper_ref, bf16[32,4096]{1,0:T(8,128)(2,1)S(1)} %collective-permute-done.14.lower_ref, f32[64,8]{1,0:T(8,128)S(1)} %copy-done.5, bf16[4096,256]{1,0:T(8,128)(2,1)S(1)} %bitcast.10, ...), custom_call_target="tpu_custom_call" | custom-call | flops 5368709120 | bytes 14680064 | tf_op jit(solution)/shard_map/pallas_call | solution.py:199
  49.8 1.6 %collective-permute-start.28 = (bf16[32,4096]{1,0:T(8,128)(2,1)S(1)}, bf16[32,4096]{1,0:T(8,128)(2,1)S(1)}, u32[]{:S(2)}, u32[]{:S(2)}) collective-permute-start(bf16[32,4096]{1,0:T(8,128)(2,1)S(1)} %convert_element_type.106), channel_id=1, source_target_pairs={{0,4},{1,3},{4,8},{5,1},{8,12},{9,5},{12,14},{13,9},{14,10},{15,13... | collective-permute-start | bytes 786440 | tf_op jit(solution)/shard_map/ppermute | solution.py:249
  51.5 2.0 %collective-permute-start.17 = (bf16[32,4096]{1,0:T(8,128)(2,1)S(1)}, bf16[32,4096]{1,0:T(8,128)(2,1)S(1)}, u32[]{:S(2)}, u32[]{:S(2)}) collective-permute-start(bf16[32,4096]{1,0:T(8,128)(2,1)S(1)} %convert_element_type.99), channel_id=1, source_target_pairs={{0,4},{1,3},{4,8},{5,1},{8,12},{9,5},{12,14},{13,9},{14,10},{15,13... | collective-permute-start | bytes 786440 | tf_op jit(solution)/shard_map/ppermute | solution.py:249
  53.5 4.7 %shard_map.111 = (f32[32,4096]{1,0:T(8,128)S(1)}, f32[32,4096]{1,0:T(8,128)S(1)}) custom-call(s32[1]{0:T(128)} %bitcast.index_ref, bf16[32,4096]{1,0:T(8,128)(2,1)S(1)} %collective-permute-done.12.upper_ref, bf16[32,4096]{1,0:T(8,128)(2,1)S(1)} %collective-permute-done.16.lower_ref, f32[64,8]{1,0:T(8,128)S(1)} %copy-done.5, bf16[4096,256]{1,0:T(8,128)(2,1)S(1)} %bitcast.11, ...), custom_call_target="tpu_custom_call" | custom-call | flops 5368709120 | bytes 14680064 | tf_op jit(solution)/shard_map/pallas_call | solution.py:199
  61.0 9.2 %collective-permute-done.19.lower_ref = bf16[32,4096]{1,0:T(8,128)(2,1)S(1)} collective-permute-done((bf16[32,4096]{1,0:T(8,128)(2,1)S(1)}, bf16[32,4096]{1,0:T(8,128)(2,1)S(1)}, u32[]{:S(2)}, u32[]{:S(2)}) %collective-permute-start.19) | collective-permute-done | bytes 262176 | tf_op jit(solution)/shard_map/ppermute | solution.py:249
  72.0 4.7 %shard_map.112 = (f32[32,4096]{1,0:T(8,128)S(1)}, f32[32,4096]{1,0:T(8,128)S(1)}) custom-call(s32[1]{0:T(128)} %bitcast.index_ref, bf16[32,4096]{1,0:T(8,128)(2,1)S(1)} %collective-permute-done.13.upper_ref, bf16[32,4096]{1,0:T(8,128)(2,1)S(1)} %collective-permute-done.19.lower_ref, f32[64,8]{1,0:T(8,128)S(1)} %copy-done.5, bf16[4096,256]{1,0:T(8,128)(2,1)S(1)} %bitcast.12, ...), custom_call_target="tpu_custom_call" | custom-call | flops 5368709120 | bytes 14680064 | tf_op jit(solution)/shard_map/pallas_call | solution.py:199
  77.8 1.7 %collective-permute-done.22.lower_ref = bf16[32,4096]{1,0:T(8,128)(2,1)S(1)} collective-permute-done((bf16[32,4096]{1,0:T(8,128)(2,1)S(1)}, bf16[32,4096]{1,0:T(8,128)(2,1)S(1)}, u32[]{:S(2)}, u32[]{:S(2)}) %collective-permute-start.22) | collective-permute-done | bytes 262176 | tf_op jit(solution)/shard_map/ppermute | solution.py:249
  81.2 4.7 %shard_map.113 = (f32[32,4096]{1,0:T(8,128)S(1)}, f32[32,4096]{1,0:T(8,128)S(1)}) custom-call(s32[1]{0:T(128)} %bitcast.index_ref, bf16[32,4096]{1,0:T(8,128)(2,1)S(1)} %collective-permute-done.15.upper_ref, bf16[32,4096]{1,0:T(8,128)(2,1)S(1)} %collective-permute-done.22.lower_ref, f32[64,8]{1,0:T(8,128)S(1)} %copy-done.5, bf16[4096,256]{1,0:T(8,128)(2,1)S(1)} %bitcast.13, ...), custom_call_target="tpu_custom_call" | custom-call | flops 5368709120 | bytes 14680064 | tf_op jit(solution)/shard_map/pallas_call | solution.py:199
  86.9 1.3 collective-permute-start.34
  88.2 3.4 %collective-permute-done.25.lower_ref = bf16[32,4096]{1,0:T(8,128)(2,1)S(1)} collective-permute-done((bf16[32,4096]{1,0:T(8,128)(2,1)S(1)}, bf16[32,4096]{1,0:T(8,128)(2,1)S(1)}, u32[]{:S(2)}, u32[]{:S(2)}) %collective-permute-start.25) | collective-permute-done | bytes 262176 | tf_op jit(solution)/shard_map/ppermute | solution.py:249
  92.5 4.7 %shard_map.116 = (f32[32,4096]{1,0:T(8,128)S(1)}, f32[32,4096]{1,0:T(8,128)S(1)}) custom-call(s32[1]{0:T(128)} %bitcast.index_ref, bf16[32,4096]{1,0:T(8,128)(2,1)S(1)} %collective-permute-done.18.upper_ref, bf16[32,4096]{1,0:T(8,128)(2,1)S(1)} %collective-permute-done.25.lower_ref, f32[64,8]{1,0:T(8,128)S(1)} %copy-done.5, bf16[4096,256]{1,0:T(8,128)(2,1)S(1)} %bitcast.14, ...), custom_call_target="tpu_custom_call" | custom-call | flops 5368709120 | bytes 14680064 | tf_op jit(solution)/shard_map/pallas_call | solution.py:199
  98.2 1.0 collective-permute-start.35
  99.3 3.5 %collective-permute-done.26.lower_ref = bf16[32,4096]{1,0:T(8,128)(2,1)S(1)} collective-permute-done((bf16[32,4096]{1,0:T(8,128)(2,1)S(1)}, bf16[32,4096]{1,0:T(8,128)(2,1)S(1)}, u32[]{:S(2)}, u32[]{:S(2)}) %collective-permute-start.26) | collective-permute-done | bytes 262176 | tf_op jit(solution)/shard_map/ppermute | solution.py:249
  103.7 4.7 %shard_map.115 = (f32[32,4096]{1,0:T(8,128)S(1)}, f32[32,4096]{1,0:T(8,128)S(1)}) custom-call(s32[1]{0:T(128)} %bitcast.index_ref, bf16[32,4096]{1,0:T(8,128)(2,1)S(1)} %collective-permute-done.21.upper_ref, bf16[32,4096]{1,0:T(8,128)(2,1)S(1)} %collective-permute-done.26.lower_ref, f32[64,8]{1,0:T(8,128)S(1)} %copy-done.5, bf16[4096,256]{1,0:T(8,128)(2,1)S(1)} %bitcast.15, ...), custom_call_target="tpu_custom_call" | custom-call | flops 5368709120 | bytes 14680064 | tf_op jit(solution)/shard_map/pallas_call | solution.py:199
  109.5 1.0 collective-permute-start.33
  111.2 2.8 %collective-permute-done.27.lower_ref = bf16[32,4096]{1,0:T(8,128)(2,1)S(1)} collective-permute-done((bf16[32,4096]{1,0:T(8,128)(2,1)S(1)}, bf16[32,4096]{1,0:T(8,128)(2,1)S(1)}, u32[]{:S(2)}, u32[]{:S(2)}) %collective-permute-start.27) | collective-permute-done | bytes 262176 | tf_op jit(solution)/shard_map/ppermute | solution.py:249
  114.0 4.7 %shard_map.114 = (f32[32,4096]{1,0:T(8,128)S(1)}, f32[32,4096]{1,0:T(8,128)S(1)}) custom-call(s32[1]{0:T(128)} %bitcast.index_ref, bf16[32,4096]{1,0:T(8,128)(2,1)S(1)} %collective-permute-done.24.upper_ref, bf16[32,4096]{1,0:T(8,128)(2,1)S(1)} %collective-permute-done.27.lower_ref, f32[64,8]{1,0:T(8,128)S(1)} %copy-done.5, bf16[4096,256]{1,0:T(8,128)(2,1)S(1)} %bitcast.16, ...), custom_call_target="tpu_custom_call" | custom-call | flops 5368709120 | bytes 14680064 | tf_op jit(solution)/shard_map/pallas_call | solution.py:199
  120.8 4.7 %shard_map.117 = (f32[32,4096]{1,0:T(8,128)S(1)}, f32[32,4096]{1,0:T(8,128)S(1)}) custom-call(s32[1]{0:T(128)} %bitcast.index_ref, bf16[32,4096]{1,0:T(8,128)(2,1)S(1)} %copy-done.3, bf16[32,4096]{1,0:T(8,128)(2,1)S(1)} %copy-done.4, f32[64,8]{1,0:T(8,128)S(1)} %copy-done.6, bf16[4096,256]{1,0:T(8,128)(2,1)S(1)} %bitcast.17, bf16[4096,256]{1,0:T(8,128)(2,1)S(1)} %bitcast.26, ...), custom_call_target="tpu_custom_call" | custom-call | flops 5368709120 | bytes 14680064 | tf_op jit(solution)/shard_map/pallas_call | solution.py:199
  125.5 3.5 %collective-permute-done.37 = bf16[32,4096]{1,0:T(8,128)(2,1)S(1)} collective-permute-done((bf16[32,4096]{1,0:T(8,128)(2,1)S(1)}, bf16[32,4096]{1,0:T(8,128)(2,1)S(1)}, u32[]{:S(2)}, u32[]{:S(2)}) %collective-permute-start.37) | collective-permute-done | bytes 262176 | tf_op jit(solution)/shard_map/ppermute | solution.py:249
  129.1 1.0 fusion.1
  (105 shorter events, 22.5 us)
Async XLA Ops:
  1.7 8.1 %collective-permute-start.3 = (bf16[64,640]{1,0:T(8,128)(2,1)S(1)}, bf16[64,640]{1,0:T(8,128)(2,1)S(1)}, u32[]{:S(2)}, u32[]{:S(2)}) collective-permute-start(bf16[64,640]{1,0:T(8,128)(2,1)S(1)} %get-tuple-element.85), channel_id=1, source_target_pairs={{0,8},{1,9},{2,10},{3,11},{4,12},{5,13},{6,14},{7,15},{8,0},{9,1},... | collective-permute-start | bytes 245768 | tf_op jit(solution)/shard_map/ppermute | solution.py:228
  9.8 7.9 %collective-permute-start.6 = (bf16[64,640]{1,0:T(8,128)(2,1)S(1)}, bf16[64,640]{1,0:T(8,128)(2,1)S(1)}, u32[]{:S(2)}, u32[]{:S(2)}) collective-permute-start(bf16[64,640]{1,0:T(8,128)(2,1)S(1)} %collective-permute-done.3), channel_id=1, source_target_pairs={{0,6},{1,7},{2,4},{3,5},{4,2},{5,3},{6,0},{7,1},{8,14},{9,15},{10,... | collective-permute-start | bytes 245768 | tf_op jit(solution)/shard_map/ppermute | solution.py:228
  19.8 14.1 %collective-permute-start.8 = (bf16[4096,256]{1,0:T(8,128)(2,1)}, bf16[4096,256]{1,0:T(8,128)(2,1)}, u32[]{:S(2)}, u32[]{:S(2)}) collective-permute-start(bf16[4096,256]{1,0:T(8,128)(2,1)} %bitcast.9), channel_id=1, source_target_pairs={{0,1},{1,0},{2,3},{3,2},{4,5},{5,4},{6,7},{7,6},{8,9},{9,8},{10,11... | collective-permute-start | bytes 6291464 | tf_op jit(solution)/shard_map/ppermute | solution.py:239
  20.0 13.9 %collective-permute-start.9 = (bf16[4096,256]{1,0:T(8,128)(2,1)}, bf16[4096,256]{1,0:T(8,128)(2,1)}, u32[]{:S(2)}, u32[]{:S(2)}) collective-permute-start(bf16[4096,256]{1,0:T(8,128)(2,1)} %bitcast.18), channel_id=1, source_target_pairs={{0,1},{1,0},{2,3},{3,2},{4,5},{5,4},{6,7},{7,6},{8,9},{9,8},{10,11... | collective-permute-start | bytes 6291464 | tf_op jit(solution)/shard_map/ppermute | solution.py:239
  20.4 13.6 %collective-permute-start.10 = (bf16[256,4096]{1,0:T(8,128)(2,1)}, bf16[256,4096]{1,0:T(8,128)(2,1)}, u32[]{:S(2)}, u32[]{:S(2)}) collective-permute-start(bf16[256,4096]{1,0:T(8,128)(2,1)} %bitcast.27), channel_id=1, source_target_pairs={{0,1},{1,0},{2,3},{3,2},{4,5},{5,4},{6,7},{7,6},{8,9},{9,8},{10,11... | collective-permute-start | bytes 6291464 | tf_op jit(solution)/shard_map/ppermute | solution.py:239
  34.9 8.4 %collective-permute-start.14 = (bf16[32,4096]{1,0:T(8,128)(2,1)}, bf16[32,4096]{1,0:T(8,128)(2,1)S(1)}, u32[]{:S(2)}, u32[]{:S(2)}) collective-permute-start(bf16[32,4096]{1,0:T(8,128)(2,1)} %get-tuple-element.79.lower_ref), channel_id=1, source_target_pairs={{0,4},{1,3},{4,8},{5,1},{8,12},{9,5},{12,14},{13,9},{14,10},{15,13... | collective-permute-start | bytes 786440 | tf_op jit(solution)/shard_map/ppermute | solution.py:249
  40.6 12.9 %collective-permute-start.12 = (bf16[32,4096]{1,0:T(8,128)(2,1)S(1)}, bf16[32,4096]{1,0:T(8,128)(2,1)S(1)}, u32[]{:S(2)}, u32[]{:S(2)}) collective-permute-start(bf16[32,4096]{1,0:T(8,128)(2,1)S(1)} %collective-permute-done.11.upper_ref), channel_id=1, source_target_pairs={{0,4},{1,3},{4,8},{5,1},{8,12},{9,5},{12,14},{13,9},{14,10},{15,13... | collective-permute-start | bytes 786440 | tf_op jit(solution)/shard_map/ppermute | solution.py:249
  43.4 10.1 %collective-permute-start.16 = (bf16[32,4096]{1,0:T(8,128)(2,1)S(1)}, bf16[32,4096]{1,0:T(8,128)(2,1)S(1)}, u32[]{:S(2)}, u32[]{:S(2)}) collective-permute-start(bf16[32,4096]{1,0:T(8,128)(2,1)S(1)} %collective-permute-done.14.lower_ref), channel_id=1, source_target_pairs={{0,4},{1,3},{4,8},{5,1},{8,12},{9,5},{12,14},{13,9},{14,10},{15,13... | collective-permute-start | bytes 786440 | tf_op jit(solution)/shard_map/ppermute | solution.py:249
  49.8 8.3 %collective-permute-start.28 = (bf16[32,4096]{1,0:T(8,128)(2,1)S(1)}, bf16[32,4096]{1,0:T(8,128)(2,1)S(1)}, u32[]{:S(2)}, u32[]{:S(2)}) collective-permute-start(bf16[32,4096]{1,0:T(8,128)(2,1)S(1)} %convert_element_type.106), channel_id=1, source_target_pairs={{0,4},{1,3},{4,8},{5,1},{8,12},{9,5},{12,14},{13,9},{14,10},{15,13... | collective-permute-start | bytes 786440 | tf_op jit(solution)/shard_map/ppermute | solution.py:249
  51.5 9.4 %collective-permute-start.17 = (bf16[32,4096]{1,0:T(8,128)(2,1)S(1)}, bf16[32,4096]{1,0:T(8,128)(2,1)S(1)}, u32[]{:S(2)}, u32[]{:S(2)}) collective-permute-start(bf16[32,4096]{1,0:T(8,128)(2,1)S(1)} %convert_element_type.99), channel_id=1, source_target_pairs={{0,4},{1,3},{4,8},{5,1},{8,12},{9,5},{12,14},{13,9},{14,10},{15,13... | collective-permute-start | bytes 786440 | tf_op jit(solution)/shard_map/ppermute | solution.py:249
  58.2 18.4 %collective-permute-start.29 = (bf16[32,4096]{1,0:T(8,128)(2,1)S(1)}, bf16[32,4096]{1,0:T(8,128)(2,1)S(1)}, u32[]{:S(2)}, u32[]{:S(2)}) collective-permute-start(bf16[32,4096]{1,0:T(8,128)(2,1)S(1)} %add_convert_fusion.8), channel_id=1, source_target_pairs={{0,4},{1,3},{4,8},{5,1},{8,12},{9,5},{12,14},{13,9},{14,10},{15,13... | collective-permute-start | bytes 786440 | tf_op jit(solution)/shard_map/ppermute | solution.py:249
  59.2 11.1 %collective-permute-start.13 = (bf16[32,4096]{1,0:T(8,128)(2,1)S(1)}, bf16[32,4096]{1,0:T(8,128)(2,1)S(1)}, u32[]{:S(2)}, u32[]{:S(2)}) collective-permute-start(bf16[32,4096]{1,0:T(8,128)(2,1)S(1)} %collective-permute-done.12.upper_ref), channel_id=1, source_target_pairs={{0,4},{1,3},{4,8},{5,1},{8,12},{9,5},{12,14},{13,9},{14,10},{15,13... | collective-permute-start | bytes 786440 | tf_op jit(solution)/shard_map/ppermute | solution.py:249
  60.0 10.3 %collective-permute-start.19 = (bf16[32,4096]{1,0:T(8,128)(2,1)S(1)}, bf16[32,4096]{1,0:T(8,128)(2,1)S(1)}, u32[]{:S(2)}, u32[]{:S(2)}) collective-permute-start(bf16[32,4096]{1,0:T(8,128)(2,1)S(1)} %collective-permute-done.16.lower_ref), channel_id=1, source_target_pairs={{0,4},{1,3},{4,8},{5,1},{8,12},{9,5},{12,14},{13,9},{14,10},{15,13... | collective-permute-start | bytes 786440 | tf_op jit(solution)/shard_map/ppermute | solution.py:249
  60.9 16.7 %collective-permute-start.20 = (bf16[32,4096]{1,0:T(8,128)(2,1)S(1)}, bf16[32,4096]{1,0:T(8,128)(2,1)S(1)}, u32[]{:S(2)}, u32[]{:S(2)}) collective-permute-start(bf16[32,4096]{1,0:T(8,128)(2,1)S(1)} %add_convert_fusion.11), channel_id=1, source_target_pairs={{0,4},{1,3},{4,8},{5,1},{8,12},{9,5},{12,14},{13,9},{14,10},{15,13... | collective-permute-start | bytes 786440 | tf_op jit(solution)/shard_map/ppermute | solution.py:249
  70.3 9.2 %collective-permute-start.15 = (bf16[32,4096]{1,0:T(8,128)(2,1)S(1)}, bf16[32,4096]{1,0:T(8,128)(2,1)S(1)}, u32[]{:S(2)}, u32[]{:S(2)}) collective-permute-start(bf16[32,4096]{1,0:T(8,128)(2,1)S(1)} %collective-permute-done.13.upper_ref), channel_id=1, source_target_pairs={{0,4},{1,3},{4,8},{5,1},{8,12},{9,5},{12,14},{13,9},{14,10},{15,13... | collective-permute-start | bytes 786440 | tf_op jit(solution)/shard_map/ppermute | solution.py:249
  71.2 8.3 %collective-permute-start.22 = (bf16[32,4096]{1,0:T(8,128)(2,1)S(1)}, bf16[32,4096]{1,0:T(8,128)(2,1)S(1)}, u32[]{:S(2)}, u32[]{:S(2)}) collective-permute-start(bf16[32,4096]{1,0:T(8,128)(2,1)S(1)} %collective-permute-done.19.lower_ref), channel_id=1, source_target_pairs={{0,4},{1,3},{4,8},{5,1},{8,12},{9,5},{12,14},{13,9},{14,10},{15,13... | collective-permute-start | bytes 786440 | tf_op jit(solution)/shard_map/ppermute | solution.py:249
  76.7 9.1 %collective-permute-start.30 = (bf16[32,4096]{1,0:T(8,128)(2,1)S(1)}, bf16[32,4096]{1,0:T(8,128)(2,1)S(1)}, u32[]{:S(2)}, u32[]{:S(2)}) collective-permute-start(bf16[32,4096]{1,0:T(8,128)(2,1)S(1)} %add_convert_fusion.7), channel_id=1, source_target_pairs={{0,4},{1,3},{4,8},{5,1},{8,12},{9,5},{12,14},{13,9},{14,10},{15,13... | collective-permute-start | bytes 786440 | tf_op jit(solution)/shard_map/ppermute | solution.py:249
  77.7 9.1 %collective-permute-start.23 = (bf16[32,4096]{1,0:T(8,128)(2,1)S(1)}, bf16[32,4096]{1,0:T(8,128)(2,1)S(1)}, u32[]{:S(2)}, u32[]{:S(2)}) collective-permute-start(bf16[32,4096]{1,0:T(8,128)(2,1)S(1)} %add_convert_fusion.10), channel_id=1, source_target_pairs={{0,4},{1,3},{4,8},{5,1},{8,12},{9,5},{12,14},{13,9},{14,10},{15,13... | collective-permute-start | bytes 786440 | tf_op jit(solution)/shard_map/ppermute | solution.py:249
  79.5 12.1 %collective-permute-start.18 = (bf16[32,4096]{1,0:T(8,128)(2,1)S(1)}, bf16[32,4096]{1,0:T(8,128)(2,1)S(1)}, u32[]{:S(2)}, u32[]{:S(2)}) collective-permute-start(bf16[32,4096]{1,0:T(8,128)(2,1)S(1)} %collective-permute-done.15.upper_ref), channel_id=1, source_target_pairs={{0,4},{1,3},{4,8},{5,1},{8,12},{9,5},{12,14},{13,9},{14,10},{15,13... | collective-permute-start | bytes 786440 | tf_op jit(solution)/shard_map/ppermute | solution.py:249
  80.4 11.2 %collective-permute-start.25 = (bf16[32,4096]{1,0:T(8,128)(2,1)S(1)}, bf16[32,4096]{1,0:T(8,128)(2,1)S(1)}, u32[]{:S(2)}, u32[]{:S(2)}) collective-permute-start(bf16[32,4096]{1,0:T(8,128)(2,1)S(1)} %collective-permute-done.22.lower_ref), channel_id=1, source_target_pairs={{0,4},{1,3},{4,8},{5,1},{8,12},{9,5},{12,14},{13,9},{14,10},{15,13... | collective-permute-start | bytes 786440 | tf_op jit(solution)/shard_map/ppermute | solution.py:249
  85.9 11.3 %collective-permute-start.31 = (bf16[32,4096]{1,0:T(8,128)(2,1)S(1)}, bf16[32,4096]{1,0:T(8,128)(2,1)S(1)}, u32[]{:S(2)}, u32[]{:S(2)}) collective-permute-start(bf16[32,4096]{1,0:T(8,128)(2,1)S(1)} %add_convert_fusion.6), channel_id=1, source_target_pairs={{0,4},{1,3},{4,8},{5,1},{8,12},{9,5},{12,14},{13,9},{14,10},{15,13... | collective-permute-start | bytes 786440 | tf_op jit(solution)/shard_map/ppermute | solution.py:249
  86.9 11.3 %collective-permute-start.34 = (bf16[32,4096]{1,0:T(8,128)(2,1)S(1)}, bf16[32,4096]{1,0:T(8,128)(2,1)S(1)}, u32[]{:S(2)}, u32[]{:S(2)}) collective-permute-start(bf16[32,4096]{1,0:T(8,128)(2,1)S(1)} %add_convert_fusion.9), channel_id=1, source_target_pairs={{0,4},{1,3},{4,8},{5,1},{8,12},{9,5},{12,14},{13,9},{14,10},{15,13... | collective-permute-start | bytes 786440 | tf_op jit(solution)/shard_map/ppermute | solution.py:249
  91.6 11.2 %collective-permute-start.21 = (bf16[32,4096]{1,0:T(8,128)(2,1)S(1)}, bf16[32,4096]{1,0:T(8,128)(2,1)S(1)}, u32[]{:S(2)}, u32[]{:S(2)}) collective-permute-start(bf16[32,4096]{1,0:T(8,128)(2,1)S(1)} %collective-permute-done.18.upper_ref), channel_id=1, source_target_pairs={{0,4},{1,3},{4,8},{5,1},{8,12},{9,5},{12,14},{13,9},{14,10},{15,13... | collective-permute-start | bytes 786440 | tf_op jit(solution)/shard_map/ppermute | solution.py:249
  92.5 10.3 %collective-permute-start.26 = (bf16[32,4096]{1,0:T(8,128)(2,1)S(1)}, bf16[32,4096]{1,0:T(8,128)(2,1)S(1)}, u32[]{:S(2)}, u32[]{:S(2)}) collective-permute-start(bf16[32,4096]{1,0:T(8,128)(2,1)S(1)} %collective-permute-done.25.lower_ref), channel_id=1, source_target_pairs={{0,4},{1,3},{4,8},{5,1},{8,12},{9,5},{12,14},{13,9},{14,10},{15,13... | collective-permute-start | bytes 786440 | tf_op jit(solution)/shard_map/ppermute | solution.py:249
  97.2 12.2 %collective-permute-start.32 = (bf16[32,4096]{1,0:T(8,128)(2,1)S(1)}, bf16[32,4096]{1,0:T(8,128)(2,1)S(1)}, u32[]{:S(2)}, u32[]{:S(2)}) collective-permute-start(bf16[32,4096]{1,0:T(8,128)(2,1)S(1)} %add_convert_fusion.5), channel_id=1, source_target_pairs={{0,4},{1,3},{4,8},{5,1},{8,12},{9,5},{12,14},{13,9},{14,10},{15,13... | collective-permute-start | bytes 786440 | tf_op jit(solution)/shard_map/ppermute | solution.py:249
  98.2 10.2 %collective-permute-start.35 = (bf16[32,4096]{1,0:T(8,128)(2,1)S(1)}, bf16[32,4096]{1,0:T(8,128)(2,1)S(1)}, u32[]{:S(2)}, u32[]{:S(2)}) collective-permute-start(bf16[32,4096]{1,0:T(8,128)(2,1)S(1)} %add_convert_fusion.2), channel_id=1, source_target_pairs={{0,4},{1,3},{4,8},{5,1},{8,12},{9,5},{12,14},{13,9},{14,10},{15,13... | collective-permute-start | bytes 786440 | tf_op jit(solution)/shard_map/ppermute | solution.py:249
  102.8 8.4 %collective-permute-start.24 = (bf16[32,4096]{1,0:T(8,128)(2,1)S(1)}, bf16[32,4096]{1,0:T(8,128)(2,1)S(1)}, u32[]{:S(2)}, u32[]{:S(2)}) collective-permute-start(bf16[32,4096]{1,0:T(8,128)(2,1)S(1)} %collective-permute-done.21.upper_ref), channel_id=1, source_target_pairs={{0,4},{1,3},{4,8},{5,1},{8,12},{9,5},{12,14},{13,9},{14,10},{15,13... | collective-permute-start | bytes 786440 | tf_op jit(solution)/shard_map/ppermute | solution.py:249
  103.7 10.3 %collective-permute-start.27 = (bf16[32,4096]{1,0:T(8,128)(2,1)S(1)}, bf16[32,4096]{1,0:T(8,128)(2,1)S(1)}, u32[]{:S(2)}, u32[]{:S(2)}) collective-permute-start(bf16[32,4096]{1,0:T(8,128)(2,1)S(1)} %collective-permute-done.26.lower_ref), channel_id=1, source_target_pairs={{0,4},{1,3},{4,8},{5,1},{8,12},{9,5},{12,14},{13,9},{14,10},{15,13... | collective-permute-start | bytes 786440 | tf_op jit(solution)/shard_map/ppermute | solution.py:249
  108.5 12.2 %collective-permute-start.36 = (bf16[32,4096]{1,0:T(8,128)(2,1)S(1)}, bf16[32,4096]{1,0:T(8,128)(2,1)S(1)}, u32[]{:S(2)}, u32[]{:S(2)}) collective-permute-start(bf16[32,4096]{1,0:T(8,128)(2,1)S(1)} %add_convert_fusion.1), channel_id=1, source_target_pairs={{0,4},{1,3},{4,8},{5,1},{8,12},{9,5},{12,14},{13,9},{14,10},{15,13... | collective-permute-start | bytes 786440 | tf_op jit(solution)/shard_map/ppermute | solution.py:249
  109.5 10.2 %collective-permute-start.33 = (bf16[32,4096]{1,0:T(8,128)(2,1)S(1)}, bf16[32,4096]{1,0:T(8,128)(2,1)S(1)}, u32[]{:S(2)}, u32[]{:S(2)}) collective-permute-start(bf16[32,4096]{1,0:T(8,128)(2,1)S(1)} %add_convert_fusion.4), channel_id=1, source_target_pairs={{0,4},{1,3},{4,8},{5,1},{8,12},{9,5},{12,14},{13,9},{14,10},{15,13... | collective-permute-start | bytes 786440 | tf_op jit(solution)/shard_map/ppermute | solution.py:249
  119.7 9.3 %collective-permute-start.38 = (bf16[32,4096]{1,0:T(8,128)(2,1)S(1)}, bf16[32,4096]{1,0:T(8,128)(2,1)S(1)}, u32[]{:S(2)}, u32[]{:S(2)}) collective-permute-start(bf16[32,4096]{1,0:T(8,128)(2,1)S(1)} %add_convert_fusion.3), channel_id=1, source_target_pairs={{0,4},{1,3},{4,8},{5,1},{8,12},{9,5},{12,14},{13,9},{14,10},{15,13... | collective-permute-start | bytes 786440 | tf_op jit(solution)/shard_map/ppermute | solution.py:249
  120.7 8.2 %collective-permute-start.37 = (bf16[32,4096]{1,0:T(8,128)(2,1)S(1)}, bf16[32,4096]{1,0:T(8,128)(2,1)S(1)}, u32[]{:S(2)}, u32[]{:S(2)}) collective-permute-start(bf16[32,4096]{1,0:T(8,128)(2,1)S(1)} %add_convert_fusion), channel_id=1, source_target_pairs={{0,4},{1,3},{4,8},{5,1},{8,12},{9,5},{12,14},{13,9},{14,10},{15,13... | collective-permute-start | bytes 786440 | tf_op jit(solution)/shard_map/ppermute | solution.py:249
  (18 other events, 139.1 us)

commit v8 on v7

--- a/solution.py
+++ b/solution.py
@@ -19,7 +19,7 @@
 NORM_EPS = 1e-06
 NEG_FILL = -1e30
 
-HEAD_GROUP = 8
+HEAD_GROUP = 16
 SUB_HEADS = 4
 LOG2_SCALE = SCORE_SCALE * math.log2(math.e)
 
@@ -63,19 +63,24 @@
         stack_ref[at, LAT : LAT + 2 * ROPE] = jnp.where(lane < ROPE, pair, jnp.zeros_like(pair))
 
     rows = SUB_HEADS * tok
+
+    def scores_of(sub, keys_ref, bias_ref):
+        queries = stack_ref[sub * rows : (sub + 1) * rows, :]
+        scores = lax.dot_general(
+            queries, keys_ref[...], (((1,), (1,)), ((), ())), preferred_element_type=jnp.float32
+        )
+        return scores.reshape(SUB_HEADS, tok, keys) * LOG2_SCALE + bias_ref[...][None]
+
+    def both_scores(sub):
+        return scores_of(sub, mine_ref, bias_a_ref), scores_of(sub, other_ref, bias_b_ref)
+
     parts = []
-    for sub in range(HEAD_GROUP // SUB_HEADS):
-        queries = stack_ref[sub * rows : (sub + 1) * rows, :]
-
-        def scores_of(keys_ref, bias_ref):
-            scores = lax.dot_general(
-                queries, keys_ref[...], (((1,), (1,)), ((), ())),
-                preferred_element_type=jnp.float32,
-            )
-            return scores.reshape(SUB_HEADS, tok, keys) * LOG2_SCALE + bias_ref[...][None]
-
-        scores_a = scores_of(mine_ref, bias_a_ref)
-        scores_b = scores_of(other_ref, bias_b_ref)
+    subs = HEAD_GROUP // SUB_HEADS
+    ready = both_scores(0)
+    for sub in range(subs):
+        scores_a, scores_b = ready
+        if sub + 1 < subs:
+            ready = both_scores(sub + 1)
         top = jnp.max(jnp.maximum(scores_a, scores_b), axis=2, keepdims=True)
         weights_a = jnp.exp2(scores_a - top)
         weights_b = jnp.exp2(scores_b - top)
@@ -160,9 +165,9 @@
 
 
 def expert_kernel(
-    index_ref, upper_ref, lower_ref, hits_ref, gate_a, up_a, down_a, gate_hbm, up_hbm, down_hbm, upper_out,
-    lower_out, gate_b, up_b, down_b, sems, *, hop, chips,
+    index_ref, hits_ref, gate_a, up_a, down_a, gate_hbm, up_hbm, down_hbm, *refs, hop, chips,
 ):
+    *rows_refs, out_ref, gate_b, up_b, down_b, sems = refs
     copies = [
         pltpu.make_async_copy(there, here, sems.at[i])
         for i, (there, here) in enumerate(((gate_hbm, gate_b), (up_hbm, up_b), (down_hbm, down_b)))
@@ -174,7 +179,7 @@
     source = ring_chip(lax.rem(place, chips), chips) ^ my_chip
     column = lax.broadcasted_iota(jnp.int32, hits_ref.shape, 1)
     keep = jnp.max(jnp.where(column == source, hits_ref[...], 0.0), axis=1, keepdims=True) > 0.0
-    rows = jnp.concatenate([upper_ref[...], lower_ref[...]], axis=0)
+    rows = jnp.concatenate([ref[...] for ref in rows_refs], axis=0)
 
     def hidden(gate_ref, up_ref):
         gate_act = jnp.dot(rows, gate_ref[...], preferred_element_type=jnp.float32)
@@ -187,27 +192,25 @@
     copies[1].wait()
     hidden_b = hidden(gate_b, up_b)
     copies[2].wait()
-    part = part + jnp.dot(hidden_b, down_b[...], preferred_element_type=jnp.float32)
-    upper_out[...] = part[: upper_ref.shape[0]]
-    lower_out[...] = part[upper_ref.shape[0] :]
+    out_ref[...] = part + jnp.dot(hidden_b, down_b[...], preferred_element_type=jnp.float32)
 
 
 def expert_part(my_index, rows, hits, own, swapped, hop, chips):
-    tok, features = 2 * rows[0].shape[0], rows[0].shape[1]
+    tok, features = hits.shape[0], rows[0].shape[1]
     units = 2 * own[0].shape[1]
     vmem, anywhere = pl.BlockSpec(memory_space=pltpu.VMEM), pl.BlockSpec(memory_space=pl.ANY)
     return pl.pallas_call(
         functools.partial(expert_kernel, hop=hop, chips=chips),
-        in_specs=[pl.BlockSpec(memory_space=pltpu.SMEM)] + [vmem] * 6 + [anywhere] * 3,
-        out_specs=[vmem] * 2,
-        out_shape=[jax.ShapeDtypeStruct(x.shape, jnp.float32) for x in rows],
+        in_specs=[pl.BlockSpec(memory_space=pltpu.SMEM)] + [vmem] * 4 + [anywhere] * 3 + [vmem] * len(rows),
+        out_specs=vmem,
+        out_shape=jax.ShapeDtypeStruct((tok, features), jnp.float32),
         scratch_shapes=[pltpu.VMEM(w.shape, w.dtype) for w in swapped]
         + [pltpu.SemaphoreType.DMA((3,))],
         compiler_params=pltpu.CompilerParams(vmem_limit_bytes=24 << 20),
         cost_estimate=pl.CostEstimate(
-            flops=40 * tok * features * units, bytes_accessed=14 << 20, transcendentals=0
+            flops=6 * tok * features * units, bytes_accessed=14 << 20, transcendentals=0
         ),
-    )(my_index.reshape(1), *rows, hits, *own, *swapped)
+    )(my_index.reshape(1), hits, *own, *swapped, *rows)
 
 
 def local(
@@ -251,24 +254,19 @@
     def after(blocks, first):
         return tuple(lax.optimization_barrier((x, first))[0] for x in blocks)
 
-    def rounded(parts):
-        return tuple(x.astype(jnp.bfloat16) for x in parts)
-
-    def added(parts, arrived):
-        return tuple(x + y.astype(jnp.float32) for x, y in zip(parts, arrived))
-
     rows = [start]
     for hop in range(1, min(4, chips)):
-        rows.append(move(rows[-1]))
-    sums = rounded(part_of(rows[1], 1))
+        last = rows[-1]
+        rows.append(move((jnp.concatenate(last, axis=0),) if hop == 3 else last))
+    sums = part_of(rows[1], 1).astype(jnp.bfloat16)
     for hop in range(1, chips):
-        arrived = move(sums)
+        (arrived,) = move((sums,))
         if hop + 3 < chips:
-            rows.append(move(after(rows[hop + 2], sums[0])))
+            rows.append(move(after(rows[hop + 2], sums)))
         if hop + 1 < chips:
-            sums = rounded(added(part_of(rows[hop + 1], hop + 1), arrived))
-    home = part_of(after(start, sums[-1]), 0)
-    expert_out = jnp.concatenate(added(home, arrived), axis=0)
+            part = part_of(rows[hop + 1], hop + 1)
+            sums = (part + arrived.astype(jnp.float32)).astype(jnp.bfloat16)
+    expert_out = part_of(after(start, sums), 0) + arrived.astype(jnp.float32)
     gate_weight = gate_fixed.astype(jnp.float32) / 65536.0
     return (values.astype(jnp.float32) + gate_weight * expert_out).astype(jnp.bfloat16)
 

time: 130 us -> 125 us (0.962)
  waiting for transfers between devices: 38.4 us -> 30.9 us
  starting transfers between devices: 36.3 us -> 40 us
  Pallas kernels: 50.4 us -> 48.8 us
    ppermute x28 -> x16, waiting for transfers between devices: 31.6 us -> 24.3 us  [move(): return tuple((lax.ppermute(x, 'ctx', route) for x in blocks))]
    ppermute x28 -> x16, starting transfers between devices: 24.5 us -> 28 us  [move(): return tuple((lax.ppermute(x, 'ctx', route) for x in blocks))]
    pallas_call x1, Pallas kernels: 13.2 us -> 11.6 us  [attention(): pl.pallas_call(functools.partial(attention_kernel, tok=tok), grid_spec=gr...]
  transfers between devices with their start and end apart: 39 -> 27, of which waited for: 14 -> 16; matrix products, arithmetic and copies ran while one was open for 1% -> 1% of each run, Pallas kernels for 39% -> 39%
where the time goes in v8:
time: 125 us; the launch traced here: 124 us
  Pallas kernels  48.8 us (39%)
  starting transfers between devices  40 us (32%)
  waiting for transfers between devices  30.9 us (25%)
  other arithmetic  3.26 us (3%)
    pallas_call x8, Pallas kernels, expert_part(): pl.pallas_call(functools.partial(expert_kernel, hop=hop, chips=chips), in...  37.3 us
    ppermute x16, starting transfers between devices, move(): return tuple((lax.ppermute(x, 'ctx', route) for x in blocks))  28 us
    ppermute x16, waiting for transfers between devices, move(): return tuple((lax.ppermute(x, 'ctx', route) for x in blocks))  24.3 us
    pallas_call x1, Pallas kernels, attention(): pl.pallas_call(functools.partial(attention_kernel, tok=tok), grid_spec=gr...  11.6 us
    ppermute x7, starting transfers between devices, from_chip(): lax.ppermute(block, 'ctx', [(i, i ^ step * CORES) for i in range(n_ctx)])  11.4 us
    ppermute x7, waiting for transfers between devices, from_chip(): lax.ppermute(block, 'ctx', [(i, i ^ step * CORES) for i in range(n_ctx)])  4.54 us
  transfers between devices with their start and end apart: 27, of which 16 were waited for; matrix products, arithmetic and copies ran while one was open for 1% of the time, Pallas kernels for 39%

profile of v8, /device:TPU:0, one launch (start us, length us, event | category | flops | bytes accessed | tf_op | source)
XLA Modules:
  0.0 124.5 jit_solution(12346225912232871112)
XLA Ops:
  1.7 4.1 %collective-permute-start.3 = (bf16[64,640]{1,0:T(8,128)(2,1)S(1)}, bf16[64,640]{1,0:T(8,128)(2,1)S(1)}, u32[]{:S(2)}, u32[]{:S(2)}) collective-permute-start(bf16[64,640]{1,0:T(8,128)(2,1)S(1)} %get-tuple-element.45), channel_id=1, source_target_pairs={{0,8},{1,9},{2,10},{3,11},{4,12},{5,13},{6,14},{7,15},{8,0},{9,1},... | collective-permute-start | bytes 245768 | tf_op jit(solution)/shard_map/ppermute | solution.py:231
  5.8 1.5 %collective-permute-start = (bf16[64,640]{1,0:T(8,128)(2,1)S(1)}, bf16[64,640]{1,0:T(8,128)(2,1)S(1)}, u32[]{:S(2)}, u32[]{:S(2)}) collective-permute-start(bf16[64,640]{1,0:T(8,128)(2,1)S(1)} %get-tuple-element.45), channel_id=1, source_target_pairs={{0,2},{1,3},{2,0},{3,1},{4,6},{5,7},{6,4},{7,5},{8,10},{9,11},{10,... | collective-permute-start | bytes 245768 | tf_op jit(solution)/shard_map/ppermute | solution.py:231
  7.3 1.6 %collective-permute-start.1 = (bf16[64,640]{1,0:T(8,128)(2,1)S(1)}, bf16[64,640]{1,0:T(8,128)(2,1)S(1)}, u32[]{:S(2)}, u32[]{:S(2)}) collective-permute-start(bf16[64,640]{1,0:T(8,128)(2,1)S(1)} %get-tuple-element.45), channel_id=1, source_target_pairs={{0,4},{1,5},{2,6},{3,7},{4,0},{5,1},{6,2},{7,3},{8,12},{9,13},{10,... | collective-permute-start | bytes 245768 | tf_op jit(solution)/shard_map/ppermute | solution.py:231
  9.8 1.6 %collective-permute-start.4 = (bf16[64,640]{1,0:T(8,128)(2,1)S(1)}, bf16[64,640]{1,0:T(8,128)(2,1)S(1)}, u32[]{:S(2)}, u32[]{:S(2)}) collective-permute-start(bf16[64,640]{1,0:T(8,128)(2,1)S(1)} %collective-permute-done.3), channel_id=1, source_target_pairs={{0,2},{1,3},{2,0},{3,1},{4,6},{5,7},{6,4},{7,5},{8,10},{9,11},{10,... | collective-permute-start | bytes 245768 | tf_op jit(solution)/shard_map/ppermute | solution.py:231
  15.9 1.8 %collective-permute-done.6 = bf16[64,640]{1,0:T(8,128)(2,1)S(1)} collective-permute-done((bf16[64,640]{1,0:T(8,128)(2,1)S(1)}, bf16[64,640]{1,0:T(8,128)(2,1)S(1)}, u32[]{:S(2)}, u32[]{:S(2)}) %collective-permute-start.6) | collective-permute-done | bytes 81952 | tf_op jit(solution)/shard_map/ppermute | solution.py:231
  17.8 2.1 %collective-permute-done.7.other_ref = bf16[512,640]{1,0:T(8,128)(2,1)S(1)} collective-permute-done((bf16[512,640]{1,0:T(8,128)(2,1)S(1)}, bf16[512,640]{1,0:T(8,128)(2,1)S(1)}, u32[]{:S(2)}, u32[]{:S(2)}) %collective-permute-start.7) | collective-permute-done | bytes 655392 | tf_op jit(solution)/shard_map/ppermute | solution.py:239
  20.7 11.6 %shard_map.109 = (bf16[64,4096]{1,0:T(8,128)(2,1)}, bf16[32,4096]{1,0:T(8,128)(2,1)}, bf16[32,4096]{1,0:T(8,128)(2,1)}, f32[64,8]{1,0:T(8,128)}) custom-call(s32[1]{0:T(128)} %bitcast.index_ref, bf16[64,16384]{1,0:T(8,128)(2,1)} %q_ref.1, bf16[64,2048]{1,0:T(8,128)(2,1)} %qr_ref.1, bf16[512,640]{1,0:T(8,128)(2,1)} %copy-done.8, bf16[512,640]{1,0:T(8,128)(2,1)} %copy-done.9, ...), custom_call_target="tpu_custom_call" | custom-call | flops 4831838208 | bytes 8388608 | tf_op jit(solution)/shard_map/pallas_call | solution.py:148
  33.5 2.7 %collective-permute-start.11 = (bf16[32,4096]{1,0:T(8,128)(2,1)}, bf16[32,4096]{1,0:T(8,128)(2,1)S(1)}, u32[]{:S(2)}, u32[]{:S(2)}) collective-permute-start(bf16[32,4096]{1,0:T(8,128)(2,1)} %get-tuple-element.43.refs_0_), channel_id=1, source_target_pairs={{0,4},{1,3},{4,8},{5,1},{8,12},{9,5},{12,14},{13,9},{14,10},{15,13... | collective-permute-start | bytes 786440 | tf_op jit(solution)/shard_map/ppermute | solution.py:252
  36.2 2.8 %collective-permute-done.13.refs_1_ = bf16[32,4096]{1,0:T(8,128)(2,1)S(1)} collective-permute-done((bf16[32,4096]{1,0:T(8,128)(2,1)}, bf16[32,4096]{1,0:T(8,128)(2,1)S(1)}, u32[]{:S(2)}, u32[]{:S(2)}) %collective-permute-start.13) | collective-permute-done | bytes 262176 | tf_op jit(solution)/shard_map/ppermute | solution.py:252
  41.8 1.5 %collective-permute-start.12 = (bf16[32,4096]{1,0:T(8,128)(2,1)S(1)}, bf16[32,4096]{1,0:T(8,128)(2,1)S(1)}, u32[]{:S(2)}, u32[]{:S(2)}) collective-permute-start(bf16[32,4096]{1,0:T(8,128)(2,1)S(1)} %collective-permute-done.11.refs_0_), channel_id=1, source_target_pairs={{0,4},{1,3},{4,8},{5,1},{8,12},{9,5},{12,14},{13,9},{14,10},{15,13... | collective-permute-start | bytes 786440 | tf_op jit(solution)/shard_map/ppermute | solution.py:252
  44.0 4.7 %shard_map.110 = f32[64,4096]{1,0:T(8,128)S(1)} custom-call(s32[1]{0:T(128)} %bitcast.index_ref, f32[64,8]{1,0:T(8,128)S(1)} %copy-done.3, bf16[4096,256]{1,0:T(8,128)(2,1)S(1)} %bitcast.10, bf16[4096,256]{1,0:T(8,128)(2,1)S(1)} %bitcast.19, bf16[256,4096]{1,0:T(8,128)(2,1)S(1)} %bitcast.28, bf16[4096,256]{1,0:T(8,128)(2,1)} %collective-permute-done.8.gate_hbm, ...), custom_call_target="tpu_custom_call" | custom-call | flops 805306368 | bytes 14680064 | tf_op jit(solution)/shard_map/pallas_call | solution.py:202
  48.7 2.4 %collective-permute-start.17 = (bf16[64,4096]{1,0:T(8,128)(2,1)S(1)}, bf16[64,4096]{1,0:T(8,128)(2,1)S(1)}, u32[]{:S(2)}, u32[]{:S(2)}) collective-permute-start(bf16[64,4096]{1,0:T(8,128)(2,1)S(1)} %convert_element_type.57), channel_id=1, source_target_pairs={{0,4},{1,3},{4,8},{5,1},{8,12},{9,5},{12,14},{13,9},{14,10},{15,13... | collective-permute-start | bytes 1572872 | tf_op jit(solution)/shard_map/ppermute | solution.py:252
  51.6 4.7 %shard_map.111 = f32[64,4096]{1,0:T(8,128)S(1)} custom-call(s32[1]{0:T(128)} %bitcast.index_ref, f32[64,8]{1,0:T(8,128)S(1)} %copy-done.3, bf16[4096,256]{1,0:T(8,128)(2,1)S(1)} %bitcast.11, bf16[4096,256]{1,0:T(8,128)(2,1)S(1)} %bitcast.20, bf16[256,4096]{1,0:T(8,128)(2,1)S(1)} %bitcast.29, bf16[4096,256]{1,0:T(8,128)(2,1)} %collective-permute-done.8.gate_hbm, ...), custom_call_target="tpu_custom_call" | custom-call | flops 805306368 | bytes 14680064 | tf_op jit(solution)/shard_map/pallas_call | solution.py:202
  56.3 1.7 %collective-permute-done.17 = bf16[64,4096]{1,0:T(8,128)(2,1)S(1)} collective-permute-done((bf16[64,4096]{1,0:T(8,128)(2,1)S(1)}, bf16[64,4096]{1,0:T(8,128)(2,1)S(1)}, u32[]{:S(2)}, u32[]{:S(2)}) %collective-permute-start.17) | collective-permute-done | bytes 524320 | tf_op jit(solution)/shard_map/ppermute | solution.py:252
  58.1 2.4 %collective-permute-start.19 = (bf16[64,4096]{1,0:T(8,128)(2,1)S(1)}, bf16[64,4096]{1,0:T(8,128)(2,1)S(1)}, u32[]{:S(2)}, u32[]{:S(2)}) collective-permute-start(bf16[64,4096]{1,0:T(8,128)(2,1)S(1)} %add_convert_fusion.6), channel_id=1, source_target_pairs={{0,4},{1,3},{4,8},{5,1},{8,12},{9,5},{12,14},{13,9},{14,10},{15,13... | collective-permute-start | bytes 1572872 | tf_op jit(solution)/shard_map/ppermute | solution.py:252
  60.5 3.1 %collective-permute-done.15.refs_0_ = bf16[64,4096]{1,0:T(8,128)(2,1)S(1)} collective-permute-done((bf16[64,4096]{1,0:T(8,128)(2,1)S(1)}, bf16[64,4096]{1,0:T(8,128)(2,1)S(1)}, u32[]{:S(2)}, u32[]{:S(2)}) %collective-permute-start.15) | collective-permute-done | bytes 524320 | tf_op jit(solution)/shard_map/ppermute | solution.py:252
  63.6 2.4 %collective-permute-start.16 = (bf16[64,4096]{1,0:T(8,128)(2,1)S(1)}, bf16[64,4096]{1,0:T(8,128)(2,1)S(1)}, u32[]{:S(2)}, u32[]{:S(2)}) collective-permute-start(bf16[64,4096]{1,0:T(8,128)(2,1)S(1)} %collective-permute-done.15.refs_0_), channel_id=1, source_target_pairs={{0,4},{1,3},{4,8},{5,1},{8,12},{9,5},{12,14},{13,9},{14,10},{15,13... | collective-permute-start | bytes 1572872 | tf_op jit(solution)/shard_map/ppermute | solution.py:252
  66.0 4.7 %shard_map.112 = f32[64,4096]{1,0:T(8,128)S(1)} custom-call(s32[1]{0:T(128)} %bitcast.index_ref, f32[64,8]{1,0:T(8,128)S(1)} %copy-done.3, bf16[4096,256]{1,0:T(8,128)(2,1)S(1)} %bitcast.12, bf16[4096,256]{1,0:T(8,128)(2,1)S(1)} %bitcast.21, bf16[256,4096]{1,0:T(8,128)(2,1)S(1)} %bitcast.30, bf16[4096,256]{1,0:T(8,128)(2,1)} %collective-permute-done.8.gate_hbm, ...), custom_call_target="tpu_custom_call" | custom-call | flops 805306368 | bytes 14680064 | tf_op jit(solution)/shard_map/pallas_call | solution.py:202
  71.7 3.1 %collective-permute-done.16.refs_0_ = bf16[64,4096]{1,0:T(8,128)(2,1)S(1)} collective-permute-done((bf16[64,4096]{1,0:T(8,128)(2,1)S(1)}, bf16[64,4096]{1,0:T(8,128)(2,1)S(1)}, u32[]{:S(2)}, u32[]{:S(2)}) %collective-permute-start.16) | collective-permute-done | bytes 524320 | tf_op jit(solution)/shard_map/ppermute | solution.py:252
  74.8 2.4 %collective-permute-start.18 = (bf16[64,4096]{1,0:T(8,128)(2,1)S(1)}, bf16[64,4096]{1,0:T(8,128)(2,1)S(1)}, u32[]{:S(2)}, u32[]{:S(2)}) collective-permute-start(bf16[64,4096]{1,0:T(8,128)(2,1)S(1)} %collective-permute-done.16.refs_0_), channel_id=1, source_target_pairs={{0,4},{1,3},{4,8},{5,1},{8,12},{9,5},{12,14},{13,9},{14,10},{15,13... | collective-permute-start | bytes 1572872 | tf_op jit(solution)/shard_map/ppermute | solution.py:252
  77.2 4.7 %shard_map.113 = f32[64,4096]{1,0:T(8,128)S(1)} custom-call(s32[1]{0:T(128)} %bitcast.index_ref, f32[64,8]{1,0:T(8,128)S(1)} %copy-done.3, bf16[4096,256]{1,0:T(8,128)(2,1)S(1)} %bitcast.13, bf16[4096,256]{1,0:T(8,128)(2,1)S(1)} %bitcast.22, bf16[256,4096]{1,0:T(8,128)(2,1)S(1)} %bitcast.31, bf16[4096,256]{1,0:T(8,128)(2,1)} %collective-permute-done.8.gate_hbm, ...), custom_call_target="tpu_custom_call" | custom-call | flops 805306368 | bytes 14680064 | tf_op jit(solution)/shard_map/pallas_call | solution.py:202
  83.0 3.1 %collective-permute-done.18.refs_0_ = bf16[64,4096]{1,0:T(8,128)(2,1)S(1)} collective-permute-done((bf16[64,4096]{1,0:T(8,128)(2,1)S(1)}, bf16[64,4096]{1,0:T(8,128)(2,1)S(1)}, u32[]{:S(2)}, u32[]{:S(2)}) %collective-permute-start.18) | collective-permute-done | bytes 524320 | tf_op jit(solution)/shard_map/ppermute | solution.py:252
  86.1 2.4 %collective-permute-start.20 = (bf16[64,4096]{1,0:T(8,128)(2,1)S(1)}, bf16[64,4096]{1,0:T(8,128)(2,1)S(1)}, u32[]{:S(2)}, u32[]{:S(2)}) collective-permute-start(bf16[64,4096]{1,0:T(8,128)(2,1)S(1)} %collective-permute-done.18.refs_0_), channel_id=1, source_target_pairs={{0,4},{1,3},{4,8},{5,1},{8,12},{9,5},{12,14},{13,9},{14,10},{15,13... | collective-permute-start | bytes 1572872 | tf_op jit(solution)/shard_map/ppermute | solution.py:252
  88.4 4.7 %shard_map.116 = f32[64,4096]{1,0:T(8,128)S(1)} custom-call(s32[1]{0:T(128)} %bitcast.index_ref, f32[64,8]{1,0:T(8,128)S(1)} %copy-done.3, bf16[4096,256]{1,0:T(8,128)(2,1)S(1)} %bitcast.14, bf16[4096,256]{1,0:T(8,128)(2,1)S(1)} %bitcast.23, bf16[256,4096]{1,0:T(8,128)(2,1)S(1)} %bitcast.32, bf16[4096,256]{1,0:T(8,128)(2,1)} %collective-permute-done.8.gate_hbm, ...), custom_call_target="tpu_custom_call" | custom-call | flops 805306368 | bytes 14680064 | tf_op jit(solution)/shard_map/pallas_call | solution.py:202
  94.2 3.1 %collective-permute-done.20.refs_0_ = bf16[64,4096]{1,0:T(8,128)(2,1)S(1)} collective-permute-done((bf16[64,4096]{1,0:T(8,128)(2,1)S(1)}, bf16[64,4096]{1,0:T(8,128)(2,1)S(1)}, u32[]{:S(2)}, u32[]{:S(2)}) %collective-permute-start.20) | collective-permute-done | bytes 524320 | tf_op jit(solution)/shard_map/ppermute | solution.py:252
  97.3 2.4 %collective-permute-start.22 = (bf16[64,4096]{1,0:T(8,128)(2,1)S(1)}, bf16[64,4096]{1,0:T(8,128)(2,1)S(1)}, u32[]{:S(2)}, u32[]{:S(2)}) collective-permute-start(bf16[64,4096]{1,0:T(8,128)(2,1)S(1)} %collective-permute-done.20.refs_0_), channel_id=1, source_target_pairs={{0,4},{1,3},{4,8},{5,1},{8,12},{9,5},{12,14},{13,9},{14,10},{15,13... | collective-permute-start | bytes 1572872 | tf_op jit(solution)/shard_map/ppermute | solution.py:252
  99.7 4.7 %shard_map.115 = f32[64,4096]{1,0:T(8,128)S(1)} custom-call(s32[1]{0:T(128)} %bitcast.index_ref, f32[64,8]{1,0:T(8,128)S(1)} %copy-done.3, bf16[4096,256]{1,0:T(8,128)(2,1)S(1)} %bitcast.15, bf16[4096,256]{1,0:T(8,128)(2,1)S(1)} %bitcast.24, bf16[256,4096]{1,0:T(8,128)(2,1)S(1)} %bitcast.33, bf16[4096,256]{1,0:T(8,128)(2,1)} %collective-permute-done.8.gate_hbm, ...), custom_call_target="tpu_custom_call" | custom-call | flops 805306368 | bytes 14680064 | tf_op jit(solution)/shard_map/pallas_call | solution.py:202
  105.4 3.1 %collective-permute-done.22.refs_0_ = bf16[64,4096]{1,0:T(8,128)(2,1)S(1)} collective-permute-done((bf16[64,4096]{1,0:T(8,128)(2,1)S(1)}, bf16[64,4096]{1,0:T(8,128)(2,1)S(1)}, u32[]{:S(2)}, u32[]{:S(2)}) %collective-permute-start.22) | collective-permute-done | bytes 524320 | tf_op jit(solution)/shard_map/ppermute | solution.py:252
  108.5 4.7 %shard_map.114 = f32[64,4096]{1,0:T(8,128)S(1)} custom-call(s32[1]{0:T(128)} %bitcast.index_ref, f32[64,8]{1,0:T(8,128)S(1)} %copy-done.3, bf16[4096,256]{1,0:T(8,128)(2,1)S(1)} %bitcast.16, bf16[4096,256]{1,0:T(8,128)(2,1)S(1)} %bitcast.25, bf16[256,4096]{1,0:T(8,128)(2,1)S(1)} %bitcast.34, bf16[4096,256]{1,0:T(8,128)(2,1)} %collective-permute-done.8.gate_hbm, ...), custom_call_target="tpu_custom_call" | custom-call | flops 805306368 | bytes 14680064 | tf_op jit(solution)/shard_map/pallas_call | solution.py:202
  114.2 2.4 %collective-permute-start.26 = (bf16[64,4096]{1,0:T(8,128)(2,1)S(1)}, bf16[64,4096]{1,0:T(8,128)(2,1)S(1)}, u32[]{:S(2)}, u32[]{:S(2)}) collective-permute-start(bf16[64,4096]{1,0:T(8,128)(2,1)S(1)} %add_convert_fusion.1), channel_id=1, source_target_pairs={{0,4},{1,3},{4,8},{5,1},{8,12},{9,5},{12,14},{13,9},{14,10},{15,13... | collective-permute-start | bytes 1572872 | tf_op jit(solution)/shard_map/ppermute | solution.py:252
  116.7 4.7 %shard_map.117 = f32[64,4096]{1,0:T(8,128)S(1)} custom-call(s32[1]{0:T(128)} %bitcast.index_ref, f32[64,8]{1,0:T(8,128)S(1)} %copy-done.4, bf16[4096,256]{1,0:T(8,128)(2,1)S(1)} %bitcast.17, bf16[4096,256]{1,0:T(8,128)(2,1)S(1)} %bitcast.26, bf16[256,4096]{1,0:T(8,128)(2,1)S(1)} %bitcast.35, bf16[4096,256]{1,0:T(8,128)(2,1)} %collective-permute-done.8.gate_hbm, ...), custom_call_target="tpu_custom_call" | custom-call | flops 805306368 | bytes 14680064 | tf_op jit(solution)/shard_map/pallas_call | solution.py:202
  121.4 2.1 %collective-permute-done.26 = bf16[64,4096]{1,0:T(8,128)(2,1)S(1)} collective-permute-done((bf16[64,4096]{1,0:T(8,128)(2,1)S(1)}, bf16[64,4096]{1,0:T(8,128)(2,1)S(1)}, u32[]{:S(2)}, u32[]{:S(2)}) %collective-permute-start.26) | collective-permute-done | bytes 524320 | tf_op jit(solution)/shard_map/ppermute | solution.py:252
  (73 shorter events, 19.7 us)
Async XLA Ops:
  1.7 8.1 %collective-permute-start.3 = (bf16[64,640]{1,0:T(8,128)(2,1)S(1)}, bf16[64,640]{1,0:T(8,128)(2,1)S(1)}, u32[]{:S(2)}, u32[]{:S(2)}) collective-permute-start(bf16[64,640]{1,0:T(8,128)(2,1)S(1)} %get-tuple-element.45), channel_id=1, source_target_pairs={{0,8},{1,9},{2,10},{3,11},{4,12},{5,13},{6,14},{7,15},{8,0},{9,1},... | collective-permute-start | bytes 245768 | tf_op jit(solution)/shard_map/ppermute | solution.py:231
  5.8 6.6 %collective-permute-start = (bf16[64,640]{1,0:T(8,128)(2,1)S(1)}, bf16[64,640]{1,0:T(8,128)(2,1)S(1)}, u32[]{:S(2)}, u32[]{:S(2)}) collective-permute-start(bf16[64,640]{1,0:T(8,128)(2,1)S(1)} %get-tuple-element.45), channel_id=1, source_target_pairs={{0,2},{1,3},{2,0},{3,1},{4,6},{5,7},{6,4},{7,5},{8,10},{9,11},{10,... | collective-permute-start | bytes 245768 | tf_op jit(solution)/shard_map/ppermute | solution.py:231
  7.3 6.3 %collective-permute-start.1 = (bf16[64,640]{1,0:T(8,128)(2,1)S(1)}, bf16[64,640]{1,0:T(8,128)(2,1)S(1)}, u32[]{:S(2)}, u32[]{:S(2)}) collective-permute-start(bf16[64,640]{1,0:T(8,128)(2,1)S(1)} %get-tuple-element.45), channel_id=1, source_target_pairs={{0,4},{1,5},{2,6},{3,7},{4,0},{5,1},{6,2},{7,3},{8,12},{9,13},{10,... | collective-permute-start | bytes 245768 | tf_op jit(solution)/shard_map/ppermute | solution.py:231
  8.9 5.6 %collective-permute-start.2 = (bf16[64,640]{1,0:T(8,128)(2,1)S(1)}, bf16[64,640]{1,0:T(8,128)(2,1)S(1)}, u32[]{:S(2)}, u32[]{:S(2)}) collective-permute-start(bf16[64,640]{1,0:T(8,128)(2,1)S(1)} %get-tuple-element.45), channel_id=1, source_target_pairs={{0,6},{1,7},{2,4},{3,5},{4,2},{5,3},{6,0},{7,1},{8,14},{9,15},{10,... | collective-permute-start | bytes 245768 | tf_op jit(solution)/shard_map/ppermute | solution.py:231
  9.8 5.5 %collective-permute-start.4 = (bf16[64,640]{1,0:T(8,128)(2,1)S(1)}, bf16[64,640]{1,0:T(8,128)(2,1)S(1)}, u32[]{:S(2)}, u32[]{:S(2)}) collective-permute-start(bf16[64,640]{1,0:T(8,128)(2,1)S(1)} %collective-permute-done.3), channel_id=1, source_target_pairs={{0,2},{1,3},{2,0},{3,1},{4,6},{5,7},{6,4},{7,5},{8,10},{9,11},{10,... | collective-permute-start | bytes 245768 | tf_op jit(solution)/shard_map/ppermute | solution.py:231
  11.4 4.5 %collective-permute-start.5 = (bf16[64,640]{1,0:T(8,128)(2,1)S(1)}, bf16[64,640]{1,0:T(8,128)(2,1)S(1)}, u32[]{:S(2)}, u32[]{:S(2)}) collective-permute-start(bf16[64,640]{1,0:T(8,128)(2,1)S(1)} %collective-permute-done.3), channel_id=1, source_target_pairs={{0,4},{1,5},{2,6},{3,7},{4,0},{5,1},{6,2},{7,3},{8,12},{9,13},{10,... | collective-permute-start | bytes 245768 | tf_op jit(solution)/shard_map/ppermute | solution.py:231
  12.4 5.3 %collective-permute-start.6 = (bf16[64,640]{1,0:T(8,128)(2,1)S(1)}, bf16[64,640]{1,0:T(8,128)(2,1)S(1)}, u32[]{:S(2)}, u32[]{:S(2)}) collective-permute-start(bf16[64,640]{1,0:T(8,128)(2,1)S(1)} %collective-permute-done.3), channel_id=1, source_target_pairs={{0,6},{1,7},{2,4},{3,5},{4,2},{5,3},{6,0},{7,1},{8,14},{9,15},{10,... | collective-permute-start | bytes 245768 | tf_op jit(solution)/shard_map/ppermute | solution.py:231
  17.7 2.2 %collective-permute-start.7 = (bf16[512,640]{1,0:T(8,128)(2,1)S(1)}, bf16[512,640]{1,0:T(8,128)(2,1)S(1)}, u32[]{:S(2)}, u32[]{:S(2)}) collective-permute-start(bf16[512,640]{1,0:T(8,128)(2,1)S(1)} %constant_dynamic-update-slice_fusion.mine_ref), channel_id=1, source_target_pairs={{0,1},{1,0},{2,3},{3,2},{4,5},{5,4},{6,7},{7,6},{8,9},{9,8},{10,11... | collective-permute-start | bytes 1966088 | tf_op jit(solution)/shard_map/ppermute | solution.py:239
  19.9 12.4 %collective-permute-start.8 = (bf16[4096,256]{1,0:T(8,128)(2,1)}, bf16[4096,256]{1,0:T(8,128)(2,1)}, u32[]{:S(2)}, u32[]{:S(2)}) collective-permute-start(bf16[4096,256]{1,0:T(8,128)(2,1)} %bitcast.9), channel_id=1, source_target_pairs={{0,1},{1,0},{2,3},{3,2},{4,5},{5,4},{6,7},{7,6},{8,9},{9,8},{10,11... | collective-permute-start | bytes 6291464 | tf_op jit(solution)/shard_map/ppermute | solution.py:242
  20.0 12.3 %collective-permute-start.9 = (bf16[4096,256]{1,0:T(8,128)(2,1)}, bf16[4096,256]{1,0:T(8,128)(2,1)}, u32[]{:S(2)}, u32[]{:S(2)}) collective-permute-start(bf16[4096,256]{1,0:T(8,128)(2,1)} %bitcast.18), channel_id=1, source_target_pairs={{0,1},{1,0},{2,3},{3,2},{4,5},{5,4},{6,7},{7,6},{8,9},{9,8},{10,11... | collective-permute-start | bytes 6291464 | tf_op jit(solution)/shard_map/ppermute | solution.py:242
  20.4 11.9 %collective-permute-start.10 = (bf16[256,4096]{1,0:T(8,128)(2,1)}, bf16[256,4096]{1,0:T(8,128)(2,1)}, u32[]{:S(2)}, u32[]{:S(2)}) collective-permute-start(bf16[256,4096]{1,0:T(8,128)(2,1)} %bitcast.27), channel_id=1, source_target_pairs={{0,1},{1,0},{2,3},{3,2},{4,5},{5,4},{6,7},{7,6},{8,9},{9,8},{10,11... | collective-permute-start | bytes 6291464 | tf_op jit(solution)/shard_map/ppermute | solution.py:242
  20.7 22.5 %copy-start = (bf16[1,4096,256]{2,1,0:T(8,128)(2,1)S(1)}, bf16[1,4096,256]{2,1,0:T(8,128)(2,1)}, u32[]{:S(2)}) copy-start(bf16[1,4096,256]{2,1,0:T(8,128)(2,1)} %param.19) | copy-start | bytes 6291460
  20.7 22.5 %copy-start.1 = (bf16[1,4096,256]{2,1,0:T(8,128)(2,1)S(1)}, bf16[1,4096,256]{2,1,0:T(8,128)(2,1)}, u32[]{:S(2)}) copy-start(bf16[1,4096,256]{2,1,0:T(8,128)(2,1)} %param.20) | copy-start | bytes 6291460
  20.7 22.5 %copy-start.2 = (bf16[1,256,4096]{2,1,0:T(8,128)(2,1)S(1)}, bf16[1,256,4096]{2,1,0:T(8,128)(2,1)}, u32[]{:S(2)}) copy-start(bf16[1,256,4096]{2,1,0:T(8,128)(2,1)} %param.21) | copy-start | bytes 6291460
  32.3 6.6 %collective-permute-start.13 = (bf16[32,4096]{1,0:T(8,128)(2,1)}, bf16[32,4096]{1,0:T(8,128)(2,1)S(1)}, u32[]{:S(2)}, u32[]{:S(2)}) collective-permute-start(bf16[32,4096]{1,0:T(8,128)(2,1)} %get-tuple-element.44.refs_1_), channel_id=1, source_target_pairs={{0,4},{1,3},{4,8},{5,1},{8,12},{9,5},{12,14},{13,9},{14,10},{15,13... | collective-permute-start | bytes 786440 | tf_op jit(solution)/shard_map/ppermute | solution.py:252
  33.5 8.3 %collective-permute-start.11 = (bf16[32,4096]{1,0:T(8,128)(2,1)}, bf16[32,4096]{1,0:T(8,128)(2,1)S(1)}, u32[]{:S(2)}, u32[]{:S(2)}) collective-permute-start(bf16[32,4096]{1,0:T(8,128)(2,1)} %get-tuple-element.43.refs_0_), channel_id=1, source_target_pairs={{0,4},{1,3},{4,8},{5,1},{8,12},{9,5},{12,14},{13,9},{14,10},{15,13... | collective-permute-start | bytes 786440 | tf_op jit(solution)/shard_map/ppermute | solution.py:252
  39.0 12.2 %collective-permute-start.14 = (bf16[32,4096]{1,0:T(8,128)(2,1)S(1)}, bf16[32,4096]{1,0:T(8,128)(2,1)S(1)}, u32[]{:S(2)}, u32[]{:S(2)}) collective-permute-start(bf16[32,4096]{1,0:T(8,128)(2,1)S(1)} %collective-permute-done.13.refs_1_), channel_id=1, source_target_pairs={{0,4},{1,3},{4,8},{5,1},{8,12},{9,5},{12,14},{13,9},{14,10},{15,13... | collective-permute-start | bytes 786440 | tf_op jit(solution)/shard_map/ppermute | solution.py:252
  41.8 9.4 %collective-permute-start.12 = (bf16[32,4096]{1,0:T(8,128)(2,1)S(1)}, bf16[32,4096]{1,0:T(8,128)(2,1)S(1)}, u32[]{:S(2)}, u32[]{:S(2)}) collective-permute-start(bf16[32,4096]{1,0:T(8,128)(2,1)S(1)} %collective-permute-done.11.refs_0_), channel_id=1, source_target_pairs={{0,4},{1,3},{4,8},{5,1},{8,12},{9,5},{12,14},{13,9},{14,10},{15,13... | collective-permute-start | bytes 786440 | tf_op jit(solution)/shard_map/ppermute | solution.py:252
  48.7 9.2 %collective-permute-start.17 = (bf16[64,4096]{1,0:T(8,128)(2,1)S(1)}, bf16[64,4096]{1,0:T(8,128)(2,1)S(1)}, u32[]{:S(2)}, u32[]{:S(2)}) collective-permute-start(bf16[64,4096]{1,0:T(8,128)(2,1)S(1)} %convert_element_type.57), channel_id=1, source_target_pairs={{0,4},{1,3},{4,8},{5,1},{8,12},{9,5},{12,14},{13,9},{14,10},{15,13... | collective-permute-start | bytes 1572872 | tf_op jit(solution)/shard_map/ppermute | solution.py:252
  51.2 12.4 %collective-permute-start.15 = (bf16[64,4096]{1,0:T(8,128)(2,1)S(1)}, bf16[64,4096]{1,0:T(8,128)(2,1)S(1)}, u32[]{:S(2)}, u32[]{:S(2)}) collective-permute-start(bf16[64,4096]{1,0:T(8,128)(2,1)S(1)} %pad_maximum_fusion), channel_id=1, source_target_pairs={{0,4},{1,3},{4,8},{5,1},{8,12},{9,5},{12,14},{13,9},{14,10},{15,13... | collective-permute-start | bytes 1572872 | tf_op jit(solution)/shard_map/ppermute | solution.py:252
  58.1 12.6 %collective-permute-start.19 = (bf16[64,4096]{1,0:T(8,128)(2,1)S(1)}, bf16[64,4096]{1,0:T(8,128)(2,1)S(1)}, u32[]{:S(2)}, u32[]{:S(2)}) collective-permute-start(bf16[64,4096]{1,0:T(8,128)(2,1)S(1)} %add_convert_fusion.6), channel_id=1, source_target_pairs={{0,4},{1,3},{4,8},{5,1},{8,12},{9,5},{12,14},{13,9},{14,10},{15,13... | collective-permute-start | bytes 1572872 | tf_op jit(solution)/shard_map/ppermute | solution.py:252
  63.6 11.2 %collective-permute-start.16 = (bf16[64,4096]{1,0:T(8,128)(2,1)S(1)}, bf16[64,4096]{1,0:T(8,128)(2,1)S(1)}, u32[]{:S(2)}, u32[]{:S(2)}) collective-permute-start(bf16[64,4096]{1,0:T(8,128)(2,1)S(1)} %collective-permute-done.15.refs_0_), channel_id=1, source_target_pairs={{0,4},{1,3},{4,8},{5,1},{8,12},{9,5},{12,14},{13,9},{14,10},{15,13... | collective-permute-start | bytes 1572872 | tf_op jit(solution)/shard_map/ppermute | solution.py:252
  70.7 11.1 %collective-permute-start.21 = (bf16[64,4096]{1,0:T(8,128)(2,1)S(1)}, bf16[64,4096]{1,0:T(8,128)(2,1)S(1)}, u32[]{:S(2)}, u32[]{:S(2)}) collective-permute-start(bf16[64,4096]{1,0:T(8,128)(2,1)S(1)} %add_convert_fusion.5), channel_id=1, source_target_pairs={{0,4},{1,3},{4,8},{5,1},{8,12},{9,5},{12,14},{13,9},{14,10},{15,13... | collective-permute-start | bytes 1572872 | tf_op jit(solution)/shard_map/ppermute | solution.py:252
  74.8 11.2 %collective-permute-start.18 = (bf16[64,4096]{1,0:T(8,128)(2,1)S(1)}, bf16[64,4096]{1,0:T(8,128)(2,1)S(1)}, u32[]{:S(2)}, u32[]{:S(2)}) collective-permute-start(bf16[64,4096]{1,0:T(8,128)(2,1)S(1)} %collective-permute-done.16.refs_0_), channel_id=1, source_target_pairs={{0,4},{1,3},{4,8},{5,1},{8,12},{9,5},{12,14},{13,9},{14,10},{15,13... | collective-permute-start | bytes 1572872 | tf_op jit(solution)/shard_map/ppermute | solution.py:252
  82.0 11.1 %collective-permute-start.23 = (bf16[64,4096]{1,0:T(8,128)(2,1)S(1)}, bf16[64,4096]{1,0:T(8,128)(2,1)S(1)}, u32[]{:S(2)}, u32[]{:S(2)}) collective-permute-start(bf16[64,4096]{1,0:T(8,128)(2,1)S(1)} %add_convert_fusion.4), channel_id=1, source_target_pairs={{0,4},{1,3},{4,8},{5,1},{8,12},{9,5},{12,14},{13,9},{14,10},{15,13... | collective-permute-start | bytes 1572872 | tf_op jit(solution)/shard_map/ppermute | solution.py:252
  86.1 11.2 %collective-permute-start.20 = (bf16[64,4096]{1,0:T(8,128)(2,1)S(1)}, bf16[64,4096]{1,0:T(8,128)(2,1)S(1)}, u32[]{:S(2)}, u32[]{:S(2)}) collective-permute-start(bf16[64,4096]{1,0:T(8,128)(2,1)S(1)} %collective-permute-done.18.refs_0_), channel_id=1, source_target_pairs={{0,4},{1,3},{4,8},{5,1},{8,12},{9,5},{12,14},{13,9},{14,10},{15,13... | collective-permute-start | bytes 1572872 | tf_op jit(solution)/shard_map/ppermute | solution.py:252
  93.2 11.1 %collective-permute-start.24 = (bf16[64,4096]{1,0:T(8,128)(2,1)S(1)}, bf16[64,4096]{1,0:T(8,128)(2,1)S(1)}, u32[]{:S(2)}, u32[]{:S(2)}) collective-permute-start(bf16[64,4096]{1,0:T(8,128)(2,1)S(1)} %add_convert_fusion.3), channel_id=1, source_target_pairs={{0,4},{1,3},{4,8},{5,1},{8,12},{9,5},{12,14},{13,9},{14,10},{15,13... | collective-permute-start | bytes 1572872 | tf_op jit(solution)/shard_map/ppermute | solution.py:252
  97.3 11.2 %collective-permute-start.22 = (bf16[64,4096]{1,0:T(8,128)(2,1)S(1)}, bf16[64,4096]{1,0:T(8,128)(2,1)S(1)}, u32[]{:S(2)}, u32[]{:S(2)}) collective-permute-start(bf16[64,4096]{1,0:T(8,128)(2,1)S(1)} %collective-permute-done.20.refs_0_), channel_id=1, source_target_pairs={{0,4},{1,3},{4,8},{5,1},{8,12},{9,5},{12,14},{13,9},{14,10},{15,13... | collective-permute-start | bytes 1572872 | tf_op jit(solution)/shard_map/ppermute | solution.py:252
  104.4 9.7 %collective-permute-start.25 = (bf16[64,4096]{1,0:T(8,128)(2,1)S(1)}, bf16[64,4096]{1,0:T(8,128)(2,1)S(1)}, u32[]{:S(2)}, u32[]{:S(2)}) collective-permute-start(bf16[64,4096]{1,0:T(8,128)(2,1)S(1)} %add_convert_fusion.2), channel_id=1, source_target_pairs={{0,4},{1,3},{4,8},{5,1},{8,12},{9,5},{12,14},{13,9},{14,10},{15,13... | collective-permute-start | bytes 1572872 | tf_op jit(solution)/shard_map/ppermute | solution.py:252
  113.2 3.5 %copy-start.10 = (s32[64,1]{0,1:T(1,128)S(1)}, s32[64,1]{0,1:T(1,128)}, u32[]{:S(2)}) copy-start(s32[64,1]{0,1:T(1,128)} %param.18) | copy-start | bytes 772
  114.2 9.2 %collective-permute-start.26 = (bf16[64,4096]{1,0:T(8,128)(2,1)S(1)}, bf16[64,4096]{1,0:T(8,128)(2,1)S(1)}, u32[]{:S(2)}, u32[]{:S(2)}) collective-permute-start(bf16[64,4096]{1,0:T(8,128)(2,1)S(1)} %add_convert_fusion.1), channel_id=1, source_target_pairs={{0,4},{1,3},{4,8},{5,1},{8,12},{9,5},{12,14},{13,9},{14,10},{15,13... | collective-permute-start | bytes 1572872 | tf_op jit(solution)/shard_map/ppermute | solution.py:252
  116.7 6.8 %copy-start.7 = (bf16[64,4096]{1,0:T(8,128)(2,1)S(1)}, bf16[64,4096]{1,0:T(8,128)(2,1)}, u32[]{:S(2)}) copy-start(bf16[64,4096]{1,0:T(8,128)(2,1)} %get-tuple-element.27) | copy-start | bytes 1572868
  (6 other events, 14.8 us)

commit v9 on v8

--- a/solution.py
+++ b/solution.py
@@ -21,6 +21,7 @@
 
 HEAD_GROUP = 16
 SUB_HEADS = 4
+SPLIT_HOPS = 2
 LOG2_SCALE = SCORE_SCALE * math.log2(math.e)
 
 
@@ -165,52 +166,61 @@
 
 
 def expert_kernel(
-    index_ref, hits_ref, gate_a, up_a, down_a, gate_hbm, up_hbm, down_hbm, *refs, hop, chips,
+    index_ref, gate_a, up_a, down_a, hits_hbm, gate_hbm, up_hbm, down_hbm, *refs, hop, chips,
+    pieces,
 ):
-    *rows_refs, out_ref, gate_b, up_b, down_b, sems = refs
+    *refs, hits_ref, gate_b, up_b, down_b, sems = refs
+    rows_refs, out_refs = refs[:-pieces], refs[-pieces:]
+    pairs = ((hits_hbm, hits_ref), (gate_hbm, gate_b), (up_hbm, up_b), (down_hbm, down_b))
     copies = [
-        pltpu.make_async_copy(there, here, sems.at[i])
-        for i, (there, here) in enumerate(((gate_hbm, gate_b), (up_hbm, up_b), (down_hbm, down_b)))
+        pltpu.make_async_copy(there, here, sems.at[i]) for i, (there, here) in enumerate(pairs)
     ]
     for copy in copies:
         copy.start()
     my_chip, my_core = index_ref[0] // CORES, lax.rem(index_ref[0], CORES)
     place = ring_place(my_chip, chips) + chips + hop * (2 * my_core - 1)
     source = ring_chip(lax.rem(place, chips), chips) ^ my_chip
-    column = lax.broadcasted_iota(jnp.int32, hits_ref.shape, 1)
-    keep = jnp.max(jnp.where(column == source, hits_ref[...], 0.0), axis=1, keepdims=True) > 0.0
     rows = jnp.concatenate([ref[...] for ref in rows_refs], axis=0)
 
     def hidden(gate_ref, up_ref):
         gate_act = jnp.dot(rows, gate_ref[...], preferred_element_type=jnp.float32)
         up_act = jnp.dot(rows, up_ref[...], preferred_element_type=jnp.float32)
-        act = gate_act * (1.0 / (1.0 + jnp.exp(-gate_act))) * up_act
+        return gate_act * (1.0 / (1.0 + jnp.exp(-gate_act))) * up_act
+
+    def kept(act):
         return jnp.where(keep, act, 0.0).astype(jnp.bfloat16)
 
-    part = jnp.dot(hidden(gate_a, up_a), down_a[...], preferred_element_type=jnp.float32)
+    act_a = hidden(gate_a, up_a)
     copies[0].wait()
+    column = lax.broadcasted_iota(jnp.int32, hits_ref.shape, 1)
+    keep = jnp.max(jnp.where(column == source, hits_ref[...], 0.0), axis=1, keepdims=True) > 0.0
+    part = jnp.dot(kept(act_a), down_a[...], preferred_element_type=jnp.float32)
     copies[1].wait()
-    hidden_b = hidden(gate_b, up_b)
     copies[2].wait()
-    out_ref[...] = part + jnp.dot(hidden_b, down_b[...], preferred_element_type=jnp.float32)
-
-
-def expert_part(my_index, rows, hits, own, swapped, hop, chips):
+    act_b = hidden(gate_b, up_b)
+    copies[3].wait()
+    part = part + jnp.dot(kept(act_b), down_b[...], preferred_element_type=jnp.float32)
+    size = part.shape[0] // pieces
+    for i, out_ref in enumerate(out_refs):
+        out_ref[...] = part[i * size : (i + 1) * size]
+
+
+def expert_part(my_index, rows, hits, own, swapped, hop, chips, pieces):
     tok, features = hits.shape[0], rows[0].shape[1]
     units = 2 * own[0].shape[1]
     vmem, anywhere = pl.BlockSpec(memory_space=pltpu.VMEM), pl.BlockSpec(memory_space=pl.ANY)
     return pl.pallas_call(
-        functools.partial(expert_kernel, hop=hop, chips=chips),
-        in_specs=[pl.BlockSpec(memory_space=pltpu.SMEM)] + [vmem] * 4 + [anywhere] * 3 + [vmem] * len(rows),
-        out_specs=vmem,
-        out_shape=jax.ShapeDtypeStruct((tok, features), jnp.float32),
-        scratch_shapes=[pltpu.VMEM(w.shape, w.dtype) for w in swapped]
-        + [pltpu.SemaphoreType.DMA((3,))],
+        functools.partial(expert_kernel, hop=hop, chips=chips, pieces=pieces),
+        in_specs=[pl.BlockSpec(memory_space=pltpu.SMEM)] + [vmem] * 3 + [anywhere] * 4 + [vmem] * len(rows),
+        out_specs=[vmem] * pieces,
+        out_shape=[jax.ShapeDtypeStruct((tok // pieces, features), jnp.float32)] * pieces,
+        scratch_shapes=[pltpu.VMEM(w.shape, w.dtype) for w in (hits, *swapped)]
+        + [pltpu.SemaphoreType.DMA((4,))],
         compiler_params=pltpu.CompilerParams(vmem_limit_bytes=24 << 20),
         cost_estimate=pl.CostEstimate(
             flops=6 * tok * features * units, bytes_accessed=14 << 20, transcendentals=0
         ),
-    )(my_index.reshape(1), hits, *own, *swapped, *rows)
+    )(my_index.reshape(1), *own, hits, *swapped, *rows)
 
 
 def local(
@@ -246,7 +256,8 @@
     start, swapped = lax.optimization_barrier(((upper, lower), swapped))
 
     def part_of(rows, hop):
-        return expert_part(my_index, rows, hits, own, swapped, hop, chips)
+        pieces = 1 if 0 < hop < chips - SPLIT_HOPS else 2
+        return expert_part(my_index, rows, hits, own, swapped, hop, chips, pieces)
 
     def move(blocks):
         return tuple(lax.ppermute(x, "ctx", route) for x in blocks)
@@ -258,15 +269,22 @@
     for hop in range(1, min(4, chips)):
         last = rows[-1]
         rows.append(move((jnp.concatenate(last, axis=0),) if hop == 3 else last))
-    sums = part_of(rows[1], 1).astype(jnp.bfloat16)
+    def added(part, arrived):
+        if len(part) > len(arrived):
+            arrived = (arrived[0][: tok // 2], arrived[0][tok // 2 :])
+        return tuple(x + y.astype(jnp.float32) for x, y in zip(part, arrived))
+
+    def rounded(part):
+        return tuple(x.astype(jnp.bfloat16) for x in part)
+
+    sums = rounded(part_of(rows[1], 1))
     for hop in range(1, chips):
-        (arrived,) = move((sums,))
+        arrived = move(sums)
         if hop + 3 < chips:
             rows.append(move(after(rows[hop + 2], sums)))
         if hop + 1 < chips:
-            part = part_of(rows[hop + 1], hop + 1)
-            sums = (part + arrived.astype(jnp.float32)).astype(jnp.bfloat16)
-    expert_out = part_of(after(start, sums), 0) + arrived.astype(jnp.float32)
+            sums = rounded(added(part_of(rows[hop + 1], hop + 1), arrived))
+    expert_out = jnp.concatenate(added(part_of(after(start, sums), 0), arrived), axis=0)
     gate_weight = gate_fixed.astype(jnp.float32) / 65536.0
     return (values.astype(jnp.float32) + gate_weight * expert_out).astype(jnp.bfloat16)
 

time: 125 us -> 124 us (level)
  waiting for transfers between devices: 30.9 us -> 28.1 us
  starting transfers between devices: 40 us -> 41.7 us
    ppermute x16 -> x18, waiting for transfers between devices: 24.3 us -> 21.4 us  [move(): return tuple((lax.ppermute(x, 'ctx', route) for x in blocks))]
    ppermute x16 -> x18, starting transfers between devices: 28 us -> 29.6 us  [move(): return tuple((lax.ppermute(x, 'ctx', route) for x in blocks))]
  transfers between devices with their start and end apart: 27 -> 29, of which waited for: 16 -> 15; matrix products, arithmetic and copies ran while one was open for 1% -> 1% of each run, Pallas kernels for 39% -> 40%
where the time goes in v9:
time: 124 us
  Pallas kernels  49 us (40%)
  starting transfers between devices  41.7 us (34%)
  waiting for transfers between devices  28.1 us (23%)
  other arithmetic  3.33 us (3%)
    pallas_call x8, Pallas kernels, expert_part(): pl.pallas_call(functools.partial(expert_kernel, hop=hop, chips=chips, pie...  37.5 us
    ppermute x18, starting transfers between devices, move(): return tuple((lax.ppermute(x, 'ctx', route) for x in blocks))  29.6 us
    ppermute x18, waiting for transfers between devices, move(): return tuple((lax.ppermute(x, 'ctx', route) for x in blocks))  21.4 us
    pallas_call x1, Pallas kernels, attention(): pl.pallas_call(functools.partial(attention_kernel, tok=tok), grid_spec=gr...  11.6 us
    ppermute x7, starting transfers between devices, from_chip(): lax.ppermute(block, 'ctx', [(i, i ^ step * CORES) for i in range(n_ctx)])  11.4 us
    ppermute x7, waiting for transfers between devices, from_chip(): lax.ppermute(block, 'ctx', [(i, i ^ step * CORES) for i in range(n_ctx)])  4.54 us
  transfers between devices with their start and end apart: 29, of which 15 were waited for; matrix products, arithmetic and copies ran while one was open for 1% of the time, Pallas kernels for 40%

profile of v9, /device:TPU:0, one launch (start us, length us, event | category | flops | bytes accessed | tf_op | source)
XLA Modules:
  0.0 123.6 jit_solution(1219740636426397738)
XLA Ops:
  1.7 4.1 %collective-permute-start.3 = (bf16[64,640]{1,0:T(8,128)(2,1)S(1)}, bf16[64,640]{1,0:T(8,128)(2,1)S(1)}, u32[]{:S(2)}, u32[]{:S(2)}) collective-permute-start(bf16[64,640]{1,0:T(8,128)(2,1)S(1)} %get-tuple-element.59), channel_id=1, source_target_pairs={{0,8},{1,9},{2,10},{3,11},{4,12},{5,13},{6,14},{7,15},{8,0},{9,1},... | collective-permute-start | bytes 245768 | tf_op jit(solution)/shard_map/ppermute | solution.py:241
  5.8 1.5 %collective-permute-start = (bf16[64,640]{1,0:T(8,128)(2,1)S(1)}, bf16[64,640]{1,0:T(8,128)(2,1)S(1)}, u32[]{:S(2)}, u32[]{:S(2)}) collective-permute-start(bf16[64,640]{1,0:T(8,128)(2,1)S(1)} %get-tuple-element.59), channel_id=1, source_target_pairs={{0,2},{1,3},{2,0},{3,1},{4,6},{5,7},{6,4},{7,5},{8,10},{9,11},{10,... | collective-permute-start | bytes 245768 | tf_op jit(solution)/shard_map/ppermute | solution.py:241
  7.3 1.6 %collective-permute-start.1 = (bf16[64,640]{1,0:T(8,128)(2,1)S(1)}, bf16[64,640]{1,0:T(8,128)(2,1)S(1)}, u32[]{:S(2)}, u32[]{:S(2)}) collective-permute-start(bf16[64,640]{1,0:T(8,128)(2,1)S(1)} %get-tuple-element.59), channel_id=1, source_target_pairs={{0,4},{1,5},{2,6},{3,7},{4,0},{5,1},{6,2},{7,3},{8,12},{9,13},{10,... | collective-permute-start | bytes 245768 | tf_op jit(solution)/shard_map/ppermute | solution.py:241
  9.8 1.6 %collective-permute-start.4 = (bf16[64,640]{1,0:T(8,128)(2,1)S(1)}, bf16[64,640]{1,0:T(8,128)(2,1)S(1)}, u32[]{:S(2)}, u32[]{:S(2)}) collective-permute-start(bf16[64,640]{1,0:T(8,128)(2,1)S(1)} %collective-permute-done.3), channel_id=1, source_target_pairs={{0,2},{1,3},{2,0},{3,1},{4,6},{5,7},{6,4},{7,5},{8,10},{9,11},{10,... | collective-permute-start | bytes 245768 | tf_op jit(solution)/shard_map/ppermute | solution.py:241
  15.9 1.8 %collective-permute-done.6 = bf16[64,640]{1,0:T(8,128)(2,1)S(1)} collective-permute-done((bf16[64,640]{1,0:T(8,128)(2,1)S(1)}, bf16[64,640]{1,0:T(8,128)(2,1)S(1)}, u32[]{:S(2)}, u32[]{:S(2)}) %collective-permute-start.6) | collective-permute-done | bytes 81952 | tf_op jit(solution)/shard_map/ppermute | solution.py:241
  17.8 2.1 %collective-permute-done.7.other_ref = bf16[512,640]{1,0:T(8,128)(2,1)S(1)} collective-permute-done((bf16[512,640]{1,0:T(8,128)(2,1)S(1)}, bf16[512,640]{1,0:T(8,128)(2,1)S(1)}, u32[]{:S(2)}, u32[]{:S(2)}) %collective-permute-start.7) | collective-permute-done | bytes 655392 | tf_op jit(solution)/shard_map/ppermute | solution.py:249
  20.7 11.6 %shard_map.109 = (bf16[64,4096]{1,0:T(8,128)(2,1)}, bf16[32,4096]{1,0:T(8,128)(2,1)}, bf16[32,4096]{1,0:T(8,128)(2,1)}, f32[64,8]{1,0:T(8,128)}) custom-call(s32[1]{0:T(128)} %bitcast.index_ref, bf16[64,16384]{1,0:T(8,128)(2,1)} %q_ref.1, bf16[64,2048]{1,0:T(8,128)(2,1)} %qr_ref.1, bf16[512,640]{1,0:T(8,128)(2,1)} %copy-done.8, bf16[512,640]{1,0:T(8,128)(2,1)} %copy-done.9, ...), custom_call_target="tpu_custom_call" | custom-call | flops 4831838208 | bytes 8388608 | tf_op jit(solution)/shard_map/pallas_call | solution.py:149
  33.5 2.7 %collective-permute-start.11 = (bf16[32,4096]{1,0:T(8,128)(2,1)}, bf16[32,4096]{1,0:T(8,128)(2,1)S(1)}, u32[]{:S(2)}, u32[]{:S(2)}) collective-permute-start(bf16[32,4096]{1,0:T(8,128)(2,1)} %get-tuple-element.53.refs_0_), channel_id=1, source_target_pairs={{0,4},{1,3},{4,8},{5,1},{8,12},{9,5},{12,14},{13,9},{14,10},{15,13... | collective-permute-start | bytes 786440 | tf_op jit(solution)/shard_map/ppermute | solution.py:263
  36.2 2.8 %collective-permute-done.13.refs_1_ = bf16[32,4096]{1,0:T(8,128)(2,1)S(1)} collective-permute-done((bf16[32,4096]{1,0:T(8,128)(2,1)}, bf16[32,4096]{1,0:T(8,128)(2,1)S(1)}, u32[]{:S(2)}, u32[]{:S(2)}) %collective-permute-start.13) | collective-permute-done | bytes 262176 | tf_op jit(solution)/shard_map/ppermute | solution.py:263
  39.0 1.5 %collective-permute-start.14 = (bf16[32,4096]{1,0:T(8,128)(2,1)S(1)}, bf16[32,4096]{1,0:T(8,128)(2,1)S(1)}, u32[]{:S(2)}, u32[]{:S(2)}) collective-permute-start(bf16[32,4096]{1,0:T(8,128)(2,1)S(1)} %collective-permute-done.13.refs_1_), channel_id=1, source_target_pairs={{0,4},{1,3},{4,8},{5,1},{8,12},{9,5},{12,14},{13,9},{14,10},{15,13... | collective-permute-start | bytes 786440 | tf_op jit(solution)/shard_map/ppermute | solution.py:263
  41.8 1.5 %collective-permute-start.12 = (bf16[32,4096]{1,0:T(8,128)(2,1)S(1)}, bf16[32,4096]{1,0:T(8,128)(2,1)S(1)}, u32[]{:S(2)}, u32[]{:S(2)}) collective-permute-start(bf16[32,4096]{1,0:T(8,128)(2,1)S(1)} %collective-permute-done.11.refs_0_), channel_id=1, source_target_pairs={{0,4},{1,3},{4,8},{5,1},{8,12},{9,5},{12,14},{13,9},{14,10},{15,13... | collective-permute-start | bytes 786440 | tf_op jit(solution)/shard_map/ppermute | solution.py:263
  44.0 4.7 %shard_map.110 = f32[64,4096]{1,0:T(8,128)S(1)} custom-call(s32[1]{0:T(128)} %bitcast.index_ref, bf16[4096,256]{1,0:T(8,128)(2,1)S(1)} %bitcast.10, bf16[4096,256]{1,0:T(8,128)(2,1)S(1)} %bitcast.19, bf16[256,4096]{1,0:T(8,128)(2,1)S(1)} %bitcast.28, f32[64,8]{1,0:T(8,128)S(1)} %copy-done.3, bf16[4096,256]{1,0:T(8,128)(2,1)} %collective-permute-done.8.gate_hbm, ...), custom_call_target="tpu_custom_call" | custom-call | flops 805306368 | bytes 14680064 | tf_op jit(solution)/shard_map/pallas_call | solution.py:212
  48.8 2.4 %collective-permute-start.17 = (bf16[64,4096]{1,0:T(8,128)(2,1)S(1)}, bf16[64,4096]{1,0:T(8,128)(2,1)S(1)}, u32[]{:S(2)}, u32[]{:S(2)}) collective-permute-start(bf16[64,4096]{1,0:T(8,128)(2,1)S(1)} %convert_element_type.72), channel_id=1, source_target_pairs={{0,4},{1,3},{4,8},{5,1},{8,12},{9,5},{12,14},{13,9},{14,10},{15,13... | collective-permute-start | bytes 1572872 | tf_op jit(solution)/shard_map/ppermute | solution.py:263
  51.7 4.7 %shard_map.111 = f32[64,4096]{1,0:T(8,128)S(1)} custom-call(s32[1]{0:T(128)} %bitcast.index_ref, bf16[4096,256]{1,0:T(8,128)(2,1)S(1)} %bitcast.11, bf16[4096,256]{1,0:T(8,128)(2,1)S(1)} %bitcast.20, bf16[256,4096]{1,0:T(8,128)(2,1)S(1)} %bitcast.29, f32[64,8]{1,0:T(8,128)S(1)} %copy-done.3, bf16[4096,256]{1,0:T(8,128)(2,1)} %collective-permute-done.8.gate_hbm, ...), custom_call_target="tpu_custom_call" | custom-call | flops 805306368 | bytes 14680064 | tf_op jit(solution)/shard_map/pallas_call | solution.py:212
  56.4 1.6 %collective-permute-done.17 = bf16[64,4096]{1,0:T(8,128)(2,1)S(1)} collective-permute-done((bf16[64,4096]{1,0:T(8,128)(2,1)S(1)}, bf16[64,4096]{1,0:T(8,128)(2,1)S(1)}, u32[]{:S(2)}, u32[]{:S(2)}) %collective-permute-start.17) | collective-permute-done | bytes 524320 | tf_op jit(solution)/shard_map/ppermute | solution.py:263
  58.1 2.4 %collective-permute-start.19 = (bf16[64,4096]{1,0:T(8,128)(2,1)S(1)}, bf16[64,4096]{1,0:T(8,128)(2,1)S(1)}, u32[]{:S(2)}, u32[]{:S(2)}) collective-permute-start(bf16[64,4096]{1,0:T(8,128)(2,1)S(1)} %add_convert_fusion.3), channel_id=1, source_target_pairs={{0,4},{1,3},{4,8},{5,1},{8,12},{9,5},{12,14},{13,9},{14,10},{15,13... | collective-permute-start | bytes 1572872 | tf_op jit(solution)/shard_map/ppermute | solution.py:263
  60.5 3.1 %collective-permute-done.15.refs_0_ = bf16[64,4096]{1,0:T(8,128)(2,1)S(1)} collective-permute-done((bf16[64,4096]{1,0:T(8,128)(2,1)S(1)}, bf16[64,4096]{1,0:T(8,128)(2,1)S(1)}, u32[]{:S(2)}, u32[]{:S(2)}) %collective-permute-start.15) | collective-permute-done | bytes 524320 | tf_op jit(solution)/shard_map/ppermute | solution.py:263
  63.6 2.4 %collective-permute-start.16 = (bf16[64,4096]{1,0:T(8,128)(2,1)S(1)}, bf16[64,4096]{1,0:T(8,128)(2,1)S(1)}, u32[]{:S(2)}, u32[]{:S(2)}) collective-permute-start(bf16[64,4096]{1,0:T(8,128)(2,1)S(1)} %collective-permute-done.15.refs_0_), channel_id=1, source_target_pairs={{0,4},{1,3},{4,8},{5,1},{8,12},{9,5},{12,14},{13,9},{14,10},{15,13... | collective-permute-start | bytes 1572872 | tf_op jit(solution)/shard_map/ppermute | solution.py:263
  66.0 4.7 %shard_map.112 = f32[64,4096]{1,0:T(8,128)S(1)} custom-call(s32[1]{0:T(128)} %bitcast.index_ref, bf16[4096,256]{1,0:T(8,128)(2,1)S(1)} %bitcast.12, bf16[4096,256]{1,0:T(8,128)(2,1)S(1)} %bitcast.21, bf16[256,4096]{1,0:T(8,128)(2,1)S(1)} %bitcast.30, f32[64,8]{1,0:T(8,128)S(1)} %copy-done.3, bf16[4096,256]{1,0:T(8,128)(2,1)} %collective-permute-done.8.gate_hbm, ...), custom_call_target="tpu_custom_call" | custom-call | flops 805306368 | bytes 14680064 | tf_op jit(solution)/shard_map/pallas_call | solution.py:212
  71.8 3.1 %collective-permute-done.16.refs_0_ = bf16[64,4096]{1,0:T(8,128)(2,1)S(1)} collective-permute-done((bf16[64,4096]{1,0:T(8,128)(2,1)S(1)}, bf16[64,4096]{1,0:T(8,128)(2,1)S(1)}, u32[]{:S(2)}, u32[]{:S(2)}) %collective-permute-start.16) | collective-permute-done | bytes 524320 | tf_op jit(solution)/shard_map/ppermute | solution.py:263
  74.8 2.4 %collective-permute-start.18 = (bf16[64,4096]{1,0:T(8,128)(2,1)S(1)}, bf16[64,4096]{1,0:T(8,128)(2,1)S(1)}, u32[]{:S(2)}, u32[]{:S(2)}) collective-permute-start(bf16[64,4096]{1,0:T(8,128)(2,1)S(1)} %collective-permute-done.16.refs_0_), channel_id=1, source_target_pairs={{0,4},{1,3},{4,8},{5,1},{8,12},{9,5},{12,14},{13,9},{14,10},{15,13... | collective-permute-start | bytes 1572872 | tf_op jit(solution)/shard_map/ppermute | solution.py:263
  77.2 4.7 %shard_map.113 = f32[64,4096]{1,0:T(8,128)S(1)} custom-call(s32[1]{0:T(128)} %bitcast.index_ref, bf16[4096,256]{1,0:T(8,128)(2,1)S(1)} %bitcast.13, bf16[4096,256]{1,0:T(8,128)(2,1)S(1)} %bitcast.22, bf16[256,4096]{1,0:T(8,128)(2,1)S(1)} %bitcast.31, f32[64,8]{1,0:T(8,128)S(1)} %copy-done.3, bf16[4096,256]{1,0:T(8,128)(2,1)} %collective-permute-done.8.gate_hbm, ...), custom_call_target="tpu_custom_call" | custom-call | flops 805306368 | bytes 14680064 | tf_op jit(solution)/shard_map/pallas_call | solution.py:212
  83.0 3.1 %collective-permute-done.18.refs_0_ = bf16[64,4096]{1,0:T(8,128)(2,1)S(1)} collective-permute-done((bf16[64,4096]{1,0:T(8,128)(2,1)S(1)}, bf16[64,4096]{1,0:T(8,128)(2,1)S(1)}, u32[]{:S(2)}, u32[]{:S(2)}) %collective-permute-start.18) | collective-permute-done | bytes 524320 | tf_op jit(solution)/shard_map/ppermute | solution.py:263
  86.1 2.4 %collective-permute-start.20 = (bf16[64,4096]{1,0:T(8,128)(2,1)S(1)}, bf16[64,4096]{1,0:T(8,128)(2,1)S(1)}, u32[]{:S(2)}, u32[]{:S(2)}) collective-permute-start(bf16[64,4096]{1,0:T(8,128)(2,1)S(1)} %collective-permute-done.18.refs_0_), channel_id=1, source_target_pairs={{0,4},{1,3},{4,8},{5,1},{8,12},{9,5},{12,14},{13,9},{14,10},{15,13... | collective-permute-start | bytes 1572872 | tf_op jit(solution)/shard_map/ppermute | solution.py:263
  88.5 4.7 %shard_map.116 = f32[64,4096]{1,0:T(8,128)S(1)} custom-call(s32[1]{0:T(128)} %bitcast.index_ref, bf16[4096,256]{1,0:T(8,128)(2,1)S(1)} %bitcast.14, bf16[4096,256]{1,0:T(8,128)(2,1)S(1)} %bitcast.23, bf16[256,4096]{1,0:T(8,128)(2,1)S(1)} %bitcast.32, f32[64,8]{1,0:T(8,128)S(1)} %copy-done.3, bf16[4096,256]{1,0:T(8,128)(2,1)} %collective-permute-done.8.gate_hbm, ...), custom_call_target="tpu_custom_call" | custom-call | flops 805306368 | bytes 14680064 | tf_op jit(solution)/shard_map/pallas_call | solution.py:212
  94.2 3.1 %collective-permute-done.20.refs_0_ = bf16[64,4096]{1,0:T(8,128)(2,1)S(1)} collective-permute-done((bf16[64,4096]{1,0:T(8,128)(2,1)S(1)}, bf16[64,4096]{1,0:T(8,128)(2,1)S(1)}, u32[]{:S(2)}, u32[]{:S(2)}) %collective-permute-start.20) | collective-permute-done | bytes 524320 | tf_op jit(solution)/shard_map/ppermute | solution.py:263
  97.3 2.4 %collective-permute-start.22 = (bf16[64,4096]{1,0:T(8,128)(2,1)S(1)}, bf16[64,4096]{1,0:T(8,128)(2,1)S(1)}, u32[]{:S(2)}, u32[]{:S(2)}) collective-permute-start(bf16[64,4096]{1,0:T(8,128)(2,1)S(1)} %collective-permute-done.20.refs_0_), channel_id=1, source_target_pairs={{0,4},{1,3},{4,8},{5,1},{8,12},{9,5},{12,14},{13,9},{14,10},{15,13... | collective-permute-start | bytes 1572872 | tf_op jit(solution)/shard_map/ppermute | solution.py:263
  99.7 4.7 %shard_map.115 = (f32[32,4096]{1,0:T(8,128)S(1)}, f32[32,4096]{1,0:T(8,128)S(1)}) custom-call(s32[1]{0:T(128)} %bitcast.index_ref, bf16[4096,256]{1,0:T(8,128)(2,1)S(1)} %bitcast.15, bf16[4096,256]{1,0:T(8,128)(2,1)S(1)} %bitcast.24, bf16[256,4096]{1,0:T(8,128)(2,1)S(1)} %bitcast.33, f32[64,8]{1,0:T(8,128)S(1)} %copy-done.3, ...), custom_call_target="tpu_custom_call" | custom-call | flops 805306368 | bytes 14680064 | tf_op jit(solution)/shard_map/pallas_call | solution.py:212
  106.4 2.2 %collective-permute-done.22.refs_0_ = bf16[64,4096]{1,0:T(8,128)(2,1)S(1)} collective-permute-done((bf16[64,4096]{1,0:T(8,128)(2,1)S(1)}, bf16[64,4096]{1,0:T(8,128)(2,1)S(1)}, u32[]{:S(2)}, u32[]{:S(2)}) %collective-permute-start.22) | collective-permute-done | bytes 524320 | tf_op jit(solution)/shard_map/ppermute | solution.py:263
  108.6 4.7 %shard_map.114 = (f32[32,4096]{1,0:T(8,128)S(1)}, f32[32,4096]{1,0:T(8,128)S(1)}) custom-call(s32[1]{0:T(128)} %bitcast.index_ref, bf16[4096,256]{1,0:T(8,128)(2,1)S(1)} %bitcast.16, bf16[4096,256]{1,0:T(8,128)(2,1)S(1)} %bitcast.25, bf16[256,4096]{1,0:T(8,128)(2,1)S(1)} %bitcast.34, f32[64,8]{1,0:T(8,128)S(1)} %copy-done.3, ...), custom_call_target="tpu_custom_call" | custom-call | flops 805306368 | bytes 14680064 | tf_op jit(solution)/shard_map/pallas_call | solution.py:212
  113.3 2.4 %collective-permute-start.28 = (bf16[32,4096]{1,0:T(8,128)(2,1)S(1)}, bf16[32,4096]{1,0:T(8,128)(2,1)S(1)}, u32[]{:S(2)}, u32[]{:S(2)}) collective-permute-start(bf16[32,4096]{1,0:T(8,128)(2,1)S(1)} %add_convert_fusion.4), channel_id=1, source_target_pairs={{0,4},{1,3},{4,8},{5,1},{8,12},{9,5},{12,14},{13,9},{14,10},{15,13... | collective-permute-start | bytes 786440 | tf_op jit(solution)/shard_map/ppermute | solution.py:263
  116.7 4.7 %shard_map.117 = (f32[32,4096]{1,0:T(8,128)S(1)}, f32[32,4096]{1,0:T(8,128)S(1)}) custom-call(s32[1]{0:T(128)} %bitcast.index_ref, bf16[4096,256]{1,0:T(8,128)(2,1)S(1)} %bitcast.17, bf16[4096,256]{1,0:T(8,128)(2,1)S(1)} %bitcast.26, bf16[256,4096]{1,0:T(8,128)(2,1)S(1)} %bitcast.35, f32[64,8]{1,0:T(8,128)S(1)} %copy-done.4, ...), custom_call_target="tpu_custom_call" | custom-call | flops 805306368 | bytes 14680064 | tf_op jit(solution)/shard_map/pallas_call | solution.py:212
  (80 shorter events, 20.2 us)
Async XLA Ops:
  1.7 8.1 %collective-permute-start.3 = (bf16[64,640]{1,0:T(8,128)(2,1)S(1)}, bf16[64,640]{1,0:T(8,128)(2,1)S(1)}, u32[]{:S(2)}, u32[]{:S(2)}) collective-permute-start(bf16[64,640]{1,0:T(8,128)(2,1)S(1)} %get-tuple-element.59), channel_id=1, source_target_pairs={{0,8},{1,9},{2,10},{3,11},{4,12},{5,13},{6,14},{7,15},{8,0},{9,1},... | collective-permute-start | bytes 245768 | tf_op jit(solution)/shard_map/ppermute | solution.py:241
  5.8 6.6 %collective-permute-start = (bf16[64,640]{1,0:T(8,128)(2,1)S(1)}, bf16[64,640]{1,0:T(8,128)(2,1)S(1)}, u32[]{:S(2)}, u32[]{:S(2)}) collective-permute-start(bf16[64,640]{1,0:T(8,128)(2,1)S(1)} %get-tuple-element.59), channel_id=1, source_target_pairs={{0,2},{1,3},{2,0},{3,1},{4,6},{5,7},{6,4},{7,5},{8,10},{9,11},{10,... | collective-permute-start | bytes 245768 | tf_op jit(solution)/shard_map/ppermute | solution.py:241
  7.3 6.3 %collective-permute-start.1 = (bf16[64,640]{1,0:T(8,128)(2,1)S(1)}, bf16[64,640]{1,0:T(8,128)(2,1)S(1)}, u32[]{:S(2)}, u32[]{:S(2)}) collective-permute-start(bf16[64,640]{1,0:T(8,128)(2,1)S(1)} %get-tuple-element.59), channel_id=1, source_target_pairs={{0,4},{1,5},{2,6},{3,7},{4,0},{5,1},{6,2},{7,3},{8,12},{9,13},{10,... | collective-permute-start | bytes 245768 | tf_op jit(solution)/shard_map/ppermute | solution.py:241
  8.9 5.6 %collective-permute-start.2 = (bf16[64,640]{1,0:T(8,128)(2,1)S(1)}, bf16[64,640]{1,0:T(8,128)(2,1)S(1)}, u32[]{:S(2)}, u32[]{:S(2)}) collective-permute-start(bf16[64,640]{1,0:T(8,128)(2,1)S(1)} %get-tuple-element.59), channel_id=1, source_target_pairs={{0,6},{1,7},{2,4},{3,5},{4,2},{5,3},{6,0},{7,1},{8,14},{9,15},{10,... | collective-permute-start | bytes 245768 | tf_op jit(solution)/shard_map/ppermute | solution.py:241
  9.8 5.5 %collective-permute-start.4 = (bf16[64,640]{1,0:T(8,128)(2,1)S(1)}, bf16[64,640]{1,0:T(8,128)(2,1)S(1)}, u32[]{:S(2)}, u32[]{:S(2)}) collective-permute-start(bf16[64,640]{1,0:T(8,128)(2,1)S(1)} %collective-permute-done.3), channel_id=1, source_target_pairs={{0,2},{1,3},{2,0},{3,1},{4,6},{5,7},{6,4},{7,5},{8,10},{9,11},{10,... | collective-permute-start | bytes 245768 | tf_op jit(solution)/shard_map/ppermute | solution.py:241
  11.4 4.5 %collective-permute-start.5 = (bf16[64,640]{1,0:T(8,128)(2,1)S(1)}, bf16[64,640]{1,0:T(8,128)(2,1)S(1)}, u32[]{:S(2)}, u32[]{:S(2)}) collective-permute-start(bf16[64,640]{1,0:T(8,128)(2,1)S(1)} %collective-permute-done.3), channel_id=1, source_target_pairs={{0,4},{1,5},{2,6},{3,7},{4,0},{5,1},{6,2},{7,3},{8,12},{9,13},{10,... | collective-permute-start | bytes 245768 | tf_op jit(solution)/shard_map/ppermute | solution.py:241
  12.4 5.3 %collective-permute-start.6 = (bf16[64,640]{1,0:T(8,128)(2,1)S(1)}, bf16[64,640]{1,0:T(8,128)(2,1)S(1)}, u32[]{:S(2)}, u32[]{:S(2)}) collective-permute-start(bf16[64,640]{1,0:T(8,128)(2,1)S(1)} %collective-permute-done.3), channel_id=1, source_target_pairs={{0,6},{1,7},{2,4},{3,5},{4,2},{5,3},{6,0},{7,1},{8,14},{9,15},{10,... | collective-permute-start | bytes 245768 | tf_op jit(solution)/shard_map/ppermute | solution.py:241
  17.7 2.2 %collective-permute-start.7 = (bf16[512,640]{1,0:T(8,128)(2,1)S(1)}, bf16[512,640]{1,0:T(8,128)(2,1)S(1)}, u32[]{:S(2)}, u32[]{:S(2)}) collective-permute-start(bf16[512,640]{1,0:T(8,128)(2,1)S(1)} %constant_dynamic-update-slice_fusion.mine_ref), channel_id=1, source_target_pairs={{0,1},{1,0},{2,3},{3,2},{4,5},{5,4},{6,7},{7,6},{8,9},{9,8},{10,11... | collective-permute-start | bytes 1966088 | tf_op jit(solution)/shard_map/ppermute | solution.py:249
  19.9 12.4 %collective-permute-start.8 = (bf16[4096,256]{1,0:T(8,128)(2,1)}, bf16[4096,256]{1,0:T(8,128)(2,1)}, u32[]{:S(2)}, u32[]{:S(2)}) collective-permute-start(bf16[4096,256]{1,0:T(8,128)(2,1)} %bitcast.9), channel_id=1, source_target_pairs={{0,1},{1,0},{2,3},{3,2},{4,5},{5,4},{6,7},{7,6},{8,9},{9,8},{10,11... | collective-permute-start | bytes 6291464 | tf_op jit(solution)/shard_map/ppermute | solution.py:252
  20.0 12.3 %collective-permute-start.9 = (bf16[4096,256]{1,0:T(8,128)(2,1)}, bf16[4096,256]{1,0:T(8,128)(2,1)}, u32[]{:S(2)}, u32[]{:S(2)}) collective-permute-start(bf16[4096,256]{1,0:T(8,128)(2,1)} %bitcast.18), channel_id=1, source_target_pairs={{0,1},{1,0},{2,3},{3,2},{4,5},{5,4},{6,7},{7,6},{8,9},{9,8},{10,11... | collective-permute-start | bytes 6291464 | tf_op jit(solution)/shard_map/ppermute | solution.py:252
  20.4 11.9 %collective-permute-start.10 = (bf16[256,4096]{1,0:T(8,128)(2,1)}, bf16[256,4096]{1,0:T(8,128)(2,1)}, u32[]{:S(2)}, u32[]{:S(2)}) collective-permute-start(bf16[256,4096]{1,0:T(8,128)(2,1)} %bitcast.27), channel_id=1, source_target_pairs={{0,1},{1,0},{2,3},{3,2},{4,5},{5,4},{6,7},{7,6},{8,9},{9,8},{10,11... | collective-permute-start | bytes 6291464 | tf_op jit(solution)/shard_map/ppermute | solution.py:252
  20.7 22.5 %copy-start = (bf16[1,4096,256]{2,1,0:T(8,128)(2,1)S(1)}, bf16[1,4096,256]{2,1,0:T(8,128)(2,1)}, u32[]{:S(2)}) copy-start(bf16[1,4096,256]{2,1,0:T(8,128)(2,1)} %param.19) | copy-start | bytes 6291460
  20.7 22.5 %copy-start.1 = (bf16[1,4096,256]{2,1,0:T(8,128)(2,1)S(1)}, bf16[1,4096,256]{2,1,0:T(8,128)(2,1)}, u32[]{:S(2)}) copy-start(bf16[1,4096,256]{2,1,0:T(8,128)(2,1)} %param.20) | copy-start | bytes 6291460
  20.7 22.5 %copy-start.2 = (bf16[1,256,4096]{2,1,0:T(8,128)(2,1)S(1)}, bf16[1,256,4096]{2,1,0:T(8,128)(2,1)}, u32[]{:S(2)}) copy-start(bf16[1,256,4096]{2,1,0:T(8,128)(2,1)} %param.21) | copy-start | bytes 6291460
  32.3 6.6 %collective-permute-start.13 = (bf16[32,4096]{1,0:T(8,128)(2,1)}, bf16[32,4096]{1,0:T(8,128)(2,1)S(1)}, u32[]{:S(2)}, u32[]{:S(2)}) collective-permute-start(bf16[32,4096]{1,0:T(8,128)(2,1)} %get-tuple-element.54.refs_1_), channel_id=1, source_target_pairs={{0,4},{1,3},{4,8},{5,1},{8,12},{9,5},{12,14},{13,9},{14,10},{15,13... | collective-permute-start | bytes 786440 | tf_op jit(solution)/shard_map/ppermute | solution.py:263
  33.5 8.3 %collective-permute-start.11 = (bf16[32,4096]{1,0:T(8,128)(2,1)}, bf16[32,4096]{1,0:T(8,128)(2,1)S(1)}, u32[]{:S(2)}, u32[]{:S(2)}) collective-permute-start(bf16[32,4096]{1,0:T(8,128)(2,1)} %get-tuple-element.53.refs_0_), channel_id=1, source_target_pairs={{0,4},{1,3},{4,8},{5,1},{8,12},{9,5},{12,14},{13,9},{14,10},{15,13... | collective-permute-start | bytes 786440 | tf_op jit(solution)/shard_map/ppermute | solution.py:263
  39.0 12.2 %collective-permute-start.14 = (bf16[32,4096]{1,0:T(8,128)(2,1)S(1)}, bf16[32,4096]{1,0:T(8,128)(2,1)S(1)}, u32[]{:S(2)}, u32[]{:S(2)}) collective-permute-start(bf16[32,4096]{1,0:T(8,128)(2,1)S(1)} %collective-permute-done.13.refs_1_), channel_id=1, source_target_pairs={{0,4},{1,3},{4,8},{5,1},{8,12},{9,5},{12,14},{13,9},{14,10},{15,13... | collective-permute-start | bytes 786440 | tf_op jit(solution)/shard_map/ppermute | solution.py:263
  41.8 9.4 %collective-permute-start.12 = (bf16[32,4096]{1,0:T(8,128)(2,1)S(1)}, bf16[32,4096]{1,0:T(8,128)(2,1)S(1)}, u32[]{:S(2)}, u32[]{:S(2)}) collective-permute-start(bf16[32,4096]{1,0:T(8,128)(2,1)S(1)} %collective-permute-done.11.refs_0_), channel_id=1, source_target_pairs={{0,4},{1,3},{4,8},{5,1},{8,12},{9,5},{12,14},{13,9},{14,10},{15,13... | collective-permute-start | bytes 786440 | tf_op jit(solution)/shard_map/ppermute | solution.py:263
  48.8 9.2 %collective-permute-start.17 = (bf16[64,4096]{1,0:T(8,128)(2,1)S(1)}, bf16[64,4096]{1,0:T(8,128)(2,1)S(1)}, u32[]{:S(2)}, u32[]{:S(2)}) collective-permute-start(bf16[64,4096]{1,0:T(8,128)(2,1)S(1)} %convert_element_type.72), channel_id=1, source_target_pairs={{0,4},{1,3},{4,8},{5,1},{8,12},{9,5},{12,14},{13,9},{14,10},{15,13... | collective-permute-start | bytes 1572872 | tf_op jit(solution)/shard_map/ppermute | solution.py:263
  51.2 12.4 %collective-permute-start.15 = (bf16[64,4096]{1,0:T(8,128)(2,1)S(1)}, bf16[64,4096]{1,0:T(8,128)(2,1)S(1)}, u32[]{:S(2)}, u32[]{:S(2)}) collective-permute-start(bf16[64,4096]{1,0:T(8,128)(2,1)S(1)} %pad_maximum_fusion), channel_id=1, source_target_pairs={{0,4},{1,3},{4,8},{5,1},{8,12},{9,5},{12,14},{13,9},{14,10},{15,13... | collective-permute-start | bytes 1572872 | tf_op jit(solution)/shard_map/ppermute | solution.py:263
  58.1 12.6 %collective-permute-start.19 = (bf16[64,4096]{1,0:T(8,128)(2,1)S(1)}, bf16[64,4096]{1,0:T(8,128)(2,1)S(1)}, u32[]{:S(2)}, u32[]{:S(2)}) collective-permute-start(bf16[64,4096]{1,0:T(8,128)(2,1)S(1)} %add_convert_fusion.3), channel_id=1, source_target_pairs={{0,4},{1,3},{4,8},{5,1},{8,12},{9,5},{12,14},{13,9},{14,10},{15,13... | collective-permute-start | bytes 1572872 | tf_op jit(solution)/shard_map/ppermute | solution.py:263
  63.6 11.2 %collective-permute-start.16 = (bf16[64,4096]{1,0:T(8,128)(2,1)S(1)}, bf16[64,4096]{1,0:T(8,128)(2,1)S(1)}, u32[]{:S(2)}, u32[]{:S(2)}) collective-permute-start(bf16[64,4096]{1,0:T(8,128)(2,1)S(1)} %collective-permute-done.15.refs_0_), channel_id=1, source_target_pairs={{0,4},{1,3},{4,8},{5,1},{8,12},{9,5},{12,14},{13,9},{14,10},{15,13... | collective-permute-start | bytes 1572872 | tf_op jit(solution)/shard_map/ppermute | solution.py:263
  70.8 11.1 %collective-permute-start.21 = (bf16[64,4096]{1,0:T(8,128)(2,1)S(1)}, bf16[64,4096]{1,0:T(8,128)(2,1)S(1)}, u32[]{:S(2)}, u32[]{:S(2)}) collective-permute-start(bf16[64,4096]{1,0:T(8,128)(2,1)S(1)} %add_convert_fusion.2), channel_id=1, source_target_pairs={{0,4},{1,3},{4,8},{5,1},{8,12},{9,5},{12,14},{13,9},{14,10},{15,13... | collective-permute-start | bytes 1572872 | tf_op jit(solution)/shard_map/ppermute | solution.py:263
  74.8 11.2 %collective-permute-start.18 = (bf16[64,4096]{1,0:T(8,128)(2,1)S(1)}, bf16[64,4096]{1,0:T(8,128)(2,1)S(1)}, u32[]{:S(2)}, u32[]{:S(2)}) collective-permute-start(bf16[64,4096]{1,0:T(8,128)(2,1)S(1)} %collective-permute-done.16.refs_0_), channel_id=1, source_target_pairs={{0,4},{1,3},{4,8},{5,1},{8,12},{9,5},{12,14},{13,9},{14,10},{15,13... | collective-permute-start | bytes 1572872 | tf_op jit(solution)/shard_map/ppermute | solution.py:263
  82.0 11.1 %collective-permute-start.23 = (bf16[64,4096]{1,0:T(8,128)(2,1)S(1)}, bf16[64,4096]{1,0:T(8,128)(2,1)S(1)}, u32[]{:S(2)}, u32[]{:S(2)}) collective-permute-start(bf16[64,4096]{1,0:T(8,128)(2,1)S(1)} %add_convert_fusion.1), channel_id=1, source_target_pairs={{0,4},{1,3},{4,8},{5,1},{8,12},{9,5},{12,14},{13,9},{14,10},{15,13... | collective-permute-start | bytes 1572872 | tf_op jit(solution)/shard_map/ppermute | solution.py:263
  86.1 11.2 %collective-permute-start.20 = (bf16[64,4096]{1,0:T(8,128)(2,1)S(1)}, bf16[64,4096]{1,0:T(8,128)(2,1)S(1)}, u32[]{:S(2)}, u32[]{:S(2)}) collective-permute-start(bf16[64,4096]{1,0:T(8,128)(2,1)S(1)} %collective-permute-done.18.refs_0_), channel_id=1, source_target_pairs={{0,4},{1,3},{4,8},{5,1},{8,12},{9,5},{12,14},{13,9},{14,10},{15,13... | collective-permute-start | bytes 1572872 | tf_op jit(solution)/shard_map/ppermute | solution.py:263
  93.3 11.1 %collective-permute-start.24 = (bf16[64,4096]{1,0:T(8,128)(2,1)S(1)}, bf16[64,4096]{1,0:T(8,128)(2,1)S(1)}, u32[]{:S(2)}, u32[]{:S(2)}) collective-permute-start(bf16[64,4096]{1,0:T(8,128)(2,1)S(1)} %add_convert_fusion), channel_id=1, source_target_pairs={{0,4},{1,3},{4,8},{5,1},{8,12},{9,5},{12,14},{13,9},{14,10},{15,13... | collective-permute-start | bytes 1572872 | tf_op jit(solution)/shard_map/ppermute | solution.py:263
  97.3 11.2 %collective-permute-start.22 = (bf16[64,4096]{1,0:T(8,128)(2,1)S(1)}, bf16[64,4096]{1,0:T(8,128)(2,1)S(1)}, u32[]{:S(2)}, u32[]{:S(2)}) collective-permute-start(bf16[64,4096]{1,0:T(8,128)(2,1)S(1)} %collective-permute-done.20.refs_0_), channel_id=1, source_target_pairs={{0,4},{1,3},{4,8},{5,1},{8,12},{9,5},{12,14},{13,9},{14,10},{15,13... | collective-permute-start | bytes 1572872 | tf_op jit(solution)/shard_map/ppermute | solution.py:263
  104.5 8.8 %collective-permute-start.26 = (bf16[32,4096]{1,0:T(8,128)(2,1)S(1)}, bf16[32,4096]{1,0:T(8,128)(2,1)S(1)}, u32[]{:S(2)}, u32[]{:S(2)}) collective-permute-start(bf16[32,4096]{1,0:T(8,128)(2,1)S(1)} %get-tuple-element.57), channel_id=1, source_target_pairs={{0,4},{1,3},{4,8},{5,1},{8,12},{9,5},{12,14},{13,9},{14,10},{15,13... | collective-permute-start | bytes 786440 | tf_op jit(solution)/shard_map/ppermute | solution.py:263
  105.5 10.3 %collective-permute-start.25 = (bf16[32,4096]{1,0:T(8,128)(2,1)S(1)}, bf16[32,4096]{1,0:T(8,128)(2,1)S(1)}, u32[]{:S(2)}, u32[]{:S(2)}) collective-permute-start(bf16[32,4096]{1,0:T(8,128)(2,1)S(1)} %get-tuple-element.58), channel_id=1, source_target_pairs={{0,4},{1,3},{4,8},{5,1},{8,12},{9,5},{12,14},{13,9},{14,10},{15,13... | collective-permute-start | bytes 786440 | tf_op jit(solution)/shard_map/ppermute | solution.py:263
  113.3 8.1 %collective-permute-start.28 = (bf16[32,4096]{1,0:T(8,128)(2,1)S(1)}, bf16[32,4096]{1,0:T(8,128)(2,1)S(1)}, u32[]{:S(2)}, u32[]{:S(2)}) collective-permute-start(bf16[32,4096]{1,0:T(8,128)(2,1)S(1)} %add_convert_fusion.4), channel_id=1, source_target_pairs={{0,4},{1,3},{4,8},{5,1},{8,12},{9,5},{12,14},{13,9},{14,10},{15,13... | collective-permute-start | bytes 786440 | tf_op jit(solution)/shard_map/ppermute | solution.py:263
  115.8 6.8 %collective-permute-start.27 = (bf16[32,4096]{1,0:T(8,128)(2,1)S(1)}, bf16[32,4096]{1,0:T(8,128)(2,1)S(1)}, u32[]{:S(2)}, u32[]{:S(2)}) collective-permute-start(bf16[32,4096]{1,0:T(8,128)(2,1)S(1)} %add_convert_fusion.6), channel_id=1, source_target_pairs={{0,4},{1,3},{4,8},{5,1},{8,12},{9,5},{12,14},{13,9},{14,10},{15,13... | collective-permute-start | bytes 786440 | tf_op jit(solution)/shard_map/ppermute | solution.py:263
  (8 other events, 17.0 us)

commit v10 on v9

--- a/solution.py
+++ b/solution.py
@@ -19,51 +19,47 @@
 NORM_EPS = 1e-06
 NEG_FILL = -1e30
 
-HEAD_GROUP = 16
 SUB_HEADS = 4
 SPLIT_HOPS = 2
 LOG2_SCALE = SCORE_SCALE * math.log2(math.e)
 
 
 def attention_kernel(
-    index_ref, q_ref, qr_ref, mine_ref, other_ref, wv_ref, gain_ref, values_ref, up_ref,
-    down_ref, hits_ref, stack_ref, bias_a_ref, bias_b_ref, *, tok,
+    index_ref, mine_hbm, other_hbm, q_hbm, qr_hbm, wv_hbm, gain_ref, values_ref, up_ref, down_ref,
+    hits_ref, mine_ref, other_ref, q_ref, qr_ref, wv_ref, stack_ref, bias_a_ref, bias_b_ref,
+    sems, *, tok,
 ):
-    group = pl.program_id(0)
+    copies = []
+
+    def fetch(there, here):
+        copies.append(pltpu.make_async_copy(there, here, sems.at[len(copies)]))
+        copies[-1].start()
+        return copies[-1]
+
+    subs = HEADS // SUB_HEADS
+    lanes = [pl.ds(sub * SUB_HEADS * LAT, SUB_HEADS * LAT) for sub in range(subs)]
+    heads = [pl.ds(sub * SUB_HEADS, SUB_HEADS) for sub in range(subs)]
+    q_copies = [fetch(q_hbm.at[:, lanes[0]], q_ref.at[:, lanes[0]])]
+    first_copies = [fetch(qr_hbm, qr_ref), fetch(mine_hbm, mine_ref), fetch(other_hbm, other_ref)]
+    wv_copies = []
+    for sub in range(subs):
+        if sub:
+            q_copies.append(fetch(q_hbm.at[:, lanes[sub]], q_ref.at[:, lanes[sub]]))
+        wv_copies.append(fetch(wv_hbm.at[heads[sub]], wv_ref.at[heads[sub]]))
     my_index = index_ref[0]
     my_chip, my_core = my_index // CORES, lax.rem(my_index, CORES)
     keys = mine_ref.shape[0]
 
-    @pl.when(group == 0)
-    def _():
-        row_pos = my_index * tok + lax.broadcasted_iota(jnp.int32, (tok, keys), 0)
-        key_iota = lax.broadcasted_iota(jnp.int32, (tok, keys), 1)
-        key_chip = (key_iota // tok) ^ my_chip
-        key_tok = lax.rem(key_iota, jnp.int32(tok))
-        for core, bias_ref in ((my_core, bias_a_ref), (1 - my_core, bias_b_ref)):
-            key_pos = (key_chip * CORES + core) * tok + key_tok
-            bias_ref[...] = jnp.where(key_pos <= row_pos, 0.0, NEG_FILL)
-        last = mine_ref[:, LAT : LAT + 2 * ROPE].astype(jnp.float32)
-        lane = lax.broadcasted_iota(jnp.int32, last.shape, 1)
-        named = jnp.max(jnp.where(lane >= ROPE, last, -1.0), axis=1, keepdims=True)
-        my_expert = (my_index // SPAN).astype(jnp.float32)
-        hits = jnp.where(named == my_expert, 1.0, 0.0)
-        column = lax.broadcasted_iota(jnp.int32, hits_ref.shape, 1)
-        table = jnp.zeros(hits_ref.shape, jnp.float32)
-        for place in range(keys // tok):
-            table = jnp.where(column == place, hits[place * tok : (place + 1) * tok], table)
-        hits_ref[...] = table
-
+    row_pos = my_index * tok + lax.broadcasted_iota(jnp.int32, (tok, keys), 0)
+    key_iota = lax.broadcasted_iota(jnp.int32, (tok, keys), 1)
+    key_chip = (key_iota // tok) ^ my_chip
+    key_tok = lax.rem(key_iota, jnp.int32(tok))
+    for core, bias_ref in ((my_core, bias_a_ref), (1 - my_core, bias_b_ref)):
+        key_pos = (key_chip * CORES + core) * tok + key_tok
+        bias_ref[...] = jnp.where(key_pos <= row_pos, 0.0, NEG_FILL)
+
+    rows = SUB_HEADS * tok
     lane = lax.broadcasted_iota(jnp.int32, (tok, 2 * ROPE), 1)
-    for head in range(HEAD_GROUP):
-        at = pl.ds(head * tok, tok)
-        stack_ref[at, 0:LAT] = q_ref[:, head * LAT : (head + 1) * LAT]
-        pair = qr_ref[:, (head // 2) * 2 * ROPE : (head // 2 + 1) * 2 * ROPE]
-        if head % 2:
-            pair = jnp.concatenate([pair[:, ROPE:], pair[:, :ROPE]], axis=1)
-        stack_ref[at, LAT : LAT + 2 * ROPE] = jnp.where(lane < ROPE, pair, jnp.zeros_like(pair))
-
-    rows = SUB_HEADS * tok
 
     def scores_of(sub, keys_ref, bias_ref):
         queries = stack_ref[sub * rows : (sub + 1) * rows, :]
@@ -73,10 +69,18 @@
         return scores.reshape(SUB_HEADS, tok, keys) * LOG2_SCALE + bias_ref[...][None]
 
     def both_scores(sub):
+        q_copies[sub].wait()
+        for copy in first_copies if sub == 0 else []:
+            copy.wait()
+        for head in range(sub * SUB_HEADS, (sub + 1) * SUB_HEADS):
+            at = pl.ds(head * tok, tok)
+            stack_ref[at, 0:LAT] = q_ref[:, head * LAT : (head + 1) * LAT]
+            pair = qr_ref[:, (head // 2) * 2 * ROPE : (head // 2 + 1) * 2 * ROPE]
+            if head % 2:
+                pair = jnp.concatenate([pair[:, ROPE:], pair[:, :ROPE]], axis=1)
+            stack_ref[at, LAT : LAT + 2 * ROPE] = jnp.where(lane < ROPE, pair, jnp.zeros_like(pair))
         return scores_of(sub, mine_ref, bias_a_ref), scores_of(sub, other_ref, bias_b_ref)
 
-    parts = []
-    subs = HEAD_GROUP // SUB_HEADS
     ready = both_scores(0)
     for sub in range(subs):
         scores_a, scores_b = ready
@@ -94,6 +98,7 @@
             preferred_element_type=jnp.float32,
         )
         latent = (mixed.reshape(SUB_HEADS, tok, LAT) / total).astype(jnp.bfloat16)
+        wv_copies[sub].wait()
         for head in range(0, SUB_HEADS, 2):
             first = sub * SUB_HEADS + head
             pair = jnp.dot(
@@ -101,60 +106,55 @@
                 jnp.concatenate([wv_ref[first], wv_ref[first + 1]], axis=1),
                 preferred_element_type=jnp.float32,
             ).astype(jnp.bfloat16)
-            parts.extend([pair[:tok, :VD], pair[tok:, VD:]])
-    wide = HEAD_GROUP * VD
-    values_ref[:, pl.ds(pl.multiple_of(group * wide, wide), wide)] = jnp.concatenate(parts, axis=1)
-
-    @pl.when(group == HEADS // HEAD_GROUP - 1)
-    def _():
-        values = values_ref[...].astype(jnp.float32)
-        square = jnp.mean(values * values, axis=1, keepdims=True)
-        normed = values * lax.rsqrt(square + NORM_EPS) * gain_ref[...]
-        normed = normed.astype(jnp.bfloat16)
-        up_ref[...] = normed[: tok // 2]
-        down_ref[...] = normed[tok // 2 :]
-
-
-def attention(my_index, q_nope, q_rope, mine, other, w_value, norm_gain):
+            values_ref[:, first * VD : (first + 1) * VD] = pair[:tok, :VD]
+            values_ref[:, (first + 1) * VD : (first + 2) * VD] = pair[tok:, VD:]
+
+    values = values_ref[...].astype(jnp.float32)
+    square = jnp.mean(values * values, axis=1, keepdims=True)
+    normed = values * lax.rsqrt(square + NORM_EPS) * gain_ref[...]
+    normed = normed.astype(jnp.bfloat16)
+    up_ref[...] = normed[: tok // 2]
+    down_ref[...] = normed[tok // 2 :]
+
+    last = mine_ref[:, LAT : LAT + 2 * ROPE].astype(jnp.float32)
+    lane = lax.broadcasted_iota(jnp.int32, last.shape, 1)
+    named = jnp.max(jnp.where(lane >= ROPE, last, -1.0), axis=1, keepdims=True)
+    my_expert = (my_index // SPAN).astype(jnp.float32)
+    hits = jnp.where(named == my_expert, 1.0, 0.0)
+    column = lax.broadcasted_iota(jnp.int32, hits_ref.shape, 1)
+    table = jnp.zeros(hits_ref.shape, jnp.float32)
+    for place in range(keys // tok):
+        table = jnp.where(column == place, hits[place * tok : (place + 1) * tok], table)
+    hits_ref[...] = table
+
+
+def attention(my_index, q_nope, q_rope, mine, other, w_value, gain):
     tok = q_nope.shape[0]
     total = mine.shape[0]
-    rows = HEAD_GROUP * tok
-    grid_spec = pltpu.PrefetchScalarGridSpec(
-        num_scalar_prefetch=1,
-        grid=(HEADS // HEAD_GROUP,),
-        in_specs=[
-            pl.BlockSpec((tok, HEAD_GROUP * LAT), lambda g, i: (0, g)),
-            pl.BlockSpec((tok, HEAD_GROUP * ROPE), lambda g, i: (0, g)),
-            pl.BlockSpec(mine.shape, lambda g, i: (0, 0)),
-            pl.BlockSpec(mine.shape, lambda g, i: (0, 0)),
-            pl.BlockSpec((HEAD_GROUP, LAT, VD), lambda g, i: (g, 0, 0)),
-            pl.BlockSpec((1, HEADS * VD), lambda g, i: (0, 0)),
-        ],
-        out_specs=[
-            pl.BlockSpec((tok, HEADS * VD), lambda g, i: (0, 0)),
-            pl.BlockSpec((tok // 2, HEADS * VD), lambda g, i: (0, 0)),
-            pl.BlockSpec((tok // 2, HEADS * VD), lambda g, i: (0, 0)),
-            pl.BlockSpec((tok, total // tok), lambda g, i: (0, 0)),
-        ],
-        scratch_shapes=[
-            pltpu.VMEM((rows, LAT + 2 * ROPE), jnp.bfloat16),
-            pltpu.VMEM((tok, total), jnp.float32),
-            pltpu.VMEM((tok, total), jnp.float32),
-        ],
-    )
+    rows = HEADS * tok
+    vmem, anywhere = pl.BlockSpec(memory_space=pltpu.VMEM), pl.BlockSpec(memory_space=pl.ANY)
     shape = jax.ShapeDtypeStruct((tok, HEADS * VD), jnp.bfloat16)
     half_shape = jax.ShapeDtypeStruct((tok // 2, HEADS * VD), jnp.bfloat16)
     hits_shape = jax.ShapeDtypeStruct((tok, total // tok), jnp.float32)
     work = HEADS * tok * total * CORES
+    fetched = (mine, other, q_nope, q_rope, w_value)
     return pl.pallas_call(
         functools.partial(attention_kernel, tok=tok),
-        grid_spec=grid_spec,
+        in_specs=[pl.BlockSpec(memory_space=pltpu.SMEM)] + [anywhere] * 5 + [vmem],
+        out_specs=[vmem] * 4,
         out_shape=[shape, half_shape, half_shape, hits_shape],
+        scratch_shapes=[pltpu.VMEM(x.shape, x.dtype) for x in fetched]
+        + [
+            pltpu.VMEM((rows, LAT + 2 * ROPE), jnp.bfloat16),
+            pltpu.VMEM((tok, total), jnp.float32),
+            pltpu.VMEM((tok, total), jnp.float32),
+            pltpu.SemaphoreType.DMA((3 + 2 * (HEADS // SUB_HEADS),)),
+        ],
         compiler_params=pltpu.CompilerParams(vmem_limit_bytes=56 << 20),
         cost_estimate=pl.CostEstimate(
             flops=2 * work * (2 * LAT + 2 * ROPE), bytes_accessed=8 << 20, transcendentals=work
         ),
-    )(my_index.reshape(1), q_nope, q_rope, mine, other, w_value, norm_gain.reshape(1, HEADS * VD))
+    )(my_index.reshape(1), *fetched, gain)
 
 
 def ring_place(chip, chips):
@@ -251,7 +251,7 @@
     own, mine, other = lax.optimization_barrier(((w_gate[0], w_up[0], w_down[0]), mine, other))
     swapped = tuple(lax.ppermute(w, "ctx", siblings) for w in own)
     values, upper, lower, hits = attention(
-        my_index, q_nope, q_rope, mine, other, w_value, norm_gain
+        my_index, q_nope, q_rope, mine, other, w_value, norm_gain.reshape(1, HEADS * VD)
     )
     start, swapped = lax.optimization_barrier(((upper, lower), swapped))
 

time: 124 us -> 126 us (1.016)
  Pallas kernels: 49 us -> 50.6 us
    pallas_call x1, Pallas kernels: 11.6 us -> 13.2 us  [attention(): pl.pallas_call(functools.partial(attention_kernel, tok=tok), in_specs=[pl...]
where the time goes in v10:
time: 126 us; the launch traced here: 125 us
  Pallas kernels  50.6 us (40%)
  starting transfers between devices  41.7 us (33%)
  waiting for transfers between devices  28 us (22%)
  other arithmetic  3.33 us (3%)
    pallas_call x8, Pallas kernels, expert_part(): pl.pallas_call(functools.partial(expert_kernel, hop=hop, chips=chips, pie...  37.5 us
    ppermute x18, starting transfers between devices, move(): return tuple((lax.ppermute(x, 'ctx', route) for x in blocks))  29.7 us
    ppermute x18, waiting for transfers between devices, move(): return tuple((lax.ppermute(x, 'ctx', route) for x in blocks))  21.4 us
    pallas_call x1, Pallas kernels, attention(): pl.pallas_call(functools.partial(attention_kernel, tok=tok), in_specs=[pl...  13.2 us
    ppermute x7, starting transfers between devices, from_chip(): lax.ppermute(block, 'ctx', [(i, i ^ step * CORES) for i in range(n_ctx)])  11.4 us
    ppermute x7, waiting for transfers between devices, from_chip(): lax.ppermute(block, 'ctx', [(i, i ^ step * CORES) for i in range(n_ctx)])  4.54 us
  transfers between devices with their start and end apart: 29, of which 15 were waited for; matrix products, arithmetic and copies ran while one was open for 1% of the time, Pallas kernels for 40%

profile of v10, /device:TPU:0, one launch (start us, length us, event | category | flops | bytes accessed | tf_op | source)
XLA Modules:
  0.0 125.2 jit_solution(8048780154296103352)
XLA Ops:
  1.7 4.1 %collective-permute-start.3 = (bf16[64,640]{1,0:T(8,128)(2,1)S(1)}, bf16[64,640]{1,0:T(8,128)(2,1)S(1)}, u32[]{:S(2)}, u32[]{:S(2)}) collective-permute-start(bf16[64,640]{1,0:T(8,128)(2,1)S(1)} %get-tuple-element.59), channel_id=1, source_target_pairs={{0,8},{1,9},{2,10},{3,11},{4,12},{5,13},{6,14},{7,15},{8,0},{9,1},... | collective-permute-start | bytes 245768 | tf_op jit(solution)/shard_map/ppermute | solution.py:241
  5.8 1.5 %collective-permute-start = (bf16[64,640]{1,0:T(8,128)(2,1)S(1)}, bf16[64,640]{1,0:T(8,128)(2,1)S(1)}, u32[]{:S(2)}, u32[]{:S(2)}) collective-permute-start(bf16[64,640]{1,0:T(8,128)(2,1)S(1)} %get-tuple-element.59), channel_id=1, source_target_pairs={{0,2},{1,3},{2,0},{3,1},{4,6},{5,7},{6,4},{7,5},{8,10},{9,11},{10,... | collective-permute-start | bytes 245768 | tf_op jit(solution)/shard_map/ppermute | solution.py:241
  7.3 1.6 %collective-permute-start.1 = (bf16[64,640]{1,0:T(8,128)(2,1)S(1)}, bf16[64,640]{1,0:T(8,128)(2,1)S(1)}, u32[]{:S(2)}, u32[]{:S(2)}) collective-permute-start(bf16[64,640]{1,0:T(8,128)(2,1)S(1)} %get-tuple-element.59), channel_id=1, source_target_pairs={{0,4},{1,5},{2,6},{3,7},{4,0},{5,1},{6,2},{7,3},{8,12},{9,13},{10,... | collective-permute-start | bytes 245768 | tf_op jit(solution)/shard_map/ppermute | solution.py:241
  9.8 1.6 %collective-permute-start.4 = (bf16[64,640]{1,0:T(8,128)(2,1)S(1)}, bf16[64,640]{1,0:T(8,128)(2,1)S(1)}, u32[]{:S(2)}, u32[]{:S(2)}) collective-permute-start(bf16[64,640]{1,0:T(8,128)(2,1)S(1)} %collective-permute-done.3), channel_id=1, source_target_pairs={{0,2},{1,3},{2,0},{3,1},{4,6},{5,7},{6,4},{7,5},{8,10},{9,11},{10,... | collective-permute-start | bytes 245768 | tf_op jit(solution)/shard_map/ppermute | solution.py:241
  15.9 1.8 %collective-permute-done.6 = bf16[64,640]{1,0:T(8,128)(2,1)S(1)} collective-permute-done((bf16[64,640]{1,0:T(8,128)(2,1)S(1)}, bf16[64,640]{1,0:T(8,128)(2,1)S(1)}, u32[]{:S(2)}, u32[]{:S(2)}) %collective-permute-start.6) | collective-permute-done | bytes 81952 | tf_op jit(solution)/shard_map/ppermute | solution.py:241
  17.8 2.1 %collective-permute-done.7.other_hbm = bf16[512,640]{1,0:T(8,128)(2,1)S(1)} collective-permute-done((bf16[512,640]{1,0:T(8,128)(2,1)S(1)}, bf16[512,640]{1,0:T(8,128)(2,1)S(1)}, u32[]{:S(2)}, u32[]{:S(2)}) %collective-permute-start.7) | collective-permute-done | bytes 655392 | tf_op jit(solution)/shard_map/ppermute | solution.py:249
  20.7 13.2 %shard_map.109 = (bf16[64,4096]{1,0:T(8,128)(2,1)}, bf16[32,4096]{1,0:T(8,128)(2,1)}, bf16[32,4096]{1,0:T(8,128)(2,1)}, f32[64,8]{1,0:T(8,128)}) custom-call(s32[1]{0:T(128)} %bitcast.index_ref, bf16[512,640]{1,0:T(8,128)(2,1)} %copy-done.8, bf16[512,640]{1,0:T(8,128)(2,1)} %copy-done.9, bf16[64,16384]{1,0:T(8,128)(2,1)} %q_hbm.1, bf16[64,2048]{1,0:T(8,128)(2,1)} %qr_hbm.1, ...), custom_call_target="tpu_custom_call" | custom-call | flops 4831838208 | bytes 8388608 | tf_op jit(solution)/shard_map/pallas_call | solution.py:141
  35.1 2.7 %collective-permute-start.11 = (bf16[32,4096]{1,0:T(8,128)(2,1)}, bf16[32,4096]{1,0:T(8,128)(2,1)S(1)}, u32[]{:S(2)}, u32[]{:S(2)}) collective-permute-start(bf16[32,4096]{1,0:T(8,128)(2,1)} %get-tuple-element.53.refs_0_), channel_id=1, source_target_pairs={{0,4},{1,3},{4,8},{5,1},{8,12},{9,5},{12,14},{13,9},{14,10},{15,13... | collective-permute-start | bytes 786440 | tf_op jit(solution)/shard_map/ppermute | solution.py:263
  37.8 2.8 %collective-permute-done.13.refs_1_ = bf16[32,4096]{1,0:T(8,128)(2,1)S(1)} collective-permute-done((bf16[32,4096]{1,0:T(8,128)(2,1)}, bf16[32,4096]{1,0:T(8,128)(2,1)S(1)}, u32[]{:S(2)}, u32[]{:S(2)}) %collective-permute-start.13) | collective-permute-done | bytes 262176 | tf_op jit(solution)/shard_map/ppermute | solution.py:263
  40.6 1.4 %collective-permute-start.14 = (bf16[32,4096]{1,0:T(8,128)(2,1)S(1)}, bf16[32,4096]{1,0:T(8,128)(2,1)S(1)}, u32[]{:S(2)}, u32[]{:S(2)}) collective-permute-start(bf16[32,4096]{1,0:T(8,128)(2,1)S(1)} %collective-permute-done.13.refs_1_), channel_id=1, source_target_pairs={{0,4},{1,3},{4,8},{5,1},{8,12},{9,5},{12,14},{13,9},{14,10},{15,13... | collective-permute-start | bytes 786440 | tf_op jit(solution)/shard_map/ppermute | solution.py:263
  43.4 1.4 %collective-permute-start.12 = (bf16[32,4096]{1,0:T(8,128)(2,1)S(1)}, bf16[32,4096]{1,0:T(8,128)(2,1)S(1)}, u32[]{:S(2)}, u32[]{:S(2)}) collective-permute-start(bf16[32,4096]{1,0:T(8,128)(2,1)S(1)} %collective-permute-done.11.refs_0_), channel_id=1, source_target_pairs={{0,4},{1,3},{4,8},{5,1},{8,12},{9,5},{12,14},{13,9},{14,10},{15,13... | collective-permute-start | bytes 786440 | tf_op jit(solution)/shard_map/ppermute | solution.py:263
  45.6 4.7 %shard_map.110 = f32[64,4096]{1,0:T(8,128)S(1)} custom-call(s32[1]{0:T(128)} %bitcast.index_ref, bf16[4096,256]{1,0:T(8,128)(2,1)S(1)} %bitcast.10, bf16[4096,256]{1,0:T(8,128)(2,1)S(1)} %bitcast.19, bf16[256,4096]{1,0:T(8,128)(2,1)S(1)} %bitcast.28, f32[64,8]{1,0:T(8,128)S(1)} %copy-done.3, bf16[4096,256]{1,0:T(8,128)(2,1)} %collective-permute-done.8.gate_hbm, ...), custom_call_target="tpu_custom_call" | custom-call | flops 805306368 | bytes 14680064 | tf_op jit(solution)/shard_map/pallas_call | solution.py:212
  50.3 2.4 %collective-permute-start.17 = (bf16[64,4096]{1,0:T(8,128)(2,1)S(1)}, bf16[64,4096]{1,0:T(8,128)(2,1)S(1)}, u32[]{:S(2)}, u32[]{:S(2)}) collective-permute-start(bf16[64,4096]{1,0:T(8,128)(2,1)S(1)} %convert_element_type.72), channel_id=1, source_target_pairs={{0,4},{1,3},{4,8},{5,1},{8,12},{9,5},{12,14},{13,9},{14,10},{15,13... | collective-permute-start | bytes 1572872 | tf_op jit(solution)/shard_map/ppermute | solution.py:263
  53.4 4.7 %shard_map.111 = f32[64,4096]{1,0:T(8,128)S(1)} custom-call(s32[1]{0:T(128)} %bitcast.index_ref, bf16[4096,256]{1,0:T(8,128)(2,1)S(1)} %bitcast.11, bf16[4096,256]{1,0:T(8,128)(2,1)S(1)} %bitcast.20, bf16[256,4096]{1,0:T(8,128)(2,1)S(1)} %bitcast.29, f32[64,8]{1,0:T(8,128)S(1)} %copy-done.3, bf16[4096,256]{1,0:T(8,128)(2,1)} %collective-permute-done.8.gate_hbm, ...), custom_call_target="tpu_custom_call" | custom-call | flops 805306368 | bytes 14680064 | tf_op jit(solution)/shard_map/pallas_call | solution.py:212
  58.1 1.5 %collective-permute-done.17 = bf16[64,4096]{1,0:T(8,128)(2,1)S(1)} collective-permute-done((bf16[64,4096]{1,0:T(8,128)(2,1)S(1)}, bf16[64,4096]{1,0:T(8,128)(2,1)S(1)}, u32[]{:S(2)}, u32[]{:S(2)}) %collective-permute-start.17) | collective-permute-done | bytes 524320 | tf_op jit(solution)/shard_map/ppermute | solution.py:263
  59.7 2.4 %collective-permute-start.19 = (bf16[64,4096]{1,0:T(8,128)(2,1)S(1)}, bf16[64,4096]{1,0:T(8,128)(2,1)S(1)}, u32[]{:S(2)}, u32[]{:S(2)}) collective-permute-start(bf16[64,4096]{1,0:T(8,128)(2,1)S(1)} %add_convert_fusion.3), channel_id=1, source_target_pairs={{0,4},{1,3},{4,8},{5,1},{8,12},{9,5},{12,14},{13,9},{14,10},{15,13... | collective-permute-start | bytes 1572872 | tf_op jit(solution)/shard_map/ppermute | solution.py:263
  62.1 3.1 %collective-permute-done.15.refs_0_ = bf16[64,4096]{1,0:T(8,128)(2,1)S(1)} collective-permute-done((bf16[64,4096]{1,0:T(8,128)(2,1)S(1)}, bf16[64,4096]{1,0:T(8,128)(2,1)S(1)}, u32[]{:S(2)}, u32[]{:S(2)}) %collective-permute-start.15) | collective-permute-done | bytes 524320 | tf_op jit(solution)/shard_map/ppermute | solution.py:263
  65.2 2.4 %collective-permute-start.16 = (bf16[64,4096]{1,0:T(8,128)(2,1)S(1)}, bf16[64,4096]{1,0:T(8,128)(2,1)S(1)}, u32[]{:S(2)}, u32[]{:S(2)}) collective-permute-start(bf16[64,4096]{1,0:T(8,128)(2,1)S(1)} %collective-permute-done.15.refs_0_), channel_id=1, source_target_pairs={{0,4},{1,3},{4,8},{5,1},{8,12},{9,5},{12,14},{13,9},{14,10},{15,13... | collective-permute-start | bytes 1572872 | tf_op jit(solution)/shard_map/ppermute | solution.py:263
  67.6 4.7 %shard_map.112 = f32[64,4096]{1,0:T(8,128)S(1)} custom-call(s32[1]{0:T(128)} %bitcast.index_ref, bf16[4096,256]{1,0:T(8,128)(2,1)S(1)} %bitcast.12, bf16[4096,256]{1,0:T(8,128)(2,1)S(1)} %bitcast.21, bf16[256,4096]{1,0:T(8,128)(2,1)S(1)} %bitcast.30, f32[64,8]{1,0:T(8,128)S(1)} %copy-done.3, bf16[4096,256]{1,0:T(8,128)(2,1)} %collective-permute-done.8.gate_hbm, ...), custom_call_target="tpu_custom_call" | custom-call | flops 805306368 | bytes 14680064 | tf_op jit(solution)/shard_map/pallas_call | solution.py:212
  73.3 3.1 %collective-permute-done.16.refs_0_ = bf16[64,4096]{1,0:T(8,128)(2,1)S(1)} collective-permute-done((bf16[64,4096]{1,0:T(8,128)(2,1)S(1)}, bf16[64,4096]{1,0:T(8,128)(2,1)S(1)}, u32[]{:S(2)}, u32[]{:S(2)}) %collective-permute-start.16) | collective-permute-done | bytes 524320 | tf_op jit(solution)/shard_map/ppermute | solution.py:263
  76.4 2.4 %collective-permute-start.18 = (bf16[64,4096]{1,0:T(8,128)(2,1)S(1)}, bf16[64,4096]{1,0:T(8,128)(2,1)S(1)}, u32[]{:S(2)}, u32[]{:S(2)}) collective-permute-start(bf16[64,4096]{1,0:T(8,128)(2,1)S(1)} %collective-permute-done.16.refs_0_), channel_id=1, source_target_pairs={{0,4},{1,3},{4,8},{5,1},{8,12},{9,5},{12,14},{13,9},{14,10},{15,13... | collective-permute-start | bytes 1572872 | tf_op jit(solution)/shard_map/ppermute | solution.py:263
  78.8 4.7 %shard_map.113 = f32[64,4096]{1,0:T(8,128)S(1)} custom-call(s32[1]{0:T(128)} %bitcast.index_ref, bf16[4096,256]{1,0:T(8,128)(2,1)S(1)} %bitcast.13, bf16[4096,256]{1,0:T(8,128)(2,1)S(1)} %bitcast.22, bf16[256,4096]{1,0:T(8,128)(2,1)S(1)} %bitcast.31, f32[64,8]{1,0:T(8,128)S(1)} %copy-done.3, bf16[4096,256]{1,0:T(8,128)(2,1)} %collective-permute-done.8.gate_hbm, ...), custom_call_target="tpu_custom_call" | custom-call | flops 805306368 | bytes 14680064 | tf_op jit(solution)/shard_map/pallas_call | solution.py:212
  84.6 3.1 %collective-permute-done.18.refs_0_ = bf16[64,4096]{1,0:T(8,128)(2,1)S(1)} collective-permute-done((bf16[64,4096]{1,0:T(8,128)(2,1)S(1)}, bf16[64,4096]{1,0:T(8,128)(2,1)S(1)}, u32[]{:S(2)}, u32[]{:S(2)}) %collective-permute-start.18) | collective-permute-done | bytes 524320 | tf_op jit(solution)/shard_map/ppermute | solution.py:263
  87.7 2.4 %collective-permute-start.20 = (bf16[64,4096]{1,0:T(8,128)(2,1)S(1)}, bf16[64,4096]{1,0:T(8,128)(2,1)S(1)}, u32[]{:S(2)}, u32[]{:S(2)}) collective-permute-start(bf16[64,4096]{1,0:T(8,128)(2,1)S(1)} %collective-permute-done.18.refs_0_), channel_id=1, source_target_pairs={{0,4},{1,3},{4,8},{5,1},{8,12},{9,5},{12,14},{13,9},{14,10},{15,13... | collective-permute-start | bytes 1572872 | tf_op jit(solution)/shard_map/ppermute | solution.py:263
  90.0 4.7 %shard_map.116 = f32[64,4096]{1,0:T(8,128)S(1)} custom-call(s32[1]{0:T(128)} %bitcast.index_ref, bf16[4096,256]{1,0:T(8,128)(2,1)S(1)} %bitcast.14, bf16[4096,256]{1,0:T(8,128)(2,1)S(1)} %bitcast.23, bf16[256,4096]{1,0:T(8,128)(2,1)S(1)} %bitcast.32, f32[64,8]{1,0:T(8,128)S(1)} %copy-done.3, bf16[4096,256]{1,0:T(8,128)(2,1)} %collective-permute-done.8.gate_hbm, ...), custom_call_target="tpu_custom_call" | custom-call | flops 805306368 | bytes 14680064 | tf_op jit(solution)/shard_map/pallas_call | solution.py:212
  95.8 3.1 %collective-permute-done.20.refs_0_ = bf16[64,4096]{1,0:T(8,128)(2,1)S(1)} collective-permute-done((bf16[64,4096]{1,0:T(8,128)(2,1)S(1)}, bf16[64,4096]{1,0:T(8,128)(2,1)S(1)}, u32[]{:S(2)}, u32[]{:S(2)}) %collective-permute-start.20) | collective-permute-done | bytes 524320 | tf_op jit(solution)/shard_map/ppermute | solution.py:263
  98.9 2.4 %collective-permute-start.22 = (bf16[64,4096]{1,0:T(8,128)(2,1)S(1)}, bf16[64,4096]{1,0:T(8,128)(2,1)S(1)}, u32[]{:S(2)}, u32[]{:S(2)}) collective-permute-start(bf16[64,4096]{1,0:T(8,128)(2,1)S(1)} %collective-permute-done.20.refs_0_), channel_id=1, source_target_pairs={{0,4},{1,3},{4,8},{5,1},{8,12},{9,5},{12,14},{13,9},{14,10},{15,13... | collective-permute-start | bytes 1572872 | tf_op jit(solution)/shard_map/ppermute | solution.py:263
  101.3 4.7 %shard_map.115 = (f32[32,4096]{1,0:T(8,128)S(1)}, f32[32,4096]{1,0:T(8,128)S(1)}) custom-call(s32[1]{0:T(128)} %bitcast.index_ref, bf16[4096,256]{1,0:T(8,128)(2,1)S(1)} %bitcast.15, bf16[4096,256]{1,0:T(8,128)(2,1)S(1)} %bitcast.24, bf16[256,4096]{1,0:T(8,128)(2,1)S(1)} %bitcast.33, f32[64,8]{1,0:T(8,128)S(1)} %copy-done.3, ...), custom_call_target="tpu_custom_call" | custom-call | flops 805306368 | bytes 14680064 | tf_op jit(solution)/shard_map/pallas_call | solution.py:212
  107.9 2.2 %collective-permute-done.22.refs_0_ = bf16[64,4096]{1,0:T(8,128)(2,1)S(1)} collective-permute-done((bf16[64,4096]{1,0:T(8,128)(2,1)S(1)}, bf16[64,4096]{1,0:T(8,128)(2,1)S(1)}, u32[]{:S(2)}, u32[]{:S(2)}) %collective-permute-start.22) | collective-permute-done | bytes 524320 | tf_op jit(solution)/shard_map/ppermute | solution.py:263
  110.1 4.7 %shard_map.114 = (f32[32,4096]{1,0:T(8,128)S(1)}, f32[32,4096]{1,0:T(8,128)S(1)}) custom-call(s32[1]{0:T(128)} %bitcast.index_ref, bf16[4096,256]{1,0:T(8,128)(2,1)S(1)} %bitcast.16, bf16[4096,256]{1,0:T(8,128)(2,1)S(1)} %bitcast.25, bf16[256,4096]{1,0:T(8,128)(2,1)S(1)} %bitcast.34, f32[64,8]{1,0:T(8,128)S(1)} %copy-done.3, ...), custom_call_target="tpu_custom_call" | custom-call | flops 805306368 | bytes 14680064 | tf_op jit(solution)/shard_map/pallas_call | solution.py:212
  114.9 2.4 %collective-permute-start.28 = (bf16[32,4096]{1,0:T(8,128)(2,1)S(1)}, bf16[32,4096]{1,0:T(8,128)(2,1)S(1)}, u32[]{:S(2)}, u32[]{:S(2)}) collective-permute-start(bf16[32,4096]{1,0:T(8,128)(2,1)S(1)} %add_convert_fusion.4), channel_id=1, source_target_pairs={{0,4},{1,3},{4,8},{5,1},{8,12},{9,5},{12,14},{13,9},{14,10},{15,13... | collective-permute-start | bytes 786440 | tf_op jit(solution)/shard_map/ppermute | solution.py:263
  118.2 4.7 %shard_map.117 = (f32[32,4096]{1,0:T(8,128)S(1)}, f32[32,4096]{1,0:T(8,128)S(1)}) custom-call(s32[1]{0:T(128)} %bitcast.index_ref, bf16[4096,256]{1,0:T(8,128)(2,1)S(1)} %bitcast.17, bf16[4096,256]{1,0:T(8,128)(2,1)S(1)} %bitcast.26, bf16[256,4096]{1,0:T(8,128)(2,1)S(1)} %bitcast.35, f32[64,8]{1,0:T(8,128)S(1)} %copy-done.4, ...), custom_call_target="tpu_custom_call" | custom-call | flops 805306368 | bytes 14680064 | tf_op jit(solution)/shard_map/pallas_call | solution.py:212
  (80 shorter events, 20.4 us)
Async XLA Ops:
  1.7 8.1 %collective-permute-start.3 = (bf16[64,640]{1,0:T(8,128)(2,1)S(1)}, bf16[64,640]{1,0:T(8,128)(2,1)S(1)}, u32[]{:S(2)}, u32[]{:S(2)}) collective-permute-start(bf16[64,640]{1,0:T(8,128)(2,1)S(1)} %get-tuple-element.59), channel_id=1, source_target_pairs={{0,8},{1,9},{2,10},{3,11},{4,12},{5,13},{6,14},{7,15},{8,0},{9,1},... | collective-permute-start | bytes 245768 | tf_op jit(solution)/shard_map/ppermute | solution.py:241
  5.8 6.6 %collective-permute-start = (bf16[64,640]{1,0:T(8,128)(2,1)S(1)}, bf16[64,640]{1,0:T(8,128)(2,1)S(1)}, u32[]{:S(2)}, u32[]{:S(2)}) collective-permute-start(bf16[64,640]{1,0:T(8,128)(2,1)S(1)} %get-tuple-element.59), channel_id=1, source_target_pairs={{0,2},{1,3},{2,0},{3,1},{4,6},{5,7},{6,4},{7,5},{8,10},{9,11},{10,... | collective-permute-start | bytes 245768 | tf_op jit(solution)/shard_map/ppermute | solution.py:241
  7.3 6.3 %collective-permute-start.1 = (bf16[64,640]{1,0:T(8,128)(2,1)S(1)}, bf16[64,640]{1,0:T(8,128)(2,1)S(1)}, u32[]{:S(2)}, u32[]{:S(2)}) collective-permute-start(bf16[64,640]{1,0:T(8,128)(2,1)S(1)} %get-tuple-element.59), channel_id=1, source_target_pairs={{0,4},{1,5},{2,6},{3,7},{4,0},{5,1},{6,2},{7,3},{8,12},{9,13},{10,... | collective-permute-start | bytes 245768 | tf_op jit(solution)/shard_map/ppermute | solution.py:241
  8.9 5.6 %collective-permute-start.2 = (bf16[64,640]{1,0:T(8,128)(2,1)S(1)}, bf16[64,640]{1,0:T(8,128)(2,1)S(1)}, u32[]{:S(2)}, u32[]{:S(2)}) collective-permute-start(bf16[64,640]{1,0:T(8,128)(2,1)S(1)} %get-tuple-element.59), channel_id=1, source_target_pairs={{0,6},{1,7},{2,4},{3,5},{4,2},{5,3},{6,0},{7,1},{8,14},{9,15},{10,... | collective-permute-start | bytes 245768 | tf_op jit(solution)/shard_map/ppermute | solution.py:241
  9.8 5.5 %collective-permute-start.4 = (bf16[64,640]{1,0:T(8,128)(2,1)S(1)}, bf16[64,640]{1,0:T(8,128)(2,1)S(1)}, u32[]{:S(2)}, u32[]{:S(2)}) collective-permute-start(bf16[64,640]{1,0:T(8,128)(2,1)S(1)} %collective-permute-done.3), channel_id=1, source_target_pairs={{0,2},{1,3},{2,0},{3,1},{4,6},{5,7},{6,4},{7,5},{8,10},{9,11},{10,... | collective-permute-start | bytes 245768 | tf_op jit(solution)/shard_map/ppermute | solution.py:241
  11.4 4.5 %collective-permute-start.5 = (bf16[64,640]{1,0:T(8,128)(2,1)S(1)}, bf16[64,640]{1,0:T(8,128)(2,1)S(1)}, u32[]{:S(2)}, u32[]{:S(2)}) collective-permute-start(bf16[64,640]{1,0:T(8,128)(2,1)S(1)} %collective-permute-done.3), channel_id=1, source_target_pairs={{0,4},{1,5},{2,6},{3,7},{4,0},{5,1},{6,2},{7,3},{8,12},{9,13},{10,... | collective-permute-start | bytes 245768 | tf_op jit(solution)/shard_map/ppermute | solution.py:241
  12.4 5.3 %collective-permute-start.6 = (bf16[64,640]{1,0:T(8,128)(2,1)S(1)}, bf16[64,640]{1,0:T(8,128)(2,1)S(1)}, u32[]{:S(2)}, u32[]{:S(2)}) collective-permute-start(bf16[64,640]{1,0:T(8,128)(2,1)S(1)} %collective-permute-done.3), channel_id=1, source_target_pairs={{0,6},{1,7},{2,4},{3,5},{4,2},{5,3},{6,0},{7,1},{8,14},{9,15},{10,... | collective-permute-start | bytes 245768 | tf_op jit(solution)/shard_map/ppermute | solution.py:241
  17.7 2.2 %collective-permute-start.7 = (bf16[512,640]{1,0:T(8,128)(2,1)S(1)}, bf16[512,640]{1,0:T(8,128)(2,1)S(1)}, u32[]{:S(2)}, u32[]{:S(2)}) collective-permute-start(bf16[512,640]{1,0:T(8,128)(2,1)S(1)} %constant_dynamic-update-slice_fusion.mine_hbm), channel_id=1, source_target_pairs={{0,1},{1,0},{2,3},{3,2},{4,5},{5,4},{6,7},{7,6},{8,9},{9,8},{10,11... | collective-permute-start | bytes 1966088 | tf_op jit(solution)/shard_map/ppermute | solution.py:249
  19.9 14.0 %collective-permute-start.8 = (bf16[4096,256]{1,0:T(8,128)(2,1)}, bf16[4096,256]{1,0:T(8,128)(2,1)}, u32[]{:S(2)}, u32[]{:S(2)}) collective-permute-start(bf16[4096,256]{1,0:T(8,128)(2,1)} %bitcast.9), channel_id=1, source_target_pairs={{0,1},{1,0},{2,3},{3,2},{4,5},{5,4},{6,7},{7,6},{8,9},{9,8},{10,11... | collective-permute-start | bytes 6291464 | tf_op jit(solution)/shard_map/ppermute | solution.py:252
  20.0 13.9 %collective-permute-start.9 = (bf16[4096,256]{1,0:T(8,128)(2,1)}, bf16[4096,256]{1,0:T(8,128)(2,1)}, u32[]{:S(2)}, u32[]{:S(2)}) collective-permute-start(bf16[4096,256]{1,0:T(8,128)(2,1)} %bitcast.18), channel_id=1, source_target_pairs={{0,1},{1,0},{2,3},{3,2},{4,5},{5,4},{6,7},{7,6},{8,9},{9,8},{10,11... | collective-permute-start | bytes 6291464 | tf_op jit(solution)/shard_map/ppermute | solution.py:252
  20.4 13.6 %collective-permute-start.10 = (bf16[256,4096]{1,0:T(8,128)(2,1)}, bf16[256,4096]{1,0:T(8,128)(2,1)}, u32[]{:S(2)}, u32[]{:S(2)}) collective-permute-start(bf16[256,4096]{1,0:T(8,128)(2,1)} %bitcast.27), channel_id=1, source_target_pairs={{0,1},{1,0},{2,3},{3,2},{4,5},{5,4},{6,7},{7,6},{8,9},{9,8},{10,11... | collective-permute-start | bytes 6291464 | tf_op jit(solution)/shard_map/ppermute | solution.py:252
  20.7 24.1 %copy-start = (bf16[1,4096,256]{2,1,0:T(8,128)(2,1)S(1)}, bf16[1,4096,256]{2,1,0:T(8,128)(2,1)}, u32[]{:S(2)}) copy-start(bf16[1,4096,256]{2,1,0:T(8,128)(2,1)} %param.19) | copy-start | bytes 6291460
  20.7 24.1 %copy-start.1 = (bf16[1,4096,256]{2,1,0:T(8,128)(2,1)S(1)}, bf16[1,4096,256]{2,1,0:T(8,128)(2,1)}, u32[]{:S(2)}) copy-start(bf16[1,4096,256]{2,1,0:T(8,128)(2,1)} %param.20) | copy-start | bytes 6291460
  20.7 24.1 %copy-start.2 = (bf16[1,256,4096]{2,1,0:T(8,128)(2,1)S(1)}, bf16[1,256,4096]{2,1,0:T(8,128)(2,1)}, u32[]{:S(2)}) copy-start(bf16[1,256,4096]{2,1,0:T(8,128)(2,1)} %param.21) | copy-start | bytes 6291460
  34.0 6.6 %collective-permute-start.13 = (bf16[32,4096]{1,0:T(8,128)(2,1)}, bf16[32,4096]{1,0:T(8,128)(2,1)S(1)}, u32[]{:S(2)}, u32[]{:S(2)}) collective-permute-start(bf16[32,4096]{1,0:T(8,128)(2,1)} %get-tuple-element.54.refs_1_), channel_id=1, source_target_pairs={{0,4},{1,3},{4,8},{5,1},{8,12},{9,5},{12,14},{13,9},{14,10},{15,13... | collective-permute-start | bytes 786440 | tf_op jit(solution)/shard_map/ppermute | solution.py:263
  35.1 8.3 %collective-permute-start.11 = (bf16[32,4096]{1,0:T(8,128)(2,1)}, bf16[32,4096]{1,0:T(8,128)(2,1)S(1)}, u32[]{:S(2)}, u32[]{:S(2)}) collective-permute-start(bf16[32,4096]{1,0:T(8,128)(2,1)} %get-tuple-element.53.refs_0_), channel_id=1, source_target_pairs={{0,4},{1,3},{4,8},{5,1},{8,12},{9,5},{12,14},{13,9},{14,10},{15,13... | collective-permute-start | bytes 786440 | tf_op jit(solution)/shard_map/ppermute | solution.py:263
  40.6 12.2 %collective-permute-start.14 = (bf16[32,4096]{1,0:T(8,128)(2,1)S(1)}, bf16[32,4096]{1,0:T(8,128)(2,1)S(1)}, u32[]{:S(2)}, u32[]{:S(2)}) collective-permute-start(bf16[32,4096]{1,0:T(8,128)(2,1)S(1)} %collective-permute-done.13.refs_1_), channel_id=1, source_target_pairs={{0,4},{1,3},{4,8},{5,1},{8,12},{9,5},{12,14},{13,9},{14,10},{15,13... | collective-permute-start | bytes 786440 | tf_op jit(solution)/shard_map/ppermute | solution.py:263
  43.4 9.4 %collective-permute-start.12 = (bf16[32,4096]{1,0:T(8,128)(2,1)S(1)}, bf16[32,4096]{1,0:T(8,128)(2,1)S(1)}, u32[]{:S(2)}, u32[]{:S(2)}) collective-permute-start(bf16[32,4096]{1,0:T(8,128)(2,1)S(1)} %collective-permute-done.11.refs_0_), channel_id=1, source_target_pairs={{0,4},{1,3},{4,8},{5,1},{8,12},{9,5},{12,14},{13,9},{14,10},{15,13... | collective-permute-start | bytes 786440 | tf_op jit(solution)/shard_map/ppermute | solution.py:263
  50.3 9.2 %collective-permute-start.17 = (bf16[64,4096]{1,0:T(8,128)(2,1)S(1)}, bf16[64,4096]{1,0:T(8,128)(2,1)S(1)}, u32[]{:S(2)}, u32[]{:S(2)}) collective-permute-start(bf16[64,4096]{1,0:T(8,128)(2,1)S(1)} %convert_element_type.72), channel_id=1, source_target_pairs={{0,4},{1,3},{4,8},{5,1},{8,12},{9,5},{12,14},{13,9},{14,10},{15,13... | collective-permute-start | bytes 1572872 | tf_op jit(solution)/shard_map/ppermute | solution.py:263
  52.8 12.4 %collective-permute-start.15 = (bf16[64,4096]{1,0:T(8,128)(2,1)S(1)}, bf16[64,4096]{1,0:T(8,128)(2,1)S(1)}, u32[]{:S(2)}, u32[]{:S(2)}) collective-permute-start(bf16[64,4096]{1,0:T(8,128)(2,1)S(1)} %pad_maximum_fusion), channel_id=1, source_target_pairs={{0,4},{1,3},{4,8},{5,1},{8,12},{9,5},{12,14},{13,9},{14,10},{15,13... | collective-permute-start | bytes 1572872 | tf_op jit(solution)/shard_map/ppermute | solution.py:263
  59.7 12.6 %collective-permute-start.19 = (bf16[64,4096]{1,0:T(8,128)(2,1)S(1)}, bf16[64,4096]{1,0:T(8,128)(2,1)S(1)}, u32[]{:S(2)}, u32[]{:S(2)}) collective-permute-start(bf16[64,4096]{1,0:T(8,128)(2,1)S(1)} %add_convert_fusion.3), channel_id=1, source_target_pairs={{0,4},{1,3},{4,8},{5,1},{8,12},{9,5},{12,14},{13,9},{14,10},{15,13... | collective-permute-start | bytes 1572872 | tf_op jit(solution)/shard_map/ppermute | solution.py:263
  65.2 11.2 %collective-permute-start.16 = (bf16[64,4096]{1,0:T(8,128)(2,1)S(1)}, bf16[64,4096]{1,0:T(8,128)(2,1)S(1)}, u32[]{:S(2)}, u32[]{:S(2)}) collective-permute-start(bf16[64,4096]{1,0:T(8,128)(2,1)S(1)} %collective-permute-done.15.refs_0_), channel_id=1, source_target_pairs={{0,4},{1,3},{4,8},{5,1},{8,12},{9,5},{12,14},{13,9},{14,10},{15,13... | collective-permute-start | bytes 1572872 | tf_op jit(solution)/shard_map/ppermute | solution.py:263
  72.4 11.1 %collective-permute-start.21 = (bf16[64,4096]{1,0:T(8,128)(2,1)S(1)}, bf16[64,4096]{1,0:T(8,128)(2,1)S(1)}, u32[]{:S(2)}, u32[]{:S(2)}) collective-permute-start(bf16[64,4096]{1,0:T(8,128)(2,1)S(1)} %add_convert_fusion.2), channel_id=1, source_target_pairs={{0,4},{1,3},{4,8},{5,1},{8,12},{9,5},{12,14},{13,9},{14,10},{15,13... | collective-permute-start | bytes 1572872 | tf_op jit(solution)/shard_map/ppermute | solution.py:263
  76.4 11.2 %collective-permute-start.18 = (bf16[64,4096]{1,0:T(8,128)(2,1)S(1)}, bf16[64,4096]{1,0:T(8,128)(2,1)S(1)}, u32[]{:S(2)}, u32[]{:S(2)}) collective-permute-start(bf16[64,4096]{1,0:T(8,128)(2,1)S(1)} %collective-permute-done.16.refs_0_), channel_id=1, source_target_pairs={{0,4},{1,3},{4,8},{5,1},{8,12},{9,5},{12,14},{13,9},{14,10},{15,13... | collective-permute-start | bytes 1572872 | tf_op jit(solution)/shard_map/ppermute | solution.py:263
  83.6 11.1 %collective-permute-start.23 = (bf16[64,4096]{1,0:T(8,128)(2,1)S(1)}, bf16[64,4096]{1,0:T(8,128)(2,1)S(1)}, u32[]{:S(2)}, u32[]{:S(2)}) collective-permute-start(bf16[64,4096]{1,0:T(8,128)(2,1)S(1)} %add_convert_fusion.1), channel_id=1, source_target_pairs={{0,4},{1,3},{4,8},{5,1},{8,12},{9,5},{12,14},{13,9},{14,10},{15,13... | collective-permute-start | bytes 1572872 | tf_op jit(solution)/shard_map/ppermute | solution.py:263
  87.7 11.2 %collective-permute-start.20 = (bf16[64,4096]{1,0:T(8,128)(2,1)S(1)}, bf16[64,4096]{1,0:T(8,128)(2,1)S(1)}, u32[]{:S(2)}, u32[]{:S(2)}) collective-permute-start(bf16[64,4096]{1,0:T(8,128)(2,1)S(1)} %collective-permute-done.18.refs_0_), channel_id=1, source_target_pairs={{0,4},{1,3},{4,8},{5,1},{8,12},{9,5},{12,14},{13,9},{14,10},{15,13... | collective-permute-start | bytes 1572872 | tf_op jit(solution)/shard_map/ppermute | solution.py:263
  94.8 11.1 %collective-permute-start.24 = (bf16[64,4096]{1,0:T(8,128)(2,1)S(1)}, bf16[64,4096]{1,0:T(8,128)(2,1)S(1)}, u32[]{:S(2)}, u32[]{:S(2)}) collective-permute-start(bf16[64,4096]{1,0:T(8,128)(2,1)S(1)} %add_convert_fusion), channel_id=1, source_target_pairs={{0,4},{1,3},{4,8},{5,1},{8,12},{9,5},{12,14},{13,9},{14,10},{15,13... | collective-permute-start | bytes 1572872 | tf_op jit(solution)/shard_map/ppermute | solution.py:263
  98.9 11.2 %collective-permute-start.22 = (bf16[64,4096]{1,0:T(8,128)(2,1)S(1)}, bf16[64,4096]{1,0:T(8,128)(2,1)S(1)}, u32[]{:S(2)}, u32[]{:S(2)}) collective-permute-start(bf16[64,4096]{1,0:T(8,128)(2,1)S(1)} %collective-permute-done.20.refs_0_), channel_id=1, source_target_pairs={{0,4},{1,3},{4,8},{5,1},{8,12},{9,5},{12,14},{13,9},{14,10},{15,13... | collective-permute-start | bytes 1572872 | tf_op jit(solution)/shard_map/ppermute | solution.py:263
  106.1 8.8 %collective-permute-start.26 = (bf16[32,4096]{1,0:T(8,128)(2,1)S(1)}, bf16[32,4096]{1,0:T(8,128)(2,1)S(1)}, u32[]{:S(2)}, u32[]{:S(2)}) collective-permute-start(bf16[32,4096]{1,0:T(8,128)(2,1)S(1)} %get-tuple-element.57), channel_id=1, source_target_pairs={{0,4},{1,3},{4,8},{5,1},{8,12},{9,5},{12,14},{13,9},{14,10},{15,13... | collective-permute-start | bytes 786440 | tf_op jit(solution)/shard_map/ppermute | solution.py:263
  107.1 10.3 %collective-permute-start.25 = (bf16[32,4096]{1,0:T(8,128)(2,1)S(1)}, bf16[32,4096]{1,0:T(8,128)(2,1)S(1)}, u32[]{:S(2)}, u32[]{:S(2)}) collective-permute-start(bf16[32,4096]{1,0:T(8,128)(2,1)S(1)} %get-tuple-element.58), channel_id=1, source_target_pairs={{0,4},{1,3},{4,8},{5,1},{8,12},{9,5},{12,14},{13,9},{14,10},{15,13... | collective-permute-start | bytes 786440 | tf_op jit(solution)/shard_map/ppermute | solution.py:263
  114.9 8.1 %collective-permute-start.28 = (bf16[32,4096]{1,0:T(8,128)(2,1)S(1)}, bf16[32,4096]{1,0:T(8,128)(2,1)S(1)}, u32[]{:S(2)}, u32[]{:S(2)}) collective-permute-start(bf16[32,4096]{1,0:T(8,128)(2,1)S(1)} %add_convert_fusion.4), channel_id=1, source_target_pairs={{0,4},{1,3},{4,8},{5,1},{8,12},{9,5},{12,14},{13,9},{14,10},{15,13... | collective-permute-start | bytes 786440 | tf_op jit(solution)/shard_map/ppermute | solution.py:263
  117.4 6.7 %collective-permute-start.27 = (bf16[32,4096]{1,0:T(8,128)(2,1)S(1)}, bf16[32,4096]{1,0:T(8,128)(2,1)S(1)}, u32[]{:S(2)}, u32[]{:S(2)}) collective-permute-start(bf16[32,4096]{1,0:T(8,128)(2,1)S(1)} %add_convert_fusion.6), channel_id=1, source_target_pairs={{0,4},{1,3},{4,8},{5,1},{8,12},{9,5},{12,14},{13,9},{14,10},{15,13... | collective-permute-start | bytes 786440 | tf_op jit(solution)/shard_map/ppermute | solution.py:263
  (8 other events, 17.0 us)

commit v11 on v9

--- a/solution.py
+++ b/solution.py
@@ -21,13 +21,13 @@
 
 HEAD_GROUP = 16
 SUB_HEADS = 4
-SPLIT_HOPS = 2
+PIECES = 2
 LOG2_SCALE = SCORE_SCALE * math.log2(math.e)
 
 
 def attention_kernel(
-    index_ref, q_ref, qr_ref, mine_ref, other_ref, wv_ref, gain_ref, values_ref, up_ref,
-    down_ref, hits_ref, stack_ref, bias_a_ref, bias_b_ref, *, tok,
+    index_ref, q_ref, qr_ref, mine_ref, other_ref, wv_ref, gain_ref, values_ref, normed_ref,
+    up_ref, down_ref, hits_ref, stack_ref, bias_a_ref, bias_b_ref, *, tok,
 ):
     group = pl.program_id(0)
     my_index = index_ref[0]
@@ -111,6 +111,7 @@
         square = jnp.mean(values * values, axis=1, keepdims=True)
         normed = values * lax.rsqrt(square + NORM_EPS) * gain_ref[...]
         normed = normed.astype(jnp.bfloat16)
+        normed_ref[...] = normed
         up_ref[...] = normed[: tok // 2]
         down_ref[...] = normed[tok // 2 :]
 
@@ -131,6 +132,7 @@
             pl.BlockSpec((1, HEADS * VD), lambda g, i: (0, 0)),
         ],
         out_specs=[
+            pl.BlockSpec((tok, HEADS * VD), lambda g, i: (0, 0)),
             pl.BlockSpec((tok, HEADS * VD), lambda g, i: (0, 0)),
             pl.BlockSpec((tok // 2, HEADS * VD), lambda g, i: (0, 0)),
             pl.BlockSpec((tok // 2, HEADS * VD), lambda g, i: (0, 0)),
@@ -149,7 +151,7 @@
     return pl.pallas_call(
         functools.partial(attention_kernel, tok=tok),
         grid_spec=grid_spec,
-        out_shape=[shape, half_shape, half_shape, hits_shape],
+        out_shape=[shape, shape, half_shape, half_shape, hits_shape],
         compiler_params=pltpu.CompilerParams(vmem_limit_bytes=56 << 20),
         cost_estimate=pl.CostEstimate(
             flops=2 * work * (2 * LAT + 2 * ROPE), bytes_accessed=8 << 20, transcendentals=work
@@ -167,10 +169,9 @@
 
 def expert_kernel(
     index_ref, gate_a, up_a, down_a, hits_hbm, gate_hbm, up_hbm, down_hbm, *refs, hop, chips,
-    pieces,
 ):
     *refs, hits_ref, gate_b, up_b, down_b, sems = refs
-    rows_refs, out_refs = refs[:-pieces], refs[-pieces:]
+    rows_refs, out_refs = refs[:-PIECES], refs[-PIECES:]
     pairs = ((hits_hbm, hits_ref), (gate_hbm, gate_b), (up_hbm, up_b), (down_hbm, down_b))
     copies = [
         pltpu.make_async_copy(there, here, sems.at[i]) for i, (there, here) in enumerate(pairs)
@@ -200,20 +201,20 @@
     act_b = hidden(gate_b, up_b)
     copies[3].wait()
     part = part + jnp.dot(kept(act_b), down_b[...], preferred_element_type=jnp.float32)
-    size = part.shape[0] // pieces
+    size = part.shape[0] // PIECES
     for i, out_ref in enumerate(out_refs):
         out_ref[...] = part[i * size : (i + 1) * size]
 
 
-def expert_part(my_index, rows, hits, own, swapped, hop, chips, pieces):
+def expert_part(my_index, rows, hits, own, swapped, hop, chips):
     tok, features = hits.shape[0], rows[0].shape[1]
     units = 2 * own[0].shape[1]
     vmem, anywhere = pl.BlockSpec(memory_space=pltpu.VMEM), pl.BlockSpec(memory_space=pl.ANY)
     return pl.pallas_call(
-        functools.partial(expert_kernel, hop=hop, chips=chips, pieces=pieces),
+        functools.partial(expert_kernel, hop=hop, chips=chips),
         in_specs=[pl.BlockSpec(memory_space=pltpu.SMEM)] + [vmem] * 3 + [anywhere] * 4 + [vmem] * len(rows),
-        out_specs=[vmem] * pieces,
-        out_shape=[jax.ShapeDtypeStruct((tok // pieces, features), jnp.float32)] * pieces,
+        out_specs=[vmem] * PIECES,
+        out_shape=[jax.ShapeDtypeStruct((tok // PIECES, features), jnp.float32)] * PIECES,
         scratch_shapes=[pltpu.VMEM(w.shape, w.dtype) for w in (hits, *swapped)]
         + [pltpu.SemaphoreType.DMA((4,))],
         compiler_params=pltpu.CompilerParams(vmem_limit_bytes=24 << 20),
@@ -236,6 +237,7 @@
         (ring[p] * CORES + core, ring[(p + 1 - 2 * core) % chips] * CORES + core)
         for p in range(chips) for core in range(CORES)
     ]
+    back = [(there, here) for here, there in route]
 
     def from_chip(block, step):
         return lax.ppermute(block, "ctx", [(i, i ^ (step * CORES)) for i in range(n_ctx)])
@@ -250,28 +252,33 @@
 
     own, mine, other = lax.optimization_barrier(((w_gate[0], w_up[0], w_down[0]), mine, other))
     swapped = tuple(lax.ppermute(w, "ctx", siblings) for w in own)
-    values, upper, lower, hits = attention(
+    values, normed, upper, lower, hits = attention(
         my_index, q_nope, q_rope, mine, other, w_value, norm_gain
     )
-    start, swapped = lax.optimization_barrier(((upper, lower), swapped))
+    start, normed, swapped = lax.optimization_barrier(((upper, lower), normed, swapped))
 
     def part_of(rows, hop):
-        pieces = 1 if 0 < hop < chips - SPLIT_HOPS else 2
-        return expert_part(my_index, rows, hits, own, swapped, hop, chips, pieces)
-
-    def move(blocks):
-        return tuple(lax.ppermute(x, "ctx", route) for x in blocks)
+        return expert_part(my_index, rows, hits, own, swapped, hop, chips)
+
+    def move(blocks, way=route):
+        return tuple(lax.ppermute(x, "ctx", way) for x in blocks)
 
     def after(blocks, first):
         return tuple(lax.optimization_barrier((x, first))[0] for x in blocks)
 
-    rows = [start]
-    for hop in range(1, min(4, chips)):
-        last = rows[-1]
-        rows.append(move((jnp.concatenate(last, axis=0),) if hop == 3 else last))
+    rows = {0: start, 1: move(start)}
+    rows[2] = move(rows[1])
+    joined = (jnp.concatenate(rows[2], axis=0),)
+    if chips == 8:
+        rows[7] = move(after((normed,), rows[1][-1]), back)
+        plan = {1: [(6, 7, back)], 2: [(4, 3, route)], 3: [(5, 6, back)]}
+        needs = {2: 7, 4: 6}
+    else:
+        plan = {hop: [(hop + 3, hop + 2, route)] for hop in range(1, chips - 3)}
+        needs = {}
+    rows[3] = move(joined)
+
     def added(part, arrived):
-        if len(part) > len(arrived):
-            arrived = (arrived[0][: tok // 2], arrived[0][tok // 2 :])
         return tuple(x + y.astype(jnp.float32) for x, y in zip(part, arrived))
 
     def rounded(part):
@@ -280,10 +287,13 @@
     sums = rounded(part_of(rows[1], 1))
     for hop in range(1, chips):
         arrived = move(sums)
-        if hop + 3 < chips:
-            rows.append(move(after(rows[hop + 2], sums)))
+        for into, source, way in plan.get(hop, []):
+            rows[into] = move(after(rows[source], sums[0]), way)
         if hop + 1 < chips:
-            sums = rounded(added(part_of(rows[hop + 1], hop + 1), arrived))
+            taken = rows[hop + 1]
+            if hop + 1 in needs:
+                taken = after(taken, rows[needs[hop + 1]][0])
+            sums = rounded(added(part_of(taken, hop + 1), arrived))
     expert_out = jnp.concatenate(added(part_of(after(start, sums), 0), arrived), axis=0)
     gate_weight = gate_fixed.astype(jnp.float32) / 65536.0
     return (values.astype(jnp.float32) + gate_weight * expert_out).astype(jnp.bfloat16)

time: 124 us -> 125 us (level)
  waiting for transfers between devices: 28.1 us -> 22.9 us
  starting transfers between devices: 41.7 us -> 46.7 us
    ppermute x18 -> x23, waiting for transfers between devices: 21.4 us -> 16.3 us  [move(): return tuple((lax.ppermute(x, 'ctx', way) for x in blocks))]
    ppermute x18 -> x23, starting transfers between devices: 29.6 us -> 34.6 us  [move(): return tuple((lax.ppermute(x, 'ctx', way) for x in blocks))]
  transfers between devices with their start and end apart: 29 -> 34, of which waited for: 15 -> 17; matrix products, arithmetic and copies ran while one was open for 1% -> 1% of each run, Pallas kernels for 40% -> 40%
where the time goes in v11:
time: 125 us
  Pallas kernels  49.3 us (39%)
  starting transfers between devices  46.7 us (37%)
  waiting for transfers between devices  22.9 us (18%)
  other arithmetic  3.35 us (3%)
  local copies, waits for them, and re-layouts  2.1 us (2%)
    pallas_call x8, Pallas kernels, expert_part(): pl.pallas_call(functools.partial(expert_kernel, hop=hop, chips=chips), in...  37.5 us
    ppermute x23, starting transfers between devices, move(): return tuple((lax.ppermute(x, 'ctx', way) for x in blocks))  34.6 us
    ppermute x23, waiting for transfers between devices, move(): return tuple((lax.ppermute(x, 'ctx', way) for x in blocks))  16.3 us
    pallas_call x1, Pallas kernels, attention(): pl.pallas_call(functools.partial(attention_kernel, tok=tok), grid_spec=gr...  11.8 us
    ppermute x7, starting transfers between devices, from_chip(): lax.ppermute(block, 'ctx', [(i, i ^ step * CORES) for i in range(n_ctx)])  11.4 us
    ppermute x7, waiting for transfers between devices, from_chip(): lax.ppermute(block, 'ctx', [(i, i ^ step * CORES) for i in range(n_ctx)])  4.54 us
  transfers between devices with their start and end apart: 34, of which 17 were waited for; matrix products, arithmetic and copies ran while one was open for 1% of the time, Pallas kernels for 40%

profile of v11, /device:TPU:0, one launch (start us, length us, event | category | flops | bytes accessed | tf_op | source)
XLA Modules:
  0.0 124.6 jit_solution(7650673878749483988)
XLA Ops:
  1.7 4.1 %collective-permute-start.3 = (bf16[64,640]{1,0:T(8,128)(2,1)S(1)}, bf16[64,640]{1,0:T(8,128)(2,1)S(1)}, u32[]{:S(2)}, u32[]{:S(2)}) collective-permute-start(bf16[64,640]{1,0:T(8,128)(2,1)S(1)} %get-tuple-element.87), channel_id=1, source_target_pairs={{0,8},{1,9},{2,10},{3,11},{4,12},{5,13},{6,14},{7,15},{8,0},{9,1},... | collective-permute-start | bytes 245768 | tf_op jit(solution)/shard_map/ppermute | solution.py:243
  5.8 1.5 %collective-permute-start = (bf16[64,640]{1,0:T(8,128)(2,1)S(1)}, bf16[64,640]{1,0:T(8,128)(2,1)S(1)}, u32[]{:S(2)}, u32[]{:S(2)}) collective-permute-start(bf16[64,640]{1,0:T(8,128)(2,1)S(1)} %get-tuple-element.87), channel_id=1, source_target_pairs={{0,2},{1,3},{2,0},{3,1},{4,6},{5,7},{6,4},{7,5},{8,10},{9,11},{10,... | collective-permute-start | bytes 245768 | tf_op jit(solution)/shard_map/ppermute | solution.py:243
  7.3 1.6 %collective-permute-start.1 = (bf16[64,640]{1,0:T(8,128)(2,1)S(1)}, bf16[64,640]{1,0:T(8,128)(2,1)S(1)}, u32[]{:S(2)}, u32[]{:S(2)}) collective-permute-start(bf16[64,640]{1,0:T(8,128)(2,1)S(1)} %get-tuple-element.87), channel_id=1, source_target_pairs={{0,4},{1,5},{2,6},{3,7},{4,0},{5,1},{6,2},{7,3},{8,12},{9,13},{10,... | collective-permute-start | bytes 245768 | tf_op jit(solution)/shard_map/ppermute | solution.py:243
  9.8 1.6 %collective-permute-start.4 = (bf16[64,640]{1,0:T(8,128)(2,1)S(1)}, bf16[64,640]{1,0:T(8,128)(2,1)S(1)}, u32[]{:S(2)}, u32[]{:S(2)}) collective-permute-start(bf16[64,640]{1,0:T(8,128)(2,1)S(1)} %collective-permute-done.3), channel_id=1, source_target_pairs={{0,2},{1,3},{2,0},{3,1},{4,6},{5,7},{6,4},{7,5},{8,10},{9,11},{10,... | collective-permute-start | bytes 245768 | tf_op jit(solution)/shard_map/ppermute | solution.py:243
  15.9 1.8 %collective-permute-done.6 = bf16[64,640]{1,0:T(8,128)(2,1)S(1)} collective-permute-done((bf16[64,640]{1,0:T(8,128)(2,1)S(1)}, bf16[64,640]{1,0:T(8,128)(2,1)S(1)}, u32[]{:S(2)}, u32[]{:S(2)}) %collective-permute-start.6) | collective-permute-done | bytes 81952 | tf_op jit(solution)/shard_map/ppermute | solution.py:243
  17.8 2.1 %collective-permute-done.7.other_ref = bf16[512,640]{1,0:T(8,128)(2,1)S(1)} collective-permute-done((bf16[512,640]{1,0:T(8,128)(2,1)S(1)}, bf16[512,640]{1,0:T(8,128)(2,1)S(1)}, u32[]{:S(2)}, u32[]{:S(2)}) %collective-permute-start.7) | collective-permute-done | bytes 655392 | tf_op jit(solution)/shard_map/ppermute | solution.py:251
  20.8 11.8 %shard_map.109 = (bf16[64,4096]{1,0:T(8,128)(2,1)}, bf16[64,4096]{1,0:T(8,128)(2,1)}, bf16[32,4096]{1,0:T(8,128)(2,1)}, bf16[32,4096]{1,0:T(8,128)(2,1)}, f32[64,8]{1,0:T(8,128)}) custom-call(s32[1]{0:T(128)} %bitcast.index_ref, bf16[64,16384]{1,0:T(8,128)(2,1)} %q_ref.1, bf16[64,2048]{1,0:T(8,128)(2,1)} %qr_ref.1, bf16[512,640]{1,0:T(8,128)(2,1)} %copy-done.8, ...), custom_call_target="tpu_custom_call" | custom-call | flops 4831838208 | bytes 8388608 | tf_op jit(solution)/shard_map/pallas_call | solution.py:151
  33.7 2.7 %collective-permute-start.13 = (bf16[32,4096]{1,0:T(8,128)(2,1)}, bf16[32,4096]{1,0:T(8,128)(2,1)S(1)}, u32[]{:S(2)}, u32[]{:S(2)}) collective-permute-start(bf16[32,4096]{1,0:T(8,128)(2,1)} %get-tuple-element.83.refs_0_), channel_id=1, source_target_pairs={{0,4},{1,3},{4,8},{5,1},{8,12},{9,5},{12,14},{13,9},{14,10},{15,13... | collective-permute-start | bytes 786440 | tf_op jit(solution)/shard_map/ppermute | solution.py:264
  36.5 2.8 %collective-permute-done.11.refs_1_ = bf16[32,4096]{1,0:T(8,128)(2,1)S(1)} collective-permute-done((bf16[32,4096]{1,0:T(8,128)(2,1)}, bf16[32,4096]{1,0:T(8,128)(2,1)S(1)}, u32[]{:S(2)}, u32[]{:S(2)}) %collective-permute-start.11) | collective-permute-done | bytes 262176 | tf_op jit(solution)/shard_map/ppermute | solution.py:264
  44.9 4.7 %shard_map.111 = (f32[32,4096]{1,0:T(8,128)S(1)}, f32[32,4096]{1,0:T(8,128)S(1)}) custom-call(s32[1]{0:T(128)} %bitcast.index_ref, bf16[4096,256]{1,0:T(8,128)(2,1)S(1)} %bitcast.10, bf16[4096,256]{1,0:T(8,128)(2,1)S(1)} %bitcast.19, bf16[256,4096]{1,0:T(8,128)(2,1)S(1)} %bitcast.28, f32[64,8]{1,0:T(8,128)S(1)} %copy-done.3, ...), custom_call_target="tpu_custom_call" | custom-call | flops 805306368 | bytes 14680064 | tf_op jit(solution)/shard_map/pallas_call | solution.py:213
  49.6 1.9 %collective-permute-start.26 = (bf16[32,4096]{1,0:T(8,128)(2,1)S(1)}, bf16[32,4096]{1,0:T(8,128)(2,1)S(1)}, u32[]{:S(2)}, u32[]{:S(2)}) collective-permute-start(bf16[32,4096]{1,0:T(8,128)(2,1)S(1)} %convert_element_type.112), channel_id=1, source_target_pairs={{0,4},{1,3},{4,8},{5,1},{8,12},{9,5},{12,14},{13,9},{14,10},{15,13... | collective-permute-start | bytes 786440 | tf_op jit(solution)/shard_map/ppermute | solution.py:264
  51.5 2.1 %collective-permute-start.18 = (bf16[32,4096]{1,0:T(8,128)(2,1)S(1)}, bf16[32,4096]{1,0:T(8,128)(2,1)S(1)}, u32[]{:S(2)}, u32[]{:S(2)}) collective-permute-start(bf16[32,4096]{1,0:T(8,128)(2,1)S(1)} %convert_element_type.99), channel_id=1, source_target_pairs={{0,4},{1,3},{4,8},{5,1},{8,12},{9,5},{12,14},{13,9},{14,10},{15,13... | collective-permute-start | bytes 786440 | tf_op jit(solution)/shard_map/ppermute | solution.py:264
  55.1 4.7 %shard_map.114 = (f32[32,4096]{1,0:T(8,128)S(1)}, f32[32,4096]{1,0:T(8,128)S(1)}) custom-call(s32[1]{0:T(128)} %bitcast.index_ref, bf16[4096,256]{1,0:T(8,128)(2,1)S(1)} %bitcast.11, bf16[4096,256]{1,0:T(8,128)(2,1)S(1)} %bitcast.20, bf16[256,4096]{1,0:T(8,128)(2,1)S(1)} %bitcast.29, f32[64,8]{1,0:T(8,128)S(1)} %copy-done.3, ...), custom_call_target="tpu_custom_call" | custom-call | flops 805306368 | bytes 14680064 | tf_op jit(solution)/shard_map/pallas_call | solution.py:213
  59.8 2.4 %collective-permute-start.19 = (bf16[32,4096]{1,0:T(8,128)(2,1)S(1)}, bf16[32,4096]{1,0:T(8,128)(2,1)S(1)}, u32[]{:S(2)}, u32[]{:S(2)}) collective-permute-start(bf16[32,4096]{1,0:T(8,128)(2,1)S(1)} %add_convert_fusion.11), channel_id=1, source_target_pairs={{0,4},{1,3},{4,8},{5,1},{8,12},{9,5},{12,14},{13,9},{14,10},{15,13... | collective-permute-start | bytes 786440 | tf_op jit(solution)/shard_map/ppermute | solution.py:264
  62.2 1.4 %collective-permute-start.27 = (bf16[32,4096]{1,0:T(8,128)(2,1)S(1)}, bf16[32,4096]{1,0:T(8,128)(2,1)S(1)}, u32[]{:S(2)}, u32[]{:S(2)}) collective-permute-start(bf16[32,4096]{1,0:T(8,128)(2,1)S(1)} %add_convert_fusion.5), channel_id=1, source_target_pairs={{0,4},{1,3},{4,8},{5,1},{8,12},{9,5},{12,14},{13,9},{14,10},{15,13... | collective-permute-start | bytes 786440 | tf_op jit(solution)/shard_map/ppermute | solution.py:264
  64.3 4.7 %shard_map.110 = (f32[32,4096]{1,0:T(8,128)S(1)}, f32[32,4096]{1,0:T(8,128)S(1)}) custom-call(s32[1]{0:T(128)} %bitcast.index_ref, bf16[4096,256]{1,0:T(8,128)(2,1)S(1)} %bitcast.12, bf16[4096,256]{1,0:T(8,128)(2,1)S(1)} %bitcast.21, bf16[256,4096]{1,0:T(8,128)(2,1)S(1)} %bitcast.30, f32[64,8]{1,0:T(8,128)S(1)} %copy-done.3, ...), custom_call_target="tpu_custom_call" | custom-call | flops 805306368 | bytes 14680064 | tf_op jit(solution)/shard_map/pallas_call | solution.py:213
  69.0 1.6 %collective-permute-start.21 = (bf16[64,4096]{1,0:T(8,128)(2,1)S(1)}, bf16[64,4096]{1,0:T(8,128)(2,1)S(1)}, u32[]{:S(2)}, u32[]{:S(2)}) collective-permute-start(bf16[64,4096]{1,0:T(8,128)(2,1)S(1)} %collective-permute-done.17.refs_0_), channel_id=1, source_target_pairs={{0,4},{1,3},{4,8},{5,1},{8,12},{9,5},{12,14},{13,9},{14,10},{15,13... | collective-permute-start | bytes 1572872 | tf_op jit(solution)/shard_map/ppermute | solution.py:264
  70.6 4.7 %shard_map.113 = (f32[32,4096]{1,0:T(8,128)S(1)}, f32[32,4096]{1,0:T(8,128)S(1)}) custom-call(s32[1]{0:T(128)} %bitcast.index_ref, bf16[4096,256]{1,0:T(8,128)(2,1)S(1)} %bitcast.13, bf16[4096,256]{1,0:T(8,128)(2,1)S(1)} %bitcast.22, bf16[256,4096]{1,0:T(8,128)(2,1)S(1)} %bitcast.31, f32[64,8]{1,0:T(8,128)S(1)} %copy-done.3, ...), custom_call_target="tpu_custom_call" | custom-call | flops 805306368 | bytes 14680064 | tf_op jit(solution)/shard_map/pallas_call | solution.py:213
  79.2 4.7 %shard_map.112 = (f32[32,4096]{1,0:T(8,128)S(1)}, f32[32,4096]{1,0:T(8,128)S(1)}) custom-call(s32[1]{0:T(128)} %bitcast.index_ref, bf16[4096,256]{1,0:T(8,128)(2,1)S(1)} %bitcast.14, bf16[4096,256]{1,0:T(8,128)(2,1)S(1)} %bitcast.23, bf16[256,4096]{1,0:T(8,128)(2,1)S(1)} %bitcast.32, f32[64,8]{1,0:T(8,128)S(1)} %copy-done.3, ...), custom_call_target="tpu_custom_call" | custom-call | flops 805306368 | bytes 14680064 | tf_op jit(solution)/shard_map/pallas_call | solution.py:213
  83.9 1.8 %collective-permute-done.21.refs_0_ = bf16[64,4096]{1,0:T(8,128)(2,1)S(1)} collective-permute-done((bf16[64,4096]{1,0:T(8,128)(2,1)S(1)}, bf16[64,4096]{1,0:T(8,128)(2,1)S(1)}, u32[]{:S(2)}, u32[]{:S(2)}) %collective-permute-start.21) | collective-permute-done | bytes 524320 | tf_op jit(solution)/shard_map/ppermute | solution.py:264
  85.7 4.7 %shard_map.116 = (f32[32,4096]{1,0:T(8,128)S(1)}, f32[32,4096]{1,0:T(8,128)S(1)}) custom-call(s32[1]{0:T(128)} %bitcast.index_ref, bf16[4096,256]{1,0:T(8,128)(2,1)S(1)} %bitcast.15, bf16[4096,256]{1,0:T(8,128)(2,1)S(1)} %bitcast.24, bf16[256,4096]{1,0:T(8,128)(2,1)S(1)} %bitcast.33, f32[64,8]{1,0:T(8,128)S(1)} %copy-done.3, ...), custom_call_target="tpu_custom_call" | custom-call | flops 805306368 | bytes 14680064 | tf_op jit(solution)/shard_map/pallas_call | solution.py:213
  90.6 2.4 %collective-permute-start.23 = (bf16[32,4096]{1,0:T(8,128)(2,1)S(1)}, bf16[32,4096]{1,0:T(8,128)(2,1)S(1)}, u32[]{:S(2)}, u32[]{:S(2)}) collective-permute-start(bf16[32,4096]{1,0:T(8,128)(2,1)S(1)} %add_convert_fusion.9), channel_id=1, source_target_pairs={{0,4},{1,3},{4,8},{5,1},{8,12},{9,5},{12,14},{13,9},{14,10},{15,13... | collective-permute-start | bytes 786440 | tf_op jit(solution)/shard_map/ppermute | solution.py:264
  93.4 2.2 %collective-permute-start.29 = (bf16[32,4096]{1,0:T(8,128)(2,1)S(1)}, bf16[32,4096]{1,0:T(8,128)(2,1)S(1)}, u32[]{:S(2)}, u32[]{:S(2)}) collective-permute-start(bf16[32,4096]{1,0:T(8,128)(2,1)S(1)} %add_convert_fusion.3), channel_id=1, source_target_pairs={{0,4},{1,3},{4,8},{5,1},{8,12},{9,5},{12,14},{13,9},{14,10},{15,13... | collective-permute-start | bytes 786440 | tf_op jit(solution)/shard_map/ppermute | solution.py:264
  95.6 4.7 %shard_map.115 = (f32[32,4096]{1,0:T(8,128)S(1)}, f32[32,4096]{1,0:T(8,128)S(1)}) custom-call(s32[1]{0:T(128)} %bitcast.index_ref, bf16[4096,256]{1,0:T(8,128)(2,1)S(1)} %bitcast.16, bf16[4096,256]{1,0:T(8,128)(2,1)S(1)} %bitcast.25, bf16[256,4096]{1,0:T(8,128)(2,1)S(1)} %bitcast.34, f32[64,8]{1,0:T(8,128)S(1)} %copy-done.3, ...), custom_call_target="tpu_custom_call" | custom-call | flops 805306368 | bytes 14680064 | tf_op jit(solution)/shard_map/pallas_call | solution.py:213
  100.4 1.7 %collective-permute-start.24 = (bf16[32,4096]{1,0:T(8,128)(2,1)S(1)}, bf16[32,4096]{1,0:T(8,128)(2,1)S(1)}, u32[]{:S(2)}, u32[]{:S(2)}) collective-permute-start(bf16[32,4096]{1,0:T(8,128)(2,1)S(1)} %add_convert_fusion.8), channel_id=1, source_target_pairs={{0,4},{1,3},{4,8},{5,1},{8,12},{9,5},{12,14},{13,9},{14,10},{15,13... | collective-permute-start | bytes 786440 | tf_op jit(solution)/shard_map/ppermute | solution.py:264
  102.6 4.2 %collective-permute-done.24 = bf16[32,4096]{1,0:T(8,128)(2,1)S(1)} collective-permute-done((bf16[32,4096]{1,0:T(8,128)(2,1)S(1)}, bf16[32,4096]{1,0:T(8,128)(2,1)S(1)}, u32[]{:S(2)}, u32[]{:S(2)}) %collective-permute-start.24) | collective-permute-done | bytes 262176 | tf_op jit(solution)/shard_map/ppermute | solution.py:264
  106.9 1.7 %collective-permute-start.25 = (bf16[32,4096]{1,0:T(8,128)(2,1)S(1)}, bf16[32,4096]{1,0:T(8,128)(2,1)S(1)}, u32[]{:S(2)}, u32[]{:S(2)}) collective-permute-start(bf16[32,4096]{1,0:T(8,128)(2,1)S(1)} %add_convert_fusion.7), channel_id=1, source_target_pairs={{0,4},{1,3},{4,8},{5,1},{8,12},{9,5},{12,14},{13,9},{14,10},{15,13... | collective-permute-start | bytes 786440 | tf_op jit(solution)/shard_map/ppermute | solution.py:264
  109.7 1.7 %collective-permute-start.31 = (bf16[32,4096]{1,0:T(8,128)(2,1)S(1)}, bf16[32,4096]{1,0:T(8,128)(2,1)S(1)}, u32[]{:S(2)}, u32[]{:S(2)}) collective-permute-start(bf16[32,4096]{1,0:T(8,128)(2,1)S(1)} %add_convert_fusion.1), channel_id=1, source_target_pairs={{0,4},{1,3},{4,8},{5,1},{8,12},{9,5},{12,14},{13,9},{14,10},{15,13... | collective-permute-start | bytes 786440 | tf_op jit(solution)/shard_map/ppermute | solution.py:264
  111.4 1.9 %collective-permute-done.25 = bf16[32,4096]{1,0:T(8,128)(2,1)S(1)} collective-permute-done((bf16[32,4096]{1,0:T(8,128)(2,1)S(1)}, bf16[32,4096]{1,0:T(8,128)(2,1)S(1)}, u32[]{:S(2)}, u32[]{:S(2)}) %collective-permute-start.25) | collective-permute-done | bytes 262176 | tf_op jit(solution)/shard_map/ppermute | solution.py:264
  113.3 1.7 %collective-permute-start.32 = (bf16[32,4096]{1,0:T(8,128)(2,1)S(1)}, bf16[32,4096]{1,0:T(8,128)(2,1)S(1)}, u32[]{:S(2)}, u32[]{:S(2)}) collective-permute-start(bf16[32,4096]{1,0:T(8,128)(2,1)S(1)} %add_convert_fusion.6), channel_id=1, source_target_pairs={{0,4},{1,3},{4,8},{5,1},{8,12},{9,5},{12,14},{13,9},{14,10},{15,13... | collective-permute-start | bytes 786440 | tf_op jit(solution)/shard_map/ppermute | solution.py:264
  116.1 1.7 %collective-permute-start.33 = (bf16[32,4096]{1,0:T(8,128)(2,1)S(1)}, bf16[32,4096]{1,0:T(8,128)(2,1)S(1)}, u32[]{:S(2)}, u32[]{:S(2)}) collective-permute-start(bf16[32,4096]{1,0:T(8,128)(2,1)S(1)} %add_convert_fusion), channel_id=1, source_target_pairs={{0,4},{1,3},{4,8},{5,1},{8,12},{9,5},{12,14},{13,9},{14,10},{15,13... | collective-permute-start | bytes 786440 | tf_op jit(solution)/shard_map/ppermute | solution.py:264
  117.9 4.7 %shard_map.117 = (f32[32,4096]{1,0:T(8,128)S(1)}, f32[32,4096]{1,0:T(8,128)S(1)}) custom-call(s32[1]{0:T(128)} %bitcast.index_ref, bf16[4096,256]{1,0:T(8,128)(2,1)S(1)} %bitcast.17, bf16[4096,256]{1,0:T(8,128)(2,1)S(1)} %bitcast.26, bf16[256,4096]{1,0:T(8,128)(2,1)S(1)} %bitcast.35, f32[64,8]{1,0:T(8,128)S(1)} %copy-done.4, ...), custom_call_target="tpu_custom_call" | custom-call | flops 805306368 | bytes 14680064 | tf_op jit(solution)/shard_map/pallas_call | solution.py:213
  (96 shorter events, 26.4 us)
Async XLA Ops:
  1.7 8.1 %collective-permute-start.3 = (bf16[64,640]{1,0:T(8,128)(2,1)S(1)}, bf16[64,640]{1,0:T(8,128)(2,1)S(1)}, u32[]{:S(2)}, u32[]{:S(2)}) collective-permute-start(bf16[64,640]{1,0:T(8,128)(2,1)S(1)} %get-tuple-element.87), channel_id=1, source_target_pairs={{0,8},{1,9},{2,10},{3,11},{4,12},{5,13},{6,14},{7,15},{8,0},{9,1},... | collective-permute-start | bytes 245768 | tf_op jit(solution)/shard_map/ppermute | solution.py:243
  5.8 6.6 %collective-permute-start = (bf16[64,640]{1,0:T(8,128)(2,1)S(1)}, bf16[64,640]{1,0:T(8,128)(2,1)S(1)}, u32[]{:S(2)}, u32[]{:S(2)}) collective-permute-start(bf16[64,640]{1,0:T(8,128)(2,1)S(1)} %get-tuple-element.87), channel_id=1, source_target_pairs={{0,2},{1,3},{2,0},{3,1},{4,6},{5,7},{6,4},{7,5},{8,10},{9,11},{10,... | collective-permute-start | bytes 245768 | tf_op jit(solution)/shard_map/ppermute | solution.py:243
  7.3 6.3 %collective-permute-start.1 = (bf16[64,640]{1,0:T(8,128)(2,1)S(1)}, bf16[64,640]{1,0:T(8,128)(2,1)S(1)}, u32[]{:S(2)}, u32[]{:S(2)}) collective-permute-start(bf16[64,640]{1,0:T(8,128)(2,1)S(1)} %get-tuple-element.87), channel_id=1, source_target_pairs={{0,4},{1,5},{2,6},{3,7},{4,0},{5,1},{6,2},{7,3},{8,12},{9,13},{10,... | collective-permute-start | bytes 245768 | tf_op jit(solution)/shard_map/ppermute | solution.py:243
  8.9 5.6 %collective-permute-start.2 = (bf16[64,640]{1,0:T(8,128)(2,1)S(1)}, bf16[64,640]{1,0:T(8,128)(2,1)S(1)}, u32[]{:S(2)}, u32[]{:S(2)}) collective-permute-start(bf16[64,640]{1,0:T(8,128)(2,1)S(1)} %get-tuple-element.87), channel_id=1, source_target_pairs={{0,6},{1,7},{2,4},{3,5},{4,2},{5,3},{6,0},{7,1},{8,14},{9,15},{10,... | collective-permute-start | bytes 245768 | tf_op jit(solution)/shard_map/ppermute | solution.py:243
  9.8 5.5 %collective-permute-start.4 = (bf16[64,640]{1,0:T(8,128)(2,1)S(1)}, bf16[64,640]{1,0:T(8,128)(2,1)S(1)}, u32[]{:S(2)}, u32[]{:S(2)}) collective-permute-start(bf16[64,640]{1,0:T(8,128)(2,1)S(1)} %collective-permute-done.3), channel_id=1, source_target_pairs={{0,2},{1,3},{2,0},{3,1},{4,6},{5,7},{6,4},{7,5},{8,10},{9,11},{10,... | collective-permute-start | bytes 245768 | tf_op jit(solution)/shard_map/ppermute | solution.py:243
  12.4 5.3 %collective-permute-start.6 = (bf16[64,640]{1,0:T(8,128)(2,1)S(1)}, bf16[64,640]{1,0:T(8,128)(2,1)S(1)}, u32[]{:S(2)}, u32[]{:S(2)}) collective-permute-start(bf16[64,640]{1,0:T(8,128)(2,1)S(1)} %collective-permute-done.3), channel_id=1, source_target_pairs={{0,6},{1,7},{2,4},{3,5},{4,2},{5,3},{6,0},{7,1},{8,14},{9,15},{10,... | collective-permute-start | bytes 245768 | tf_op jit(solution)/shard_map/ppermute | solution.py:243
  19.9 12.7 %collective-permute-start.10 = (bf16[256,4096]{1,0:T(8,128)(2,1)}, bf16[256,4096]{1,0:T(8,128)(2,1)}, u32[]{:S(2)}, u32[]{:S(2)}) collective-permute-start(bf16[256,4096]{1,0:T(8,128)(2,1)} %bitcast.27), channel_id=1, source_target_pairs={{0,1},{1,0},{2,3},{3,2},{4,5},{5,4},{6,7},{7,6},{8,9},{9,8},{10,11... | collective-permute-start | bytes 6291464 | tf_op jit(solution)/shard_map/ppermute | solution.py:254
  20.0 12.6 %collective-permute-start.8 = (bf16[4096,256]{1,0:T(8,128)(2,1)}, bf16[4096,256]{1,0:T(8,128)(2,1)}, u32[]{:S(2)}, u32[]{:S(2)}) collective-permute-start(bf16[4096,256]{1,0:T(8,128)(2,1)} %bitcast.9), channel_id=1, source_target_pairs={{0,1},{1,0},{2,3},{3,2},{4,5},{5,4},{6,7},{7,6},{8,9},{9,8},{10,11... | collective-permute-start | bytes 6291464 | tf_op jit(solution)/shard_map/ppermute | solution.py:254
  20.4 12.2 %collective-permute-start.9 = (bf16[4096,256]{1,0:T(8,128)(2,1)}, bf16[4096,256]{1,0:T(8,128)(2,1)}, u32[]{:S(2)}, u32[]{:S(2)}) collective-permute-start(bf16[4096,256]{1,0:T(8,128)(2,1)} %bitcast.18), channel_id=1, source_target_pairs={{0,1},{1,0},{2,3},{3,2},{4,5},{5,4},{6,7},{7,6},{8,9},{9,8},{10,11... | collective-permute-start | bytes 6291464 | tf_op jit(solution)/shard_map/ppermute | solution.py:254
  32.6 6.6 %collective-permute-start.11 = (bf16[32,4096]{1,0:T(8,128)(2,1)}, bf16[32,4096]{1,0:T(8,128)(2,1)S(1)}, u32[]{:S(2)}, u32[]{:S(2)}) collective-permute-start(bf16[32,4096]{1,0:T(8,128)(2,1)} %get-tuple-element.84.refs_1_), channel_id=1, source_target_pairs={{0,4},{1,3},{4,8},{5,1},{8,12},{9,5},{12,14},{13,9},{14,10},{15,13... | collective-permute-start | bytes 786440 | tf_op jit(solution)/shard_map/ppermute | solution.py:264
  33.7 8.3 %collective-permute-start.13 = (bf16[32,4096]{1,0:T(8,128)(2,1)}, bf16[32,4096]{1,0:T(8,128)(2,1)S(1)}, u32[]{:S(2)}, u32[]{:S(2)}) collective-permute-start(bf16[32,4096]{1,0:T(8,128)(2,1)} %get-tuple-element.83.refs_0_), channel_id=1, source_target_pairs={{0,4},{1,3},{4,8},{5,1},{8,12},{9,5},{12,14},{13,9},{14,10},{15,13... | collective-permute-start | bytes 786440 | tf_op jit(solution)/shard_map/ppermute | solution.py:264
  39.2 14.3 %collective-permute-start.16 = (bf16[32,4096]{1,0:T(8,128)(2,1)S(1)}, bf16[32,4096]{1,0:T(8,128)(2,1)S(1)}, u32[]{:S(2)}, u32[]{:S(2)}) collective-permute-start(bf16[32,4096]{1,0:T(8,128)(2,1)S(1)} %collective-permute-done.11.refs_1_), channel_id=1, source_target_pairs={{0,4},{1,3},{4,8},{5,1},{8,12},{9,5},{12,14},{13,9},{14,10},{15,13... | collective-permute-start | bytes 786440 | tf_op jit(solution)/shard_map/ppermute | solution.py:264
  42.1 11.5 %collective-permute-start.15 = (bf16[32,4096]{1,0:T(8,128)(2,1)S(1)}, bf16[32,4096]{1,0:T(8,128)(2,1)S(1)}, u32[]{:S(2)}, u32[]{:S(2)}) collective-permute-start(bf16[32,4096]{1,0:T(8,128)(2,1)S(1)} %collective-permute-done.13.refs_0_), channel_id=1, source_target_pairs={{0,4},{1,3},{4,8},{5,1},{8,12},{9,5},{12,14},{13,9},{14,10},{15,13... | collective-permute-start | bytes 786440 | tf_op jit(solution)/shard_map/ppermute | solution.py:264
  43.5 11.6 %collective-permute-start.12 = (bf16[64,4096]{1,0:T(8,128)(2,1)}, bf16[64,4096]{1,0:T(8,128)(2,1)S(1)}, u32[]{:S(2)}, u32[]{:S(2)}) collective-permute-start(bf16[64,4096]{1,0:T(8,128)(2,1)} %get-tuple-element.62), channel_id=1, source_target_pairs={{4,0},{3,1},{8,4},{1,5},{12,8},{5,9},{14,12},{9,13},{10,14},{13,15... | collective-permute-start | bytes 1572872 | tf_op jit(solution)/shard_map/ppermute | solution.py:264
  49.6 12.6 %collective-permute-start.26 = (bf16[32,4096]{1,0:T(8,128)(2,1)S(1)}, bf16[32,4096]{1,0:T(8,128)(2,1)S(1)}, u32[]{:S(2)}, u32[]{:S(2)}) collective-permute-start(bf16[32,4096]{1,0:T(8,128)(2,1)S(1)} %convert_element_type.112), channel_id=1, source_target_pairs={{0,4},{1,3},{4,8},{5,1},{8,12},{9,5},{12,14},{13,9},{14,10},{15,13... | collective-permute-start | bytes 786440 | tf_op jit(solution)/shard_map/ppermute | solution.py:264
  51.5 8.3 %collective-permute-start.18 = (bf16[32,4096]{1,0:T(8,128)(2,1)S(1)}, bf16[32,4096]{1,0:T(8,128)(2,1)S(1)}, u32[]{:S(2)}, u32[]{:S(2)}) collective-permute-start(bf16[32,4096]{1,0:T(8,128)(2,1)S(1)} %convert_element_type.99), channel_id=1, source_target_pairs={{0,4},{1,3},{4,8},{5,1},{8,12},{9,5},{12,14},{13,9},{14,10},{15,13... | collective-permute-start | bytes 786440 | tf_op jit(solution)/shard_map/ppermute | solution.py:264
  53.6 15.4 %collective-permute-start.17 = (bf16[64,4096]{1,0:T(8,128)(2,1)S(1)}, bf16[64,4096]{1,0:T(8,128)(2,1)S(1)}, u32[]{:S(2)}, u32[]{:S(2)}) collective-permute-start(bf16[64,4096]{1,0:T(8,128)(2,1)S(1)} %pad_maximum_fusion), channel_id=1, source_target_pairs={{0,4},{1,3},{4,8},{5,1},{8,12},{9,5},{12,14},{13,9},{14,10},{15,13... | collective-permute-start | bytes 1572872 | tf_op jit(solution)/shard_map/ppermute | solution.py:264
  59.8 15.5 %collective-permute-start.19 = (bf16[32,4096]{1,0:T(8,128)(2,1)S(1)}, bf16[32,4096]{1,0:T(8,128)(2,1)S(1)}, u32[]{:S(2)}, u32[]{:S(2)}) collective-permute-start(bf16[32,4096]{1,0:T(8,128)(2,1)S(1)} %add_convert_fusion.11), channel_id=1, source_target_pairs={{0,4},{1,3},{4,8},{5,1},{8,12},{9,5},{12,14},{13,9},{14,10},{15,13... | collective-permute-start | bytes 786440 | tf_op jit(solution)/shard_map/ppermute | solution.py:264
  62.2 14.3 %collective-permute-start.27 = (bf16[32,4096]{1,0:T(8,128)(2,1)S(1)}, bf16[32,4096]{1,0:T(8,128)(2,1)S(1)}, u32[]{:S(2)}, u32[]{:S(2)}) collective-permute-start(bf16[32,4096]{1,0:T(8,128)(2,1)S(1)} %add_convert_fusion.5), channel_id=1, source_target_pairs={{0,4},{1,3},{4,8},{5,1},{8,12},{9,5},{12,14},{13,9},{14,10},{15,13... | collective-permute-start | bytes 786440 | tf_op jit(solution)/shard_map/ppermute | solution.py:264
  63.7 14.9 %collective-permute-start.14 = (bf16[64,4096]{1,0:T(8,128)(2,1)S(1)}, bf16[64,4096]{1,0:T(8,128)(2,1)S(1)}, u32[]{:S(2)}, u32[]{:S(2)}) collective-permute-start(bf16[64,4096]{1,0:T(8,128)(2,1)S(1)} %collective-permute-done.12.refs_0_), channel_id=1, source_target_pairs={{4,0},{3,1},{8,4},{1,5},{12,8},{5,9},{14,12},{9,13},{10,14},{13,15... | collective-permute-start | bytes 1572872 | tf_op jit(solution)/shard_map/ppermute | solution.py:264
  69.0 16.6 %collective-permute-start.21 = (bf16[64,4096]{1,0:T(8,128)(2,1)S(1)}, bf16[64,4096]{1,0:T(8,128)(2,1)S(1)}, u32[]{:S(2)}, u32[]{:S(2)}) collective-permute-start(bf16[64,4096]{1,0:T(8,128)(2,1)S(1)} %collective-permute-done.17.refs_0_), channel_id=1, source_target_pairs={{0,4},{1,3},{4,8},{5,1},{8,12},{9,5},{12,14},{13,9},{14,10},{15,13... | collective-permute-start | bytes 1572872 | tf_op jit(solution)/shard_map/ppermute | solution.py:264
  75.4 15.2 %collective-permute-start.22 = (bf16[32,4096]{1,0:T(8,128)(2,1)S(1)}, bf16[32,4096]{1,0:T(8,128)(2,1)S(1)}, u32[]{:S(2)}, u32[]{:S(2)}) collective-permute-start(bf16[32,4096]{1,0:T(8,128)(2,1)S(1)} %add_convert_fusion.10), channel_id=1, source_target_pairs={{0,4},{1,3},{4,8},{5,1},{8,12},{9,5},{12,14},{13,9},{14,10},{15,13... | collective-permute-start | bytes 786440 | tf_op jit(solution)/shard_map/ppermute | solution.py:264
  76.6 16.8 %collective-permute-start.28 = (bf16[32,4096]{1,0:T(8,128)(2,1)S(1)}, bf16[32,4096]{1,0:T(8,128)(2,1)S(1)}, u32[]{:S(2)}, u32[]{:S(2)}) collective-permute-start(bf16[32,4096]{1,0:T(8,128)(2,1)S(1)} %add_convert_fusion.4), channel_id=1, source_target_pairs={{0,4},{1,3},{4,8},{5,1},{8,12},{9,5},{12,14},{13,9},{14,10},{15,13... | collective-permute-start | bytes 786440 | tf_op jit(solution)/shard_map/ppermute | solution.py:264
  78.5 17.1 %collective-permute-start.20 = (bf16[64,4096]{1,0:T(8,128)(2,1)S(1)}, bf16[64,4096]{1,0:T(8,128)(2,1)S(1)}, u32[]{:S(2)}, u32[]{:S(2)}) collective-permute-start(bf16[64,4096]{1,0:T(8,128)(2,1)S(1)} %collective-permute-done.14.refs_0_), channel_id=1, source_target_pairs={{4,0},{3,1},{8,4},{1,5},{12,8},{5,9},{14,12},{9,13},{10,14},{13,15... | collective-permute-start | bytes 1572872 | tf_op jit(solution)/shard_map/ppermute | solution.py:264
  90.6 9.7 %collective-permute-start.23 = (bf16[32,4096]{1,0:T(8,128)(2,1)S(1)}, bf16[32,4096]{1,0:T(8,128)(2,1)S(1)}, u32[]{:S(2)}, u32[]{:S(2)}) collective-permute-start(bf16[32,4096]{1,0:T(8,128)(2,1)S(1)} %add_convert_fusion.9), channel_id=1, source_target_pairs={{0,4},{1,3},{4,8},{5,1},{8,12},{9,5},{12,14},{13,9},{14,10},{15,13... | collective-permute-start | bytes 786440 | tf_op jit(solution)/shard_map/ppermute | solution.py:264
  93.4 8.7 %collective-permute-start.29 = (bf16[32,4096]{1,0:T(8,128)(2,1)S(1)}, bf16[32,4096]{1,0:T(8,128)(2,1)S(1)}, u32[]{:S(2)}, u32[]{:S(2)}) collective-permute-start(bf16[32,4096]{1,0:T(8,128)(2,1)S(1)} %add_convert_fusion.3), channel_id=1, source_target_pairs={{0,4},{1,3},{4,8},{5,1},{8,12},{9,5},{12,14},{13,9},{14,10},{15,13... | collective-permute-start | bytes 786440 | tf_op jit(solution)/shard_map/ppermute | solution.py:264
  100.4 6.4 %collective-permute-start.24 = (bf16[32,4096]{1,0:T(8,128)(2,1)S(1)}, bf16[32,4096]{1,0:T(8,128)(2,1)S(1)}, u32[]{:S(2)}, u32[]{:S(2)}) collective-permute-start(bf16[32,4096]{1,0:T(8,128)(2,1)S(1)} %add_convert_fusion.8), channel_id=1, source_target_pairs={{0,4},{1,3},{4,8},{5,1},{8,12},{9,5},{12,14},{13,9},{14,10},{15,13... | collective-permute-start | bytes 786440 | tf_op jit(solution)/shard_map/ppermute | solution.py:264
  102.2 7.5 %collective-permute-start.30 = (bf16[32,4096]{1,0:T(8,128)(2,1)S(1)}, bf16[32,4096]{1,0:T(8,128)(2,1)S(1)}, u32[]{:S(2)}, u32[]{:S(2)}) collective-permute-start(bf16[32,4096]{1,0:T(8,128)(2,1)S(1)} %add_convert_fusion.2), channel_id=1, source_target_pairs={{0,4},{1,3},{4,8},{5,1},{8,12},{9,5},{12,14},{13,9},{14,10},{15,13... | collective-permute-start | bytes 786440 | tf_op jit(solution)/shard_map/ppermute | solution.py:264
  106.9 6.4 %collective-permute-start.25 = (bf16[32,4096]{1,0:T(8,128)(2,1)S(1)}, bf16[32,4096]{1,0:T(8,128)(2,1)S(1)}, u32[]{:S(2)}, u32[]{:S(2)}) collective-permute-start(bf16[32,4096]{1,0:T(8,128)(2,1)S(1)} %add_convert_fusion.7), channel_id=1, source_target_pairs={{0,4},{1,3},{4,8},{5,1},{8,12},{9,5},{12,14},{13,9},{14,10},{15,13... | collective-permute-start | bytes 786440 | tf_op jit(solution)/shard_map/ppermute | solution.py:264
  109.7 6.4 %collective-permute-start.31 = (bf16[32,4096]{1,0:T(8,128)(2,1)S(1)}, bf16[32,4096]{1,0:T(8,128)(2,1)S(1)}, u32[]{:S(2)}, u32[]{:S(2)}) collective-permute-start(bf16[32,4096]{1,0:T(8,128)(2,1)S(1)} %add_convert_fusion.1), channel_id=1, source_target_pairs={{0,4},{1,3},{4,8},{5,1},{8,12},{9,5},{12,14},{13,9},{14,10},{15,13... | collective-permute-start | bytes 786440 | tf_op jit(solution)/shard_map/ppermute | solution.py:264
  113.3 9.3 %collective-permute-start.32 = (bf16[32,4096]{1,0:T(8,128)(2,1)S(1)}, bf16[32,4096]{1,0:T(8,128)(2,1)S(1)}, u32[]{:S(2)}, u32[]{:S(2)}) collective-permute-start(bf16[32,4096]{1,0:T(8,128)(2,1)S(1)} %add_convert_fusion.6), channel_id=1, source_target_pairs={{0,4},{1,3},{4,8},{5,1},{8,12},{9,5},{12,14},{13,9},{14,10},{15,13... | collective-permute-start | bytes 786440 | tf_op jit(solution)/shard_map/ppermute | solution.py:264
  116.1 6.5 %collective-permute-start.33 = (bf16[32,4096]{1,0:T(8,128)(2,1)S(1)}, bf16[32,4096]{1,0:T(8,128)(2,1)S(1)}, u32[]{:S(2)}, u32[]{:S(2)}) collective-permute-start(bf16[32,4096]{1,0:T(8,128)(2,1)S(1)} %add_convert_fusion), channel_id=1, source_target_pairs={{0,4},{1,3},{4,8},{5,1},{8,12},{9,5},{12,14},{13,9},{14,10},{15,13... | collective-permute-start | bytes 786440 | tf_op jit(solution)/shard_map/ppermute | solution.py:264
  (13 other events, 138.0 us)

commit v12 on v11

--- a/solution.py
+++ b/solution.py
@@ -168,10 +168,11 @@
 
 
 def expert_kernel(
-    index_ref, gate_a, up_a, down_a, hits_hbm, gate_hbm, up_hbm, down_hbm, *refs, hop, chips,
+    index_ref, gate_a, up_a, down_a, hits_hbm, gate_hbm, up_hbm, down_hbm, *refs, hops, chips,
 ):
     *refs, hits_ref, gate_b, up_b, down_b, sems = refs
-    rows_refs, out_refs = refs[:-PIECES], refs[-PIECES:]
+    outs = PIECES * len(hops)
+    rows_refs, out_refs = refs[:-outs], refs[-outs:]
     pairs = ((hits_hbm, hits_ref), (gate_hbm, gate_b), (up_hbm, up_b), (down_hbm, down_b))
     copies = [
         pltpu.make_async_copy(there, here, sems.at[i]) for i, (there, here) in enumerate(pairs)
@@ -179,9 +180,13 @@
     for copy in copies:
         copy.start()
     my_chip, my_core = index_ref[0] // CORES, lax.rem(index_ref[0], CORES)
-    place = ring_place(my_chip, chips) + chips + hop * (2 * my_core - 1)
-    source = ring_chip(lax.rem(place, chips), chips) ^ my_chip
     rows = jnp.concatenate([ref[...] for ref in rows_refs], axis=0)
+
+    def hit(hop):
+        place = ring_place(my_chip, chips) + chips + hop * (2 * my_core - 1)
+        source = ring_chip(lax.rem(place, chips), chips) ^ my_chip
+        column = lax.broadcasted_iota(jnp.int32, hits_ref.shape, 1)
+        return jnp.max(jnp.where(column == source, hits_ref[...], 0.0), axis=1, keepdims=True)
 
     def hidden(gate_ref, up_ref):
         gate_act = jnp.dot(rows, gate_ref[...], preferred_element_type=jnp.float32)
@@ -193,35 +198,37 @@
 
     act_a = hidden(gate_a, up_a)
     copies[0].wait()
-    column = lax.broadcasted_iota(jnp.int32, hits_ref.shape, 1)
-    keep = jnp.max(jnp.where(column == source, hits_ref[...], 0.0), axis=1, keepdims=True) > 0.0
+    keep = jnp.concatenate([hit(hop) for hop in hops], axis=0) > 0.0
     part = jnp.dot(kept(act_a), down_a[...], preferred_element_type=jnp.float32)
     copies[1].wait()
     copies[2].wait()
     act_b = hidden(gate_b, up_b)
     copies[3].wait()
     part = part + jnp.dot(kept(act_b), down_b[...], preferred_element_type=jnp.float32)
-    size = part.shape[0] // PIECES
+    size = part.shape[0] // outs
     for i, out_ref in enumerate(out_refs):
         out_ref[...] = part[i * size : (i + 1) * size]
 
 
-def expert_part(my_index, rows, hits, own, swapped, hop, chips):
+def expert_parts(my_index, rows, hits, own, swapped, hops, chips):
     tok, features = hits.shape[0], rows[0].shape[1]
     units = 2 * own[0].shape[1]
+    outs = PIECES * len(hops)
     vmem, anywhere = pl.BlockSpec(memory_space=pltpu.VMEM), pl.BlockSpec(memory_space=pl.ANY)
-    return pl.pallas_call(
-        functools.partial(expert_kernel, hop=hop, chips=chips),
-        in_specs=[pl.BlockSpec(memory_space=pltpu.SMEM)] + [vmem] * 3 + [anywhere] * 4 + [vmem] * len(rows),
-        out_specs=[vmem] * PIECES,
-        out_shape=[jax.ShapeDtypeStruct((tok // PIECES, features), jnp.float32)] * PIECES,
+    parts = pl.pallas_call(
+        functools.partial(expert_kernel, hops=hops, chips=chips),
+        in_specs=[pl.BlockSpec(memory_space=pltpu.SMEM)]
+        + [vmem] * 3 + [anywhere] * 4 + [vmem] * len(rows),
+        out_specs=[vmem] * outs,
+        out_shape=[jax.ShapeDtypeStruct((tok // PIECES, features), jnp.float32)] * outs,
         scratch_shapes=[pltpu.VMEM(w.shape, w.dtype) for w in (hits, *swapped)]
         + [pltpu.SemaphoreType.DMA((4,))],
-        compiler_params=pltpu.CompilerParams(vmem_limit_bytes=24 << 20),
+        compiler_params=pltpu.CompilerParams(vmem_limit_bytes=28 << 20),
         cost_estimate=pl.CostEstimate(
             flops=6 * tok * features * units, bytes_accessed=14 << 20, transcendentals=0
         ),
     )(my_index.reshape(1), *own, hits, *swapped, *rows)
+    return [tuple(parts[i : i + PIECES]) for i in range(0, outs, PIECES)]
 
 
 def local(
@@ -257,8 +264,9 @@
     )
     start, normed, swapped = lax.optimization_barrier(((upper, lower), normed, swapped))
 
-    def part_of(rows, hop):
-        return expert_part(my_index, rows, hits, own, swapped, hop, chips)
+    def parts_of(rows, hops):
+        blocks = [block for hop in hops for block in rows[hop]]
+        return expert_parts(my_index, blocks, hits, own, swapped, hops, chips)
 
     def move(blocks, way=route):
         return tuple(lax.ppermute(x, "ctx", way) for x in blocks)
@@ -266,35 +274,32 @@
     def after(blocks, first):
         return tuple(lax.optimization_barrier((x, first))[0] for x in blocks)
 
+    def added(part, arrived):
+        return tuple(x + y.astype(jnp.float32) for x, y in zip(part, arrived))
+
+    def rounded(part):
+        return tuple(x.astype(jnp.bfloat16) for x in part)
+
+    turn = chips // 2
     rows = {0: start, 1: move(start)}
     rows[2] = move(rows[1])
-    joined = (jnp.concatenate(rows[2], axis=0),)
-    if chips == 8:
-        rows[7] = move(after((normed,), rows[1][-1]), back)
-        plan = {1: [(6, 7, back)], 2: [(4, 3, route)], 3: [(5, 6, back)]}
-        needs = {2: 7, 4: 6}
-    else:
-        plan = {hop: [(hop + 3, hop + 2, route)] for hop in range(1, chips - 3)}
-        needs = {}
-    rows[3] = move(joined)
-
-    def added(part, arrived):
-        return tuple(x + y.astype(jnp.float32) for x, y in zip(part, arrived))
-
-    def rounded(part):
-        return tuple(x.astype(jnp.bfloat16) for x in part)
-
-    sums = rounded(part_of(rows[1], 1))
+    rows[chips - 1] = move(after((normed,), rows[1][-1]), back)
+    rows[3] = move((jnp.concatenate(rows[2], axis=0),))
+    parts = dict(zip((1,), parts_of(rows, (1,))))
+    sums = rounded(parts[1])
     for hop in range(1, chips):
         arrived = move(sums)
-        for into, source, way in plan.get(hop, []):
-            rows[into] = move(after(rows[source], sums[0]), way)
-        if hop + 1 < chips:
-            taken = rows[hop + 1]
-            if hop + 1 in needs:
-                taken = after(taken, rows[needs[hop + 1]][0])
-            sums = rounded(added(part_of(taken, hop + 1), arrived))
-    expert_out = jnp.concatenate(added(part_of(after(start, sums), 0), arrived), axis=0)
+        here, there = hop + 1, chips - hop
+        if here <= turn:
+            if 3 < here + 1 <= turn:
+                rows[here + 1] = move(after(rows[here], sums[0]))
+            if here < turn:
+                rows[there - 1] = move(after(rows[there], sums[0]), back)
+            hops = (here, there, 0) if hop == 1 else (here, there)
+            parts.update(zip(hops, parts_of(rows, hops)))
+        if here < chips:
+            sums = rounded(added(parts[here], arrived))
+    expert_out = jnp.concatenate(added(parts[0], arrived), axis=0)
     gate_weight = gate_fixed.astype(jnp.float32) / 65536.0
     return (values.astype(jnp.float32) + gate_weight * expert_out).astype(jnp.bfloat16)
 

time: 125 us -> 122 us (0.976)
  waiting for transfers between devices: 22.9 us -> 48.1 us
  Pallas kernels: 49.3 us -> 30.3 us
  starting transfers between devices: 46.7 us -> 38.5 us
    ppermute x23, waiting for transfers between devices: 16.3 us -> 41.3 us  [move(): return tuple((lax.ppermute(x, 'ctx', way) for x in blocks))]
    pallas_call x8 -> x4, Pallas kernels: 37.5 us -> 18.5 us  [expert_parts(): pl.pallas_call(functools.partial(expert_kernel, hops=hops, chips=chips),...]
    ppermute x23, starting transfers between devices: 34.6 us -> 26.7 us  [move(): return tuple((lax.ppermute(x, 'ctx', way) for x in blocks))]
  transfers between devices with their start and end apart: 34 -> 34, of which waited for: 17 -> 19; matrix products, arithmetic and copies ran while one was open for 1% -> 1% of each run, Pallas kernels for 40% -> 25%
where the time goes in v12:
time: 122 us
  waiting for transfers between devices  48.1 us (39%)
  starting transfers between devices  38.5 us (32%)
  Pallas kernels  30.3 us (25%)
  other arithmetic  3.36 us (3%)
    ppermute x23, waiting for transfers between devices, move(): return tuple((lax.ppermute(x, 'ctx', way) for x in blocks))  41.3 us
    ppermute x23, starting transfers between devices, move(): return tuple((lax.ppermute(x, 'ctx', way) for x in blocks))  26.7 us
    pallas_call x4, Pallas kernels, expert_parts(): pl.pallas_call(functools.partial(expert_kernel, hops=hops, chips=chips),...  18.5 us
    pallas_call x1, Pallas kernels, attention(): pl.pallas_call(functools.partial(attention_kernel, tok=tok), grid_spec=gr...  11.8 us
    ppermute x7, starting transfers between devices, from_chip(): lax.ppermute(block, 'ctx', [(i, i ^ step * CORES) for i in range(n_ctx)])  11.1 us
    ppermute x7, waiting for transfers between devices, from_chip(): lax.ppermute(block, 'ctx', [(i, i ^ step * CORES) for i in range(n_ctx)])  4.77 us
  transfers between devices with their start and end apart: 34, of which 19 were waited for; matrix products, arithmetic and copies ran while one was open for 1% of the time, Pallas kernels for 25%

profile of v12, /device:TPU:0, one launch (start us, length us, event | category | flops | bytes accessed | tf_op | source)
XLA Modules:
  0.0 121.8 jit_solution(328736155203261974)
XLA Ops:
  1.7 4.1 %collective-permute-start.3 = (bf16[64,640]{1,0:T(8,128)(2,1)S(1)}, bf16[64,640]{1,0:T(8,128)(2,1)S(1)}, u32[]{:S(2)}, u32[]{:S(2)}) collective-permute-start(bf16[64,640]{1,0:T(8,128)(2,1)S(1)} %get-tuple-element.77), channel_id=1, source_target_pairs={{0,8},{1,9},{2,10},{3,11},{4,12},{5,13},{6,14},{7,15},{8,0},{9,1},... | collective-permute-start | bytes 245768 | tf_op jit(solution)/shard_map/ppermute | solution.py:250
  5.8 1.5 %collective-permute-start = (bf16[64,640]{1,0:T(8,128)(2,1)S(1)}, bf16[64,640]{1,0:T(8,128)(2,1)S(1)}, u32[]{:S(2)}, u32[]{:S(2)}) collective-permute-start(bf16[64,640]{1,0:T(8,128)(2,1)S(1)} %get-tuple-element.77), channel_id=1, source_target_pairs={{0,2},{1,3},{2,0},{3,1},{4,6},{5,7},{6,4},{7,5},{8,10},{9,11},{10,... | collective-permute-start | bytes 245768 | tf_op jit(solution)/shard_map/ppermute | solution.py:250
  7.3 1.5 %collective-permute-start.2 = (bf16[64,640]{1,0:T(8,128)(2,1)S(1)}, bf16[64,640]{1,0:T(8,128)(2,1)S(1)}, u32[]{:S(2)}, u32[]{:S(2)}) collective-permute-start(bf16[64,640]{1,0:T(8,128)(2,1)S(1)} %get-tuple-element.77), channel_id=1, source_target_pairs={{0,6},{1,7},{2,4},{3,5},{4,2},{5,3},{6,0},{7,1},{8,14},{9,15},{10,... | collective-permute-start | bytes 245768 | tf_op jit(solution)/shard_map/ppermute | solution.py:250
  9.8 2.0 %collective-permute-start.6 = (bf16[64,640]{1,0:T(8,128)(2,1)S(1)}, bf16[64,640]{1,0:T(8,128)(2,1)S(1)}, u32[]{:S(2)}, u32[]{:S(2)}) collective-permute-start(bf16[64,640]{1,0:T(8,128)(2,1)S(1)} %collective-permute-done.3), channel_id=1, source_target_pairs={{0,6},{1,7},{2,4},{3,5},{4,2},{5,3},{6,0},{7,1},{8,14},{9,15},{10,... | collective-permute-start | bytes 245768 | tf_op jit(solution)/shard_map/ppermute | solution.py:250
  11.8 1.3 %collective-permute-start.5 = (bf16[64,640]{1,0:T(8,128)(2,1)S(1)}, bf16[64,640]{1,0:T(8,128)(2,1)S(1)}, u32[]{:S(2)}, u32[]{:S(2)}) collective-permute-start(bf16[64,640]{1,0:T(8,128)(2,1)S(1)} %collective-permute-done.3), channel_id=1, source_target_pairs={{0,4},{1,5},{2,6},{3,7},{4,0},{5,1},{6,2},{7,3},{8,12},{9,13},{10,... | collective-permute-start | bytes 245768 | tf_op jit(solution)/shard_map/ppermute | solution.py:250
  14.0 3.6 %collective-permute-done.4 = bf16[64,640]{1,0:T(8,128)(2,1)S(1)} collective-permute-done((bf16[64,640]{1,0:T(8,128)(2,1)S(1)}, bf16[64,640]{1,0:T(8,128)(2,1)S(1)}, u32[]{:S(2)}, u32[]{:S(2)}) %collective-permute-start.4) | collective-permute-done | bytes 81952 | tf_op jit(solution)/shard_map/ppermute | solution.py:250
  17.8 2.1 %collective-permute-done.7.other_ref = bf16[512,640]{1,0:T(8,128)(2,1)S(1)} collective-permute-done((bf16[512,640]{1,0:T(8,128)(2,1)S(1)}, bf16[512,640]{1,0:T(8,128)(2,1)S(1)}, u32[]{:S(2)}, u32[]{:S(2)}) %collective-permute-start.7) | collective-permute-done | bytes 655392 | tf_op jit(solution)/shard_map/ppermute | solution.py:258
  20.7 11.8 %shard_map.109 = (bf16[64,4096]{1,0:T(8,128)(2,1)}, bf16[64,4096]{1,0:T(8,128)(2,1)}, bf16[32,4096]{1,0:T(8,128)(2,1)}, bf16[32,4096]{1,0:T(8,128)(2,1)}, f32[64,8]{1,0:T(8,128)}) custom-call(s32[1]{0:T(128)} %bitcast.index_ref, bf16[64,16384]{1,0:T(8,128)(2,1)} %q_ref.1, bf16[64,2048]{1,0:T(8,128)(2,1)} %qr_ref.1, bf16[512,640]{1,0:T(8,128)(2,1)} %copy-done.8, ...), custom_call_target="tpu_custom_call" | custom-call | flops 4831838208 | bytes 8388608 | tf_op jit(solution)/shard_map/pallas_call | solution.py:151
  32.5 1.0 collective-permute-start.11
  33.6 1.6 %collective-permute-start.13 = (bf16[32,4096]{1,0:T(8,128)(2,1)}, bf16[32,4096]{1,0:T(8,128)(2,1)S(1)}, u32[]{:S(2)}, u32[]{:S(2)}) collective-permute-start(bf16[32,4096]{1,0:T(8,128)(2,1)} %get-tuple-element.55.refs_4_), channel_id=1, source_target_pairs={{0,4},{1,3},{4,8},{5,1},{8,12},{9,5},{12,14},{13,9},{14,10},{15,13... | collective-permute-start | bytes 786440 | tf_op jit(solution)/shard_map/ppermute | solution.py:272
  35.1 4.0 %collective-permute-done.11.refs_0_ = bf16[32,4096]{1,0:T(8,128)(2,1)S(1)} collective-permute-done((bf16[32,4096]{1,0:T(8,128)(2,1)}, bf16[32,4096]{1,0:T(8,128)(2,1)S(1)}, u32[]{:S(2)}, u32[]{:S(2)}) %collective-permute-start.11) | collective-permute-done | bytes 262176 | tf_op jit(solution)/shard_map/ppermute | solution.py:272
  40.1 1.8 %collective-permute-done.13.refs_1_ = bf16[32,4096]{1,0:T(8,128)(2,1)S(1)} collective-permute-done((bf16[32,4096]{1,0:T(8,128)(2,1)}, bf16[32,4096]{1,0:T(8,128)(2,1)S(1)}, u32[]{:S(2)}, u32[]{:S(2)}) %collective-permute-start.13) | collective-permute-done | bytes 262176 | tf_op jit(solution)/shard_map/ppermute | solution.py:272
  44.8 4.7 %shard_map.111 = (f32[32,4096]{1,0:T(8,128)S(1)}, f32[32,4096]{1,0:T(8,128)S(1)}) custom-call(s32[1]{0:T(128)} %bitcast.index_ref, bf16[4096,256]{1,0:T(8,128)(2,1)S(1)} %bitcast.10, bf16[4096,256]{1,0:T(8,128)(2,1)S(1)} %bitcast.15, bf16[256,4096]{1,0:T(8,128)(2,1)S(1)} %bitcast.20, f32[64,8]{1,0:T(8,128)S(1)} %copy-done.3, ...), custom_call_target="tpu_custom_call" | custom-call | flops 805306368 | bytes 14680064 | tf_op jit(solution)/shard_map/pallas_call | solution.py:218
  50.6 1.6 %collective-permute-start.18 = (bf16[32,4096]{1,0:T(8,128)(2,1)S(1)}, bf16[32,4096]{1,0:T(8,128)(2,1)S(1)}, u32[]{:S(2)}, u32[]{:S(2)}) collective-permute-start(bf16[32,4096]{1,0:T(8,128)(2,1)S(1)} %convert_element_type.99), channel_id=1, source_target_pairs={{0,4},{1,3},{4,8},{5,1},{8,12},{9,5},{12,14},{13,9},{14,10},{15,13... | collective-permute-start | bytes 786440 | tf_op jit(solution)/shard_map/ppermute | solution.py:272
  52.3 2.0 %collective-permute-start.16 = (bf16[64,4096]{1,0:T(8,128)(2,1)S(1)}, bf16[64,4096]{1,0:T(8,128)(2,1)S(1)}, u32[]{:S(2)}, u32[]{:S(2)}) collective-permute-start(bf16[64,4096]{1,0:T(8,128)(2,1)S(1)} %pad_maximum_fusion), channel_id=1, source_target_pairs={{0,4},{1,3},{4,8},{5,1},{8,12},{9,5},{12,14},{13,9},{14,10},{15,13... | collective-permute-start | bytes 1572872 | tf_op jit(solution)/shard_map/ppermute | solution.py:272
  55.2 5.2 %shard_map.110 = (f32[32,4096]{1,0:T(8,128)S(1)}, f32[32,4096]{1,0:T(8,128)S(1)}, f32[32,4096]{1,0:T(8,128)S(1)}, f32[32,4096]{1,0:T(8,128)S(1)}, f32[32,4096]{1,0:T(8,128)S(1)}, /*index=5*/f32[32,4096]{1,0:T(8,128)S(1)}) custom-call(s32[1]{0:T(128)} %bitcast.index_ref, bf16[4096,256]{1,0:T(8,128)(2,1)S(1)} %bitcast.11, bf16[4096,256]{1,0:T(8,128)(2,1)S(1)} %bitcast.16, ...), custom_call_target="tpu_custom_call" | custom-call | flops 805306368 | bytes 14680064 | tf_op jit(solution)/shard_map/pallas_call | solution.py:218
  60.4 1.3 %collective-permute-done.18 = bf16[32,4096]{1,0:T(8,128)(2,1)S(1)} collective-permute-done((bf16[32,4096]{1,0:T(8,128)(2,1)S(1)}, bf16[32,4096]{1,0:T(8,128)(2,1)S(1)}, u32[]{:S(2)}, u32[]{:S(2)}) %collective-permute-start.18) | collective-permute-done | bytes 262176 | tf_op jit(solution)/shard_map/ppermute | solution.py:272
  62.9 1.6 %collective-permute-start.28 = (bf16[32,4096]{1,0:T(8,128)(2,1)S(1)}, bf16[32,4096]{1,0:T(8,128)(2,1)S(1)}, u32[]{:S(2)}, u32[]{:S(2)}) collective-permute-start(bf16[32,4096]{1,0:T(8,128)(2,1)S(1)} %add_convert_fusion.5), channel_id=1, source_target_pairs={{0,4},{1,3},{4,8},{5,1},{8,12},{9,5},{12,14},{13,9},{14,10},{15,13... | collective-permute-start | bytes 786440 | tf_op jit(solution)/shard_map/ppermute | solution.py:272
  64.5 6.3 %collective-permute-done.16.refs_0_ = bf16[64,4096]{1,0:T(8,128)(2,1)S(1)} collective-permute-done((bf16[64,4096]{1,0:T(8,128)(2,1)S(1)}, bf16[64,4096]{1,0:T(8,128)(2,1)S(1)}, u32[]{:S(2)}, u32[]{:S(2)}) %collective-permute-start.16) | collective-permute-done | bytes 524320 | tf_op jit(solution)/shard_map/ppermute | solution.py:272
  72.8 4.3 %shard_map.112 = (f32[32,4096]{1,0:T(8,128)S(1)}, f32[32,4096]{1,0:T(8,128)S(1)}, f32[32,4096]{1,0:T(8,128)S(1)}, f32[32,4096]{1,0:T(8,128)S(1)}) custom-call(s32[1]{0:T(128)} %bitcast.index_ref, bf16[4096,256]{1,0:T(8,128)(2,1)S(1)} %bitcast.12, bf16[4096,256]{1,0:T(8,128)(2,1)S(1)} %bitcast.17, bf16[256,4096]{1,0:T(8,128)(2,1)S(1)} %bitcast.22, ...), custom_call_target="tpu_custom_call" | custom-call | flops 805306368 | bytes 14680064 | tf_op jit(solution)/shard_map/pallas_call | solution.py:218
  78.3 1.8 %collective-permute-done.28 = bf16[32,4096]{1,0:T(8,128)(2,1)S(1)} collective-permute-done((bf16[32,4096]{1,0:T(8,128)(2,1)S(1)}, bf16[32,4096]{1,0:T(8,128)(2,1)S(1)}, u32[]{:S(2)}, u32[]{:S(2)}) %collective-permute-start.28) | collective-permute-done | bytes 262176 | tf_op jit(solution)/shard_map/ppermute | solution.py:272
  81.2 6.5 %collective-permute-done.19.refs_0_ = bf16[64,4096]{1,0:T(8,128)(2,1)S(1)} collective-permute-done((bf16[64,4096]{1,0:T(8,128)(2,1)S(1)}, bf16[64,4096]{1,0:T(8,128)(2,1)S(1)}, u32[]{:S(2)}, u32[]{:S(2)}) %collective-permute-start.19) | collective-permute-done | bytes 524320 | tf_op jit(solution)/shard_map/ppermute | solution.py:272
  87.7 4.3 %shard_map.113 = (f32[32,4096]{1,0:T(8,128)S(1)}, f32[32,4096]{1,0:T(8,128)S(1)}, f32[32,4096]{1,0:T(8,128)S(1)}, f32[32,4096]{1,0:T(8,128)S(1)}) custom-call(s32[1]{0:T(128)} %bitcast.index_ref, bf16[4096,256]{1,0:T(8,128)(2,1)S(1)} %bitcast.13, bf16[4096,256]{1,0:T(8,128)(2,1)S(1)} %bitcast.18, bf16[256,4096]{1,0:T(8,128)(2,1)S(1)} %bitcast.23, ...), custom_call_target="tpu_custom_call" | custom-call | flops 805306368 | bytes 14680064 | tf_op jit(solution)/shard_map/pallas_call | solution.py:218
  93.3 1.5 %collective-permute-start.30 = (bf16[32,4096]{1,0:T(8,128)(2,1)S(1)}, bf16[32,4096]{1,0:T(8,128)(2,1)S(1)}, u32[]{:S(2)}, u32[]{:S(2)}) collective-permute-start(bf16[32,4096]{1,0:T(8,128)(2,1)S(1)} %add_convert_fusion.3), channel_id=1, source_target_pairs={{0,4},{1,3},{4,8},{5,1},{8,12},{9,5},{12,14},{13,9},{14,10},{15,13... | collective-permute-start | bytes 786440 | tf_op jit(solution)/shard_map/ppermute | solution.py:272
  94.8 3.7 %collective-permute-done.23 = bf16[32,4096]{1,0:T(8,128)(2,1)S(1)} collective-permute-done((bf16[32,4096]{1,0:T(8,128)(2,1)S(1)}, bf16[32,4096]{1,0:T(8,128)(2,1)S(1)}, u32[]{:S(2)}, u32[]{:S(2)}) %collective-permute-start.23) | collective-permute-done | bytes 262176 | tf_op jit(solution)/shard_map/ppermute | solution.py:272
  99.6 1.7 %collective-permute-done.30 = bf16[32,4096]{1,0:T(8,128)(2,1)S(1)} collective-permute-done((bf16[32,4096]{1,0:T(8,128)(2,1)S(1)}, bf16[32,4096]{1,0:T(8,128)(2,1)S(1)}, u32[]{:S(2)}, u32[]{:S(2)}) %collective-permute-start.30) | collective-permute-done | bytes 262176 | tf_op jit(solution)/shard_map/ppermute | solution.py:272
  102.4 2.6 %collective-permute-done.24 = bf16[32,4096]{1,0:T(8,128)(2,1)S(1)} collective-permute-done((bf16[32,4096]{1,0:T(8,128)(2,1)S(1)}, bf16[32,4096]{1,0:T(8,128)(2,1)S(1)}, u32[]{:S(2)}, u32[]{:S(2)}) %collective-permute-start.24) | collective-permute-done | bytes 262176 | tf_op jit(solution)/shard_map/ppermute | solution.py:272
  106.1 1.7 %collective-permute-done.31 = bf16[32,4096]{1,0:T(8,128)(2,1)S(1)} collective-permute-done((bf16[32,4096]{1,0:T(8,128)(2,1)S(1)}, bf16[32,4096]{1,0:T(8,128)(2,1)S(1)}, u32[]{:S(2)}, u32[]{:S(2)}) %collective-permute-start.31) | collective-permute-done | bytes 262176 | tf_op jit(solution)/shard_map/ppermute | solution.py:272
  108.9 2.6 %collective-permute-done.25 = bf16[32,4096]{1,0:T(8,128)(2,1)S(1)} collective-permute-done((bf16[32,4096]{1,0:T(8,128)(2,1)S(1)}, bf16[32,4096]{1,0:T(8,128)(2,1)S(1)}, u32[]{:S(2)}, u32[]{:S(2)}) %collective-permute-start.25) | collective-permute-done | bytes 262176 | tf_op jit(solution)/shard_map/ppermute | solution.py:272
  112.6 1.7 %collective-permute-done.32 = bf16[32,4096]{1,0:T(8,128)(2,1)S(1)} collective-permute-done((bf16[32,4096]{1,0:T(8,128)(2,1)S(1)}, bf16[32,4096]{1,0:T(8,128)(2,1)S(1)}, u32[]{:S(2)}, u32[]{:S(2)}) %collective-permute-start.32) | collective-permute-done | bytes 262176 | tf_op jit(solution)/shard_map/ppermute | solution.py:272
  115.4 2.6 %collective-permute-done.26 = bf16[32,4096]{1,0:T(8,128)(2,1)S(1)} collective-permute-done((bf16[32,4096]{1,0:T(8,128)(2,1)S(1)}, bf16[32,4096]{1,0:T(8,128)(2,1)S(1)}, u32[]{:S(2)}, u32[]{:S(2)}) %collective-permute-start.26) | collective-permute-done | bytes 262176 | tf_op jit(solution)/shard_map/ppermute | solution.py:272
  118.0 2.7 %collective-permute-done.33 = bf16[32,4096]{1,0:T(8,128)(2,1)S(1)} collective-permute-done((bf16[32,4096]{1,0:T(8,128)(2,1)S(1)}, bf16[32,4096]{1,0:T(8,128)(2,1)S(1)}, u32[]{:S(2)}, u32[]{:S(2)}) %collective-permute-start.33) | collective-permute-done | bytes 262176 | tf_op jit(solution)/shard_map/ppermute | solution.py:272
  (92 shorter events, 24.7 us)
Async XLA Ops:
  1.7 8.1 %collective-permute-start.3 = (bf16[64,640]{1,0:T(8,128)(2,1)S(1)}, bf16[64,640]{1,0:T(8,128)(2,1)S(1)}, u32[]{:S(2)}, u32[]{:S(2)}) collective-permute-start(bf16[64,640]{1,0:T(8,128)(2,1)S(1)} %get-tuple-element.77), channel_id=1, source_target_pairs={{0,8},{1,9},{2,10},{3,11},{4,12},{5,13},{6,14},{7,15},{8,0},{9,1},... | collective-permute-start | bytes 245768 | tf_op jit(solution)/shard_map/ppermute | solution.py:250
  5.8 7.3 %collective-permute-start = (bf16[64,640]{1,0:T(8,128)(2,1)S(1)}, bf16[64,640]{1,0:T(8,128)(2,1)S(1)}, u32[]{:S(2)}, u32[]{:S(2)}) collective-permute-start(bf16[64,640]{1,0:T(8,128)(2,1)S(1)} %get-tuple-element.77), channel_id=1, source_target_pairs={{0,2},{1,3},{2,0},{3,1},{4,6},{5,7},{6,4},{7,5},{8,10},{9,11},{10,... | collective-permute-start | bytes 245768 | tf_op jit(solution)/shard_map/ppermute | solution.py:250
  7.3 6.6 %collective-permute-start.2 = (bf16[64,640]{1,0:T(8,128)(2,1)S(1)}, bf16[64,640]{1,0:T(8,128)(2,1)S(1)}, u32[]{:S(2)}, u32[]{:S(2)}) collective-permute-start(bf16[64,640]{1,0:T(8,128)(2,1)S(1)} %get-tuple-element.77), channel_id=1, source_target_pairs={{0,6},{1,7},{2,4},{3,5},{4,2},{5,3},{6,0},{7,1},{8,14},{9,15},{10,... | collective-permute-start | bytes 245768 | tf_op jit(solution)/shard_map/ppermute | solution.py:250
  8.8 5.1 %collective-permute-start.1 = (bf16[64,640]{1,0:T(8,128)(2,1)S(1)}, bf16[64,640]{1,0:T(8,128)(2,1)S(1)}, u32[]{:S(2)}, u32[]{:S(2)}) collective-permute-start(bf16[64,640]{1,0:T(8,128)(2,1)S(1)} %get-tuple-element.77), channel_id=1, source_target_pairs={{0,4},{1,5},{2,6},{3,7},{4,0},{5,1},{6,2},{7,3},{8,12},{9,13},{10,... | collective-permute-start | bytes 245768 | tf_op jit(solution)/shard_map/ppermute | solution.py:250
  9.8 7.9 %collective-permute-start.6 = (bf16[64,640]{1,0:T(8,128)(2,1)S(1)}, bf16[64,640]{1,0:T(8,128)(2,1)S(1)}, u32[]{:S(2)}, u32[]{:S(2)}) collective-permute-start(bf16[64,640]{1,0:T(8,128)(2,1)S(1)} %collective-permute-done.3), channel_id=1, source_target_pairs={{0,6},{1,7},{2,4},{3,5},{4,2},{5,3},{6,0},{7,1},{8,14},{9,15},{10,... | collective-permute-start | bytes 245768 | tf_op jit(solution)/shard_map/ppermute | solution.py:250
  11.8 5.8 %collective-permute-start.5 = (bf16[64,640]{1,0:T(8,128)(2,1)S(1)}, bf16[64,640]{1,0:T(8,128)(2,1)S(1)}, u32[]{:S(2)}, u32[]{:S(2)}) collective-permute-start(bf16[64,640]{1,0:T(8,128)(2,1)S(1)} %collective-permute-done.3), channel_id=1, source_target_pairs={{0,4},{1,5},{2,6},{3,7},{4,0},{5,1},{6,2},{7,3},{8,12},{9,13},{10,... | collective-permute-start | bytes 245768 | tf_op jit(solution)/shard_map/ppermute | solution.py:250
  19.8 12.7 %collective-permute-start.8 = (bf16[4096,256]{1,0:T(8,128)(2,1)}, bf16[4096,256]{1,0:T(8,128)(2,1)}, u32[]{:S(2)}, u32[]{:S(2)}) collective-permute-start(bf16[4096,256]{1,0:T(8,128)(2,1)} %bitcast.9), channel_id=1, source_target_pairs={{0,1},{1,0},{2,3},{3,2},{4,5},{5,4},{6,7},{7,6},{8,9},{9,8},{10,11... | collective-permute-start | bytes 6291464 | tf_op jit(solution)/shard_map/ppermute | solution.py:261
  20.0 12.5 %collective-permute-start.9 = (bf16[4096,256]{1,0:T(8,128)(2,1)}, bf16[4096,256]{1,0:T(8,128)(2,1)}, u32[]{:S(2)}, u32[]{:S(2)}) collective-permute-start(bf16[4096,256]{1,0:T(8,128)(2,1)} %bitcast.14), channel_id=1, source_target_pairs={{0,1},{1,0},{2,3},{3,2},{4,5},{5,4},{6,7},{7,6},{8,9},{9,8},{10,11... | collective-permute-start | bytes 6291464 | tf_op jit(solution)/shard_map/ppermute | solution.py:261
  20.4 12.2 %collective-permute-start.10 = (bf16[256,4096]{1,0:T(8,128)(2,1)}, bf16[256,4096]{1,0:T(8,128)(2,1)}, u32[]{:S(2)}, u32[]{:S(2)}) collective-permute-start(bf16[256,4096]{1,0:T(8,128)(2,1)} %bitcast.19), channel_id=1, source_target_pairs={{0,1},{1,0},{2,3},{3,2},{4,5},{5,4},{6,7},{7,6},{8,9},{9,8},{10,11... | collective-permute-start | bytes 6291464 | tf_op jit(solution)/shard_map/ppermute | solution.py:261
  32.5 6.6 %collective-permute-start.11 = (bf16[32,4096]{1,0:T(8,128)(2,1)}, bf16[32,4096]{1,0:T(8,128)(2,1)S(1)}, u32[]{:S(2)}, u32[]{:S(2)}) collective-permute-start(bf16[32,4096]{1,0:T(8,128)(2,1)} %get-tuple-element.54.refs_3_), channel_id=1, source_target_pairs={{0,4},{1,3},{4,8},{5,1},{8,12},{9,5},{12,14},{13,9},{14,10},{15,13... | collective-permute-start | bytes 786440 | tf_op jit(solution)/shard_map/ppermute | solution.py:272
  33.6 8.4 %collective-permute-start.13 = (bf16[32,4096]{1,0:T(8,128)(2,1)}, bf16[32,4096]{1,0:T(8,128)(2,1)S(1)}, u32[]{:S(2)}, u32[]{:S(2)}) collective-permute-start(bf16[32,4096]{1,0:T(8,128)(2,1)} %get-tuple-element.55.refs_4_), channel_id=1, source_target_pairs={{0,4},{1,3},{4,8},{5,1},{8,12},{9,5},{12,14},{13,9},{14,10},{15,13... | collective-permute-start | bytes 786440 | tf_op jit(solution)/shard_map/ppermute | solution.py:272
  39.2 13.0 %collective-permute-start.12 = (bf16[32,4096]{1,0:T(8,128)(2,1)S(1)}, bf16[32,4096]{1,0:T(8,128)(2,1)S(1)}, u32[]{:S(2)}, u32[]{:S(2)}) collective-permute-start(bf16[32,4096]{1,0:T(8,128)(2,1)S(1)} %collective-permute-done.11.refs_0_), channel_id=1, source_target_pairs={{0,4},{1,3},{4,8},{5,1},{8,12},{9,5},{12,14},{13,9},{14,10},{15,13... | collective-permute-start | bytes 786440 | tf_op jit(solution)/shard_map/ppermute | solution.py:272
  42.0 10.3 %collective-permute-start.14 = (bf16[32,4096]{1,0:T(8,128)(2,1)S(1)}, bf16[32,4096]{1,0:T(8,128)(2,1)S(1)}, u32[]{:S(2)}, u32[]{:S(2)}) collective-permute-start(bf16[32,4096]{1,0:T(8,128)(2,1)S(1)} %collective-permute-done.13.refs_1_), channel_id=1, source_target_pairs={{0,4},{1,3},{4,8},{5,1},{8,12},{9,5},{12,14},{13,9},{14,10},{15,13... | collective-permute-start | bytes 786440 | tf_op jit(solution)/shard_map/ppermute | solution.py:272
  43.0 11.3 %collective-permute-start.15 = (bf16[64,4096]{1,0:T(8,128)(2,1)}, bf16[64,4096]{1,0:T(8,128)(2,1)S(1)}, u32[]{:S(2)}, u32[]{:S(2)}) collective-permute-start(bf16[64,4096]{1,0:T(8,128)(2,1)} %get-tuple-element.57), channel_id=1, source_target_pairs={{4,0},{3,1},{8,4},{1,5},{12,8},{5,9},{14,12},{9,13},{10,14},{13,15... | collective-permute-start | bytes 1572872 | tf_op jit(solution)/shard_map/ppermute | solution.py:272
  49.6 13.2 %collective-permute-start.27 = (bf16[32,4096]{1,0:T(8,128)(2,1)S(1)}, bf16[32,4096]{1,0:T(8,128)(2,1)S(1)}, u32[]{:S(2)}, u32[]{:S(2)}) collective-permute-start(bf16[32,4096]{1,0:T(8,128)(2,1)S(1)} %convert_element_type.113), channel_id=1, source_target_pairs={{0,4},{1,3},{4,8},{5,1},{8,12},{9,5},{12,14},{13,9},{14,10},{15,13... | collective-permute-start | bytes 786440 | tf_op jit(solution)/shard_map/ppermute | solution.py:272
  50.6 11.1 %collective-permute-start.18 = (bf16[32,4096]{1,0:T(8,128)(2,1)S(1)}, bf16[32,4096]{1,0:T(8,128)(2,1)S(1)}, u32[]{:S(2)}, u32[]{:S(2)}) collective-permute-start(bf16[32,4096]{1,0:T(8,128)(2,1)S(1)} %convert_element_type.99), channel_id=1, source_target_pairs={{0,4},{1,3},{4,8},{5,1},{8,12},{9,5},{12,14},{13,9},{14,10},{15,13... | collective-permute-start | bytes 786440 | tf_op jit(solution)/shard_map/ppermute | solution.py:272
  52.3 18.5 %collective-permute-start.16 = (bf16[64,4096]{1,0:T(8,128)(2,1)S(1)}, bf16[64,4096]{1,0:T(8,128)(2,1)S(1)}, u32[]{:S(2)}, u32[]{:S(2)}) collective-permute-start(bf16[64,4096]{1,0:T(8,128)(2,1)S(1)} %pad_maximum_fusion), channel_id=1, source_target_pairs={{0,4},{1,3},{4,8},{5,1},{8,12},{9,5},{12,14},{13,9},{14,10},{15,13... | collective-permute-start | bytes 1572872 | tf_op jit(solution)/shard_map/ppermute | solution.py:272
  54.3 17.5 %collective-permute-start.17 = (bf16[64,4096]{1,0:T(8,128)(2,1)S(1)}, bf16[64,4096]{1,0:T(8,128)(2,1)S(1)}, u32[]{:S(2)}, u32[]{:S(2)}) collective-permute-start(bf16[64,4096]{1,0:T(8,128)(2,1)S(1)} %collective-permute-done.15.refs_2_), channel_id=1, source_target_pairs={{4,0},{3,1},{8,4},{1,5},{12,8},{5,9},{14,12},{9,13},{10,14},{13,15... | collective-permute-start | bytes 1572872 | tf_op jit(solution)/shard_map/ppermute | solution.py:272
  61.7 15.4 %collective-permute-start.21 = (bf16[32,4096]{1,0:T(8,128)(2,1)S(1)}, bf16[32,4096]{1,0:T(8,128)(2,1)S(1)}, u32[]{:S(2)}, u32[]{:S(2)}) collective-permute-start(bf16[32,4096]{1,0:T(8,128)(2,1)S(1)} %add_convert_fusion.11), channel_id=1, source_target_pairs={{0,4},{1,3},{4,8},{5,1},{8,12},{9,5},{12,14},{13,9},{14,10},{15,13... | collective-permute-start | bytes 786440 | tf_op jit(solution)/shard_map/ppermute | solution.py:272
  62.9 17.3 %collective-permute-start.28 = (bf16[32,4096]{1,0:T(8,128)(2,1)S(1)}, bf16[32,4096]{1,0:T(8,128)(2,1)S(1)}, u32[]{:S(2)}, u32[]{:S(2)}) collective-permute-start(bf16[32,4096]{1,0:T(8,128)(2,1)S(1)} %add_convert_fusion.5), channel_id=1, source_target_pairs={{0,4},{1,3},{4,8},{5,1},{8,12},{9,5},{12,14},{13,9},{14,10},{15,13... | collective-permute-start | bytes 786440 | tf_op jit(solution)/shard_map/ppermute | solution.py:272
  70.8 16.9 %collective-permute-start.19 = (bf16[64,4096]{1,0:T(8,128)(2,1)S(1)}, bf16[64,4096]{1,0:T(8,128)(2,1)S(1)}, u32[]{:S(2)}, u32[]{:S(2)}) collective-permute-start(bf16[64,4096]{1,0:T(8,128)(2,1)S(1)} %collective-permute-done.16.refs_0_), channel_id=1, source_target_pairs={{0,4},{1,3},{4,8},{5,1},{8,12},{9,5},{12,14},{13,9},{14,10},{15,13... | collective-permute-start | bytes 1572872 | tf_op jit(solution)/shard_map/ppermute | solution.py:272
  71.8 15.9 %collective-permute-start.20 = (bf16[64,4096]{1,0:T(8,128)(2,1)S(1)}, bf16[64,4096]{1,0:T(8,128)(2,1)S(1)}, u32[]{:S(2)}, u32[]{:S(2)}) collective-permute-start(bf16[64,4096]{1,0:T(8,128)(2,1)S(1)} %collective-permute-done.17.refs_1_), channel_id=1, source_target_pairs={{4,0},{3,1},{8,4},{1,5},{12,8},{5,9},{14,12},{9,13},{10,14},{13,15... | collective-permute-start | bytes 1572872 | tf_op jit(solution)/shard_map/ppermute | solution.py:272
  77.2 14.8 %collective-permute-start.22 = (bf16[32,4096]{1,0:T(8,128)(2,1)S(1)}, bf16[32,4096]{1,0:T(8,128)(2,1)S(1)}, u32[]{:S(2)}, u32[]{:S(2)}) collective-permute-start(bf16[32,4096]{1,0:T(8,128)(2,1)S(1)} %add_convert_fusion.10), channel_id=1, source_target_pairs={{0,4},{1,3},{4,8},{5,1},{8,12},{9,5},{12,14},{13,9},{14,10},{15,13... | collective-permute-start | bytes 786440 | tf_op jit(solution)/shard_map/ppermute | solution.py:272
  80.2 13.1 %collective-permute-start.29 = (bf16[32,4096]{1,0:T(8,128)(2,1)S(1)}, bf16[32,4096]{1,0:T(8,128)(2,1)S(1)}, u32[]{:S(2)}, u32[]{:S(2)}) collective-permute-start(bf16[32,4096]{1,0:T(8,128)(2,1)S(1)} %add_convert_fusion.4), channel_id=1, source_target_pairs={{0,4},{1,3},{4,8},{5,1},{8,12},{9,5},{12,14},{13,9},{14,10},{15,13... | collective-permute-start | bytes 786440 | tf_op jit(solution)/shard_map/ppermute | solution.py:272
  92.1 6.4 %collective-permute-start.23 = (bf16[32,4096]{1,0:T(8,128)(2,1)S(1)}, bf16[32,4096]{1,0:T(8,128)(2,1)S(1)}, u32[]{:S(2)}, u32[]{:S(2)}) collective-permute-start(bf16[32,4096]{1,0:T(8,128)(2,1)S(1)} %add_convert_fusion.9), channel_id=1, source_target_pairs={{0,4},{1,3},{4,8},{5,1},{8,12},{9,5},{12,14},{13,9},{14,10},{15,13... | collective-permute-start | bytes 786440 | tf_op jit(solution)/shard_map/ppermute | solution.py:272
  93.3 8.0 %collective-permute-start.30 = (bf16[32,4096]{1,0:T(8,128)(2,1)S(1)}, bf16[32,4096]{1,0:T(8,128)(2,1)S(1)}, u32[]{:S(2)}, u32[]{:S(2)}) collective-permute-start(bf16[32,4096]{1,0:T(8,128)(2,1)S(1)} %add_convert_fusion.3), channel_id=1, source_target_pairs={{0,4},{1,3},{4,8},{5,1},{8,12},{9,5},{12,14},{13,9},{14,10},{15,13... | collective-permute-start | bytes 786440 | tf_op jit(solution)/shard_map/ppermute | solution.py:272
  98.5 6.4 %collective-permute-start.24 = (bf16[32,4096]{1,0:T(8,128)(2,1)S(1)}, bf16[32,4096]{1,0:T(8,128)(2,1)S(1)}, u32[]{:S(2)}, u32[]{:S(2)}) collective-permute-start(bf16[32,4096]{1,0:T(8,128)(2,1)S(1)} %add_convert_fusion.8), channel_id=1, source_target_pairs={{0,4},{1,3},{4,8},{5,1},{8,12},{9,5},{12,14},{13,9},{14,10},{15,13... | collective-permute-start | bytes 786440 | tf_op jit(solution)/shard_map/ppermute | solution.py:272
  101.4 6.4 %collective-permute-start.31 = (bf16[32,4096]{1,0:T(8,128)(2,1)S(1)}, bf16[32,4096]{1,0:T(8,128)(2,1)S(1)}, u32[]{:S(2)}, u32[]{:S(2)}) collective-permute-start(bf16[32,4096]{1,0:T(8,128)(2,1)S(1)} %add_convert_fusion.2), channel_id=1, source_target_pairs={{0,4},{1,3},{4,8},{5,1},{8,12},{9,5},{12,14},{13,9},{14,10},{15,13... | collective-permute-start | bytes 786440 | tf_op jit(solution)/shard_map/ppermute | solution.py:272
  105.0 6.4 %collective-permute-start.25 = (bf16[32,4096]{1,0:T(8,128)(2,1)S(1)}, bf16[32,4096]{1,0:T(8,128)(2,1)S(1)}, u32[]{:S(2)}, u32[]{:S(2)}) collective-permute-start(bf16[32,4096]{1,0:T(8,128)(2,1)S(1)} %add_convert_fusion.7), channel_id=1, source_target_pairs={{0,4},{1,3},{4,8},{5,1},{8,12},{9,5},{12,14},{13,9},{14,10},{15,13... | collective-permute-start | bytes 786440 | tf_op jit(solution)/shard_map/ppermute | solution.py:272
  107.8 6.4 %collective-permute-start.32 = (bf16[32,4096]{1,0:T(8,128)(2,1)S(1)}, bf16[32,4096]{1,0:T(8,128)(2,1)S(1)}, u32[]{:S(2)}, u32[]{:S(2)}) collective-permute-start(bf16[32,4096]{1,0:T(8,128)(2,1)S(1)} %add_convert_fusion.1), channel_id=1, source_target_pairs={{0,4},{1,3},{4,8},{5,1},{8,12},{9,5},{12,14},{13,9},{14,10},{15,13... | collective-permute-start | bytes 786440 | tf_op jit(solution)/shard_map/ppermute | solution.py:272
  111.5 6.4 %collective-permute-start.26 = (bf16[32,4096]{1,0:T(8,128)(2,1)S(1)}, bf16[32,4096]{1,0:T(8,128)(2,1)S(1)}, u32[]{:S(2)}, u32[]{:S(2)}) collective-permute-start(bf16[32,4096]{1,0:T(8,128)(2,1)S(1)} %add_convert_fusion.6), channel_id=1, source_target_pairs={{0,4},{1,3},{4,8},{5,1},{8,12},{9,5},{12,14},{13,9},{14,10},{15,13... | collective-permute-start | bytes 786440 | tf_op jit(solution)/shard_map/ppermute | solution.py:272
  114.3 6.4 %collective-permute-start.33 = (bf16[32,4096]{1,0:T(8,128)(2,1)S(1)}, bf16[32,4096]{1,0:T(8,128)(2,1)S(1)}, u32[]{:S(2)}, u32[]{:S(2)}) collective-permute-start(bf16[32,4096]{1,0:T(8,128)(2,1)S(1)} %add_convert_fusion), channel_id=1, source_target_pairs={{0,4},{1,3},{4,8},{5,1},{8,12},{9,5},{12,14},{13,9},{14,10},{15,13... | collective-permute-start | bytes 786440 | tf_op jit(solution)/shard_map/ppermute | solution.py:272
  (13 other events, 129.7 us)

commit v13 on v12

--- a/solution.py
+++ b/solution.py
@@ -266,7 +266,7 @@
 
     def parts_of(rows, hops):
         blocks = [block for hop in hops for block in rows[hop]]
-        return expert_parts(my_index, blocks, hits, own, swapped, hops, chips)
+        return expert_parts(my_index, blocks, table, own, swapped, hops, chips)
 
     def move(blocks, way=route):
         return tuple(lax.ppermute(x, "ctx", way) for x in blocks)
@@ -282,7 +282,8 @@
 
     turn = chips // 2
     rows = {0: start, 1: move(start)}
-    rows[2] = move(rows[1])
+    table = jnp.where(hits > 0.5, 1.0, 0.0)
+    rows[2] = move(after(rows[1], table))
     rows[chips - 1] = move(after((normed,), rows[1][-1]), back)
     rows[3] = move((jnp.concatenate(rows[2], axis=0),))
     parts = dict(zip((1,), parts_of(rows, (1,))))
@@ -299,9 +300,14 @@
             parts.update(zip(hops, parts_of(rows, hops)))
         if here < chips:
             sums = rounded(added(parts[here], arrived))
-    expert_out = jnp.concatenate(added(parts[0], arrived), axis=0)
     gate_weight = gate_fixed.astype(jnp.float32) / 65536.0
-    return (values.astype(jnp.float32) + gate_weight * expert_out).astype(jnp.bfloat16)
+    mixed = values
+    for piece, total in enumerate(added(parts[0], arrived)):
+        first = piece * (tok // PIECES)
+        at = slice(first, first + tok // PIECES)
+        done = values[at].astype(jnp.float32) + gate_weight[at] * total
+        mixed = lax.dynamic_update_slice(mixed, done.astype(jnp.bfloat16), (first, 0))
+    return mixed
 
 
 def solution(mesh):

time: 122 us -> 125 us (1.025)
  starting transfers between devices: 38.5 us -> 47 us
  waiting for transfers between devices: 48.1 us -> 41.5 us
    ppermute x23, starting transfers between devices: 26.7 us -> 34.9 us  [move(): return tuple((lax.ppermute(x, 'ctx', way) for x in blocks))]
    ppermute x23, waiting for transfers between devices: 41.3 us -> 34.8 us  [move(): return tuple((lax.ppermute(x, 'ctx', way) for x in blocks))]
  transfers between devices with their start and end apart: 34 -> 34, of which waited for: 19 -> 22; matrix products, arithmetic and copies ran while one was open for 1% -> 2% of each run, Pallas kernels for 25% -> 24%
where the time goes in v13:
time: 125 us
  starting transfers between devices  47 us (38%)
  waiting for transfers between devices  41.5 us (33%)
  Pallas kernels  30.4 us (24%)
  other arithmetic  3.99 us (3%)
  local copies, waits for them, and re-layouts  1.55 us (1%)
    ppermute x23, starting transfers between devices, move(): return tuple((lax.ppermute(x, 'ctx', way) for x in blocks))  34.9 us
    ppermute x23, waiting for transfers between devices, move(): return tuple((lax.ppermute(x, 'ctx', way) for x in blocks))  34.8 us
    pallas_call x4, Pallas kernels, expert_parts(): pl.pallas_call(functools.partial(expert_kernel, hops=hops, chips=chips),...  18.6 us
    pallas_call x1, Pallas kernels, attention(): pl.pallas_call(functools.partial(attention_kernel, tok=tok), grid_spec=gr...  11.8 us
    ppermute x7, starting transfers between devices, from_chip(): lax.ppermute(block, 'ctx', [(i, i ^ step * CORES) for i in range(n_ctx)])  11.4 us
    ppermute x7, waiting for transfers between devices, from_chip(): lax.ppermute(block, 'ctx', [(i, i ^ step * CORES) for i in range(n_ctx)])  4.54 us
  transfers between devices with their start and end apart: 34, of which 22 were waited for; matrix products, arithmetic and copies ran while one was open for 2% of the time, Pallas kernels for 24%

profile of v13, /device:TPU:0, one launch (start us, length us, event | category | flops | bytes accessed | tf_op | source)
XLA Modules:
  0.0 124.6 jit_solution(17065951263378916266)
XLA Ops:
  1.7 4.1 %collective-permute-start.3 = (bf16[64,640]{1,0:T(8,128)(2,1)S(1)}, bf16[64,640]{1,0:T(8,128)(2,1)S(1)}, u32[]{:S(2)}, u32[]{:S(2)}) collective-permute-start(bf16[64,640]{1,0:T(8,128)(2,1)S(1)} %get-tuple-element.81), channel_id=1, source_target_pairs={{0,8},{1,9},{2,10},{3,11},{4,12},{5,13},{6,14},{7,15},{8,0},{9,1},... | collective-permute-start | bytes 245768 | tf_op jit(solution)/shard_map/ppermute | solution.py:250
  15.9 1.8 %collective-permute-done.6 = bf16[64,640]{1,0:T(8,128)(2,1)S(1)} collective-permute-done((bf16[64,640]{1,0:T(8,128)(2,1)S(1)}, bf16[64,640]{1,0:T(8,128)(2,1)S(1)}, u32[]{:S(2)}, u32[]{:S(2)}) %collective-permute-start.6) | collective-permute-done | bytes 81952 | tf_op jit(solution)/shard_map/ppermute | solution.py:250
  17.8 2.1 %collective-permute-done.7.other_ref = bf16[512,640]{1,0:T(8,128)(2,1)S(1)} collective-permute-done((bf16[512,640]{1,0:T(8,128)(2,1)S(1)}, bf16[512,640]{1,0:T(8,128)(2,1)S(1)}, u32[]{:S(2)}, u32[]{:S(2)}) %collective-permute-start.7) | collective-permute-done | bytes 655392 | tf_op jit(solution)/shard_map/ppermute | solution.py:258
  20.8 11.8 %shard_map.109 = (bf16[64,4096]{1,0:T(8,128)(2,1)}, bf16[64,4096]{1,0:T(8,128)(2,1)}, bf16[32,4096]{1,0:T(8,128)(2,1)}, bf16[32,4096]{1,0:T(8,128)(2,1)}, f32[64,8]{1,0:T(8,128)}) custom-call(s32[1]{0:T(128)} %bitcast.index_ref, bf16[64,16384]{1,0:T(8,128)(2,1)} %q_ref.1, bf16[64,2048]{1,0:T(8,128)(2,1)} %qr_ref.1, bf16[512,640]{1,0:T(8,128)(2,1)} %copy-done.7, ...), custom_call_target="tpu_custom_call" | custom-call | flops 4831838208 | bytes 8388608 | tf_op jit(solution)/shard_map/pallas_call | solution.py:151
  33.7 2.7 %collective-permute-start.13 = (bf16[32,4096]{1,0:T(8,128)(2,1)}, bf16[32,4096]{1,0:T(8,128)(2,1)S(1)}, u32[]{:S(2)}, u32[]{:S(2)}) collective-permute-start(bf16[32,4096]{1,0:T(8,128)(2,1)} %get-tuple-element.58.refs_4_), channel_id=1, source_target_pairs={{0,4},{1,3},{4,8},{5,1},{8,12},{9,5},{12,14},{13,9},{14,10},{15,13... | collective-permute-start | bytes 786440 | tf_op jit(solution)/shard_map/ppermute | solution.py:272
  37.2 4.8 %collective-permute-done.13.refs_1_ = bf16[32,4096]{1,0:T(8,128)(2,1)S(1)} collective-permute-done((bf16[32,4096]{1,0:T(8,128)(2,1)}, bf16[32,4096]{1,0:T(8,128)(2,1)S(1)}, u32[]{:S(2)}, u32[]{:S(2)}) %collective-permute-start.13) | collective-permute-done | bytes 262176 | tf_op jit(solution)/shard_map/ppermute | solution.py:272
  43.4 2.4 %collective-permute-start.12 = (bf16[32,4096]{1,0:T(8,128)(2,1)S(1)}, bf16[32,4096]{1,0:T(8,128)(2,1)S(1)}, u32[]{:S(2)}, u32[]{:S(2)}) collective-permute-start(bf16[32,4096]{1,0:T(8,128)(2,1)S(1)} %collective-permute-done.11.refs_0_), channel_id=1, source_target_pairs={{0,4},{1,3},{4,8},{5,1},{8,12},{9,5},{12,14},{13,9},{14,10},{15,13... | collective-permute-start | bytes 786440 | tf_op jit(solution)/shard_map/ppermute | solution.py:272
  47.0 4.7 %shard_map.111 = (f32[32,4096]{1,0:T(8,128)S(1)}, f32[32,4096]{1,0:T(8,128)S(1)}) custom-call(s32[1]{0:T(128)} %bitcast.index_ref, bf16[4096,256]{1,0:T(8,128)(2,1)S(1)} %bitcast.12, bf16[4096,256]{1,0:T(8,128)(2,1)S(1)} %bitcast.17, bf16[256,4096]{1,0:T(8,128)(2,1)S(1)} %bitcast.22, f32[64,8]{1,0:T(8,128)S(1)} %compare_select_fusion.hits_hbm, ...), custom_call_target="tpu_custom_call" | custom-call | flops 805306368 | bytes 14680064 | tf_op jit(solution)/shard_map/pallas_call | solution.py:218
  51.7 2.1 %collective-permute-start.27 = (bf16[32,4096]{1,0:T(8,128)(2,1)S(1)}, bf16[32,4096]{1,0:T(8,128)(2,1)S(1)}, u32[]{:S(2)}, u32[]{:S(2)}) collective-permute-start(bf16[32,4096]{1,0:T(8,128)(2,1)S(1)} %convert_element_type.121), channel_id=1, source_target_pairs={{0,4},{1,3},{4,8},{5,1},{8,12},{9,5},{12,14},{13,9},{14,10},{15,13... | collective-permute-start | bytes 786440 | tf_op jit(solution)/shard_map/ppermute | solution.py:272
  55.6 2.5 %collective-permute-start.16 = (bf16[64,4096]{1,0:T(8,128)(2,1)S(1)}, bf16[64,4096]{1,0:T(8,128)(2,1)S(1)}, u32[]{:S(2)}, u32[]{:S(2)}) collective-permute-start(bf16[64,4096]{1,0:T(8,128)(2,1)S(1)} %pad_maximum_fusion), channel_id=1, source_target_pairs={{0,4},{1,3},{4,8},{5,1},{8,12},{9,5},{12,14},{13,9},{14,10},{15,13... | collective-permute-start | bytes 1572872 | tf_op jit(solution)/shard_map/ppermute | solution.py:272
  58.1 2.9 %collective-permute-done.15.refs_2_ = bf16[64,4096]{1,0:T(8,128)(2,1)S(1)} collective-permute-done((bf16[64,4096]{1,0:T(8,128)(2,1)}, bf16[64,4096]{1,0:T(8,128)(2,1)S(1)}, u32[]{:S(2)}, u32[]{:S(2)}) %collective-permute-start.15) | collective-permute-done | bytes 524320 | tf_op jit(solution)/shard_map/ppermute | solution.py:272
  61.0 5.2 %shard_map.110 = (f32[32,4096]{1,0:T(8,128)S(1)}, f32[32,4096]{1,0:T(8,128)S(1)}, f32[32,4096]{1,0:T(8,128)S(1)}, f32[32,4096]{1,0:T(8,128)S(1)}, f32[32,4096]{1,0:T(8,128)S(1)}, /*index=5*/f32[32,4096]{1,0:T(8,128)S(1)}) custom-call(s32[1]{0:T(128)} %bitcast.index_ref, bf16[4096,256]{1,0:T(8,128)(2,1)S(1)} %bitcast.13, bf16[4096,256]{1,0:T(8,128)(2,1)S(1)} %bitcast.18, ...), custom_call_target="tpu_custom_call" | custom-call | flops 805306368 | bytes 14680064 | tf_op jit(solution)/shard_map/pallas_call | solution.py:218
  66.3 2.0 %collective-permute-start.21 = (bf16[32,4096]{1,0:T(8,128)(2,1)S(1)}, bf16[32,4096]{1,0:T(8,128)(2,1)S(1)}, u32[]{:S(2)}, u32[]{:S(2)}) collective-permute-start(bf16[32,4096]{1,0:T(8,128)(2,1)S(1)} %add_convert_fusion.13), channel_id=1, source_target_pairs={{0,4},{1,3},{4,8},{5,1},{8,12},{9,5},{12,14},{13,9},{14,10},{15,13... | collective-permute-start | bytes 786440 | tf_op jit(solution)/shard_map/ppermute | solution.py:272
  69.3 4.4 %collective-permute-done.16.refs_0_ = bf16[64,4096]{1,0:T(8,128)(2,1)S(1)} collective-permute-done((bf16[64,4096]{1,0:T(8,128)(2,1)S(1)}, bf16[64,4096]{1,0:T(8,128)(2,1)S(1)}, u32[]{:S(2)}, u32[]{:S(2)}) %collective-permute-start.16) | collective-permute-done | bytes 524320 | tf_op jit(solution)/shard_map/ppermute | solution.py:272
  75.8 4.3 %shard_map.112 = (f32[32,4096]{1,0:T(8,128)S(1)}, f32[32,4096]{1,0:T(8,128)S(1)}, f32[32,4096]{1,0:T(8,128)S(1)}, f32[32,4096]{1,0:T(8,128)S(1)}) custom-call(s32[1]{0:T(128)} %bitcast.index_ref, bf16[4096,256]{1,0:T(8,128)(2,1)S(1)} %bitcast.14, bf16[4096,256]{1,0:T(8,128)(2,1)S(1)} %bitcast.19, bf16[256,4096]{1,0:T(8,128)(2,1)S(1)} %bitcast.24, ...), custom_call_target="tpu_custom_call" | custom-call | flops 805306368 | bytes 14680064 | tf_op jit(solution)/shard_map/pallas_call | solution.py:218
  80.3 2.1 %collective-permute-start.22 = (bf16[32,4096]{1,0:T(8,128)(2,1)S(1)}, bf16[32,4096]{1,0:T(8,128)(2,1)S(1)}, u32[]{:S(2)}, u32[]{:S(2)}) collective-permute-start(bf16[32,4096]{1,0:T(8,128)(2,1)S(1)} %add_convert_fusion.12), channel_id=1, source_target_pairs={{0,4},{1,3},{4,8},{5,1},{8,12},{9,5},{12,14},{13,9},{14,10},{15,13... | collective-permute-start | bytes 786440 | tf_op jit(solution)/shard_map/ppermute | solution.py:272
  83.7 2.5 %collective-permute-start.29 = (bf16[32,4096]{1,0:T(8,128)(2,1)S(1)}, bf16[32,4096]{1,0:T(8,128)(2,1)S(1)}, u32[]{:S(2)}, u32[]{:S(2)}) collective-permute-start(bf16[32,4096]{1,0:T(8,128)(2,1)S(1)} %add_convert_fusion.5), channel_id=1, source_target_pairs={{0,4},{1,3},{4,8},{5,1},{8,12},{9,5},{12,14},{13,9},{14,10},{15,13... | collective-permute-start | bytes 786440 | tf_op jit(solution)/shard_map/ppermute | solution.py:272
  86.2 4.3 %collective-permute-done.19.refs_0_ = bf16[64,4096]{1,0:T(8,128)(2,1)S(1)} collective-permute-done((bf16[64,4096]{1,0:T(8,128)(2,1)S(1)}, bf16[64,4096]{1,0:T(8,128)(2,1)S(1)}, u32[]{:S(2)}, u32[]{:S(2)}) %collective-permute-start.19) | collective-permute-done | bytes 524320 | tf_op jit(solution)/shard_map/ppermute | solution.py:272
  90.7 4.3 %shard_map.113 = (f32[32,4096]{1,0:T(8,128)S(1)}, f32[32,4096]{1,0:T(8,128)S(1)}, f32[32,4096]{1,0:T(8,128)S(1)}, f32[32,4096]{1,0:T(8,128)S(1)}) custom-call(s32[1]{0:T(128)} %bitcast.index_ref, bf16[4096,256]{1,0:T(8,128)(2,1)S(1)} %bitcast.15, bf16[4096,256]{1,0:T(8,128)(2,1)S(1)} %bitcast.20, bf16[256,4096]{1,0:T(8,128)(2,1)S(1)} %bitcast.25, ...), custom_call_target="tpu_custom_call" | custom-call | flops 805306368 | bytes 14680064 | tf_op jit(solution)/shard_map/pallas_call | solution.py:218
  95.1 1.6 %collective-permute-start.23 = (bf16[32,4096]{1,0:T(8,128)(2,1)S(1)}, bf16[32,4096]{1,0:T(8,128)(2,1)S(1)}, u32[]{:S(2)}, u32[]{:S(2)}) collective-permute-start(bf16[32,4096]{1,0:T(8,128)(2,1)S(1)} %add_convert_fusion.11), channel_id=1, source_target_pairs={{0,4},{1,3},{4,8},{5,1},{8,12},{9,5},{12,14},{13,9},{14,10},{15,13... | collective-permute-start | bytes 786440 | tf_op jit(solution)/shard_map/ppermute | solution.py:272
  96.8 1.8 %collective-permute-start.30 = (bf16[32,4096]{1,0:T(8,128)(2,1)S(1)}, bf16[32,4096]{1,0:T(8,128)(2,1)S(1)}, u32[]{:S(2)}, u32[]{:S(2)}) collective-permute-start(bf16[32,4096]{1,0:T(8,128)(2,1)S(1)} %add_convert_fusion.4), channel_id=1, source_target_pairs={{0,4},{1,3},{4,8},{5,1},{8,12},{9,5},{12,14},{13,9},{14,10},{15,13... | collective-permute-start | bytes 786440 | tf_op jit(solution)/shard_map/ppermute | solution.py:272
  98.6 2.9 %collective-permute-done.23 = bf16[32,4096]{1,0:T(8,128)(2,1)S(1)} collective-permute-done((bf16[32,4096]{1,0:T(8,128)(2,1)S(1)}, bf16[32,4096]{1,0:T(8,128)(2,1)S(1)}, u32[]{:S(2)}, u32[]{:S(2)}) %collective-permute-start.23) | collective-permute-done | bytes 262176 | tf_op jit(solution)/shard_map/ppermute | solution.py:272
  101.6 1.6 %collective-permute-start.24 = (bf16[32,4096]{1,0:T(8,128)(2,1)S(1)}, bf16[32,4096]{1,0:T(8,128)(2,1)S(1)}, u32[]{:S(2)}, u32[]{:S(2)}) collective-permute-start(bf16[32,4096]{1,0:T(8,128)(2,1)S(1)} %add_convert_fusion.10), channel_id=1, source_target_pairs={{0,4},{1,3},{4,8},{5,1},{8,12},{9,5},{12,14},{13,9},{14,10},{15,13... | collective-permute-start | bytes 786440 | tf_op jit(solution)/shard_map/ppermute | solution.py:272
  104.4 1.6 %collective-permute-start.31 = (bf16[32,4096]{1,0:T(8,128)(2,1)S(1)}, bf16[32,4096]{1,0:T(8,128)(2,1)S(1)}, u32[]{:S(2)}, u32[]{:S(2)}) collective-permute-start(bf16[32,4096]{1,0:T(8,128)(2,1)S(1)} %add_convert_fusion.3), channel_id=1, source_target_pairs={{0,4},{1,3},{4,8},{5,1},{8,12},{9,5},{12,14},{13,9},{14,10},{15,13... | collective-permute-start | bytes 786440 | tf_op jit(solution)/shard_map/ppermute | solution.py:272
  106.0 2.0 %collective-permute-done.24 = bf16[32,4096]{1,0:T(8,128)(2,1)S(1)} collective-permute-done((bf16[32,4096]{1,0:T(8,128)(2,1)S(1)}, bf16[32,4096]{1,0:T(8,128)(2,1)S(1)}, u32[]{:S(2)}, u32[]{:S(2)}) %collective-permute-start.24) | collective-permute-done | bytes 262176 | tf_op jit(solution)/shard_map/ppermute | solution.py:272
  108.1 1.6 %collective-permute-start.25 = (bf16[32,4096]{1,0:T(8,128)(2,1)S(1)}, bf16[32,4096]{1,0:T(8,128)(2,1)S(1)}, u32[]{:S(2)}, u32[]{:S(2)}) collective-permute-start(bf16[32,4096]{1,0:T(8,128)(2,1)S(1)} %add_convert_fusion.9), channel_id=1, source_target_pairs={{0,4},{1,3},{4,8},{5,1},{8,12},{9,5},{12,14},{13,9},{14,10},{15,13... | collective-permute-start | bytes 786440 | tf_op jit(solution)/shard_map/ppermute | solution.py:272
  110.9 1.6 %collective-permute-start.32 = (bf16[32,4096]{1,0:T(8,128)(2,1)S(1)}, bf16[32,4096]{1,0:T(8,128)(2,1)S(1)}, u32[]{:S(2)}, u32[]{:S(2)}) collective-permute-start(bf16[32,4096]{1,0:T(8,128)(2,1)S(1)} %add_convert_fusion.2), channel_id=1, source_target_pairs={{0,4},{1,3},{4,8},{5,1},{8,12},{9,5},{12,14},{13,9},{14,10},{15,13... | collective-permute-start | bytes 786440 | tf_op jit(solution)/shard_map/ppermute | solution.py:272
  112.5 2.0 %collective-permute-done.25 = bf16[32,4096]{1,0:T(8,128)(2,1)S(1)} collective-permute-done((bf16[32,4096]{1,0:T(8,128)(2,1)S(1)}, bf16[32,4096]{1,0:T(8,128)(2,1)S(1)}, u32[]{:S(2)}, u32[]{:S(2)}) %collective-permute-start.25) | collective-permute-done | bytes 262176 | tf_op jit(solution)/shard_map/ppermute | solution.py:272
  114.5 1.6 %collective-permute-start.26 = (bf16[32,4096]{1,0:T(8,128)(2,1)S(1)}, bf16[32,4096]{1,0:T(8,128)(2,1)S(1)}, u32[]{:S(2)}, u32[]{:S(2)}) collective-permute-start(bf16[32,4096]{1,0:T(8,128)(2,1)S(1)} %add_convert_fusion.8), channel_id=1, source_target_pairs={{0,4},{1,3},{4,8},{5,1},{8,12},{9,5},{12,14},{13,9},{14,10},{15,13... | collective-permute-start | bytes 786440 | tf_op jit(solution)/shard_map/ppermute | solution.py:272
  117.3 1.6 %collective-permute-start.33 = (bf16[32,4096]{1,0:T(8,128)(2,1)S(1)}, bf16[32,4096]{1,0:T(8,128)(2,1)S(1)}, u32[]{:S(2)}, u32[]{:S(2)}) collective-permute-start(bf16[32,4096]{1,0:T(8,128)(2,1)S(1)} %add_convert_fusion.1), channel_id=1, source_target_pairs={{0,4},{1,3},{4,8},{5,1},{8,12},{9,5},{12,14},{13,9},{14,10},{15,13... | collective-permute-start | bytes 786440 | tf_op jit(solution)/shard_map/ppermute | solution.py:272
  119.0 2.0 %collective-permute-done.26 = bf16[32,4096]{1,0:T(8,128)(2,1)S(1)} collective-permute-done((bf16[32,4096]{1,0:T(8,128)(2,1)S(1)}, bf16[32,4096]{1,0:T(8,128)(2,1)S(1)}, u32[]{:S(2)}, u32[]{:S(2)}) %collective-permute-start.26) | collective-permute-done | bytes 262176 | tf_op jit(solution)/shard_map/ppermute | solution.py:272
  121.1 2.7 %collective-permute-done.33 = bf16[32,4096]{1,0:T(8,128)(2,1)S(1)} collective-permute-done((bf16[32,4096]{1,0:T(8,128)(2,1)S(1)}, bf16[32,4096]{1,0:T(8,128)(2,1)S(1)}, u32[]{:S(2)}, u32[]{:S(2)}) %collective-permute-start.33) | collective-permute-done | bytes 262176 | tf_op jit(solution)/shard_map/ppermute | solution.py:272
  (92 shorter events, 28.5 us)
Async XLA Ops:
  1.7 8.1 %collective-permute-start.3 = (bf16[64,640]{1,0:T(8,128)(2,1)S(1)}, bf16[64,640]{1,0:T(8,128)(2,1)S(1)}, u32[]{:S(2)}, u32[]{:S(2)}) collective-permute-start(bf16[64,640]{1,0:T(8,128)(2,1)S(1)} %get-tuple-element.81), channel_id=1, source_target_pairs={{0,8},{1,9},{2,10},{3,11},{4,12},{5,13},{6,14},{7,15},{8,0},{9,1},... | collective-permute-start | bytes 245768 | tf_op jit(solution)/shard_map/ppermute | solution.py:250
  5.8 6.6 %collective-permute-start = (bf16[64,640]{1,0:T(8,128)(2,1)S(1)}, bf16[64,640]{1,0:T(8,128)(2,1)S(1)}, u32[]{:S(2)}, u32[]{:S(2)}) collective-permute-start(bf16[64,640]{1,0:T(8,128)(2,1)S(1)} %get-tuple-element.81), channel_id=1, source_target_pairs={{0,2},{1,3},{2,0},{3,1},{4,6},{5,7},{6,4},{7,5},{8,10},{9,11},{10,... | collective-permute-start | bytes 245768 | tf_op jit(solution)/shard_map/ppermute | solution.py:250
  7.3 6.3 %collective-permute-start.1 = (bf16[64,640]{1,0:T(8,128)(2,1)S(1)}, bf16[64,640]{1,0:T(8,128)(2,1)S(1)}, u32[]{:S(2)}, u32[]{:S(2)}) collective-permute-start(bf16[64,640]{1,0:T(8,128)(2,1)S(1)} %get-tuple-element.81), channel_id=1, source_target_pairs={{0,4},{1,5},{2,6},{3,7},{4,0},{5,1},{6,2},{7,3},{8,12},{9,13},{10,... | collective-permute-start | bytes 245768 | tf_op jit(solution)/shard_map/ppermute | solution.py:250
  8.9 5.6 %collective-permute-start.2 = (bf16[64,640]{1,0:T(8,128)(2,1)S(1)}, bf16[64,640]{1,0:T(8,128)(2,1)S(1)}, u32[]{:S(2)}, u32[]{:S(2)}) collective-permute-start(bf16[64,640]{1,0:T(8,128)(2,1)S(1)} %get-tuple-element.81), channel_id=1, source_target_pairs={{0,6},{1,7},{2,4},{3,5},{4,2},{5,3},{6,0},{7,1},{8,14},{9,15},{10,... | collective-permute-start | bytes 245768 | tf_op jit(solution)/shard_map/ppermute | solution.py:250
  9.8 5.5 %collective-permute-start.4 = (bf16[64,640]{1,0:T(8,128)(2,1)S(1)}, bf16[64,640]{1,0:T(8,128)(2,1)S(1)}, u32[]{:S(2)}, u32[]{:S(2)}) collective-permute-start(bf16[64,640]{1,0:T(8,128)(2,1)S(1)} %collective-permute-done.3), channel_id=1, source_target_pairs={{0,2},{1,3},{2,0},{3,1},{4,6},{5,7},{6,4},{7,5},{8,10},{9,11},{10,... | collective-permute-start | bytes 245768 | tf_op jit(solution)/shard_map/ppermute | solution.py:250
  12.4 5.3 %collective-permute-start.6 = (bf16[64,640]{1,0:T(8,128)(2,1)S(1)}, bf16[64,640]{1,0:T(8,128)(2,1)S(1)}, u32[]{:S(2)}, u32[]{:S(2)}) collective-permute-start(bf16[64,640]{1,0:T(8,128)(2,1)S(1)} %collective-permute-done.3), channel_id=1, source_target_pairs={{0,6},{1,7},{2,4},{3,5},{4,2},{5,3},{6,0},{7,1},{8,14},{9,15},{10,... | collective-permute-start | bytes 245768 | tf_op jit(solution)/shard_map/ppermute | solution.py:250
  19.9 12.7 %collective-permute-start.10 = (bf16[256,4096]{1,0:T(8,128)(2,1)}, bf16[256,4096]{1,0:T(8,128)(2,1)}, u32[]{:S(2)}, u32[]{:S(2)}) collective-permute-start(bf16[256,4096]{1,0:T(8,128)(2,1)} %bitcast.21), channel_id=1, source_target_pairs={{0,1},{1,0},{2,3},{3,2},{4,5},{5,4},{6,7},{7,6},{8,9},{9,8},{10,11... | collective-permute-start | bytes 6291464 | tf_op jit(solution)/shard_map/ppermute | solution.py:261
  20.0 12.5 %collective-permute-start.8 = (bf16[4096,256]{1,0:T(8,128)(2,1)}, bf16[4096,256]{1,0:T(8,128)(2,1)}, u32[]{:S(2)}, u32[]{:S(2)}) collective-permute-start(bf16[4096,256]{1,0:T(8,128)(2,1)} %bitcast.11), channel_id=1, source_target_pairs={{0,1},{1,0},{2,3},{3,2},{4,5},{5,4},{6,7},{7,6},{8,9},{9,8},{10,11... | collective-permute-start | bytes 6291464 | tf_op jit(solution)/shard_map/ppermute | solution.py:261
  20.4 12.2 %collective-permute-start.9 = (bf16[4096,256]{1,0:T(8,128)(2,1)}, bf16[4096,256]{1,0:T(8,128)(2,1)}, u32[]{:S(2)}, u32[]{:S(2)}) collective-permute-start(bf16[4096,256]{1,0:T(8,128)(2,1)} %bitcast.16), channel_id=1, source_target_pairs={{0,1},{1,0},{2,3},{3,2},{4,5},{5,4},{6,7},{7,6},{8,9},{9,8},{10,11... | collective-permute-start | bytes 6291464 | tf_op jit(solution)/shard_map/ppermute | solution.py:261
  32.6 10.9 %collective-permute-start.11 = (bf16[32,4096]{1,0:T(8,128)(2,1)}, bf16[32,4096]{1,0:T(8,128)(2,1)S(1)}, u32[]{:S(2)}, u32[]{:S(2)}) collective-permute-start(bf16[32,4096]{1,0:T(8,128)(2,1)} %get-tuple-element.56.refs_3_), channel_id=1, source_target_pairs={{0,4},{1,3},{4,8},{5,1},{8,12},{9,5},{12,14},{13,9},{14,10},{15,13... | collective-permute-start | bytes 786440 | tf_op jit(solution)/shard_map/ppermute | solution.py:272
  33.7 8.3 %collective-permute-start.13 = (bf16[32,4096]{1,0:T(8,128)(2,1)}, bf16[32,4096]{1,0:T(8,128)(2,1)S(1)}, u32[]{:S(2)}, u32[]{:S(2)}) collective-permute-start(bf16[32,4096]{1,0:T(8,128)(2,1)} %get-tuple-element.58.refs_4_), channel_id=1, source_target_pairs={{0,4},{1,3},{4,8},{5,1},{8,12},{9,5},{12,14},{13,9},{14,10},{15,13... | collective-permute-start | bytes 786440 | tf_op jit(solution)/shard_map/ppermute | solution.py:272
  42.0 12.2 %collective-permute-start.14 = (bf16[32,4096]{1,0:T(8,128)(2,1)S(1)}, bf16[32,4096]{1,0:T(8,128)(2,1)S(1)}, u32[]{:S(2)}, u32[]{:S(2)}) collective-permute-start(bf16[32,4096]{1,0:T(8,128)(2,1)S(1)} %collective-permute-done.13.refs_1_), channel_id=1, source_target_pairs={{0,4},{1,3},{4,8},{5,1},{8,12},{9,5},{12,14},{13,9},{14,10},{15,13... | collective-permute-start | bytes 786440 | tf_op jit(solution)/shard_map/ppermute | solution.py:272
  43.4 12.1 %collective-permute-start.12 = (bf16[32,4096]{1,0:T(8,128)(2,1)S(1)}, bf16[32,4096]{1,0:T(8,128)(2,1)S(1)}, u32[]{:S(2)}, u32[]{:S(2)}) collective-permute-start(bf16[32,4096]{1,0:T(8,128)(2,1)S(1)} %collective-permute-done.11.refs_0_), channel_id=1, source_target_pairs={{0,4},{1,3},{4,8},{5,1},{8,12},{9,5},{12,14},{13,9},{14,10},{15,13... | collective-permute-start | bytes 786440 | tf_op jit(solution)/shard_map/ppermute | solution.py:272
  46.9 14.0 %collective-permute-start.15 = (bf16[64,4096]{1,0:T(8,128)(2,1)}, bf16[64,4096]{1,0:T(8,128)(2,1)S(1)}, u32[]{:S(2)}, u32[]{:S(2)}) collective-permute-start(bf16[64,4096]{1,0:T(8,128)(2,1)} %get-tuple-element.61), channel_id=1, source_target_pairs={{4,0},{3,1},{8,4},{1,5},{12,8},{5,9},{14,12},{9,13},{10,14},{13,15... | collective-permute-start | bytes 1572872 | tf_op jit(solution)/shard_map/ppermute | solution.py:272
  51.7 16.6 %collective-permute-start.27 = (bf16[32,4096]{1,0:T(8,128)(2,1)S(1)}, bf16[32,4096]{1,0:T(8,128)(2,1)S(1)}, u32[]{:S(2)}, u32[]{:S(2)}) collective-permute-start(bf16[32,4096]{1,0:T(8,128)(2,1)S(1)} %convert_element_type.121), channel_id=1, source_target_pairs={{0,4},{1,3},{4,8},{5,1},{8,12},{9,5},{12,14},{13,9},{14,10},{15,13... | collective-permute-start | bytes 786440 | tf_op jit(solution)/shard_map/ppermute | solution.py:272
  53.8 12.4 %collective-permute-start.18 = (bf16[32,4096]{1,0:T(8,128)(2,1)S(1)}, bf16[32,4096]{1,0:T(8,128)(2,1)S(1)}, u32[]{:S(2)}, u32[]{:S(2)}) collective-permute-start(bf16[32,4096]{1,0:T(8,128)(2,1)S(1)} %convert_element_type.105), channel_id=1, source_target_pairs={{0,4},{1,3},{4,8},{5,1},{8,12},{9,5},{12,14},{13,9},{14,10},{15,13... | collective-permute-start | bytes 786440 | tf_op jit(solution)/shard_map/ppermute | solution.py:272
  55.6 18.1 %collective-permute-start.16 = (bf16[64,4096]{1,0:T(8,128)(2,1)S(1)}, bf16[64,4096]{1,0:T(8,128)(2,1)S(1)}, u32[]{:S(2)}, u32[]{:S(2)}) collective-permute-start(bf16[64,4096]{1,0:T(8,128)(2,1)S(1)} %pad_maximum_fusion), channel_id=1, source_target_pairs={{0,4},{1,3},{4,8},{5,1},{8,12},{9,5},{12,14},{13,9},{14,10},{15,13... | collective-permute-start | bytes 1572872 | tf_op jit(solution)/shard_map/ppermute | solution.py:272
  61.0 14.9 %collective-permute-start.17 = (bf16[64,4096]{1,0:T(8,128)(2,1)S(1)}, bf16[64,4096]{1,0:T(8,128)(2,1)S(1)}, u32[]{:S(2)}, u32[]{:S(2)}) collective-permute-start(bf16[64,4096]{1,0:T(8,128)(2,1)S(1)} %collective-permute-done.15.refs_2_), channel_id=1, source_target_pairs={{4,0},{3,1},{8,4},{1,5},{12,8},{5,9},{14,12},{9,13},{10,14},{13,15... | collective-permute-start | bytes 1572872 | tf_op jit(solution)/shard_map/ppermute | solution.py:272
  66.3 13.9 %collective-permute-start.21 = (bf16[32,4096]{1,0:T(8,128)(2,1)S(1)}, bf16[32,4096]{1,0:T(8,128)(2,1)S(1)}, u32[]{:S(2)}, u32[]{:S(2)}) collective-permute-start(bf16[32,4096]{1,0:T(8,128)(2,1)S(1)} %add_convert_fusion.13), channel_id=1, source_target_pairs={{0,4},{1,3},{4,8},{5,1},{8,12},{9,5},{12,14},{13,9},{14,10},{15,13... | collective-permute-start | bytes 786440 | tf_op jit(solution)/shard_map/ppermute | solution.py:272
  68.3 15.3 %collective-permute-start.28 = (bf16[32,4096]{1,0:T(8,128)(2,1)S(1)}, bf16[32,4096]{1,0:T(8,128)(2,1)S(1)}, u32[]{:S(2)}, u32[]{:S(2)}) collective-permute-start(bf16[32,4096]{1,0:T(8,128)(2,1)S(1)} %add_convert_fusion.6), channel_id=1, source_target_pairs={{0,4},{1,3},{4,8},{5,1},{8,12},{9,5},{12,14},{13,9},{14,10},{15,13... | collective-permute-start | bytes 786440 | tf_op jit(solution)/shard_map/ppermute | solution.py:272
  73.7 16.9 %collective-permute-start.19 = (bf16[64,4096]{1,0:T(8,128)(2,1)S(1)}, bf16[64,4096]{1,0:T(8,128)(2,1)S(1)}, u32[]{:S(2)}, u32[]{:S(2)}) collective-permute-start(bf16[64,4096]{1,0:T(8,128)(2,1)S(1)} %collective-permute-done.16.refs_0_), channel_id=1, source_target_pairs={{0,4},{1,3},{4,8},{5,1},{8,12},{9,5},{12,14},{13,9},{14,10},{15,13... | collective-permute-start | bytes 1572872 | tf_op jit(solution)/shard_map/ppermute | solution.py:272
  75.8 14.9 %collective-permute-start.20 = (bf16[64,4096]{1,0:T(8,128)(2,1)S(1)}, bf16[64,4096]{1,0:T(8,128)(2,1)S(1)}, u32[]{:S(2)}, u32[]{:S(2)}) collective-permute-start(bf16[64,4096]{1,0:T(8,128)(2,1)S(1)} %collective-permute-done.17.refs_1_), channel_id=1, source_target_pairs={{4,0},{3,1},{8,4},{1,5},{12,8},{5,9},{14,12},{9,13},{10,14},{13,15... | collective-permute-start | bytes 1572872 | tf_op jit(solution)/shard_map/ppermute | solution.py:272
  80.3 14.8 %collective-permute-start.22 = (bf16[32,4096]{1,0:T(8,128)(2,1)S(1)}, bf16[32,4096]{1,0:T(8,128)(2,1)S(1)}, u32[]{:S(2)}, u32[]{:S(2)}) collective-permute-start(bf16[32,4096]{1,0:T(8,128)(2,1)S(1)} %add_convert_fusion.12), channel_id=1, source_target_pairs={{0,4},{1,3},{4,8},{5,1},{8,12},{9,5},{12,14},{13,9},{14,10},{15,13... | collective-permute-start | bytes 786440 | tf_op jit(solution)/shard_map/ppermute | solution.py:272
  83.7 13.1 %collective-permute-start.29 = (bf16[32,4096]{1,0:T(8,128)(2,1)S(1)}, bf16[32,4096]{1,0:T(8,128)(2,1)S(1)}, u32[]{:S(2)}, u32[]{:S(2)}) collective-permute-start(bf16[32,4096]{1,0:T(8,128)(2,1)S(1)} %add_convert_fusion.5), channel_id=1, source_target_pairs={{0,4},{1,3},{4,8},{5,1},{8,12},{9,5},{12,14},{13,9},{14,10},{15,13... | collective-permute-start | bytes 786440 | tf_op jit(solution)/shard_map/ppermute | solution.py:272
  95.1 6.4 %collective-permute-start.23 = (bf16[32,4096]{1,0:T(8,128)(2,1)S(1)}, bf16[32,4096]{1,0:T(8,128)(2,1)S(1)}, u32[]{:S(2)}, u32[]{:S(2)}) collective-permute-start(bf16[32,4096]{1,0:T(8,128)(2,1)S(1)} %add_convert_fusion.11), channel_id=1, source_target_pairs={{0,4},{1,3},{4,8},{5,1},{8,12},{9,5},{12,14},{13,9},{14,10},{15,13... | collective-permute-start | bytes 786440 | tf_op jit(solution)/shard_map/ppermute | solution.py:272
  96.8 7.5 %collective-permute-start.30 = (bf16[32,4096]{1,0:T(8,128)(2,1)S(1)}, bf16[32,4096]{1,0:T(8,128)(2,1)S(1)}, u32[]{:S(2)}, u32[]{:S(2)}) collective-permute-start(bf16[32,4096]{1,0:T(8,128)(2,1)S(1)} %add_convert_fusion.4), channel_id=1, source_target_pairs={{0,4},{1,3},{4,8},{5,1},{8,12},{9,5},{12,14},{13,9},{14,10},{15,13... | collective-permute-start | bytes 786440 | tf_op jit(solution)/shard_map/ppermute | solution.py:272
  101.6 6.4 %collective-permute-start.24 = (bf16[32,4096]{1,0:T(8,128)(2,1)S(1)}, bf16[32,4096]{1,0:T(8,128)(2,1)S(1)}, u32[]{:S(2)}, u32[]{:S(2)}) collective-permute-start(bf16[32,4096]{1,0:T(8,128)(2,1)S(1)} %add_convert_fusion.10), channel_id=1, source_target_pairs={{0,4},{1,3},{4,8},{5,1},{8,12},{9,5},{12,14},{13,9},{14,10},{15,13... | collective-permute-start | bytes 786440 | tf_op jit(solution)/shard_map/ppermute | solution.py:272
  104.4 6.4 %collective-permute-start.31 = (bf16[32,4096]{1,0:T(8,128)(2,1)S(1)}, bf16[32,4096]{1,0:T(8,128)(2,1)S(1)}, u32[]{:S(2)}, u32[]{:S(2)}) collective-permute-start(bf16[32,4096]{1,0:T(8,128)(2,1)S(1)} %add_convert_fusion.3), channel_id=1, source_target_pairs={{0,4},{1,3},{4,8},{5,1},{8,12},{9,5},{12,14},{13,9},{14,10},{15,13... | collective-permute-start | bytes 786440 | tf_op jit(solution)/shard_map/ppermute | solution.py:272
  108.1 6.4 %collective-permute-start.25 = (bf16[32,4096]{1,0:T(8,128)(2,1)S(1)}, bf16[32,4096]{1,0:T(8,128)(2,1)S(1)}, u32[]{:S(2)}, u32[]{:S(2)}) collective-permute-start(bf16[32,4096]{1,0:T(8,128)(2,1)S(1)} %add_convert_fusion.9), channel_id=1, source_target_pairs={{0,4},{1,3},{4,8},{5,1},{8,12},{9,5},{12,14},{13,9},{14,10},{15,13... | collective-permute-start | bytes 786440 | tf_op jit(solution)/shard_map/ppermute | solution.py:272
  110.9 6.4 %collective-permute-start.32 = (bf16[32,4096]{1,0:T(8,128)(2,1)S(1)}, bf16[32,4096]{1,0:T(8,128)(2,1)S(1)}, u32[]{:S(2)}, u32[]{:S(2)}) collective-permute-start(bf16[32,4096]{1,0:T(8,128)(2,1)S(1)} %add_convert_fusion.2), channel_id=1, source_target_pairs={{0,4},{1,3},{4,8},{5,1},{8,12},{9,5},{12,14},{13,9},{14,10},{15,13... | collective-permute-start | bytes 786440 | tf_op jit(solution)/shard_map/ppermute | solution.py:272
  114.5 6.4 %collective-permute-start.26 = (bf16[32,4096]{1,0:T(8,128)(2,1)S(1)}, bf16[32,4096]{1,0:T(8,128)(2,1)S(1)}, u32[]{:S(2)}, u32[]{:S(2)}) collective-permute-start(bf16[32,4096]{1,0:T(8,128)(2,1)S(1)} %add_convert_fusion.8), channel_id=1, source_target_pairs={{0,4},{1,3},{4,8},{5,1},{8,12},{9,5},{12,14},{13,9},{14,10},{15,13... | collective-permute-start | bytes 786440 | tf_op jit(solution)/shard_map/ppermute | solution.py:272
  117.3 6.4 %collective-permute-start.33 = (bf16[32,4096]{1,0:T(8,128)(2,1)S(1)}, bf16[32,4096]{1,0:T(8,128)(2,1)S(1)}, u32[]{:S(2)}, u32[]{:S(2)}) collective-permute-start(bf16[32,4096]{1,0:T(8,128)(2,1)S(1)} %add_convert_fusion.1), channel_id=1, source_target_pairs={{0,4},{1,3},{4,8},{5,1},{8,12},{9,5},{12,14},{13,9},{14,10},{15,13... | collective-permute-start | bytes 786440 | tf_op jit(solution)/shard_map/ppermute | solution.py:272
  (12 other events, 138.8 us)

commit v14 on v12

--- a/solution.py
+++ b/solution.py
@@ -285,21 +285,26 @@
     rows[2] = move(rows[1])
     rows[chips - 1] = move(after((normed,), rows[1][-1]), back)
     rows[3] = move((jnp.concatenate(rows[2], axis=0),))
-    parts = dict(zip((1,), parts_of(rows, (1,))))
-    sums = rounded(parts[1])
-    for hop in range(1, chips):
+    hops = (2, chips - 1, 1)
+    parts = dict(zip(hops, parts_of(rows, hops)))
+    sums = rounded(parts[2])
+    rows[chips - 2] = move(rows[chips - 1], back)
+    direct = []
+    for hop in range(2, chips):
         arrived = move(sums)
         here, there = hop + 1, chips - hop
         if here <= turn:
-            if 3 < here + 1 <= turn:
+            if here < turn:
                 rows[here + 1] = move(after(rows[here], sums[0]))
-            if here < turn:
                 rows[there - 1] = move(after(rows[there], sums[0]), back)
-            hops = (here, there, 0) if hop == 1 else (here, there)
+            hops = (here, there, 0) if hop == 2 else (here, there)
             parts.update(zip(hops, parts_of(rows, hops)))
+        elif len(direct) < PIECES:
+            piece = parts[1][len(direct)].astype(jnp.bfloat16)
+            direct += move(after((piece,), sums[0]), back)
         if here < chips:
             sums = rounded(added(parts[here], arrived))
-    expert_out = jnp.concatenate(added(parts[0], arrived), axis=0)
+    expert_out = jnp.concatenate(added(added(parts[0], direct), arrived), axis=0)
     gate_weight = gate_fixed.astype(jnp.float32) / 65536.0
     return (values.astype(jnp.float32) + gate_weight * expert_out).astype(jnp.bfloat16)
 

time: 122 us -> 127 us (1.041)
  waiting for transfers between devices: 48.1 us -> 55.9 us
  Pallas kernels: 30.3 us -> 26.4 us
    ppermute x23, waiting for transfers between devices: 41.3 us -> 49.2 us  [move(): return tuple((lax.ppermute(x, 'ctx', way) for x in blocks))]
    pallas_call x4 -> x3, Pallas kernels: 18.5 us -> 14.6 us  [expert_parts(): pl.pallas_call(functools.partial(expert_kernel, hops=hops, chips=chips),...]
  transfers between devices with their start and end apart: 34 -> 34, of which waited for: 19 -> 22; matrix products, arithmetic and copies ran while one was open for 1% -> 1% of each run, Pallas kernels for 25% -> 21%
where the time goes in v14:
time: 127 us
  waiting for transfers between devices  55.9 us (44%)
  starting transfers between devices  39.7 us (31%)
  Pallas kernels  26.4 us (21%)
  other arithmetic  3.36 us (3%)
    ppermute x23, waiting for transfers between devices, move(): return tuple((lax.ppermute(x, 'ctx', way) for x in blocks))  49.2 us
    ppermute x23, starting transfers between devices, move(): return tuple((lax.ppermute(x, 'ctx', way) for x in blocks))  27.6 us
    pallas_call x3, Pallas kernels, expert_parts(): pl.pallas_call(functools.partial(expert_kernel, hops=hops, chips=chips),...  14.6 us
    pallas_call x1, Pallas kernels, attention(): pl.pallas_call(functools.partial(attention_kernel, tok=tok), grid_spec=gr...  11.8 us
    ppermute x7, starting transfers between devices, from_chip(): lax.ppermute(block, 'ctx', [(i, i ^ step * CORES) for i in range(n_ctx)])  11.4 us
    ppermute x7, waiting for transfers between devices, from_chip(): lax.ppermute(block, 'ctx', [(i, i ^ step * CORES) for i in range(n_ctx)])  4.54 us
  transfers between devices with their start and end apart: 34, of which 22 were waited for; matrix products, arithmetic and copies ran while one was open for 1% of the time, Pallas kernels for 21%

profile of v14, /device:TPU:0, one launch (start us, length us, event | category | flops | bytes accessed | tf_op | source)
XLA Modules:
  0.0 126.8 jit_solution(4160443505955461024)
XLA Ops:
  1.7 4.1 %collective-permute-start.3 = (bf16[64,640]{1,0:T(8,128)(2,1)S(1)}, bf16[64,640]{1,0:T(8,128)(2,1)S(1)}, u32[]{:S(2)}, u32[]{:S(2)}) collective-permute-start(bf16[64,640]{1,0:T(8,128)(2,1)S(1)} %get-tuple-element.79), channel_id=1, source_target_pairs={{0,8},{1,9},{2,10},{3,11},{4,12},{5,13},{6,14},{7,15},{8,0},{9,1},... | collective-permute-start | bytes 245768 | tf_op jit(solution)/shard_map/ppermute | solution.py:250
  7.3 1.6 %collective-permute-start.1 = (bf16[64,640]{1,0:T(8,128)(2,1)S(1)}, bf16[64,640]{1,0:T(8,128)(2,1)S(1)}, u32[]{:S(2)}, u32[]{:S(2)}) collective-permute-start(bf16[64,640]{1,0:T(8,128)(2,1)S(1)} %get-tuple-element.79), channel_id=1, source_target_pairs={{0,4},{1,5},{2,6},{3,7},{4,0},{5,1},{6,2},{7,3},{8,12},{9,13},{10,... | collective-permute-start | bytes 245768 | tf_op jit(solution)/shard_map/ppermute | solution.py:250
  9.8 1.6 %collective-permute-start.4 = (bf16[64,640]{1,0:T(8,128)(2,1)S(1)}, bf16[64,640]{1,0:T(8,128)(2,1)S(1)}, u32[]{:S(2)}, u32[]{:S(2)}) collective-permute-start(bf16[64,640]{1,0:T(8,128)(2,1)S(1)} %collective-permute-done.3), channel_id=1, source_target_pairs={{0,2},{1,3},{2,0},{3,1},{4,6},{5,7},{6,4},{7,5},{8,10},{9,11},{10,... | collective-permute-start | bytes 245768 | tf_op jit(solution)/shard_map/ppermute | solution.py:250
  15.9 1.8 %collective-permute-done.6 = bf16[64,640]{1,0:T(8,128)(2,1)S(1)} collective-permute-done((bf16[64,640]{1,0:T(8,128)(2,1)S(1)}, bf16[64,640]{1,0:T(8,128)(2,1)S(1)}, u32[]{:S(2)}, u32[]{:S(2)}) %collective-permute-start.6) | collective-permute-done | bytes 81952 | tf_op jit(solution)/shard_map/ppermute | solution.py:250
  17.8 2.1 %collective-permute-done.7.other_ref = bf16[512,640]{1,0:T(8,128)(2,1)S(1)} collective-permute-done((bf16[512,640]{1,0:T(8,128)(2,1)S(1)}, bf16[512,640]{1,0:T(8,128)(2,1)S(1)}, u32[]{:S(2)}, u32[]{:S(2)}) %collective-permute-start.7) | collective-permute-done | bytes 655392 | tf_op jit(solution)/shard_map/ppermute | solution.py:258
  20.8 11.8 %shard_map.109 = (bf16[64,4096]{1,0:T(8,128)(2,1)}, bf16[64,4096]{1,0:T(8,128)(2,1)}, bf16[32,4096]{1,0:T(8,128)(2,1)}, bf16[32,4096]{1,0:T(8,128)(2,1)}, f32[64,8]{1,0:T(8,128)}) custom-call(s32[1]{0:T(128)} %bitcast.index_ref, bf16[64,16384]{1,0:T(8,128)(2,1)} %q_ref.1, bf16[64,2048]{1,0:T(8,128)(2,1)} %qr_ref.1, bf16[512,640]{1,0:T(8,128)(2,1)} %copy-done.8, ...), custom_call_target="tpu_custom_call" | custom-call | flops 4831838208 | bytes 8388608 | tf_op jit(solution)/shard_map/pallas_call | solution.py:151
  33.7 2.7 %collective-permute-start.13 = (bf16[32,4096]{1,0:T(8,128)(2,1)}, bf16[32,4096]{1,0:T(8,128)(2,1)S(1)}, u32[]{:S(2)}, u32[]{:S(2)}) collective-permute-start(bf16[32,4096]{1,0:T(8,128)(2,1)} %get-tuple-element.56.refs_3_), channel_id=1, source_target_pairs={{0,4},{1,3},{4,8},{5,1},{8,12},{9,5},{12,14},{13,9},{14,10},{15,13... | collective-permute-start | bytes 786440 | tf_op jit(solution)/shard_map/ppermute | solution.py:272
  36.4 2.8 %collective-permute-done.11.refs_3_ = bf16[32,4096]{1,0:T(8,128)(2,1)S(1)} collective-permute-done((bf16[32,4096]{1,0:T(8,128)(2,1)}, bf16[32,4096]{1,0:T(8,128)(2,1)S(1)}, u32[]{:S(2)}, u32[]{:S(2)}) %collective-permute-start.11) | collective-permute-done | bytes 262176 | tf_op jit(solution)/shard_map/ppermute | solution.py:272
  44.0 2.7 %collective-permute-done.12.refs_0_ = bf16[32,4096]{1,0:T(8,128)(2,1)S(1)} collective-permute-done((bf16[32,4096]{1,0:T(8,128)(2,1)S(1)}, bf16[32,4096]{1,0:T(8,128)(2,1)S(1)}, u32[]{:S(2)}, u32[]{:S(2)}) %collective-permute-start.12) | collective-permute-done | bytes 262176 | tf_op jit(solution)/shard_map/ppermute | solution.py:272
  46.7 5.6 %collective-permute-done.14.refs_1_ = bf16[32,4096]{1,0:T(8,128)(2,1)S(1)} collective-permute-done((bf16[32,4096]{1,0:T(8,128)(2,1)S(1)}, bf16[32,4096]{1,0:T(8,128)(2,1)S(1)}, u32[]{:S(2)}, u32[]{:S(2)}) %collective-permute-start.14) | collective-permute-done | bytes 262176 | tf_op jit(solution)/shard_map/ppermute | solution.py:272
  52.3 1.6 %collective-permute-start.15 = (bf16[64,4096]{1,0:T(8,128)(2,1)S(1)}, bf16[64,4096]{1,0:T(8,128)(2,1)S(1)}, u32[]{:S(2)}, u32[]{:S(2)}) collective-permute-start(bf16[64,4096]{1,0:T(8,128)(2,1)S(1)} %pad_maximum_fusion), channel_id=1, source_target_pairs={{0,4},{1,3},{4,8},{5,1},{8,12},{9,5},{12,14},{13,9},{14,10},{15,13... | collective-permute-start | bytes 1572872 | tf_op jit(solution)/shard_map/ppermute | solution.py:272
  54.0 2.4 %collective-permute-done.16.refs_2_ = bf16[64,4096]{1,0:T(8,128)(2,1)S(1)} collective-permute-done((bf16[64,4096]{1,0:T(8,128)(2,1)}, bf16[64,4096]{1,0:T(8,128)(2,1)S(1)}, u32[]{:S(2)}, u32[]{:S(2)}) %collective-permute-start.16) | collective-permute-done | bytes 524320 | tf_op jit(solution)/shard_map/ppermute | solution.py:272
  57.4 5.1 %shard_map.111 = (f32[32,4096]{1,0:T(8,128)S(1)}, f32[32,4096]{1,0:T(8,128)S(1)}, f32[32,4096]{1,0:T(8,128)S(1)}, f32[32,4096]{1,0:T(8,128)S(1)}, f32[32,4096]{1,0:T(8,128)S(1)}, /*index=5*/f32[32,4096]{1,0:T(8,128)S(1)}) custom-call(s32[1]{0:T(128)} %bitcast.index_ref, bf16[4096,256]{1,0:T(8,128)(2,1)S(1)} %bitcast.10, bf16[4096,256]{1,0:T(8,128)(2,1)S(1)} %bitcast.14, ...), custom_call_target="tpu_custom_call" | custom-call | flops 805306368 | bytes 14680064 | tf_op jit(solution)/shard_map/pallas_call | solution.py:218
  62.6 1.8 %collective-permute-start.20 = (bf16[32,4096]{1,0:T(8,128)(2,1)S(1)}, bf16[32,4096]{1,0:T(8,128)(2,1)S(1)}, u32[]{:S(2)}, u32[]{:S(2)}) collective-permute-start(bf16[32,4096]{1,0:T(8,128)(2,1)S(1)} %convert_element_type.100), channel_id=1, source_target_pairs={{0,4},{1,3},{4,8},{5,1},{8,12},{9,5},{12,14},{13,9},{14,10},{15,13... | collective-permute-start | bytes 786440 | tf_op jit(solution)/shard_map/ppermute | solution.py:272
  64.5 1.7 %collective-permute-start.28 = (bf16[32,4096]{1,0:T(8,128)(2,1)S(1)}, bf16[32,4096]{1,0:T(8,128)(2,1)S(1)}, u32[]{:S(2)}, u32[]{:S(2)}) collective-permute-start(bf16[32,4096]{1,0:T(8,128)(2,1)S(1)} %convert_element_type.115), channel_id=1, source_target_pairs={{0,4},{1,3},{4,8},{5,1},{8,12},{9,5},{12,14},{13,9},{14,10},{15,13... | collective-permute-start | bytes 786440 | tf_op jit(solution)/shard_map/ppermute | solution.py:272
  66.5 1.9 %collective-permute-start.18 = (bf16[64,4096]{1,0:T(8,128)(2,1)S(1)}, bf16[64,4096]{1,0:T(8,128)(2,1)S(1)}, u32[]{:S(2)}, u32[]{:S(2)}) collective-permute-start(bf16[64,4096]{1,0:T(8,128)(2,1)S(1)} %collective-permute-done.15.refs_0_), channel_id=1, source_target_pairs={{0,4},{1,3},{4,8},{5,1},{8,12},{9,5},{12,14},{13,9},{14,10},{15,13... | collective-permute-start | bytes 1572872 | tf_op jit(solution)/shard_map/ppermute | solution.py:272
  68.4 5.2 %shard_map.110 = (f32[32,4096]{1,0:T(8,128)S(1)}, f32[32,4096]{1,0:T(8,128)S(1)}, f32[32,4096]{1,0:T(8,128)S(1)}, f32[32,4096]{1,0:T(8,128)S(1)}, f32[32,4096]{1,0:T(8,128)S(1)}, /*index=5*/f32[32,4096]{1,0:T(8,128)S(1)}) custom-call(s32[1]{0:T(128)} %bitcast.index_ref, bf16[4096,256]{1,0:T(8,128)(2,1)S(1)} %bitcast.11, bf16[4096,256]{1,0:T(8,128)(2,1)S(1)} %bitcast.15, ...), custom_call_target="tpu_custom_call" | custom-call | flops 805306368 | bytes 14680064 | tf_op jit(solution)/shard_map/pallas_call | solution.py:218
  73.6 2.5 %collective-permute-start.21 = (bf16[32,4096]{1,0:T(8,128)(2,1)S(1)}, bf16[32,4096]{1,0:T(8,128)(2,1)S(1)}, u32[]{:S(2)}, u32[]{:S(2)}) collective-permute-start(bf16[32,4096]{1,0:T(8,128)(2,1)S(1)} %add_convert_fusion.9), channel_id=1, source_target_pairs={{0,4},{1,3},{4,8},{5,1},{8,12},{9,5},{12,14},{13,9},{14,10},{15,13... | collective-permute-start | bytes 786440 | tf_op jit(solution)/shard_map/ppermute | solution.py:272
  76.2 2.3 %collective-permute-start.29 = (bf16[32,4096]{1,0:T(8,128)(2,1)S(1)}, bf16[32,4096]{1,0:T(8,128)(2,1)S(1)}, u32[]{:S(2)}, u32[]{:S(2)}) collective-permute-start(bf16[32,4096]{1,0:T(8,128)(2,1)S(1)} %add_convert_fusion.4), channel_id=1, source_target_pairs={{0,4},{1,3},{4,8},{5,1},{8,12},{9,5},{12,14},{13,9},{14,10},{15,13... | collective-permute-start | bytes 786440 | tf_op jit(solution)/shard_map/ppermute | solution.py:272
  78.5 2.3 %collective-permute-done.18.refs_0_ = bf16[64,4096]{1,0:T(8,128)(2,1)S(1)} collective-permute-done((bf16[64,4096]{1,0:T(8,128)(2,1)S(1)}, bf16[64,4096]{1,0:T(8,128)(2,1)S(1)}, u32[]{:S(2)}, u32[]{:S(2)}) %collective-permute-start.18) | collective-permute-done | bytes 524320 | tf_op jit(solution)/shard_map/ppermute | solution.py:272
  80.8 7.2 %collective-permute-done.19.refs_1_ = bf16[64,4096]{1,0:T(8,128)(2,1)S(1)} collective-permute-done((bf16[64,4096]{1,0:T(8,128)(2,1)S(1)}, bf16[64,4096]{1,0:T(8,128)(2,1)S(1)}, u32[]{:S(2)}, u32[]{:S(2)}) %collective-permute-start.19) | collective-permute-done | bytes 524320 | tf_op jit(solution)/shard_map/ppermute | solution.py:272
  88.0 4.3 %shard_map.112 = (f32[32,4096]{1,0:T(8,128)S(1)}, f32[32,4096]{1,0:T(8,128)S(1)}, f32[32,4096]{1,0:T(8,128)S(1)}, f32[32,4096]{1,0:T(8,128)S(1)}) custom-call(s32[1]{0:T(128)} %bitcast.index_ref, bf16[4096,256]{1,0:T(8,128)(2,1)S(1)} %bitcast.12, bf16[4096,256]{1,0:T(8,128)(2,1)S(1)} %bitcast.16, bf16[256,4096]{1,0:T(8,128)(2,1)S(1)} %bitcast.20, ...), custom_call_target="tpu_custom_call" | custom-call | flops 805306368 | bytes 14680064 | tf_op jit(solution)/shard_map/pallas_call | solution.py:218
  92.4 1.7 %collective-permute-start.23 = (bf16[32,4096]{1,0:T(8,128)(2,1)S(1)}, bf16[32,4096]{1,0:T(8,128)(2,1)S(1)}, u32[]{:S(2)}, u32[]{:S(2)}) collective-permute-start(bf16[32,4096]{1,0:T(8,128)(2,1)S(1)} %add_convert_fusion.8), channel_id=1, source_target_pairs={{0,4},{1,3},{4,8},{5,1},{8,12},{9,5},{12,14},{13,9},{14,10},{15,13... | collective-permute-start | bytes 786440 | tf_op jit(solution)/shard_map/ppermute | solution.py:272
  94.5 1.7 %collective-permute-start.30 = (bf16[32,4096]{1,0:T(8,128)(2,1)S(1)}, bf16[32,4096]{1,0:T(8,128)(2,1)S(1)}, u32[]{:S(2)}, u32[]{:S(2)}) collective-permute-start(bf16[32,4096]{1,0:T(8,128)(2,1)S(1)} %add_convert_fusion.3), channel_id=1, source_target_pairs={{0,4},{1,3},{4,8},{5,1},{8,12},{9,5},{12,14},{13,9},{14,10},{15,13... | collective-permute-start | bytes 786440 | tf_op jit(solution)/shard_map/ppermute | solution.py:272
  96.2 5.3 %collective-permute-done.23 = bf16[32,4096]{1,0:T(8,128)(2,1)S(1)} collective-permute-done((bf16[32,4096]{1,0:T(8,128)(2,1)S(1)}, bf16[32,4096]{1,0:T(8,128)(2,1)S(1)}, u32[]{:S(2)}, u32[]{:S(2)}) %collective-permute-start.23) | collective-permute-done | bytes 262176 | tf_op jit(solution)/shard_map/ppermute | solution.py:272
  101.9 1.8 %collective-permute-start.27 = (bf16[32,4096]{1,0:T(8,128)(2,1)S(1)}, bf16[32,4096]{1,0:T(8,128)(2,1)S(1)}, u32[]{:S(2)}, u32[]{:S(2)}) collective-permute-start(bf16[32,4096]{1,0:T(8,128)(2,1)S(1)} %convert_element_type.113), channel_id=1, source_target_pairs={{4,0},{3,1},{8,4},{1,5},{12,8},{5,9},{14,12},{9,13},{10,14},{13,15... | collective-permute-start | bytes 786440 | tf_op jit(solution)/shard_map/ppermute | solution.py:272
  105.9 4.1 %collective-permute-done.24 = bf16[32,4096]{1,0:T(8,128)(2,1)S(1)} collective-permute-done((bf16[32,4096]{1,0:T(8,128)(2,1)S(1)}, bf16[32,4096]{1,0:T(8,128)(2,1)S(1)}, u32[]{:S(2)}, u32[]{:S(2)}) %collective-permute-start.24) | collective-permute-done | bytes 262176 | tf_op jit(solution)/shard_map/ppermute | solution.py:272
  110.3 2.5 %collective-permute-done.31 = bf16[32,4096]{1,0:T(8,128)(2,1)S(1)} collective-permute-done((bf16[32,4096]{1,0:T(8,128)(2,1)S(1)}, bf16[32,4096]{1,0:T(8,128)(2,1)S(1)}, u32[]{:S(2)}, u32[]{:S(2)}) %collective-permute-start.31) | collective-permute-done | bytes 262176 | tf_op jit(solution)/shard_map/ppermute | solution.py:272
  113.1 3.3 %collective-permute-done.25 = bf16[32,4096]{1,0:T(8,128)(2,1)S(1)} collective-permute-done((bf16[32,4096]{1,0:T(8,128)(2,1)S(1)}, bf16[32,4096]{1,0:T(8,128)(2,1)S(1)}, u32[]{:S(2)}, u32[]{:S(2)}) %collective-permute-start.25) | collective-permute-done | bytes 262176 | tf_op jit(solution)/shard_map/ppermute | solution.py:272
  116.8 2.5 %collective-permute-done.32 = bf16[32,4096]{1,0:T(8,128)(2,1)S(1)} collective-permute-done((bf16[32,4096]{1,0:T(8,128)(2,1)S(1)}, bf16[32,4096]{1,0:T(8,128)(2,1)S(1)}, u32[]{:S(2)}, u32[]{:S(2)}) %collective-permute-start.32) | collective-permute-done | bytes 262176 | tf_op jit(solution)/shard_map/ppermute | solution.py:272
  119.6 3.3 %collective-permute-done.26 = bf16[32,4096]{1,0:T(8,128)(2,1)S(1)} collective-permute-done((bf16[32,4096]{1,0:T(8,128)(2,1)S(1)}, bf16[32,4096]{1,0:T(8,128)(2,1)S(1)}, u32[]{:S(2)}, u32[]{:S(2)}) %collective-permute-start.26) | collective-permute-done | bytes 262176 | tf_op jit(solution)/shard_map/ppermute | solution.py:272
  123.0 2.7 %collective-permute-done.33 = bf16[32,4096]{1,0:T(8,128)(2,1)S(1)} collective-permute-done((bf16[32,4096]{1,0:T(8,128)(2,1)S(1)}, bf16[32,4096]{1,0:T(8,128)(2,1)S(1)}, u32[]{:S(2)}, u32[]{:S(2)}) %collective-permute-start.33) | collective-permute-done | bytes 262176 | tf_op jit(solution)/shard_map/ppermute | solution.py:272
  (91 shorter events, 22.5 us)
Async XLA Ops:
  1.7 8.1 %collective-permute-start.3 = (bf16[64,640]{1,0:T(8,128)(2,1)S(1)}, bf16[64,640]{1,0:T(8,128)(2,1)S(1)}, u32[]{:S(2)}, u32[]{:S(2)}) collective-permute-start(bf16[64,640]{1,0:T(8,128)(2,1)S(1)} %get-tuple-element.79), channel_id=1, source_target_pairs={{0,8},{1,9},{2,10},{3,11},{4,12},{5,13},{6,14},{7,15},{8,0},{9,1},... | collective-permute-start | bytes 245768 | tf_op jit(solution)/shard_map/ppermute | solution.py:250
  5.8 6.6 %collective-permute-start = (bf16[64,640]{1,0:T(8,128)(2,1)S(1)}, bf16[64,640]{1,0:T(8,128)(2,1)S(1)}, u32[]{:S(2)}, u32[]{:S(2)}) collective-permute-start(bf16[64,640]{1,0:T(8,128)(2,1)S(1)} %get-tuple-element.79), channel_id=1, source_target_pairs={{0,2},{1,3},{2,0},{3,1},{4,6},{5,7},{6,4},{7,5},{8,10},{9,11},{10,... | collective-permute-start | bytes 245768 | tf_op jit(solution)/shard_map/ppermute | solution.py:250
  7.3 6.3 %collective-permute-start.1 = (bf16[64,640]{1,0:T(8,128)(2,1)S(1)}, bf16[64,640]{1,0:T(8,128)(2,1)S(1)}, u32[]{:S(2)}, u32[]{:S(2)}) collective-permute-start(bf16[64,640]{1,0:T(8,128)(2,1)S(1)} %get-tuple-element.79), channel_id=1, source_target_pairs={{0,4},{1,5},{2,6},{3,7},{4,0},{5,1},{6,2},{7,3},{8,12},{9,13},{10,... | collective-permute-start | bytes 245768 | tf_op jit(solution)/shard_map/ppermute | solution.py:250
  8.9 5.6 %collective-permute-start.2 = (bf16[64,640]{1,0:T(8,128)(2,1)S(1)}, bf16[64,640]{1,0:T(8,128)(2,1)S(1)}, u32[]{:S(2)}, u32[]{:S(2)}) collective-permute-start(bf16[64,640]{1,0:T(8,128)(2,1)S(1)} %get-tuple-element.79), channel_id=1, source_target_pairs={{0,6},{1,7},{2,4},{3,5},{4,2},{5,3},{6,0},{7,1},{8,14},{9,15},{10,... | collective-permute-start | bytes 245768 | tf_op jit(solution)/shard_map/ppermute | solution.py:250
  9.8 5.5 %collective-permute-start.4 = (bf16[64,640]{1,0:T(8,128)(2,1)S(1)}, bf16[64,640]{1,0:T(8,128)(2,1)S(1)}, u32[]{:S(2)}, u32[]{:S(2)}) collective-permute-start(bf16[64,640]{1,0:T(8,128)(2,1)S(1)} %collective-permute-done.3), channel_id=1, source_target_pairs={{0,2},{1,3},{2,0},{3,1},{4,6},{5,7},{6,4},{7,5},{8,10},{9,11},{10,... | collective-permute-start | bytes 245768 | tf_op jit(solution)/shard_map/ppermute | solution.py:250
  12.4 5.3 %collective-permute-start.6 = (bf16[64,640]{1,0:T(8,128)(2,1)S(1)}, bf16[64,640]{1,0:T(8,128)(2,1)S(1)}, u32[]{:S(2)}, u32[]{:S(2)}) collective-permute-start(bf16[64,640]{1,0:T(8,128)(2,1)S(1)} %collective-permute-done.3), channel_id=1, source_target_pairs={{0,6},{1,7},{2,4},{3,5},{4,2},{5,3},{6,0},{7,1},{8,14},{9,15},{10,... | collective-permute-start | bytes 245768 | tf_op jit(solution)/shard_map/ppermute | solution.py:250
  19.9 12.6 %collective-permute-start.10 = (bf16[256,4096]{1,0:T(8,128)(2,1)}, bf16[256,4096]{1,0:T(8,128)(2,1)}, u32[]{:S(2)}, u32[]{:S(2)}) collective-permute-start(bf16[256,4096]{1,0:T(8,128)(2,1)} %bitcast.17), channel_id=1, source_target_pairs={{0,1},{1,0},{2,3},{3,2},{4,5},{5,4},{6,7},{7,6},{8,9},{9,8},{10,11... | collective-permute-start | bytes 6291464 | tf_op jit(solution)/shard_map/ppermute | solution.py:261
  20.0 12.5 %collective-permute-start.8 = (bf16[4096,256]{1,0:T(8,128)(2,1)}, bf16[4096,256]{1,0:T(8,128)(2,1)}, u32[]{:S(2)}, u32[]{:S(2)}) collective-permute-start(bf16[4096,256]{1,0:T(8,128)(2,1)} %bitcast.9), channel_id=1, source_target_pairs={{0,1},{1,0},{2,3},{3,2},{4,5},{5,4},{6,7},{7,6},{8,9},{9,8},{10,11... | collective-permute-start | bytes 6291464 | tf_op jit(solution)/shard_map/ppermute | solution.py:261
  20.4 12.1 %collective-permute-start.9 = (bf16[4096,256]{1,0:T(8,128)(2,1)}, bf16[4096,256]{1,0:T(8,128)(2,1)}, u32[]{:S(2)}, u32[]{:S(2)}) collective-permute-start(bf16[4096,256]{1,0:T(8,128)(2,1)} %bitcast.13), channel_id=1, source_target_pairs={{0,1},{1,0},{2,3},{3,2},{4,5},{5,4},{6,7},{7,6},{8,9},{9,8},{10,11... | collective-permute-start | bytes 6291464 | tf_op jit(solution)/shard_map/ppermute | solution.py:261
  32.5 6.6 %collective-permute-start.11 = (bf16[32,4096]{1,0:T(8,128)(2,1)}, bf16[32,4096]{1,0:T(8,128)(2,1)S(1)}, u32[]{:S(2)}, u32[]{:S(2)}) collective-permute-start(bf16[32,4096]{1,0:T(8,128)(2,1)} %get-tuple-element.55.refs_2_), channel_id=1, source_target_pairs={{0,4},{1,3},{4,8},{5,1},{8,12},{9,5},{12,14},{13,9},{14,10},{15,13... | collective-permute-start | bytes 786440 | tf_op jit(solution)/shard_map/ppermute | solution.py:272
  33.7 8.3 %collective-permute-start.13 = (bf16[32,4096]{1,0:T(8,128)(2,1)}, bf16[32,4096]{1,0:T(8,128)(2,1)S(1)}, u32[]{:S(2)}, u32[]{:S(2)}) collective-permute-start(bf16[32,4096]{1,0:T(8,128)(2,1)} %get-tuple-element.56.refs_3_), channel_id=1, source_target_pairs={{0,4},{1,3},{4,8},{5,1},{8,12},{9,5},{12,14},{13,9},{14,10},{15,13... | collective-permute-start | bytes 786440 | tf_op jit(solution)/shard_map/ppermute | solution.py:272
  39.2 7.5 %collective-permute-start.12 = (bf16[32,4096]{1,0:T(8,128)(2,1)S(1)}, bf16[32,4096]{1,0:T(8,128)(2,1)S(1)}, u32[]{:S(2)}, u32[]{:S(2)}) collective-permute-start(bf16[32,4096]{1,0:T(8,128)(2,1)S(1)} %collective-permute-done.11.refs_3_), channel_id=1, source_target_pairs={{0,4},{1,3},{4,8},{5,1},{8,12},{9,5},{12,14},{13,9},{14,10},{15,13... | collective-permute-start | bytes 786440 | tf_op jit(solution)/shard_map/ppermute | solution.py:272
  42.0 10.3 %collective-permute-start.14 = (bf16[32,4096]{1,0:T(8,128)(2,1)S(1)}, bf16[32,4096]{1,0:T(8,128)(2,1)S(1)}, u32[]{:S(2)}, u32[]{:S(2)}) collective-permute-start(bf16[32,4096]{1,0:T(8,128)(2,1)S(1)} %collective-permute-done.13.refs_4_), channel_id=1, source_target_pairs={{0,4},{1,3},{4,8},{5,1},{8,12},{9,5},{12,14},{13,9},{14,10},{15,13... | collective-permute-start | bytes 786440 | tf_op jit(solution)/shard_map/ppermute | solution.py:272
  43.4 12.9 %collective-permute-start.16 = (bf16[64,4096]{1,0:T(8,128)(2,1)}, bf16[64,4096]{1,0:T(8,128)(2,1)S(1)}, u32[]{:S(2)}, u32[]{:S(2)}) collective-permute-start(bf16[64,4096]{1,0:T(8,128)(2,1)} %get-tuple-element.58), channel_id=1, source_target_pairs={{4,0},{3,1},{8,4},{1,5},{12,8},{5,9},{14,12},{9,13},{10,14},{13,15... | collective-permute-start | bytes 1572872 | tf_op jit(solution)/shard_map/ppermute | solution.py:272
  52.3 14.1 %collective-permute-start.15 = (bf16[64,4096]{1,0:T(8,128)(2,1)S(1)}, bf16[64,4096]{1,0:T(8,128)(2,1)S(1)}, u32[]{:S(2)}, u32[]{:S(2)}) collective-permute-start(bf16[64,4096]{1,0:T(8,128)(2,1)S(1)} %pad_maximum_fusion), channel_id=1, source_target_pairs={{0,4},{1,3},{4,8},{5,1},{8,12},{9,5},{12,14},{13,9},{14,10},{15,13... | collective-permute-start | bytes 1572872 | tf_op jit(solution)/shard_map/ppermute | solution.py:272
  56.3 12.0 %collective-permute-start.17 = (bf16[64,4096]{1,0:T(8,128)(2,1)S(1)}, bf16[64,4096]{1,0:T(8,128)(2,1)S(1)}, u32[]{:S(2)}, u32[]{:S(2)}) collective-permute-start(bf16[64,4096]{1,0:T(8,128)(2,1)S(1)} %collective-permute-done.16.refs_2_), channel_id=1, source_target_pairs={{4,0},{3,1},{8,4},{1,5},{12,8},{5,9},{14,12},{9,13},{10,14},{13,15... | collective-permute-start | bytes 1572872 | tf_op jit(solution)/shard_map/ppermute | solution.py:272
  62.6 11.0 %collective-permute-start.20 = (bf16[32,4096]{1,0:T(8,128)(2,1)S(1)}, bf16[32,4096]{1,0:T(8,128)(2,1)S(1)}, u32[]{:S(2)}, u32[]{:S(2)}) collective-permute-start(bf16[32,4096]{1,0:T(8,128)(2,1)S(1)} %convert_element_type.100), channel_id=1, source_target_pairs={{0,4},{1,3},{4,8},{5,1},{8,12},{9,5},{12,14},{13,9},{14,10},{15,13... | collective-permute-start | bytes 786440 | tf_op jit(solution)/shard_map/ppermute | solution.py:272
  64.5 11.7 %collective-permute-start.28 = (bf16[32,4096]{1,0:T(8,128)(2,1)S(1)}, bf16[32,4096]{1,0:T(8,128)(2,1)S(1)}, u32[]{:S(2)}, u32[]{:S(2)}) collective-permute-start(bf16[32,4096]{1,0:T(8,128)(2,1)S(1)} %convert_element_type.115), channel_id=1, source_target_pairs={{0,4},{1,3},{4,8},{5,1},{8,12},{9,5},{12,14},{13,9},{14,10},{15,13... | collective-permute-start | bytes 786440 | tf_op jit(solution)/shard_map/ppermute | solution.py:272
  66.5 14.3 %collective-permute-start.18 = (bf16[64,4096]{1,0:T(8,128)(2,1)S(1)}, bf16[64,4096]{1,0:T(8,128)(2,1)S(1)}, u32[]{:S(2)}, u32[]{:S(2)}) collective-permute-start(bf16[64,4096]{1,0:T(8,128)(2,1)S(1)} %collective-permute-done.15.refs_0_), channel_id=1, source_target_pairs={{0,4},{1,3},{4,8},{5,1},{8,12},{9,5},{12,14},{13,9},{14,10},{15,13... | collective-permute-start | bytes 1572872 | tf_op jit(solution)/shard_map/ppermute | solution.py:272
  73.6 18.7 %collective-permute-start.21 = (bf16[32,4096]{1,0:T(8,128)(2,1)S(1)}, bf16[32,4096]{1,0:T(8,128)(2,1)S(1)}, u32[]{:S(2)}, u32[]{:S(2)}) collective-permute-start(bf16[32,4096]{1,0:T(8,128)(2,1)S(1)} %add_convert_fusion.9), channel_id=1, source_target_pairs={{0,4},{1,3},{4,8},{5,1},{8,12},{9,5},{12,14},{13,9},{14,10},{15,13... | collective-permute-start | bytes 786440 | tf_op jit(solution)/shard_map/ppermute | solution.py:272
  76.2 11.8 %collective-permute-start.19 = (bf16[64,4096]{1,0:T(8,128)(2,1)S(1)}, bf16[64,4096]{1,0:T(8,128)(2,1)S(1)}, u32[]{:S(2)}, u32[]{:S(2)}) collective-permute-start(bf16[64,4096]{1,0:T(8,128)(2,1)S(1)} %collective-permute-done.17.refs_1_), channel_id=1, source_target_pairs={{4,0},{3,1},{8,4},{1,5},{12,8},{5,9},{14,12},{9,13},{10,14},{13,15... | collective-permute-start | bytes 1572872 | tf_op jit(solution)/shard_map/ppermute | solution.py:272
  76.2 18.2 %collective-permute-start.29 = (bf16[32,4096]{1,0:T(8,128)(2,1)S(1)}, bf16[32,4096]{1,0:T(8,128)(2,1)S(1)}, u32[]{:S(2)}, u32[]{:S(2)}) collective-permute-start(bf16[32,4096]{1,0:T(8,128)(2,1)S(1)} %add_convert_fusion.4), channel_id=1, source_target_pairs={{0,4},{1,3},{4,8},{5,1},{8,12},{9,5},{12,14},{13,9},{14,10},{15,13... | collective-permute-start | bytes 786440 | tf_op jit(solution)/shard_map/ppermute | solution.py:272
  92.4 9.2 %collective-permute-start.23 = (bf16[32,4096]{1,0:T(8,128)(2,1)S(1)}, bf16[32,4096]{1,0:T(8,128)(2,1)S(1)}, u32[]{:S(2)}, u32[]{:S(2)}) collective-permute-start(bf16[32,4096]{1,0:T(8,128)(2,1)S(1)} %add_convert_fusion.8), channel_id=1, source_target_pairs={{0,4},{1,3},{4,8},{5,1},{8,12},{9,5},{12,14},{13,9},{14,10},{15,13... | collective-permute-start | bytes 786440 | tf_op jit(solution)/shard_map/ppermute | solution.py:272
  94.1 25.5 %collective-permute-start.22 = (bf16[32,4096]{1,0:T(8,128)(2,1)S(1)}, bf16[32,4096]{1,0:T(8,128)(2,1)S(1)}, u32[]{:S(2)}, u32[]{:S(2)}) collective-permute-start(bf16[32,4096]{1,0:T(8,128)(2,1)S(1)} %convert_element_type.99), channel_id=1, source_target_pairs={{4,0},{3,1},{8,4},{1,5},{12,8},{5,9},{14,12},{9,13},{10,14},{13,15... | collective-permute-start | bytes 786440 | tf_op jit(solution)/shard_map/ppermute | solution.py:272
  94.5 10.1 %collective-permute-start.30 = (bf16[32,4096]{1,0:T(8,128)(2,1)S(1)}, bf16[32,4096]{1,0:T(8,128)(2,1)S(1)}, u32[]{:S(2)}, u32[]{:S(2)}) collective-permute-start(bf16[32,4096]{1,0:T(8,128)(2,1)S(1)} %add_convert_fusion.3), channel_id=1, source_target_pairs={{0,4},{1,3},{4,8},{5,1},{8,12},{9,5},{12,14},{13,9},{14,10},{15,13... | collective-permute-start | bytes 786440 | tf_op jit(solution)/shard_map/ppermute | solution.py:272
  101.6 8.4 %collective-permute-start.24 = (bf16[32,4096]{1,0:T(8,128)(2,1)S(1)}, bf16[32,4096]{1,0:T(8,128)(2,1)S(1)}, u32[]{:S(2)}, u32[]{:S(2)}) collective-permute-start(bf16[32,4096]{1,0:T(8,128)(2,1)S(1)} %add_convert_fusion.7), channel_id=1, source_target_pairs={{0,4},{1,3},{4,8},{5,1},{8,12},{9,5},{12,14},{13,9},{14,10},{15,13... | collective-permute-start | bytes 786440 | tf_op jit(solution)/shard_map/ppermute | solution.py:272
  101.9 21.1 %collective-permute-start.27 = (bf16[32,4096]{1,0:T(8,128)(2,1)S(1)}, bf16[32,4096]{1,0:T(8,128)(2,1)S(1)}, u32[]{:S(2)}, u32[]{:S(2)}) collective-permute-start(bf16[32,4096]{1,0:T(8,128)(2,1)S(1)} %convert_element_type.113), channel_id=1, source_target_pairs={{4,0},{3,1},{8,4},{1,5},{12,8},{5,9},{14,12},{9,13},{10,14},{13,15... | collective-permute-start | bytes 786440 | tf_op jit(solution)/shard_map/ppermute | solution.py:272
  104.7 8.1 %collective-permute-start.31 = (bf16[32,4096]{1,0:T(8,128)(2,1)S(1)}, bf16[32,4096]{1,0:T(8,128)(2,1)S(1)}, u32[]{:S(2)}, u32[]{:S(2)}) collective-permute-start(bf16[32,4096]{1,0:T(8,128)(2,1)S(1)} %add_convert_fusion.2), channel_id=1, source_target_pairs={{0,4},{1,3},{4,8},{5,1},{8,12},{9,5},{12,14},{13,9},{14,10},{15,13... | collective-permute-start | bytes 786440 | tf_op jit(solution)/shard_map/ppermute | solution.py:272
  110.0 6.4 %collective-permute-start.25 = (bf16[32,4096]{1,0:T(8,128)(2,1)S(1)}, bf16[32,4096]{1,0:T(8,128)(2,1)S(1)}, u32[]{:S(2)}, u32[]{:S(2)}) collective-permute-start(bf16[32,4096]{1,0:T(8,128)(2,1)S(1)} %add_convert_fusion.6), channel_id=1, source_target_pairs={{0,4},{1,3},{4,8},{5,1},{8,12},{9,5},{12,14},{13,9},{14,10},{15,13... | collective-permute-start | bytes 786440 | tf_op jit(solution)/shard_map/ppermute | solution.py:272
  112.9 6.4 %collective-permute-start.32 = (bf16[32,4096]{1,0:T(8,128)(2,1)S(1)}, bf16[32,4096]{1,0:T(8,128)(2,1)S(1)}, u32[]{:S(2)}, u32[]{:S(2)}) collective-permute-start(bf16[32,4096]{1,0:T(8,128)(2,1)S(1)} %add_convert_fusion.1), channel_id=1, source_target_pairs={{0,4},{1,3},{4,8},{5,1},{8,12},{9,5},{12,14},{13,9},{14,10},{15,13... | collective-permute-start | bytes 786440 | tf_op jit(solution)/shard_map/ppermute | solution.py:272
  116.5 6.4 %collective-permute-start.26 = (bf16[32,4096]{1,0:T(8,128)(2,1)S(1)}, bf16[32,4096]{1,0:T(8,128)(2,1)S(1)}, u32[]{:S(2)}, u32[]{:S(2)}) collective-permute-start(bf16[32,4096]{1,0:T(8,128)(2,1)S(1)} %add_convert_fusion.5), channel_id=1, source_target_pairs={{0,4},{1,3},{4,8},{5,1},{8,12},{9,5},{12,14},{13,9},{14,10},{15,13... | collective-permute-start | bytes 786440 | tf_op jit(solution)/shard_map/ppermute | solution.py:272
  119.3 6.4 %collective-permute-start.33 = (bf16[32,4096]{1,0:T(8,128)(2,1)S(1)}, bf16[32,4096]{1,0:T(8,128)(2,1)S(1)}, u32[]{:S(2)}, u32[]{:S(2)}) collective-permute-start(bf16[32,4096]{1,0:T(8,128)(2,1)S(1)} %add_convert_fusion), channel_id=1, source_target_pairs={{0,4},{1,3},{4,8},{5,1},{8,12},{9,5},{12,14},{13,9},{14,10},{15,13... | collective-permute-start | bytes 786440 | tf_op jit(solution)/shard_map/ppermute | solution.py:272
  (13 other events, 149.7 us)

commit v15 on v12

--- a/solution.py
+++ b/solution.py
@@ -20,7 +20,7 @@
 NEG_FILL = -1e30
 
 HEAD_GROUP = 16
-SUB_HEADS = 4
+SUB_HEADS = 8
 PIECES = 2
 LOG2_SCALE = SCORE_SCALE * math.log2(math.e)
 
@@ -266,7 +266,7 @@
 
     def parts_of(rows, hops):
         blocks = [block for hop in hops for block in rows[hop]]
-        return expert_parts(my_index, blocks, hits, own, swapped, hops, chips)
+        return expert_parts(my_index, blocks, table, own, swapped, hops, chips)
 
     def move(blocks, way=route):
         return tuple(lax.ppermute(x, "ctx", way) for x in blocks)
@@ -282,7 +282,8 @@
 
     turn = chips // 2
     rows = {0: start, 1: move(start)}
-    rows[2] = move(rows[1])
+    table = jnp.where(hits > 0.5, 1.0, 0.0)
+    rows[2] = move(after(rows[1][:1], table)) + move(rows[1][1:])
     rows[chips - 1] = move(after((normed,), rows[1][-1]), back)
     rows[3] = move((jnp.concatenate(rows[2], axis=0),))
     parts = dict(zip((1,), parts_of(rows, (1,))))

time: 122 us -> 122 us (level)
  transfers between devices with their start and end apart: 34 -> 34, of which waited for: 19 -> 20; matrix products, arithmetic and copies ran while one was open for 1% -> 1% of each run, Pallas kernels for 25% -> 25%
where the time goes in v15:
time: 122 us
  waiting for transfers between devices  48.9 us (40%)
  starting transfers between devices  37.8 us (31%)
  Pallas kernels  30.1 us (25%)
  other arithmetic  4.12 us (3%)
    ppermute x23, waiting for transfers between devices, move(): return tuple((lax.ppermute(x, 'ctx', way) for x in blocks))  42 us
    ppermute x23, starting transfers between devices, move(): return tuple((lax.ppermute(x, 'ctx', way) for x in blocks))  26 us
    pallas_call x4, Pallas kernels, expert_parts(): pl.pallas_call(functools.partial(expert_kernel, hops=hops, chips=chips),...  18.5 us
    pallas_call x1, Pallas kernels, attention(): pl.pallas_call(functools.partial(attention_kernel, tok=tok), grid_spec=gr...  11.5 us
    ppermute x7, starting transfers between devices, from_chip(): lax.ppermute(block, 'ctx', [(i, i ^ step * CORES) for i in range(n_ctx)])  11.1 us
    ppermute x7, waiting for transfers between devices, from_chip(): lax.ppermute(block, 'ctx', [(i, i ^ step * CORES) for i in range(n_ctx)])  4.77 us
  transfers between devices with their start and end apart: 34, of which 20 were waited for; matrix products, arithmetic and copies ran while one was open for 1% of the time, Pallas kernels for 25%

profile of v15, /device:TPU:0, one launch (start us, length us, event | category | flops | bytes accessed | tf_op | source)
XLA Modules:
  0.0 121.5 jit_solution(3052379489454855170)
XLA Ops:
  1.7 4.1 %collective-permute-start.3 = (bf16[64,640]{1,0:T(8,128)(2,1)S(1)}, bf16[64,640]{1,0:T(8,128)(2,1)S(1)}, u32[]{:S(2)}, u32[]{:S(2)}) collective-permute-start(bf16[64,640]{1,0:T(8,128)(2,1)S(1)} %get-tuple-element.79), channel_id=1, source_target_pairs={{0,8},{1,9},{2,10},{3,11},{4,12},{5,13},{6,14},{7,15},{8,0},{9,1},... | collective-permute-start | bytes 245768 | tf_op jit(solution)/shard_map/ppermute | solution.py:250
  5.8 1.5 %collective-permute-start = (bf16[64,640]{1,0:T(8,128)(2,1)S(1)}, bf16[64,640]{1,0:T(8,128)(2,1)S(1)}, u32[]{:S(2)}, u32[]{:S(2)}) collective-permute-start(bf16[64,640]{1,0:T(8,128)(2,1)S(1)} %get-tuple-element.79), channel_id=1, source_target_pairs={{0,2},{1,3},{2,0},{3,1},{4,6},{5,7},{6,4},{7,5},{8,10},{9,11},{10,... | collective-permute-start | bytes 245768 | tf_op jit(solution)/shard_map/ppermute | solution.py:250
  7.3 1.5 %collective-permute-start.2 = (bf16[64,640]{1,0:T(8,128)(2,1)S(1)}, bf16[64,640]{1,0:T(8,128)(2,1)S(1)}, u32[]{:S(2)}, u32[]{:S(2)}) collective-permute-start(bf16[64,640]{1,0:T(8,128)(2,1)S(1)} %get-tuple-element.79), channel_id=1, source_target_pairs={{0,6},{1,7},{2,4},{3,5},{4,2},{5,3},{6,0},{7,1},{8,14},{9,15},{10,... | collective-permute-start | bytes 245768 | tf_op jit(solution)/shard_map/ppermute | solution.py:250
  9.8 2.0 %collective-permute-start.6 = (bf16[64,640]{1,0:T(8,128)(2,1)S(1)}, bf16[64,640]{1,0:T(8,128)(2,1)S(1)}, u32[]{:S(2)}, u32[]{:S(2)}) collective-permute-start(bf16[64,640]{1,0:T(8,128)(2,1)S(1)} %collective-permute-done.3), channel_id=1, source_target_pairs={{0,6},{1,7},{2,4},{3,5},{4,2},{5,3},{6,0},{7,1},{8,14},{9,15},{10,... | collective-permute-start | bytes 245768 | tf_op jit(solution)/shard_map/ppermute | solution.py:250
  11.8 1.3 %collective-permute-start.5 = (bf16[64,640]{1,0:T(8,128)(2,1)S(1)}, bf16[64,640]{1,0:T(8,128)(2,1)S(1)}, u32[]{:S(2)}, u32[]{:S(2)}) collective-permute-start(bf16[64,640]{1,0:T(8,128)(2,1)S(1)} %collective-permute-done.3), channel_id=1, source_target_pairs={{0,4},{1,5},{2,6},{3,7},{4,0},{5,1},{6,2},{7,3},{8,12},{9,13},{10,... | collective-permute-start | bytes 245768 | tf_op jit(solution)/shard_map/ppermute | solution.py:250
  14.0 3.6 %collective-permute-done.4 = bf16[64,640]{1,0:T(8,128)(2,1)S(1)} collective-permute-done((bf16[64,640]{1,0:T(8,128)(2,1)S(1)}, bf16[64,640]{1,0:T(8,128)(2,1)S(1)}, u32[]{:S(2)}, u32[]{:S(2)}) %collective-permute-start.4) | collective-permute-done | bytes 81952 | tf_op jit(solution)/shard_map/ppermute | solution.py:250
  17.8 2.1 %collective-permute-done.7.other_ref = bf16[512,640]{1,0:T(8,128)(2,1)S(1)} collective-permute-done((bf16[512,640]{1,0:T(8,128)(2,1)S(1)}, bf16[512,640]{1,0:T(8,128)(2,1)S(1)}, u32[]{:S(2)}, u32[]{:S(2)}) %collective-permute-start.7) | collective-permute-done | bytes 655392 | tf_op jit(solution)/shard_map/ppermute | solution.py:258
  20.7 11.5 %shard_map.109 = (bf16[64,4096]{1,0:T(8,128)(2,1)}, bf16[64,4096]{1,0:T(8,128)(2,1)}, bf16[32,4096]{1,0:T(8,128)(2,1)}, bf16[32,4096]{1,0:T(8,128)(2,1)}, f32[64,8]{1,0:T(8,128)}) custom-call(s32[1]{0:T(128)} %bitcast.index_ref, bf16[64,16384]{1,0:T(8,128)(2,1)} %q_ref.1, bf16[64,2048]{1,0:T(8,128)(2,1)} %qr_ref.1, bf16[512,640]{1,0:T(8,128)(2,1)} %copy-done.6, ...), custom_call_target="tpu_custom_call" | custom-call | flops 4831838208 | bytes 8388608 | tf_op jit(solution)/shard_map/pallas_call | solution.py:151
  33.3 1.6 %collective-permute-start.13 = (bf16[32,4096]{1,0:T(8,128)(2,1)}, bf16[32,4096]{1,0:T(8,128)(2,1)S(1)}, u32[]{:S(2)}, u32[]{:S(2)}) collective-permute-start(bf16[32,4096]{1,0:T(8,128)(2,1)} %get-tuple-element.57.refs_4_), channel_id=1, source_target_pairs={{0,4},{1,3},{4,8},{5,1},{8,12},{9,5},{12,14},{13,9},{14,10},{15,13... | collective-permute-start | bytes 786440 | tf_op jit(solution)/shard_map/ppermute | solution.py:272
  35.6 3.3 %collective-permute-done.11.refs_0_ = bf16[32,4096]{1,0:T(8,128)(2,1)S(1)} collective-permute-done((bf16[32,4096]{1,0:T(8,128)(2,1)}, bf16[32,4096]{1,0:T(8,128)(2,1)S(1)}, u32[]{:S(2)}, u32[]{:S(2)}) %collective-permute-start.11) | collective-permute-done | bytes 262176 | tf_op jit(solution)/shard_map/ppermute | solution.py:272
  39.9 1.8 %collective-permute-done.13.refs_1_ = bf16[32,4096]{1,0:T(8,128)(2,1)S(1)} collective-permute-done((bf16[32,4096]{1,0:T(8,128)(2,1)}, bf16[32,4096]{1,0:T(8,128)(2,1)S(1)}, u32[]{:S(2)}, u32[]{:S(2)}) %collective-permute-start.13) | collective-permute-done | bytes 262176 | tf_op jit(solution)/shard_map/ppermute | solution.py:272
  43.8 4.7 %shard_map.111 = (f32[32,4096]{1,0:T(8,128)S(1)}, f32[32,4096]{1,0:T(8,128)S(1)}) custom-call(s32[1]{0:T(128)} %bitcast.index_ref, bf16[4096,256]{1,0:T(8,128)(2,1)S(1)} %bitcast.10, bf16[4096,256]{1,0:T(8,128)(2,1)S(1)} %bitcast.15, bf16[256,4096]{1,0:T(8,128)(2,1)S(1)} %bitcast.20, f32[64,8]{1,0:T(8,128)S(1)} %compare_select_fusion.hits_hbm, ...), custom_call_target="tpu_custom_call" | custom-call | flops 805306368 | bytes 14680064 | tf_op jit(solution)/shard_map/pallas_call | solution.py:218
  49.6 1.6 %collective-permute-start.18 = (bf16[32,4096]{1,0:T(8,128)(2,1)S(1)}, bf16[32,4096]{1,0:T(8,128)(2,1)S(1)}, u32[]{:S(2)}, u32[]{:S(2)}) collective-permute-start(bf16[32,4096]{1,0:T(8,128)(2,1)S(1)} %convert_element_type.99), channel_id=1, source_target_pairs={{0,4},{1,3},{4,8},{5,1},{8,12},{9,5},{12,14},{13,9},{14,10},{15,13... | collective-permute-start | bytes 786440 | tf_op jit(solution)/shard_map/ppermute | solution.py:272
  52.0 1.3 %collective-permute-start.16 = (bf16[64,4096]{1,0:T(8,128)(2,1)S(1)}, bf16[64,4096]{1,0:T(8,128)(2,1)S(1)}, u32[]{:S(2)}, u32[]{:S(2)}) collective-permute-start(bf16[64,4096]{1,0:T(8,128)(2,1)S(1)} %pad_maximum_fusion), channel_id=1, source_target_pairs={{0,4},{1,3},{4,8},{5,1},{8,12},{9,5},{12,14},{13,9},{14,10},{15,13... | collective-permute-start | bytes 1572872 | tf_op jit(solution)/shard_map/ppermute | solution.py:272
  54.3 1.4 %collective-permute-start.17 = (bf16[64,4096]{1,0:T(8,128)(2,1)S(1)}, bf16[64,4096]{1,0:T(8,128)(2,1)S(1)}, u32[]{:S(2)}, u32[]{:S(2)}) collective-permute-start(bf16[64,4096]{1,0:T(8,128)(2,1)S(1)} %collective-permute-done.15.refs_2_), channel_id=1, source_target_pairs={{4,0},{3,1},{8,4},{1,5},{12,8},{5,9},{14,12},{9,13},{10,14},{13,15... | collective-permute-start | bytes 1572872 | tf_op jit(solution)/shard_map/ppermute | solution.py:272
  55.7 5.2 %shard_map.110 = (f32[32,4096]{1,0:T(8,128)S(1)}, f32[32,4096]{1,0:T(8,128)S(1)}, f32[32,4096]{1,0:T(8,128)S(1)}, f32[32,4096]{1,0:T(8,128)S(1)}, f32[32,4096]{1,0:T(8,128)S(1)}, /*index=5*/f32[32,4096]{1,0:T(8,128)S(1)}) custom-call(s32[1]{0:T(128)} %bitcast.index_ref, bf16[4096,256]{1,0:T(8,128)(2,1)S(1)} %bitcast.11, bf16[4096,256]{1,0:T(8,128)(2,1)S(1)} %bitcast.16, ...), custom_call_target="tpu_custom_call" | custom-call | flops 805306368 | bytes 14680064 | tf_op jit(solution)/shard_map/pallas_call | solution.py:218
  61.8 2.0 %collective-permute-start.28 = (bf16[32,4096]{1,0:T(8,128)(2,1)S(1)}, bf16[32,4096]{1,0:T(8,128)(2,1)S(1)}, u32[]{:S(2)}, u32[]{:S(2)}) collective-permute-start(bf16[32,4096]{1,0:T(8,128)(2,1)S(1)} %add_convert_fusion.5), channel_id=1, source_target_pairs={{0,4},{1,3},{4,8},{5,1},{8,12},{9,5},{12,14},{13,9},{14,10},{15,13... | collective-permute-start | bytes 786440 | tf_op jit(solution)/shard_map/ppermute | solution.py:272
  63.9 6.7 %collective-permute-done.16.refs_0_ = bf16[64,4096]{1,0:T(8,128)(2,1)S(1)} collective-permute-done((bf16[64,4096]{1,0:T(8,128)(2,1)S(1)}, bf16[64,4096]{1,0:T(8,128)(2,1)S(1)}, u32[]{:S(2)}, u32[]{:S(2)}) %collective-permute-start.16) | collective-permute-done | bytes 524320 | tf_op jit(solution)/shard_map/ppermute | solution.py:272
  71.5 1.1 collective-permute-start.20
  72.6 4.3 %shard_map.112 = (f32[32,4096]{1,0:T(8,128)S(1)}, f32[32,4096]{1,0:T(8,128)S(1)}, f32[32,4096]{1,0:T(8,128)S(1)}, f32[32,4096]{1,0:T(8,128)S(1)}) custom-call(s32[1]{0:T(128)} %bitcast.index_ref, bf16[4096,256]{1,0:T(8,128)(2,1)S(1)} %bitcast.12, bf16[4096,256]{1,0:T(8,128)(2,1)S(1)} %bitcast.17, bf16[256,4096]{1,0:T(8,128)(2,1)S(1)} %bitcast.22, ...), custom_call_target="tpu_custom_call" | custom-call | flops 805306368 | bytes 14680064 | tf_op jit(solution)/shard_map/pallas_call | solution.py:218
  78.0 2.4 %collective-permute-done.28 = bf16[32,4096]{1,0:T(8,128)(2,1)S(1)} collective-permute-done((bf16[32,4096]{1,0:T(8,128)(2,1)S(1)}, bf16[32,4096]{1,0:T(8,128)(2,1)S(1)}, u32[]{:S(2)}, u32[]{:S(2)}) %collective-permute-start.28) | collective-permute-done | bytes 262176 | tf_op jit(solution)/shard_map/ppermute | solution.py:272
  81.0 6.4 %collective-permute-done.19.refs_0_ = bf16[64,4096]{1,0:T(8,128)(2,1)S(1)} collective-permute-done((bf16[64,4096]{1,0:T(8,128)(2,1)S(1)}, bf16[64,4096]{1,0:T(8,128)(2,1)S(1)}, u32[]{:S(2)}, u32[]{:S(2)}) %collective-permute-start.19) | collective-permute-done | bytes 524320 | tf_op jit(solution)/shard_map/ppermute | solution.py:272
  87.4 4.3 %shard_map.113 = (f32[32,4096]{1,0:T(8,128)S(1)}, f32[32,4096]{1,0:T(8,128)S(1)}, f32[32,4096]{1,0:T(8,128)S(1)}, f32[32,4096]{1,0:T(8,128)S(1)}) custom-call(s32[1]{0:T(128)} %bitcast.index_ref, bf16[4096,256]{1,0:T(8,128)(2,1)S(1)} %bitcast.13, bf16[4096,256]{1,0:T(8,128)(2,1)S(1)} %bitcast.18, bf16[256,4096]{1,0:T(8,128)(2,1)S(1)} %bitcast.23, ...), custom_call_target="tpu_custom_call" | custom-call | flops 805306368 | bytes 14680064 | tf_op jit(solution)/shard_map/pallas_call | solution.py:218
  93.1 1.5 %collective-permute-start.30 = (bf16[32,4096]{1,0:T(8,128)(2,1)S(1)}, bf16[32,4096]{1,0:T(8,128)(2,1)S(1)}, u32[]{:S(2)}, u32[]{:S(2)}) collective-permute-start(bf16[32,4096]{1,0:T(8,128)(2,1)S(1)} %add_convert_fusion.3), channel_id=1, source_target_pairs={{0,4},{1,3},{4,8},{5,1},{8,12},{9,5},{12,14},{13,9},{14,10},{15,13... | collective-permute-start | bytes 786440 | tf_op jit(solution)/shard_map/ppermute | solution.py:272
  94.6 3.7 %collective-permute-done.23 = bf16[32,4096]{1,0:T(8,128)(2,1)S(1)} collective-permute-done((bf16[32,4096]{1,0:T(8,128)(2,1)S(1)}, bf16[32,4096]{1,0:T(8,128)(2,1)S(1)}, u32[]{:S(2)}, u32[]{:S(2)}) %collective-permute-start.23) | collective-permute-done | bytes 262176 | tf_op jit(solution)/shard_map/ppermute | solution.py:272
  99.3 1.7 %collective-permute-done.30 = bf16[32,4096]{1,0:T(8,128)(2,1)S(1)} collective-permute-done((bf16[32,4096]{1,0:T(8,128)(2,1)S(1)}, bf16[32,4096]{1,0:T(8,128)(2,1)S(1)}, u32[]{:S(2)}, u32[]{:S(2)}) %collective-permute-start.30) | collective-permute-done | bytes 262176 | tf_op jit(solution)/shard_map/ppermute | solution.py:272
  102.1 2.6 %collective-permute-done.24 = bf16[32,4096]{1,0:T(8,128)(2,1)S(1)} collective-permute-done((bf16[32,4096]{1,0:T(8,128)(2,1)S(1)}, bf16[32,4096]{1,0:T(8,128)(2,1)S(1)}, u32[]{:S(2)}, u32[]{:S(2)}) %collective-permute-start.24) | collective-permute-done | bytes 262176 | tf_op jit(solution)/shard_map/ppermute | solution.py:272
  105.8 1.7 %collective-permute-done.31 = bf16[32,4096]{1,0:T(8,128)(2,1)S(1)} collective-permute-done((bf16[32,4096]{1,0:T(8,128)(2,1)S(1)}, bf16[32,4096]{1,0:T(8,128)(2,1)S(1)}, u32[]{:S(2)}, u32[]{:S(2)}) %collective-permute-start.31) | collective-permute-done | bytes 262176 | tf_op jit(solution)/shard_map/ppermute | solution.py:272
  108.6 2.6 %collective-permute-done.25 = bf16[32,4096]{1,0:T(8,128)(2,1)S(1)} collective-permute-done((bf16[32,4096]{1,0:T(8,128)(2,1)S(1)}, bf16[32,4096]{1,0:T(8,128)(2,1)S(1)}, u32[]{:S(2)}, u32[]{:S(2)}) %collective-permute-start.25) | collective-permute-done | bytes 262176 | tf_op jit(solution)/shard_map/ppermute | solution.py:272
  112.3 1.7 %collective-permute-done.32 = bf16[32,4096]{1,0:T(8,128)(2,1)S(1)} collective-permute-done((bf16[32,4096]{1,0:T(8,128)(2,1)S(1)}, bf16[32,4096]{1,0:T(8,128)(2,1)S(1)}, u32[]{:S(2)}, u32[]{:S(2)}) %collective-permute-start.32) | collective-permute-done | bytes 262176 | tf_op jit(solution)/shard_map/ppermute | solution.py:272
  115.1 2.6 %collective-permute-done.26 = bf16[32,4096]{1,0:T(8,128)(2,1)S(1)} collective-permute-done((bf16[32,4096]{1,0:T(8,128)(2,1)S(1)}, bf16[32,4096]{1,0:T(8,128)(2,1)S(1)}, u32[]{:S(2)}, u32[]{:S(2)}) %collective-permute-start.26) | collective-permute-done | bytes 262176 | tf_op jit(solution)/shard_map/ppermute | solution.py:272
  117.8 2.7 %collective-permute-done.33 = bf16[32,4096]{1,0:T(8,128)(2,1)S(1)} collective-permute-done((bf16[32,4096]{1,0:T(8,128)(2,1)S(1)}, bf16[32,4096]{1,0:T(8,128)(2,1)S(1)}, u32[]{:S(2)}, u32[]{:S(2)}) %collective-permute-start.33) | collective-permute-done | bytes 262176 | tf_op jit(solution)/shard_map/ppermute | solution.py:272
  (89 shorter events, 24.5 us)
Async XLA Ops:
  1.7 8.1 %collective-permute-start.3 = (bf16[64,640]{1,0:T(8,128)(2,1)S(1)}, bf16[64,640]{1,0:T(8,128)(2,1)S(1)}, u32[]{:S(2)}, u32[]{:S(2)}) collective-permute-start(bf16[64,640]{1,0:T(8,128)(2,1)S(1)} %get-tuple-element.79), channel_id=1, source_target_pairs={{0,8},{1,9},{2,10},{3,11},{4,12},{5,13},{6,14},{7,15},{8,0},{9,1},... | collective-permute-start | bytes 245768 | tf_op jit(solution)/shard_map/ppermute | solution.py:250
  5.8 7.3 %collective-permute-start = (bf16[64,640]{1,0:T(8,128)(2,1)S(1)}, bf16[64,640]{1,0:T(8,128)(2,1)S(1)}, u32[]{:S(2)}, u32[]{:S(2)}) collective-permute-start(bf16[64,640]{1,0:T(8,128)(2,1)S(1)} %get-tuple-element.79), channel_id=1, source_target_pairs={{0,2},{1,3},{2,0},{3,1},{4,6},{5,7},{6,4},{7,5},{8,10},{9,11},{10,... | collective-permute-start | bytes 245768 | tf_op jit(solution)/shard_map/ppermute | solution.py:250
  7.3 6.6 %collective-permute-start.2 = (bf16[64,640]{1,0:T(8,128)(2,1)S(1)}, bf16[64,640]{1,0:T(8,128)(2,1)S(1)}, u32[]{:S(2)}, u32[]{:S(2)}) collective-permute-start(bf16[64,640]{1,0:T(8,128)(2,1)S(1)} %get-tuple-element.79), channel_id=1, source_target_pairs={{0,6},{1,7},{2,4},{3,5},{4,2},{5,3},{6,0},{7,1},{8,14},{9,15},{10,... | collective-permute-start | bytes 245768 | tf_op jit(solution)/shard_map/ppermute | solution.py:250
  8.8 5.1 %collective-permute-start.1 = (bf16[64,640]{1,0:T(8,128)(2,1)S(1)}, bf16[64,640]{1,0:T(8,128)(2,1)S(1)}, u32[]{:S(2)}, u32[]{:S(2)}) collective-permute-start(bf16[64,640]{1,0:T(8,128)(2,1)S(1)} %get-tuple-element.79), channel_id=1, source_target_pairs={{0,4},{1,5},{2,6},{3,7},{4,0},{5,1},{6,2},{7,3},{8,12},{9,13},{10,... | collective-permute-start | bytes 245768 | tf_op jit(solution)/shard_map/ppermute | solution.py:250
  9.8 7.9 %collective-permute-start.6 = (bf16[64,640]{1,0:T(8,128)(2,1)S(1)}, bf16[64,640]{1,0:T(8,128)(2,1)S(1)}, u32[]{:S(2)}, u32[]{:S(2)}) collective-permute-start(bf16[64,640]{1,0:T(8,128)(2,1)S(1)} %collective-permute-done.3), channel_id=1, source_target_pairs={{0,6},{1,7},{2,4},{3,5},{4,2},{5,3},{6,0},{7,1},{8,14},{9,15},{10,... | collective-permute-start | bytes 245768 | tf_op jit(solution)/shard_map/ppermute | solution.py:250
  11.8 5.8 %collective-permute-start.5 = (bf16[64,640]{1,0:T(8,128)(2,1)S(1)}, bf16[64,640]{1,0:T(8,128)(2,1)S(1)}, u32[]{:S(2)}, u32[]{:S(2)}) collective-permute-start(bf16[64,640]{1,0:T(8,128)(2,1)S(1)} %collective-permute-done.3), channel_id=1, source_target_pairs={{0,4},{1,5},{2,6},{3,7},{4,0},{5,1},{6,2},{7,3},{8,12},{9,13},{10,... | collective-permute-start | bytes 245768 | tf_op jit(solution)/shard_map/ppermute | solution.py:250
  19.8 12.4 %collective-permute-start.8 = (bf16[4096,256]{1,0:T(8,128)(2,1)}, bf16[4096,256]{1,0:T(8,128)(2,1)}, u32[]{:S(2)}, u32[]{:S(2)}) collective-permute-start(bf16[4096,256]{1,0:T(8,128)(2,1)} %bitcast.9), channel_id=1, source_target_pairs={{0,1},{1,0},{2,3},{3,2},{4,5},{5,4},{6,7},{7,6},{8,9},{9,8},{10,11... | collective-permute-start | bytes 6291464 | tf_op jit(solution)/shard_map/ppermute | solution.py:261
  20.0 12.3 %collective-permute-start.9 = (bf16[4096,256]{1,0:T(8,128)(2,1)}, bf16[4096,256]{1,0:T(8,128)(2,1)}, u32[]{:S(2)}, u32[]{:S(2)}) collective-permute-start(bf16[4096,256]{1,0:T(8,128)(2,1)} %bitcast.14), channel_id=1, source_target_pairs={{0,1},{1,0},{2,3},{3,2},{4,5},{5,4},{6,7},{7,6},{8,9},{9,8},{10,11... | collective-permute-start | bytes 6291464 | tf_op jit(solution)/shard_map/ppermute | solution.py:261
  20.4 11.9 %collective-permute-start.10 = (bf16[256,4096]{1,0:T(8,128)(2,1)}, bf16[256,4096]{1,0:T(8,128)(2,1)}, u32[]{:S(2)}, u32[]{:S(2)}) collective-permute-start(bf16[256,4096]{1,0:T(8,128)(2,1)} %bitcast.19), channel_id=1, source_target_pairs={{0,1},{1,0},{2,3},{3,2},{4,5},{5,4},{6,7},{7,6},{8,9},{9,8},{10,11... | collective-permute-start | bytes 6291464 | tf_op jit(solution)/shard_map/ppermute | solution.py:261
  32.3 6.6 %collective-permute-start.11 = (bf16[32,4096]{1,0:T(8,128)(2,1)}, bf16[32,4096]{1,0:T(8,128)(2,1)S(1)}, u32[]{:S(2)}, u32[]{:S(2)}) collective-permute-start(bf16[32,4096]{1,0:T(8,128)(2,1)} %get-tuple-element.55.refs_3_), channel_id=1, source_target_pairs={{0,4},{1,3},{4,8},{5,1},{8,12},{9,5},{12,14},{13,9},{14,10},{15,13... | collective-permute-start | bytes 786440 | tf_op jit(solution)/shard_map/ppermute | solution.py:272
  33.3 8.4 %collective-permute-start.13 = (bf16[32,4096]{1,0:T(8,128)(2,1)}, bf16[32,4096]{1,0:T(8,128)(2,1)S(1)}, u32[]{:S(2)}, u32[]{:S(2)}) collective-permute-start(bf16[32,4096]{1,0:T(8,128)(2,1)} %get-tuple-element.57.refs_4_), channel_id=1, source_target_pairs={{0,4},{1,3},{4,8},{5,1},{8,12},{9,5},{12,14},{13,9},{14,10},{15,13... | collective-permute-start | bytes 786440 | tf_op jit(solution)/shard_map/ppermute | solution.py:272
  38.9 12.3 %collective-permute-start.12 = (bf16[32,4096]{1,0:T(8,128)(2,1)S(1)}, bf16[32,4096]{1,0:T(8,128)(2,1)S(1)}, u32[]{:S(2)}, u32[]{:S(2)}) collective-permute-start(bf16[32,4096]{1,0:T(8,128)(2,1)S(1)} %collective-permute-done.11.refs_0_), channel_id=1, source_target_pairs={{0,4},{1,3},{4,8},{5,1},{8,12},{9,5},{12,14},{13,9},{14,10},{15,13... | collective-permute-start | bytes 786440 | tf_op jit(solution)/shard_map/ppermute | solution.py:272
  41.7 10.3 %collective-permute-start.14 = (bf16[32,4096]{1,0:T(8,128)(2,1)S(1)}, bf16[32,4096]{1,0:T(8,128)(2,1)S(1)}, u32[]{:S(2)}, u32[]{:S(2)}) collective-permute-start(bf16[32,4096]{1,0:T(8,128)(2,1)S(1)} %collective-permute-done.13.refs_1_), channel_id=1, source_target_pairs={{0,4},{1,3},{4,8},{5,1},{8,12},{9,5},{12,14},{13,9},{14,10},{15,13... | collective-permute-start | bytes 786440 | tf_op jit(solution)/shard_map/ppermute | solution.py:272
  42.7 11.6 %collective-permute-start.15 = (bf16[64,4096]{1,0:T(8,128)(2,1)}, bf16[64,4096]{1,0:T(8,128)(2,1)S(1)}, u32[]{:S(2)}, u32[]{:S(2)}) collective-permute-start(bf16[64,4096]{1,0:T(8,128)(2,1)} %get-tuple-element.59), channel_id=1, source_target_pairs={{4,0},{3,1},{8,4},{1,5},{12,8},{5,9},{14,12},{9,13},{10,14},{13,15... | collective-permute-start | bytes 1572872 | tf_op jit(solution)/shard_map/ppermute | solution.py:272
  48.6 13.2 %collective-permute-start.27 = (bf16[32,4096]{1,0:T(8,128)(2,1)S(1)}, bf16[32,4096]{1,0:T(8,128)(2,1)S(1)}, u32[]{:S(2)}, u32[]{:S(2)}) collective-permute-start(bf16[32,4096]{1,0:T(8,128)(2,1)S(1)} %convert_element_type.113), channel_id=1, source_target_pairs={{0,4},{1,3},{4,8},{5,1},{8,12},{9,5},{12,14},{13,9},{14,10},{15,13... | collective-permute-start | bytes 786440 | tf_op jit(solution)/shard_map/ppermute | solution.py:272
  49.6 11.3 %collective-permute-start.18 = (bf16[32,4096]{1,0:T(8,128)(2,1)S(1)}, bf16[32,4096]{1,0:T(8,128)(2,1)S(1)}, u32[]{:S(2)}, u32[]{:S(2)}) collective-permute-start(bf16[32,4096]{1,0:T(8,128)(2,1)S(1)} %convert_element_type.99), channel_id=1, source_target_pairs={{0,4},{1,3},{4,8},{5,1},{8,12},{9,5},{12,14},{13,9},{14,10},{15,13... | collective-permute-start | bytes 786440 | tf_op jit(solution)/shard_map/ppermute | solution.py:272
  52.0 18.5 %collective-permute-start.16 = (bf16[64,4096]{1,0:T(8,128)(2,1)S(1)}, bf16[64,4096]{1,0:T(8,128)(2,1)S(1)}, u32[]{:S(2)}, u32[]{:S(2)}) collective-permute-start(bf16[64,4096]{1,0:T(8,128)(2,1)S(1)} %pad_maximum_fusion), channel_id=1, source_target_pairs={{0,4},{1,3},{4,8},{5,1},{8,12},{9,5},{12,14},{13,9},{14,10},{15,13... | collective-permute-start | bytes 1572872 | tf_op jit(solution)/shard_map/ppermute | solution.py:272
  54.3 17.3 %collective-permute-start.17 = (bf16[64,4096]{1,0:T(8,128)(2,1)S(1)}, bf16[64,4096]{1,0:T(8,128)(2,1)S(1)}, u32[]{:S(2)}, u32[]{:S(2)}) collective-permute-start(bf16[64,4096]{1,0:T(8,128)(2,1)S(1)} %collective-permute-done.15.refs_2_), channel_id=1, source_target_pairs={{4,0},{3,1},{8,4},{1,5},{12,8},{5,9},{14,12},{9,13},{10,14},{13,15... | collective-permute-start | bytes 1572872 | tf_op jit(solution)/shard_map/ppermute | solution.py:272
  60.9 16.0 %collective-permute-start.21 = (bf16[32,4096]{1,0:T(8,128)(2,1)S(1)}, bf16[32,4096]{1,0:T(8,128)(2,1)S(1)}, u32[]{:S(2)}, u32[]{:S(2)}) collective-permute-start(bf16[32,4096]{1,0:T(8,128)(2,1)S(1)} %add_convert_fusion.11), channel_id=1, source_target_pairs={{0,4},{1,3},{4,8},{5,1},{8,12},{9,5},{12,14},{13,9},{14,10},{15,13... | collective-permute-start | bytes 786440 | tf_op jit(solution)/shard_map/ppermute | solution.py:272
  61.8 18.6 %collective-permute-start.28 = (bf16[32,4096]{1,0:T(8,128)(2,1)S(1)}, bf16[32,4096]{1,0:T(8,128)(2,1)S(1)}, u32[]{:S(2)}, u32[]{:S(2)}) collective-permute-start(bf16[32,4096]{1,0:T(8,128)(2,1)S(1)} %add_convert_fusion.5), channel_id=1, source_target_pairs={{0,4},{1,3},{4,8},{5,1},{8,12},{9,5},{12,14},{13,9},{14,10},{15,13... | collective-permute-start | bytes 786440 | tf_op jit(solution)/shard_map/ppermute | solution.py:272
  70.6 16.9 %collective-permute-start.19 = (bf16[64,4096]{1,0:T(8,128)(2,1)S(1)}, bf16[64,4096]{1,0:T(8,128)(2,1)S(1)}, u32[]{:S(2)}, u32[]{:S(2)}) collective-permute-start(bf16[64,4096]{1,0:T(8,128)(2,1)S(1)} %collective-permute-done.16.refs_0_), channel_id=1, source_target_pairs={{0,4},{1,3},{4,8},{5,1},{8,12},{9,5},{12,14},{13,9},{14,10},{15,13... | collective-permute-start | bytes 1572872 | tf_op jit(solution)/shard_map/ppermute | solution.py:272
  71.5 15.9 %collective-permute-start.20 = (bf16[64,4096]{1,0:T(8,128)(2,1)S(1)}, bf16[64,4096]{1,0:T(8,128)(2,1)S(1)}, u32[]{:S(2)}, u32[]{:S(2)}) collective-permute-start(bf16[64,4096]{1,0:T(8,128)(2,1)S(1)} %collective-permute-done.17.refs_1_), channel_id=1, source_target_pairs={{4,0},{3,1},{8,4},{1,5},{12,8},{5,9},{14,12},{9,13},{10,14},{13,15... | collective-permute-start | bytes 1572872 | tf_op jit(solution)/shard_map/ppermute | solution.py:272
  77.0 14.8 %collective-permute-start.22 = (bf16[32,4096]{1,0:T(8,128)(2,1)S(1)}, bf16[32,4096]{1,0:T(8,128)(2,1)S(1)}, u32[]{:S(2)}, u32[]{:S(2)}) collective-permute-start(bf16[32,4096]{1,0:T(8,128)(2,1)S(1)} %add_convert_fusion.10), channel_id=1, source_target_pairs={{0,4},{1,3},{4,8},{5,1},{8,12},{9,5},{12,14},{13,9},{14,10},{15,13... | collective-permute-start | bytes 786440 | tf_op jit(solution)/shard_map/ppermute | solution.py:272
  80.5 12.6 %collective-permute-start.29 = (bf16[32,4096]{1,0:T(8,128)(2,1)S(1)}, bf16[32,4096]{1,0:T(8,128)(2,1)S(1)}, u32[]{:S(2)}, u32[]{:S(2)}) collective-permute-start(bf16[32,4096]{1,0:T(8,128)(2,1)S(1)} %add_convert_fusion.4), channel_id=1, source_target_pairs={{0,4},{1,3},{4,8},{5,1},{8,12},{9,5},{12,14},{13,9},{14,10},{15,13... | collective-permute-start | bytes 786440 | tf_op jit(solution)/shard_map/ppermute | solution.py:272
  91.8 6.4 %collective-permute-start.23 = (bf16[32,4096]{1,0:T(8,128)(2,1)S(1)}, bf16[32,4096]{1,0:T(8,128)(2,1)S(1)}, u32[]{:S(2)}, u32[]{:S(2)}) collective-permute-start(bf16[32,4096]{1,0:T(8,128)(2,1)S(1)} %add_convert_fusion.9), channel_id=1, source_target_pairs={{0,4},{1,3},{4,8},{5,1},{8,12},{9,5},{12,14},{13,9},{14,10},{15,13... | collective-permute-start | bytes 786440 | tf_op jit(solution)/shard_map/ppermute | solution.py:272
  93.1 8.0 %collective-permute-start.30 = (bf16[32,4096]{1,0:T(8,128)(2,1)S(1)}, bf16[32,4096]{1,0:T(8,128)(2,1)S(1)}, u32[]{:S(2)}, u32[]{:S(2)}) collective-permute-start(bf16[32,4096]{1,0:T(8,128)(2,1)S(1)} %add_convert_fusion.3), channel_id=1, source_target_pairs={{0,4},{1,3},{4,8},{5,1},{8,12},{9,5},{12,14},{13,9},{14,10},{15,13... | collective-permute-start | bytes 786440 | tf_op jit(solution)/shard_map/ppermute | solution.py:272
  98.3 6.4 %collective-permute-start.24 = (bf16[32,4096]{1,0:T(8,128)(2,1)S(1)}, bf16[32,4096]{1,0:T(8,128)(2,1)S(1)}, u32[]{:S(2)}, u32[]{:S(2)}) collective-permute-start(bf16[32,4096]{1,0:T(8,128)(2,1)S(1)} %add_convert_fusion.8), channel_id=1, source_target_pairs={{0,4},{1,3},{4,8},{5,1},{8,12},{9,5},{12,14},{13,9},{14,10},{15,13... | collective-permute-start | bytes 786440 | tf_op jit(solution)/shard_map/ppermute | solution.py:272
  101.1 6.4 %collective-permute-start.31 = (bf16[32,4096]{1,0:T(8,128)(2,1)S(1)}, bf16[32,4096]{1,0:T(8,128)(2,1)S(1)}, u32[]{:S(2)}, u32[]{:S(2)}) collective-permute-start(bf16[32,4096]{1,0:T(8,128)(2,1)S(1)} %add_convert_fusion.2), channel_id=1, source_target_pairs={{0,4},{1,3},{4,8},{5,1},{8,12},{9,5},{12,14},{13,9},{14,10},{15,13... | collective-permute-start | bytes 786440 | tf_op jit(solution)/shard_map/ppermute | solution.py:272
  104.8 6.4 %collective-permute-start.25 = (bf16[32,4096]{1,0:T(8,128)(2,1)S(1)}, bf16[32,4096]{1,0:T(8,128)(2,1)S(1)}, u32[]{:S(2)}, u32[]{:S(2)}) collective-permute-start(bf16[32,4096]{1,0:T(8,128)(2,1)S(1)} %add_convert_fusion.7), channel_id=1, source_target_pairs={{0,4},{1,3},{4,8},{5,1},{8,12},{9,5},{12,14},{13,9},{14,10},{15,13... | collective-permute-start | bytes 786440 | tf_op jit(solution)/shard_map/ppermute | solution.py:272
  107.6 6.4 %collective-permute-start.32 = (bf16[32,4096]{1,0:T(8,128)(2,1)S(1)}, bf16[32,4096]{1,0:T(8,128)(2,1)S(1)}, u32[]{:S(2)}, u32[]{:S(2)}) collective-permute-start(bf16[32,4096]{1,0:T(8,128)(2,1)S(1)} %add_convert_fusion.1), channel_id=1, source_target_pairs={{0,4},{1,3},{4,8},{5,1},{8,12},{9,5},{12,14},{13,9},{14,10},{15,13... | collective-permute-start | bytes 786440 | tf_op jit(solution)/shard_map/ppermute | solution.py:272
  111.3 6.4 %collective-permute-start.26 = (bf16[32,4096]{1,0:T(8,128)(2,1)S(1)}, bf16[32,4096]{1,0:T(8,128)(2,1)S(1)}, u32[]{:S(2)}, u32[]{:S(2)}) collective-permute-start(bf16[32,4096]{1,0:T(8,128)(2,1)S(1)} %add_convert_fusion.6), channel_id=1, source_target_pairs={{0,4},{1,3},{4,8},{5,1},{8,12},{9,5},{12,14},{13,9},{14,10},{15,13... | collective-permute-start | bytes 786440 | tf_op jit(solution)/shard_map/ppermute | solution.py:272
  114.1 6.4 %collective-permute-start.33 = (bf16[32,4096]{1,0:T(8,128)(2,1)S(1)}, bf16[32,4096]{1,0:T(8,128)(2,1)S(1)}, u32[]{:S(2)}, u32[]{:S(2)}) collective-permute-start(bf16[32,4096]{1,0:T(8,128)(2,1)S(1)} %add_convert_fusion), channel_id=1, source_target_pairs={{0,4},{1,3},{4,8},{5,1},{8,12},{9,5},{12,14},{13,9},{14,10},{15,13... | collective-permute-start | bytes 786440 | tf_op jit(solution)/shard_map/ppermute | solution.py:272
  (11 other events, 125.2 us)

commit v16 on v15

--- a/solution.py
+++ b/solution.py
@@ -280,7 +280,6 @@
     def rounded(part):
         return tuple(x.astype(jnp.bfloat16) for x in part)
 
-    turn = chips // 2
     rows = {0: start, 1: move(start)}
     table = jnp.where(hits > 0.5, 1.0, 0.0)
     rows[2] = move(after(rows[1][:1], table)) + move(rows[1][1:])
@@ -290,13 +289,11 @@
     sums = rounded(parts[1])
     for hop in range(1, chips):
         arrived = move(sums)
-        here, there = hop + 1, chips - hop
-        if here <= turn:
-            if 3 < here + 1 <= turn:
-                rows[here + 1] = move(after(rows[here], sums[0]))
-            if here < turn:
-                rows[there - 1] = move(after(rows[there], sums[0]), back)
-            hops = (here, there, 0) if hop == 1 else (here, there)
+        here = hop + 1
+        if hop + 3 < chips - 1:
+            rows[hop + 3] = move(after(rows[hop + 2], sums[0]))
+        if here < chips - 1:
+            hops = (here, chips - 1, 0) if hop == 1 else (here,)
             parts.update(zip(hops, parts_of(rows, hops)))
         if here < chips:
             sums = rounded(added(parts[here], arrived))

time: 122 us -> 120 us (0.984)
  waiting for transfers between devices: 48.9 us -> 27.9 us
  Pallas kernels: 30.1 us -> 40.1 us
  starting transfers between devices: 37.8 us -> 47.3 us
    ppermute x23, waiting for transfers between devices: 42 us -> 21.3 us  [move(): return tuple((lax.ppermute(x, 'ctx', way) for x in blocks))]
    pallas_call x4 -> x6, Pallas kernels: 18.5 us -> 28.6 us  [expert_parts(): pl.pallas_call(functools.partial(expert_kernel, hops=hops, chips=chips),...]
    ppermute x23, starting transfers between devices: 26 us -> 35.2 us  [move(): return tuple((lax.ppermute(x, 'ctx', way) for x in blocks))]
  transfers between devices with their start and end apart: 34 -> 34, of which waited for: 20 -> 17; matrix products, arithmetic and copies ran while one was open for 1% -> 1% of each run, Pallas kernels for 25% -> 33%
where the time goes in v16:
time: 120 us
  starting transfers between devices  47.3 us (39%)
  Pallas kernels  40.1 us (33%)
  waiting for transfers between devices  27.9 us (23%)
  other arithmetic  4.12 us (3%)
    ppermute x23, starting transfers between devices, move(): return tuple((lax.ppermute(x, 'ctx', way) for x in blocks))  35.2 us
    pallas_call x6, Pallas kernels, expert_parts(): pl.pallas_call(functools.partial(expert_kernel, hops=hops, chips=chips),...  28.6 us
    ppermute x23, waiting for transfers between devices, move(): return tuple((lax.ppermute(x, 'ctx', way) for x in blocks))  21.3 us
    pallas_call x1, Pallas kernels, attention(): pl.pallas_call(functools.partial(attention_kernel, tok=tok), grid_spec=gr...  11.5 us
    ppermute x7, starting transfers between devices, from_chip(): lax.ppermute(block, 'ctx', [(i, i ^ step * CORES) for i in range(n_ctx)])  11.4 us
    ppermute x7, waiting for transfers between devices, from_chip(): lax.ppermute(block, 'ctx', [(i, i ^ step * CORES) for i in range(n_ctx)])  4.54 us
  transfers between devices with their start and end apart: 34, of which 17 were waited for; matrix products, arithmetic and copies ran while one was open for 1% of the time, Pallas kernels for 33%

profile of v16, /device:TPU:0, one launch (start us, length us, event | category | flops | bytes accessed | tf_op | source)
XLA Modules:
  0.0 120.2 jit_solution(11540880758396979159)
XLA Ops:
  1.7 4.1 %collective-permute-start.3 = (bf16[64,640]{1,0:T(8,128)(2,1)S(1)}, bf16[64,640]{1,0:T(8,128)(2,1)S(1)}, u32[]{:S(2)}, u32[]{:S(2)}) collective-permute-start(bf16[64,640]{1,0:T(8,128)(2,1)S(1)} %get-tuple-element.79), channel_id=1, source_target_pairs={{0,8},{1,9},{2,10},{3,11},{4,12},{5,13},{6,14},{7,15},{8,0},{9,1},... | collective-permute-start | bytes 245768 | tf_op jit(solution)/shard_map/ppermute | solution.py:250
  9.8 1.6 %collective-permute-start.4 = (bf16[64,640]{1,0:T(8,128)(2,1)S(1)}, bf16[64,640]{1,0:T(8,128)(2,1)S(1)}, u32[]{:S(2)}, u32[]{:S(2)}) collective-permute-start(bf16[64,640]{1,0:T(8,128)(2,1)S(1)} %collective-permute-done.3), channel_id=1, source_target_pairs={{0,2},{1,3},{2,0},{3,1},{4,6},{5,7},{6,4},{7,5},{8,10},{9,11},{10,... | collective-permute-start | bytes 245768 | tf_op jit(solution)/shard_map/ppermute | solution.py:250
  15.9 1.8 %collective-permute-done.6 = bf16[64,640]{1,0:T(8,128)(2,1)S(1)} collective-permute-done((bf16[64,640]{1,0:T(8,128)(2,1)S(1)}, bf16[64,640]{1,0:T(8,128)(2,1)S(1)}, u32[]{:S(2)}, u32[]{:S(2)}) %collective-permute-start.6) | collective-permute-done | bytes 81952 | tf_op jit(solution)/shard_map/ppermute | solution.py:250
  17.8 2.1 %collective-permute-done.7.other_ref = bf16[512,640]{1,0:T(8,128)(2,1)S(1)} collective-permute-done((bf16[512,640]{1,0:T(8,128)(2,1)S(1)}, bf16[512,640]{1,0:T(8,128)(2,1)S(1)}, u32[]{:S(2)}, u32[]{:S(2)}) %collective-permute-start.7) | collective-permute-done | bytes 655392 | tf_op jit(solution)/shard_map/ppermute | solution.py:258
  20.8 11.5 %shard_map.109 = (bf16[64,4096]{1,0:T(8,128)(2,1)}, bf16[64,4096]{1,0:T(8,128)(2,1)}, bf16[32,4096]{1,0:T(8,128)(2,1)}, bf16[32,4096]{1,0:T(8,128)(2,1)}, f32[64,8]{1,0:T(8,128)}) custom-call(s32[1]{0:T(128)} %bitcast.index_ref, bf16[64,16384]{1,0:T(8,128)(2,1)} %q_ref.1, bf16[64,2048]{1,0:T(8,128)(2,1)} %qr_ref.1, bf16[512,640]{1,0:T(8,128)(2,1)} %copy-done.6, ...), custom_call_target="tpu_custom_call" | custom-call | flops 4831838208 | bytes 8388608 | tf_op jit(solution)/shard_map/pallas_call | solution.py:151
  33.4 2.7 %collective-permute-start.13 = (bf16[32,4096]{1,0:T(8,128)(2,1)}, bf16[32,4096]{1,0:T(8,128)(2,1)S(1)}, u32[]{:S(2)}, u32[]{:S(2)}) collective-permute-start(bf16[32,4096]{1,0:T(8,128)(2,1)} %get-tuple-element.57.refs_4_), channel_id=1, source_target_pairs={{0,4},{1,3},{4,8},{5,1},{8,12},{9,5},{12,14},{13,9},{14,10},{15,13... | collective-permute-start | bytes 786440 | tf_op jit(solution)/shard_map/ppermute | solution.py:272
  36.9 2.0 %collective-permute-done.11.refs_0_ = bf16[32,4096]{1,0:T(8,128)(2,1)S(1)} collective-permute-done((bf16[32,4096]{1,0:T(8,128)(2,1)}, bf16[32,4096]{1,0:T(8,128)(2,1)S(1)}, u32[]{:S(2)}, u32[]{:S(2)}) %collective-permute-start.11) | collective-permute-done | bytes 262176 | tf_op jit(solution)/shard_map/ppermute | solution.py:272
  43.8 4.7 %shard_map.111 = (f32[32,4096]{1,0:T(8,128)S(1)}, f32[32,4096]{1,0:T(8,128)S(1)}) custom-call(s32[1]{0:T(128)} %bitcast.index_ref, bf16[4096,256]{1,0:T(8,128)(2,1)S(1)} %bitcast.10, bf16[4096,256]{1,0:T(8,128)(2,1)S(1)} %bitcast.17, bf16[256,4096]{1,0:T(8,128)(2,1)S(1)} %bitcast.24, f32[64,8]{1,0:T(8,128)S(1)} %compare_select_fusion.hits_hbm, ...), custom_call_target="tpu_custom_call" | custom-call | flops 805306368 | bytes 14680064 | tf_op jit(solution)/shard_map/pallas_call | solution.py:218
  48.6 1.9 %collective-permute-start.18 = (bf16[32,4096]{1,0:T(8,128)(2,1)S(1)}, bf16[32,4096]{1,0:T(8,128)(2,1)S(1)}, u32[]{:S(2)}, u32[]{:S(2)}) collective-permute-start(bf16[32,4096]{1,0:T(8,128)(2,1)S(1)} %convert_element_type.99), channel_id=1, source_target_pairs={{0,4},{1,3},{4,8},{5,1},{8,12},{9,5},{12,14},{13,9},{14,10},{15,13... | collective-permute-start | bytes 786440 | tf_op jit(solution)/shard_map/ppermute | solution.py:272
  50.5 2.0 %collective-permute-start.27 = (bf16[32,4096]{1,0:T(8,128)(2,1)S(1)}, bf16[32,4096]{1,0:T(8,128)(2,1)S(1)}, u32[]{:S(2)}, u32[]{:S(2)}) collective-permute-start(bf16[32,4096]{1,0:T(8,128)(2,1)S(1)} %convert_element_type.113), channel_id=1, source_target_pairs={{0,4},{1,3},{4,8},{5,1},{8,12},{9,5},{12,14},{13,9},{14,10},{15,13... | collective-permute-start | bytes 786440 | tf_op jit(solution)/shard_map/ppermute | solution.py:272
  53.7 1.8 %collective-permute-done.15.refs_2_ = bf16[64,4096]{1,0:T(8,128)(2,1)S(1)} collective-permute-done((bf16[64,4096]{1,0:T(8,128)(2,1)}, bf16[64,4096]{1,0:T(8,128)(2,1)S(1)}, u32[]{:S(2)}, u32[]{:S(2)}) %collective-permute-start.15) | collective-permute-done | bytes 524320 | tf_op jit(solution)/shard_map/ppermute | solution.py:272
  55.5 5.2 %shard_map.110 = (f32[32,4096]{1,0:T(8,128)S(1)}, f32[32,4096]{1,0:T(8,128)S(1)}, f32[32,4096]{1,0:T(8,128)S(1)}, f32[32,4096]{1,0:T(8,128)S(1)}, f32[32,4096]{1,0:T(8,128)S(1)}, /*index=5*/f32[32,4096]{1,0:T(8,128)S(1)}) custom-call(s32[1]{0:T(128)} %bitcast.index_ref, bf16[4096,256]{1,0:T(8,128)(2,1)S(1)} %bitcast.11, bf16[4096,256]{1,0:T(8,128)(2,1)S(1)} %bitcast.18, ...), custom_call_target="tpu_custom_call" | custom-call | flops 805306368 | bytes 14680064 | tf_op jit(solution)/shard_map/pallas_call | solution.py:218
  60.7 2.4 %collective-permute-start.28 = (bf16[32,4096]{1,0:T(8,128)(2,1)S(1)}, bf16[32,4096]{1,0:T(8,128)(2,1)S(1)}, u32[]{:S(2)}, u32[]{:S(2)}) collective-permute-start(bf16[32,4096]{1,0:T(8,128)(2,1)S(1)} %add_convert_fusion.5), channel_id=1, source_target_pairs={{0,4},{1,3},{4,8},{5,1},{8,12},{9,5},{12,14},{13,9},{14,10},{15,13... | collective-permute-start | bytes 786440 | tf_op jit(solution)/shard_map/ppermute | solution.py:272
  66.4 4.7 %shard_map.112 = (f32[32,4096]{1,0:T(8,128)S(1)}, f32[32,4096]{1,0:T(8,128)S(1)}) custom-call(s32[1]{0:T(128)} %bitcast.index_ref, bf16[4096,256]{1,0:T(8,128)(2,1)S(1)} %bitcast.12, bf16[4096,256]{1,0:T(8,128)(2,1)S(1)} %bitcast.19, bf16[256,4096]{1,0:T(8,128)(2,1)S(1)} %bitcast.26, f32[64,8]{1,0:T(8,128)S(1)} %compare_select_fusion.hits_hbm, ...), custom_call_target="tpu_custom_call" | custom-call | flops 805306368 | bytes 14680064 | tf_op jit(solution)/shard_map/pallas_call | solution.py:218
  71.2 2.4 %collective-permute-start.29 = (bf16[32,4096]{1,0:T(8,128)(2,1)S(1)}, bf16[32,4096]{1,0:T(8,128)(2,1)S(1)}, u32[]{:S(2)}, u32[]{:S(2)}) collective-permute-start(bf16[32,4096]{1,0:T(8,128)(2,1)S(1)} %add_convert_fusion.4), channel_id=1, source_target_pairs={{0,4},{1,3},{4,8},{5,1},{8,12},{9,5},{12,14},{13,9},{14,10},{15,13... | collective-permute-start | bytes 786440 | tf_op jit(solution)/shard_map/ppermute | solution.py:272
  74.1 2.2 %collective-permute-done.17.refs_0_ = bf16[64,4096]{1,0:T(8,128)(2,1)S(1)} collective-permute-done((bf16[64,4096]{1,0:T(8,128)(2,1)S(1)}, bf16[64,4096]{1,0:T(8,128)(2,1)S(1)}, u32[]{:S(2)}, u32[]{:S(2)}) %collective-permute-start.17) | collective-permute-done | bytes 524320 | tf_op jit(solution)/shard_map/ppermute | solution.py:272
  76.2 1.6 %collective-permute-start.19 = (bf16[64,4096]{1,0:T(8,128)(2,1)S(1)}, bf16[64,4096]{1,0:T(8,128)(2,1)S(1)}, u32[]{:S(2)}, u32[]{:S(2)}) collective-permute-start(bf16[64,4096]{1,0:T(8,128)(2,1)S(1)} %collective-permute-done.17.refs_0_), channel_id=1, source_target_pairs={{0,4},{1,3},{4,8},{5,1},{8,12},{9,5},{12,14},{13,9},{14,10},{15,13... | collective-permute-start | bytes 1572872 | tf_op jit(solution)/shard_map/ppermute | solution.py:272
  77.9 4.7 %shard_map.115 = (f32[32,4096]{1,0:T(8,128)S(1)}, f32[32,4096]{1,0:T(8,128)S(1)}) custom-call(s32[1]{0:T(128)} %bitcast.index_ref, bf16[4096,256]{1,0:T(8,128)(2,1)S(1)} %bitcast.13, bf16[4096,256]{1,0:T(8,128)(2,1)S(1)} %bitcast.20, bf16[256,4096]{1,0:T(8,128)(2,1)S(1)} %bitcast.27, f32[64,8]{1,0:T(8,128)S(1)} %compare_select_fusion.hits_hbm, ...), custom_call_target="tpu_custom_call" | custom-call | flops 805306368 | bytes 14680064 | tf_op jit(solution)/shard_map/pallas_call | solution.py:218
  82.6 2.2 %collective-permute-start.30 = (bf16[32,4096]{1,0:T(8,128)(2,1)S(1)}, bf16[32,4096]{1,0:T(8,128)(2,1)S(1)}, u32[]{:S(2)}, u32[]{:S(2)}) collective-permute-start(bf16[32,4096]{1,0:T(8,128)(2,1)S(1)} %add_convert_fusion.3), channel_id=1, source_target_pairs={{0,4},{1,3},{4,8},{5,1},{8,12},{9,5},{12,14},{13,9},{14,10},{15,13... | collective-permute-start | bytes 786440 | tf_op jit(solution)/shard_map/ppermute | solution.py:272
  85.3 2.2 %collective-permute-done.19.refs_0_ = bf16[64,4096]{1,0:T(8,128)(2,1)S(1)} collective-permute-done((bf16[64,4096]{1,0:T(8,128)(2,1)S(1)}, bf16[64,4096]{1,0:T(8,128)(2,1)S(1)}, u32[]{:S(2)}, u32[]{:S(2)}) %collective-permute-start.19) | collective-permute-done | bytes 524320 | tf_op jit(solution)/shard_map/ppermute | solution.py:272
  87.5 1.6 %collective-permute-start.21 = (bf16[64,4096]{1,0:T(8,128)(2,1)S(1)}, bf16[64,4096]{1,0:T(8,128)(2,1)S(1)}, u32[]{:S(2)}, u32[]{:S(2)}) collective-permute-start(bf16[64,4096]{1,0:T(8,128)(2,1)S(1)} %collective-permute-done.19.refs_0_), channel_id=1, source_target_pairs={{0,4},{1,3},{4,8},{5,1},{8,12},{9,5},{12,14},{13,9},{14,10},{15,13... | collective-permute-start | bytes 1572872 | tf_op jit(solution)/shard_map/ppermute | solution.py:272
  89.1 4.7 %shard_map.114 = (f32[32,4096]{1,0:T(8,128)S(1)}, f32[32,4096]{1,0:T(8,128)S(1)}) custom-call(s32[1]{0:T(128)} %bitcast.index_ref, bf16[4096,256]{1,0:T(8,128)(2,1)S(1)} %bitcast.14, bf16[4096,256]{1,0:T(8,128)(2,1)S(1)} %bitcast.21, bf16[256,4096]{1,0:T(8,128)(2,1)S(1)} %bitcast.28, f32[64,8]{1,0:T(8,128)S(1)} %compare_select_fusion.hits_hbm, ...), custom_call_target="tpu_custom_call" | custom-call | flops 805306368 | bytes 14680064 | tf_op jit(solution)/shard_map/pallas_call | solution.py:218
  93.8 2.2 %collective-permute-start.31 = (bf16[32,4096]{1,0:T(8,128)(2,1)S(1)}, bf16[32,4096]{1,0:T(8,128)(2,1)S(1)}, u32[]{:S(2)}, u32[]{:S(2)}) collective-permute-start(bf16[32,4096]{1,0:T(8,128)(2,1)S(1)} %add_convert_fusion.2), channel_id=1, source_target_pairs={{0,4},{1,3},{4,8},{5,1},{8,12},{9,5},{12,14},{13,9},{14,10},{15,13... | collective-permute-start | bytes 786440 | tf_op jit(solution)/shard_map/ppermute | solution.py:272
  96.5 2.2 %collective-permute-done.21.refs_0_ = bf16[64,4096]{1,0:T(8,128)(2,1)S(1)} collective-permute-done((bf16[64,4096]{1,0:T(8,128)(2,1)S(1)}, bf16[64,4096]{1,0:T(8,128)(2,1)S(1)}, u32[]{:S(2)}, u32[]{:S(2)}) %collective-permute-start.21) | collective-permute-done | bytes 524320 | tf_op jit(solution)/shard_map/ppermute | solution.py:272
  98.7 4.7 %shard_map.113 = (f32[32,4096]{1,0:T(8,128)S(1)}, f32[32,4096]{1,0:T(8,128)S(1)}) custom-call(s32[1]{0:T(128)} %bitcast.index_ref, bf16[4096,256]{1,0:T(8,128)(2,1)S(1)} %bitcast.15, bf16[4096,256]{1,0:T(8,128)(2,1)S(1)} %bitcast.22, bf16[256,4096]{1,0:T(8,128)(2,1)S(1)} %bitcast.29, f32[64,8]{1,0:T(8,128)S(1)} %compare_select_fusion.hits_hbm, ...), custom_call_target="tpu_custom_call" | custom-call | flops 805306368 | bytes 14680064 | tf_op jit(solution)/shard_map/pallas_call | solution.py:218
  103.4 1.7 %collective-permute-start.32 = (bf16[32,4096]{1,0:T(8,128)(2,1)S(1)}, bf16[32,4096]{1,0:T(8,128)(2,1)S(1)}, u32[]{:S(2)}, u32[]{:S(2)}) collective-permute-start(bf16[32,4096]{1,0:T(8,128)(2,1)S(1)} %add_convert_fusion.1), channel_id=1, source_target_pairs={{0,4},{1,3},{4,8},{5,1},{8,12},{9,5},{12,14},{13,9},{14,10},{15,13... | collective-permute-start | bytes 786440 | tf_op jit(solution)/shard_map/ppermute | solution.py:272
  105.2 2.2 %collective-permute-start.25 = (bf16[32,4096]{1,0:T(8,128)(2,1)S(1)}, bf16[32,4096]{1,0:T(8,128)(2,1)S(1)}, u32[]{:S(2)}, u32[]{:S(2)}) collective-permute-start(bf16[32,4096]{1,0:T(8,128)(2,1)S(1)} %add_convert_fusion.7), channel_id=1, source_target_pairs={{0,4},{1,3},{4,8},{5,1},{8,12},{9,5},{12,14},{13,9},{14,10},{15,13... | collective-permute-start | bytes 786440 | tf_op jit(solution)/shard_map/ppermute | solution.py:272
  107.4 2.5 %collective-permute-done.32 = bf16[32,4096]{1,0:T(8,128)(2,1)S(1)} collective-permute-done((bf16[32,4096]{1,0:T(8,128)(2,1)S(1)}, bf16[32,4096]{1,0:T(8,128)(2,1)S(1)}, u32[]{:S(2)}, u32[]{:S(2)}) %collective-permute-start.32) | collective-permute-done | bytes 262176 | tf_op jit(solution)/shard_map/ppermute | solution.py:272
  109.9 1.7 %collective-permute-start.33 = (bf16[32,4096]{1,0:T(8,128)(2,1)S(1)}, bf16[32,4096]{1,0:T(8,128)(2,1)S(1)}, u32[]{:S(2)}, u32[]{:S(2)}) collective-permute-start(bf16[32,4096]{1,0:T(8,128)(2,1)S(1)} %add_convert_fusion), channel_id=1, source_target_pairs={{0,4},{1,3},{4,8},{5,1},{8,12},{9,5},{12,14},{13,9},{14,10},{15,13... | collective-permute-start | bytes 786440 | tf_op jit(solution)/shard_map/ppermute | solution.py:272
  112.7 1.7 %collective-permute-start.26 = (bf16[32,4096]{1,0:T(8,128)(2,1)S(1)}, bf16[32,4096]{1,0:T(8,128)(2,1)S(1)}, u32[]{:S(2)}, u32[]{:S(2)}) collective-permute-start(bf16[32,4096]{1,0:T(8,128)(2,1)S(1)} %add_convert_fusion.6), channel_id=1, source_target_pairs={{0,4},{1,3},{4,8},{5,1},{8,12},{9,5},{12,14},{13,9},{14,10},{15,13... | collective-permute-start | bytes 786440 | tf_op jit(solution)/shard_map/ppermute | solution.py:272
  114.4 1.9 %collective-permute-done.33 = bf16[32,4096]{1,0:T(8,128)(2,1)S(1)} collective-permute-done((bf16[32,4096]{1,0:T(8,128)(2,1)S(1)}, bf16[32,4096]{1,0:T(8,128)(2,1)S(1)}, u32[]{:S(2)}, u32[]{:S(2)}) %collective-permute-start.33) | collective-permute-done | bytes 262176 | tf_op jit(solution)/shard_map/ppermute | solution.py:272
  116.4 2.8 %collective-permute-done.26 = bf16[32,4096]{1,0:T(8,128)(2,1)S(1)} collective-permute-done((bf16[32,4096]{1,0:T(8,128)(2,1)S(1)}, bf16[32,4096]{1,0:T(8,128)(2,1)S(1)}, u32[]{:S(2)}, u32[]{:S(2)}) %collective-permute-start.26) | collective-permute-done | bytes 262176 | tf_op jit(solution)/shard_map/ppermute | solution.py:272
  (91 shorter events, 26.4 us)
Async XLA Ops:
  1.7 8.1 %collective-permute-start.3 = (bf16[64,640]{1,0:T(8,128)(2,1)S(1)}, bf16[64,640]{1,0:T(8,128)(2,1)S(1)}, u32[]{:S(2)}, u32[]{:S(2)}) collective-permute-start(bf16[64,640]{1,0:T(8,128)(2,1)S(1)} %get-tuple-element.79), channel_id=1, source_target_pairs={{0,8},{1,9},{2,10},{3,11},{4,12},{5,13},{6,14},{7,15},{8,0},{9,1},... | collective-permute-start | bytes 245768 | tf_op jit(solution)/shard_map/ppermute | solution.py:250
  5.8 6.6 %collective-permute-start = (bf16[64,640]{1,0:T(8,128)(2,1)S(1)}, bf16[64,640]{1,0:T(8,128)(2,1)S(1)}, u32[]{:S(2)}, u32[]{:S(2)}) collective-permute-start(bf16[64,640]{1,0:T(8,128)(2,1)S(1)} %get-tuple-element.79), channel_id=1, source_target_pairs={{0,2},{1,3},{2,0},{3,1},{4,6},{5,7},{6,4},{7,5},{8,10},{9,11},{10,... | collective-permute-start | bytes 245768 | tf_op jit(solution)/shard_map/ppermute | solution.py:250
  7.3 6.3 %collective-permute-start.1 = (bf16[64,640]{1,0:T(8,128)(2,1)S(1)}, bf16[64,640]{1,0:T(8,128)(2,1)S(1)}, u32[]{:S(2)}, u32[]{:S(2)}) collective-permute-start(bf16[64,640]{1,0:T(8,128)(2,1)S(1)} %get-tuple-element.79), channel_id=1, source_target_pairs={{0,4},{1,5},{2,6},{3,7},{4,0},{5,1},{6,2},{7,3},{8,12},{9,13},{10,... | collective-permute-start | bytes 245768 | tf_op jit(solution)/shard_map/ppermute | solution.py:250
  8.9 5.6 %collective-permute-start.2 = (bf16[64,640]{1,0:T(8,128)(2,1)S(1)}, bf16[64,640]{1,0:T(8,128)(2,1)S(1)}, u32[]{:S(2)}, u32[]{:S(2)}) collective-permute-start(bf16[64,640]{1,0:T(8,128)(2,1)S(1)} %get-tuple-element.79), channel_id=1, source_target_pairs={{0,6},{1,7},{2,4},{3,5},{4,2},{5,3},{6,0},{7,1},{8,14},{9,15},{10,... | collective-permute-start | bytes 245768 | tf_op jit(solution)/shard_map/ppermute | solution.py:250
  9.8 5.5 %collective-permute-start.4 = (bf16[64,640]{1,0:T(8,128)(2,1)S(1)}, bf16[64,640]{1,0:T(8,128)(2,1)S(1)}, u32[]{:S(2)}, u32[]{:S(2)}) collective-permute-start(bf16[64,640]{1,0:T(8,128)(2,1)S(1)} %collective-permute-done.3), channel_id=1, source_target_pairs={{0,2},{1,3},{2,0},{3,1},{4,6},{5,7},{6,4},{7,5},{8,10},{9,11},{10,... | collective-permute-start | bytes 245768 | tf_op jit(solution)/shard_map/ppermute | solution.py:250
  12.4 5.3 %collective-permute-start.6 = (bf16[64,640]{1,0:T(8,128)(2,1)S(1)}, bf16[64,640]{1,0:T(8,128)(2,1)S(1)}, u32[]{:S(2)}, u32[]{:S(2)}) collective-permute-start(bf16[64,640]{1,0:T(8,128)(2,1)S(1)} %collective-permute-done.3), channel_id=1, source_target_pairs={{0,6},{1,7},{2,4},{3,5},{4,2},{5,3},{6,0},{7,1},{8,14},{9,15},{10,... | collective-permute-start | bytes 245768 | tf_op jit(solution)/shard_map/ppermute | solution.py:250
  19.9 12.4 %collective-permute-start.8 = (bf16[4096,256]{1,0:T(8,128)(2,1)}, bf16[4096,256]{1,0:T(8,128)(2,1)}, u32[]{:S(2)}, u32[]{:S(2)}) collective-permute-start(bf16[4096,256]{1,0:T(8,128)(2,1)} %bitcast.9), channel_id=1, source_target_pairs={{0,1},{1,0},{2,3},{3,2},{4,5},{5,4},{6,7},{7,6},{8,9},{9,8},{10,11... | collective-permute-start | bytes 6291464 | tf_op jit(solution)/shard_map/ppermute | solution.py:261
  20.0 12.3 %collective-permute-start.9 = (bf16[4096,256]{1,0:T(8,128)(2,1)}, bf16[4096,256]{1,0:T(8,128)(2,1)}, u32[]{:S(2)}, u32[]{:S(2)}) collective-permute-start(bf16[4096,256]{1,0:T(8,128)(2,1)} %bitcast.16), channel_id=1, source_target_pairs={{0,1},{1,0},{2,3},{3,2},{4,5},{5,4},{6,7},{7,6},{8,9},{9,8},{10,11... | collective-permute-start | bytes 6291464 | tf_op jit(solution)/shard_map/ppermute | solution.py:261
  20.4 11.9 %collective-permute-start.10 = (bf16[256,4096]{1,0:T(8,128)(2,1)}, bf16[256,4096]{1,0:T(8,128)(2,1)}, u32[]{:S(2)}, u32[]{:S(2)}) collective-permute-start(bf16[256,4096]{1,0:T(8,128)(2,1)} %bitcast.23), channel_id=1, source_target_pairs={{0,1},{1,0},{2,3},{3,2},{4,5},{5,4},{6,7},{7,6},{8,9},{9,8},{10,11... | collective-permute-start | bytes 6291464 | tf_op jit(solution)/shard_map/ppermute | solution.py:261
  32.3 6.6 %collective-permute-start.11 = (bf16[32,4096]{1,0:T(8,128)(2,1)}, bf16[32,4096]{1,0:T(8,128)(2,1)S(1)}, u32[]{:S(2)}, u32[]{:S(2)}) collective-permute-start(bf16[32,4096]{1,0:T(8,128)(2,1)} %get-tuple-element.55.refs_3_), channel_id=1, source_target_pairs={{0,4},{1,3},{4,8},{5,1},{8,12},{9,5},{12,14},{13,9},{14,10},{15,13... | collective-permute-start | bytes 786440 | tf_op jit(solution)/shard_map/ppermute | solution.py:272
  33.4 8.3 %collective-permute-start.13 = (bf16[32,4096]{1,0:T(8,128)(2,1)}, bf16[32,4096]{1,0:T(8,128)(2,1)S(1)}, u32[]{:S(2)}, u32[]{:S(2)}) collective-permute-start(bf16[32,4096]{1,0:T(8,128)(2,1)} %get-tuple-element.57.refs_4_), channel_id=1, source_target_pairs={{0,4},{1,3},{4,8},{5,1},{8,12},{9,5},{12,14},{13,9},{14,10},{15,13... | collective-permute-start | bytes 786440 | tf_op jit(solution)/shard_map/ppermute | solution.py:272
  38.9 13.6 %collective-permute-start.12 = (bf16[32,4096]{1,0:T(8,128)(2,1)S(1)}, bf16[32,4096]{1,0:T(8,128)(2,1)S(1)}, u32[]{:S(2)}, u32[]{:S(2)}) collective-permute-start(bf16[32,4096]{1,0:T(8,128)(2,1)S(1)} %collective-permute-done.11.refs_0_), channel_id=1, source_target_pairs={{0,4},{1,3},{4,8},{5,1},{8,12},{9,5},{12,14},{13,9},{14,10},{15,13... | collective-permute-start | bytes 786440 | tf_op jit(solution)/shard_map/ppermute | solution.py:272
  41.8 10.8 %collective-permute-start.14 = (bf16[32,4096]{1,0:T(8,128)(2,1)S(1)}, bf16[32,4096]{1,0:T(8,128)(2,1)S(1)}, u32[]{:S(2)}, u32[]{:S(2)}) collective-permute-start(bf16[32,4096]{1,0:T(8,128)(2,1)S(1)} %collective-permute-done.13.refs_1_), channel_id=1, source_target_pairs={{0,4},{1,3},{4,8},{5,1},{8,12},{9,5},{12,14},{13,9},{14,10},{15,13... | collective-permute-start | bytes 786440 | tf_op jit(solution)/shard_map/ppermute | solution.py:272
  43.2 12.3 %collective-permute-start.15 = (bf16[64,4096]{1,0:T(8,128)(2,1)}, bf16[64,4096]{1,0:T(8,128)(2,1)S(1)}, u32[]{:S(2)}, u32[]{:S(2)}) collective-permute-start(bf16[64,4096]{1,0:T(8,128)(2,1)} %get-tuple-element.59), channel_id=1, source_target_pairs={{4,0},{3,1},{8,4},{1,5},{12,8},{5,9},{14,12},{9,13},{10,14},{13,15... | collective-permute-start | bytes 1572872 | tf_op jit(solution)/shard_map/ppermute | solution.py:272
  48.6 14.5 %collective-permute-start.18 = (bf16[32,4096]{1,0:T(8,128)(2,1)S(1)}, bf16[32,4096]{1,0:T(8,128)(2,1)S(1)}, u32[]{:S(2)}, u32[]{:S(2)}) collective-permute-start(bf16[32,4096]{1,0:T(8,128)(2,1)S(1)} %convert_element_type.99), channel_id=1, source_target_pairs={{0,4},{1,3},{4,8},{5,1},{8,12},{9,5},{12,14},{13,9},{14,10},{15,13... | collective-permute-start | bytes 786440 | tf_op jit(solution)/shard_map/ppermute | solution.py:272
  50.5 10.2 %collective-permute-start.27 = (bf16[32,4096]{1,0:T(8,128)(2,1)S(1)}, bf16[32,4096]{1,0:T(8,128)(2,1)S(1)}, u32[]{:S(2)}, u32[]{:S(2)}) collective-permute-start(bf16[32,4096]{1,0:T(8,128)(2,1)S(1)} %convert_element_type.113), channel_id=1, source_target_pairs={{0,4},{1,3},{4,8},{5,1},{8,12},{9,5},{12,14},{13,9},{14,10},{15,13... | collective-permute-start | bytes 786440 | tf_op jit(solution)/shard_map/ppermute | solution.py:272
  52.6 12.4 %collective-permute-start.16 = (bf16[64,4096]{1,0:T(8,128)(2,1)S(1)}, bf16[64,4096]{1,0:T(8,128)(2,1)S(1)}, u32[]{:S(2)}, u32[]{:S(2)}) collective-permute-start(bf16[64,4096]{1,0:T(8,128)(2,1)S(1)} %pad_maximum_fusion), channel_id=1, source_target_pairs={{0,4},{1,3},{4,8},{5,1},{8,12},{9,5},{12,14},{13,9},{14,10},{15,13... | collective-permute-start | bytes 1572872 | tf_op jit(solution)/shard_map/ppermute | solution.py:272
  60.7 10.4 %collective-permute-start.28 = (bf16[32,4096]{1,0:T(8,128)(2,1)S(1)}, bf16[32,4096]{1,0:T(8,128)(2,1)S(1)}, u32[]{:S(2)}, u32[]{:S(2)}) collective-permute-start(bf16[32,4096]{1,0:T(8,128)(2,1)S(1)} %add_convert_fusion.5), channel_id=1, source_target_pairs={{0,4},{1,3},{4,8},{5,1},{8,12},{9,5},{12,14},{13,9},{14,10},{15,13... | collective-permute-start | bytes 786440 | tf_op jit(solution)/shard_map/ppermute | solution.py:272
  63.1 10.5 %collective-permute-start.20 = (bf16[32,4096]{1,0:T(8,128)(2,1)S(1)}, bf16[32,4096]{1,0:T(8,128)(2,1)S(1)}, u32[]{:S(2)}, u32[]{:S(2)}) collective-permute-start(bf16[32,4096]{1,0:T(8,128)(2,1)S(1)} %add_convert_fusion.11), channel_id=1, source_target_pairs={{0,4},{1,3},{4,8},{5,1},{8,12},{9,5},{12,14},{13,9},{14,10},{15,13... | collective-permute-start | bytes 786440 | tf_op jit(solution)/shard_map/ppermute | solution.py:272
  65.0 11.2 %collective-permute-start.17 = (bf16[64,4096]{1,0:T(8,128)(2,1)S(1)}, bf16[64,4096]{1,0:T(8,128)(2,1)S(1)}, u32[]{:S(2)}, u32[]{:S(2)}) collective-permute-start(bf16[64,4096]{1,0:T(8,128)(2,1)S(1)} %collective-permute-done.16.refs_0_), channel_id=1, source_target_pairs={{0,4},{1,3},{4,8},{5,1},{8,12},{9,5},{12,14},{13,9},{14,10},{15,13... | collective-permute-start | bytes 1572872 | tf_op jit(solution)/shard_map/ppermute | solution.py:272
  71.2 11.4 %collective-permute-start.29 = (bf16[32,4096]{1,0:T(8,128)(2,1)S(1)}, bf16[32,4096]{1,0:T(8,128)(2,1)S(1)}, u32[]{:S(2)}, u32[]{:S(2)}) collective-permute-start(bf16[32,4096]{1,0:T(8,128)(2,1)S(1)} %add_convert_fusion.4), channel_id=1, source_target_pairs={{0,4},{1,3},{4,8},{5,1},{8,12},{9,5},{12,14},{13,9},{14,10},{15,13... | collective-permute-start | bytes 786440 | tf_op jit(solution)/shard_map/ppermute | solution.py:272
  73.6 11.2 %collective-permute-start.22 = (bf16[32,4096]{1,0:T(8,128)(2,1)S(1)}, bf16[32,4096]{1,0:T(8,128)(2,1)S(1)}, u32[]{:S(2)}, u32[]{:S(2)}) collective-permute-start(bf16[32,4096]{1,0:T(8,128)(2,1)S(1)} %add_convert_fusion.10), channel_id=1, source_target_pairs={{0,4},{1,3},{4,8},{5,1},{8,12},{9,5},{12,14},{13,9},{14,10},{15,13... | collective-permute-start | bytes 786440 | tf_op jit(solution)/shard_map/ppermute | solution.py:272
  76.2 11.2 %collective-permute-start.19 = (bf16[64,4096]{1,0:T(8,128)(2,1)S(1)}, bf16[64,4096]{1,0:T(8,128)(2,1)S(1)}, u32[]{:S(2)}, u32[]{:S(2)}) collective-permute-start(bf16[64,4096]{1,0:T(8,128)(2,1)S(1)} %collective-permute-done.17.refs_0_), channel_id=1, source_target_pairs={{0,4},{1,3},{4,8},{5,1},{8,12},{9,5},{12,14},{13,9},{14,10},{15,13... | collective-permute-start | bytes 1572872 | tf_op jit(solution)/shard_map/ppermute | solution.py:272
  82.6 11.2 %collective-permute-start.30 = (bf16[32,4096]{1,0:T(8,128)(2,1)S(1)}, bf16[32,4096]{1,0:T(8,128)(2,1)S(1)}, u32[]{:S(2)}, u32[]{:S(2)}) collective-permute-start(bf16[32,4096]{1,0:T(8,128)(2,1)S(1)} %add_convert_fusion.3), channel_id=1, source_target_pairs={{0,4},{1,3},{4,8},{5,1},{8,12},{9,5},{12,14},{13,9},{14,10},{15,13... | collective-permute-start | bytes 786440 | tf_op jit(solution)/shard_map/ppermute | solution.py:272
  84.9 11.2 %collective-permute-start.23 = (bf16[32,4096]{1,0:T(8,128)(2,1)S(1)}, bf16[32,4096]{1,0:T(8,128)(2,1)S(1)}, u32[]{:S(2)}, u32[]{:S(2)}) collective-permute-start(bf16[32,4096]{1,0:T(8,128)(2,1)S(1)} %add_convert_fusion.9), channel_id=1, source_target_pairs={{0,4},{1,3},{4,8},{5,1},{8,12},{9,5},{12,14},{13,9},{14,10},{15,13... | collective-permute-start | bytes 786440 | tf_op jit(solution)/shard_map/ppermute | solution.py:272
  87.5 11.2 %collective-permute-start.21 = (bf16[64,4096]{1,0:T(8,128)(2,1)S(1)}, bf16[64,4096]{1,0:T(8,128)(2,1)S(1)}, u32[]{:S(2)}, u32[]{:S(2)}) collective-permute-start(bf16[64,4096]{1,0:T(8,128)(2,1)S(1)} %collective-permute-done.19.refs_0_), channel_id=1, source_target_pairs={{0,4},{1,3},{4,8},{5,1},{8,12},{9,5},{12,14},{13,9},{14,10},{15,13... | collective-permute-start | bytes 1572872 | tf_op jit(solution)/shard_map/ppermute | solution.py:272
  93.8 9.5 %collective-permute-start.31 = (bf16[32,4096]{1,0:T(8,128)(2,1)S(1)}, bf16[32,4096]{1,0:T(8,128)(2,1)S(1)}, u32[]{:S(2)}, u32[]{:S(2)}) collective-permute-start(bf16[32,4096]{1,0:T(8,128)(2,1)S(1)} %add_convert_fusion.2), channel_id=1, source_target_pairs={{0,4},{1,3},{4,8},{5,1},{8,12},{9,5},{12,14},{13,9},{14,10},{15,13... | collective-permute-start | bytes 786440 | tf_op jit(solution)/shard_map/ppermute | solution.py:272
  96.1 9.0 %collective-permute-start.24 = (bf16[32,4096]{1,0:T(8,128)(2,1)S(1)}, bf16[32,4096]{1,0:T(8,128)(2,1)S(1)}, u32[]{:S(2)}, u32[]{:S(2)}) collective-permute-start(bf16[32,4096]{1,0:T(8,128)(2,1)S(1)} %add_convert_fusion.8), channel_id=1, source_target_pairs={{0,4},{1,3},{4,8},{5,1},{8,12},{9,5},{12,14},{13,9},{14,10},{15,13... | collective-permute-start | bytes 786440 | tf_op jit(solution)/shard_map/ppermute | solution.py:272
  103.4 6.4 %collective-permute-start.32 = (bf16[32,4096]{1,0:T(8,128)(2,1)S(1)}, bf16[32,4096]{1,0:T(8,128)(2,1)S(1)}, u32[]{:S(2)}, u32[]{:S(2)}) collective-permute-start(bf16[32,4096]{1,0:T(8,128)(2,1)S(1)} %add_convert_fusion.1), channel_id=1, source_target_pairs={{0,4},{1,3},{4,8},{5,1},{8,12},{9,5},{12,14},{13,9},{14,10},{15,13... | collective-permute-start | bytes 786440 | tf_op jit(solution)/shard_map/ppermute | solution.py:272
  105.2 7.5 %collective-permute-start.25 = (bf16[32,4096]{1,0:T(8,128)(2,1)S(1)}, bf16[32,4096]{1,0:T(8,128)(2,1)S(1)}, u32[]{:S(2)}, u32[]{:S(2)}) collective-permute-start(bf16[32,4096]{1,0:T(8,128)(2,1)S(1)} %add_convert_fusion.7), channel_id=1, source_target_pairs={{0,4},{1,3},{4,8},{5,1},{8,12},{9,5},{12,14},{13,9},{14,10},{15,13... | collective-permute-start | bytes 786440 | tf_op jit(solution)/shard_map/ppermute | solution.py:272
  109.9 6.4 %collective-permute-start.33 = (bf16[32,4096]{1,0:T(8,128)(2,1)S(1)}, bf16[32,4096]{1,0:T(8,128)(2,1)S(1)}, u32[]{:S(2)}, u32[]{:S(2)}) collective-permute-start(bf16[32,4096]{1,0:T(8,128)(2,1)S(1)} %add_convert_fusion), channel_id=1, source_target_pairs={{0,4},{1,3},{4,8},{5,1},{8,12},{9,5},{12,14},{13,9},{14,10},{15,13... | collective-permute-start | bytes 786440 | tf_op jit(solution)/shard_map/ppermute | solution.py:272
  112.7 6.4 %collective-permute-start.26 = (bf16[32,4096]{1,0:T(8,128)(2,1)S(1)}, bf16[32,4096]{1,0:T(8,128)(2,1)S(1)}, u32[]{:S(2)}, u32[]{:S(2)}) collective-permute-start(bf16[32,4096]{1,0:T(8,128)(2,1)S(1)} %add_convert_fusion.6), channel_id=1, source_target_pairs={{0,4},{1,3},{4,8},{5,1},{8,12},{9,5},{12,14},{13,9},{14,10},{15,13... | collective-permute-start | bytes 786440 | tf_op jit(solution)/shard_map/ppermute | solution.py:272
  (11 other events, 125.0 us)

commit v17 on v16

--- a/solution.py
+++ b/solution.py
@@ -290,10 +290,12 @@
     for hop in range(1, chips):
         arrived = move(sums)
         here = hop + 1
-        if hop + 3 < chips - 1:
+        if hop + 3 < chips - 2:
             rows[hop + 3] = move(after(rows[hop + 2], sums[0]))
-        if here < chips - 1:
-            hops = (here, chips - 1, 0) if hop == 1 else (here,)
+        if hop == 3:
+            rows[chips - 2] = move(after(rows[chips - 1], sums[0]), back)
+        if here < chips - 2:
+            hops = {1: (2, chips - 1, 0), chips - 4: (here, here + 1)}.get(hop, (here,))
             parts.update(zip(hops, parts_of(rows, hops)))
         if here < chips:
             sums = rounded(added(parts[here], arrived))

time: 120 us -> 121 us (level)
  Pallas kernels: 40.1 us -> 35.1 us
  waiting for transfers between devices: 27.9 us -> 31 us
  starting transfers between devices: 47.3 us -> 49.8 us
    pallas_call x6 -> x5, Pallas kernels: 28.6 us -> 23.6 us  [expert_parts(): pl.pallas_call(functools.partial(expert_kernel, hops=hops, chips=chips),...]
    ppermute x23, waiting for transfers between devices: 21.3 us -> 24.4 us  [move(): return tuple((lax.ppermute(x, 'ctx', way) for x in blocks))]
    ppermute x23, starting transfers between devices: 35.2 us -> 37.7 us  [move(): return tuple((lax.ppermute(x, 'ctx', way) for x in blocks))]
  transfers between devices with their start and end apart: 34 -> 34, of which waited for: 17 -> 18; matrix products, arithmetic and copies ran while one was open for 1% -> 1% of each run, Pallas kernels for 33% -> 29%
where the time goes in v17:
time: 121 us
  starting transfers between devices  49.8 us (41%)
  Pallas kernels  35.1 us (29%)
  waiting for transfers between devices  31 us (26%)
  other arithmetic  4.11 us (3%)
    ppermute x23, starting transfers between devices, move(): return tuple((lax.ppermute(x, 'ctx', way) for x in blocks))  37.7 us
    ppermute x23, waiting for transfers between devices, move(): return tuple((lax.ppermute(x, 'ctx', way) for x in blocks))  24.4 us
    pallas_call x5, Pallas kernels, expert_parts(): pl.pallas_call(functools.partial(expert_kernel, hops=hops, chips=chips),...  23.6 us
    pallas_call x1, Pallas kernels, attention(): pl.pallas_call(functools.partial(attention_kernel, tok=tok), grid_spec=gr...  11.5 us
    ppermute x7, starting transfers between devices, from_chip(): lax.ppermute(block, 'ctx', [(i, i ^ step * CORES) for i in range(n_ctx)])  11.4 us
    ppermute x7, waiting for transfers between devices, from_chip(): lax.ppermute(block, 'ctx', [(i, i ^ step * CORES) for i in range(n_ctx)])  4.54 us
  transfers between devices with their start and end apart: 34, of which 18 were waited for; matrix products, arithmetic and copies ran while one was open for 1% of the time, Pallas kernels for 29%

profile of v17, /device:TPU:0, one launch (start us, length us, event | category | flops | bytes accessed | tf_op | source)
XLA Modules:
  0.0 120.7 jit_solution(14075510547698704812)
XLA Ops:
  1.7 4.1 %collective-permute-start.3 = (bf16[64,640]{1,0:T(8,128)(2,1)S(1)}, bf16[64,640]{1,0:T(8,128)(2,1)S(1)}, u32[]{:S(2)}, u32[]{:S(2)}) collective-permute-start(bf16[64,640]{1,0:T(8,128)(2,1)S(1)} %get-tuple-element.79), channel_id=1, source_target_pairs={{0,8},{1,9},{2,10},{3,11},{4,12},{5,13},{6,14},{7,15},{8,0},{9,1},... | collective-permute-start | bytes 245768 | tf_op jit(solution)/shard_map/ppermute | solution.py:250
  9.8 1.6 %collective-permute-start.4 = (bf16[64,640]{1,0:T(8,128)(2,1)S(1)}, bf16[64,640]{1,0:T(8,128)(2,1)S(1)}, u32[]{:S(2)}, u32[]{:S(2)}) collective-permute-start(bf16[64,640]{1,0:T(8,128)(2,1)S(1)} %collective-permute-done.3), channel_id=1, source_target_pairs={{0,2},{1,3},{2,0},{3,1},{4,6},{5,7},{6,4},{7,5},{8,10},{9,11},{10,... | collective-permute-start | bytes 245768 | tf_op jit(solution)/shard_map/ppermute | solution.py:250
  15.9 1.8 %collective-permute-done.6 = bf16[64,640]{1,0:T(8,128)(2,1)S(1)} collective-permute-done((bf16[64,640]{1,0:T(8,128)(2,1)S(1)}, bf16[64,640]{1,0:T(8,128)(2,1)S(1)}, u32[]{:S(2)}, u32[]{:S(2)}) %collective-permute-start.6) | collective-permute-done | bytes 81952 | tf_op jit(solution)/shard_map/ppermute | solution.py:250
  17.8 2.1 %collective-permute-done.7.other_ref = bf16[512,640]{1,0:T(8,128)(2,1)S(1)} collective-permute-done((bf16[512,640]{1,0:T(8,128)(2,1)S(1)}, bf16[512,640]{1,0:T(8,128)(2,1)S(1)}, u32[]{:S(2)}, u32[]{:S(2)}) %collective-permute-start.7) | collective-permute-done | bytes 655392 | tf_op jit(solution)/shard_map/ppermute | solution.py:258
  20.8 11.5 %shard_map.109 = (bf16[64,4096]{1,0:T(8,128)(2,1)}, bf16[64,4096]{1,0:T(8,128)(2,1)}, bf16[32,4096]{1,0:T(8,128)(2,1)}, bf16[32,4096]{1,0:T(8,128)(2,1)}, f32[64,8]{1,0:T(8,128)}) custom-call(s32[1]{0:T(128)} %bitcast.index_ref, bf16[64,16384]{1,0:T(8,128)(2,1)} %q_ref.1, bf16[64,2048]{1,0:T(8,128)(2,1)} %qr_ref.1, bf16[512,640]{1,0:T(8,128)(2,1)} %copy-done.6, ...), custom_call_target="tpu_custom_call" | custom-call | flops 4831838208 | bytes 8388608 | tf_op jit(solution)/shard_map/pallas_call | solution.py:151
  33.4 2.7 %collective-permute-start.13 = (bf16[32,4096]{1,0:T(8,128)(2,1)}, bf16[32,4096]{1,0:T(8,128)(2,1)S(1)}, u32[]{:S(2)}, u32[]{:S(2)}) collective-permute-start(bf16[32,4096]{1,0:T(8,128)(2,1)} %get-tuple-element.57.refs_4_), channel_id=1, source_target_pairs={{0,4},{1,3},{4,8},{5,1},{8,12},{9,5},{12,14},{13,9},{14,10},{15,13... | collective-permute-start | bytes 786440 | tf_op jit(solution)/shard_map/ppermute | solution.py:272
  36.9 2.0 %collective-permute-done.11.refs_0_ = bf16[32,4096]{1,0:T(8,128)(2,1)S(1)} collective-permute-done((bf16[32,4096]{1,0:T(8,128)(2,1)}, bf16[32,4096]{1,0:T(8,128)(2,1)S(1)}, u32[]{:S(2)}, u32[]{:S(2)}) %collective-permute-start.11) | collective-permute-done | bytes 262176 | tf_op jit(solution)/shard_map/ppermute | solution.py:272
  43.8 4.7 %shard_map.111 = (f32[32,4096]{1,0:T(8,128)S(1)}, f32[32,4096]{1,0:T(8,128)S(1)}) custom-call(s32[1]{0:T(128)} %bitcast.index_ref, bf16[4096,256]{1,0:T(8,128)(2,1)S(1)} %bitcast.10, bf16[4096,256]{1,0:T(8,128)(2,1)S(1)} %bitcast.16, bf16[256,4096]{1,0:T(8,128)(2,1)S(1)} %bitcast.22, f32[64,8]{1,0:T(8,128)S(1)} %compare_select_fusion.hits_hbm, ...), custom_call_target="tpu_custom_call" | custom-call | flops 805306368 | bytes 14680064 | tf_op jit(solution)/shard_map/pallas_call | solution.py:218
  48.6 1.9 %collective-permute-start.18 = (bf16[32,4096]{1,0:T(8,128)(2,1)S(1)}, bf16[32,4096]{1,0:T(8,128)(2,1)S(1)}, u32[]{:S(2)}, u32[]{:S(2)}) collective-permute-start(bf16[32,4096]{1,0:T(8,128)(2,1)S(1)} %convert_element_type.99), channel_id=1, source_target_pairs={{0,4},{1,3},{4,8},{5,1},{8,12},{9,5},{12,14},{13,9},{14,10},{15,13... | collective-permute-start | bytes 786440 | tf_op jit(solution)/shard_map/ppermute | solution.py:272
  50.5 2.0 %collective-permute-start.27 = (bf16[32,4096]{1,0:T(8,128)(2,1)S(1)}, bf16[32,4096]{1,0:T(8,128)(2,1)S(1)}, u32[]{:S(2)}, u32[]{:S(2)}) collective-permute-start(bf16[32,4096]{1,0:T(8,128)(2,1)S(1)} %convert_element_type.113), channel_id=1, source_target_pairs={{0,4},{1,3},{4,8},{5,1},{8,12},{9,5},{12,14},{13,9},{14,10},{15,13... | collective-permute-start | bytes 786440 | tf_op jit(solution)/shard_map/ppermute | solution.py:272
  53.6 1.8 %collective-permute-done.15.refs_2_ = bf16[64,4096]{1,0:T(8,128)(2,1)S(1)} collective-permute-done((bf16[64,4096]{1,0:T(8,128)(2,1)}, bf16[64,4096]{1,0:T(8,128)(2,1)S(1)}, u32[]{:S(2)}, u32[]{:S(2)}) %collective-permute-start.15) | collective-permute-done | bytes 524320 | tf_op jit(solution)/shard_map/ppermute | solution.py:272
  55.4 5.2 %shard_map.110 = (f32[32,4096]{1,0:T(8,128)S(1)}, f32[32,4096]{1,0:T(8,128)S(1)}, f32[32,4096]{1,0:T(8,128)S(1)}, f32[32,4096]{1,0:T(8,128)S(1)}, f32[32,4096]{1,0:T(8,128)S(1)}, /*index=5*/f32[32,4096]{1,0:T(8,128)S(1)}) custom-call(s32[1]{0:T(128)} %bitcast.index_ref, bf16[4096,256]{1,0:T(8,128)(2,1)S(1)} %bitcast.11, bf16[4096,256]{1,0:T(8,128)(2,1)S(1)} %bitcast.17, ...), custom_call_target="tpu_custom_call" | custom-call | flops 805306368 | bytes 14680064 | tf_op jit(solution)/shard_map/pallas_call | solution.py:218
  60.7 2.4 %collective-permute-start.28 = (bf16[32,4096]{1,0:T(8,128)(2,1)S(1)}, bf16[32,4096]{1,0:T(8,128)(2,1)S(1)}, u32[]{:S(2)}, u32[]{:S(2)}) collective-permute-start(bf16[32,4096]{1,0:T(8,128)(2,1)S(1)} %add_convert_fusion.5), channel_id=1, source_target_pairs={{0,4},{1,3},{4,8},{5,1},{8,12},{9,5},{12,14},{13,9},{14,10},{15,13... | collective-permute-start | bytes 786440 | tf_op jit(solution)/shard_map/ppermute | solution.py:272
  66.4 4.7 %shard_map.112 = (f32[32,4096]{1,0:T(8,128)S(1)}, f32[32,4096]{1,0:T(8,128)S(1)}) custom-call(s32[1]{0:T(128)} %bitcast.index_ref, bf16[4096,256]{1,0:T(8,128)(2,1)S(1)} %bitcast.12, bf16[4096,256]{1,0:T(8,128)(2,1)S(1)} %bitcast.18, bf16[256,4096]{1,0:T(8,128)(2,1)S(1)} %bitcast.24, f32[64,8]{1,0:T(8,128)S(1)} %compare_select_fusion.hits_hbm, ...), custom_call_target="tpu_custom_call" | custom-call | flops 805306368 | bytes 14680064 | tf_op jit(solution)/shard_map/pallas_call | solution.py:218
  71.1 2.4 %collective-permute-start.29 = (bf16[32,4096]{1,0:T(8,128)(2,1)S(1)}, bf16[32,4096]{1,0:T(8,128)(2,1)S(1)}, u32[]{:S(2)}, u32[]{:S(2)}) collective-permute-start(bf16[32,4096]{1,0:T(8,128)(2,1)S(1)} %add_convert_fusion.4), channel_id=1, source_target_pairs={{0,4},{1,3},{4,8},{5,1},{8,12},{9,5},{12,14},{13,9},{14,10},{15,13... | collective-permute-start | bytes 786440 | tf_op jit(solution)/shard_map/ppermute | solution.py:272
  74.0 1.7 %collective-permute-start.21 = (bf16[64,4096]{1,0:T(8,128)(2,1)S(1)}, bf16[64,4096]{1,0:T(8,128)(2,1)S(1)}, u32[]{:S(2)}, u32[]{:S(2)}) collective-permute-start(bf16[64,4096]{1,0:T(8,128)(2,1)S(1)} %collective-permute-done.15.refs_2_), channel_id=1, source_target_pairs={{4,0},{3,1},{8,4},{1,5},{12,8},{5,9},{14,12},{9,13},{10,14},{13,15... | collective-permute-start | bytes 1572872 | tf_op jit(solution)/shard_map/ppermute | solution.py:272
  75.7 2.5 %collective-permute-done.17.refs_0_ = bf16[64,4096]{1,0:T(8,128)(2,1)S(1)} collective-permute-done((bf16[64,4096]{1,0:T(8,128)(2,1)S(1)}, bf16[64,4096]{1,0:T(8,128)(2,1)S(1)}, u32[]{:S(2)}, u32[]{:S(2)}) %collective-permute-start.17) | collective-permute-done | bytes 524320 | tf_op jit(solution)/shard_map/ppermute | solution.py:272
  78.2 2.9 %collective-permute-start.19 = (bf16[64,4096]{1,0:T(8,128)(2,1)S(1)}, bf16[64,4096]{1,0:T(8,128)(2,1)S(1)}, u32[]{:S(2)}, u32[]{:S(2)}) collective-permute-start(bf16[64,4096]{1,0:T(8,128)(2,1)S(1)} %collective-permute-done.17.refs_0_), channel_id=1, source_target_pairs={{0,4},{1,3},{4,8},{5,1},{8,12},{9,5},{12,14},{13,9},{14,10},{15,13... | collective-permute-start | bytes 1572872 | tf_op jit(solution)/shard_map/ppermute | solution.py:272
  81.1 4.7 %shard_map.114 = (f32[32,4096]{1,0:T(8,128)S(1)}, f32[32,4096]{1,0:T(8,128)S(1)}) custom-call(s32[1]{0:T(128)} %bitcast.index_ref, bf16[4096,256]{1,0:T(8,128)(2,1)S(1)} %bitcast.13, bf16[4096,256]{1,0:T(8,128)(2,1)S(1)} %bitcast.19, bf16[256,4096]{1,0:T(8,128)(2,1)S(1)} %bitcast.25, f32[64,8]{1,0:T(8,128)S(1)} %compare_select_fusion.hits_hbm, ...), custom_call_target="tpu_custom_call" | custom-call | flops 805306368 | bytes 14680064 | tf_op jit(solution)/shard_map/pallas_call | solution.py:218
  85.9 2.5 %collective-permute-start.30 = (bf16[32,4096]{1,0:T(8,128)(2,1)S(1)}, bf16[32,4096]{1,0:T(8,128)(2,1)S(1)}, u32[]{:S(2)}, u32[]{:S(2)}) collective-permute-start(bf16[32,4096]{1,0:T(8,128)(2,1)S(1)} %add_convert_fusion.3), channel_id=1, source_target_pairs={{0,4},{1,3},{4,8},{5,1},{8,12},{9,5},{12,14},{13,9},{14,10},{15,13... | collective-permute-start | bytes 786440 | tf_op jit(solution)/shard_map/ppermute | solution.py:272
  89.2 3.9 %collective-permute-done.19.refs_0_ = bf16[64,4096]{1,0:T(8,128)(2,1)S(1)} collective-permute-done((bf16[64,4096]{1,0:T(8,128)(2,1)S(1)}, bf16[64,4096]{1,0:T(8,128)(2,1)S(1)}, u32[]{:S(2)}, u32[]{:S(2)}) %collective-permute-start.19) | collective-permute-done | bytes 524320 | tf_op jit(solution)/shard_map/ppermute | solution.py:272
  93.1 4.3 %shard_map.113 = (f32[32,4096]{1,0:T(8,128)S(1)}, f32[32,4096]{1,0:T(8,128)S(1)}, f32[32,4096]{1,0:T(8,128)S(1)}, f32[32,4096]{1,0:T(8,128)S(1)}) custom-call(s32[1]{0:T(128)} %bitcast.index_ref, bf16[4096,256]{1,0:T(8,128)(2,1)S(1)} %bitcast.14, bf16[4096,256]{1,0:T(8,128)(2,1)S(1)} %bitcast.20, bf16[256,4096]{1,0:T(8,128)(2,1)S(1)} %bitcast.26, ...), custom_call_target="tpu_custom_call" | custom-call | flops 805306368 | bytes 14680064 | tf_op jit(solution)/shard_map/pallas_call | solution.py:218
  97.5 1.7 %collective-permute-start.31 = (bf16[32,4096]{1,0:T(8,128)(2,1)S(1)}, bf16[32,4096]{1,0:T(8,128)(2,1)S(1)}, u32[]{:S(2)}, u32[]{:S(2)}) collective-permute-start(bf16[32,4096]{1,0:T(8,128)(2,1)S(1)} %add_convert_fusion.2), channel_id=1, source_target_pairs={{0,4},{1,3},{4,8},{5,1},{8,12},{9,5},{12,14},{13,9},{14,10},{15,13... | collective-permute-start | bytes 786440 | tf_op jit(solution)/shard_map/ppermute | solution.py:272
  99.2 2.2 %collective-permute-start.24 = (bf16[32,4096]{1,0:T(8,128)(2,1)S(1)}, bf16[32,4096]{1,0:T(8,128)(2,1)S(1)}, u32[]{:S(2)}, u32[]{:S(2)}) collective-permute-start(bf16[32,4096]{1,0:T(8,128)(2,1)S(1)} %add_convert_fusion.8), channel_id=1, source_target_pairs={{0,4},{1,3},{4,8},{5,1},{8,12},{9,5},{12,14},{13,9},{14,10},{15,13... | collective-permute-start | bytes 786440 | tf_op jit(solution)/shard_map/ppermute | solution.py:272
  101.4 2.5 %collective-permute-done.31 = bf16[32,4096]{1,0:T(8,128)(2,1)S(1)} collective-permute-done((bf16[32,4096]{1,0:T(8,128)(2,1)S(1)}, bf16[32,4096]{1,0:T(8,128)(2,1)S(1)}, u32[]{:S(2)}, u32[]{:S(2)}) %collective-permute-start.31) | collective-permute-done | bytes 262176 | tf_op jit(solution)/shard_map/ppermute | solution.py:272
  103.9 1.7 %collective-permute-start.32 = (bf16[32,4096]{1,0:T(8,128)(2,1)S(1)}, bf16[32,4096]{1,0:T(8,128)(2,1)S(1)}, u32[]{:S(2)}, u32[]{:S(2)}) collective-permute-start(bf16[32,4096]{1,0:T(8,128)(2,1)S(1)} %add_convert_fusion.1), channel_id=1, source_target_pairs={{0,4},{1,3},{4,8},{5,1},{8,12},{9,5},{12,14},{13,9},{14,10},{15,13... | collective-permute-start | bytes 786440 | tf_op jit(solution)/shard_map/ppermute | solution.py:272
  106.7 1.7 %collective-permute-start.25 = (bf16[32,4096]{1,0:T(8,128)(2,1)S(1)}, bf16[32,4096]{1,0:T(8,128)(2,1)S(1)}, u32[]{:S(2)}, u32[]{:S(2)}) collective-permute-start(bf16[32,4096]{1,0:T(8,128)(2,1)S(1)} %add_convert_fusion.7), channel_id=1, source_target_pairs={{0,4},{1,3},{4,8},{5,1},{8,12},{9,5},{12,14},{13,9},{14,10},{15,13... | collective-permute-start | bytes 786440 | tf_op jit(solution)/shard_map/ppermute | solution.py:272
  108.4 2.0 %collective-permute-done.32 = bf16[32,4096]{1,0:T(8,128)(2,1)S(1)} collective-permute-done((bf16[32,4096]{1,0:T(8,128)(2,1)S(1)}, bf16[32,4096]{1,0:T(8,128)(2,1)S(1)}, u32[]{:S(2)}, u32[]{:S(2)}) %collective-permute-start.32) | collective-permute-done | bytes 262176 | tf_op jit(solution)/shard_map/ppermute | solution.py:272
  110.4 1.7 %collective-permute-start.33 = (bf16[32,4096]{1,0:T(8,128)(2,1)S(1)}, bf16[32,4096]{1,0:T(8,128)(2,1)S(1)}, u32[]{:S(2)}, u32[]{:S(2)}) collective-permute-start(bf16[32,4096]{1,0:T(8,128)(2,1)S(1)} %add_convert_fusion), channel_id=1, source_target_pairs={{0,4},{1,3},{4,8},{5,1},{8,12},{9,5},{12,14},{13,9},{14,10},{15,13... | collective-permute-start | bytes 786440 | tf_op jit(solution)/shard_map/ppermute | solution.py:272
  113.2 1.7 %collective-permute-start.26 = (bf16[32,4096]{1,0:T(8,128)(2,1)S(1)}, bf16[32,4096]{1,0:T(8,128)(2,1)S(1)}, u32[]{:S(2)}, u32[]{:S(2)}) collective-permute-start(bf16[32,4096]{1,0:T(8,128)(2,1)S(1)} %add_convert_fusion.6), channel_id=1, source_target_pairs={{0,4},{1,3},{4,8},{5,1},{8,12},{9,5},{12,14},{13,9},{14,10},{15,13... | collective-permute-start | bytes 786440 | tf_op jit(solution)/shard_map/ppermute | solution.py:272
  114.9 2.0 %collective-permute-done.33 = bf16[32,4096]{1,0:T(8,128)(2,1)S(1)} collective-permute-done((bf16[32,4096]{1,0:T(8,128)(2,1)S(1)}, bf16[32,4096]{1,0:T(8,128)(2,1)S(1)}, u32[]{:S(2)}, u32[]{:S(2)}) %collective-permute-start.33) | collective-permute-done | bytes 262176 | tf_op jit(solution)/shard_map/ppermute | solution.py:272
  116.9 2.8 %collective-permute-done.26 = bf16[32,4096]{1,0:T(8,128)(2,1)S(1)} collective-permute-done((bf16[32,4096]{1,0:T(8,128)(2,1)S(1)}, bf16[32,4096]{1,0:T(8,128)(2,1)S(1)}, u32[]{:S(2)}, u32[]{:S(2)}) %collective-permute-start.26) | collective-permute-done | bytes 262176 | tf_op jit(solution)/shard_map/ppermute | solution.py:272
  (90 shorter events, 27.4 us)
Async XLA Ops:
  1.7 8.1 %collective-permute-start.3 = (bf16[64,640]{1,0:T(8,128)(2,1)S(1)}, bf16[64,640]{1,0:T(8,128)(2,1)S(1)}, u32[]{:S(2)}, u32[]{:S(2)}) collective-permute-start(bf16[64,640]{1,0:T(8,128)(2,1)S(1)} %get-tuple-element.79), channel_id=1, source_target_pairs={{0,8},{1,9},{2,10},{3,11},{4,12},{5,13},{6,14},{7,15},{8,0},{9,1},... | collective-permute-start | bytes 245768 | tf_op jit(solution)/shard_map/ppermute | solution.py:250
  5.8 6.6 %collective-permute-start = (bf16[64,640]{1,0:T(8,128)(2,1)S(1)}, bf16[64,640]{1,0:T(8,128)(2,1)S(1)}, u32[]{:S(2)}, u32[]{:S(2)}) collective-permute-start(bf16[64,640]{1,0:T(8,128)(2,1)S(1)} %get-tuple-element.79), channel_id=1, source_target_pairs={{0,2},{1,3},{2,0},{3,1},{4,6},{5,7},{6,4},{7,5},{8,10},{9,11},{10,... | collective-permute-start | bytes 245768 | tf_op jit(solution)/shard_map/ppermute | solution.py:250
  7.3 6.3 %collective-permute-start.1 = (bf16[64,640]{1,0:T(8,128)(2,1)S(1)}, bf16[64,640]{1,0:T(8,128)(2,1)S(1)}, u32[]{:S(2)}, u32[]{:S(2)}) collective-permute-start(bf16[64,640]{1,0:T(8,128)(2,1)S(1)} %get-tuple-element.79), channel_id=1, source_target_pairs={{0,4},{1,5},{2,6},{3,7},{4,0},{5,1},{6,2},{7,3},{8,12},{9,13},{10,... | collective-permute-start | bytes 245768 | tf_op jit(solution)/shard_map/ppermute | solution.py:250
  8.9 5.6 %collective-permute-start.2 = (bf16[64,640]{1,0:T(8,128)(2,1)S(1)}, bf16[64,640]{1,0:T(8,128)(2,1)S(1)}, u32[]{:S(2)}, u32[]{:S(2)}) collective-permute-start(bf16[64,640]{1,0:T(8,128)(2,1)S(1)} %get-tuple-element.79), channel_id=1, source_target_pairs={{0,6},{1,7},{2,4},{3,5},{4,2},{5,3},{6,0},{7,1},{8,14},{9,15},{10,... | collective-permute-start | bytes 245768 | tf_op jit(solution)/shard_map/ppermute | solution.py:250
  9.8 5.5 %collective-permute-start.4 = (bf16[64,640]{1,0:T(8,128)(2,1)S(1)}, bf16[64,640]{1,0:T(8,128)(2,1)S(1)}, u32[]{:S(2)}, u32[]{:S(2)}) collective-permute-start(bf16[64,640]{1,0:T(8,128)(2,1)S(1)} %collective-permute-done.3), channel_id=1, source_target_pairs={{0,2},{1,3},{2,0},{3,1},{4,6},{5,7},{6,4},{7,5},{8,10},{9,11},{10,... | collective-permute-start | bytes 245768 | tf_op jit(solution)/shard_map/ppermute | solution.py:250
  12.4 5.3 %collective-permute-start.6 = (bf16[64,640]{1,0:T(8,128)(2,1)S(1)}, bf16[64,640]{1,0:T(8,128)(2,1)S(1)}, u32[]{:S(2)}, u32[]{:S(2)}) collective-permute-start(bf16[64,640]{1,0:T(8,128)(2,1)S(1)} %collective-permute-done.3), channel_id=1, source_target_pairs={{0,6},{1,7},{2,4},{3,5},{4,2},{5,3},{6,0},{7,1},{8,14},{9,15},{10,... | collective-permute-start | bytes 245768 | tf_op jit(solution)/shard_map/ppermute | solution.py:250
  19.9 12.4 %collective-permute-start.8 = (bf16[4096,256]{1,0:T(8,128)(2,1)}, bf16[4096,256]{1,0:T(8,128)(2,1)}, u32[]{:S(2)}, u32[]{:S(2)}) collective-permute-start(bf16[4096,256]{1,0:T(8,128)(2,1)} %bitcast.9), channel_id=1, source_target_pairs={{0,1},{1,0},{2,3},{3,2},{4,5},{5,4},{6,7},{7,6},{8,9},{9,8},{10,11... | collective-permute-start | bytes 6291464 | tf_op jit(solution)/shard_map/ppermute | solution.py:261
  20.0 12.3 %collective-permute-start.9 = (bf16[4096,256]{1,0:T(8,128)(2,1)}, bf16[4096,256]{1,0:T(8,128)(2,1)}, u32[]{:S(2)}, u32[]{:S(2)}) collective-permute-start(bf16[4096,256]{1,0:T(8,128)(2,1)} %bitcast.15), channel_id=1, source_target_pairs={{0,1},{1,0},{2,3},{3,2},{4,5},{5,4},{6,7},{7,6},{8,9},{9,8},{10,11... | collective-permute-start | bytes 6291464 | tf_op jit(solution)/shard_map/ppermute | solution.py:261
  20.4 11.9 %collective-permute-start.10 = (bf16[256,4096]{1,0:T(8,128)(2,1)}, bf16[256,4096]{1,0:T(8,128)(2,1)}, u32[]{:S(2)}, u32[]{:S(2)}) collective-permute-start(bf16[256,4096]{1,0:T(8,128)(2,1)} %bitcast.21), channel_id=1, source_target_pairs={{0,1},{1,0},{2,3},{3,2},{4,5},{5,4},{6,7},{7,6},{8,9},{9,8},{10,11... | collective-permute-start | bytes 6291464 | tf_op jit(solution)/shard_map/ppermute | solution.py:261
  32.3 6.6 %collective-permute-start.11 = (bf16[32,4096]{1,0:T(8,128)(2,1)}, bf16[32,4096]{1,0:T(8,128)(2,1)S(1)}, u32[]{:S(2)}, u32[]{:S(2)}) collective-permute-start(bf16[32,4096]{1,0:T(8,128)(2,1)} %get-tuple-element.55.refs_3_), channel_id=1, source_target_pairs={{0,4},{1,3},{4,8},{5,1},{8,12},{9,5},{12,14},{13,9},{14,10},{15,13... | collective-permute-start | bytes 786440 | tf_op jit(solution)/shard_map/ppermute | solution.py:272
  33.4 8.3 %collective-permute-start.13 = (bf16[32,4096]{1,0:T(8,128)(2,1)}, bf16[32,4096]{1,0:T(8,128)(2,1)S(1)}, u32[]{:S(2)}, u32[]{:S(2)}) collective-permute-start(bf16[32,4096]{1,0:T(8,128)(2,1)} %get-tuple-element.57.refs_4_), channel_id=1, source_target_pairs={{0,4},{1,3},{4,8},{5,1},{8,12},{9,5},{12,14},{13,9},{14,10},{15,13... | collective-permute-start | bytes 786440 | tf_op jit(solution)/shard_map/ppermute | solution.py:272
  38.9 13.6 %collective-permute-start.12 = (bf16[32,4096]{1,0:T(8,128)(2,1)S(1)}, bf16[32,4096]{1,0:T(8,128)(2,1)S(1)}, u32[]{:S(2)}, u32[]{:S(2)}) collective-permute-start(bf16[32,4096]{1,0:T(8,128)(2,1)S(1)} %collective-permute-done.11.refs_0_), channel_id=1, source_target_pairs={{0,4},{1,3},{4,8},{5,1},{8,12},{9,5},{12,14},{13,9},{14,10},{15,13... | collective-permute-start | bytes 786440 | tf_op jit(solution)/shard_map/ppermute | solution.py:272
  41.7 10.8 %collective-permute-start.14 = (bf16[32,4096]{1,0:T(8,128)(2,1)S(1)}, bf16[32,4096]{1,0:T(8,128)(2,1)S(1)}, u32[]{:S(2)}, u32[]{:S(2)}) collective-permute-start(bf16[32,4096]{1,0:T(8,128)(2,1)S(1)} %collective-permute-done.13.refs_1_), channel_id=1, source_target_pairs={{0,4},{1,3},{4,8},{5,1},{8,12},{9,5},{12,14},{13,9},{14,10},{15,13... | collective-permute-start | bytes 786440 | tf_op jit(solution)/shard_map/ppermute | solution.py:272
  43.2 12.2 %collective-permute-start.15 = (bf16[64,4096]{1,0:T(8,128)(2,1)}, bf16[64,4096]{1,0:T(8,128)(2,1)S(1)}, u32[]{:S(2)}, u32[]{:S(2)}) collective-permute-start(bf16[64,4096]{1,0:T(8,128)(2,1)} %get-tuple-element.59), channel_id=1, source_target_pairs={{4,0},{3,1},{8,4},{1,5},{12,8},{5,9},{14,12},{9,13},{10,14},{13,15... | collective-permute-start | bytes 1572872 | tf_op jit(solution)/shard_map/ppermute | solution.py:272
  48.6 14.4 %collective-permute-start.18 = (bf16[32,4096]{1,0:T(8,128)(2,1)S(1)}, bf16[32,4096]{1,0:T(8,128)(2,1)S(1)}, u32[]{:S(2)}, u32[]{:S(2)}) collective-permute-start(bf16[32,4096]{1,0:T(8,128)(2,1)S(1)} %convert_element_type.99), channel_id=1, source_target_pairs={{0,4},{1,3},{4,8},{5,1},{8,12},{9,5},{12,14},{13,9},{14,10},{15,13... | collective-permute-start | bytes 786440 | tf_op jit(solution)/shard_map/ppermute | solution.py:272
  50.5 10.1 %collective-permute-start.27 = (bf16[32,4096]{1,0:T(8,128)(2,1)S(1)}, bf16[32,4096]{1,0:T(8,128)(2,1)S(1)}, u32[]{:S(2)}, u32[]{:S(2)}) collective-permute-start(bf16[32,4096]{1,0:T(8,128)(2,1)S(1)} %convert_element_type.113), channel_id=1, source_target_pairs={{0,4},{1,3},{4,8},{5,1},{8,12},{9,5},{12,14},{13,9},{14,10},{15,13... | collective-permute-start | bytes 786440 | tf_op jit(solution)/shard_map/ppermute | solution.py:272
  52.5 12.4 %collective-permute-start.16 = (bf16[64,4096]{1,0:T(8,128)(2,1)S(1)}, bf16[64,4096]{1,0:T(8,128)(2,1)S(1)}, u32[]{:S(2)}, u32[]{:S(2)}) collective-permute-start(bf16[64,4096]{1,0:T(8,128)(2,1)S(1)} %pad_maximum_fusion), channel_id=1, source_target_pairs={{0,4},{1,3},{4,8},{5,1},{8,12},{9,5},{12,14},{13,9},{14,10},{15,13... | collective-permute-start | bytes 1572872 | tf_op jit(solution)/shard_map/ppermute | solution.py:272
  60.7 10.4 %collective-permute-start.28 = (bf16[32,4096]{1,0:T(8,128)(2,1)S(1)}, bf16[32,4096]{1,0:T(8,128)(2,1)S(1)}, u32[]{:S(2)}, u32[]{:S(2)}) collective-permute-start(bf16[32,4096]{1,0:T(8,128)(2,1)S(1)} %add_convert_fusion.5), channel_id=1, source_target_pairs={{0,4},{1,3},{4,8},{5,1},{8,12},{9,5},{12,14},{13,9},{14,10},{15,13... | collective-permute-start | bytes 786440 | tf_op jit(solution)/shard_map/ppermute | solution.py:272
  63.1 10.5 %collective-permute-start.20 = (bf16[32,4096]{1,0:T(8,128)(2,1)S(1)}, bf16[32,4096]{1,0:T(8,128)(2,1)S(1)}, u32[]{:S(2)}, u32[]{:S(2)}) collective-permute-start(bf16[32,4096]{1,0:T(8,128)(2,1)S(1)} %add_convert_fusion.11), channel_id=1, source_target_pairs={{0,4},{1,3},{4,8},{5,1},{8,12},{9,5},{12,14},{13,9},{14,10},{15,13... | collective-permute-start | bytes 786440 | tf_op jit(solution)/shard_map/ppermute | solution.py:272
  65.0 13.2 %collective-permute-start.17 = (bf16[64,4096]{1,0:T(8,128)(2,1)S(1)}, bf16[64,4096]{1,0:T(8,128)(2,1)S(1)}, u32[]{:S(2)}, u32[]{:S(2)}) collective-permute-start(bf16[64,4096]{1,0:T(8,128)(2,1)S(1)} %collective-permute-done.16.refs_0_), channel_id=1, source_target_pairs={{0,4},{1,3},{4,8},{5,1},{8,12},{9,5},{12,14},{13,9},{14,10},{15,13... | collective-permute-start | bytes 1572872 | tf_op jit(solution)/shard_map/ppermute | solution.py:272
  71.1 14.6 %collective-permute-start.29 = (bf16[32,4096]{1,0:T(8,128)(2,1)S(1)}, bf16[32,4096]{1,0:T(8,128)(2,1)S(1)}, u32[]{:S(2)}, u32[]{:S(2)}) collective-permute-start(bf16[32,4096]{1,0:T(8,128)(2,1)S(1)} %add_convert_fusion.4), channel_id=1, source_target_pairs={{0,4},{1,3},{4,8},{5,1},{8,12},{9,5},{12,14},{13,9},{14,10},{15,13... | collective-permute-start | bytes 786440 | tf_op jit(solution)/shard_map/ppermute | solution.py:272
  73.6 14.8 %collective-permute-start.22 = (bf16[32,4096]{1,0:T(8,128)(2,1)S(1)}, bf16[32,4096]{1,0:T(8,128)(2,1)S(1)}, u32[]{:S(2)}, u32[]{:S(2)}) collective-permute-start(bf16[32,4096]{1,0:T(8,128)(2,1)S(1)} %add_convert_fusion.10), channel_id=1, source_target_pairs={{0,4},{1,3},{4,8},{5,1},{8,12},{9,5},{12,14},{13,9},{14,10},{15,13... | collective-permute-start | bytes 786440 | tf_op jit(solution)/shard_map/ppermute | solution.py:272
  74.0 15.1 %collective-permute-start.21 = (bf16[64,4096]{1,0:T(8,128)(2,1)S(1)}, bf16[64,4096]{1,0:T(8,128)(2,1)S(1)}, u32[]{:S(2)}, u32[]{:S(2)}) collective-permute-start(bf16[64,4096]{1,0:T(8,128)(2,1)S(1)} %collective-permute-done.15.refs_2_), channel_id=1, source_target_pairs={{4,0},{3,1},{8,4},{1,5},{12,8},{5,9},{14,12},{9,13},{10,14},{13,15... | collective-permute-start | bytes 1572872 | tf_op jit(solution)/shard_map/ppermute | solution.py:272
  78.2 14.9 %collective-permute-start.19 = (bf16[64,4096]{1,0:T(8,128)(2,1)S(1)}, bf16[64,4096]{1,0:T(8,128)(2,1)S(1)}, u32[]{:S(2)}, u32[]{:S(2)}) collective-permute-start(bf16[64,4096]{1,0:T(8,128)(2,1)S(1)} %collective-permute-done.17.refs_0_), channel_id=1, source_target_pairs={{0,4},{1,3},{4,8},{5,1},{8,12},{9,5},{12,14},{13,9},{14,10},{15,13... | collective-permute-start | bytes 1572872 | tf_op jit(solution)/shard_map/ppermute | solution.py:272
  85.9 11.5 %collective-permute-start.30 = (bf16[32,4096]{1,0:T(8,128)(2,1)S(1)}, bf16[32,4096]{1,0:T(8,128)(2,1)S(1)}, u32[]{:S(2)}, u32[]{:S(2)}) collective-permute-start(bf16[32,4096]{1,0:T(8,128)(2,1)S(1)} %add_convert_fusion.3), channel_id=1, source_target_pairs={{0,4},{1,3},{4,8},{5,1},{8,12},{9,5},{12,14},{13,9},{14,10},{15,13... | collective-permute-start | bytes 786440 | tf_op jit(solution)/shard_map/ppermute | solution.py:272
  88.4 10.7 %collective-permute-start.23 = (bf16[32,4096]{1,0:T(8,128)(2,1)S(1)}, bf16[32,4096]{1,0:T(8,128)(2,1)S(1)}, u32[]{:S(2)}, u32[]{:S(2)}) collective-permute-start(bf16[32,4096]{1,0:T(8,128)(2,1)S(1)} %add_convert_fusion.9), channel_id=1, source_target_pairs={{0,4},{1,3},{4,8},{5,1},{8,12},{9,5},{12,14},{13,9},{14,10},{15,13... | collective-permute-start | bytes 786440 | tf_op jit(solution)/shard_map/ppermute | solution.py:272
  97.5 6.4 %collective-permute-start.31 = (bf16[32,4096]{1,0:T(8,128)(2,1)S(1)}, bf16[32,4096]{1,0:T(8,128)(2,1)S(1)}, u32[]{:S(2)}, u32[]{:S(2)}) collective-permute-start(bf16[32,4096]{1,0:T(8,128)(2,1)S(1)} %add_convert_fusion.2), channel_id=1, source_target_pairs={{0,4},{1,3},{4,8},{5,1},{8,12},{9,5},{12,14},{13,9},{14,10},{15,13... | collective-permute-start | bytes 786440 | tf_op jit(solution)/shard_map/ppermute | solution.py:272
  99.2 7.5 %collective-permute-start.24 = (bf16[32,4096]{1,0:T(8,128)(2,1)S(1)}, bf16[32,4096]{1,0:T(8,128)(2,1)S(1)}, u32[]{:S(2)}, u32[]{:S(2)}) collective-permute-start(bf16[32,4096]{1,0:T(8,128)(2,1)S(1)} %add_convert_fusion.8), channel_id=1, source_target_pairs={{0,4},{1,3},{4,8},{5,1},{8,12},{9,5},{12,14},{13,9},{14,10},{15,13... | collective-permute-start | bytes 786440 | tf_op jit(solution)/shard_map/ppermute | solution.py:272
  103.9 6.4 %collective-permute-start.32 = (bf16[32,4096]{1,0:T(8,128)(2,1)S(1)}, bf16[32,4096]{1,0:T(8,128)(2,1)S(1)}, u32[]{:S(2)}, u32[]{:S(2)}) collective-permute-start(bf16[32,4096]{1,0:T(8,128)(2,1)S(1)} %add_convert_fusion.1), channel_id=1, source_target_pairs={{0,4},{1,3},{4,8},{5,1},{8,12},{9,5},{12,14},{13,9},{14,10},{15,13... | collective-permute-start | bytes 786440 | tf_op jit(solution)/shard_map/ppermute | solution.py:272
  106.7 6.4 %collective-permute-start.25 = (bf16[32,4096]{1,0:T(8,128)(2,1)S(1)}, bf16[32,4096]{1,0:T(8,128)(2,1)S(1)}, u32[]{:S(2)}, u32[]{:S(2)}) collective-permute-start(bf16[32,4096]{1,0:T(8,128)(2,1)S(1)} %add_convert_fusion.7), channel_id=1, source_target_pairs={{0,4},{1,3},{4,8},{5,1},{8,12},{9,5},{12,14},{13,9},{14,10},{15,13... | collective-permute-start | bytes 786440 | tf_op jit(solution)/shard_map/ppermute | solution.py:272
  110.4 6.4 %collective-permute-start.33 = (bf16[32,4096]{1,0:T(8,128)(2,1)S(1)}, bf16[32,4096]{1,0:T(8,128)(2,1)S(1)}, u32[]{:S(2)}, u32[]{:S(2)}) collective-permute-start(bf16[32,4096]{1,0:T(8,128)(2,1)S(1)} %add_convert_fusion), channel_id=1, source_target_pairs={{0,4},{1,3},{4,8},{5,1},{8,12},{9,5},{12,14},{13,9},{14,10},{15,13... | collective-permute-start | bytes 786440 | tf_op jit(solution)/shard_map/ppermute | solution.py:272
  113.2 6.4 %collective-permute-start.26 = (bf16[32,4096]{1,0:T(8,128)(2,1)S(1)}, bf16[32,4096]{1,0:T(8,128)(2,1)S(1)}, u32[]{:S(2)}, u32[]{:S(2)}) collective-permute-start(bf16[32,4096]{1,0:T(8,128)(2,1)S(1)} %add_convert_fusion.6), channel_id=1, source_target_pairs={{0,4},{1,3},{4,8},{5,1},{8,12},{9,5},{12,14},{13,9},{14,10},{15,13... | collective-permute-start | bytes 786440 | tf_op jit(solution)/shard_map/ppermute | solution.py:272
  (11 other events, 125.0 us)

commit v18 on v16

--- a/solution.py
+++ b/solution.py
@@ -290,8 +290,10 @@
     for hop in range(1, chips):
         arrived = move(sums)
         here = hop + 1
-        if hop + 3 < chips - 1:
+        if hop + 3 < chips - 2:
             rows[hop + 3] = move(after(rows[hop + 2], sums[0]))
+        if hop == chips - 4:
+            rows[chips - 2] = move(after(rows[chips - 1], sums[0]), back)
         if here < chips - 1:
             hops = (here, chips - 1, 0) if hop == 1 else (here,)
             parts.update(zip(hops, parts_of(rows, hops)))

time: 120 us -> 122 us (1.017)
  waiting for transfers between devices: 27.9 us -> 29.3 us
    ppermute x23, waiting for transfers between devices: 21.3 us -> 22.6 us  [move(): return tuple((lax.ppermute(x, 'ctx', way) for x in blocks))]
  transfers between devices with their start and end apart: 34 -> 34, of which waited for: 17 -> 18; matrix products, arithmetic and copies ran while one was open for 1% -> 1% of each run, Pallas kernels for 33% -> 33%
where the time goes in v18:
time: 122 us
  starting transfers between devices  47.9 us (39%)
  Pallas kernels  40.1 us (33%)
  waiting for transfers between devices  29.3 us (24%)
  other arithmetic  4.12 us (3%)
    ppermute x23, starting transfers between devices, move(): return tuple((lax.ppermute(x, 'ctx', way) for x in blocks))  35.8 us
    pallas_call x6, Pallas kernels, expert_parts(): pl.pallas_call(functools.partial(expert_kernel, hops=hops, chips=chips),...  28.6 us
    ppermute x23, waiting for transfers between devices, move(): return tuple((lax.ppermute(x, 'ctx', way) for x in blocks))  22.6 us
    pallas_call x1, Pallas kernels, attention(): pl.pallas_call(functools.partial(attention_kernel, tok=tok), grid_spec=gr...  11.5 us
    ppermute x7, starting transfers between devices, from_chip(): lax.ppermute(block, 'ctx', [(i, i ^ step * CORES) for i in range(n_ctx)])  11.4 us
    ppermute x7, waiting for transfers between devices, from_chip(): lax.ppermute(block, 'ctx', [(i, i ^ step * CORES) for i in range(n_ctx)])  4.54 us
  transfers between devices with their start and end apart: 34, of which 18 were waited for; matrix products, arithmetic and copies ran while one was open for 1% of the time, Pallas kernels for 33%

profile of v18, /device:TPU:0, one launch (start us, length us, event | category | flops | bytes accessed | tf_op | source)
XLA Modules:
  0.0 122.1 jit_solution(16753203415316908661)
XLA Ops:
  1.7 4.1 %collective-permute-start.3 = (bf16[64,640]{1,0:T(8,128)(2,1)S(1)}, bf16[64,640]{1,0:T(8,128)(2,1)S(1)}, u32[]{:S(2)}, u32[]{:S(2)}) collective-permute-start(bf16[64,640]{1,0:T(8,128)(2,1)S(1)} %get-tuple-element.79), channel_id=1, source_target_pairs={{0,8},{1,9},{2,10},{3,11},{4,12},{5,13},{6,14},{7,15},{8,0},{9,1},... | collective-permute-start | bytes 245768 | tf_op jit(solution)/shard_map/ppermute | solution.py:250
  7.3 1.6 %collective-permute-start.1 = (bf16[64,640]{1,0:T(8,128)(2,1)S(1)}, bf16[64,640]{1,0:T(8,128)(2,1)S(1)}, u32[]{:S(2)}, u32[]{:S(2)}) collective-permute-start(bf16[64,640]{1,0:T(8,128)(2,1)S(1)} %get-tuple-element.79), channel_id=1, source_target_pairs={{0,4},{1,5},{2,6},{3,7},{4,0},{5,1},{6,2},{7,3},{8,12},{9,13},{10,... | collective-permute-start | bytes 245768 | tf_op jit(solution)/shard_map/ppermute | solution.py:250
  9.8 1.6 %collective-permute-start.4 = (bf16[64,640]{1,0:T(8,128)(2,1)S(1)}, bf16[64,640]{1,0:T(8,128)(2,1)S(1)}, u32[]{:S(2)}, u32[]{:S(2)}) collective-permute-start(bf16[64,640]{1,0:T(8,128)(2,1)S(1)} %collective-permute-done.3), channel_id=1, source_target_pairs={{0,2},{1,3},{2,0},{3,1},{4,6},{5,7},{6,4},{7,5},{8,10},{9,11},{10,... | collective-permute-start | bytes 245768 | tf_op jit(solution)/shard_map/ppermute | solution.py:250
  15.9 1.8 %collective-permute-done.6 = bf16[64,640]{1,0:T(8,128)(2,1)S(1)} collective-permute-done((bf16[64,640]{1,0:T(8,128)(2,1)S(1)}, bf16[64,640]{1,0:T(8,128)(2,1)S(1)}, u32[]{:S(2)}, u32[]{:S(2)}) %collective-permute-start.6) | collective-permute-done | bytes 81952 | tf_op jit(solution)/shard_map/ppermute | solution.py:250
  17.8 2.1 %collective-permute-done.7.other_ref = bf16[512,640]{1,0:T(8,128)(2,1)S(1)} collective-permute-done((bf16[512,640]{1,0:T(8,128)(2,1)S(1)}, bf16[512,640]{1,0:T(8,128)(2,1)S(1)}, u32[]{:S(2)}, u32[]{:S(2)}) %collective-permute-start.7) | collective-permute-done | bytes 655392 | tf_op jit(solution)/shard_map/ppermute | solution.py:258
  20.8 11.5 %shard_map.109 = (bf16[64,4096]{1,0:T(8,128)(2,1)}, bf16[64,4096]{1,0:T(8,128)(2,1)}, bf16[32,4096]{1,0:T(8,128)(2,1)}, bf16[32,4096]{1,0:T(8,128)(2,1)}, f32[64,8]{1,0:T(8,128)}) custom-call(s32[1]{0:T(128)} %bitcast.index_ref, bf16[64,16384]{1,0:T(8,128)(2,1)} %q_ref.1, bf16[64,2048]{1,0:T(8,128)(2,1)} %qr_ref.1, bf16[512,640]{1,0:T(8,128)(2,1)} %copy-done.6, ...), custom_call_target="tpu_custom_call" | custom-call | flops 4831838208 | bytes 8388608 | tf_op jit(solution)/shard_map/pallas_call | solution.py:151
  33.4 2.7 %collective-permute-start.13 = (bf16[32,4096]{1,0:T(8,128)(2,1)}, bf16[32,4096]{1,0:T(8,128)(2,1)S(1)}, u32[]{:S(2)}, u32[]{:S(2)}) collective-permute-start(bf16[32,4096]{1,0:T(8,128)(2,1)} %get-tuple-element.57.refs_4_), channel_id=1, source_target_pairs={{0,4},{1,3},{4,8},{5,1},{8,12},{9,5},{12,14},{13,9},{14,10},{15,13... | collective-permute-start | bytes 786440 | tf_op jit(solution)/shard_map/ppermute | solution.py:272
  36.9 2.0 %collective-permute-done.11.refs_0_ = bf16[32,4096]{1,0:T(8,128)(2,1)S(1)} collective-permute-done((bf16[32,4096]{1,0:T(8,128)(2,1)}, bf16[32,4096]{1,0:T(8,128)(2,1)S(1)}, u32[]{:S(2)}, u32[]{:S(2)}) %collective-permute-start.11) | collective-permute-done | bytes 262176 | tf_op jit(solution)/shard_map/ppermute | solution.py:272
  43.8 4.7 %shard_map.111 = (f32[32,4096]{1,0:T(8,128)S(1)}, f32[32,4096]{1,0:T(8,128)S(1)}) custom-call(s32[1]{0:T(128)} %bitcast.index_ref, bf16[4096,256]{1,0:T(8,128)(2,1)S(1)} %bitcast.10, bf16[4096,256]{1,0:T(8,128)(2,1)S(1)} %bitcast.17, bf16[256,4096]{1,0:T(8,128)(2,1)S(1)} %bitcast.24, f32[64,8]{1,0:T(8,128)S(1)} %compare_select_fusion.hits_hbm, ...), custom_call_target="tpu_custom_call" | custom-call | flops 805306368 | bytes 14680064 | tf_op jit(solution)/shard_map/pallas_call | solution.py:218
  48.6 1.9 %collective-permute-start.18 = (bf16[32,4096]{1,0:T(8,128)(2,1)S(1)}, bf16[32,4096]{1,0:T(8,128)(2,1)S(1)}, u32[]{:S(2)}, u32[]{:S(2)}) collective-permute-start(bf16[32,4096]{1,0:T(8,128)(2,1)S(1)} %convert_element_type.99), channel_id=1, source_target_pairs={{0,4},{1,3},{4,8},{5,1},{8,12},{9,5},{12,14},{13,9},{14,10},{15,13... | collective-permute-start | bytes 786440 | tf_op jit(solution)/shard_map/ppermute | solution.py:272
  50.5 2.0 %collective-permute-start.27 = (bf16[32,4096]{1,0:T(8,128)(2,1)S(1)}, bf16[32,4096]{1,0:T(8,128)(2,1)S(1)}, u32[]{:S(2)}, u32[]{:S(2)}) collective-permute-start(bf16[32,4096]{1,0:T(8,128)(2,1)S(1)} %convert_element_type.113), channel_id=1, source_target_pairs={{0,4},{1,3},{4,8},{5,1},{8,12},{9,5},{12,14},{13,9},{14,10},{15,13... | collective-permute-start | bytes 786440 | tf_op jit(solution)/shard_map/ppermute | solution.py:272
  53.7 1.8 %collective-permute-done.15.refs_2_ = bf16[64,4096]{1,0:T(8,128)(2,1)S(1)} collective-permute-done((bf16[64,4096]{1,0:T(8,128)(2,1)}, bf16[64,4096]{1,0:T(8,128)(2,1)S(1)}, u32[]{:S(2)}, u32[]{:S(2)}) %collective-permute-start.15) | collective-permute-done | bytes 524320 | tf_op jit(solution)/shard_map/ppermute | solution.py:272
  55.5 5.2 %shard_map.110 = (f32[32,4096]{1,0:T(8,128)S(1)}, f32[32,4096]{1,0:T(8,128)S(1)}, f32[32,4096]{1,0:T(8,128)S(1)}, f32[32,4096]{1,0:T(8,128)S(1)}, f32[32,4096]{1,0:T(8,128)S(1)}, /*index=5*/f32[32,4096]{1,0:T(8,128)S(1)}) custom-call(s32[1]{0:T(128)} %bitcast.index_ref, bf16[4096,256]{1,0:T(8,128)(2,1)S(1)} %bitcast.11, bf16[4096,256]{1,0:T(8,128)(2,1)S(1)} %bitcast.18, ...), custom_call_target="tpu_custom_call" | custom-call | flops 805306368 | bytes 14680064 | tf_op jit(solution)/shard_map/pallas_call | solution.py:218
  60.7 2.4 %collective-permute-start.19 = (bf16[32,4096]{1,0:T(8,128)(2,1)S(1)}, bf16[32,4096]{1,0:T(8,128)(2,1)S(1)}, u32[]{:S(2)}, u32[]{:S(2)}) collective-permute-start(bf16[32,4096]{1,0:T(8,128)(2,1)S(1)} %add_convert_fusion.11), channel_id=1, source_target_pairs={{0,4},{1,3},{4,8},{5,1},{8,12},{9,5},{12,14},{13,9},{14,10},{15,13... | collective-permute-start | bytes 786440 | tf_op jit(solution)/shard_map/ppermute | solution.py:272
  66.4 4.7 %shard_map.113 = (f32[32,4096]{1,0:T(8,128)S(1)}, f32[32,4096]{1,0:T(8,128)S(1)}) custom-call(s32[1]{0:T(128)} %bitcast.index_ref, bf16[4096,256]{1,0:T(8,128)(2,1)S(1)} %bitcast.12, bf16[4096,256]{1,0:T(8,128)(2,1)S(1)} %bitcast.19, bf16[256,4096]{1,0:T(8,128)(2,1)S(1)} %bitcast.26, f32[64,8]{1,0:T(8,128)S(1)} %compare_select_fusion.hits_hbm, ...), custom_call_target="tpu_custom_call" | custom-call | flops 805306368 | bytes 14680064 | tf_op jit(solution)/shard_map/pallas_call | solution.py:218
  71.2 2.4 %collective-permute-start.20 = (bf16[32,4096]{1,0:T(8,128)(2,1)S(1)}, bf16[32,4096]{1,0:T(8,128)(2,1)S(1)}, u32[]{:S(2)}, u32[]{:S(2)}) collective-permute-start(bf16[32,4096]{1,0:T(8,128)(2,1)S(1)} %add_convert_fusion.10), channel_id=1, source_target_pairs={{0,4},{1,3},{4,8},{5,1},{8,12},{9,5},{12,14},{13,9},{14,10},{15,13... | collective-permute-start | bytes 786440 | tf_op jit(solution)/shard_map/ppermute | solution.py:272
  74.1 2.2 %collective-permute-done.17.refs_0_ = bf16[64,4096]{1,0:T(8,128)(2,1)S(1)} collective-permute-done((bf16[64,4096]{1,0:T(8,128)(2,1)S(1)}, bf16[64,4096]{1,0:T(8,128)(2,1)S(1)}, u32[]{:S(2)}, u32[]{:S(2)}) %collective-permute-start.17) | collective-permute-done | bytes 524320 | tf_op jit(solution)/shard_map/ppermute | solution.py:272
  76.2 1.6 %collective-permute-start.22 = (bf16[64,4096]{1,0:T(8,128)(2,1)S(1)}, bf16[64,4096]{1,0:T(8,128)(2,1)S(1)}, u32[]{:S(2)}, u32[]{:S(2)}) collective-permute-start(bf16[64,4096]{1,0:T(8,128)(2,1)S(1)} %collective-permute-done.17.refs_0_), channel_id=1, source_target_pairs={{0,4},{1,3},{4,8},{5,1},{8,12},{9,5},{12,14},{13,9},{14,10},{15,13... | collective-permute-start | bytes 1572872 | tf_op jit(solution)/shard_map/ppermute | solution.py:272
  77.9 4.7 %shard_map.112 = (f32[32,4096]{1,0:T(8,128)S(1)}, f32[32,4096]{1,0:T(8,128)S(1)}) custom-call(s32[1]{0:T(128)} %bitcast.index_ref, bf16[4096,256]{1,0:T(8,128)(2,1)S(1)} %bitcast.13, bf16[4096,256]{1,0:T(8,128)(2,1)S(1)} %bitcast.20, bf16[256,4096]{1,0:T(8,128)(2,1)S(1)} %bitcast.27, f32[64,8]{1,0:T(8,128)S(1)} %compare_select_fusion.hits_hbm, ...), custom_call_target="tpu_custom_call" | custom-call | flops 805306368 | bytes 14680064 | tf_op jit(solution)/shard_map/pallas_call | solution.py:218
  82.6 2.2 %collective-permute-start.23 = (bf16[32,4096]{1,0:T(8,128)(2,1)S(1)}, bf16[32,4096]{1,0:T(8,128)(2,1)S(1)}, u32[]{:S(2)}, u32[]{:S(2)}) collective-permute-start(bf16[32,4096]{1,0:T(8,128)(2,1)S(1)} %add_convert_fusion.9), channel_id=1, source_target_pairs={{0,4},{1,3},{4,8},{5,1},{8,12},{9,5},{12,14},{13,9},{14,10},{15,13... | collective-permute-start | bytes 786440 | tf_op jit(solution)/shard_map/ppermute | solution.py:272
  84.9 2.1 %collective-permute-start.30 = (bf16[32,4096]{1,0:T(8,128)(2,1)S(1)}, bf16[32,4096]{1,0:T(8,128)(2,1)S(1)}, u32[]{:S(2)}, u32[]{:S(2)}) collective-permute-start(bf16[32,4096]{1,0:T(8,128)(2,1)S(1)} %add_convert_fusion.3), channel_id=1, source_target_pairs={{0,4},{1,3},{4,8},{5,1},{8,12},{9,5},{12,14},{13,9},{14,10},{15,13... | collective-permute-start | bytes 786440 | tf_op jit(solution)/shard_map/ppermute | solution.py:272
  87.0 3.6 %collective-permute-done.22.refs_0_ = bf16[64,4096]{1,0:T(8,128)(2,1)S(1)} collective-permute-done((bf16[64,4096]{1,0:T(8,128)(2,1)S(1)}, bf16[64,4096]{1,0:T(8,128)(2,1)S(1)}, u32[]{:S(2)}, u32[]{:S(2)}) %collective-permute-start.22) | collective-permute-done | bytes 524320 | tf_op jit(solution)/shard_map/ppermute | solution.py:272
  90.6 4.7 %shard_map.115 = (f32[32,4096]{1,0:T(8,128)S(1)}, f32[32,4096]{1,0:T(8,128)S(1)}) custom-call(s32[1]{0:T(128)} %bitcast.index_ref, bf16[4096,256]{1,0:T(8,128)(2,1)S(1)} %bitcast.14, bf16[4096,256]{1,0:T(8,128)(2,1)S(1)} %bitcast.21, bf16[256,4096]{1,0:T(8,128)(2,1)S(1)} %bitcast.28, f32[64,8]{1,0:T(8,128)S(1)} %compare_select_fusion.hits_hbm, ...), custom_call_target="tpu_custom_call" | custom-call | flops 805306368 | bytes 14680064 | tf_op jit(solution)/shard_map/pallas_call | solution.py:218
  95.9 2.1 %collective-permute-start.24 = (bf16[32,4096]{1,0:T(8,128)(2,1)S(1)}, bf16[32,4096]{1,0:T(8,128)(2,1)S(1)}, u32[]{:S(2)}, u32[]{:S(2)}) collective-permute-start(bf16[32,4096]{1,0:T(8,128)(2,1)S(1)} %add_convert_fusion.8), channel_id=1, source_target_pairs={{0,4},{1,3},{4,8},{5,1},{8,12},{9,5},{12,14},{13,9},{14,10},{15,13... | collective-permute-start | bytes 786440 | tf_op jit(solution)/shard_map/ppermute | solution.py:272
  98.7 1.9 %collective-permute-start.31 = (bf16[32,4096]{1,0:T(8,128)(2,1)S(1)}, bf16[32,4096]{1,0:T(8,128)(2,1)S(1)}, u32[]{:S(2)}, u32[]{:S(2)}) collective-permute-start(bf16[32,4096]{1,0:T(8,128)(2,1)S(1)} %add_convert_fusion.2), channel_id=1, source_target_pairs={{0,4},{1,3},{4,8},{5,1},{8,12},{9,5},{12,14},{13,9},{14,10},{15,13... | collective-permute-start | bytes 786440 | tf_op jit(solution)/shard_map/ppermute | solution.py:272
  100.6 4.7 %shard_map.114 = (f32[32,4096]{1,0:T(8,128)S(1)}, f32[32,4096]{1,0:T(8,128)S(1)}) custom-call(s32[1]{0:T(128)} %bitcast.index_ref, bf16[4096,256]{1,0:T(8,128)(2,1)S(1)} %bitcast.15, bf16[4096,256]{1,0:T(8,128)(2,1)S(1)} %bitcast.22, bf16[256,4096]{1,0:T(8,128)(2,1)S(1)} %bitcast.29, f32[64,8]{1,0:T(8,128)S(1)} %compare_select_fusion.hits_hbm, ...), custom_call_target="tpu_custom_call" | custom-call | flops 805306368 | bytes 14680064 | tf_op jit(solution)/shard_map/pallas_call | solution.py:218
  105.4 2.0 %collective-permute-start.25 = (bf16[32,4096]{1,0:T(8,128)(2,1)S(1)}, bf16[32,4096]{1,0:T(8,128)(2,1)S(1)}, u32[]{:S(2)}, u32[]{:S(2)}) collective-permute-start(bf16[32,4096]{1,0:T(8,128)(2,1)S(1)} %add_convert_fusion.7), channel_id=1, source_target_pairs={{0,4},{1,3},{4,8},{5,1},{8,12},{9,5},{12,14},{13,9},{14,10},{15,13... | collective-permute-start | bytes 786440 | tf_op jit(solution)/shard_map/ppermute | solution.py:272
  107.9 3.9 %collective-permute-done.25 = bf16[32,4096]{1,0:T(8,128)(2,1)S(1)} collective-permute-done((bf16[32,4096]{1,0:T(8,128)(2,1)S(1)}, bf16[32,4096]{1,0:T(8,128)(2,1)S(1)}, u32[]{:S(2)}, u32[]{:S(2)}) %collective-permute-start.25) | collective-permute-done | bytes 262176 | tf_op jit(solution)/shard_map/ppermute | solution.py:272
  111.9 2.0 %collective-permute-start.26 = (bf16[32,4096]{1,0:T(8,128)(2,1)S(1)}, bf16[32,4096]{1,0:T(8,128)(2,1)S(1)}, u32[]{:S(2)}, u32[]{:S(2)}) collective-permute-start(bf16[32,4096]{1,0:T(8,128)(2,1)S(1)} %add_convert_fusion.6), channel_id=1, source_target_pairs={{0,4},{1,3},{4,8},{5,1},{8,12},{9,5},{12,14},{13,9},{14,10},{15,13... | collective-permute-start | bytes 786440 | tf_op jit(solution)/shard_map/ppermute | solution.py:272
  114.6 2.0 %collective-permute-start.33 = (bf16[32,4096]{1,0:T(8,128)(2,1)S(1)}, bf16[32,4096]{1,0:T(8,128)(2,1)S(1)}, u32[]{:S(2)}, u32[]{:S(2)}) collective-permute-start(bf16[32,4096]{1,0:T(8,128)(2,1)S(1)} %add_convert_fusion), channel_id=1, source_target_pairs={{0,4},{1,3},{4,8},{5,1},{8,12},{9,5},{12,14},{13,9},{14,10},{15,13... | collective-permute-start | bytes 786440 | tf_op jit(solution)/shard_map/ppermute | solution.py:272
  116.7 1.6 %collective-permute-done.26 = bf16[32,4096]{1,0:T(8,128)(2,1)S(1)} collective-permute-done((bf16[32,4096]{1,0:T(8,128)(2,1)S(1)}, bf16[32,4096]{1,0:T(8,128)(2,1)S(1)}, u32[]{:S(2)}, u32[]{:S(2)}) %collective-permute-start.26) | collective-permute-done | bytes 262176 | tf_op jit(solution)/shard_map/ppermute | solution.py:272
  118.3 2.7 %collective-permute-done.33 = bf16[32,4096]{1,0:T(8,128)(2,1)S(1)} collective-permute-done((bf16[32,4096]{1,0:T(8,128)(2,1)S(1)}, bf16[32,4096]{1,0:T(8,128)(2,1)S(1)}, u32[]{:S(2)}, u32[]{:S(2)}) %collective-permute-start.33) | collective-permute-done | bytes 262176 | tf_op jit(solution)/shard_map/ppermute | solution.py:272
  (91 shorter events, 25.3 us)
Async XLA Ops:
  1.7 8.1 %collective-permute-start.3 = (bf16[64,640]{1,0:T(8,128)(2,1)S(1)}, bf16[64,640]{1,0:T(8,128)(2,1)S(1)}, u32[]{:S(2)}, u32[]{:S(2)}) collective-permute-start(bf16[64,640]{1,0:T(8,128)(2,1)S(1)} %get-tuple-element.79), channel_id=1, source_target_pairs={{0,8},{1,9},{2,10},{3,11},{4,12},{5,13},{6,14},{7,15},{8,0},{9,1},... | collective-permute-start | bytes 245768 | tf_op jit(solution)/shard_map/ppermute | solution.py:250
  5.8 6.6 %collective-permute-start = (bf16[64,640]{1,0:T(8,128)(2,1)S(1)}, bf16[64,640]{1,0:T(8,128)(2,1)S(1)}, u32[]{:S(2)}, u32[]{:S(2)}) collective-permute-start(bf16[64,640]{1,0:T(8,128)(2,1)S(1)} %get-tuple-element.79), channel_id=1, source_target_pairs={{0,2},{1,3},{2,0},{3,1},{4,6},{5,7},{6,4},{7,5},{8,10},{9,11},{10,... | collective-permute-start | bytes 245768 | tf_op jit(solution)/shard_map/ppermute | solution.py:250
  7.3 6.3 %collective-permute-start.1 = (bf16[64,640]{1,0:T(8,128)(2,1)S(1)}, bf16[64,640]{1,0:T(8,128)(2,1)S(1)}, u32[]{:S(2)}, u32[]{:S(2)}) collective-permute-start(bf16[64,640]{1,0:T(8,128)(2,1)S(1)} %get-tuple-element.79), channel_id=1, source_target_pairs={{0,4},{1,5},{2,6},{3,7},{4,0},{5,1},{6,2},{7,3},{8,12},{9,13},{10,... | collective-permute-start | bytes 245768 | tf_op jit(solution)/shard_map/ppermute | solution.py:250
  8.9 5.6 %collective-permute-start.2 = (bf16[64,640]{1,0:T(8,128)(2,1)S(1)}, bf16[64,640]{1,0:T(8,128)(2,1)S(1)}, u32[]{:S(2)}, u32[]{:S(2)}) collective-permute-start(bf16[64,640]{1,0:T(8,128)(2,1)S(1)} %get-tuple-element.79), channel_id=1, source_target_pairs={{0,6},{1,7},{2,4},{3,5},{4,2},{5,3},{6,0},{7,1},{8,14},{9,15},{10,... | collective-permute-start | bytes 245768 | tf_op jit(solution)/shard_map/ppermute | solution.py:250
  9.8 5.5 %collective-permute-start.4 = (bf16[64,640]{1,0:T(8,128)(2,1)S(1)}, bf16[64,640]{1,0:T(8,128)(2,1)S(1)}, u32[]{:S(2)}, u32[]{:S(2)}) collective-permute-start(bf16[64,640]{1,0:T(8,128)(2,1)S(1)} %collective-permute-done.3), channel_id=1, source_target_pairs={{0,2},{1,3},{2,0},{3,1},{4,6},{5,7},{6,4},{7,5},{8,10},{9,11},{10,... | collective-permute-start | bytes 245768 | tf_op jit(solution)/shard_map/ppermute | solution.py:250
  12.4 5.3 %collective-permute-start.6 = (bf16[64,640]{1,0:T(8,128)(2,1)S(1)}, bf16[64,640]{1,0:T(8,128)(2,1)S(1)}, u32[]{:S(2)}, u32[]{:S(2)}) collective-permute-start(bf16[64,640]{1,0:T(8,128)(2,1)S(1)} %collective-permute-done.3), channel_id=1, source_target_pairs={{0,6},{1,7},{2,4},{3,5},{4,2},{5,3},{6,0},{7,1},{8,14},{9,15},{10,... | collective-permute-start | bytes 245768 | tf_op jit(solution)/shard_map/ppermute | solution.py:250
  19.9 12.4 %collective-permute-start.10 = (bf16[256,4096]{1,0:T(8,128)(2,1)}, bf16[256,4096]{1,0:T(8,128)(2,1)}, u32[]{:S(2)}, u32[]{:S(2)}) collective-permute-start(bf16[256,4096]{1,0:T(8,128)(2,1)} %bitcast.23), channel_id=1, source_target_pairs={{0,1},{1,0},{2,3},{3,2},{4,5},{5,4},{6,7},{7,6},{8,9},{9,8},{10,11... | collective-permute-start | bytes 6291464 | tf_op jit(solution)/shard_map/ppermute | solution.py:261
  20.0 12.3 %collective-permute-start.8 = (bf16[4096,256]{1,0:T(8,128)(2,1)}, bf16[4096,256]{1,0:T(8,128)(2,1)}, u32[]{:S(2)}, u32[]{:S(2)}) collective-permute-start(bf16[4096,256]{1,0:T(8,128)(2,1)} %bitcast.9), channel_id=1, source_target_pairs={{0,1},{1,0},{2,3},{3,2},{4,5},{5,4},{6,7},{7,6},{8,9},{9,8},{10,11... | collective-permute-start | bytes 6291464 | tf_op jit(solution)/shard_map/ppermute | solution.py:261
  20.4 11.9 %collective-permute-start.9 = (bf16[4096,256]{1,0:T(8,128)(2,1)}, bf16[4096,256]{1,0:T(8,128)(2,1)}, u32[]{:S(2)}, u32[]{:S(2)}) collective-permute-start(bf16[4096,256]{1,0:T(8,128)(2,1)} %bitcast.16), channel_id=1, source_target_pairs={{0,1},{1,0},{2,3},{3,2},{4,5},{5,4},{6,7},{7,6},{8,9},{9,8},{10,11... | collective-permute-start | bytes 6291464 | tf_op jit(solution)/shard_map/ppermute | solution.py:261
  32.3 6.6 %collective-permute-start.11 = (bf16[32,4096]{1,0:T(8,128)(2,1)}, bf16[32,4096]{1,0:T(8,128)(2,1)S(1)}, u32[]{:S(2)}, u32[]{:S(2)}) collective-permute-start(bf16[32,4096]{1,0:T(8,128)(2,1)} %get-tuple-element.55.refs_3_), channel_id=1, source_target_pairs={{0,4},{1,3},{4,8},{5,1},{8,12},{9,5},{12,14},{13,9},{14,10},{15,13... | collective-permute-start | bytes 786440 | tf_op jit(solution)/shard_map/ppermute | solution.py:272
  33.4 8.3 %collective-permute-start.13 = (bf16[32,4096]{1,0:T(8,128)(2,1)}, bf16[32,4096]{1,0:T(8,128)(2,1)S(1)}, u32[]{:S(2)}, u32[]{:S(2)}) collective-permute-start(bf16[32,4096]{1,0:T(8,128)(2,1)} %get-tuple-element.57.refs_4_), channel_id=1, source_target_pairs={{0,4},{1,3},{4,8},{5,1},{8,12},{9,5},{12,14},{13,9},{14,10},{15,13... | collective-permute-start | bytes 786440 | tf_op jit(solution)/shard_map/ppermute | solution.py:272
  38.9 13.6 %collective-permute-start.12 = (bf16[32,4096]{1,0:T(8,128)(2,1)S(1)}, bf16[32,4096]{1,0:T(8,128)(2,1)S(1)}, u32[]{:S(2)}, u32[]{:S(2)}) collective-permute-start(bf16[32,4096]{1,0:T(8,128)(2,1)S(1)} %collective-permute-done.11.refs_0_), channel_id=1, source_target_pairs={{0,4},{1,3},{4,8},{5,1},{8,12},{9,5},{12,14},{13,9},{14,10},{15,13... | collective-permute-start | bytes 786440 | tf_op jit(solution)/shard_map/ppermute | solution.py:272
  41.8 10.8 %collective-permute-start.14 = (bf16[32,4096]{1,0:T(8,128)(2,1)S(1)}, bf16[32,4096]{1,0:T(8,128)(2,1)S(1)}, u32[]{:S(2)}, u32[]{:S(2)}) collective-permute-start(bf16[32,4096]{1,0:T(8,128)(2,1)S(1)} %collective-permute-done.13.refs_1_), channel_id=1, source_target_pairs={{0,4},{1,3},{4,8},{5,1},{8,12},{9,5},{12,14},{13,9},{14,10},{15,13... | collective-permute-start | bytes 786440 | tf_op jit(solution)/shard_map/ppermute | solution.py:272
  43.2 12.3 %collective-permute-start.15 = (bf16[64,4096]{1,0:T(8,128)(2,1)}, bf16[64,4096]{1,0:T(8,128)(2,1)S(1)}, u32[]{:S(2)}, u32[]{:S(2)}) collective-permute-start(bf16[64,4096]{1,0:T(8,128)(2,1)} %get-tuple-element.59), channel_id=1, source_target_pairs={{4,0},{3,1},{8,4},{1,5},{12,8},{5,9},{14,12},{9,13},{10,14},{13,15... | collective-permute-start | bytes 1572872 | tf_op jit(solution)/shard_map/ppermute | solution.py:272
  48.6 12.1 %collective-permute-start.18 = (bf16[32,4096]{1,0:T(8,128)(2,1)S(1)}, bf16[32,4096]{1,0:T(8,128)(2,1)S(1)}, u32[]{:S(2)}, u32[]{:S(2)}) collective-permute-start(bf16[32,4096]{1,0:T(8,128)(2,1)S(1)} %convert_element_type.99), channel_id=1, source_target_pairs={{0,4},{1,3},{4,8},{5,1},{8,12},{9,5},{12,14},{13,9},{14,10},{15,13... | collective-permute-start | bytes 786440 | tf_op jit(solution)/shard_map/ppermute | solution.py:272
  50.5 12.6 %collective-permute-start.27 = (bf16[32,4096]{1,0:T(8,128)(2,1)S(1)}, bf16[32,4096]{1,0:T(8,128)(2,1)S(1)}, u32[]{:S(2)}, u32[]{:S(2)}) collective-permute-start(bf16[32,4096]{1,0:T(8,128)(2,1)S(1)} %convert_element_type.113), channel_id=1, source_target_pairs={{0,4},{1,3},{4,8},{5,1},{8,12},{9,5},{12,14},{13,9},{14,10},{15,13... | collective-permute-start | bytes 786440 | tf_op jit(solution)/shard_map/ppermute | solution.py:272
  52.6 12.4 %collective-permute-start.16 = (bf16[64,4096]{1,0:T(8,128)(2,1)S(1)}, bf16[64,4096]{1,0:T(8,128)(2,1)S(1)}, u32[]{:S(2)}, u32[]{:S(2)}) collective-permute-start(bf16[64,4096]{1,0:T(8,128)(2,1)S(1)} %pad_maximum_fusion), channel_id=1, source_target_pairs={{0,4},{1,3},{4,8},{5,1},{8,12},{9,5},{12,14},{13,9},{14,10},{15,13... | collective-permute-start | bytes 1572872 | tf_op jit(solution)/shard_map/ppermute | solution.py:272
  60.7 10.4 %collective-permute-start.19 = (bf16[32,4096]{1,0:T(8,128)(2,1)S(1)}, bf16[32,4096]{1,0:T(8,128)(2,1)S(1)}, u32[]{:S(2)}, u32[]{:S(2)}) collective-permute-start(bf16[32,4096]{1,0:T(8,128)(2,1)S(1)} %add_convert_fusion.11), channel_id=1, source_target_pairs={{0,4},{1,3},{4,8},{5,1},{8,12},{9,5},{12,14},{13,9},{14,10},{15,13... | collective-permute-start | bytes 786440 | tf_op jit(solution)/shard_map/ppermute | solution.py:272
  63.1 10.5 %collective-permute-start.28 = (bf16[32,4096]{1,0:T(8,128)(2,1)S(1)}, bf16[32,4096]{1,0:T(8,128)(2,1)S(1)}, u32[]{:S(2)}, u32[]{:S(2)}) collective-permute-start(bf16[32,4096]{1,0:T(8,128)(2,1)S(1)} %add_convert_fusion.5), channel_id=1, source_target_pairs={{0,4},{1,3},{4,8},{5,1},{8,12},{9,5},{12,14},{13,9},{14,10},{15,13... | collective-permute-start | bytes 786440 | tf_op jit(solution)/shard_map/ppermute | solution.py:272
  65.0 11.2 %collective-permute-start.17 = (bf16[64,4096]{1,0:T(8,128)(2,1)S(1)}, bf16[64,4096]{1,0:T(8,128)(2,1)S(1)}, u32[]{:S(2)}, u32[]{:S(2)}) collective-permute-start(bf16[64,4096]{1,0:T(8,128)(2,1)S(1)} %collective-permute-done.16.refs_0_), channel_id=1, source_target_pairs={{0,4},{1,3},{4,8},{5,1},{8,12},{9,5},{12,14},{13,9},{14,10},{15,13... | collective-permute-start | bytes 1572872 | tf_op jit(solution)/shard_map/ppermute | solution.py:272
  71.2 11.4 %collective-permute-start.20 = (bf16[32,4096]{1,0:T(8,128)(2,1)S(1)}, bf16[32,4096]{1,0:T(8,128)(2,1)S(1)}, u32[]{:S(2)}, u32[]{:S(2)}) collective-permute-start(bf16[32,4096]{1,0:T(8,128)(2,1)S(1)} %add_convert_fusion.10), channel_id=1, source_target_pairs={{0,4},{1,3},{4,8},{5,1},{8,12},{9,5},{12,14},{13,9},{14,10},{15,13... | collective-permute-start | bytes 786440 | tf_op jit(solution)/shard_map/ppermute | solution.py:272
  73.6 11.2 %collective-permute-start.29 = (bf16[32,4096]{1,0:T(8,128)(2,1)S(1)}, bf16[32,4096]{1,0:T(8,128)(2,1)S(1)}, u32[]{:S(2)}, u32[]{:S(2)}) collective-permute-start(bf16[32,4096]{1,0:T(8,128)(2,1)S(1)} %add_convert_fusion.4), channel_id=1, source_target_pairs={{0,4},{1,3},{4,8},{5,1},{8,12},{9,5},{12,14},{13,9},{14,10},{15,13... | collective-permute-start | bytes 786440 | tf_op jit(solution)/shard_map/ppermute | solution.py:272
  76.2 14.4 %collective-permute-start.22 = (bf16[64,4096]{1,0:T(8,128)(2,1)S(1)}, bf16[64,4096]{1,0:T(8,128)(2,1)S(1)}, u32[]{:S(2)}, u32[]{:S(2)}) collective-permute-start(bf16[64,4096]{1,0:T(8,128)(2,1)S(1)} %collective-permute-done.17.refs_0_), channel_id=1, source_target_pairs={{0,4},{1,3},{4,8},{5,1},{8,12},{9,5},{12,14},{13,9},{14,10},{15,13... | collective-permute-start | bytes 1572872 | tf_op jit(solution)/shard_map/ppermute | solution.py:272
  82.6 13.3 %collective-permute-start.23 = (bf16[32,4096]{1,0:T(8,128)(2,1)S(1)}, bf16[32,4096]{1,0:T(8,128)(2,1)S(1)}, u32[]{:S(2)}, u32[]{:S(2)}) collective-permute-start(bf16[32,4096]{1,0:T(8,128)(2,1)S(1)} %add_convert_fusion.9), channel_id=1, source_target_pairs={{0,4},{1,3},{4,8},{5,1},{8,12},{9,5},{12,14},{13,9},{14,10},{15,13... | collective-permute-start | bytes 786440 | tf_op jit(solution)/shard_map/ppermute | solution.py:272
  84.8 15.8 %collective-permute-start.21 = (bf16[64,4096]{1,0:T(8,128)(2,1)S(1)}, bf16[64,4096]{1,0:T(8,128)(2,1)S(1)}, u32[]{:S(2)}, u32[]{:S(2)}) collective-permute-start(bf16[64,4096]{1,0:T(8,128)(2,1)S(1)} %collective-permute-done.15.refs_2_), channel_id=1, source_target_pairs={{4,0},{3,1},{8,4},{1,5},{12,8},{5,9},{14,12},{9,13},{10,14},{13,15... | collective-permute-start | bytes 1572872 | tf_op jit(solution)/shard_map/ppermute | solution.py:272
  84.9 13.8 %collective-permute-start.30 = (bf16[32,4096]{1,0:T(8,128)(2,1)S(1)}, bf16[32,4096]{1,0:T(8,128)(2,1)S(1)}, u32[]{:S(2)}, u32[]{:S(2)}) collective-permute-start(bf16[32,4096]{1,0:T(8,128)(2,1)S(1)} %add_convert_fusion.3), channel_id=1, source_target_pairs={{0,4},{1,3},{4,8},{5,1},{8,12},{9,5},{12,14},{13,9},{14,10},{15,13... | collective-permute-start | bytes 786440 | tf_op jit(solution)/shard_map/ppermute | solution.py:272
  95.9 9.4 %collective-permute-start.24 = (bf16[32,4096]{1,0:T(8,128)(2,1)S(1)}, bf16[32,4096]{1,0:T(8,128)(2,1)S(1)}, u32[]{:S(2)}, u32[]{:S(2)}) collective-permute-start(bf16[32,4096]{1,0:T(8,128)(2,1)S(1)} %add_convert_fusion.8), channel_id=1, source_target_pairs={{0,4},{1,3},{4,8},{5,1},{8,12},{9,5},{12,14},{13,9},{14,10},{15,13... | collective-permute-start | bytes 786440 | tf_op jit(solution)/shard_map/ppermute | solution.py:272
  98.7 8.7 %collective-permute-start.31 = (bf16[32,4096]{1,0:T(8,128)(2,1)S(1)}, bf16[32,4096]{1,0:T(8,128)(2,1)S(1)}, u32[]{:S(2)}, u32[]{:S(2)}) collective-permute-start(bf16[32,4096]{1,0:T(8,128)(2,1)S(1)} %add_convert_fusion.2), channel_id=1, source_target_pairs={{0,4},{1,3},{4,8},{5,1},{8,12},{9,5},{12,14},{13,9},{14,10},{15,13... | collective-permute-start | bytes 786440 | tf_op jit(solution)/shard_map/ppermute | solution.py:272
  105.4 6.4 %collective-permute-start.25 = (bf16[32,4096]{1,0:T(8,128)(2,1)S(1)}, bf16[32,4096]{1,0:T(8,128)(2,1)S(1)}, u32[]{:S(2)}, u32[]{:S(2)}) collective-permute-start(bf16[32,4096]{1,0:T(8,128)(2,1)S(1)} %add_convert_fusion.7), channel_id=1, source_target_pairs={{0,4},{1,3},{4,8},{5,1},{8,12},{9,5},{12,14},{13,9},{14,10},{15,13... | collective-permute-start | bytes 786440 | tf_op jit(solution)/shard_map/ppermute | solution.py:272
  107.5 7.1 %collective-permute-start.32 = (bf16[32,4096]{1,0:T(8,128)(2,1)S(1)}, bf16[32,4096]{1,0:T(8,128)(2,1)S(1)}, u32[]{:S(2)}, u32[]{:S(2)}) collective-permute-start(bf16[32,4096]{1,0:T(8,128)(2,1)S(1)} %add_convert_fusion.1), channel_id=1, source_target_pairs={{0,4},{1,3},{4,8},{5,1},{8,12},{9,5},{12,14},{13,9},{14,10},{15,13... | collective-permute-start | bytes 786440 | tf_op jit(solution)/shard_map/ppermute | solution.py:272
  111.9 6.4 %collective-permute-start.26 = (bf16[32,4096]{1,0:T(8,128)(2,1)S(1)}, bf16[32,4096]{1,0:T(8,128)(2,1)S(1)}, u32[]{:S(2)}, u32[]{:S(2)}) collective-permute-start(bf16[32,4096]{1,0:T(8,128)(2,1)S(1)} %add_convert_fusion.6), channel_id=1, source_target_pairs={{0,4},{1,3},{4,8},{5,1},{8,12},{9,5},{12,14},{13,9},{14,10},{15,13... | collective-permute-start | bytes 786440 | tf_op jit(solution)/shard_map/ppermute | solution.py:272
  114.6 6.4 %collective-permute-start.33 = (bf16[32,4096]{1,0:T(8,128)(2,1)S(1)}, bf16[32,4096]{1,0:T(8,128)(2,1)S(1)}, u32[]{:S(2)}, u32[]{:S(2)}) collective-permute-start(bf16[32,4096]{1,0:T(8,128)(2,1)S(1)} %add_convert_fusion), channel_id=1, source_target_pairs={{0,4},{1,3},{4,8},{5,1},{8,12},{9,5},{12,14},{13,9},{14,10},{15,13... | collective-permute-start | bytes 786440 | tf_op jit(solution)/shard_map/ppermute | solution.py:272
  (11 other events, 125.0 us)

commit v19 on v16

--- a/solution.py
+++ b/solution.py
@@ -180,7 +180,8 @@
     for copy in copies:
         copy.start()
     my_chip, my_core = index_ref[0] // CORES, lax.rem(index_ref[0], CORES)
-    rows = jnp.concatenate([ref[...] for ref in rows_refs], axis=0)
+    copies_of = 2 if len(hops) == 1 else 1
+    rows = jnp.concatenate([ref[...] for ref in rows_refs] * copies_of, axis=0)
 
     def hit(hop):
         place = ring_place(my_chip, chips) + chips + hop * (2 * my_core - 1)
@@ -198,14 +199,14 @@
 
     act_a = hidden(gate_a, up_a)
     copies[0].wait()
-    keep = jnp.concatenate([hit(hop) for hop in hops], axis=0) > 0.0
+    keep = jnp.concatenate([hit(hop) for hop in hops] * copies_of, axis=0) > 0.0
     part = jnp.dot(kept(act_a), down_a[...], preferred_element_type=jnp.float32)
     copies[1].wait()
     copies[2].wait()
     act_b = hidden(gate_b, up_b)
     copies[3].wait()
     part = part + jnp.dot(kept(act_b), down_b[...], preferred_element_type=jnp.float32)
-    size = part.shape[0] // outs
+    size = part.shape[0] // copies_of // outs
     for i, out_ref in enumerate(out_refs):
         out_ref[...] = part[i * size : (i + 1) * size]
 

time: 120 us -> 120 us (level)
  Pallas kernels: 40.1 us -> 38.3 us
    pallas_call x6, Pallas kernels: 28.6 us -> 26.7 us  [expert_parts(): pl.pallas_call(functools.partial(expert_kernel, hops=hops, chips=chips),...]
  transfers between devices with their start and end apart: 34 -> 34, of which waited for: 17 -> 17; matrix products, arithmetic and copies ran while one was open for 1% -> 1% of each run, Pallas kernels for 33% -> 32%
where the time goes in v19:
time: 120 us
  starting transfers between devices  48.4 us (40%)
  Pallas kernels  38.3 us (32%)
  waiting for transfers between devices  28.3 us (24%)
  other arithmetic  4.12 us (3%)
    ppermute x23, starting transfers between devices, move(): return tuple((lax.ppermute(x, 'ctx', way) for x in blocks))  36.3 us
    pallas_call x6, Pallas kernels, expert_parts(): pl.pallas_call(functools.partial(expert_kernel, hops=hops, chips=chips),...  26.7 us
    ppermute x23, waiting for transfers between devices, move(): return tuple((lax.ppermute(x, 'ctx', way) for x in blocks))  21.7 us
    pallas_call x1, Pallas kernels, attention(): pl.pallas_call(functools.partial(attention_kernel, tok=tok), grid_spec=gr...  11.5 us
    ppermute x7, starting transfers between devices, from_chip(): lax.ppermute(block, 'ctx', [(i, i ^ step * CORES) for i in range(n_ctx)])  11.4 us
    ppermute x7, waiting for transfers between devices, from_chip(): lax.ppermute(block, 'ctx', [(i, i ^ step * CORES) for i in range(n_ctx)])  4.54 us
  transfers between devices with their start and end apart: 34, of which 17 were waited for; matrix products, arithmetic and copies ran while one was open for 1% of the time, Pallas kernels for 32%

profile of v19, /device:TPU:0, one launch (start us, length us, event | category | flops | bytes accessed | tf_op | source)
XLA Modules:
  0.0 119.8 jit_solution(5232058168918060538)
XLA Ops:
  1.7 4.1 %collective-permute-start.3 = (bf16[64,640]{1,0:T(8,128)(2,1)S(1)}, bf16[64,640]{1,0:T(8,128)(2,1)S(1)}, u32[]{:S(2)}, u32[]{:S(2)}) collective-permute-start(bf16[64,640]{1,0:T(8,128)(2,1)S(1)} %get-tuple-element.79), channel_id=1, source_target_pairs={{0,8},{1,9},{2,10},{3,11},{4,12},{5,13},{6,14},{7,15},{8,0},{9,1},... | collective-permute-start | bytes 245768 | tf_op jit(solution)/shard_map/ppermute | solution.py:251
  7.3 1.6 %collective-permute-start.1 = (bf16[64,640]{1,0:T(8,128)(2,1)S(1)}, bf16[64,640]{1,0:T(8,128)(2,1)S(1)}, u32[]{:S(2)}, u32[]{:S(2)}) collective-permute-start(bf16[64,640]{1,0:T(8,128)(2,1)S(1)} %get-tuple-element.79), channel_id=1, source_target_pairs={{0,4},{1,5},{2,6},{3,7},{4,0},{5,1},{6,2},{7,3},{8,12},{9,13},{10,... | collective-permute-start | bytes 245768 | tf_op jit(solution)/shard_map/ppermute | solution.py:251
  9.8 1.6 %collective-permute-start.4 = (bf16[64,640]{1,0:T(8,128)(2,1)S(1)}, bf16[64,640]{1,0:T(8,128)(2,1)S(1)}, u32[]{:S(2)}, u32[]{:S(2)}) collective-permute-start(bf16[64,640]{1,0:T(8,128)(2,1)S(1)} %collective-permute-done.3), channel_id=1, source_target_pairs={{0,2},{1,3},{2,0},{3,1},{4,6},{5,7},{6,4},{7,5},{8,10},{9,11},{10,... | collective-permute-start | bytes 245768 | tf_op jit(solution)/shard_map/ppermute | solution.py:251
  15.9 1.8 %collective-permute-done.6 = bf16[64,640]{1,0:T(8,128)(2,1)S(1)} collective-permute-done((bf16[64,640]{1,0:T(8,128)(2,1)S(1)}, bf16[64,640]{1,0:T(8,128)(2,1)S(1)}, u32[]{:S(2)}, u32[]{:S(2)}) %collective-permute-start.6) | collective-permute-done | bytes 81952 | tf_op jit(solution)/shard_map/ppermute | solution.py:251
  17.8 2.1 %collective-permute-done.7.other_ref = bf16[512,640]{1,0:T(8,128)(2,1)S(1)} collective-permute-done((bf16[512,640]{1,0:T(8,128)(2,1)S(1)}, bf16[512,640]{1,0:T(8,128)(2,1)S(1)}, u32[]{:S(2)}, u32[]{:S(2)}) %collective-permute-start.7) | collective-permute-done | bytes 655392 | tf_op jit(solution)/shard_map/ppermute | solution.py:259
  20.8 11.5 %shard_map.109 = (bf16[64,4096]{1,0:T(8,128)(2,1)}, bf16[64,4096]{1,0:T(8,128)(2,1)}, bf16[32,4096]{1,0:T(8,128)(2,1)}, bf16[32,4096]{1,0:T(8,128)(2,1)}, f32[64,8]{1,0:T(8,128)}) custom-call(s32[1]{0:T(128)} %bitcast.index_ref, bf16[64,16384]{1,0:T(8,128)(2,1)} %q_ref.1, bf16[64,2048]{1,0:T(8,128)(2,1)} %qr_ref.1, bf16[512,640]{1,0:T(8,128)(2,1)} %copy-done.6, ...), custom_call_target="tpu_custom_call" | custom-call | flops 4831838208 | bytes 8388608 | tf_op jit(solution)/shard_map/pallas_call | solution.py:151
  33.4 2.7 %collective-permute-start.13 = (bf16[32,4096]{1,0:T(8,128)(2,1)}, bf16[32,4096]{1,0:T(8,128)(2,1)S(1)}, u32[]{:S(2)}, u32[]{:S(2)}) collective-permute-start(bf16[32,4096]{1,0:T(8,128)(2,1)} %get-tuple-element.57.refs_4_), channel_id=1, source_target_pairs={{0,4},{1,3},{4,8},{5,1},{8,12},{9,5},{12,14},{13,9},{14,10},{15,13... | collective-permute-start | bytes 786440 | tf_op jit(solution)/shard_map/ppermute | solution.py:273
  36.9 2.0 %collective-permute-done.11.refs_0_ = bf16[32,4096]{1,0:T(8,128)(2,1)S(1)} collective-permute-done((bf16[32,4096]{1,0:T(8,128)(2,1)}, bf16[32,4096]{1,0:T(8,128)(2,1)S(1)}, u32[]{:S(2)}, u32[]{:S(2)}) %collective-permute-start.11) | collective-permute-done | bytes 262176 | tf_op jit(solution)/shard_map/ppermute | solution.py:273
  43.8 4.3 %shard_map.111 = (f32[32,4096]{1,0:T(8,128)S(1)}, f32[32,4096]{1,0:T(8,128)S(1)}) custom-call(s32[1]{0:T(128)} %bitcast.index_ref, bf16[4096,256]{1,0:T(8,128)(2,1)S(1)} %bitcast.10, bf16[4096,256]{1,0:T(8,128)(2,1)S(1)} %bitcast.17, bf16[256,4096]{1,0:T(8,128)(2,1)S(1)} %bitcast.24, f32[64,8]{1,0:T(8,128)S(1)} %compare_select_fusion.hits_hbm, ...), custom_call_target="tpu_custom_call" | custom-call | flops 805306368 | bytes 14680064 | tf_op jit(solution)/shard_map/pallas_call | solution.py:219
  48.2 1.9 %collective-permute-start.18 = (bf16[32,4096]{1,0:T(8,128)(2,1)S(1)}, bf16[32,4096]{1,0:T(8,128)(2,1)S(1)}, u32[]{:S(2)}, u32[]{:S(2)}) collective-permute-start(bf16[32,4096]{1,0:T(8,128)(2,1)S(1)} %convert_element_type.99), channel_id=1, source_target_pairs={{0,4},{1,3},{4,8},{5,1},{8,12},{9,5},{12,14},{13,9},{14,10},{15,13... | collective-permute-start | bytes 786440 | tf_op jit(solution)/shard_map/ppermute | solution.py:273
  50.1 2.0 %collective-permute-start.27 = (bf16[32,4096]{1,0:T(8,128)(2,1)S(1)}, bf16[32,4096]{1,0:T(8,128)(2,1)S(1)}, u32[]{:S(2)}, u32[]{:S(2)}) collective-permute-start(bf16[32,4096]{1,0:T(8,128)(2,1)S(1)} %convert_element_type.113), channel_id=1, source_target_pairs={{0,4},{1,3},{4,8},{5,1},{8,12},{9,5},{12,14},{13,9},{14,10},{15,13... | collective-permute-start | bytes 786440 | tf_op jit(solution)/shard_map/ppermute | solution.py:273
  53.7 2.1 %collective-permute-done.15.refs_2_ = bf16[64,4096]{1,0:T(8,128)(2,1)S(1)} collective-permute-done((bf16[64,4096]{1,0:T(8,128)(2,1)}, bf16[64,4096]{1,0:T(8,128)(2,1)S(1)}, u32[]{:S(2)}, u32[]{:S(2)}) %collective-permute-start.15) | collective-permute-done | bytes 524320 | tf_op jit(solution)/shard_map/ppermute | solution.py:273
  55.8 5.2 %shard_map.110 = (f32[32,4096]{1,0:T(8,128)S(1)}, f32[32,4096]{1,0:T(8,128)S(1)}, f32[32,4096]{1,0:T(8,128)S(1)}, f32[32,4096]{1,0:T(8,128)S(1)}, f32[32,4096]{1,0:T(8,128)S(1)}, /*index=5*/f32[32,4096]{1,0:T(8,128)S(1)}) custom-call(s32[1]{0:T(128)} %bitcast.index_ref, bf16[4096,256]{1,0:T(8,128)(2,1)S(1)} %bitcast.11, bf16[4096,256]{1,0:T(8,128)(2,1)S(1)} %bitcast.18, ...), custom_call_target="tpu_custom_call" | custom-call | flops 805306368 | bytes 14680064 | tf_op jit(solution)/shard_map/pallas_call | solution.py:219
  61.1 2.4 %collective-permute-start.28 = (bf16[32,4096]{1,0:T(8,128)(2,1)S(1)}, bf16[32,4096]{1,0:T(8,128)(2,1)S(1)}, u32[]{:S(2)}, u32[]{:S(2)}) collective-permute-start(bf16[32,4096]{1,0:T(8,128)(2,1)S(1)} %add_convert_fusion.5), channel_id=1, source_target_pairs={{0,4},{1,3},{4,8},{5,1},{8,12},{9,5},{12,14},{13,9},{14,10},{15,13... | collective-permute-start | bytes 786440 | tf_op jit(solution)/shard_map/ppermute | solution.py:273
  66.4 4.3 %shard_map.112 = (f32[32,4096]{1,0:T(8,128)S(1)}, f32[32,4096]{1,0:T(8,128)S(1)}) custom-call(s32[1]{0:T(128)} %bitcast.index_ref, bf16[4096,256]{1,0:T(8,128)(2,1)S(1)} %bitcast.12, bf16[4096,256]{1,0:T(8,128)(2,1)S(1)} %bitcast.19, bf16[256,4096]{1,0:T(8,128)(2,1)S(1)} %bitcast.26, f32[64,8]{1,0:T(8,128)S(1)} %compare_select_fusion.hits_hbm, ...), custom_call_target="tpu_custom_call" | custom-call | flops 805306368 | bytes 14680064 | tf_op jit(solution)/shard_map/pallas_call | solution.py:219
  70.8 2.4 %collective-permute-start.29 = (bf16[32,4096]{1,0:T(8,128)(2,1)S(1)}, bf16[32,4096]{1,0:T(8,128)(2,1)S(1)}, u32[]{:S(2)}, u32[]{:S(2)}) collective-permute-start(bf16[32,4096]{1,0:T(8,128)(2,1)S(1)} %add_convert_fusion.4), channel_id=1, source_target_pairs={{0,4},{1,3},{4,8},{5,1},{8,12},{9,5},{12,14},{13,9},{14,10},{15,13... | collective-permute-start | bytes 786440 | tf_op jit(solution)/shard_map/ppermute | solution.py:273
  73.7 2.5 %collective-permute-done.17.refs_0_ = bf16[64,4096]{1,0:T(8,128)(2,1)S(1)} collective-permute-done((bf16[64,4096]{1,0:T(8,128)(2,1)S(1)}, bf16[64,4096]{1,0:T(8,128)(2,1)S(1)}, u32[]{:S(2)}, u32[]{:S(2)}) %collective-permute-start.17) | collective-permute-done | bytes 524320 | tf_op jit(solution)/shard_map/ppermute | solution.py:273
  76.2 2.0 %collective-permute-start.19 = (bf16[64,4096]{1,0:T(8,128)(2,1)S(1)}, bf16[64,4096]{1,0:T(8,128)(2,1)S(1)}, u32[]{:S(2)}, u32[]{:S(2)}) collective-permute-start(bf16[64,4096]{1,0:T(8,128)(2,1)S(1)} %collective-permute-done.17.refs_0_), channel_id=1, source_target_pairs={{0,4},{1,3},{4,8},{5,1},{8,12},{9,5},{12,14},{13,9},{14,10},{15,13... | collective-permute-start | bytes 1572872 | tf_op jit(solution)/shard_map/ppermute | solution.py:273
  78.2 4.3 %shard_map.115 = (f32[32,4096]{1,0:T(8,128)S(1)}, f32[32,4096]{1,0:T(8,128)S(1)}) custom-call(s32[1]{0:T(128)} %bitcast.index_ref, bf16[4096,256]{1,0:T(8,128)(2,1)S(1)} %bitcast.13, bf16[4096,256]{1,0:T(8,128)(2,1)S(1)} %bitcast.20, bf16[256,4096]{1,0:T(8,128)(2,1)S(1)} %bitcast.27, f32[64,8]{1,0:T(8,128)S(1)} %compare_select_fusion.hits_hbm, ...), custom_call_target="tpu_custom_call" | custom-call | flops 805306368 | bytes 14680064 | tf_op jit(solution)/shard_map/pallas_call | solution.py:219
  82.6 1.9 %collective-permute-start.30 = (bf16[32,4096]{1,0:T(8,128)(2,1)S(1)}, bf16[32,4096]{1,0:T(8,128)(2,1)S(1)}, u32[]{:S(2)}, u32[]{:S(2)}) collective-permute-start(bf16[32,4096]{1,0:T(8,128)(2,1)S(1)} %add_convert_fusion.3), channel_id=1, source_target_pairs={{0,4},{1,3},{4,8},{5,1},{8,12},{9,5},{12,14},{13,9},{14,10},{15,13... | collective-permute-start | bytes 786440 | tf_op jit(solution)/shard_map/ppermute | solution.py:273
  84.9 2.5 %collective-permute-done.19.refs_0_ = bf16[64,4096]{1,0:T(8,128)(2,1)S(1)} collective-permute-done((bf16[64,4096]{1,0:T(8,128)(2,1)S(1)}, bf16[64,4096]{1,0:T(8,128)(2,1)S(1)}, u32[]{:S(2)}, u32[]{:S(2)}) %collective-permute-start.19) | collective-permute-done | bytes 524320 | tf_op jit(solution)/shard_map/ppermute | solution.py:273
  87.5 2.0 %collective-permute-start.21 = (bf16[64,4096]{1,0:T(8,128)(2,1)S(1)}, bf16[64,4096]{1,0:T(8,128)(2,1)S(1)}, u32[]{:S(2)}, u32[]{:S(2)}) collective-permute-start(bf16[64,4096]{1,0:T(8,128)(2,1)S(1)} %collective-permute-done.19.refs_0_), channel_id=1, source_target_pairs={{0,4},{1,3},{4,8},{5,1},{8,12},{9,5},{12,14},{13,9},{14,10},{15,13... | collective-permute-start | bytes 1572872 | tf_op jit(solution)/shard_map/ppermute | solution.py:273
  89.4 4.3 %shard_map.114 = (f32[32,4096]{1,0:T(8,128)S(1)}, f32[32,4096]{1,0:T(8,128)S(1)}) custom-call(s32[1]{0:T(128)} %bitcast.index_ref, bf16[4096,256]{1,0:T(8,128)(2,1)S(1)} %bitcast.14, bf16[4096,256]{1,0:T(8,128)(2,1)S(1)} %bitcast.21, bf16[256,4096]{1,0:T(8,128)(2,1)S(1)} %bitcast.28, f32[64,8]{1,0:T(8,128)S(1)} %compare_select_fusion.hits_hbm, ...), custom_call_target="tpu_custom_call" | custom-call | flops 805306368 | bytes 14680064 | tf_op jit(solution)/shard_map/pallas_call | solution.py:219
  93.8 1.9 %collective-permute-start.31 = (bf16[32,4096]{1,0:T(8,128)(2,1)S(1)}, bf16[32,4096]{1,0:T(8,128)(2,1)S(1)}, u32[]{:S(2)}, u32[]{:S(2)}) collective-permute-start(bf16[32,4096]{1,0:T(8,128)(2,1)S(1)} %add_convert_fusion.2), channel_id=1, source_target_pairs={{0,4},{1,3},{4,8},{5,1},{8,12},{9,5},{12,14},{13,9},{14,10},{15,13... | collective-permute-start | bytes 786440 | tf_op jit(solution)/shard_map/ppermute | solution.py:273
  96.2 2.5 %collective-permute-done.21.refs_0_ = bf16[64,4096]{1,0:T(8,128)(2,1)S(1)} collective-permute-done((bf16[64,4096]{1,0:T(8,128)(2,1)S(1)}, bf16[64,4096]{1,0:T(8,128)(2,1)S(1)}, u32[]{:S(2)}, u32[]{:S(2)}) %collective-permute-start.21) | collective-permute-done | bytes 524320 | tf_op jit(solution)/shard_map/ppermute | solution.py:273
  98.7 4.3 %shard_map.113 = (f32[32,4096]{1,0:T(8,128)S(1)}, f32[32,4096]{1,0:T(8,128)S(1)}) custom-call(s32[1]{0:T(128)} %bitcast.index_ref, bf16[4096,256]{1,0:T(8,128)(2,1)S(1)} %bitcast.15, bf16[4096,256]{1,0:T(8,128)(2,1)S(1)} %bitcast.22, bf16[256,4096]{1,0:T(8,128)(2,1)S(1)} %bitcast.29, f32[64,8]{1,0:T(8,128)S(1)} %compare_select_fusion.hits_hbm, ...), custom_call_target="tpu_custom_call" | custom-call | flops 805306368 | bytes 14680064 | tf_op jit(solution)/shard_map/pallas_call | solution.py:219
  103.1 2.1 %collective-permute-start.32 = (bf16[32,4096]{1,0:T(8,128)(2,1)S(1)}, bf16[32,4096]{1,0:T(8,128)(2,1)S(1)}, u32[]{:S(2)}, u32[]{:S(2)}) collective-permute-start(bf16[32,4096]{1,0:T(8,128)(2,1)S(1)} %add_convert_fusion.1), channel_id=1, source_target_pairs={{0,4},{1,3},{4,8},{5,1},{8,12},{9,5},{12,14},{13,9},{14,10},{15,13... | collective-permute-start | bytes 786440 | tf_op jit(solution)/shard_map/ppermute | solution.py:273
  105.2 1.9 %collective-permute-start.25 = (bf16[32,4096]{1,0:T(8,128)(2,1)S(1)}, bf16[32,4096]{1,0:T(8,128)(2,1)S(1)}, u32[]{:S(2)}, u32[]{:S(2)}) collective-permute-start(bf16[32,4096]{1,0:T(8,128)(2,1)S(1)} %add_convert_fusion.7), channel_id=1, source_target_pairs={{0,4},{1,3},{4,8},{5,1},{8,12},{9,5},{12,14},{13,9},{14,10},{15,13... | collective-permute-start | bytes 786440 | tf_op jit(solution)/shard_map/ppermute | solution.py:273
  107.0 2.5 %collective-permute-done.32 = bf16[32,4096]{1,0:T(8,128)(2,1)S(1)} collective-permute-done((bf16[32,4096]{1,0:T(8,128)(2,1)S(1)}, bf16[32,4096]{1,0:T(8,128)(2,1)S(1)}, u32[]{:S(2)}, u32[]{:S(2)}) %collective-permute-start.32) | collective-permute-done | bytes 262176 | tf_op jit(solution)/shard_map/ppermute | solution.py:273
  109.6 2.1 %collective-permute-start.33 = (bf16[32,4096]{1,0:T(8,128)(2,1)S(1)}, bf16[32,4096]{1,0:T(8,128)(2,1)S(1)}, u32[]{:S(2)}, u32[]{:S(2)}) collective-permute-start(bf16[32,4096]{1,0:T(8,128)(2,1)S(1)} %add_convert_fusion), channel_id=1, source_target_pairs={{0,4},{1,3},{4,8},{5,1},{8,12},{9,5},{12,14},{13,9},{14,10},{15,13... | collective-permute-start | bytes 786440 | tf_op jit(solution)/shard_map/ppermute | solution.py:273
  112.4 2.1 %collective-permute-start.26 = (bf16[32,4096]{1,0:T(8,128)(2,1)S(1)}, bf16[32,4096]{1,0:T(8,128)(2,1)S(1)}, u32[]{:S(2)}, u32[]{:S(2)}) collective-permute-start(bf16[32,4096]{1,0:T(8,128)(2,1)S(1)} %add_convert_fusion.6), channel_id=1, source_target_pairs={{0,4},{1,3},{4,8},{5,1},{8,12},{9,5},{12,14},{13,9},{14,10},{15,13... | collective-permute-start | bytes 786440 | tf_op jit(solution)/shard_map/ppermute | solution.py:273
  116.0 2.8 %collective-permute-done.26 = bf16[32,4096]{1,0:T(8,128)(2,1)S(1)} collective-permute-done((bf16[32,4096]{1,0:T(8,128)(2,1)S(1)}, bf16[32,4096]{1,0:T(8,128)(2,1)S(1)}, u32[]{:S(2)}, u32[]{:S(2)}) %collective-permute-start.26) | collective-permute-done | bytes 262176 | tf_op jit(solution)/shard_map/ppermute | solution.py:273
  (91 shorter events, 26.0 us)
Async XLA Ops:
  1.7 8.1 %collective-permute-start.3 = (bf16[64,640]{1,0:T(8,128)(2,1)S(1)}, bf16[64,640]{1,0:T(8,128)(2,1)S(1)}, u32[]{:S(2)}, u32[]{:S(2)}) collective-permute-start(bf16[64,640]{1,0:T(8,128)(2,1)S(1)} %get-tuple-element.79), channel_id=1, source_target_pairs={{0,8},{1,9},{2,10},{3,11},{4,12},{5,13},{6,14},{7,15},{8,0},{9,1},... | collective-permute-start | bytes 245768 | tf_op jit(solution)/shard_map/ppermute | solution.py:251
  5.8 6.6 %collective-permute-start = (bf16[64,640]{1,0:T(8,128)(2,1)S(1)}, bf16[64,640]{1,0:T(8,128)(2,1)S(1)}, u32[]{:S(2)}, u32[]{:S(2)}) collective-permute-start(bf16[64,640]{1,0:T(8,128)(2,1)S(1)} %get-tuple-element.79), channel_id=1, source_target_pairs={{0,2},{1,3},{2,0},{3,1},{4,6},{5,7},{6,4},{7,5},{8,10},{9,11},{10,... | collective-permute-start | bytes 245768 | tf_op jit(solution)/shard_map/ppermute | solution.py:251
  7.3 6.3 %collective-permute-start.1 = (bf16[64,640]{1,0:T(8,128)(2,1)S(1)}, bf16[64,640]{1,0:T(8,128)(2,1)S(1)}, u32[]{:S(2)}, u32[]{:S(2)}) collective-permute-start(bf16[64,640]{1,0:T(8,128)(2,1)S(1)} %get-tuple-element.79), channel_id=1, source_target_pairs={{0,4},{1,5},{2,6},{3,7},{4,0},{5,1},{6,2},{7,3},{8,12},{9,13},{10,... | collective-permute-start | bytes 245768 | tf_op jit(solution)/shard_map/ppermute | solution.py:251
  8.9 5.6 %collective-permute-start.2 = (bf16[64,640]{1,0:T(8,128)(2,1)S(1)}, bf16[64,640]{1,0:T(8,128)(2,1)S(1)}, u32[]{:S(2)}, u32[]{:S(2)}) collective-permute-start(bf16[64,640]{1,0:T(8,128)(2,1)S(1)} %get-tuple-element.79), channel_id=1, source_target_pairs={{0,6},{1,7},{2,4},{3,5},{4,2},{5,3},{6,0},{7,1},{8,14},{9,15},{10,... | collective-permute-start | bytes 245768 | tf_op jit(solution)/shard_map/ppermute | solution.py:251
  9.8 5.5 %collective-permute-start.4 = (bf16[64,640]{1,0:T(8,128)(2,1)S(1)}, bf16[64,640]{1,0:T(8,128)(2,1)S(1)}, u32[]{:S(2)}, u32[]{:S(2)}) collective-permute-start(bf16[64,640]{1,0:T(8,128)(2,1)S(1)} %collective-permute-done.3), channel_id=1, source_target_pairs={{0,2},{1,3},{2,0},{3,1},{4,6},{5,7},{6,4},{7,5},{8,10},{9,11},{10,... | collective-permute-start | bytes 245768 | tf_op jit(solution)/shard_map/ppermute | solution.py:251
  12.4 5.3 %collective-permute-start.6 = (bf16[64,640]{1,0:T(8,128)(2,1)S(1)}, bf16[64,640]{1,0:T(8,128)(2,1)S(1)}, u32[]{:S(2)}, u32[]{:S(2)}) collective-permute-start(bf16[64,640]{1,0:T(8,128)(2,1)S(1)} %collective-permute-done.3), channel_id=1, source_target_pairs={{0,6},{1,7},{2,4},{3,5},{4,2},{5,3},{6,0},{7,1},{8,14},{9,15},{10,... | collective-permute-start | bytes 245768 | tf_op jit(solution)/shard_map/ppermute | solution.py:251
  19.9 12.4 %collective-permute-start.8 = (bf16[4096,256]{1,0:T(8,128)(2,1)}, bf16[4096,256]{1,0:T(8,128)(2,1)}, u32[]{:S(2)}, u32[]{:S(2)}) collective-permute-start(bf16[4096,256]{1,0:T(8,128)(2,1)} %bitcast.9), channel_id=1, source_target_pairs={{0,1},{1,0},{2,3},{3,2},{4,5},{5,4},{6,7},{7,6},{8,9},{9,8},{10,11... | collective-permute-start | bytes 6291464 | tf_op jit(solution)/shard_map/ppermute | solution.py:262
  20.0 12.3 %collective-permute-start.9 = (bf16[4096,256]{1,0:T(8,128)(2,1)}, bf16[4096,256]{1,0:T(8,128)(2,1)}, u32[]{:S(2)}, u32[]{:S(2)}) collective-permute-start(bf16[4096,256]{1,0:T(8,128)(2,1)} %bitcast.16), channel_id=1, source_target_pairs={{0,1},{1,0},{2,3},{3,2},{4,5},{5,4},{6,7},{7,6},{8,9},{9,8},{10,11... | collective-permute-start | bytes 6291464 | tf_op jit(solution)/shard_map/ppermute | solution.py:262
  20.4 11.9 %collective-permute-start.10 = (bf16[256,4096]{1,0:T(8,128)(2,1)}, bf16[256,4096]{1,0:T(8,128)(2,1)}, u32[]{:S(2)}, u32[]{:S(2)}) collective-permute-start(bf16[256,4096]{1,0:T(8,128)(2,1)} %bitcast.23), channel_id=1, source_target_pairs={{0,1},{1,0},{2,3},{3,2},{4,5},{5,4},{6,7},{7,6},{8,9},{9,8},{10,11... | collective-permute-start | bytes 6291464 | tf_op jit(solution)/shard_map/ppermute | solution.py:262
  32.3 6.6 %collective-permute-start.11 = (bf16[32,4096]{1,0:T(8,128)(2,1)}, bf16[32,4096]{1,0:T(8,128)(2,1)S(1)}, u32[]{:S(2)}, u32[]{:S(2)}) collective-permute-start(bf16[32,4096]{1,0:T(8,128)(2,1)} %get-tuple-element.55.refs_3_), channel_id=1, source_target_pairs={{0,4},{1,3},{4,8},{5,1},{8,12},{9,5},{12,14},{13,9},{14,10},{15,13... | collective-permute-start | bytes 786440 | tf_op jit(solution)/shard_map/ppermute | solution.py:273
  33.4 8.3 %collective-permute-start.13 = (bf16[32,4096]{1,0:T(8,128)(2,1)}, bf16[32,4096]{1,0:T(8,128)(2,1)S(1)}, u32[]{:S(2)}, u32[]{:S(2)}) collective-permute-start(bf16[32,4096]{1,0:T(8,128)(2,1)} %get-tuple-element.57.refs_4_), channel_id=1, source_target_pairs={{0,4},{1,3},{4,8},{5,1},{8,12},{9,5},{12,14},{13,9},{14,10},{15,13... | collective-permute-start | bytes 786440 | tf_op jit(solution)/shard_map/ppermute | solution.py:273
  38.9 13.2 %collective-permute-start.12 = (bf16[32,4096]{1,0:T(8,128)(2,1)S(1)}, bf16[32,4096]{1,0:T(8,128)(2,1)S(1)}, u32[]{:S(2)}, u32[]{:S(2)}) collective-permute-start(bf16[32,4096]{1,0:T(8,128)(2,1)S(1)} %collective-permute-done.11.refs_0_), channel_id=1, source_target_pairs={{0,4},{1,3},{4,8},{5,1},{8,12},{9,5},{12,14},{13,9},{14,10},{15,13... | collective-permute-start | bytes 786440 | tf_op jit(solution)/shard_map/ppermute | solution.py:273
  41.8 10.4 %collective-permute-start.14 = (bf16[32,4096]{1,0:T(8,128)(2,1)S(1)}, bf16[32,4096]{1,0:T(8,128)(2,1)S(1)}, u32[]{:S(2)}, u32[]{:S(2)}) collective-permute-start(bf16[32,4096]{1,0:T(8,128)(2,1)S(1)} %collective-permute-done.13.refs_1_), channel_id=1, source_target_pairs={{0,4},{1,3},{4,8},{5,1},{8,12},{9,5},{12,14},{13,9},{14,10},{15,13... | collective-permute-start | bytes 786440 | tf_op jit(solution)/shard_map/ppermute | solution.py:273
  43.2 12.6 %collective-permute-start.15 = (bf16[64,4096]{1,0:T(8,128)(2,1)}, bf16[64,4096]{1,0:T(8,128)(2,1)S(1)}, u32[]{:S(2)}, u32[]{:S(2)}) collective-permute-start(bf16[64,4096]{1,0:T(8,128)(2,1)} %get-tuple-element.59), channel_id=1, source_target_pairs={{4,0},{3,1},{8,4},{1,5},{12,8},{5,9},{14,12},{9,13},{10,14},{13,15... | collective-permute-start | bytes 1572872 | tf_op jit(solution)/shard_map/ppermute | solution.py:273
  48.2 15.2 %collective-permute-start.18 = (bf16[32,4096]{1,0:T(8,128)(2,1)S(1)}, bf16[32,4096]{1,0:T(8,128)(2,1)S(1)}, u32[]{:S(2)}, u32[]{:S(2)}) collective-permute-start(bf16[32,4096]{1,0:T(8,128)(2,1)S(1)} %convert_element_type.99), channel_id=1, source_target_pairs={{0,4},{1,3},{4,8},{5,1},{8,12},{9,5},{12,14},{13,9},{14,10},{15,13... | collective-permute-start | bytes 786440 | tf_op jit(solution)/shard_map/ppermute | solution.py:273
  50.1 10.9 %collective-permute-start.27 = (bf16[32,4096]{1,0:T(8,128)(2,1)S(1)}, bf16[32,4096]{1,0:T(8,128)(2,1)S(1)}, u32[]{:S(2)}, u32[]{:S(2)}) collective-permute-start(bf16[32,4096]{1,0:T(8,128)(2,1)S(1)} %convert_element_type.113), channel_id=1, source_target_pairs={{0,4},{1,3},{4,8},{5,1},{8,12},{9,5},{12,14},{13,9},{14,10},{15,13... | collective-permute-start | bytes 786440 | tf_op jit(solution)/shard_map/ppermute | solution.py:273
  52.2 12.8 %collective-permute-start.16 = (bf16[64,4096]{1,0:T(8,128)(2,1)S(1)}, bf16[64,4096]{1,0:T(8,128)(2,1)S(1)}, u32[]{:S(2)}, u32[]{:S(2)}) collective-permute-start(bf16[64,4096]{1,0:T(8,128)(2,1)S(1)} %pad_maximum_fusion), channel_id=1, source_target_pairs={{0,4},{1,3},{4,8},{5,1},{8,12},{9,5},{12,14},{13,9},{14,10},{15,13... | collective-permute-start | bytes 1572872 | tf_op jit(solution)/shard_map/ppermute | solution.py:273
  61.1 9.7 %collective-permute-start.28 = (bf16[32,4096]{1,0:T(8,128)(2,1)S(1)}, bf16[32,4096]{1,0:T(8,128)(2,1)S(1)}, u32[]{:S(2)}, u32[]{:S(2)}) collective-permute-start(bf16[32,4096]{1,0:T(8,128)(2,1)S(1)} %add_convert_fusion.5), channel_id=1, source_target_pairs={{0,4},{1,3},{4,8},{5,1},{8,12},{9,5},{12,14},{13,9},{14,10},{15,13... | collective-permute-start | bytes 786440 | tf_op jit(solution)/shard_map/ppermute | solution.py:273
  63.5 9.8 %collective-permute-start.20 = (bf16[32,4096]{1,0:T(8,128)(2,1)S(1)}, bf16[32,4096]{1,0:T(8,128)(2,1)S(1)}, u32[]{:S(2)}, u32[]{:S(2)}) collective-permute-start(bf16[32,4096]{1,0:T(8,128)(2,1)S(1)} %add_convert_fusion.11), channel_id=1, source_target_pairs={{0,4},{1,3},{4,8},{5,1},{8,12},{9,5},{12,14},{13,9},{14,10},{15,13... | collective-permute-start | bytes 786440 | tf_op jit(solution)/shard_map/ppermute | solution.py:273
  65.0 11.2 %collective-permute-start.17 = (bf16[64,4096]{1,0:T(8,128)(2,1)S(1)}, bf16[64,4096]{1,0:T(8,128)(2,1)S(1)}, u32[]{:S(2)}, u32[]{:S(2)}) collective-permute-start(bf16[64,4096]{1,0:T(8,128)(2,1)S(1)} %collective-permute-done.16.refs_0_), channel_id=1, source_target_pairs={{0,4},{1,3},{4,8},{5,1},{8,12},{9,5},{12,14},{13,9},{14,10},{15,13... | collective-permute-start | bytes 1572872 | tf_op jit(solution)/shard_map/ppermute | solution.py:273
  70.8 11.7 %collective-permute-start.29 = (bf16[32,4096]{1,0:T(8,128)(2,1)S(1)}, bf16[32,4096]{1,0:T(8,128)(2,1)S(1)}, u32[]{:S(2)}, u32[]{:S(2)}) collective-permute-start(bf16[32,4096]{1,0:T(8,128)(2,1)S(1)} %add_convert_fusion.4), channel_id=1, source_target_pairs={{0,4},{1,3},{4,8},{5,1},{8,12},{9,5},{12,14},{13,9},{14,10},{15,13... | collective-permute-start | bytes 786440 | tf_op jit(solution)/shard_map/ppermute | solution.py:273
  73.3 11.2 %collective-permute-start.22 = (bf16[32,4096]{1,0:T(8,128)(2,1)S(1)}, bf16[32,4096]{1,0:T(8,128)(2,1)S(1)}, u32[]{:S(2)}, u32[]{:S(2)}) collective-permute-start(bf16[32,4096]{1,0:T(8,128)(2,1)S(1)} %add_convert_fusion.10), channel_id=1, source_target_pairs={{0,4},{1,3},{4,8},{5,1},{8,12},{9,5},{12,14},{13,9},{14,10},{15,13... | collective-permute-start | bytes 786440 | tf_op jit(solution)/shard_map/ppermute | solution.py:273
  76.2 11.2 %collective-permute-start.19 = (bf16[64,4096]{1,0:T(8,128)(2,1)S(1)}, bf16[64,4096]{1,0:T(8,128)(2,1)S(1)}, u32[]{:S(2)}, u32[]{:S(2)}) collective-permute-start(bf16[64,4096]{1,0:T(8,128)(2,1)S(1)} %collective-permute-done.17.refs_0_), channel_id=1, source_target_pairs={{0,4},{1,3},{4,8},{5,1},{8,12},{9,5},{12,14},{13,9},{14,10},{15,13... | collective-permute-start | bytes 1572872 | tf_op jit(solution)/shard_map/ppermute | solution.py:273
  82.6 11.2 %collective-permute-start.30 = (bf16[32,4096]{1,0:T(8,128)(2,1)S(1)}, bf16[32,4096]{1,0:T(8,128)(2,1)S(1)}, u32[]{:S(2)}, u32[]{:S(2)}) collective-permute-start(bf16[32,4096]{1,0:T(8,128)(2,1)S(1)} %add_convert_fusion.3), channel_id=1, source_target_pairs={{0,4},{1,3},{4,8},{5,1},{8,12},{9,5},{12,14},{13,9},{14,10},{15,13... | collective-permute-start | bytes 786440 | tf_op jit(solution)/shard_map/ppermute | solution.py:273
  84.5 11.2 %collective-permute-start.23 = (bf16[32,4096]{1,0:T(8,128)(2,1)S(1)}, bf16[32,4096]{1,0:T(8,128)(2,1)S(1)}, u32[]{:S(2)}, u32[]{:S(2)}) collective-permute-start(bf16[32,4096]{1,0:T(8,128)(2,1)S(1)} %add_convert_fusion.9), channel_id=1, source_target_pairs={{0,4},{1,3},{4,8},{5,1},{8,12},{9,5},{12,14},{13,9},{14,10},{15,13... | collective-permute-start | bytes 786440 | tf_op jit(solution)/shard_map/ppermute | solution.py:273
  87.5 11.2 %collective-permute-start.21 = (bf16[64,4096]{1,0:T(8,128)(2,1)S(1)}, bf16[64,4096]{1,0:T(8,128)(2,1)S(1)}, u32[]{:S(2)}, u32[]{:S(2)}) collective-permute-start(bf16[64,4096]{1,0:T(8,128)(2,1)S(1)} %collective-permute-done.19.refs_0_), channel_id=1, source_target_pairs={{0,4},{1,3},{4,8},{5,1},{8,12},{9,5},{12,14},{13,9},{14,10},{15,13... | collective-permute-start | bytes 1572872 | tf_op jit(solution)/shard_map/ppermute | solution.py:273
  93.8 9.2 %collective-permute-start.31 = (bf16[32,4096]{1,0:T(8,128)(2,1)S(1)}, bf16[32,4096]{1,0:T(8,128)(2,1)S(1)}, u32[]{:S(2)}, u32[]{:S(2)}) collective-permute-start(bf16[32,4096]{1,0:T(8,128)(2,1)S(1)} %add_convert_fusion.2), channel_id=1, source_target_pairs={{0,4},{1,3},{4,8},{5,1},{8,12},{9,5},{12,14},{13,9},{14,10},{15,13... | collective-permute-start | bytes 786440 | tf_op jit(solution)/shard_map/ppermute | solution.py:273
  95.7 9.4 %collective-permute-start.24 = (bf16[32,4096]{1,0:T(8,128)(2,1)S(1)}, bf16[32,4096]{1,0:T(8,128)(2,1)S(1)}, u32[]{:S(2)}, u32[]{:S(2)}) collective-permute-start(bf16[32,4096]{1,0:T(8,128)(2,1)S(1)} %add_convert_fusion.8), channel_id=1, source_target_pairs={{0,4},{1,3},{4,8},{5,1},{8,12},{9,5},{12,14},{13,9},{14,10},{15,13... | collective-permute-start | bytes 786440 | tf_op jit(solution)/shard_map/ppermute | solution.py:273
  103.1 6.4 %collective-permute-start.32 = (bf16[32,4096]{1,0:T(8,128)(2,1)S(1)}, bf16[32,4096]{1,0:T(8,128)(2,1)S(1)}, u32[]{:S(2)}, u32[]{:S(2)}) collective-permute-start(bf16[32,4096]{1,0:T(8,128)(2,1)S(1)} %add_convert_fusion.1), channel_id=1, source_target_pairs={{0,4},{1,3},{4,8},{5,1},{8,12},{9,5},{12,14},{13,9},{14,10},{15,13... | collective-permute-start | bytes 786440 | tf_op jit(solution)/shard_map/ppermute | solution.py:273
  105.2 7.1 %collective-permute-start.25 = (bf16[32,4096]{1,0:T(8,128)(2,1)S(1)}, bf16[32,4096]{1,0:T(8,128)(2,1)S(1)}, u32[]{:S(2)}, u32[]{:S(2)}) collective-permute-start(bf16[32,4096]{1,0:T(8,128)(2,1)S(1)} %add_convert_fusion.7), channel_id=1, source_target_pairs={{0,4},{1,3},{4,8},{5,1},{8,12},{9,5},{12,14},{13,9},{14,10},{15,13... | collective-permute-start | bytes 786440 | tf_op jit(solution)/shard_map/ppermute | solution.py:273
  109.6 6.4 %collective-permute-start.33 = (bf16[32,4096]{1,0:T(8,128)(2,1)S(1)}, bf16[32,4096]{1,0:T(8,128)(2,1)S(1)}, u32[]{:S(2)}, u32[]{:S(2)}) collective-permute-start(bf16[32,4096]{1,0:T(8,128)(2,1)S(1)} %add_convert_fusion), channel_id=1, source_target_pairs={{0,4},{1,3},{4,8},{5,1},{8,12},{9,5},{12,14},{13,9},{14,10},{15,13... | collective-permute-start | bytes 786440 | tf_op jit(solution)/shard_map/ppermute | solution.py:273
  112.4 6.4 %collective-permute-start.26 = (bf16[32,4096]{1,0:T(8,128)(2,1)S(1)}, bf16[32,4096]{1,0:T(8,128)(2,1)S(1)}, u32[]{:S(2)}, u32[]{:S(2)}) collective-permute-start(bf16[32,4096]{1,0:T(8,128)(2,1)S(1)} %add_convert_fusion.6), channel_id=1, source_target_pairs={{0,4},{1,3},{4,8},{5,1},{8,12},{9,5},{12,14},{13,9},{14,10},{15,13... | collective-permute-start | bytes 786440 | tf_op jit(solution)/shard_map/ppermute | solution.py:273
  (11 other events, 126.5 us)

commit v20 on v19

--- a/solution.py
+++ b/solution.py
@@ -93,7 +93,7 @@
             weights_b.astype(jnp.bfloat16).reshape(rows, keys), other_ref[:, 0:LAT],
             preferred_element_type=jnp.float32,
         )
-        latent = (mixed.reshape(SUB_HEADS, tok, LAT) / total).astype(jnp.bfloat16)
+        latent = (mixed.reshape(SUB_HEADS, tok, LAT) * (1.0 / total)).astype(jnp.bfloat16)
         for head in range(0, SUB_HEADS, 2):
             first = sub * SUB_HEADS + head
             pair = jnp.dot(

time: 120 us -> 120 us (level)
  no operation moved by 1% of the time
where the time goes in v20:
time: 120 us
  starting transfers between devices  48.4 us (40%)
  Pallas kernels  38.3 us (32%)
  waiting for transfers between devices  28.3 us (24%)
  other arithmetic  4.12 us (3%)
    ppermute x23, starting transfers between devices, move(): return tuple((lax.ppermute(x, 'ctx', way) for x in blocks))  36.3 us
    pallas_call x6, Pallas kernels, expert_parts(): pl.pallas_call(functools.partial(expert_kernel, hops=hops, chips=chips),...  26.7 us
    ppermute x23, waiting for transfers between devices, move(): return tuple((lax.ppermute(x, 'ctx', way) for x in blocks))  21.7 us
    pallas_call x1, Pallas kernels, attention(): pl.pallas_call(functools.partial(attention_kernel, tok=tok), grid_spec=gr...  11.5 us
    ppermute x7, starting transfers between devices, from_chip(): lax.ppermute(block, 'ctx', [(i, i ^ step * CORES) for i in range(n_ctx)])  11.4 us
    ppermute x7, waiting for transfers between devices, from_chip(): lax.ppermute(block, 'ctx', [(i, i ^ step * CORES) for i in range(n_ctx)])  4.54 us
  transfers between devices with their start and end apart: 34, of which 17 were waited for; matrix products, arithmetic and copies ran while one was open for 1% of the time, Pallas kernels for 32%

profile of v20, /device:TPU:0, one launch (start us, length us, event | category | flops | bytes accessed | tf_op | source)
XLA Modules:
  0.0 119.8 jit_solution(5232058168918060538)
XLA Ops:
  1.7 4.1 %collective-permute-start.3 = (bf16[64,640]{1,0:T(8,128)(2,1)S(1)}, bf16[64,640]{1,0:T(8,128)(2,1)S(1)}, u32[]{:S(2)}, u32[]{:S(2)}) collective-permute-start(bf16[64,640]{1,0:T(8,128)(2,1)S(1)} %get-tuple-element.79), channel_id=1, source_target_pairs={{0,8},{1,9},{2,10},{3,11},{4,12},{5,13},{6,14},{7,15},{8,0},{9,1},... | collective-permute-start | bytes 245768 | tf_op jit(solution)/shard_map/ppermute | solution.py:251
  7.3 1.6 %collective-permute-start.1 = (bf16[64,640]{1,0:T(8,128)(2,1)S(1)}, bf16[64,640]{1,0:T(8,128)(2,1)S(1)}, u32[]{:S(2)}, u32[]{:S(2)}) collective-permute-start(bf16[64,640]{1,0:T(8,128)(2,1)S(1)} %get-tuple-element.79), channel_id=1, source_target_pairs={{0,4},{1,5},{2,6},{3,7},{4,0},{5,1},{6,2},{7,3},{8,12},{9,13},{10,... | collective-permute-start | bytes 245768 | tf_op jit(solution)/shard_map/ppermute | solution.py:251
  9.8 1.6 %collective-permute-start.4 = (bf16[64,640]{1,0:T(8,128)(2,1)S(1)}, bf16[64,640]{1,0:T(8,128)(2,1)S(1)}, u32[]{:S(2)}, u32[]{:S(2)}) collective-permute-start(bf16[64,640]{1,0:T(8,128)(2,1)S(1)} %collective-permute-done.3), channel_id=1, source_target_pairs={{0,2},{1,3},{2,0},{3,1},{4,6},{5,7},{6,4},{7,5},{8,10},{9,11},{10,... | collective-permute-start | bytes 245768 | tf_op jit(solution)/shard_map/ppermute | solution.py:251
  15.9 1.8 %collective-permute-done.6 = bf16[64,640]{1,0:T(8,128)(2,1)S(1)} collective-permute-done((bf16[64,640]{1,0:T(8,128)(2,1)S(1)}, bf16[64,640]{1,0:T(8,128)(2,1)S(1)}, u32[]{:S(2)}, u32[]{:S(2)}) %collective-permute-start.6) | collective-permute-done | bytes 81952 | tf_op jit(solution)/shard_map/ppermute | solution.py:251
  17.8 2.1 %collective-permute-done.7.other_ref = bf16[512,640]{1,0:T(8,128)(2,1)S(1)} collective-permute-done((bf16[512,640]{1,0:T(8,128)(2,1)S(1)}, bf16[512,640]{1,0:T(8,128)(2,1)S(1)}, u32[]{:S(2)}, u32[]{:S(2)}) %collective-permute-start.7) | collective-permute-done | bytes 655392 | tf_op jit(solution)/shard_map/ppermute | solution.py:259
  20.8 11.5 %shard_map.109 = (bf16[64,4096]{1,0:T(8,128)(2,1)}, bf16[64,4096]{1,0:T(8,128)(2,1)}, bf16[32,4096]{1,0:T(8,128)(2,1)}, bf16[32,4096]{1,0:T(8,128)(2,1)}, f32[64,8]{1,0:T(8,128)}) custom-call(s32[1]{0:T(128)} %bitcast.index_ref, bf16[64,16384]{1,0:T(8,128)(2,1)} %q_ref.1, bf16[64,2048]{1,0:T(8,128)(2,1)} %qr_ref.1, bf16[512,640]{1,0:T(8,128)(2,1)} %copy-done.6, ...), custom_call_target="tpu_custom_call" | custom-call | flops 4831838208 | bytes 8388608 | tf_op jit(solution)/shard_map/pallas_call | solution.py:151
  33.4 2.7 %collective-permute-start.13 = (bf16[32,4096]{1,0:T(8,128)(2,1)}, bf16[32,4096]{1,0:T(8,128)(2,1)S(1)}, u32[]{:S(2)}, u32[]{:S(2)}) collective-permute-start(bf16[32,4096]{1,0:T(8,128)(2,1)} %get-tuple-element.57.refs_4_), channel_id=1, source_target_pairs={{0,4},{1,3},{4,8},{5,1},{8,12},{9,5},{12,14},{13,9},{14,10},{15,13... | collective-permute-start | bytes 786440 | tf_op jit(solution)/shard_map/ppermute | solution.py:273
  36.9 2.0 %collective-permute-done.11.refs_0_ = bf16[32,4096]{1,0:T(8,128)(2,1)S(1)} collective-permute-done((bf16[32,4096]{1,0:T(8,128)(2,1)}, bf16[32,4096]{1,0:T(8,128)(2,1)S(1)}, u32[]{:S(2)}, u32[]{:S(2)}) %collective-permute-start.11) | collective-permute-done | bytes 262176 | tf_op jit(solution)/shard_map/ppermute | solution.py:273
  43.8 4.3 %shard_map.111 = (f32[32,4096]{1,0:T(8,128)S(1)}, f32[32,4096]{1,0:T(8,128)S(1)}) custom-call(s32[1]{0:T(128)} %bitcast.index_ref, bf16[4096,256]{1,0:T(8,128)(2,1)S(1)} %bitcast.10, bf16[4096,256]{1,0:T(8,128)(2,1)S(1)} %bitcast.17, bf16[256,4096]{1,0:T(8,128)(2,1)S(1)} %bitcast.24, f32[64,8]{1,0:T(8,128)S(1)} %compare_select_fusion.hits_hbm, ...), custom_call_target="tpu_custom_call" | custom-call | flops 805306368 | bytes 14680064 | tf_op jit(solution)/shard_map/pallas_call | solution.py:219
  48.2 1.9 %collective-permute-start.18 = (bf16[32,4096]{1,0:T(8,128)(2,1)S(1)}, bf16[32,4096]{1,0:T(8,128)(2,1)S(1)}, u32[]{:S(2)}, u32[]{:S(2)}) collective-permute-start(bf16[32,4096]{1,0:T(8,128)(2,1)S(1)} %convert_element_type.99), channel_id=1, source_target_pairs={{0,4},{1,3},{4,8},{5,1},{8,12},{9,5},{12,14},{13,9},{14,10},{15,13... | collective-permute-start | bytes 786440 | tf_op jit(solution)/shard_map/ppermute | solution.py:273
  50.1 2.0 %collective-permute-start.27 = (bf16[32,4096]{1,0:T(8,128)(2,1)S(1)}, bf16[32,4096]{1,0:T(8,128)(2,1)S(1)}, u32[]{:S(2)}, u32[]{:S(2)}) collective-permute-start(bf16[32,4096]{1,0:T(8,128)(2,1)S(1)} %convert_element_type.113), channel_id=1, source_target_pairs={{0,4},{1,3},{4,8},{5,1},{8,12},{9,5},{12,14},{13,9},{14,10},{15,13... | collective-permute-start | bytes 786440 | tf_op jit(solution)/shard_map/ppermute | solution.py:273
  53.7 2.1 %collective-permute-done.15.refs_2_ = bf16[64,4096]{1,0:T(8,128)(2,1)S(1)} collective-permute-done((bf16[64,4096]{1,0:T(8,128)(2,1)}, bf16[64,4096]{1,0:T(8,128)(2,1)S(1)}, u32[]{:S(2)}, u32[]{:S(2)}) %collective-permute-start.15) | collective-permute-done | bytes 524320 | tf_op jit(solution)/shard_map/ppermute | solution.py:273
  55.8 5.2 %shard_map.110 = (f32[32,4096]{1,0:T(8,128)S(1)}, f32[32,4096]{1,0:T(8,128)S(1)}, f32[32,4096]{1,0:T(8,128)S(1)}, f32[32,4096]{1,0:T(8,128)S(1)}, f32[32,4096]{1,0:T(8,128)S(1)}, /*index=5*/f32[32,4096]{1,0:T(8,128)S(1)}) custom-call(s32[1]{0:T(128)} %bitcast.index_ref, bf16[4096,256]{1,0:T(8,128)(2,1)S(1)} %bitcast.11, bf16[4096,256]{1,0:T(8,128)(2,1)S(1)} %bitcast.18, ...), custom_call_target="tpu_custom_call" | custom-call | flops 805306368 | bytes 14680064 | tf_op jit(solution)/shard_map/pallas_call | solution.py:219
  61.1 2.4 %collective-permute-start.28 = (bf16[32,4096]{1,0:T(8,128)(2,1)S(1)}, bf16[32,4096]{1,0:T(8,128)(2,1)S(1)}, u32[]{:S(2)}, u32[]{:S(2)}) collective-permute-start(bf16[32,4096]{1,0:T(8,128)(2,1)S(1)} %add_convert_fusion.5), channel_id=1, source_target_pairs={{0,4},{1,3},{4,8},{5,1},{8,12},{9,5},{12,14},{13,9},{14,10},{15,13... | collective-permute-start | bytes 786440 | tf_op jit(solution)/shard_map/ppermute | solution.py:273
  66.4 4.3 %shard_map.112 = (f32[32,4096]{1,0:T(8,128)S(1)}, f32[32,4096]{1,0:T(8,128)S(1)}) custom-call(s32[1]{0:T(128)} %bitcast.index_ref, bf16[4096,256]{1,0:T(8,128)(2,1)S(1)} %bitcast.12, bf16[4096,256]{1,0:T(8,128)(2,1)S(1)} %bitcast.19, bf16[256,4096]{1,0:T(8,128)(2,1)S(1)} %bitcast.26, f32[64,8]{1,0:T(8,128)S(1)} %compare_select_fusion.hits_hbm, ...), custom_call_target="tpu_custom_call" | custom-call | flops 805306368 | bytes 14680064 | tf_op jit(solution)/shard_map/pallas_call | solution.py:219
  70.8 2.4 %collective-permute-start.29 = (bf16[32,4096]{1,0:T(8,128)(2,1)S(1)}, bf16[32,4096]{1,0:T(8,128)(2,1)S(1)}, u32[]{:S(2)}, u32[]{:S(2)}) collective-permute-start(bf16[32,4096]{1,0:T(8,128)(2,1)S(1)} %add_convert_fusion.4), channel_id=1, source_target_pairs={{0,4},{1,3},{4,8},{5,1},{8,12},{9,5},{12,14},{13,9},{14,10},{15,13... | collective-permute-start | bytes 786440 | tf_op jit(solution)/shard_map/ppermute | solution.py:273
  73.7 2.5 %collective-permute-done.17.refs_0_ = bf16[64,4096]{1,0:T(8,128)(2,1)S(1)} collective-permute-done((bf16[64,4096]{1,0:T(8,128)(2,1)S(1)}, bf16[64,4096]{1,0:T(8,128)(2,1)S(1)}, u32[]{:S(2)}, u32[]{:S(2)}) %collective-permute-start.17) | collective-permute-done | bytes 524320 | tf_op jit(solution)/shard_map/ppermute | solution.py:273
  76.2 2.0 %collective-permute-start.19 = (bf16[64,4096]{1,0:T(8,128)(2,1)S(1)}, bf16[64,4096]{1,0:T(8,128)(2,1)S(1)}, u32[]{:S(2)}, u32[]{:S(2)}) collective-permute-start(bf16[64,4096]{1,0:T(8,128)(2,1)S(1)} %collective-permute-done.17.refs_0_), channel_id=1, source_target_pairs={{0,4},{1,3},{4,8},{5,1},{8,12},{9,5},{12,14},{13,9},{14,10},{15,13... | collective-permute-start | bytes 1572872 | tf_op jit(solution)/shard_map/ppermute | solution.py:273
  78.2 4.3 %shard_map.115 = (f32[32,4096]{1,0:T(8,128)S(1)}, f32[32,4096]{1,0:T(8,128)S(1)}) custom-call(s32[1]{0:T(128)} %bitcast.index_ref, bf16[4096,256]{1,0:T(8,128)(2,1)S(1)} %bitcast.13, bf16[4096,256]{1,0:T(8,128)(2,1)S(1)} %bitcast.20, bf16[256,4096]{1,0:T(8,128)(2,1)S(1)} %bitcast.27, f32[64,8]{1,0:T(8,128)S(1)} %compare_select_fusion.hits_hbm, ...), custom_call_target="tpu_custom_call" | custom-call | flops 805306368 | bytes 14680064 | tf_op jit(solution)/shard_map/pallas_call | solution.py:219
  82.6 1.9 %collective-permute-start.30 = (bf16[32,4096]{1,0:T(8,128)(2,1)S(1)}, bf16[32,4096]{1,0:T(8,128)(2,1)S(1)}, u32[]{:S(2)}, u32[]{:S(2)}) collective-permute-start(bf16[32,4096]{1,0:T(8,128)(2,1)S(1)} %add_convert_fusion.3), channel_id=1, source_target_pairs={{0,4},{1,3},{4,8},{5,1},{8,12},{9,5},{12,14},{13,9},{14,10},{15,13... | collective-permute-start | bytes 786440 | tf_op jit(solution)/shard_map/ppermute | solution.py:273
  84.9 2.5 %collective-permute-done.19.refs_0_ = bf16[64,4096]{1,0:T(8,128)(2,1)S(1)} collective-permute-done((bf16[64,4096]{1,0:T(8,128)(2,1)S(1)}, bf16[64,4096]{1,0:T(8,128)(2,1)S(1)}, u32[]{:S(2)}, u32[]{:S(2)}) %collective-permute-start.19) | collective-permute-done | bytes 524320 | tf_op jit(solution)/shard_map/ppermute | solution.py:273
  87.5 2.0 %collective-permute-start.21 = (bf16[64,4096]{1,0:T(8,128)(2,1)S(1)}, bf16[64,4096]{1,0:T(8,128)(2,1)S(1)}, u32[]{:S(2)}, u32[]{:S(2)}) collective-permute-start(bf16[64,4096]{1,0:T(8,128)(2,1)S(1)} %collective-permute-done.19.refs_0_), channel_id=1, source_target_pairs={{0,4},{1,3},{4,8},{5,1},{8,12},{9,5},{12,14},{13,9},{14,10},{15,13... | collective-permute-start | bytes 1572872 | tf_op jit(solution)/shard_map/ppermute | solution.py:273
  89.4 4.3 %shard_map.114 = (f32[32,4096]{1,0:T(8,128)S(1)}, f32[32,4096]{1,0:T(8,128)S(1)}) custom-call(s32[1]{0:T(128)} %bitcast.index_ref, bf16[4096,256]{1,0:T(8,128)(2,1)S(1)} %bitcast.14, bf16[4096,256]{1,0:T(8,128)(2,1)S(1)} %bitcast.21, bf16[256,4096]{1,0:T(8,128)(2,1)S(1)} %bitcast.28, f32[64,8]{1,0:T(8,128)S(1)} %compare_select_fusion.hits_hbm, ...), custom_call_target="tpu_custom_call" | custom-call | flops 805306368 | bytes 14680064 | tf_op jit(solution)/shard_map/pallas_call | solution.py:219
  93.8 1.9 %collective-permute-start.31 = (bf16[32,4096]{1,0:T(8,128)(2,1)S(1)}, bf16[32,4096]{1,0:T(8,128)(2,1)S(1)}, u32[]{:S(2)}, u32[]{:S(2)}) collective-permute-start(bf16[32,4096]{1,0:T(8,128)(2,1)S(1)} %add_convert_fusion.2), channel_id=1, source_target_pairs={{0,4},{1,3},{4,8},{5,1},{8,12},{9,5},{12,14},{13,9},{14,10},{15,13... | collective-permute-start | bytes 786440 | tf_op jit(solution)/shard_map/ppermute | solution.py:273
  96.2 2.5 %collective-permute-done.21.refs_0_ = bf16[64,4096]{1,0:T(8,128)(2,1)S(1)} collective-permute-done((bf16[64,4096]{1,0:T(8,128)(2,1)S(1)}, bf16[64,4096]{1,0:T(8,128)(2,1)S(1)}, u32[]{:S(2)}, u32[]{:S(2)}) %collective-permute-start.21) | collective-permute-done | bytes 524320 | tf_op jit(solution)/shard_map/ppermute | solution.py:273
  98.7 4.3 %shard_map.113 = (f32[32,4096]{1,0:T(8,128)S(1)}, f32[32,4096]{1,0:T(8,128)S(1)}) custom-call(s32[1]{0:T(128)} %bitcast.index_ref, bf16[4096,256]{1,0:T(8,128)(2,1)S(1)} %bitcast.15, bf16[4096,256]{1,0:T(8,128)(2,1)S(1)} %bitcast.22, bf16[256,4096]{1,0:T(8,128)(2,1)S(1)} %bitcast.29, f32[64,8]{1,0:T(8,128)S(1)} %compare_select_fusion.hits_hbm, ...), custom_call_target="tpu_custom_call" | custom-call | flops 805306368 | bytes 14680064 | tf_op jit(solution)/shard_map/pallas_call | solution.py:219
  103.1 2.1 %collective-permute-start.32 = (bf16[32,4096]{1,0:T(8,128)(2,1)S(1)}, bf16[32,4096]{1,0:T(8,128)(2,1)S(1)}, u32[]{:S(2)}, u32[]{:S(2)}) collective-permute-start(bf16[32,4096]{1,0:T(8,128)(2,1)S(1)} %add_convert_fusion.1), channel_id=1, source_target_pairs={{0,4},{1,3},{4,8},{5,1},{8,12},{9,5},{12,14},{13,9},{14,10},{15,13... | collective-permute-start | bytes 786440 | tf_op jit(solution)/shard_map/ppermute | solution.py:273
  105.2 1.9 %collective-permute-start.25 = (bf16[32,4096]{1,0:T(8,128)(2,1)S(1)}, bf16[32,4096]{1,0:T(8,128)(2,1)S(1)}, u32[]{:S(2)}, u32[]{:S(2)}) collective-permute-start(bf16[32,4096]{1,0:T(8,128)(2,1)S(1)} %add_convert_fusion.7), channel_id=1, source_target_pairs={{0,4},{1,3},{4,8},{5,1},{8,12},{9,5},{12,14},{13,9},{14,10},{15,13... | collective-permute-start | bytes 786440 | tf_op jit(solution)/shard_map/ppermute | solution.py:273
  107.0 2.5 %collective-permute-done.32 = bf16[32,4096]{1,0:T(8,128)(2,1)S(1)} collective-permute-done((bf16[32,4096]{1,0:T(8,128)(2,1)S(1)}, bf16[32,4096]{1,0:T(8,128)(2,1)S(1)}, u32[]{:S(2)}, u32[]{:S(2)}) %collective-permute-start.32) | collective-permute-done | bytes 262176 | tf_op jit(solution)/shard_map/ppermute | solution.py:273
  109.6 2.1 %collective-permute-start.33 = (bf16[32,4096]{1,0:T(8,128)(2,1)S(1)}, bf16[32,4096]{1,0:T(8,128)(2,1)S(1)}, u32[]{:S(2)}, u32[]{:S(2)}) collective-permute-start(bf16[32,4096]{1,0:T(8,128)(2,1)S(1)} %add_convert_fusion), channel_id=1, source_target_pairs={{0,4},{1,3},{4,8},{5,1},{8,12},{9,5},{12,14},{13,9},{14,10},{15,13... | collective-permute-start | bytes 786440 | tf_op jit(solution)/shard_map/ppermute | solution.py:273
  112.4 2.1 %collective-permute-start.26 = (bf16[32,4096]{1,0:T(8,128)(2,1)S(1)}, bf16[32,4096]{1,0:T(8,128)(2,1)S(1)}, u32[]{:S(2)}, u32[]{:S(2)}) collective-permute-start(bf16[32,4096]{1,0:T(8,128)(2,1)S(1)} %add_convert_fusion.6), channel_id=1, source_target_pairs={{0,4},{1,3},{4,8},{5,1},{8,12},{9,5},{12,14},{13,9},{14,10},{15,13... | collective-permute-start | bytes 786440 | tf_op jit(solution)/shard_map/ppermute | solution.py:273
  116.0 2.8 %collective-permute-done.26 = bf16[32,4096]{1,0:T(8,128)(2,1)S(1)} collective-permute-done((bf16[32,4096]{1,0:T(8,128)(2,1)S(1)}, bf16[32,4096]{1,0:T(8,128)(2,1)S(1)}, u32[]{:S(2)}, u32[]{:S(2)}) %collective-permute-start.26) | collective-permute-done | bytes 262176 | tf_op jit(solution)/shard_map/ppermute | solution.py:273
  (91 shorter events, 26.0 us)
Async XLA Ops:
  1.7 8.1 %collective-permute-start.3 = (bf16[64,640]{1,0:T(8,128)(2,1)S(1)}, bf16[64,640]{1,0:T(8,128)(2,1)S(1)}, u32[]{:S(2)}, u32[]{:S(2)}) collective-permute-start(bf16[64,640]{1,0:T(8,128)(2,1)S(1)} %get-tuple-element.79), channel_id=1, source_target_pairs={{0,8},{1,9},{2,10},{3,11},{4,12},{5,13},{6,14},{7,15},{8,0},{9,1},... | collective-permute-start | bytes 245768 | tf_op jit(solution)/shard_map/ppermute | solution.py:251
  5.8 6.6 %collective-permute-start = (bf16[64,640]{1,0:T(8,128)(2,1)S(1)}, bf16[64,640]{1,0:T(8,128)(2,1)S(1)}, u32[]{:S(2)}, u32[]{:S(2)}) collective-permute-start(bf16[64,640]{1,0:T(8,128)(2,1)S(1)} %get-tuple-element.79), channel_id=1, source_target_pairs={{0,2},{1,3},{2,0},{3,1},{4,6},{5,7},{6,4},{7,5},{8,10},{9,11},{10,... | collective-permute-start | bytes 245768 | tf_op jit(solution)/shard_map/ppermute | solution.py:251
  7.3 6.3 %collective-permute-start.1 = (bf16[64,640]{1,0:T(8,128)(2,1)S(1)}, bf16[64,640]{1,0:T(8,128)(2,1)S(1)}, u32[]{:S(2)}, u32[]{:S(2)}) collective-permute-start(bf16[64,640]{1,0:T(8,128)(2,1)S(1)} %get-tuple-element.79), channel_id=1, source_target_pairs={{0,4},{1,5},{2,6},{3,7},{4,0},{5,1},{6,2},{7,3},{8,12},{9,13},{10,... | collective-permute-start | bytes 245768 | tf_op jit(solution)/shard_map/ppermute | solution.py:251
  8.9 5.6 %collective-permute-start.2 = (bf16[64,640]{1,0:T(8,128)(2,1)S(1)}, bf16[64,640]{1,0:T(8,128)(2,1)S(1)}, u32[]{:S(2)}, u32[]{:S(2)}) collective-permute-start(bf16[64,640]{1,0:T(8,128)(2,1)S(1)} %get-tuple-element.79), channel_id=1, source_target_pairs={{0,6},{1,7},{2,4},{3,5},{4,2},{5,3},{6,0},{7,1},{8,14},{9,15},{10,... | collective-permute-start | bytes 245768 | tf_op jit(solution)/shard_map/ppermute | solution.py:251
  9.8 5.5 %collective-permute-start.4 = (bf16[64,640]{1,0:T(8,128)(2,1)S(1)}, bf16[64,640]{1,0:T(8,128)(2,1)S(1)}, u32[]{:S(2)}, u32[]{:S(2)}) collective-permute-start(bf16[64,640]{1,0:T(8,128)(2,1)S(1)} %collective-permute-done.3), channel_id=1, source_target_pairs={{0,2},{1,3},{2,0},{3,1},{4,6},{5,7},{6,4},{7,5},{8,10},{9,11},{10,... | collective-permute-start | bytes 245768 | tf_op jit(solution)/shard_map/ppermute | solution.py:251
  12.4 5.3 %collective-permute-start.6 = (bf16[64,640]{1,0:T(8,128)(2,1)S(1)}, bf16[64,640]{1,0:T(8,128)(2,1)S(1)}, u32[]{:S(2)}, u32[]{:S(2)}) collective-permute-start(bf16[64,640]{1,0:T(8,128)(2,1)S(1)} %collective-permute-done.3), channel_id=1, source_target_pairs={{0,6},{1,7},{2,4},{3,5},{4,2},{5,3},{6,0},{7,1},{8,14},{9,15},{10,... | collective-permute-start | bytes 245768 | tf_op jit(solution)/shard_map/ppermute | solution.py:251
  19.9 12.4 %collective-permute-start.8 = (bf16[4096,256]{1,0:T(8,128)(2,1)}, bf16[4096,256]{1,0:T(8,128)(2,1)}, u32[]{:S(2)}, u32[]{:S(2)}) collective-permute-start(bf16[4096,256]{1,0:T(8,128)(2,1)} %bitcast.9), channel_id=1, source_target_pairs={{0,1},{1,0},{2,3},{3,2},{4,5},{5,4},{6,7},{7,6},{8,9},{9,8},{10,11... | collective-permute-start | bytes 6291464 | tf_op jit(solution)/shard_map/ppermute | solution.py:262
  20.0 12.3 %collective-permute-start.9 = (bf16[4096,256]{1,0:T(8,128)(2,1)}, bf16[4096,256]{1,0:T(8,128)(2,1)}, u32[]{:S(2)}, u32[]{:S(2)}) collective-permute-start(bf16[4096,256]{1,0:T(8,128)(2,1)} %bitcast.16), channel_id=1, source_target_pairs={{0,1},{1,0},{2,3},{3,2},{4,5},{5,4},{6,7},{7,6},{8,9},{9,8},{10,11... | collective-permute-start | bytes 6291464 | tf_op jit(solution)/shard_map/ppermute | solution.py:262
  20.4 11.9 %collective-permute-start.10 = (bf16[256,4096]{1,0:T(8,128)(2,1)}, bf16[256,4096]{1,0:T(8,128)(2,1)}, u32[]{:S(2)}, u32[]{:S(2)}) collective-permute-start(bf16[256,4096]{1,0:T(8,128)(2,1)} %bitcast.23), channel_id=1, source_target_pairs={{0,1},{1,0},{2,3},{3,2},{4,5},{5,4},{6,7},{7,6},{8,9},{9,8},{10,11... | collective-permute-start | bytes 6291464 | tf_op jit(solution)/shard_map/ppermute | solution.py:262
  32.3 6.6 %collective-permute-start.11 = (bf16[32,4096]{1,0:T(8,128)(2,1)}, bf16[32,4096]{1,0:T(8,128)(2,1)S(1)}, u32[]{:S(2)}, u32[]{:S(2)}) collective-permute-start(bf16[32,4096]{1,0:T(8,128)(2,1)} %get-tuple-element.55.refs_3_), channel_id=1, source_target_pairs={{0,4},{1,3},{4,8},{5,1},{8,12},{9,5},{12,14},{13,9},{14,10},{15,13... | collective-permute-start | bytes 786440 | tf_op jit(solution)/shard_map/ppermute | solution.py:273
  33.4 8.3 %collective-permute-start.13 = (bf16[32,4096]{1,0:T(8,128)(2,1)}, bf16[32,4096]{1,0:T(8,128)(2,1)S(1)}, u32[]{:S(2)}, u32[]{:S(2)}) collective-permute-start(bf16[32,4096]{1,0:T(8,128)(2,1)} %get-tuple-element.57.refs_4_), channel_id=1, source_target_pairs={{0,4},{1,3},{4,8},{5,1},{8,12},{9,5},{12,14},{13,9},{14,10},{15,13... | collective-permute-start | bytes 786440 | tf_op jit(solution)/shard_map/ppermute | solution.py:273
  38.9 13.2 %collective-permute-start.12 = (bf16[32,4096]{1,0:T(8,128)(2,1)S(1)}, bf16[32,4096]{1,0:T(8,128)(2,1)S(1)}, u32[]{:S(2)}, u32[]{:S(2)}) collective-permute-start(bf16[32,4096]{1,0:T(8,128)(2,1)S(1)} %collective-permute-done.11.refs_0_), channel_id=1, source_target_pairs={{0,4},{1,3},{4,8},{5,1},{8,12},{9,5},{12,14},{13,9},{14,10},{15,13... | collective-permute-start | bytes 786440 | tf_op jit(solution)/shard_map/ppermute | solution.py:273
  41.8 10.4 %collective-permute-start.14 = (bf16[32,4096]{1,0:T(8,128)(2,1)S(1)}, bf16[32,4096]{1,0:T(8,128)(2,1)S(1)}, u32[]{:S(2)}, u32[]{:S(2)}) collective-permute-start(bf16[32,4096]{1,0:T(8,128)(2,1)S(1)} %collective-permute-done.13.refs_1_), channel_id=1, source_target_pairs={{0,4},{1,3},{4,8},{5,1},{8,12},{9,5},{12,14},{13,9},{14,10},{15,13... | collective-permute-start | bytes 786440 | tf_op jit(solution)/shard_map/ppermute | solution.py:273
  43.2 12.6 %collective-permute-start.15 = (bf16[64,4096]{1,0:T(8,128)(2,1)}, bf16[64,4096]{1,0:T(8,128)(2,1)S(1)}, u32[]{:S(2)}, u32[]{:S(2)}) collective-permute-start(bf16[64,4096]{1,0:T(8,128)(2,1)} %get-tuple-element.59), channel_id=1, source_target_pairs={{4,0},{3,1},{8,4},{1,5},{12,8},{5,9},{14,12},{9,13},{10,14},{13,15... | collective-permute-start | bytes 1572872 | tf_op jit(solution)/shard_map/ppermute | solution.py:273
  48.2 15.2 %collective-permute-start.18 = (bf16[32,4096]{1,0:T(8,128)(2,1)S(1)}, bf16[32,4096]{1,0:T(8,128)(2,1)S(1)}, u32[]{:S(2)}, u32[]{:S(2)}) collective-permute-start(bf16[32,4096]{1,0:T(8,128)(2,1)S(1)} %convert_element_type.99), channel_id=1, source_target_pairs={{0,4},{1,3},{4,8},{5,1},{8,12},{9,5},{12,14},{13,9},{14,10},{15,13... | collective-permute-start | bytes 786440 | tf_op jit(solution)/shard_map/ppermute | solution.py:273
  50.1 10.9 %collective-permute-start.27 = (bf16[32,4096]{1,0:T(8,128)(2,1)S(1)}, bf16[32,4096]{1,0:T(8,128)(2,1)S(1)}, u32[]{:S(2)}, u32[]{:S(2)}) collective-permute-start(bf16[32,4096]{1,0:T(8,128)(2,1)S(1)} %convert_element_type.113), channel_id=1, source_target_pairs={{0,4},{1,3},{4,8},{5,1},{8,12},{9,5},{12,14},{13,9},{14,10},{15,13... | collective-permute-start | bytes 786440 | tf_op jit(solution)/shard_map/ppermute | solution.py:273
  52.2 12.8 %collective-permute-start.16 = (bf16[64,4096]{1,0:T(8,128)(2,1)S(1)}, bf16[64,4096]{1,0:T(8,128)(2,1)S(1)}, u32[]{:S(2)}, u32[]{:S(2)}) collective-permute-start(bf16[64,4096]{1,0:T(8,128)(2,1)S(1)} %pad_maximum_fusion), channel_id=1, source_target_pairs={{0,4},{1,3},{4,8},{5,1},{8,12},{9,5},{12,14},{13,9},{14,10},{15,13... | collective-permute-start | bytes 1572872 | tf_op jit(solution)/shard_map/ppermute | solution.py:273
  61.1 9.7 %collective-permute-start.28 = (bf16[32,4096]{1,0:T(8,128)(2,1)S(1)}, bf16[32,4096]{1,0:T(8,128)(2,1)S(1)}, u32[]{:S(2)}, u32[]{:S(2)}) collective-permute-start(bf16[32,4096]{1,0:T(8,128)(2,1)S(1)} %add_convert_fusion.5), channel_id=1, source_target_pairs={{0,4},{1,3},{4,8},{5,1},{8,12},{9,5},{12,14},{13,9},{14,10},{15,13... | collective-permute-start | bytes 786440 | tf_op jit(solution)/shard_map/ppermute | solution.py:273
  63.5 9.8 %collective-permute-start.20 = (bf16[32,4096]{1,0:T(8,128)(2,1)S(1)}, bf16[32,4096]{1,0:T(8,128)(2,1)S(1)}, u32[]{:S(2)}, u32[]{:S(2)}) collective-permute-start(bf16[32,4096]{1,0:T(8,128)(2,1)S(1)} %add_convert_fusion.11), channel_id=1, source_target_pairs={{0,4},{1,3},{4,8},{5,1},{8,12},{9,5},{12,14},{13,9},{14,10},{15,13... | collective-permute-start | bytes 786440 | tf_op jit(solution)/shard_map/ppermute | solution.py:273
  65.0 11.2 %collective-permute-start.17 = (bf16[64,4096]{1,0:T(8,128)(2,1)S(1)}, bf16[64,4096]{1,0:T(8,128)(2,1)S(1)}, u32[]{:S(2)}, u32[]{:S(2)}) collective-permute-start(bf16[64,4096]{1,0:T(8,128)(2,1)S(1)} %collective-permute-done.16.refs_0_), channel_id=1, source_target_pairs={{0,4},{1,3},{4,8},{5,1},{8,12},{9,5},{12,14},{13,9},{14,10},{15,13... | collective-permute-start | bytes 1572872 | tf_op jit(solution)/shard_map/ppermute | solution.py:273
  70.8 11.7 %collective-permute-start.29 = (bf16[32,4096]{1,0:T(8,128)(2,1)S(1)}, bf16[32,4096]{1,0:T(8,128)(2,1)S(1)}, u32[]{:S(2)}, u32[]{:S(2)}) collective-permute-start(bf16[32,4096]{1,0:T(8,128)(2,1)S(1)} %add_convert_fusion.4), channel_id=1, source_target_pairs={{0,4},{1,3},{4,8},{5,1},{8,12},{9,5},{12,14},{13,9},{14,10},{15,13... | collective-permute-start | bytes 786440 | tf_op jit(solution)/shard_map/ppermute | solution.py:273
  73.3 11.2 %collective-permute-start.22 = (bf16[32,4096]{1,0:T(8,128)(2,1)S(1)}, bf16[32,4096]{1,0:T(8,128)(2,1)S(1)}, u32[]{:S(2)}, u32[]{:S(2)}) collective-permute-start(bf16[32,4096]{1,0:T(8,128)(2,1)S(1)} %add_convert_fusion.10), channel_id=1, source_target_pairs={{0,4},{1,3},{4,8},{5,1},{8,12},{9,5},{12,14},{13,9},{14,10},{15,13... | collective-permute-start | bytes 786440 | tf_op jit(solution)/shard_map/ppermute | solution.py:273
  76.2 11.2 %collective-permute-start.19 = (bf16[64,4096]{1,0:T(8,128)(2,1)S(1)}, bf16[64,4096]{1,0:T(8,128)(2,1)S(1)}, u32[]{:S(2)}, u32[]{:S(2)}) collective-permute-start(bf16[64,4096]{1,0:T(8,128)(2,1)S(1)} %collective-permute-done.17.refs_0_), channel_id=1, source_target_pairs={{0,4},{1,3},{4,8},{5,1},{8,12},{9,5},{12,14},{13,9},{14,10},{15,13... | collective-permute-start | bytes 1572872 | tf_op jit(solution)/shard_map/ppermute | solution.py:273
  82.6 11.2 %collective-permute-start.30 = (bf16[32,4096]{1,0:T(8,128)(2,1)S(1)}, bf16[32,4096]{1,0:T(8,128)(2,1)S(1)}, u32[]{:S(2)}, u32[]{:S(2)}) collective-permute-start(bf16[32,4096]{1,0:T(8,128)(2,1)S(1)} %add_convert_fusion.3), channel_id=1, source_target_pairs={{0,4},{1,3},{4,8},{5,1},{8,12},{9,5},{12,14},{13,9},{14,10},{15,13... | collective-permute-start | bytes 786440 | tf_op jit(solution)/shard_map/ppermute | solution.py:273
  84.5 11.2 %collective-permute-start.23 = (bf16[32,4096]{1,0:T(8,128)(2,1)S(1)}, bf16[32,4096]{1,0:T(8,128)(2,1)S(1)}, u32[]{:S(2)}, u32[]{:S(2)}) collective-permute-start(bf16[32,4096]{1,0:T(8,128)(2,1)S(1)} %add_convert_fusion.9), channel_id=1, source_target_pairs={{0,4},{1,3},{4,8},{5,1},{8,12},{9,5},{12,14},{13,9},{14,10},{15,13... | collective-permute-start | bytes 786440 | tf_op jit(solution)/shard_map/ppermute | solution.py:273
  87.5 11.2 %collective-permute-start.21 = (bf16[64,4096]{1,0:T(8,128)(2,1)S(1)}, bf16[64,4096]{1,0:T(8,128)(2,1)S(1)}, u32[]{:S(2)}, u32[]{:S(2)}) collective-permute-start(bf16[64,4096]{1,0:T(8,128)(2,1)S(1)} %collective-permute-done.19.refs_0_), channel_id=1, source_target_pairs={{0,4},{1,3},{4,8},{5,1},{8,12},{9,5},{12,14},{13,9},{14,10},{15,13... | collective-permute-start | bytes 1572872 | tf_op jit(solution)/shard_map/ppermute | solution.py:273
  93.8 9.2 %collective-permute-start.31 = (bf16[32,4096]{1,0:T(8,128)(2,1)S(1)}, bf16[32,4096]{1,0:T(8,128)(2,1)S(1)}, u32[]{:S(2)}, u32[]{:S(2)}) collective-permute-start(bf16[32,4096]{1,0:T(8,128)(2,1)S(1)} %add_convert_fusion.2), channel_id=1, source_target_pairs={{0,4},{1,3},{4,8},{5,1},{8,12},{9,5},{12,14},{13,9},{14,10},{15,13... | collective-permute-start | bytes 786440 | tf_op jit(solution)/shard_map/ppermute | solution.py:273
  95.7 9.4 %collective-permute-start.24 = (bf16[32,4096]{1,0:T(8,128)(2,1)S(1)}, bf16[32,4096]{1,0:T(8,128)(2,1)S(1)}, u32[]{:S(2)}, u32[]{:S(2)}) collective-permute-start(bf16[32,4096]{1,0:T(8,128)(2,1)S(1)} %add_convert_fusion.8), channel_id=1, source_target_pairs={{0,4},{1,3},{4,8},{5,1},{8,12},{9,5},{12,14},{13,9},{14,10},{15,13... | collective-permute-start | bytes 786440 | tf_op jit(solution)/shard_map/ppermute | solution.py:273
  103.1 6.4 %collective-permute-start.32 = (bf16[32,4096]{1,0:T(8,128)(2,1)S(1)}, bf16[32,4096]{1,0:T(8,128)(2,1)S(1)}, u32[]{:S(2)}, u32[]{:S(2)}) collective-permute-start(bf16[32,4096]{1,0:T(8,128)(2,1)S(1)} %add_convert_fusion.1), channel_id=1, source_target_pairs={{0,4},{1,3},{4,8},{5,1},{8,12},{9,5},{12,14},{13,9},{14,10},{15,13... | collective-permute-start | bytes 786440 | tf_op jit(solution)/shard_map/ppermute | solution.py:273
  105.2 7.1 %collective-permute-start.25 = (bf16[32,4096]{1,0:T(8,128)(2,1)S(1)}, bf16[32,4096]{1,0:T(8,128)(2,1)S(1)}, u32[]{:S(2)}, u32[]{:S(2)}) collective-permute-start(bf16[32,4096]{1,0:T(8,128)(2,1)S(1)} %add_convert_fusion.7), channel_id=1, source_target_pairs={{0,4},{1,3},{4,8},{5,1},{8,12},{9,5},{12,14},{13,9},{14,10},{15,13... | collective-permute-start | bytes 786440 | tf_op jit(solution)/shard_map/ppermute | solution.py:273
  109.6 6.4 %collective-permute-start.33 = (bf16[32,4096]{1,0:T(8,128)(2,1)S(1)}, bf16[32,4096]{1,0:T(8,128)(2,1)S(1)}, u32[]{:S(2)}, u32[]{:S(2)}) collective-permute-start(bf16[32,4096]{1,0:T(8,128)(2,1)S(1)} %add_convert_fusion), channel_id=1, source_target_pairs={{0,4},{1,3},{4,8},{5,1},{8,12},{9,5},{12,14},{13,9},{14,10},{15,13... | collective-permute-start | bytes 786440 | tf_op jit(solution)/shard_map/ppermute | solution.py:273
  112.4 6.4 %collective-permute-start.26 = (bf16[32,4096]{1,0:T(8,128)(2,1)S(1)}, bf16[32,4096]{1,0:T(8,128)(2,1)S(1)}, u32[]{:S(2)}, u32[]{:S(2)}) collective-permute-start(bf16[32,4096]{1,0:T(8,128)(2,1)S(1)} %add_convert_fusion.6), channel_id=1, source_target_pairs={{0,4},{1,3},{4,8},{5,1},{8,12},{9,5},{12,14},{13,9},{14,10},{15,13... | collective-permute-start | bytes 786440 | tf_op jit(solution)/shard_map/ppermute | solution.py:273
  (11 other events, 126.5 us)
